TPU v7x, 32 devices: a whole 2x2x4 slice. The times are simulated.
32 devices in a mesh: expert: 4 (over y, core), fsdp: 8 (over z, x).
Axes of the slice: x: 2, y: 2, z: 4, core: 2. Of those that a mesh axis runs over, the one named last changes fastest.
Arguments:
- hidden_in: bfloat16 [4096, 2048], P(('expert', 'fsdp')), may hold values from -6 to 6
- segment_ids: int32 [32, 128], P(('expert', 'fsdp')), may hold values from 0 to 3, never falling along the last dimension, each value on 1 to 64 neighbouring positions
- att_route: int32 [4096, 2], P(('expert', 'fsdp')), may hold values from 0 to 3, all different within a row; in each aligned block of 128 rows (0 to 127, 128 to 255, ...) at most 96 rows name the same one
- mlp_route: int32 [4096, 2], P(('expert', 'fsdp')), may hold values from 0 to 3, all different within a row; in each aligned block of 128 rows (0 to 127, 128 to 255, ...) at most 96 rows name the same one
- norm_gain1: float32 [2048], replicated, may hold values from 0.5 to 1.5
- norm_gain2: float32 [2048], replicated, may hold values from 0.5 to 1.5
- att_router: float32 [2048, 4], replicated, may hold values from -0.09375 to 0.09375
- mlp_router: float32 [2048, 4], replicated, may hold values from -0.09375 to 0.09375
- kv_weight: bfloat16 [2048, 4096], P(('expert', 'fsdp')), may hold values from -0.125 to 0.125
- query_weight: bfloat16 [4, 2048, 2048], P('expert', 'fsdp'), may hold values from -0.125 to 0.125
- out_weight: bfloat16 [4, 2048, 2048], P('expert', 'fsdp'), may hold values from -0.5 to 0.5
- att_bias: float32 [2048], replicated, may hold values from -0.6 to 0.6
- up_weight: bfloat16 [4, 2, 5632, 2048], P('expert', None, 'fsdp'), may hold values from -0.125 to 0.125
- down_weight: bfloat16 [4, 5632, 2048], P('expert', 'fsdp'), may hold values from -0.078125 to 0.078125
- mlp_bias: float32 [2048], replicated, may hold values from -0.6 to 0.6
- cotangent: float32 [4096, 2048], P(('expert', 'fsdp')), may hold values from -6 to 6
Outputs:
- layer_out: float32 [4096, 2048], P(('expert', 'fsdp'))
- grad_input: float32 [4096, 2048], P(('expert', 'fsdp'))
- grad_gain1: float32 [2048], replicated
- grad_gain2: float32 [2048], replicated
- grad_att_router: float32 [2048, 4], replicated
- grad_mlp_router: float32 [2048, 4], replicated
- grad_kv: float32 [2048, 4096], P(('expert', 'fsdp'))
- grad_query: float32 [4, 2048, 2048], P('expert', 'fsdp')
- grad_out: float32 [4, 2048, 2048], P('expert', 'fsdp')
- grad_att_bias: float32 [2048], replicated
- grad_up: float32 [4, 2, 5632, 2048], P('expert', None, 'fsdp')
- grad_down: float32 [4, 5632, 2048], P('expert', 'fsdp')
- grad_mlp_bias: float32 [2048], replicated
Inputs may be any that keep to these rules, and one draw needn't show every extreme that they name: `att_route`: the 128 rows of one device name one expert at most 96 times, and this bound is reached; no row names one expert twice. `mlp_route`: the 128 rows of one device name one expert at most 96 times, and this bound is reached; no row names one expert twice. `segment_ids`: along a sequence segment ids never fall; a document holds at most 64 positions.
All inputs are finite; a program needn't handle non-finite values.
Results may differ from a plain program's by a relative error of at most 0.018.
Values may be sent and summed in bfloat16 or wider, within the bound.
No kernel may reach another device: no remote copies, remote signals or barrier semaphores. Data moves between devices by JAX's collectives and lax.ppermute only.
A program may use at most 512 MiB of HBM per device.

v0:
```python
import math

import jax
import jax.numpy as jnp
from jax import lax
from jax.sharding import PartitionSpec as P

HEADS = 16
HD = 128
TOP = 2


EPSILON = 1e-06
HIGHEST = lax.Precision.HIGHEST
MASKED = -1e30


def rope_tables(length):
    half_dim = HD // 2
    frequency = jnp.exp(jnp.arange(half_dim, dtype=jnp.float32) * (-2.0 * math.log(10000.0) / HD))
    angles = jnp.arange(length, dtype=jnp.float32)[:, None] * frequency[None, :]
    return (jnp.cos(angles), jnp.sin(angles))


def rotate(tensor, cosine, sine_table):
    half_dim = tensor.shape[-1] // 2
    first_half = tensor[..., :half_dim]
    second_half = tensor[..., half_dim:]
    return jnp.concatenate(
        [
            first_half * cosine - second_half * sine_table,
            second_half * cosine + first_half * sine_table,
        ],
        axis=-1,
    )


def rotate_back(tensor, cosine, sine_table):
    half_dim = tensor.shape[-1] // 2
    first_half = tensor[..., :half_dim]
    second_half = tensor[..., half_dim:]
    return jnp.concatenate(
        [
            first_half * cosine + second_half * sine_table,
            second_half * cosine - first_half * sine_table,
        ],
        axis=-1,
    )


def norm_rows(stream, gain):
    inverse = lax.rsqrt(jnp.mean(stream * stream, axis=-1, keepdims=True) + EPSILON)
    return (stream * inverse * gain, inverse)


def norm_back(stream, inverse, gain, upstream):
    scaled = upstream * gain
    d_stream = inverse * scaled - stream * inverse**3 * jnp.mean(
        scaled * stream, axis=-1, keepdims=True
    )
    d_gain = jnp.sum(upstream * stream * inverse, axis=0)
    return (d_stream, d_gain)


def slot_index(route, experts, slot_count):
    flat_route = route.reshape(-1)
    onehot = (flat_route[:, None] == jnp.arange(experts, dtype=jnp.int32)[None, :]).astype(
        jnp.int32
    )
    earlier = jnp.cumsum(onehot, axis=0) - onehot
    return flat_route * slot_count + jnp.sum(earlier * onehot, axis=1)


def dispatch(rows, dest, experts, slot_count):
    buffer = jnp.zeros((experts * slot_count, rows.shape[1]), rows.dtype).at[dest].set(rows)
    return buffer.reshape(experts, slot_count, rows.shape[1])


def collect(buffer, dest, tokens):
    width = buffer.shape[2]
    return buffer.reshape(-1, width)[dest].reshape(tokens, TOP, width)


def spread_rows(rows):
    return jnp.broadcast_to(rows[:, None, :], (rows.shape[0], TOP, rows.shape[1])).reshape(
        -1, rows.shape[1]
    )


def heads_first(matrix):
    return matrix.reshape(matrix.shape[0], HEADS, HD).transpose(1, 0, 2)


def heads_last(tensor):
    return tensor.transpose(1, 0, 2).reshape(tensor.shape[1], HEADS * HD)


def choice_heads(rows):
    return rows.reshape(rows.shape[0], TOP, HEADS, HD).transpose(1, 2, 0, 3)


def rows_from_heads(tensor):
    return tensor.transpose(2, 0, 1, 3).reshape(tensor.shape[2] * TOP, HEADS * HD)


def pair_gates(normed, router, route, experts):
    logits = jnp.dot(normed.astype(jnp.float32), router, precision=HIGHEST)
    onehot = (route[:, :, None] == jnp.arange(experts, dtype=jnp.int32)[None, None, :]).astype(
        jnp.float32
    )
    picked = jnp.sum(logits[:, None, :] * onehot, axis=-1)
    return (jax.nn.softmax(picked, axis=-1), onehot)


def gates_back(gates, onehot, d_gates, normed, router):
    d_picked = gates * (d_gates - jnp.sum(gates * d_gates, axis=-1, keepdims=True))
    d_logits = jnp.sum(d_picked[:, :, None] * onehot, axis=1)
    d_router = jnp.dot(normed.astype(jnp.float32).T, d_logits, precision=HIGHEST)
    d_normed = jnp.dot(d_logits, router.T, precision=HIGHEST)
    return (d_router, d_normed)


def score_block(queries, key_rows, allowed):
    scores = jnp.einsum("chqd,hkd->chqk", queries, key_rows, preferred_element_type=jnp.float32) * (
        1.0 / math.sqrt(HD)
    )
    return jnp.where(allowed[None, None], scores, MASKED)


def mlp_hidden(rows, upper_mats):
    gate_in = jnp.einsum("esd,fd->esf", rows, upper_mats[0], preferred_element_type=jnp.float32)
    up_in = jnp.einsum("esd,fd->esf", rows, upper_mats[1], preferred_element_type=jnp.float32)
    hidden_units = (jax.nn.silu(gate_in) * up_in).astype(jnp.bfloat16)
    return (gate_in, up_in, hidden_units)


def down_rows(hidden_units, lower_mat):
    return jnp.einsum("esf,fd->esd", hidden_units, lower_mat, preferred_element_type=jnp.float32)


def mlp_grads_local(rows, lower_mat, gate_in, up_in, hidden_units, d_out):
    d_lower = jnp.einsum("esf,esd->fd", hidden_units, d_out, preferred_element_type=jnp.float32)
    d_hidden = jnp.einsum("esd,fd->esf", d_out, lower_mat, preferred_element_type=jnp.float32)
    sigma = jax.nn.sigmoid(gate_in)
    d_gate = (d_hidden * up_in * sigma * (1.0 + gate_in * (1.0 - sigma))).astype(jnp.bfloat16)
    d_up = (d_hidden * gate_in * sigma).astype(jnp.bfloat16)
    d_upper = jnp.stack(
        [
            jnp.einsum("esf,esd->fd", d_gate, rows, preferred_element_type=jnp.float32),
            jnp.einsum("esf,esd->fd", d_up, rows, preferred_element_type=jnp.float32),
        ]
    )
    return (d_upper, d_lower, d_gate, d_up)


def rows_back(d_gate, d_up, upper_mats):
    return jnp.einsum(
        "esf,fd->esd", d_gate, upper_mats[0], preferred_element_type=jnp.float32
    ) + jnp.einsum("esf,fd->esd", d_up, upper_mats[1], preferred_element_type=jnp.float32)


def send_out(buffer):
    return lax.all_to_all(buffer, "expert", split_axis=0, concat_axis=0, tiled=True)


def send_back(buffer):
    return lax.all_to_all(buffer, "expert", split_axis=0, concat_axis=0, tiled=True)


def shards(
    hidden_in,
    segment_ids,
    att_route,
    mlp_route,
    norm_gain1,
    norm_gain2,
    att_router,
    mlp_router,
    kv_weight,
    query_weight,
    out_weight,
    att_bias,
    up_weight,
    down_weight,
    mlp_bias,
    cotangent,
):
    experts = lax.axis_size("expert")
    tokens = hidden_in.shape[0]
    slot_count = 3 * TOP * tokens // (2 * experts)
    score_scale = 1.0 / math.sqrt(HD)
    cosine, sine_table = rope_tables(tokens)
    segment = segment_ids[0]
    position = jnp.arange(tokens)
    allowed = (segment[:, None] == segment[None, :]) & (position[None, :] <= position[:, None])
    residual = hidden_in.astype(jnp.float32)
    att_dest = slot_index(att_route, experts, slot_count)
    mlp_dest = slot_index(mlp_route, experts, slot_count)
    kv_full = lax.all_gather(kv_weight, ("expert", "fsdp"), axis=0, tiled=True)
    query_full, output_full = (
        lax.all_gather(query_weight, "fsdp", axis=1, tiled=True),
        lax.all_gather(out_weight, "fsdp", axis=1, tiled=True),
    )
    normed_one, inverse_one = norm_rows(residual, norm_gain1)
    attn_input = normed_one.astype(jnp.bfloat16)
    kv_raw = jnp.dot(attn_input, kv_full, preferred_element_type=jnp.float32)
    key_rows = rotate(heads_first(kv_raw[:, : HEADS * HD]), cosine, sine_table).astype(jnp.bfloat16)
    value_rows = heads_first(kv_raw[:, HEADS * HD :]).astype(jnp.bfloat16)
    att_gate, att_onehot = pair_gates(attn_input, att_router, att_route, experts)
    attn_recv = send_out(dispatch(spread_rows(attn_input), att_dest, experts, slot_count))
    query_out = jnp.einsum(
        "esd,df->esf", attn_recv, query_full[0], preferred_element_type=jnp.float32
    ).astype(jnp.bfloat16)
    query_rows = collect(send_back(query_out), att_dest, tokens)
    queries = rotate(choice_heads(query_rows.astype(jnp.float32)), cosine, sine_table).astype(
        jnp.bfloat16
    )
    scores = score_block(queries, key_rows, allowed)
    row_max = jnp.max(scores, axis=-1, keepdims=True)
    exponent = jnp.exp(scores - row_max)
    row_total = jnp.sum(exponent, axis=-1, keepdims=True)
    log_total = row_max + jnp.log(row_total)
    att_probs = (exponent / row_total).astype(jnp.bfloat16)
    attended = jnp.einsum(
        "chqk,hkd->chqd", att_probs, value_rows, preferred_element_type=jnp.float32
    ).astype(jnp.bfloat16)
    attended_recv = send_out(dispatch(rows_from_heads(attended), att_dest, experts, slot_count))
    branch_out = jnp.einsum(
        "esf,fd->esd", attended_recv, output_full[0], preferred_element_type=jnp.float32
    ).astype(jnp.bfloat16)
    branch_rows = collect(send_back(branch_out), att_dest, tokens).astype(jnp.float32)
    middle = residual + jnp.sum(att_gate[:, :, None] * branch_rows, axis=1) + att_bias
    normed_two, inverse_two = norm_rows(middle, norm_gain2)
    mlp_input = normed_two.astype(jnp.bfloat16)
    mlp_gate, mlp_onehot = pair_gates(mlp_input, mlp_router, mlp_route, experts)
    mlp_recv = send_out(dispatch(spread_rows(mlp_input), mlp_dest, experts, slot_count))
    upper_full, lower_full = (
        lax.all_gather(up_weight, "fsdp", axis=2, tiled=True),
        lax.all_gather(down_weight, "fsdp", axis=1, tiled=True),
    )
    upper_mats = upper_full[0]
    lower_mat = lower_full[0]
    gate_in, up_in, hidden_units = mlp_hidden(mlp_recv, upper_mats)
    mlp_out = down_rows(hidden_units, lower_mat).astype(jnp.bfloat16)
    mlp_rows = collect(send_back(mlp_out), mlp_dest, tokens).astype(jnp.float32)
    layer_out = middle + jnp.sum(mlp_gate[:, :, None] * mlp_rows, axis=1) + mlp_bias
    d_mlp_bias = jnp.sum(cotangent, axis=0)
    d_mlp_gate = jnp.sum(mlp_rows * cotangent[:, None, :], axis=-1)
    d_mlp_rows = (
        (mlp_gate[:, :, None] * cotangent[:, None, :])
        .astype(jnp.bfloat16)
        .reshape(tokens * TOP, -1)
    )
    d_expert_recv = send_out(dispatch(d_mlp_rows, mlp_dest, experts, slot_count))
    d_upper, d_lower, d_gate, d_up = mlp_grads_local(
        mlp_recv, lower_mat, gate_in, up_in, hidden_units, d_expert_recv
    )
    d_upper, d_lower = (
        lax.psum_scatter(
            d_upper[None].astype(jnp.bfloat16), "fsdp", scatter_dimension=2, tiled=True
        ).astype(jnp.float32),
        lax.psum_scatter(
            d_lower[None].astype(jnp.bfloat16), "fsdp", scatter_dimension=1, tiled=True
        ).astype(jnp.float32),
    )
    d_mlp_send = rows_back(d_gate, d_up, upper_mats).astype(jnp.bfloat16)
    d_mlp_input = jnp.sum(
        collect(send_back(d_mlp_send), mlp_dest, tokens).astype(jnp.float32), axis=1
    )
    d_mlp_router, d_mlp_from_router = gates_back(
        mlp_gate, mlp_onehot, d_mlp_gate, mlp_input, mlp_router
    )
    d_norm_two, d_gain_two = norm_back(
        middle, inverse_two, norm_gain2, d_mlp_input + d_mlp_from_router
    )
    d_middle = cotangent + d_norm_two
    d_att_bias = jnp.sum(d_middle, axis=0)
    d_att_gate = jnp.sum(branch_rows * d_middle[:, None, :], axis=-1)
    d_branch = (
        (att_gate[:, :, None] * d_middle[:, None, :]).astype(jnp.bfloat16).reshape(tokens * TOP, -1)
    )
    d_branch_recv = send_out(dispatch(d_branch, att_dest, experts, slot_count))
    d_output = jnp.einsum(
        "esf,esd->fd", attended_recv, d_branch_recv, preferred_element_type=jnp.float32
    )
    d_attended_out = jnp.einsum(
        "esd,fd->esf", d_branch_recv, output_full[0], preferred_element_type=jnp.float32
    ).astype(jnp.bfloat16)
    d_attended = choice_heads(collect(send_back(d_attended_out), att_dest, tokens))
    again = score_block(queries, key_rows, allowed)
    probs_full = jnp.exp(again - log_total)
    d_probs = jnp.einsum(
        "chqd,hkd->chqk", d_attended, value_rows, preferred_element_type=jnp.float32
    )
    d_scores = (
        probs_full * (d_probs - jnp.sum(probs_full * d_probs, axis=-1, keepdims=True))
    ).astype(jnp.bfloat16)
    d_queries = (
        jnp.einsum("chqk,hkd->chqd", d_scores, key_rows, preferred_element_type=jnp.float32)
        * score_scale
    )
    d_keys = (
        jnp.einsum("chqk,chqd->hkd", d_scores, queries, preferred_element_type=jnp.float32)
        * score_scale
    )
    d_values = jnp.einsum(
        "chqk,chqd->hkd",
        probs_full.astype(jnp.bfloat16),
        d_attended,
        preferred_element_type=jnp.float32,
    )
    d_query_rows = rows_from_heads(rotate_back(d_queries, cosine, sine_table)).astype(jnp.bfloat16)
    d_query_recv = send_out(dispatch(d_query_rows, att_dest, experts, slot_count))
    d_query = jnp.einsum("esd,esf->df", attn_recv, d_query_recv, preferred_element_type=jnp.float32)
    d_input_out = jnp.einsum(
        "esf,df->esd", d_query_recv, query_full[0], preferred_element_type=jnp.float32
    ).astype(jnp.bfloat16)
    d_attn_input = jnp.sum(
        collect(send_back(d_input_out), att_dest, tokens).astype(jnp.float32), axis=1
    )
    d_kv = jnp.concatenate(
        [heads_last(rotate_back(d_keys, cosine, sine_table)), heads_last(d_values)], axis=1
    ).astype(jnp.bfloat16)
    d_attn_input = d_attn_input + jnp.einsum(
        "tf,df->td", d_kv, kv_full, preferred_element_type=jnp.float32
    )
    d_att_router, d_att_from_router = gates_back(
        att_gate, att_onehot, d_att_gate, attn_input, att_router
    )
    d_norm_one, d_gain_one = norm_back(
        residual, inverse_one, norm_gain1, d_attn_input + d_att_from_router
    )
    d_input = d_middle + d_norm_one
    d_query, d_output = (
        lax.psum_scatter(
            d_query[None].astype(jnp.bfloat16), "fsdp", scatter_dimension=1, tiled=True
        ).astype(jnp.float32),
        lax.psum_scatter(
            d_output[None].astype(jnp.bfloat16), "fsdp", scatter_dimension=1, tiled=True
        ).astype(jnp.float32),
    )
    d_kv_weight = lax.psum_scatter(
        jnp.einsum("td,tf->df", attn_input, d_kv, preferred_element_type=jnp.float32),
        ("expert", "fsdp"),
        scatter_dimension=0,
        tiled=True,
    )
    summed_small = lax.psum(
        (d_gain_one, d_gain_two, d_att_router, d_mlp_router, d_att_bias, d_mlp_bias),
        ("expert", "fsdp"),
    )
    return (
        layer_out,
        d_input,
        summed_small[0],
        summed_small[1],
        summed_small[2],
        summed_small[3],
        d_kv_weight,
        d_query,
        d_output,
        summed_small[4],
        d_upper,
        d_lower,
        summed_small[5],
    )


def solution(mesh):
    placed = (
        P(("expert", "fsdp"), None),
        P(("expert", "fsdp"), None),
        P(("expert", "fsdp"), None),
        P(("expert", "fsdp"), None),
        P(),
        P(),
        P(),
        P(),
        P(("expert", "fsdp"), None),
        P("expert", "fsdp", None),
        P("expert", "fsdp", None),
        P(),
        P("expert", None, "fsdp", None),
        P("expert", "fsdp", None),
        P(),
        P(("expert", "fsdp"), None),
    )
    return jax.shard_map(
        shards,
        mesh=mesh,
        in_specs=placed,
        out_specs=(
            P(("expert", "fsdp"), None),
            P(("expert", "fsdp"), None),
            P(),
            P(),
            P(),
            P(),
            P(("expert", "fsdp"), None),
            P("expert", "fsdp", None),
            P("expert", "fsdp", None),
            P(),
            P("expert", None, "fsdp", None),
            P("expert", "fsdp", None),
            P(),
        ),
        check_vma=False,
    )
```

profile of v0, /device:TPU:0, one launch (start us, length us, event | category | flops | bytes accessed | tf_op | source)
XLA Modules:
  0.0 4116.5 jit_solution(314814623038143285)
XLA Ops:
  15.8 3.3 scatter_custom_fusion
  19.1 24.2 all_to_all.60
  43.3 94.5 %all-gather.8.cloned.1.call-done = bf16[1,2048,2048]{2,1,0:T(8,128)(2,1)} async-done(((bf16[1,256,2048]{2,1,0:T(8,128)(2,1)}), bf16[1,2048,2048]{2,1,0:T(8,128)(2,1)}) %all-gather.8.cloned.1.call-update) | async-done | bytes 8388624 | tf_op jit(solution)/shard_map/all_gather | solution.py:201
  137.8 8.4 fusion.21
  146.3 3.9 all-to-all-start.1
  150.6 20.6 all-to-all-done.1
  178.3 78.5 %all-gather.6.cloned.1.call-done = bf16[2048,4096]{1,0:T(8,128)(2,1)} async-done(((bf16[64,4096]{1,0:T(8,128)(2,1)}), bf16[2048,4096]{1,0:T(8,128)(2,1)}) %all-gather.6.cloned.1.call-update) | async-done | bytes 16777232 | tf_op jit(solution)/shard_map/all_gather | solution.py:199
  256.9 8.1 fusion.100
  277.4 3.9 scatter_custom_fusion.1
  281.3 3.7 all-to-all-start.2
  287.2 94.9 %all-gather.10.cloned.1.call-done = bf16[1,2048,2048]{2,1,0:T(8,128)(2,1)} async-done(((bf16[1,256,2048]{2,1,0:T(8,128)(2,1)}), bf16[1,2048,2048]{2,1,0:T(8,128)(2,1)}) %all-gather.10.cloned.1.call-update) | async-done | bytes 8388624 | tf_op jit(solution)/shard_map/all_gather | solution.py:202
  382.1 8.4 fusion.27
  390.6 3.7 all-to-all-start.3
  395.2 19.2 all-to-all-done.3
  424.9 3.4 scatter_custom_fusion.2
  428.3 3.7 all-to-all-start.4
  434.6 3.6 mul.652
  439.1 4.5 scatter_custom_fusion.3
  443.6 8.4 all-to-all-done.4
  452.1 3.6 all-to-all-start.6
  455.7 799.8 %all-gather.12.cloned.1.call-done = bf16[1,2,5632,2048]{3,2,1,0:T(8,128)(2,1)} async-done(((bf16[1,2,704,2048]{3,2,1,0:T(8,128)(2,1)}), bf16[1,2,5632,2048]{3,2,1,0:T(8,128)(2,1)}) %all-gather.12.cloned.1.call-update) | async-done | bytes 46137360 | tf_op jit(solution)/shard_map/all_gather | solution.py:238
  1255.4 15.8 fusion.7
  1271.2 15.7 fusion.5
  1286.9 411.1 %all-gather.14.cloned.1.call-done = bf16[1,5632,2048]{2,1,0:T(8,128)(2,1)} async-done(((bf16[1,704,2048]{2,1,0:T(8,128)(2,1)}), bf16[1,5632,2048]{2,1,0:T(8,128)(2,1)}) %all-gather.14.cloned.1.call-update) | async-done | bytes 23068688 | tf_op jit(solution)/shard_map/all_gather | solution.py:239
  1697.9 23.4 multiply_convert_fusion
  1721.3 16.1 fusion.33
  1737.3 3.7 all-to-all-start.5
  1741.1 16.1 fusion.4
  1757.1 14.9 add_convert_fusion
  1772.0 3.6 all-to-all-start.7
  1778.1 3.6 reshape.656
  1781.7 6.3 multiply_reduce_fusion.1
  1788.1 7.6 all-to-all-done.7
  1798.0 3.3 reshape.657
  1801.3 5.2 reduce_sum.251
  1806.5 3.2 multiply_reduce_fusion.4
  1818.1 3.8 scatter_custom_fusion.4
  1821.9 23.7 all_to_all.61
  1845.7 6.9 fusion.20
  1852.6 10.1 fusion.30
  1862.7 3.7 all-to-all-start.9
  1866.5 20.0 all-to-all-done.9
  1900.2 22.7 all_to_all.62
  1924.1 6.8 fusion.19
  1932.3 17.5 fusion.10
  1951.3 17.8 fusion.9
  1969.0 17.8 fusion.8
  1986.8 30.5 pad_maximum_fusion
  2022.4 8.5 fusion.24
  2030.9 3.7 all-to-all-start.11
  2044.9 3.6 fusion.43
  2048.5 6.1 all-to-all-done.11
  2057.0 3.3 reshape.658
  2060.3 5.2 reduce_sum.257
  2065.5 12.9 convolution_add_fusion.2
  2078.5 4.1 fusion.56
  2082.6 14.3 fusion.77
  2102.4 51.0 %reduce-scatter.8.cloned.1.call-done = bf16[1,256,2048]{2,1,0:T(8,128)(2,1)} async-done(((bf16[1,2048,2048]{2,1,0:T(8,128)(2,1)}), bf16[1,256,2048]{2,1,0:T(8,128)(2,1)}) %reduce-scatter.8.cloned.1.call-update) | async-done | bytes 1048592 | tf_op jit(solution)/shard_map/reduce_scatter | solution.py:335
  2156.2 373.7 %reduce-scatter.14.cloned.1.call-done = bf16[1,704,2048]{2,1,0:T(8,128)(2,1)} async-done(((bf16[1,5632,2048]{2,1,0:T(8,128)(2,1)}), bf16[1,704,2048]{2,1,0:T(8,128)(2,1)}) %reduce-scatter.14.cloned.1.call-update) | async-done | bytes 2883600 | tf_op jit(solution)/shard_map/reduce_scatter | solution.py:262
  2529.9 5.1 convert_element_type.218
  2535.0 725.6 %reduce-scatter.12.cloned.1.call-done = bf16[1,2,704,2048]{3,2,1,0:T(8,128)(2,1)} async-done(((bf16[1,2,5632,2048]{3,2,1,0:T(8,128)(2,1)}), bf16[1,2,704,2048]{3,2,1,0:T(8,128)(2,1)}) %reduce-scatter.12.cloned.1.call-update) | async-done | bytes 5767184 | tf_op jit(solution)/shard_map/reduce_scatter | solution.py:259
  3260.6 8.7 convert_element_type.215
  3269.3 122.4 %all-reduce.3.cloned.1.call-done = (f32[2048]{0:T(1024)}, f32[2048]{0:T(1024)}, f32[2048,4]{0,1:T(4,128)}, f32[2048,4]{0,1:T(4,128)}, f32[2048]{0:T(1024)}, /*index=5*/f32[2048]{0:T(1024)}) async-done(((f32[2048]{0:T(1024)}, f32[2048]{0:T(1024)}, f32[2048,4]{0,1:T(4,128)}, f32[2048,4]{0,1:T(4,128)}, f32[2048]{0:T(1024)}, /*index=5*/f32[2048]{0:T(1024)}), (f32[2048]{0:T(1024)}, f32[2048]{0:T(1024)}, ...) | async-done | bytes 98320 | tf_op jit(solution)/shard_map/psum | solution.py:348
  3391.7 710.0 %reduce-scatter.6.cloned.1.call-done = f32[64,4096]{1,0:T(8,128)} async-done(((f32[2048,4096]{1,0:T(8,128)}), f32[64,4096]{1,0:T(8,128)}) %reduce-scatter.6.cloned.1.call-update) | async-done | bytes 1048592 | tf_op jit(solution)/shard_map/reduce_scatter | solution.py:342
  (298 shorter events, 110.0 us)
Async XLA Ops:
  7.2 431.1 %copy-start = (f32[2048,4]{0,1:T(4,128)S(1)}, f32[2048,4]{0,1:T(4,128)}, u32[]{:S(2)}) copy-start(f32[2048,4]{0,1:T(4,128)} %param.23) | copy-start | bytes 98308
  7.2 130.7 %all-gather.8.cloned.1.call-start = ((), (), s32[]{:S(2)}) async-start(), calls=%async_computation.18 | async-start | bytes 9437184 | tf_op jit(solution)/shard_map/all_gather | solution.py:201
  7.9 248.9 %all-gather.6.cloned.1.call-start = ((), (), s32[]{:S(2)}) async-start(), calls=%async_computation.17 | async-start | bytes 17301504 | tf_op jit(solution)/shard_map/all_gather | solution.py:199
  8.7 373.5 %all-gather.10.cloned.1.call-start = ((), (), s32[]{:S(2)}) async-start(), calls=%async_computation.19 | async-start | bytes 9437184 | tf_op jit(solution)/shard_map/all_gather | solution.py:202
  9.4 1246.0 %all-gather.12.cloned.1.call-start = ((), (), s32[]{:S(2)}) async-start(), calls=%async_computation.20 | async-start | bytes 51904512 | tf_op jit(solution)/shard_map/all_gather | solution.py:238
  10.0 2.9 copy-start.12
  10.0 3.6 copy-start.49
  10.0 1687.9 %all-gather.14.cloned.1.call-start = ((), (), s32[]{:S(2)}) async-start(), calls=%async_computation.21 | async-start | bytes 25952256 | tf_op jit(solution)/shard_map/all_gather | solution.py:239
  13.8 380.5 %copy-start.4 = (bf16[128,2048]{1,0:T(8,128)(2,1)}, bf16[128,2048]{1,0:T(8,128)(2,1)S(1)}, u32[]{:S(2)}) copy-start(bf16[128,2048]{1,0:T(8,128)(2,1)S(1)} %fusion.49) | copy-start | bytes 1572868
  15.8 261.6 %copy-start.70 = (s32[256,1]{0,1:T(1,128)}, s32[256,1]{0,1:T(1,128)S(1)}, u32[]{:S(2)}) copy-start(s32[256,1]{0,1:T(1,128)S(1)} %compare_select_fusion.1) | copy-start | bytes 3076
  146.3 4.0 copy-start.71
  146.3 24.9 all-to-all-start.1
  150.2 264.2 %copy-start.57 = (s32[1024]{0:T(1024)}, s32[1024]{0:T(1024)S(1)}, u32[]{:S(2)}) copy-start(s32[1024]{0:T(1024)S(1)} %pad_clamp_fusion.1) | copy-start | bytes 12292
  150.6 117.7 %copy-start.32 = (f32[128,64]{1,0:T(8,128)}, f32[128,64]{1,0:T(8,128)S(1)}, u32[]{:S(2)}) copy-start(f32[128,64]{1,0:T(8,128)S(1)} %get-tuple-element.46) | copy-start | bytes 98308
  150.6 117.7 %copy-start.34 = (f32[128,64]{1,0:T(8,128)}, f32[128,64]{1,0:T(8,128)S(1)}, u32[]{:S(2)}) copy-start(f32[128,64]{1,0:T(8,128)S(1)} %get-tuple-element.47) | copy-start | bytes 98308
  178.3 90.4 %copy-start.14 = (bf16[2,16,128,64]{3,2,0,1:T(8,128)(2,1)}, bf16[2,16,128,64]{3,2,0,1:T(8,128)(2,1)S(1)}, u32[]{:S(2)}) copy-start(bf16[2,16,128,64]{3,2,0,1:T(8,128)(2,1)S(1)} %get-tuple-element.34) | copy-start | bytes 1572868
  266.6 5.8 copy-start.30
  281.3 3.7 copy-start.59
  281.3 100.9 %all-to-all-start.2 = ((bf16[4,96,2048]{2,1,0:T(8,128)(2,1)}), bf16[4,96,2048]{2,1,0:T(8,128)(2,1)S(1)}, u32[]{:S(2)}, u32[]{:S(2)}) async-start(bf16[4,96,2048]{2,1,0:T(8,128)(2,1)} %bitcast.19), calls=%async_computation.2 | async-start | bytes 3145728 | tf_op jit(solution)/shard_map/all_to_all | solution.py:163
  382.1 8.4 copy-start.39
  390.6 3.8 copy-start.46
  390.6 23.8 all-to-all-start.3
  394.9 21.8 copy-start.53
  394.9 21.8 copy-start.62
  395.0 21.8 copy-start.66
  419.1 3.5 copy-start.6
  419.1 3.2 copy-start.64
  423.8 14.4 copy-start.20
  424.9 7.2 copy-start.16
  428.3 23.8 all-to-all-start.4
  452.1 819.1 %copy-start.37 = (bf16[4,96,2048]{2,1,0:T(8,128)(2,1)}, bf16[4,96,2048]{2,1,0:T(8,128)(2,1)S(1)}, u32[]{:S(2)}) copy-start(bf16[4,96,2048]{2,1,0:T(8,128)(2,1)S(1)} %all-to-all-done.4) | copy-start | bytes 4718596
  452.1 834.8 %all-to-all-start.6 = ((bf16[4,96,2048]{2,1,0:T(8,128)(2,1)}), bf16[4,96,2048]{2,1,0:T(8,128)(2,1)S(1)}, u32[]{:S(2)}, u32[]{:S(2)}) async-start(bf16[4,96,2048]{2,1,0:T(8,128)(2,1)} %bitcast.35), calls=%async_computation.6 | async-start | bytes 3145728 | tf_op jit(solution)/shard_map/all_to_all | solution.py:163
  1286.9 434.4 %copy-start.41 = (bf16[4,96,2048]{2,1,0:T(8,128)(2,1)}, bf16[4,96,2048]{2,1,0:T(8,128)(2,1)S(1)}, u32[]{:S(2)}) copy-start(bf16[4,96,2048]{2,1,0:T(8,128)(2,1)S(1)} %all-to-all-done.6) | copy-start | bytes 4718596
  1737.3 19.8 slice-start
  1737.3 34.7 all-to-all-start.5
  1741.0 16.1 slice-start.1
  1772.0 23.6 all-to-all-start.7
  1775.6 324.0 %reduce-scatter.10.cloned.1.call-start = ((), (), s32[]{:S(2)}) async-start(), calls=%async_computation.24 | async-start | bytes 9437184 | tf_op jit(solution)/shard_map/reduce_scatter | solution.py:338
  1778.1 3.6 copy-start.17
  1788.1 18.4 copy-start.55
  1801.3 5.2 copy-start.11
  1806.5 3.2 copy-start.29
  1806.5 3.2 copy-start.65
  1821.9 23.7 copy-start.40
  1862.7 3.8 copy-start.45
  1862.7 3.8 copy-start.52
  1862.7 23.8 copy-start.58
  1862.7 23.7 all-to-all-start.9
  1866.4 287.1 %reduce-scatter.8.cloned.1.call-start = ((), (), s32[]{:S(2)}) async-start(), calls=%async_computation.23 | async-start | bytes 9437184 | tf_op jit(solution)/shard_map/reduce_scatter | solution.py:335
  1888.0 4.1 copy-start.18
  1900.2 23.8 copy-start.36
  1930.9 599.1 %reduce-scatter.14.cloned.1.call-start = ((), (), s32[]{:S(2)}) async-start(), calls=%async_computation.26 | async-start | bytes 25952256 | tf_op jit(solution)/shard_map/reduce_scatter | solution.py:262
  1949.9 1310.7 %reduce-scatter.12.cloned.1.call-start = ((), (), s32[]{:S(2)}) async-start(), calls=%async_computation.25 | async-start | bytes 51904512 | tf_op jit(solution)/shard_map/reduce_scatter | solution.py:259
  2030.9 3.8 copy-start.5
  2030.9 23.8 all-to-all-start.11
  2034.6 1357.1 %all-reduce.3.cloned.1.call-start = ((), (), s32[]{:S(2)}) async-start(), calls=%async_computation.27 | async-start | bytes 196608 | tf_op jit(solution)/shard_map/psum | solution.py:348
  2060.3 5.2 copy-start.22
  2060.3 5.2 copy-start.23
  2065.5 13.0 copy-start.13
  2065.5 13.0 copy-start.47
  2065.5 13.0 copy-start.50
  2065.5 12.9 copy-start.69
  2082.6 2019.2 %reduce-scatter.6.cloned.1.call-start = ((), (), s32[]{:S(2)}) async-start(), calls=%async_computation.22 | async-start | bytes 34603008 | tf_op jit(solution)/shard_map/reduce_scatter | solution.py:342
  3260.6 849.1 %copy-start.1 = (f32[2048,4]{0,1:T(4,128)S(1)}, f32[2048,4]{0,1:T(4,128)}, u32[]{:S(2)}) copy-start(f32[2048,4]{0,1:T(4,128)} %param.23) | copy-start | bytes 98308
  (31 other events, 41.9 us)
Sparse Core Ops, SparseCore 0:
  10.2 127.6 all-gather.7
  140.8 115.9 all-gather.5
  259.0 123.0 all-gather.9
  383.5 871.8 all-gather.11
  1256.8 441.0 all-gather.13
  1852.7 148.0 reduce-scatter.9
  2005.4 147.9 reduce-scatter.7
  2157.3 372.5 reduce-scatter.13
  2533.8 726.7 reduce-scatter.11
  3269.2 122.5 all-reduce.2
  3394.7 707.0 reduce-scatter.5
where the time goes:
time: 4120 us
  waiting for transfers between devices  3550 us (86%)
  matrix products  264 us (6%)
  other arithmetic  96.7 us (2%)
  local copies, waits for them, and re-layouts  89.9 us (2%)
  blocking collectives  70.6 us (2%)
    all_gather x1, waiting for transfers between devices, shards(): lax.all_gather(up_weight, 'fsdp', axis=2, tiled=True)  800 us
    reduce_scatter x1, waiting for transfers between devices, shards(): lax.psum_scatter(d_upper[None].astype(jnp.bfloat16), 'fsdp', scatter_dime...  726 us
    reduce_scatter x1, waiting for transfers between devices, shards(): lax.psum_scatter(jnp.einsum('td,tf->df', attn_input, d_kv, preferred_elem...  710 us
    all_gather x1, waiting for transfers between devices, shards(): lax.all_gather(down_weight, 'fsdp', axis=1, tiled=True)  411 us
    reduce_scatter x1, waiting for transfers between devices, shards(): lax.psum_scatter(d_lower[None].astype(jnp.bfloat16), 'fsdp', scatter_dime...  374 us
    psum x1, waiting for transfers between devices, shards(): lax.psum((d_gain_one, d_gain_two, d_att_router, d_mlp_router, d_att_bias,...  122 us
    all_gather x1, waiting for transfers between devices, shards(): lax.all_gather(out_weight, 'fsdp', axis=1, tiled=True)  94.9 us
    all_gather x1, waiting for transfers between devices, shards(): lax.all_gather(query_weight, 'fsdp', axis=1, tiled=True)  94.5 us
  transfers between devices with their start and end apart: 20, of which 16 were waited for; matrix products, arithmetic and copies ran while one was open for 9% of the time, Pallas kernels for 0%

commit v1 on v0

v1 whole, which is shorter than its diff:
```python
import math

import jax
import jax.numpy as jnp
from jax import lax
from jax.sharding import Mesh, PartitionSpec as P

HEADS = 16
HD = 128
TOP = 2


EPSILON = 1e-06
HIGHEST = lax.Precision.HIGHEST
MASKED = -1e30

GROUP = ("y", "c", "o")
EXPERT = ("y", "c")
ALL = ("y", "c", "o", "i")
OUTER = 4
F32 = jnp.float32
BF16 = jnp.bfloat16


def rope_tables(length):
    half_dim = HD // 2
    frequency = jnp.exp(jnp.arange(half_dim, dtype=F32) * (-2.0 * math.log(10000.0) / HD))
    angles = jnp.arange(length, dtype=F32)[:, None] * frequency[None, :]
    return (jnp.cos(angles), jnp.sin(angles))


def rotate(tensor, cosine, sine_table):
    half_dim = tensor.shape[-1] // 2
    first_half = tensor[..., :half_dim]
    second_half = tensor[..., half_dim:]
    return jnp.concatenate(
        [
            first_half * cosine - second_half * sine_table,
            second_half * cosine + first_half * sine_table,
        ],
        axis=-1,
    )


def rotate_back(tensor, cosine, sine_table):
    return rotate(tensor, cosine, -sine_table)


def norm_rows(stream, gain):
    inverse = lax.rsqrt(jnp.mean(stream * stream, axis=-1, keepdims=True) + EPSILON)
    return (stream * inverse * gain, inverse)


def norm_back(stream, inverse, gain, upstream):
    scaled = upstream * gain
    d_stream = inverse * scaled - stream * inverse**3 * jnp.mean(
        scaled * stream, axis=-1, keepdims=True
    )
    d_gain = jnp.sum(upstream * stream * inverse, axis=0)
    return (d_stream, d_gain)


def shift(value, axis):
    size = lax.axis_size(axis)
    return lax.ppermute(value, axis, [((k + 1) % size, k) for k in range(size)])


def ring_gather(value, axis):
    parts = [value]
    for _ in range(lax.axis_size(axis) - 1):
        parts.append(shift(parts[-1], axis))
    return parts


def ring_scatter(blocks, axis):
    size = lax.axis_size(axis)
    travelling = blocks[1].astype(BF16)
    for j in range(2, size):
        travelling = (shift(travelling, axis).astype(F32) + blocks[j]).astype(BF16)
    return shift(travelling, axis).astype(F32) + blocks[0]


def in_order(parts, axis):
    return jnp.roll(jnp.stack(parts), lax.axis_index(axis), axis=0)


def from_order(stacked, axis):
    return jnp.roll(stacked, -lax.axis_index(axis), axis=0)


def sum_all(value):
    for axis in ALL:
        size = lax.axis_size(axis)
        step = 1
        while step < size:
            value = value + lax.ppermute(value, axis, [(k, k ^ step) for k in range(size)])
            step *= 2
    return value


def pair_gates(normed, router, route, experts):
    logits = jnp.dot(normed.astype(F32), router, precision=HIGHEST)
    onehot = (route[:, :, None] == jnp.arange(experts, dtype=jnp.int32)[None, None, :]).astype(F32)
    picked = jnp.sum(logits[:, None, :] * onehot, axis=-1)
    return (jax.nn.softmax(picked, axis=-1), onehot)


def gates_back(gates, onehot, d_gates, normed, router):
    d_picked = gates * (d_gates - jnp.sum(gates * d_gates, axis=-1, keepdims=True))
    d_logits = jnp.sum(d_picked[:, :, None] * onehot, axis=1)
    d_router = jnp.dot(d_logits.T, normed.astype(F32), precision=HIGHEST)
    d_normed = jnp.dot(d_logits, router.T, precision=HIGHEST)
    return (d_router, d_normed)


def to_experts(gates, onehot, extra):
    by_expert = jnp.sum(gates[:, :, None] * onehot, axis=1).T
    rows = jnp.repeat(by_expert, OUTER, axis=0)[:, None, :]
    if extra is not None:
        rows = jnp.concatenate(
            [rows, jnp.broadcast_to(extra[None, None, :], rows.shape)], axis=1
        )
    return lax.all_to_all(rows, GROUP, split_axis=0, concat_axis=0, tiled=True)


def from_experts(d_gates, onehot, experts):
    rows = lax.all_to_all(d_gates, GROUP, split_axis=0, concat_axis=0, tiled=True)
    by_expert = jnp.sum(rows.reshape(experts, OUTER, -1), axis=1)
    return jnp.einsum("tce,et->tc", onehot, by_expert, precision=HIGHEST)


def meet(rows):
    return lax.all_gather(rows, GROUP, axis=0, tiled=True)


def part(rows):
    return lax.psum_scatter(rows, GROUP, scatter_dimension=0, tiled=True)


def mm(form, first, second):
    return jnp.einsum(form, first, second, preferred_element_type=F32)


def gather_query(weight):
    rows, columns = weight.shape
    mine = lax.all_to_all(
        weight.reshape(rows, OUTER, columns // OUTER), "o", split_axis=1, concat_axis=0
    )
    whole = in_order(ring_gather(mine, "i"), "i")
    return whole.transpose(1, 0, 2, 3).reshape(-1, columns // OUTER)


def scatter_query(grad):
    inner = lax.axis_size("i")
    wide = grad.shape[1]
    blocks = grad.reshape(OUTER, inner, -1, wide).transpose(1, 0, 2, 3)
    mine = ring_scatter(from_order(blocks, "i"), "i").astype(BF16)
    back = lax.all_to_all(mine, "o", split_axis=0, concat_axis=0, tiled=True)
    return back.transpose(1, 0, 2).reshape(back.shape[1], -1).astype(F32)


def gather_kv(weight):
    rows, columns = weight.shape
    wide = columns // (2 * OUTER)
    mine = lax.all_to_all(
        weight.reshape(rows, 2, OUTER, wide), "o", split_axis=2, concat_axis=0
    )
    whole = in_order(ring_gather(mine, "y"), "y")
    whole = in_order(ring_gather(whole, "i"), "i")
    whole = in_order(ring_gather(whole, "c"), "c")
    return whole.transpose(2, 0, 3, 1, 4, 5, 6).reshape(-1, 2 * wide)


def scatter_kv(grad):
    high, inner = lax.axis_size("y"), lax.axis_size("i")
    wide = grad.shape[1]
    blocks = grad.reshape(high, 2, OUTER, inner, -1, wide).transpose(1, 0, 3, 2, 4, 5)
    mine = ring_scatter(from_order(blocks, "c"), "c")
    mine = ring_scatter(from_order(mine, "y"), "y")
    mine = ring_scatter(from_order(mine, "i"), "i").astype(BF16)
    back = lax.all_to_all(mine, "o", split_axis=0, concat_axis=0, tiled=True)
    rows = back.shape[1]
    back = back.reshape(OUTER, rows, 2, wide // 2).transpose(1, 2, 0, 3)
    return back.reshape(rows, -1).astype(F32)


def shards(
    hidden_in,
    segment_ids,
    att_route,
    mlp_route,
    norm_gain1,
    norm_gain2,
    att_router,
    mlp_router,
    kv_weight,
    query_weight,
    out_weight,
    att_bias,
    up_weight,
    down_weight,
    mlp_bias,
    cotangent,
):
    experts = lax.axis_size(EXPERT)
    blocks = lax.axis_size(GROUP)
    inner = lax.axis_size("i")
    tokens, width = hidden_in.shape
    heads = HEADS // OUTER
    span = heads * HD
    score_scale = 1.0 / math.sqrt(HD)
    cosine, sine_table = rope_tables(tokens)
    position = jnp.arange(tokens)

    up_parts = ring_gather(up_weight[0], "i")
    down_parts = ring_gather(down_weight[0], "i")
    query_mat = gather_query(query_weight[0])
    kv_mat = gather_kv(kv_weight)
    slab = jnp.concatenate([query_mat, kv_mat], axis=1)
    out_mat = in_order(ring_gather(out_weight[0], "i"), "i").reshape(span, width)

    residual = hidden_in.astype(F32)
    normed_one, inverse_one = norm_rows(residual, norm_gain1)
    attn_input = normed_one.astype(BF16)
    att_gate, att_onehot = pair_gates(attn_input, att_router, att_route, experts)
    received = to_experts(att_gate, att_onehot, segment_ids[0].astype(F32))
    gate_a = received[:, 0, :]
    segment = received[:, 1, :]
    allowed = (segment[:, :, None] == segment[:, None, :]) & (
        position[None, None, :] <= position[None, :, None]
    )
    all_attn = meet(attn_input)
    cot_low = cotangent.astype(BF16)
    all_cot = meet(cot_low)
    qkv = mm("td,df->tf", all_attn, slab)

    def split_heads(columns):
        return columns.reshape(blocks, tokens, heads, HD).transpose(0, 2, 1, 3)

    queries = rotate(
        split_heads(qkv[:, :span].astype(BF16)).astype(F32), cosine, sine_table
    ).astype(BF16)
    key_rows = rotate(split_heads(qkv[:, span : 2 * span]), cosine, sine_table).astype(BF16)
    value_rows = split_heads(qkv[:, 2 * span :].astype(BF16))

    def probs():
        scores = mm("ghqd,ghkd->ghqk", queries, key_rows) * score_scale
        return jax.nn.softmax(jnp.where(allowed[:, None], scores, MASKED), axis=-1)

    attended = mm("ghqk,ghkd->ghqd", probs().astype(BF16), value_rows)
    gated = (attended * gate_a[:, None, :, None]).astype(BF16)
    gated = gated.transpose(0, 2, 1, 3).reshape(blocks * tokens, span)
    branch = part(mm("tf,fd->td", gated, out_mat).astype(BF16))

    middle = residual + branch.astype(F32) + att_bias
    normed_two, inverse_two = norm_rows(middle, norm_gain2)
    mlp_input = normed_two.astype(BF16)
    mlp_gate, mlp_onehot = pair_gates(mlp_input, mlp_router, mlp_route, experts)
    gate_m = to_experts(mlp_gate, mlp_onehot, None).reshape(-1, 1)
    all_mlp = meet(mlp_input)
    rows_out = None
    rows_back = None
    d_gate_m = None
    grad_up_parts = []
    grad_down_parts = []
    for up, down in zip(up_parts, down_parts):
        units = down.shape[0]
        flat_up = up.reshape(2 * units, width)
        d_units = mm("td,fd->tf", all_cot, down)
        both = mm("td,fd->tf", all_mlp, flat_up)
        gate_in, up_in = both[:, :units], both[:, units:]
        sigma = jax.nn.sigmoid(gate_in)
        hidden_units = gate_in * sigma * up_in
        d_here = jnp.sum(hidden_units * d_units, axis=-1)
        d_gate_m = d_here if d_gate_m is None else d_gate_m + d_here
        gated_units = (hidden_units * gate_m).astype(BF16)
        d_units = d_units * gate_m
        d_both = jnp.concatenate(
            [
                (d_units * up_in * sigma * (1.0 + gate_in * (1.0 - sigma))).astype(BF16),
                (d_units * gate_in * sigma).astype(BF16),
            ],
            axis=1,
        )
        back = mm("tf,fd->td", d_both, flat_up)
        rows_back = back if rows_back is None else rows_back + back
        ahead = mm("tf,fd->td", gated_units, down)
        rows_out = ahead if rows_out is None else rows_out + ahead
        grad_up_parts.append(mm("tf,td->fd", d_both, all_mlp).reshape(2, units, width))
        grad_down_parts.append(mm("tf,td->fd", gated_units, all_cot))
    d_mlp_input = part(rows_back.astype(BF16)).astype(F32)
    d_mlp_gate = from_experts(d_gate_m.reshape(blocks, tokens), mlp_onehot, experts)
    layer_out = middle + part(rows_out.astype(BF16)).astype(F32) + mlp_bias
    d_upper = ring_scatter(grad_up_parts, "i")[None]
    d_lower = ring_scatter(grad_down_parts, "i")[None]
    d_mlp_router, d_mlp_from_router = gates_back(
        mlp_gate, mlp_onehot, d_mlp_gate, mlp_input, mlp_router
    )
    d_norm_two, d_gain_two = norm_back(
        middle, inverse_two, norm_gain2, d_mlp_input + d_mlp_from_router
    )
    d_middle = cotangent + d_norm_two
    summed_one = sum_all(
        jnp.concatenate(
            [
                jnp.stack([d_gain_two, jnp.sum(d_middle, axis=0), jnp.sum(cotangent, axis=0)]),
                d_mlp_router,
            ]
        )
    )

    all_mid = meet(d_middle.astype(BF16))
    d_out = mm("tf,td->fd", gated, all_mid).reshape(inner, -1, width)
    d_output = ring_scatter(from_order(d_out, "i"), "i")[None]
    d_rows = split_heads(mm("td,fd->tf", all_mid, out_mat))
    probs_full = probs()
    gate_b = gate_a[:, None, :, None]
    d_att = (d_rows * gate_b).astype(BF16)
    d_probs = mm("ghqd,ghkd->ghqk", d_rows.astype(BF16), value_rows)
    inner_sum = jnp.sum(probs_full * d_probs, axis=-1, keepdims=True)
    d_scores = (probs_full * (d_probs - inner_sum) * gate_b).astype(BF16)
    d_att_gate = from_experts(jnp.sum(inner_sum[..., 0], axis=1), att_onehot, experts)
    d_queries = mm("ghqk,ghkd->ghqd", d_scores, key_rows) * score_scale
    d_keys = mm("ghqk,ghqd->ghkd", d_scores, queries) * score_scale
    d_values = mm("ghqk,ghqd->ghkd", probs_full.astype(BF16), d_att)

    def join_heads(tensor):
        return tensor.astype(BF16).transpose(0, 2, 1, 3).reshape(blocks * tokens, span)

    d_qkv = jnp.concatenate(
        [
            join_heads(rotate_back(d_queries, cosine, sine_table)),
            join_heads(rotate_back(d_keys, cosine, sine_table)),
            join_heads(d_values),
        ],
        axis=1,
    )
    d_attn_input = part(mm("tf,df->td", d_qkv, slab).astype(BF16)).astype(F32)
    d_slab = mm("td,tf->df", all_attn, d_qkv)
    d_query = scatter_query(d_slab[:, :span])[None]
    d_kv_weight = scatter_kv(d_slab[:, span:])
    d_att_router, d_att_from_router = gates_back(
        att_gate, att_onehot, d_att_gate, attn_input, att_router
    )
    d_norm_one, d_gain_one = norm_back(
        residual, inverse_one, norm_gain1, d_attn_input + d_att_from_router
    )
    d_input = d_middle + d_norm_one
    summed_two = sum_all(jnp.concatenate([d_gain_one[None], d_att_router]))
    return (
        layer_out,
        d_input,
        summed_two[0],
        summed_one[0],
        summed_two[1:].T,
        summed_one[3:].T,
        d_kv_weight,
        d_query,
        d_output,
        summed_one[1],
        d_upper,
        d_lower,
        summed_one[2],
    )


def solution(mesh):
    experts, fsdp = mesh.shape["expert"], mesh.shape["fsdp"]
    fine = Mesh(mesh.devices.reshape(experts // 2, 2, OUTER, fsdp // OUTER), ALL)
    shard = ("o", "i")
    rows = P(ALL, None)
    placed = (
        rows,
        rows,
        rows,
        rows,
        P(),
        P(),
        P(),
        P(),
        rows,
        P(EXPERT, shard, None),
        P(EXPERT, shard, None),
        P(),
        P(EXPERT, None, shard, None),
        P(EXPERT, shard, None),
        P(),
        rows,
    )
    return jax.shard_map(
        shards,
        mesh=fine,
        in_specs=placed,
        out_specs=(
            rows,
            rows,
            P(),
            P(),
            P(),
            P(),
            rows,
            P(EXPERT, shard, None),
            P(EXPERT, shard, None),
            P(),
            P(EXPERT, None, shard, None),
            P(EXPERT, shard, None),
            P(),
        ),
        check_vma=False,
    )
```

time: 4120 us -> 1290 us (0.31)
  waiting for transfers between devices: 3550 us -> 535 us
  matrix products: 264 us -> 404 us
  other arithmetic: 96.7 us -> 160 us
  blocking collectives: 70.6 us -> 9.2 us
    reduce_scatter x5 -> x4, waiting for transfers between devices: 1860 us -> 280 us  [part(): return lax.psum_scatter(rows, GROUP, scatter_dimension=0, tiled=True)]
    all_gather x5 -> x4, waiting for transfers between devices: 1480 us -> 147 us  [meet(): return lax.all_gather(rows, GROUP, axis=0, tiled=True)]
    dot_general x28, matrix products: 256 us -> 397 us  [the longest x24 393 us: mm(): return jnp.einsum(form, first, second, preferred_element_type=F32)]
    psum x1 -> x0, waiting for transfers between devices: 122 us -> none  [shards(): lax.psum((d_gain_one, d_gain_two, d_att_router, d_mlp_router, d_att_bias,...]
    ppermute x0 -> x24, waiting for transfers between devices: none -> 67.4 us  [the longest x14 62.1 us: shift(): return lax.ppermute(value, axis, [((k + 1) % size, k) for k in range(size)])]
    all_to_all x3 -> x1, blocking collectives: 70.6 us -> 9.2 us  [to_experts(): return lax.all_to_all(rows, GROUP, split_axis=0, concat_axis=0, tiled=True)]
  transfers between devices with their start and end apart: 20 -> 39, of which waited for: 16 -> 20; matrix products, arithmetic and copies ran while one was open for 9% -> 39% of each run, Pallas kernels for 0% -> 0%
where the time goes in v1:
time: 1290 us; the launch traced here: 1280 us
  waiting for transfers between devices  535 us (41%)
  matrix products  404 us (31%)
  other arithmetic  160 us (12%)
  local copies, waits for them, and re-layouts  103 us (8%)
  starting transfers between devices  57.8 us (4%)
  between operations  15.5 us (1%)
    dot_general x24, matrix products, mm(): return jnp.einsum(form, first, second, preferred_element_type=F32)  393 us
    reduce_scatter x4, waiting for transfers between devices, part(): return lax.psum_scatter(rows, GROUP, scatter_dimension=0, tiled=True)  280 us
    all_gather x4, waiting for transfers between devices, meet(): return lax.all_gather(rows, GROUP, axis=0, tiled=True)  147 us
    ppermute x14, waiting for transfers between devices, shift(): return lax.ppermute(value, axis, [((k + 1) % size, k) for k in range(size)])  62.1 us
    unnamed x163, local copies, waits for them, and re-layouts  26.1 us
  transfers between devices with their start and end apart: 39, of which 20 were waited for; matrix products, arithmetic and copies ran while one was open for 39% of the time, Pallas kernels for 0%

profile of v1, /device:TPU:0, one launch (start us, length us, event | category | flops | bytes accessed | tf_op | source)
XLA Modules:
  0.0 1284.4 jit_solution(6147287791731070335)
XLA Ops:
  14.3 6.4 all-to-all-start.2
  22.4 25.1 %all-to-all-done.2 = bf16[1,64,2,4,512]{4,2,1,0,3:T(2,128)(2,1)S(1)} async-done(((bf16[1,64,2,4,512]{4,2,1,0,3:T(2,128)(2,1)}), bf16[1,64,2,4,512]{4,2,1,0,3:T(2,128)(2,1)S(1)}, u32[]{:S(2)}, u32[]{:S(2)}) %all-to-all-start.2) | async-done | bytes 524320 | tf_op jit(solution)/shard_map/all_to_all | solution.py:165
  48.9 7.8 collective-permute-done.1
  56.7 5.4 fusion.71
  70.5 4.6 fusion.168
  75.1 4.8 all-to-all-start.1
  80.1 8.3 collective-permute-done.2
  88.3 9.9 fusion.32
  99.3 4.4 collective-permute-done.4
  103.7 4.6 fusion.39
  108.4 8.6 all-to-all-done.1
  120.6 9.1 fusion.167
  129.7 13.9 %collective-permute-done = bf16[4,256,512]{2,1,0:T(8,128)(2,1)S(1)} collective-permute-done((bf16[4,256,512]{2,1,0:T(8,128)(2,1)}, bf16[4,256,512]{2,1,0:T(8,128)(2,1)S(1)}, u32[]{:S(2)}, u32[]{:S(2)}) %collective-permute-start) | collective-permute-done | bytes 1048608 | tf_op jit(solution)/shard_map/ppermute | solution.py:65
  145.1 20.3 %fusion.12 = bf16[2,2,4,2,64,2,512]{6,5,4,2,0,3,1:T(2,128)(2,1)S(1)} fusion(s32[]{:T(128)S(6)} %select_n.97, bf16[1,2,2,4,64,2,512]{6,5,4,3,2,1,0:T(2,128)(2,1)} %bitcast.30, bf16[1,2,2,4,64,2,512]{6,5,4,3,2,1,0:T(2,128)(2,1)S(1)} %fusion.167), kind=kLoop, calls=%fused_computation.77 | loop fusion | flops 6291456 | bytes 8388612 | tf_op jit(solution)/shard_map/transpose | solution.py:171
  165.4 5.5 copy.200
  170.9 5.4 copy.246
  176.3 18.7 %fusion.123 = (bf16[2048,1536]{1,0:T(8,128)(2,1)S(1)}, f32[2048,1536]{1,0:T(8,128)}) fusion(bf16[2048,2048]{1,0:T(8,128)(2,1)} %all-gather.5.cloned.1.call-done, bf16[2048,1024]{1,0:T(8,128)(2,1)} %bitcast.260, bf16[2048,512]{1,0:T(8,128)(2,1)S(1)} %bitcast.266), kind=kOutput, calls=%fused_computation.248 | convolution fusion | flops 12900630528 | bytes 33554432 | tf_op jit(solution)/shard_map/td,df->tf/dot_general | solution.py:141
  197.8 5.2 reshape.368
  203.0 4.6 slice.151
  207.6 5.2 reshape.353
  214.9 4.7 copy_bitcast_fusion
  238.8 9.5 convolution_convert_fusion.2
  248.4 103.4 %reduce-scatter.5.cloned.1.call-done = bf16[128,2048]{1,0:T(8,128)(2,1)} async-done(((bf16[2048,2048]{1,0:T(8,128)(2,1)}), bf16[128,2048]{1,0:T(8,128)(2,1)}) %reduce-scatter.5.cloned.1.call-update) | async-done | bytes 524304 | tf_op jit(solution)/shard_map/reduce_scatter | solution.py:137
  361.6 69.6 %all-gather.7.cloned.1.call-done = bf16[2048,2048]{1,0:T(8,128)(2,1)} async-done(((bf16[128,2048]{1,0:T(8,128)(2,1)}), bf16[2048,2048]{1,0:T(8,128)(2,1)}) %all-gather.7.cloned.1.call-update) | async-done | bytes 8388624 | tf_op jit(solution)/shard_map/all_gather | solution.py:133
  431.1 18.9 %fusion.126 = f32[2048,1408]{0,1:T(8,128)} fusion(bf16[2048,2048]{1,0:T(8,128)(2,1)} %all-gather.7.cloned.1.call-done, bf16[1408,2048]{1,0:T(8,128)(2,1)} %bitcast.307), kind=kOutput, calls=%fused_computation.251 | convolution fusion | flops 11811160064 | bytes 25690112 | tf_op jit(solution)/shard_map/td,fd->tf/dot_general | solution.py:141
  450.0 56.9 %all-gather.9.cloned.1.call-done = bf16[2048,2048]{1,0:T(8,128)(2,1)} async-done(((bf16[128,2048]{1,0:T(8,128)(2,1)}), bf16[2048,2048]{1,0:T(8,128)(2,1)}) %all-gather.9.cloned.1.call-update) | async-done | bytes 8388624 | tf_op jit(solution)/shard_map/all_gather | solution.py:133
  507.0 16.1 %multiply_reduce_fusion.1 = (f32[2048]{0:T(1024)S(1)}, f32[2048,704]{0,1:T(8,128)}, f32[2048,704]{0,1:T(8,128)}) fusion(f32[2048,1408]{0,1:T(8,128)} %fusion.126, bf16[2048,2048]{1,0:T(8,128)(2,1)} %all-gather.9.cloned.1.call-done, bf16[1,704,2048]{2,1,0:T(8,128)(2,1)} %param.29), kind=kOutput, calls=%fused_computation.28 | convolution fusion | flops 5915670528 | bytes 34349056 | tf_op jit(solution)/shard_map/td,fd->tf/dot_general | solution.py:141
  523.1 16.9 %fusion.128 = f32[2048,1408]{0,1:T(8,128)S(1)} fusion(bf16[2048,2048]{1,0:T(8,128)(2,1)} %all-gather.7.cloned.1.call-done, bf16[1408,2048]{1,0:T(8,128)(2,1)} %bitcast.46), kind=kOutput, calls=%fused_computation.253 | convolution fusion | flops 11811160064 | bytes 25690112 | tf_op jit(solution)/shard_map/td,fd->tf/dot_general | solution.py:141
  540.0 6.1 collective-permute-done.6
  546.1 12.8 multiply_reduce_fusion
  559.5 4.6 all-to-all-start.4
  564.3 6.2 all-to-all-done.4
  570.6 9.2 all_to_all.65
  579.8 14.7 %multiply_convert_fusion.1 = (bf16[2048,704]{0,1:T(8,128)(2,1)S(1)}, bf16[2048,704]{0,1:T(8,128)(2,1)}, bf16[2048,704]{0,1:T(8,128)(2,1)S(1)}, bf16[2048,704]{0,1:T(8,128)(2,1)S(1)}) fusion(f32[2048,1408]{0,1:T(8,128)} %copy-done.9, f32[2048,704]{0,1:T(8,128)} %get-tuple-element.67, f32[2048]{0:T(1024)S(1)} %bitcast.278, f32[2048,1408]{0,1:T(8,128)} %fusion.126, ...), kind=kLoop, calls=%fused_computation.30 | loop fusion | flops 40370176 | bytes 46145536 | tf_op jit(solution)/shard_map/convert_element_type | solution.py:280
  594.5 21.1 %fusion.15 = f32[2048,2048]{1,0:T(8,128)} fusion(bf16[1408,2048]{1,0:T(8,128)(2,1)} %bitcast.308, bf16[2048,704]{0,1:T(8,128)(2,1)S(1)} %get-tuple-element.53, bf16[2048,704]{0,1:T(8,128)(2,1)S(1)} %get-tuple-element.54), kind=kOutput, calls=%fused_computation.80 | convolution fusion | flops 11822694400 | bytes 28311552 | tf_op jit(solution)/shard_map/tf,fd->td/dot_general | solution.py:141
  615.6 21.7 %add_convert_fusion = bf16[2048,2048]{1,0:T(8,128)(2,1)} fusion(f32[2048,2048]{1,0:T(8,128)} %fusion.15, bf16[1408,2048]{1,0:T(8,128)(2,1)} %bitcast.46, bf16[2048,704]{0,1:T(8,128)(2,1)} %get-tuple-element.28, bf16[2048,704]{0,1:T(8,128)(2,1)S(1)} %get-tuple-element.27), kind=kOutput, calls=%fused_computation.4 | convolution fusion | flops 11831083008 | bytes 36700160 | tf_op jit(solution)/shard_map/tf,fd->td/dot_general | solution.py:141
  639.1 14.1 %fusion.68 = f32[2048,2048]{1,0:T(8,128)} fusion(f32[2048,704]{0,1:T(8,128)} %get-tuple-element.26, f32[2048]{0:T(1024)S(1)} %bitcast.279, bf16[1,704,2048]{2,1,0:T(8,128)(2,1)S(1)} %copy-done.71), kind=kOutput, calls=%fused_computation.152 | convolution fusion | flops 5908463616 | bytes 25436160 | tf_op jit(solution)/shard_map/tf,fd->td/dot_general | solution.py:141
  653.2 14.9 %add_convert_fusion.1 = bf16[2048,2048]{1,0:T(8,128)(2,1)} fusion(f32[2048,2048]{1,0:T(8,128)} %fusion.68, bf16[704,2048]{1,0:T(8,128)(2,1)} %collective-permute-done.6, f32[2048,704]{0,1:T(8,128)} %get-tuple-element.24, f32[2048]{0:T(1024)S(1)} %bitcast.280), kind=kOutput, calls=%fused_computation.5 | convolution fusion | flops 5916852224 | bytes 33824768 | tf_op jit(solution)/shard_map/tf,fd->td/dot_general | solution.py:141
  668.2 71.1 %reduce-scatter.9.cloned.1.call-done = bf16[128,2048]{1,0:T(8,128)(2,1)} async-done(((bf16[2048,2048]{1,0:T(8,128)(2,1)}), bf16[128,2048]{1,0:T(8,128)(2,1)}) %reduce-scatter.9.cloned.1.call-update) | async-done | bytes 524304 | tf_op jit(solution)/shard_map/reduce_scatter | solution.py:137
  742.7 104.9 %reduce-scatter.7.cloned.1.call-done = bf16[128,2048]{1,0:T(8,128)(2,1)} async-done(((bf16[2048,2048]{1,0:T(8,128)(2,1)}), bf16[128,2048]{1,0:T(8,128)(2,1)}) %reduce-scatter.7.cloned.1.call-update) | async-done | bytes 524304 | tf_op jit(solution)/shard_map/reduce_scatter | solution.py:137
  857.1 13.2 %convolution_convert_fusion.3 = bf16[704,2048]{1,0:T(8,128)(2,1)} fusion(bf16[2048,2048]{1,0:T(8,128)(2,1)} %all-gather.9.cloned.1.call-done, f32[2048,704]{0,1:T(8,128)} %get-tuple-element.24, f32[2048]{0:T(1024)S(1)} %bitcast.281), kind=kOutput, calls=%fused_computation.81 | convolution fusion | flops 5909905408 | bytes 17047552 | tf_op jit(solution)/shard_map/tf,td->fd/dot_general | solution.py:141
  871.8 16.2 %convolution_convert_fusion = bf16[1408,2048]{1,0:T(8,128)(2,1)} fusion(bf16[2048,2048]{1,0:T(8,128)(2,1)S(1)} %bitcast.304, bf16[2048,704]{0,1:T(8,128)(2,1)S(1)} %copy-done.33, bf16[2048,704]{0,1:T(8,128)(2,1)S(1)} %copy-done.32), kind=kOutput, calls=%fused_computation.20 | convolution fusion | flops 11825577984 | bytes 19922944 | tf_op jit(solution)/shard_map/tf,td->fd/dot_general | solution.py:141
  890.4 17.2 %fusion.14 = f32[1408,2048]{1,0:T(8,128)} fusion(bf16[2048,2048]{1,0:T(8,128)(2,1)} %all-gather.7.cloned.1.call-done, bf16[2048,704]{0,1:T(8,128)(2,1)S(1)} %copy-done.28, bf16[2048,704]{0,1:T(8,128)(2,1)S(1)} %copy-done.30), kind=kOutput, calls=%fused_computation.79 | convolution fusion | flops 11822694400 | bytes 25690112 | tf_op jit(solution)/shard_map/tf,td->fd/dot_general | solution.py:141
  908.7 20.5 %all-gather.11.cloned.1.call-done = bf16[2048,2048]{1,0:T(8,128)(2,1)} async-done(((bf16[128,2048]{1,0:T(8,128)(2,1)}), bf16[2048,2048]{1,0:T(8,128)(2,1)}) %all-gather.11.cloned.1.call-update) | async-done | bytes 8388624 | tf_op jit(solution)/shard_map/all_gather | solution.py:133
  929.2 7.6 fusion.129
  945.1 51.9 %fusion.24 = f32[16,4,128,128]{3,2,1,0:T(8,128)} fusion(f32[16,4,128,128]{3,2,1,0:T(8,128)} %get-tuple-element.70, f32[16,128]{1,0:T(8,128)S(1)} %bitcast.298, bf16[16,4,128,64]{3,2,1,0:T(8,128)(2,1)} %copy-done.15, bf16[16,4,128,64]{3,2,1,0:T(8,128)(2,1)} %copy-done.16, f32[16,4,128,128]{3,2,1,0:T(8,128)} %copy-done.73, f32[16,4,128]{2,1,0:T(4,128)S(1)} %copy-done.76), kind=kOutput, calls=%fused_computation.95 | convolution fusion | flops 281026688 | bytes 14721024 | tf_op jit(solution)/shard_map/ghqk,ghkd->ghqd/dot_general | solution.py:141
  997.0 52.3 %fusion.27 = f32[16,4,128,128]{3,2,1,0:T(8,128)} fusion(f32[16,4,128,128]{3,2,1,0:T(8,128)} %get-tuple-element.70, f32[16,128]{1,0:T(8,128)S(1)} %bitcast.299, bf16[16,4,128,64]{3,2,1,0:T(8,128)(2,1)} %copy-done.14, bf16[16,4,128,64]{3,2,1,0:T(8,128)(2,1)S(1)} %copy-done.13, f32[16,4,128,128]{3,2,1,0:T(8,128)} %copy-done.73, f32[16,4,128]{2,1,0:T(4,128)S(1)} %copy-done.76), kind=kOutput, calls=%fused_computation.96 | convolution fusion | flops 281026688 | bytes 14721024 | tf_op jit(solution)/shard_map/ghqk,ghqd->ghkd/dot_general | solution.py:141
  1049.3 4.6 copy.215
  1053.9 8.4 subtract_convert_fusion
  1064.7 4.5 copy.213
  1073.3 4.6 copy.210
  1085.1 16.1 %convolution_convert_fusion.1 = bf16[2048,2048]{1,0:T(8,128)(2,1)} fusion(bf16[2048,1536]{0,1:T(8,128)(2,1)S(1)} %bitcast_dynamic-update-slice_fusion, bf16[2048,1024]{1,0:T(8,128)(2,1)S(1)} %bitcast.261, bf16[2048,512]{1,0:T(8,128)(2,1)S(1)} %bitcast.267), kind=kOutput, calls=%fused_computation.21 | convolution fusion | flops 12901679104 | bytes 20971520 | tf_op jit(solution)/shard_map/tf,df->td/dot_general | solution.py:141
  1101.2 13.0 %add_bitcast_fusion.1 = f32[1,704,2048]{2,1,0:T(8,128)} fusion(bf16[704,2048]{1,0:T(8,128)(2,1)} %collective-permute-done.23, bf16[2048,2048]{1,0:T(8,128)(2,1)} %all-gather.9.cloned.1.call-done, f32[2048,704]{0,1:T(8,128)} %get-tuple-element.26, f32[2048]{0:T(1024)S(1)} %bitcast.282), kind=kOutput, calls=%fused_computation.26 | convolution fusion | flops 5911347200 | bytes 22814720 | tf_op jit(solution)/shard_map/tf,td->fd/dot_general | solution.py:141
  1115.7 14.7 %add_bitcast_fusion = f32[1,2,704,2048]{3,2,1,0:T(8,128)} fusion(f32[2,704,2048]{2,1,0:T(8,128)} %bitcast.247, bf16[2,704,2048]{2,1,0:T(8,128)(2,1)} %collective-permute-done.22), kind=kLoop, calls=%fused_computation.6 | loop fusion | flops 5767168 | bytes 28835840 | tf_op jit(solution)/shard_map/broadcast_in_dim | solution.py:294
  1131.0 19.4 %fusion.132 = f32[2048,1536]{1,0:T(8,128)S(1)} fusion(bf16[2048,2048]{1,0:T(8,128)(2,1)} %all-gather.5.cloned.1.call-done, bf16[2048,1536]{0,1:T(8,128)(2,1)} %copy-done.40), kind=kOutput, calls=%fused_computation.257 | convolution fusion | flops 12884901888 | bytes 27262976 | tf_op jit(solution)/shard_map/td,tf->df/dot_general | solution.py:141
  1150.5 4.7 slice.168
  1157.6 9.7 fusion.2
  1182.5 8.0 fusion.3
  1191.5 4.4 fusion.11
  1206.2 4.2 all-to-all-start.7
  1210.4 12.2 collective-permute-done.18
  1231.4 7.4 collective-permute-done.19
  1240.9 4.8 all-to-all-start.6
  1267.4 4.3 collective-permute-done.10
  (327 shorter events, 169.4 us)
Async XLA Ops:
  7.2 352.8 %copy-start = (f32[2048,4]{0,1:T(4,128)S(1)}, f32[2048,4]{0,1:T(4,128)}, u32[]{:S(2)}) copy-start(f32[2048,4]{0,1:T(4,128)} %param.23) | copy-start | bytes 98308
  7.2 41.7 %copy-start.72 = (s32[1,128]{1,0:T(1,128)S(1)}, s32[1,128]{1,0:T(1,128)}, u32[]{:S(2)}) copy-start(s32[1,128]{1,0:T(1,128)} %param.17) | copy-start | bytes 1540
  7.2 169.1 %all-gather.5.cloned.1.call-start = ((), (), s32[]{:S(2)}) async-start(), calls=%async_computation.12 | async-start | bytes 8912896 | tf_op jit(solution)/shard_map/all_gather | solution.py:133
  14.3 54.0 %copy-start.39 = (bf16[1,256,2048]{2,1,0:T(8,128)(2,1)S(1)}, bf16[1,256,2048]{2,1,0:T(8,128)(2,1)}, u32[]{:S(2)}) copy-start(bf16[1,256,2048]{2,1,0:T(8,128)(2,1)} %param.25) | copy-start | bytes 3145732
  14.3 33.2 %all-to-all-start.2 = ((bf16[1,64,2,4,512]{4,2,1,0,3:T(2,128)(2,1)}), bf16[1,64,2,4,512]{4,2,1,0,3:T(2,128)(2,1)S(1)}, u32[]{:S(2)}, u32[]{:S(2)}) async-start(bf16[1,64,2,4,512]{4,2,1,0,3:T(2,128)(2,1)} %copy.199), calls=%async_computation.2 | async-start | bytes 1048576 | tf_op jit(solution)/shard_map/all_to_all | solution.py:165
  22.3 34.3 %copy-start.48 = (f32[128,2]{0,1:T(2,128)}, f32[128,2]{0,1:T(2,128)S(1)}, u32[]{:S(2)}) copy-start(f32[128,2]{0,1:T(2,128)S(1)} %select_reduce_fusion.7) | copy-start | bytes 3076
  22.4 34.3 %copy-start.57 = (f32[128]{0:T(128)}, f32[128]{0:T(128)S(1)}, u32[]{:S(2)}) copy-start(f32[128]{0:T(128)S(1)} %reduce_max.27) | copy-start | bytes 1540
  22.4 34.3 %copy-start.61 = (f32[128]{0:T(128)}, f32[128]{0:T(128)S(1)}, u32[]{:S(2)}) copy-start(f32[128]{0:T(128)S(1)} %fusion.98) | copy-start | bytes 1540
  47.5 9.2 collective-permute-start.1
  62.0 26.3 %collective-permute-start.2 = (bf16[2,4,64,2,512]{4,3,2,1,0:T(2,128)(2,1)}, bf16[2,4,64,2,512]{4,3,2,1,0:T(2,128)(2,1)S(1)}, u32[]{:S(2)}, u32[]{:S(2)}) collective-permute-start(bf16[2,4,64,2,512]{4,3,2,1,0:T(2,128)(2,1)} %fusion.71), channel_id=1, source_target_pairs={{1,0},{0,1},{3,2},{2,3},{5,4},{4,5},{7,6},{6,7},{9,8},{8,9},{11,10... | collective-permute-start | bytes 3145736 | tf_op jit(solution)/shard_map/ppermute | solution.py:65
  64.0 11.0 all-to-all-start
  67.5 36.2 %collective-permute-start.4 = (bf16[256,2048]{1,0:T(8,128)(2,1)}, bf16[256,2048]{1,0:T(8,128)(2,1)}, u32[]{:S(2)}, u32[]{:S(2)}) collective-permute-start(bf16[256,2048]{1,0:T(8,128)(2,1)} %bitcast.271), channel_id=1, source_target_pairs={{1,0},{0,1},{3,2},{2,3},{5,4},{4,5},{7,6},{6,7},{9,8},{8,9},{11,10... | collective-permute-start | bytes 3145736 | tf_op jit(solution)/shard_map/ppermute | solution.py:65
  70.5 149.1 %copy-start.41 = (f32[128,64]{1,0:T(8,128)}, f32[128,64]{1,0:T(8,128)S(1)}, u32[]{:S(2)}) copy-start(f32[128,64]{1,0:T(8,128)S(1)} %get-tuple-element.59) | copy-start | bytes 98308
  75.1 41.9 %all-to-all-start.1 = ((bf16[1,256,4,512]{1,3,0,2:T(8,128)(2,1)}), bf16[1,256,4,512]{1,3,0,2:T(8,128)(2,1)}, u32[]{:S(2)}, u32[]{:S(2)}) async-start(bf16[1,256,4,512]{1,3,0,2:T(8,128)(2,1)} %bitcast.262), calls=%async_computation.1 | async-start | bytes 2097152 | tf_op jit(solution)/shard_map/all_to_all | solution.py:146
  79.9 272.0 %reduce-scatter.5.cloned.1.call-start = ((), (), s32[]{:S(2)}) async-start(), calls=%async_computation.13 | async-start | bytes 8912896 | tf_op jit(solution)/shard_map/reduce_scatter | solution.py:137
  98.2 46.9 %collective-permute-start.3 = (bf16[2,2,4,64,2,512]{5,4,3,2,1,0:T(2,128)(2,1)}, bf16[2,2,4,64,2,512]{5,4,3,2,1,0:T(2,128)(2,1)}, u32[]{:S(2)}, u32[]{:S(2)}) collective-permute-start(bf16[2,2,4,64,2,512]{5,4,3,2,1,0:T(2,128)(2,1)} %fusion.32), channel_id=1, source_target_pairs={{8,0},{0,8},{9,1},{1,9},{10,2},{2,10},{11,3},{3,11},{12,4},{4,12},... | collective-permute-start | bytes 6291464 | tf_op jit(solution)/shard_map/ppermute | solution.py:65
  98.2 132.1 %copy-start.63 = (f32[16,1,128]{2,1,0:T(1,128)}, f32[16,1,128]{2,1,0:T(1,128)S(1)}, u32[]{:S(2)}) copy-start(f32[16,1,128]{2,1,0:T(1,128)S(1)} %get-tuple-element.52) | copy-start | bytes 24580
  119.3 24.3 %copy-start.24 = (bf16[1,256,4,512]{3,1,2,0:T(8,128)(2,1)S(1)}, bf16[1,256,4,512]{3,1,2,0:T(8,128)(2,1)}, u32[]{:S(2)}) copy-start(bf16[1,256,4,512]{3,1,2,0:T(8,128)(2,1)} %copy.196) | copy-start | bytes 3145732
  119.3 24.3 %collective-permute-start = (bf16[4,256,512]{2,1,0:T(8,128)(2,1)}, bf16[4,256,512]{2,1,0:T(8,128)(2,1)S(1)}, u32[]{:S(2)}, u32[]{:S(2)}) collective-permute-start(bf16[4,256,512]{2,1,0:T(8,128)(2,1)} %bitcast.258), channel_id=1, source_target_pairs={{1,0},{0,1},{3,2},{2,3},{5,4},{4,5},{7,6},{6,7},{9,8},{8,9},{11,10... | collective-permute-start | bytes 3145736 | tf_op jit(solution)/shard_map/ppermute | solution.py:65
  145.1 31.2 %copy-start.34 = (bf16[2,4,256,512]{3,2,0,1:T(8,128)(2,1)}, bf16[2,4,256,512]{3,2,0,1:T(8,128)(2,1)S(1)}, u32[]{:S(2)}) copy-start(bf16[2,4,256,512]{3,2,0,1:T(8,128)(2,1)S(1)} %fusion.42) | copy-start | bytes 6291460
  248.3 103.6 %copy-start.2 = (bf16[128,2048]{1,0:T(8,128)(2,1)S(1)}, bf16[128,2048]{1,0:T(8,128)(2,1)}, u32[]{:S(2)}) copy-start(bf16[128,2048]{1,0:T(8,128)(2,1)} %param.16) | copy-start | bytes 1572868
  248.3 103.6 %copy-start.45 = (f32[2048]{0:T(1024)S(1)}, f32[2048]{0:T(1024)}, u32[]{:S(2)}) copy-start(f32[2048]{0:T(1024)} %param.27) | copy-start | bytes 24580
  248.3 105.9 %copy-start.50 = (f32[2048]{0:T(1024)S(1)}, f32[2048]{0:T(1024)}, u32[]{:S(2)}) copy-start(f32[2048]{0:T(1024)} %param.21) | copy-start | bytes 24580
  248.3 108.1 %copy-start.26 = (f32[128,2048]{1,0:T(8,128)S(1)}, f32[128,2048]{1,0:T(8,128)}, u32[]{:S(2)}) copy-start(f32[128,2048]{1,0:T(8,128)} %param.31) | copy-start | bytes 3145732
  248.3 113.2 %copy-start.59 = (s32[128,2]{0,1:T(2,128)S(1)}, s32[128,2]{0,1:T(2,128)}, u32[]{:S(2)}) copy-start(s32[128,2]{0,1:T(2,128)} %param.19) | copy-start | bytes 3076
  248.3 182.8 %all-gather.7.cloned.1.call-start = ((), (), s32[]{:S(2)}) async-start(), calls=%async_computation.14 | async-start | bytes 8912896 | tf_op jit(solution)/shard_map/all_gather | solution.py:133
  356.3 150.6 %all-gather.9.cloned.1.call-start = ((), (), s32[]{:S(2)}) async-start(), calls=%async_computation.16 | async-start | bytes 8912896 | tf_op jit(solution)/shard_map/all_gather | solution.py:133
  357.9 165.2 %collective-permute-start.5 = (bf16[2,704,2048]{2,1,0:T(8,128)(2,1)}, bf16[2,704,2048]{2,1,0:T(8,128)(2,1)}, u32[]{:S(2)}, u32[]{:S(2)}) collective-permute-start(bf16[2,704,2048]{2,1,0:T(8,128)(2,1)} %bitcast.306), channel_id=1, source_target_pairs={{1,0},{0,1},{3,2},{2,3},{5,4},{4,5},{7,6},{6,7},{9,8},{8,9},{11,10... | collective-permute-start | bytes 17301512 | tf_op jit(solution)/shard_map/ppermute | solution.py:65
  359.4 186.7 %collective-permute-start.6 = (bf16[704,2048]{1,0:T(8,128)(2,1)}, bf16[704,2048]{1,0:T(8,128)(2,1)}, u32[]{:S(2)}, u32[]{:S(2)}) collective-permute-start(bf16[704,2048]{1,0:T(8,128)(2,1)} %bitcast.310), channel_id=1, source_target_pairs={{1,0},{0,1},{3,2},{2,3},{5,4},{4,5},{7,6},{6,7},{9,8},{8,9},{11,10... | collective-permute-start | bytes 8650760 | tf_op jit(solution)/shard_map/ppermute | solution.py:65
  559.5 10.9 all-to-all-start.4
  564.2 175.2 %reduce-scatter.9.cloned.1.call-start = ((), (), s32[]{:S(2)}) async-start(), calls=%async_computation.17 | async-start | bytes 8912896 | tf_op jit(solution)/shard_map/reduce_scatter | solution.py:137
  594.5 21.1 %copy-start.29 = (bf16[2048,704]{0,1:T(8,128)(2,1)}, bf16[2048,704]{0,1:T(8,128)(2,1)S(1)}, u32[]{:S(2)}) copy-start(bf16[2048,704]{0,1:T(8,128)(2,1)S(1)} %get-tuple-element.54) | copy-start | bytes 8650756
  637.3 210.4 %reduce-scatter.7.cloned.1.call-start = ((), (), s32[]{:S(2)}) async-start(), calls=%async_computation.15 | async-start | bytes 8912896 | tf_op jit(solution)/shard_map/reduce_scatter | solution.py:137
  668.1 71.3 %copy-start.3 = (bf16[128,2048]{1,0:T(8,128)(2,1)S(1)}, bf16[128,2048]{1,0:T(8,128)(2,1)}, u32[]{:S(2)}) copy-start(bf16[128,2048]{1,0:T(8,128)(2,1)} %param.16) | copy-start | bytes 1572868
  668.1 71.3 %copy-start.23 = (bf16[128,2048]{1,0:T(8,128)(2,1)S(1)}, bf16[128,2048]{1,0:T(8,128)(2,1)}, u32[]{:S(2)}) copy-start(bf16[128,2048]{1,0:T(8,128)(2,1)} %reduce-scatter.5.cloned.1.call-done) | copy-start | bytes 1572868
  668.1 71.3 %copy-start.46 = (f32[2048]{0:T(1024)S(1)}, f32[2048]{0:T(1024)}, u32[]{:S(2)}) copy-start(f32[2048]{0:T(1024)} %param.27) | copy-start | bytes 24580
  668.1 71.2 %copy-start.51 = (f32[2048]{0:T(1024)S(1)}, f32[2048]{0:T(1024)}, u32[]{:S(2)}) copy-start(f32[2048]{0:T(1024)} %param.21) | copy-start | bytes 24580
  668.1 71.2 %copy-start.68 = (f32[128]{0:T(128)S(1)}, f32[128]{0:T(128)}, u32[]{:S(2)}) copy-start(f32[128]{0:T(128)} %copy-done.67) | copy-start | bytes 1540
  668.1 179.6 %copy-start.60 = (f32[2048]{0:T(1024)S(1)}, f32[2048]{0:T(1024)}, u32[]{:S(2)}) copy-start(f32[2048]{0:T(1024)} %param.30) | copy-start | bytes 24580
  668.1 179.5 %copy-start.70 = (f32[128]{0:T(128)S(1)}, f32[128]{0:T(128)}, u32[]{:S(2)}) copy-start(f32[128]{0:T(128)} %get-tuple-element.60) | copy-start | bytes 1540
  668.2 261.0 %all-gather.11.cloned.1.call-start = ((), (), s32[]{:S(2)}) async-start(), calls=%async_computation.18 | async-start | bytes 8912896 | tf_op jit(solution)/shard_map/all_gather | solution.py:133
  853.1 373.1 %reduce-scatter.11.cloned.1.call-start = ((), (), s32[]{:S(2)}) async-start(), calls=%async_computation.19 | async-start | bytes 8912896 | tf_op jit(solution)/shard_map/reduce_scatter | solution.py:137
  855.6 16.1 %collective-permute-start.12 = (f32[7,2048]{1,0:T(8,128)S(1)}, f32[7,2048]{1,0:T(8,128)S(1)}, u32[]{:S(2)}, u32[]{:S(2)}) collective-permute-start(f32[7,2048]{1,0:T(8,128)S(1)} %pad_maximum_fusion.16), channel_id=1, source_target_pairs={{0,16},{16,0},{1,17},{17,1},{2,18},{18,2},{3,19},{19,3},{4,20},{20... | collective-permute-start | bytes 172040 | tf_op jit(solution)/shard_map/ppermute | solution.py:96
  870.3 230.9 %collective-permute-start.23 = (bf16[704,2048]{1,0:T(8,128)(2,1)}, bf16[704,2048]{1,0:T(8,128)(2,1)}, u32[]{:S(2)}, u32[]{:S(2)}) collective-permute-start(bf16[704,2048]{1,0:T(8,128)(2,1)} %convolution_convert_fusion.3), channel_id=1, source_target_pairs={{1,0},{0,1},{3,2},{2,3},{5,4},{4,5},{7,6},{6,7},{9,8},{8,9},{11,10... | collective-permute-start | bytes 8650760 | tf_op jit(solution)/shard_map/ppermute | solution.py:65
  871.7 17.0 %collective-permute-start.13 = (f32[7,2048]{1,0:T(8,128)S(1)}, f32[7,2048]{1,0:T(8,128)S(1)}, u32[]{:S(2)}, u32[]{:S(2)}) collective-permute-start(f32[7,2048]{1,0:T(8,128)S(1)} %fusion.117), channel_id=1, source_target_pairs={{0,8},{8,0},{1,9},{9,1},{2,10},{10,2},{3,11},{11,3},{4,12},{12,4},... | collective-permute-start | bytes 172040 | tf_op jit(solution)/shard_map/ppermute | solution.py:96
  888.0 227.7 %collective-permute-start.22 = (bf16[2,704,2048]{2,1,0:T(8,128)(2,1)}, bf16[2,704,2048]{2,1,0:T(8,128)(2,1)}, u32[]{:S(2)}, u32[]{:S(2)}) collective-permute-start(bf16[2,704,2048]{2,1,0:T(8,128)(2,1)} %bitcast.309), channel_id=1, source_target_pairs={{1,0},{0,1},{3,2},{2,3},{5,4},{4,5},{7,6},{6,7},{9,8},{8,9},{11,10... | collective-permute-start | bytes 17301512 | tf_op jit(solution)/shard_map/ppermute | solution.py:65
  888.7 40.5 %copy-start.36 = (bf16[2,256,2048]{2,1,0:T(8,128)(2,1)S(1)}, bf16[2,256,2048]{2,1,0:T(8,128)(2,1)}, u32[]{:S(2)}) copy-start(bf16[2,256,2048]{2,1,0:T(8,128)(2,1)} %fusion.39) | copy-start | bytes 6291460
  888.7 18.9 %collective-permute-start.14 = (f32[7,2048]{1,0:T(8,128)S(1)}, f32[7,2048]{1,0:T(8,128)S(1)}, u32[]{:S(2)}, u32[]{:S(2)}) collective-permute-start(f32[7,2048]{1,0:T(8,128)S(1)} %add.266), channel_id=1, source_target_pairs={{0,2},{2,0},{4,6},{6,4},{1,3},{3,1},{5,7},{7,5},{8,10},{10,8},{12,... | collective-permute-start | bytes 172040 | tf_op jit(solution)/shard_map/ppermute | solution.py:96
  907.7 206.5 %collective-permute-start.15 = (f32[7,2048]{1,0:T(8,128)S(1)}, f32[7,2048]{1,0:T(8,128)S(1)}, u32[]{:S(2)}, u32[]{:S(2)}) collective-permute-start(f32[7,2048]{1,0:T(8,128)S(1)} %add.267), channel_id=1, source_target_pairs={{0,4},{2,6},{4,0},{6,2},{1,5},{3,7},{5,1},{7,3},{8,12},{10,14},{12... | collective-permute-start | bytes 172040 | tf_op jit(solution)/shard_map/ppermute | solution.py:96
  945.1 51.9 %copy-start.13 = (bf16[16,4,128,64]{3,2,1,0:T(8,128)(2,1)S(1)}, bf16[16,4,128,64]{3,2,1,0:T(8,128)(2,1)}, u32[]{:S(2)}) copy-start(bf16[16,4,128,64]{3,2,1,0:T(8,128)(2,1)} %copy-done.12) | copy-start | bytes 3145732
  1114.2 16.2 %collective-permute-start.16 = (f32[7,2048]{1,0:T(8,128)S(1)}, f32[7,2048]{1,0:T(8,128)S(1)}, u32[]{:S(2)}, u32[]{:S(2)}) collective-permute-start(f32[7,2048]{1,0:T(8,128)S(1)} %add.268), channel_id=1, source_target_pairs={{0,1},{1,0},{2,3},{3,2},{4,5},{5,4},{6,7},{7,6},{8,9},{9,8},{10,11... | collective-permute-start | bytes 172040 | tf_op jit(solution)/shard_map/ppermute | solution.py:96
  1171.2 20.3 %collective-permute-start.17 = (bf16[2,2,4,64,1024]{4,3,1,2,0:T(8,128)(2,1)}, bf16[2,2,4,64,1024]{4,3,1,2,0:T(8,128)(2,1)S(1)}, u32[]{:S(2)}, u32[]{:S(2)}) collective-permute-start(bf16[2,2,4,64,1024]{4,3,1,2,0:T(8,128)(2,1)} %fusion.43), channel_id=1, source_target_pairs={{8,0},{0,8},{9,1},{1,9},{10,2},{2,10},{11,3},{3,11},{12,4},{4,12},... | collective-permute-start | bytes 6291464 | tf_op jit(solution)/shard_map/ppermute | solution.py:65
  1177.4 25.5 %collective-permute-start.20 = (bf16[4,256,512]{2,1,0:T(8,128)(2,1)S(1)}, bf16[4,256,512]{2,1,0:T(8,128)(2,1)}, u32[]{:S(2)}, u32[]{:S(2)}) collective-permute-start(bf16[4,256,512]{2,1,0:T(8,128)(2,1)S(1)} %fusion.74), channel_id=1, source_target_pairs={{1,0},{0,1},{3,2},{2,3},{5,4},{4,5},{7,6},{6,7},{9,8},{8,9},{11,10... | collective-permute-start | bytes 3145736 | tf_op jit(solution)/shard_map/ppermute | solution.py:65
  1178.8 22.1 %all-to-all-start.5 = ((f32[16,1,128]{2,1,0:T(1,128)}), f32[16,1,128]{2,1,0:T(1,128)S(1)}, u32[]{:S(2)}, u32[]{:S(2)}) async-start(f32[16,1,128]{2,1,0:T(1,128)} %bitcast.59), calls=%async_computation.9 | async-start | bytes 16384 | tf_op jit(solution)/shard_map/all_to_all | solution.py:127
  1197.2 25.5 %collective-permute-start.18 = (bf16[2,4,64,1024]{3,2,0,1:T(8,128)(2,1)S(1)}, bf16[2,4,64,1024]{3,2,0,1:T(8,128)(2,1)S(1)}, u32[]{:S(2)}, u32[]{:S(2)}) collective-permute-start(bf16[2,4,64,1024]{3,2,0,1:T(8,128)(2,1)S(1)} %fusion.72), channel_id=1, source_target_pairs={{16,0},{0,16},{17,1},{1,17},{18,2},{2,18},{19,3},{3,19},{20,4},{4,... | collective-permute-start | bytes 3145736 | tf_op jit(solution)/shard_map/ppermute | solution.py:65
  1200.2 45.5 %collective-permute-start.21 = (bf16[256,2048]{1,0:T(8,128)(2,1)}, bf16[256,2048]{1,0:T(8,128)(2,1)}, u32[]{:S(2)}, u32[]{:S(2)}) collective-permute-start(bf16[256,2048]{1,0:T(8,128)(2,1)} %fusion.73), channel_id=1, source_target_pairs={{1,0},{0,1},{3,2},{2,3},{5,4},{4,5},{7,6},{6,7},{9,8},{8,9},{11,10... | collective-permute-start | bytes 3145736 | tf_op jit(solution)/shard_map/ppermute | solution.py:65
  1206.2 34.7 %all-to-all-start.7 = ((bf16[4,256,512]{2,1,0:T(8,128)(2,1)}), bf16[4,256,512]{2,1,0:T(8,128)(2,1)}, u32[]{:S(2)}, u32[]{:S(2)}) async-start(bf16[4,256,512]{2,1,0:T(8,128)(2,1)} %fusion.47), calls=%async_computation.11 | async-start | bytes 2097152 | tf_op jit(solution)/shard_map/all_to_all | solution.py:158
  1225.2 13.6 %collective-permute-start.19 = (bf16[4,64,1024]{2,1,0:T(8,128)(2,1)S(1)}, bf16[4,64,1024]{2,1,0:T(8,128)(2,1)}, u32[]{:S(2)}, u32[]{:S(2)}) collective-permute-start(bf16[4,64,1024]{2,1,0:T(8,128)(2,1)S(1)} %fusion.89), channel_id=1, source_target_pairs={{1,0},{0,1},{3,2},{2,3},{5,4},{4,5},{7,6},{6,7},{9,8},{8,9},{11,10... | collective-permute-start | bytes 1572872 | tf_op jit(solution)/shard_map/ppermute | solution.py:65
  1229.6 11.2 collective-permute-start.7
  1240.8 8.4 collective-permute-start.8
  1240.9 19.9 %all-to-all-start.6 = ((bf16[4,64,1024]{2,1,0:T(8,128)(2,1)}), bf16[4,64,1024]{2,1,0:T(8,128)(2,1)S(1)}, u32[]{:S(2)}, u32[]{:S(2)}) async-start(bf16[4,64,1024]{2,1,0:T(8,128)(2,1)} %fusion.86), calls=%async_computation.10 | async-start | bytes 1048576 | tf_op jit(solution)/shard_map/all_to_all | solution.py:181
  1249.3 17.2 %collective-permute-start.9 = (f32[5,2048]{1,0:T(8,128)S(1)}, f32[5,2048]{1,0:T(8,128)S(1)}, u32[]{:S(2)}, u32[]{:S(2)}) collective-permute-start(f32[5,2048]{1,0:T(8,128)S(1)} %add.261), channel_id=1, source_target_pairs={{0,2},{2,0},{4,6},{6,4},{1,3},{3,1},{5,7},{7,5},{8,10},{10,8},{12,... | collective-permute-start | bytes 122888 | tf_op jit(solution)/shard_map/ppermute | solution.py:96
  1266.5 5.2 collective-permute-start.10
  1271.7 4.3 collective-permute-start.11
  (55 other events, 411.9 us)
Sparse Core Ops, SparseCore 0:
  11.8 102.4 all-gather.4
  248.5 103.3 reduce-scatter.4
  356.4 74.6 all-gather.6
  433.8 73.1 all-gather.8
  637.4 101.8 reduce-scatter.8
  743.3 104.3 reduce-scatter.6
  853.2 75.9 all-gather.10
  1101.3 103.0 reduce-scatter.10

commit v2 on v1

v2 whole, which is shorter than its diff:
```python
import functools
import math

import jax
import jax.numpy as jnp
from jax import lax
from jax.experimental import pallas as pl
from jax.experimental.pallas import tpu as pltpu
from jax.sharding import Mesh, PartitionSpec as P

HEADS = 16
HD = 128
TOP = 2


EPSILON = 1e-06
HIGHEST = lax.Precision.HIGHEST
MASKED = -1e30

GROUP = ("y", "c", "o")
EXPERT = ("y", "c")
ALL = ("y", "c", "o", "i")
OUTER = 4
F32 = jnp.float32
BF16 = jnp.bfloat16


def rope_tables(length):
    half_dim = HD // 2
    frequency = jnp.exp(jnp.arange(half_dim, dtype=F32) * (-2.0 * math.log(10000.0) / HD))
    angles = jnp.arange(length, dtype=F32)[:, None] * frequency[None, :]
    cosine, sine = jnp.cos(angles), jnp.sin(angles)
    return (
        jnp.concatenate([cosine, cosine], axis=1),
        jnp.concatenate([-sine, sine], axis=1),
    )


def norm_rows(stream, gain):
    inverse = lax.rsqrt(jnp.mean(stream * stream, axis=-1, keepdims=True) + EPSILON)
    return (stream * inverse * gain, inverse)


def norm_back(stream, inverse, gain, upstream):
    scaled = upstream * gain
    d_stream = inverse * scaled - stream * inverse**3 * jnp.mean(
        scaled * stream, axis=-1, keepdims=True
    )
    d_gain = jnp.sum(upstream * stream * inverse, axis=0)
    return (d_stream, d_gain)


def shift(value, axis):
    size = lax.axis_size(axis)
    return lax.ppermute(value, axis, [((k + 1) % size, k) for k in range(size)])


def ring_gather(value, axis):
    parts = [value]
    for _ in range(lax.axis_size(axis) - 1):
        parts.append(shift(parts[-1], axis))
    return parts


def ring_scatter(blocks, axis):
    size = lax.axis_size(axis)
    travelling = blocks[1].astype(BF16)
    for j in range(2, size):
        travelling = (shift(travelling, axis).astype(F32) + blocks[j]).astype(BF16)
    return shift(travelling, axis).astype(F32) + blocks[0]


def in_order(parts, axis):
    if len(parts) == 2:
        first = lax.axis_index(axis) == 0
        return jnp.stack([jnp.where(first, *parts), jnp.where(first, *parts[::-1])])
    return jnp.roll(jnp.stack(parts), lax.axis_index(axis), axis=0)


def from_order(parts, axis):
    if len(parts) == 2:
        first = lax.axis_index(axis) == 0
        return [jnp.where(first, *parts), jnp.where(first, *parts[::-1])]
    return list(jnp.roll(jnp.stack(parts), -lax.axis_index(axis), axis=0))


def sum_all(value):
    for axis in ALL:
        size = lax.axis_size(axis)
        step = 1
        while step < size:
            value = value + lax.ppermute(value, axis, [(k, k ^ step) for k in range(size)])
            step *= 2
    return value


def pair_gates(normed, router, route, experts):
    logits = jnp.dot(normed.astype(F32), router, precision=HIGHEST)
    onehot = (route[:, :, None] == jnp.arange(experts, dtype=jnp.int32)[None, None, :]).astype(F32)
    picked = jnp.sum(logits[:, None, :] * onehot, axis=-1)
    return (jax.nn.softmax(picked, axis=-1), onehot)


def gates_back(gates, onehot, d_gates, normed, router):
    d_picked = gates * (d_gates - jnp.sum(gates * d_gates, axis=-1, keepdims=True))
    d_logits = jnp.sum(d_picked[:, :, None] * onehot, axis=1)
    d_router = jnp.dot(d_logits.T, normed.astype(F32), precision=HIGHEST)
    d_normed = jnp.dot(d_logits, router.T, precision=HIGHEST)
    return (d_router, d_normed)


def to_experts(gates, onehot, extra):
    by_expert = jnp.sum(gates[:, :, None] * onehot, axis=1).T
    rows = jnp.repeat(by_expert, OUTER, axis=0)[:, None, :]
    if extra is not None:
        rows = jnp.concatenate(
            [rows, jnp.broadcast_to(extra[None, None, :], rows.shape)], axis=1
        )
    return lax.all_to_all(rows, GROUP, split_axis=0, concat_axis=0, tiled=True)


def from_experts(d_gates, onehot, experts):
    rows = lax.all_to_all(d_gates, GROUP, split_axis=0, concat_axis=0, tiled=True)
    by_expert = jnp.sum(rows.reshape(experts, OUTER, -1), axis=1)
    return jnp.einsum("tce,et->tc", onehot, by_expert, precision=HIGHEST)


def meet(rows):
    return lax.all_gather(rows, GROUP, axis=0, tiled=True)


def part(rows):
    return lax.psum_scatter(rows, GROUP, scatter_dimension=0, tiled=True)


def mm(form, first, second):
    return jnp.einsum(form, first, second, preferred_element_type=F32)


def head_columns(matrix):
    span = HEADS // OUTER * HD
    whole = HEADS * HD
    return [
        jnp.concatenate(
            [
                matrix[:, start + k * span : start + (k + 1) * span]
                for start in range(0, matrix.shape[1], whole)
            ],
            axis=1,
        )
        for k in range(OUTER)
    ]


def gather_rows(weight):
    inner = lax.axis_size("i")
    sent = jnp.stack([block for block in head_columns(weight) for _ in range(inner)])
    here = lax.all_to_all(sent, ("o", "i"), split_axis=0, concat_axis=0, tiled=True)
    return here.reshape(-1, here.shape[2])


def scatter_rows(grad):
    inner = lax.axis_size("i")
    sent = grad.astype(BF16).reshape(OUTER * inner, -1, grad.shape[1])
    here = lax.all_to_all(sent, ("o", "i"), split_axis=0, concat_axis=0, tiled=True)
    total = jnp.sum(here.reshape((OUTER, inner) + here.shape[1:]).astype(F32), axis=1)
    span = HEADS // OUTER * HD
    return jnp.concatenate(
        [
            total[k, :, start : start + span]
            for start in range(0, grad.shape[1], span)
            for k in range(OUTER)
        ],
        axis=1,
    )


def gather_kv(weight):
    here = gather_rows(weight)
    wide = here.shape[1]
    here = in_order(ring_gather(here, "y"), "y")
    whole = in_order(ring_gather(here, "c"), "c")
    return whole.transpose(1, 0, 2, 3).reshape(-1, wide)


def scatter_kv(grad):
    high = lax.axis_size("y")
    blocks = grad.reshape(high, 2, -1, grad.shape[1])
    mine = ring_scatter(from_order([blocks[:, 0], blocks[:, 1]], "c"), "c")
    mine = ring_scatter(from_order([mine[k] for k in range(high)], "y"), "y")
    return scatter_rows(mine)


VMEM = 56 * 1024 * 1024
SEQ_STEP = 4
ROW_STEP = 256


def nn(first, second):
    return jnp.dot(first, second, preferred_element_type=F32)


def nt(first, second):
    return lax.dot_general(first, second, (((1,), (1,)), ((), ())), preferred_element_type=F32)


def tn(first, second):
    return lax.dot_general(first, second, (((0,), (0,)), ((), ())), preferred_element_type=F32)


def as_column(row, rows):
    return jnp.broadcast_to(row, (rows, rows)).T[:, :1]


def turn(head, cosine, sine):
    return head * cosine + pltpu.roll(head, HD // 2, 1) * sine


def turn_back(head, cosine, sine):
    return head * cosine - pltpu.roll(head, HD // 2, 1) * sine


def allowed_keys(segment, length):
    keys = jnp.broadcast_to(segment, (length, length))
    row = lax.broadcasted_iota(jnp.int32, (length, length), 0)
    column = lax.broadcasted_iota(jnp.int32, (length, length), 1)
    return (keys == keys.T) & (column <= row)


def softmax_rows(queries, keys, allowed):
    scores = jnp.where(allowed, nt(queries, keys) * (1.0 / math.sqrt(HD)), MASKED)
    exponent = jnp.exp(scores - jnp.max(scores, axis=-1, keepdims=True))
    return exponent / jnp.sum(exponent, axis=-1, keepdims=True)


def attend_kernel(x_ref, info_ref, cos_ref, sin_ref, slab_ref, out_ref, qkv_ref, gated_ref, part_ref):
    length = cos_ref.shape[0]
    span = out_ref.shape[0]
    raw = nn(x_ref[...], slab_ref[...])
    cosine, sine = cos_ref[...], sin_ref[...]
    for seq in range(info_ref.shape[0]):
        rows = slice(seq * length, (seq + 1) * length)
        gate = as_column(info_ref[seq, 0:1, :], length)
        allowed = allowed_keys(info_ref[seq, 1:2, :], length)
        for start in range(0, span, HD):
            cols = slice(start, start + HD)
            key_cols = slice(span + start, span + start + HD)
            value_cols = slice(2 * span + start, 2 * span + start + HD)
            queries = turn(raw[rows, cols].astype(BF16).astype(F32), cosine, sine).astype(BF16)
            keys = turn(raw[rows, key_cols], cosine, sine).astype(BF16)
            values = raw[rows, value_cols].astype(BF16)
            qkv_ref[rows, cols] = queries
            qkv_ref[rows, key_cols] = keys
            qkv_ref[rows, value_cols] = values
            probs = softmax_rows(queries, keys, allowed)
            gated_ref[rows, cols] = (nn(probs.astype(BF16), values) * gate).astype(BF16)
    part_ref[...] = nn(gated_ref[...], out_ref[...]).astype(BF16)


def attend_back_kernel(
    mid_ref, info_ref, cos_ref, sin_ref, qkv_ref, slab_ref, out_ref, d_qkv_ref, part_ref, d_gate_ref
):
    length = cos_ref.shape[0]
    span = out_ref.shape[0]
    scale = 1.0 / math.sqrt(HD)
    d_rows = nt(mid_ref[...], out_ref[...])
    cosine, sine = cos_ref[...], sin_ref[...]
    for seq in range(info_ref.shape[0]):
        rows = slice(seq * length, (seq + 1) * length)
        gate = as_column(info_ref[seq, 0:1, :], length)
        allowed = allowed_keys(info_ref[seq, 1:2, :], length)
        d_gate = jnp.zeros((length, length), F32)
        for start in range(0, span, HD):
            cols = slice(start, start + HD)
            key_cols = slice(span + start, span + start + HD)
            value_cols = slice(2 * span + start, 2 * span + start + HD)
            queries, keys, values = qkv_ref[rows, cols], qkv_ref[rows, key_cols], qkv_ref[rows, value_cols]
            probs = softmax_rows(queries, keys, allowed)
            d_head = d_rows[rows, cols]
            weighted = probs * nt(d_head.astype(BF16), values)
            d_gate = d_gate + weighted
            d_scores = (
                (weighted - probs * jnp.sum(weighted, axis=-1, keepdims=True)) * gate
            ).astype(BF16)
            d_qkv_ref[rows, cols] = turn_back(nn(d_scores, keys) * scale, cosine, sine).astype(BF16)
            d_qkv_ref[rows, key_cols] = turn_back(
                tn(d_scores, queries) * scale, cosine, sine
            ).astype(BF16)
            d_qkv_ref[rows, value_cols] = tn(
                probs.astype(BF16), (d_head * gate).astype(BF16)
            ).astype(BF16)
        d_gate_ref[seq] = jnp.sum(d_gate.T, axis=0, keepdims=True)
    part_ref[...] = nt(d_qkv_ref[...], slab_ref[...]).astype(BF16)


def fixed(shape):
    return pl.BlockSpec(shape, lambda step: (0,) * len(shape))


def rows_spec(rows, columns):
    return pl.BlockSpec((rows, columns), lambda step: (step, 0))


def info_spec(seqs, kinds, length):
    return pl.BlockSpec((seqs, kinds, length), lambda step: (step, 0, 0))


def shape(dims, dtype=BF16):
    return jax.ShapeDtypeStruct(dims, dtype)


def attend(rows, info, cosine, sine, slab, out_mat):
    count, width = rows.shape
    length = cosine.shape[0]
    step = SEQ_STEP * length
    span = out_mat.shape[0]
    flops = 2 * count * width * 4 * span + 4 * count * length * span
    return pl.pallas_call(
        attend_kernel,
        grid=(count // step,),
        in_specs=[
            rows_spec(step, width),
            info_spec(SEQ_STEP, 2, length),
            fixed(cosine.shape),
            fixed(sine.shape),
            fixed(slab.shape),
            fixed(out_mat.shape),
        ],
        out_specs=[rows_spec(step, 3 * span), rows_spec(step, span), rows_spec(step, width)],
        out_shape=[shape((count, 3 * span)), shape((count, span)), shape((count, width))],
        compiler_params=pltpu.CompilerParams(vmem_limit_bytes=VMEM),
        cost_estimate=pl.CostEstimate(
            flops=flops, bytes_accessed=4 * count * (width + 2 * span), transcendentals=0
        ),
        name="attend",
    )(rows, info, cosine, sine, slab, out_mat)


def attend_back(d_middle, info, cosine, sine, qkv, slab, out_mat):
    count, width = d_middle.shape
    length = cosine.shape[0]
    step = SEQ_STEP * length
    span = out_mat.shape[0]
    flops = 2 * count * width * 4 * span + 10 * count * length * span
    return pl.pallas_call(
        attend_back_kernel,
        grid=(count // step,),
        in_specs=[
            rows_spec(step, width),
            info_spec(SEQ_STEP, 2, length),
            fixed(cosine.shape),
            fixed(sine.shape),
            rows_spec(step, 3 * span),
            fixed(slab.shape),
            fixed(out_mat.shape),
        ],
        out_specs=[rows_spec(step, 3 * span), rows_spec(step, width), info_spec(SEQ_STEP, 1, length)],
        out_shape=[
            shape((count, 3 * span)),
            shape((count, width)),
            shape((count // length, 1, length), F32),
        ],
        compiler_params=pltpu.CompilerParams(vmem_limit_bytes=VMEM),
        cost_estimate=pl.CostEstimate(
            flops=flops, bytes_accessed=4 * count * (width + 3 * span), transcendentals=0
        ),
        name="attend_back",
    )(d_middle, info, cosine, sine, qkv, slab, out_mat)


def units_kernel(parts, x_ref, info_ref, *refs):
    d_units_refs, up_refs = refs[:parts], refs[parts : 2 * parts]
    d_both_refs, gated_refs = refs[2 * parts : 3 * parts], refs[3 * parts : 4 * parts]
    back_ref, d_gate_ref = refs[4 * parts :]
    length = info_ref.shape[2]
    rows = x_ref[...]
    gate = jnp.concatenate(
        [as_column(info_ref[seq], length) for seq in range(info_ref.shape[0])], axis=0
    )
    back = jnp.zeros(back_ref.shape, F32)
    d_gate = jnp.zeros((rows.shape[0], 1), F32)
    for part in range(parts):
        up_ref = up_refs[part]
        units = up_ref.shape[0] // 2
        gate_in = nt(rows, up_ref[:units])
        up_in = nt(rows, up_ref[units:])
        sigma = jax.nn.sigmoid(gate_in)
        active = gate_in * sigma
        hidden_units = active * up_in
        d_units = d_units_refs[part][...].astype(F32)
        d_gate = d_gate + jnp.sum(hidden_units * d_units, axis=-1, keepdims=True)
        gated_refs[part][...] = (hidden_units * gate).astype(BF16)
        d_units = d_units * gate
        d_first = (d_units * up_in * (sigma + active * (1.0 - sigma))).astype(BF16)
        d_second = (d_units * active).astype(BF16)
        d_both_refs[part][:, :units] = d_first
        d_both_refs[part][:, units:] = d_second
        back = back + nn(d_first, up_ref[:units]) + nn(d_second, up_ref[units:])
    back_ref[...] = back.astype(BF16)
    for seq in range(info_ref.shape[0]):
        column = jnp.broadcast_to(d_gate[seq * length : (seq + 1) * length], (length, length))
        d_gate_ref[seq] = column.T[:1]


def run_units(rows, info, d_units, up_parts):
    count, width = rows.shape
    length = info.shape[2]
    parts = len(up_parts)
    units = d_units[0].shape[1]
    seqs = ROW_STEP // length
    return pl.pallas_call(
        functools.partial(units_kernel, parts),
        grid=(count // ROW_STEP,),
        in_specs=[rows_spec(ROW_STEP, width), info_spec(seqs, 1, length)]
        + [rows_spec(ROW_STEP, units)] * parts
        + [fixed(up.shape) for up in up_parts],
        out_specs=[rows_spec(ROW_STEP, 2 * units)] * parts
        + [rows_spec(ROW_STEP, units)] * parts
        + [rows_spec(ROW_STEP, width), info_spec(seqs, 1, length)],
        out_shape=[shape((count, 2 * units))] * parts
        + [shape((count, units))] * parts
        + [shape((count, width)), shape((count // length, 1, length), F32)],
        compiler_params=pltpu.CompilerParams(vmem_limit_bytes=VMEM),
        cost_estimate=pl.CostEstimate(
            flops=8 * count * width * units * parts,
            bytes_accessed=4 * count * (width + 2 * units * parts),
            transcendentals=0,
        ),
        name="units",
    )(rows, info, *d_units, *up_parts)


def shards(
    hidden_in,
    segment_ids,
    att_route,
    mlp_route,
    norm_gain1,
    norm_gain2,
    att_router,
    mlp_router,
    kv_weight,
    query_weight,
    out_weight,
    att_bias,
    up_weight,
    down_weight,
    mlp_bias,
    cotangent,
):
    experts = lax.axis_size(EXPERT)
    inner = lax.axis_size("i")
    tokens, width = hidden_in.shape
    span = HEADS // OUTER * HD
    cosine, sine_table = rope_tables(tokens)

    kv_mat = gather_kv(kv_weight)
    query_mat = gather_rows(query_weight[0])
    slab = jnp.concatenate([query_mat, kv_mat], axis=1)
    out_mat = in_order(ring_gather(out_weight[0], "i"), "i").reshape(span, width)
    down_parts = ring_gather(down_weight[0], "i")
    up_parts = ring_gather(up_weight[0].reshape(-1, width), "i")

    residual = hidden_in.astype(F32)
    normed_one, inverse_one = norm_rows(residual, norm_gain1)
    attn_input = normed_one.astype(BF16)
    att_gate, att_onehot = pair_gates(attn_input, att_router, att_route, experts)
    info = to_experts(att_gate, att_onehot, segment_ids[0].astype(F32))
    all_attn = meet(attn_input)
    cot_low, all_attn_seen = lax.optimization_barrier((cotangent.astype(BF16), all_attn[:8, :128]))
    all_cot = meet(cot_low)
    qkv, gated, branch = attend(all_attn, info, cosine, sine_table, slab, out_mat)
    branch, all_cot = lax.optimization_barrier((branch, all_cot))
    branch = part(branch)

    middle = residual + branch.astype(F32) + att_bias
    normed_two, inverse_two = norm_rows(middle, norm_gain2)
    mlp_input = normed_two.astype(BF16)
    mlp_gate, mlp_onehot = pair_gates(mlp_input, mlp_router, mlp_route, experts)
    gate_m = to_experts(mlp_gate, mlp_onehot, None)
    all_mlp = meet(mlp_input)
    d_units = [mm("td,fd->tf", all_cot, down).astype(BF16) for down in down_parts]
    found = run_units(all_mlp, gate_m, d_units, up_parts)
    d_both, gated_units = found[:inner], found[inner : 2 * inner]
    rows_back, d_gate_m = found[2 * inner :]
    d_mlp_input = part(rows_back)
    gated_units, d_both, d_mlp_input = lax.optimization_barrier((gated_units, d_both, d_mlp_input))
    d_mlp_input = d_mlp_input.astype(F32)
    d_mlp_gate = from_experts(d_gate_m[:, 0], mlp_onehot, experts)
    d_mlp_router, d_mlp_from_router = gates_back(
        mlp_gate, mlp_onehot, d_mlp_gate, mlp_input, mlp_router
    )
    d_norm_two, d_gain_two = norm_back(
        middle, inverse_two, norm_gain2, d_mlp_input + d_mlp_from_router
    )
    d_middle = cotangent + d_norm_two
    summed_one = sum_all(
        jnp.concatenate(
            [
                jnp.stack([d_gain_two, jnp.sum(d_middle, axis=0), jnp.sum(cotangent, axis=0)]),
                d_mlp_router,
            ]
        )
    )

    all_mid = meet(d_middle.astype(BF16))
    d_qkv, rows_one, d_gate_a = attend_back(
        all_mid, info, cosine, sine_table, qkv, slab, out_mat
    )
    d_attn_input = part(rows_one).astype(F32)
    d_att_gate = from_experts(d_gate_a[:, 0], att_onehot, experts)
    rows_out = None
    for units_here, down in zip(gated_units, down_parts):
        ahead = mm("tf,fd->td", units_here, down)
        rows_out = ahead if rows_out is None else rows_out + ahead
    layer_out = middle + part(rows_out.astype(BF16)).astype(F32) + mlp_bias
    d_upper = ring_scatter([mm("tf,td->fd", d_here, all_mlp) for d_here in d_both], "i")
    d_upper = d_upper.reshape(up_weight.shape)
    d_lower = ring_scatter([mm("tf,td->fd", here, all_cot) for here in gated_units], "i")[None]
    d_out = mm("tf,td->fd", gated, all_mid).reshape(inner, -1, width)
    d_output = ring_scatter(from_order([d_out[k] for k in range(inner)], "i"), "i")[None]
    d_slab = mm("td,tf->df", all_attn, d_qkv)
    d_query = scatter_rows(d_slab[:, :span])[None]
    d_kv_weight = scatter_kv(d_slab[:, span:])
    d_att_router, d_att_from_router = gates_back(
        att_gate, att_onehot, d_att_gate, attn_input, att_router
    )
    d_norm_one, d_gain_one = norm_back(
        residual, inverse_one, norm_gain1, d_attn_input + d_att_from_router
    )
    d_input = d_middle + d_norm_one
    summed_two = sum_all(jnp.concatenate([d_gain_one[None], d_att_router]))
    return (
        layer_out,
        d_input,
        summed_two[0],
        summed_one[0],
        summed_two[1:].T,
        summed_one[3:].T,
        d_kv_weight,
        d_query,
        d_output,
        summed_one[1],
        d_upper,
        d_lower,
        summed_one[2],
    )


def solution(mesh):
    experts, fsdp = mesh.shape["expert"], mesh.shape["fsdp"]
    fine = Mesh(mesh.devices.reshape(experts // 2, 2, OUTER, fsdp // OUTER), ALL)
    shard = ("o", "i")
    rows = P(ALL, None)
    placed = (
        rows,
        rows,
        rows,
        rows,
        P(),
        P(),
        P(),
        P(),
        rows,
        P(EXPERT, shard, None),
        P(EXPERT, shard, None),
        P(),
        P(EXPERT, None, shard, None),
        P(EXPERT, shard, None),
        P(),
        rows,
    )
    return jax.shard_map(
        shards,
        mesh=fine,
        in_specs=placed,
        out_specs=(
            rows,
            rows,
            P(),
            P(),
            P(),
            P(),
            rows,
            P(EXPERT, shard, None),
            P(EXPERT, shard, None),
            P(),
            P(EXPERT, None, shard, None),
            P(EXPERT, shard, None),
            P(),
        ),
        check_vma=False,
    )
```

time: 1290 us -> 1210 us (0.938)
  matrix products: 404 us -> 137 us
  waiting for transfers between devices: 535 us -> 721 us
  Pallas kernels: 0 us -> 166 us
  other arithmetic: 160 us -> 64.1 us
  local copies, waits for them, and re-layouts: 103 us -> 36.3 us
    dot_general x24 -> x10, matrix products: 393 us -> 130 us  [mm(): return jnp.einsum(form, first, second, preferred_element_type=F32)]
    ppermute x14 -> x10, waiting for transfers between devices: 62.1 us -> 289 us  [shift(): return lax.ppermute(value, axis, [((k + 1) % size, k) for k in range(size)])]
    pallas_call x0 -> x3, Pallas kernels: none -> 166 us  [the longest x1 64.3 us: run_units(): pl.pallas_call(functools.partial(units_kernel, parts), grid=(count // ROW...]
    all_gather x4, waiting for transfers between devices: 147 us -> 17.3 us  [meet(): return lax.all_gather(rows, GROUP, axis=0, tiled=True)]
    all_to_all x4, waiting for transfers between devices: 35.2 us -> 96 us  [the longest x2 56.9 us: gather_rows(): lax.all_to_all(sent, ('o', 'i'), split_axis=0, concat_axis=0, tiled=True)]
    concatenate x9 -> x2, other arithmetic: 34.7 us -> 7.04 us  [the longest x1 6.28 us: shards(): slab = jnp.concatenate([query_mat, kv_mat], axis=1)]
    transpose x3 -> x0, other arithmetic: 26.9 us -> none  [the longest x1 20.3 us: gather_kv(): return whole.transpose(2, 0, 3, 1, 4, 5, 6).reshape(-1, 2 * wide)]
    reduce_scatter x4, waiting for transfers between devices: 280 us -> 302 us  [part(): return lax.psum_scatter(rows, GROUP, scatter_dimension=0, tiled=True)]
  transfers between devices with their start and end apart: 39 -> 35, of which waited for: 20 -> 21; matrix products, arithmetic and copies ran while one was open for 39% -> 16% of each run, Pallas kernels for 0% -> 8%
where the time goes in v2:
time: 1210 us; the launch traced here: 1200 us
  waiting for transfers between devices  721 us (60%)
  Pallas kernels  166 us (14%)
  matrix products  137 us (11%)
  other arithmetic  64.1 us (5%)
  starting transfers between devices  53.5 us (4%)
  local copies, waits for them, and re-layouts  36.3 us (3%)
  between operations  15.3 us (1%)
    reduce_scatter x4, waiting for transfers between devices, part(): return lax.psum_scatter(rows, GROUP, scatter_dimension=0, tiled=True)  302 us
    ppermute x10, waiting for transfers between devices, shift(): return lax.ppermute(value, axis, [((k + 1) % size, k) for k in range(size)])  289 us
    dot_general x10, matrix products, mm(): return jnp.einsum(form, first, second, preferred_element_type=F32)  130 us
    pallas_call x1, Pallas kernels, run_units(): pl.pallas_call(functools.partial(units_kernel, parts), grid=(count // ROW...  64.3 us
    all_to_all x2, waiting for transfers between devices, gather_rows(): lax.all_to_all(sent, ('o', 'i'), split_axis=0, concat_axis=0, tiled=True)  56.9 us
    pallas_call x1, Pallas kernels, attend_back(): pl.pallas_call(attend_back_kernel, grid=(count // step,), in_specs=[rows_...  56.6 us
    pallas_call x1, Pallas kernels, attend(): pl.pallas_call(attend_kernel, grid=(count // step,), in_specs=[rows_spec(...  44.9 us
    all_to_all x2, waiting for transfers between devices, scatter_rows(): lax.all_to_all(sent, ('o', 'i'), split_axis=0, concat_axis=0, tiled=True)  39.1 us
  transfers between devices with their start and end apart: 35, of which 21 were waited for; matrix products, arithmetic and copies ran while one was open for 16% of the time, Pallas kernels for 8%

profile of v2, /device:TPU:0, one launch (start us, length us, event | category | flops | bytes accessed | tf_op | source)
XLA Modules:
  0.0 1203.6 jit_solution(9843988952509289664)
XLA Ops:
  9.6 2.0 fusion.6
  11.7 3.0 fusion.53
  20.1 7.3 all-to-all-start.2
  31.0 35.0 %all-to-all-done.2 = bf16[8,64,1024]{2,1,0:T(8,128)(2,1)S(1)} async-done(((bf16[8,64,1024]{2,1,0:T(8,128)(2,1)}), bf16[8,64,1024]{2,1,0:T(8,128)(2,1)S(1)}, u32[]{:S(2)}, u32[]{:S(2)}) %all-to-all-start.2) | async-done | bytes 1048608 | tf_op jit(solution)/shard_map/all_to_all | solution.py:158
  69.6 4.4 all-to-all-start.1
  73.9 1.9 collective-permute-start.2
  76.3 36.4 %collective-permute-done = bf16[512,1024]{1,0:T(8,128)(2,1)} collective-permute-done((bf16[512,1024]{1,0:T(8,128)(2,1)S(1)}, bf16[512,1024]{1,0:T(8,128)(2,1)}, u32[]{:S(2)}, u32[]{:S(2)}) %collective-permute-start) | collective-permute-done | bytes 1048608 | tf_op jit(solution)/shard_map/ppermute | solution.py:55
  112.8 1.9 select_bitcast_fusion.5
  118.1 1.7 select_bitcast_fusion.3
  121.2 1.9 select_bitcast_fusion.1
  123.1 2.4 pad_maximum_fusion.1
  125.5 21.9 %all-to-all-done.1 = bf16[8,256,512]{2,1,0:T(8,128)(2,1)} async-done(((bf16[8,256,512]{2,1,0:T(8,128)(2,1)}), bf16[8,256,512]{2,1,0:T(8,128)(2,1)}, u32[]{:S(2)}, u32[]{:S(2)}) %all-to-all-start.1) | async-done | bytes 2097184 | tf_op jit(solution)/shard_map/all_to_all | solution.py:158
  147.4 3.7 all-to-all-start
  151.2 6.3 pad_maximum_fusion.slab_ref
  158.3 44.9 %attend.1 = (bf16[2048,1536]{1,0:T(8,128)(2,1)}, bf16[2048,512]{1,0:T(8,128)(2,1)}, bf16[2048,2048]{1,0:T(8,128)(2,1)}) custom-call(bf16[2048,2048]{1,0:T(8,128)(2,1)} %all-gather.5.cloned.1.call-done.x_ref, f32[16,2,128]{2,1,0:T(2,128)} %copy-done.21, f32[128,128]{1,0:T(8,128)} %get-tuple-element.90.cos_ref, f32[128,128]{1,0:T(8,128)} %get-tuple-element.91.sin_ref, ...), custom_call_target="tpu_custom_call" | custom-call | flops 17716740096 | bytes 25165824 | tf_op jit(solution)/shard_map/attend/pallas_call | solution.py:318
  203.2 17.2 %all-gather.7.cloned.1.call-done = bf16[2048,2048]{1,0:T(8,128)(2,1)} async-done(((bf16[128,2048]{1,0:T(8,128)(2,1)}), bf16[2048,2048]{1,0:T(8,128)(2,1)}) %all-gather.7.cloned.1.call-update) | async-done | bytes 8388624 | tf_op jit(solution)/shard_map/all_gather | solution.py:129
  220.7 107.2 %reduce-scatter.5.cloned.1.call-done = bf16[128,2048]{1,0:T(8,128)(2,1)} async-done(((bf16[2048,2048]{1,0:T(8,128)(2,1)}), bf16[128,2048]{1,0:T(8,128)(2,1)}) %reduce-scatter.5.cloned.1.call-update) | async-done | bytes 524304 | tf_op jit(solution)/shard_map/reduce_scatter | solution.py:133
  329.3 2.1 multiply_convert_fusion
  333.5 10.6 convolution_convert_fusion.3
  345.3 4.5 all-to-all-start.3
  349.8 169.8 %collective-permute-done.3 = bf16[704,2048]{1,0:T(8,128)(2,1)} collective-permute-done((bf16[704,2048]{1,0:T(8,128)(2,1)}, bf16[704,2048]{1,0:T(8,128)(2,1)}, u32[]{:S(2)}, u32[]{:S(2)}) %collective-permute-start.3) | collective-permute-done | bytes 2883616 | tf_op jit(solution)/shard_map/ppermute | solution.py:55
  519.6 10.5 convolution_convert_fusion.2
  530.2 4.6 copy.49.refs_1_
  534.8 4.6 copy.48.refs_0_
  540.0 64.3 %units.1 = (bf16[2048,1408]{1,0:T(8,128)(2,1)}, bf16[2048,1408]{1,0:T(8,128)(2,1)}, bf16[2048,704]{1,0:T(8,128)(2,1)}, bf16[2048,704]{1,0:T(8,128)(2,1)}, bf16[2...) custom-call(bf16[2048,2048]{1,0:T(8,128)(2,1)} %all-gather.9.cloned.1.call-done.x_ref, f32[16,1,128]{2,1,0:T(1,128)} %copy-done.29, ...), custom_call_target="tpu_custom_call" | custom-call | flops 47244640256 | bytes 39845888 | tf_op jit(solution)/shard_map/units/pallas_call | solution.py:411
  604.8 104.2 %reduce-scatter.7.cloned.1.call-done = bf16[128,2048]{1,0:T(8,128)(2,1)} async-done(((bf16[2048,2048]{1,0:T(8,128)(2,1)}), bf16[128,2048]{1,0:T(8,128)(2,1)}) %reduce-scatter.7.cloned.1.call-update) | async-done | bytes 524304 | tf_op jit(solution)/shard_map/reduce_scatter | solution.py:133
  709.0 12.6 %fusion.48 = f32[2048,2048]{1,0:T(8,128)} fusion(bf16[2048,704]{1,0:T(8,128)(2,1)} %get-tuple-element.40, bf16[1,704,2048]{2,1,0:T(8,128)(2,1)} %param.29), kind=kOutput, calls=%fused_computation.141 | convolution fusion | flops 5905580032 | bytes 22544384 | tf_op jit(solution)/shard_map/tf,fd->td/dot_general | solution.py:137
  721.6 13.2 %add_convert_fusion = bf16[2048,2048]{1,0:T(8,128)(2,1)} fusion(f32[2048,2048]{1,0:T(8,128)} %fusion.48, bf16[2048,704]{1,0:T(8,128)(2,1)S(1)} %copy-done.38, bf16[704,2048]{1,0:T(8,128)(2,1)} %collective-permute-done.3), kind=kOutput, calls=%fused_computation | convolution fusion | flops 5913968640 | bytes 30932992 | tf_op jit(solution)/shard_map/tf,fd->td/dot_general | solution.py:137
  735.5 10.6 all_to_all.42
  746.2 2.3 multiply_reduce_fusion
  748.6 90.9 %reduce-scatter.9.cloned.1.call-done = bf16[128,2048]{1,0:T(8,128)(2,1)} async-done(((bf16[2048,2048]{1,0:T(8,128)(2,1)}), bf16[128,2048]{1,0:T(8,128)(2,1)}) %reduce-scatter.9.cloned.1.call-update) | async-done | bytes 524304 | tf_op jit(solution)/shard_map/reduce_scatter | solution.py:133
  839.5 3.2 fusion.52
  845.7 10.3 convolution_convert_fusion.1
  856.0 1.5 collective-permute-start.19
  858.9 1.8 collective-permute-start.12
  860.7 17.4 %convolution_convert_fusion = bf16[1408,2048]{1,0:T(8,128)(2,1)} fusion(bf16[2048,1408]{1,0:T(8,128)(2,1)} %get-tuple-element.49, bf16[2048,2048]{1,0:T(8,128)(2,1)S(1)} %bitcast.257), kind=kOutput, calls=%fused_computation.2 | convolution fusion | flops 11814043648 | bytes 19922944 | tf_op jit(solution)/shard_map/tf,td->fd/dot_general | solution.py:137
  879.4 42.0 %collective-permute-done.19 = bf16[704,2048]{1,0:T(8,128)(2,1)S(1)} collective-permute-done((bf16[704,2048]{1,0:T(8,128)(2,1)S(1)}, bf16[704,2048]{1,0:T(8,128)(2,1)S(1)}, u32[]{:S(2)}, u32[]{:S(2)}) %collective-permute-start.19) | collective-permute-done | bytes 2883616 | tf_op jit(solution)/shard_map/ppermute | solution.py:55
  921.5 10.0 add_bitcast_fusion
  933.0 56.6 %attend_back.1 = (bf16[2048,1536]{1,0:T(8,128)(2,1)}, bf16[2048,2048]{1,0:T(8,128)(2,1)}, f32[16,1,128]{2,1,0:T(1,128)}) custom-call(bf16[2048,2048]{1,0:T(8,128)(2,1)} %all-gather.11.cloned.1.call-done.mid_ref, f32[16,2,128]{2,1,0:T(2,128)} %copy-done.21, f32[128,128]{1,0:T(8,128)} %get-tuple-element.90.cos_ref, f32[128,128]{1,0:T(8,128)} %get-tuple-element.91.sin_ref, ...), custom_call_target="tpu_custom_call" | custom-call | flops 18522046464 | bytes 29360128 | tf_op jit(solution)/shard_map/attend_back/pallas_call | solution.py:345
  989.7 19.0 %fusion.60 = f32[2048,1536]{1,0:T(8,128)} fusion(bf16[2048,2048]{1,0:T(8,128)(2,1)} %all-gather.5.cloned.1.call-done.x_ref, bf16[2048,1536]{1,0:T(8,128)(2,1)} %get-tuple-element.47), kind=kOutput, calls=%fused_computation.153 | convolution fusion | flops 12884901888 | bytes 27262976 | tf_op jit(solution)/shard_map/td,tf->df/dot_general | solution.py:137
  1008.6 4.5 slice.164
  1013.2 1.9 fusion.1
  1015.1 29.2 %collective-permute-done.18 = bf16[1408,2048]{1,0:T(8,128)(2,1)} collective-permute-done((bf16[1408,2048]{1,0:T(8,128)(2,1)}, bf16[1408,2048]{1,0:T(8,128)(2,1)}, u32[]{:S(2)}, u32[]{:S(2)}) %collective-permute-start.18) | collective-permute-done | bytes 5767200 | tf_op jit(solution)/shard_map/ppermute | solution.py:55
  1044.3 20.0 %convert_add_fusion = f32[1408,2048]{1,0:T(8,128)} fusion(bf16[1408,2048]{1,0:T(8,128)(2,1)} %collective-permute-done.18, bf16[2048,1408]{1,0:T(8,128)(2,1)} %get-tuple-element.50, bf16[2048,2048]{1,0:T(8,128)(2,1)} %all-gather.9.cloned.1.call-done.x_ref), kind=kOutput, calls=%fused_computation.1 | convolution fusion | flops 11816927232 | bytes 31457280 | tf_op jit(solution)/shard_map/tf,td->fd/dot_general | solution.py:137
  1064.3 3.9 all-to-all-start.5
  1068.8 3.8 slice.257
  1072.6 1.9 all-to-all-done.5
  1074.5 4.3 all-to-all-start.7
  1079.5 5.7 bitcast_add_fusion
  1088.4 6.9 fusion.61
  1097.7 1.9 collective-permute-start.17
  1099.6 11.9 collective-permute-done.16
  1111.5 3.8 fusion.2
  1115.3 21.7 %all-to-all-done.7 = bf16[8,256,512]{2,1,0:T(8,128)(2,1)} async-done(((bf16[8,256,512]{2,1,0:T(8,128)(2,1)}), bf16[8,256,512]{2,1,0:T(8,128)(2,1)}, u32[]{:S(2)}, u32[]{:S(2)}) %all-to-all-start.7) | async-done | bytes 2097184 | tf_op jit(solution)/shard_map/all_to_all | solution.py:165
  1137.1 4.5 all-to-all-start.6
  1142.0 4.5 add_bitcast_fusion.1
  1146.5 2.2 convert_reduce_fusion
  1150.4 17.3 %all-to-all-done.6 = bf16[8,64,1024]{2,1,0:T(8,128)(2,1)} async-done(((bf16[8,64,1024]{2,1,0:T(8,128)(2,1)}), bf16[8,64,1024]{2,1,0:T(8,128)(2,1)}, u32[]{:S(2)}, u32[]{:S(2)}) %all-to-all-start.6) | async-done | bytes 1048608 | tf_op jit(solution)/shard_map/all_to_all | solution.py:165
  1167.7 1.5 convert_reduce_fusion.1
  1172.6 2.4 fusion.13
  1175.1 1.6 collective-permute-start.5
  1177.3 2.1 collective-permute-done.5
  1181.5 3.6 collective-permute-done.7
  1185.7 5.0 collective-permute-done.8
  (224 shorter events, 56.2 us)
Async XLA Ops:
  7.2 336.8 %copy-start = (f32[2048,4]{0,1:T(4,128)S(1)}, f32[2048,4]{0,1:T(4,128)}, u32[]{:S(2)}) copy-start(f32[2048,4]{0,1:T(4,128)} %param.23) | copy-start | bytes 98308
  7.2 7.5 copy-start.12
  7.2 150.5 %all-gather.5.cloned.1.call-start = ((), (), s32[]{:S(2)}) async-start(), calls=%async_computation.12 | async-start | bytes 8912896 | tf_op jit(solution)/shard_map/all_gather | solution.py:129
  11.6 208.8 %all-gather.7.cloned.1.call-start = ((), (), s32[]{:S(2)}) async-start(), calls=%async_computation.13 | async-start | bytes 8912896 | tf_op jit(solution)/shard_map/all_gather | solution.py:129
  14.7 12.7 %copy-start.10 = (bf16[1,256,2048]{2,1,0:T(8,128)(2,1)S(1)}, bf16[1,256,2048]{2,1,0:T(8,128)(2,1)}, u32[]{:S(2)}) copy-start(bf16[1,256,2048]{2,1,0:T(8,128)(2,1)} %param.25) | copy-start | bytes 3145732
  20.1 45.8 %all-to-all-start.2 = ((bf16[8,64,1024]{2,1,0:T(8,128)(2,1)}), bf16[8,64,1024]{2,1,0:T(8,128)(2,1)S(1)}, u32[]{:S(2)}, u32[]{:S(2)}) async-start(bf16[8,64,1024]{2,1,0:T(8,128)(2,1)} %fusion.31), calls=%async_computation.2 | async-start | bytes 2097152 | tf_op jit(solution)/shard_map/all_to_all | solution.py:158
  30.2 45.6 %copy-start.6 = (bf16[128,2048]{1,0:T(8,128)(2,1)S(1)}, bf16[128,2048]{1,0:T(8,128)(2,1)}, u32[]{:S(2)}) copy-start(bf16[128,2048]{1,0:T(8,128)(2,1)} %fusion.6) | copy-start | bytes 1572868
  30.2 45.6 %copy-start.19 = (f32[2048,4]{0,1:T(4,128)S(1)}, f32[2048,4]{0,1:T(4,128)}, u32[]{:S(2)}) copy-start(f32[2048,4]{0,1:T(4,128)} %param.22) | copy-start | bytes 98308
  65.9 10.4 copy-start.11
  65.9 46.8 %collective-permute-start = (bf16[512,1024]{1,0:T(8,128)(2,1)S(1)}, bf16[512,1024]{1,0:T(8,128)(2,1)}, u32[]{:S(2)}, u32[]{:S(2)}) collective-permute-start(bf16[512,1024]{1,0:T(8,128)(2,1)S(1)} %bitcast.232), channel_id=1, source_target_pairs={{16,0},{0,16},{17,1},{1,17},{18,2},{2,18},{19,3},{3,19},{20,4},{4,... | collective-permute-start | bytes 3145736 | tf_op jit(solution)/shard_map/ppermute | solution.py:55
  69.6 77.9 %all-to-all-start.1 = ((bf16[8,256,512]{2,1,0:T(8,128)(2,1)}), bf16[8,256,512]{2,1,0:T(8,128)(2,1)}, u32[]{:S(2)}, u32[]{:S(2)}) async-start(bf16[8,256,512]{2,1,0:T(8,128)(2,1)} %fusion.21), calls=%async_computation.1 | async-start | bytes 4194304 | tf_op jit(solution)/shard_map/all_to_all | solution.py:158
  73.9 44.1 %collective-permute-start.2 = (bf16[256,2048]{1,0:T(8,128)(2,1)}, bf16[256,2048]{1,0:T(8,128)(2,1)}, u32[]{:S(2)}, u32[]{:S(2)}) collective-permute-start(bf16[256,2048]{1,0:T(8,128)(2,1)} %bitcast.25), channel_id=1, source_target_pairs={{1,0},{0,1},{3,2},{2,3},{5,4},{4,5},{7,6},{6,7},{9,8},{8,9},{11,10... | collective-permute-start | bytes 3145736 | tf_op jit(solution)/shard_map/ppermute | solution.py:55
  116.2 5.0 collective-permute-start.1
  116.3 5.0 copy-start.15
  116.3 5.0 copy-start.25
  147.4 10.2 all-to-all-start
  151.1 176.8 %reduce-scatter.5.cloned.1.call-start = ((), (), s32[]{:S(2)}) async-start(), calls=%async_computation.14 | async-start | bytes 8912896 | tf_op jit(solution)/shard_map/reduce_scatter | solution.py:133
  220.4 107.5 %copy-start.4 = (bf16[128,2048]{1,0:T(8,128)(2,1)S(1)}, bf16[128,2048]{1,0:T(8,128)(2,1)}, u32[]{:S(2)}) copy-start(bf16[128,2048]{1,0:T(8,128)(2,1)} %param.16) | copy-start | bytes 1572868
  220.4 107.5 %copy-start.13 = (f32[2048]{0:T(1024)S(1)}, f32[2048]{0:T(1024)}, u32[]{:S(2)}) copy-start(f32[2048]{0:T(1024)} %param.27) | copy-start | bytes 24580
  220.4 108.9 %copy-start.17 = (f32[2048]{0:T(1024)S(1)}, f32[2048]{0:T(1024)}, u32[]{:S(2)}) copy-start(f32[2048]{0:T(1024)} %param.21) | copy-start | bytes 24580
  220.4 319.0 %all-gather.9.cloned.1.call-start = ((), (), s32[]{:S(2)}) async-start(), calls=%async_computation.15 | async-start | bytes 8912896 | tf_op jit(solution)/shard_map/all_gather | solution.py:129
  331.4 208.0 %collective-permute-start.4 = (bf16[1408,2048]{1,0:T(8,128)(2,1)}, bf16[1408,2048]{1,0:T(8,128)(2,1)}, u32[]{:S(2)}, u32[]{:S(2)}) collective-permute-start(bf16[1408,2048]{1,0:T(8,128)(2,1)} %bitcast.258), channel_id=1, source_target_pairs={{1,0},{0,1},{3,2},{2,3},{5,4},{4,5},{7,6},{6,7},{9,8},{8,9},{11,10... | collective-permute-start | bytes 17301512 | tf_op jit(solution)/shard_map/ppermute | solution.py:55
  332.9 11.1 copy-start.8
  332.9 11.6 copy-start.22
  332.9 186.7 %collective-permute-start.3 = (bf16[704,2048]{1,0:T(8,128)(2,1)}, bf16[704,2048]{1,0:T(8,128)(2,1)}, u32[]{:S(2)}, u32[]{:S(2)}) collective-permute-start(bf16[704,2048]{1,0:T(8,128)(2,1)} %bitcast.260), channel_id=1, source_target_pairs={{1,0},{0,1},{3,2},{2,3},{5,4},{4,5},{7,6},{6,7},{9,8},{8,9},{11,10... | collective-permute-start | bytes 8650760 | tf_op jit(solution)/shard_map/ppermute | solution.py:55
  345.3 194.1 %all-to-all-start.3 = ((f32[16,1,128]{2,1,0:T(1,128)}), f32[16,1,128]{2,1,0:T(1,128)S(1)}, u32[]{:S(2)}, u32[]{:S(2)}) async-start(f32[16,1,128]{2,1,0:T(1,128)} %bitcast.30), calls=%async_computation.4 | async-start | bytes 16384 | tf_op jit(solution)/shard_map/all_to_all | solution.py:119
  349.8 359.2 %reduce-scatter.7.cloned.1.call-start = ((), (), s32[]{:S(2)}) async-start(), calls=%async_computation.16 | async-start | bytes 8912896 | tf_op jit(solution)/shard_map/reduce_scatter | solution.py:133
  604.3 235.1 %reduce-scatter.9.cloned.1.call-start = ((), (), s32[]{:S(2)}) async-start(), calls=%async_computation.17 | async-start | bytes 8912896 | tf_op jit(solution)/shard_map/reduce_scatter | solution.py:133
  709.0 12.6 %copy-start.38 = (bf16[2048,704]{1,0:T(8,128)(2,1)S(1)}, bf16[2048,704]{1,0:T(8,128)(2,1)}, u32[]{:S(2)}) copy-start(bf16[2048,704]{1,0:T(8,128)(2,1)} %get-tuple-element.41) | copy-start | bytes 8650756
  734.8 11.4 copy-start.9
  734.8 11.4 copy-start.35
  734.8 104.7 %copy-start.27 = (f32[2048]{0:T(1024)S(1)}, f32[2048]{0:T(1024)}, u32[]{:S(2)}) copy-start(f32[2048]{0:T(1024)} %param.30) | copy-start | bytes 24580
  734.8 198.2 %all-gather.11.cloned.1.call-start = ((), (), s32[]{:S(2)}) async-start(), calls=%async_computation.18 | async-start | bytes 8912896 | tf_op jit(solution)/shard_map/all_gather | solution.py:129
  843.6 329.0 %reduce-scatter.11.cloned.1.call-start = ((), (), s32[]{:S(2)}) async-start(), calls=%async_computation.19 | async-start | bytes 8912896 | tf_op jit(solution)/shard_map/reduce_scatter | solution.py:133
  844.1 16.6 %slice-start.2 = ((s8[8388608]{0:T(1024)(128)(4,1)}), s8[4194304]{0:T(1024)(128)(4,1)S(1)}, s32[]{:S(2)}) async-start(s8[8388608]{0:T(1024)(128)(4,1)} %bitcast.256), calls=%async_computation.22 | async-start | bytes 8388608
  844.1 16.5 %slice-start.3 = ((s8[8388608]{0:T(1024)(128)(4,1)}), s8[4194304]{0:T(1024)(128)(4,1)S(1)}, s32[]{:S(2)}) async-start(s8[8388608]{0:T(1024)(128)(4,1)} %bitcast.256), calls=%async_computation.23 | async-start | bytes 8388608
  844.2 13.3 %collective-permute-start.10 = (f32[7,2048]{1,0:T(8,128)S(1)}, f32[7,2048]{1,0:T(8,128)S(1)}, u32[]{:S(2)}, u32[]{:S(2)}) collective-permute-start(f32[7,2048]{1,0:T(8,128)S(1)} %pad_maximum_fusion.7), channel_id=1, source_target_pairs={{0,16},{16,0},{1,17},{17,1},{2,18},{18,2},{3,19},{19,3},{4,20},{20... | collective-permute-start | bytes 172040 | tf_op jit(solution)/shard_map/ppermute | solution.py:92
  856.0 65.5 %collective-permute-start.19 = (bf16[704,2048]{1,0:T(8,128)(2,1)S(1)}, bf16[704,2048]{1,0:T(8,128)(2,1)S(1)}, u32[]{:S(2)}, u32[]{:S(2)}) collective-permute-start(bf16[704,2048]{1,0:T(8,128)(2,1)S(1)} %convolution_convert_fusion.1), channel_id=1, source_target_pairs={{1,0},{0,1},{3,2},{2,3},{5,4},{4,5},{7,6},{6,7},{9,8},{8,9},{11,10... | collective-permute-start | bytes 8650760 | tf_op jit(solution)/shard_map/ppermute | solution.py:55
  857.5 1.3 collective-permute-start.11
  858.9 62.6 %slice-start = ((s8[8388608]{0:T(1024)(128)(4,1)}), s8[4194304]{0:T(1024)(128)(4,1)S(1)}, s32[]{:S(2)}) async-start(s8[8388608]{0:T(1024)(128)(4,1)} %bitcast.254), calls=%async_computation.20 | async-start | bytes 8388608
  858.9 62.6 %slice-start.1 = ((s8[8388608]{0:T(1024)(128)(4,1)}), s8[4194304]{0:T(1024)(128)(4,1)S(1)}, s32[]{:S(2)}) async-start(s8[8388608]{0:T(1024)(128)(4,1)} %bitcast.254), calls=%async_computation.21 | async-start | bytes 8388608
  858.9 19.8 %collective-permute-start.12 = (f32[7,2048]{1,0:T(8,128)S(1)}, f32[7,2048]{1,0:T(8,128)S(1)}, u32[]{:S(2)}, u32[]{:S(2)}) collective-permute-start(f32[7,2048]{1,0:T(8,128)S(1)} %add.131), channel_id=1, source_target_pairs={{0,2},{2,0},{4,6},{6,4},{1,3},{3,1},{5,7},{7,5},{8,10},{10,8},{12,... | collective-permute-start | bytes 172040 | tf_op jit(solution)/shard_map/ppermute | solution.py:92
  878.1 166.2 %collective-permute-start.18 = (bf16[1408,2048]{1,0:T(8,128)(2,1)}, bf16[1408,2048]{1,0:T(8,128)(2,1)}, u32[]{:S(2)}, u32[]{:S(2)}) collective-permute-start(bf16[1408,2048]{1,0:T(8,128)(2,1)} %convolution_convert_fusion), channel_id=1, source_target_pairs={{1,0},{0,1},{3,2},{2,3},{5,4},{4,5},{7,6},{6,7},{9,8},{8,9},{11,10... | collective-permute-start | bytes 17301512 | tf_op jit(solution)/shard_map/ppermute | solution.py:55
  878.7 52.8 %collective-permute-start.13 = (f32[7,2048]{1,0:T(8,128)S(1)}, f32[7,2048]{1,0:T(8,128)S(1)}, u32[]{:S(2)}, u32[]{:S(2)}) collective-permute-start(f32[7,2048]{1,0:T(8,128)S(1)} %add.132), channel_id=1, source_target_pairs={{0,4},{2,6},{4,0},{6,2},{1,5},{3,7},{5,1},{7,3},{8,12},{10,14},{12... | collective-permute-start | bytes 172040 | tf_op jit(solution)/shard_map/ppermute | solution.py:92
  931.5 132.8 %collective-permute-start.14 = (f32[7,2048]{1,0:T(8,128)S(1)}, f32[7,2048]{1,0:T(8,128)S(1)}, u32[]{:S(2)}, u32[]{:S(2)}) collective-permute-start(f32[7,2048]{1,0:T(8,128)S(1)} %add.133), channel_id=1, source_target_pairs={{0,1},{1,0},{2,3},{3,2},{4,5},{5,4},{6,7},{7,6},{8,9},{9,8},{10,11... | collective-permute-start | bytes 172040 | tf_op jit(solution)/shard_map/ppermute | solution.py:92
  1013.2 51.1 %copy-start.2 = (f32[2048,1024]{1,0:T(8,128)}, f32[2048,1024]{1,0:T(8,128)S(1)}, u32[]{:S(2)}) copy-start(f32[2048,1024]{1,0:T(8,128)S(1)} %slice.164) | copy-start | bytes 25165828
  1015.1 64.4 %collective-permute-start.15 = (bf16[2,512,1024]{2,1,0:T(8,128)(2,1)}, bf16[2,512,1024]{2,1,0:T(8,128)(2,1)}, u32[]{:S(2)}, u32[]{:S(2)}) collective-permute-start(bf16[2,512,1024]{2,1,0:T(8,128)(2,1)} %fusion.1), channel_id=1, source_target_pairs={{8,0},{0,8},{9,1},{1,9},{10,2},{2,10},{11,3},{3,11},{12,4},{4,12},... | collective-permute-start | bytes 6291464 | tf_op jit(solution)/shard_map/ppermute | solution.py:55
  1064.3 10.2 all-to-all-start.5
  1074.5 62.6 %all-to-all-start.7 = ((bf16[8,256,512]{2,1,0:T(8,128)(2,1)}), bf16[8,256,512]{2,1,0:T(8,128)(2,1)}, u32[]{:S(2)}, u32[]{:S(2)}) async-start(bf16[8,256,512]{2,1,0:T(8,128)(2,1)} %bitcast.223), calls=%async_computation.11 | async-start | bytes 4194304 | tf_op jit(solution)/shard_map/all_to_all | solution.py:165
  1085.2 10.1 copy-start.3
  1086.4 25.1 %collective-permute-start.16 = (bf16[512,1024]{1,0:T(8,128)(2,1)}, bf16[512,1024]{1,0:T(8,128)(2,1)S(1)}, u32[]{:S(2)}, u32[]{:S(2)}) collective-permute-start(bf16[512,1024]{1,0:T(8,128)(2,1)} %fusion.3), channel_id=1, source_target_pairs={{16,0},{0,16},{17,1},{1,17},{18,2},{2,18},{19,3},{3,19},{20,4},{4,... | collective-permute-start | bytes 3145736 | tf_op jit(solution)/shard_map/ppermute | solution.py:55
  1097.7 44.3 %collective-permute-start.17 = (bf16[256,2048]{1,0:T(8,128)(2,1)}, bf16[256,2048]{1,0:T(8,128)(2,1)}, u32[]{:S(2)}, u32[]{:S(2)}) collective-permute-start(bf16[256,2048]{1,0:T(8,128)(2,1)} %select_convert_fusion), channel_id=1, source_target_pairs={{1,0},{0,1},{3,2},{2,3},{5,4},{4,5},{7,6},{6,7},{9,8},{8,9},{11,10... | collective-permute-start | bytes 3145736 | tf_op jit(solution)/shard_map/ppermute | solution.py:55
  1099.6 42.0 %copy-start.7 = (bf16[128,2048]{1,0:T(8,128)(2,1)S(1)}, bf16[128,2048]{1,0:T(8,128)(2,1)}, u32[]{:S(2)}) copy-start(bf16[128,2048]{1,0:T(8,128)(2,1)} %fusion.6) | copy-start | bytes 1572868
  1137.1 30.7 %all-to-all-start.6 = ((bf16[8,64,1024]{2,1,0:T(8,128)(2,1)}), bf16[8,64,1024]{2,1,0:T(8,128)(2,1)}, u32[]{:S(2)}, u32[]{:S(2)}) async-start(bf16[8,64,1024]{2,1,0:T(8,128)(2,1)} %bitcast.51), calls=%async_computation.10 | async-start | bytes 2097152 | tf_op jit(solution)/shard_map/all_to_all | solution.py:165
  1148.9 23.8 %copy-start.18 = (f32[2048]{0:T(1024)S(1)}, f32[2048]{0:T(1024)}, u32[]{:S(2)}) copy-start(f32[2048]{0:T(1024)} %param.20) | copy-start | bytes 24580
  1148.9 23.7 %copy-start.20 = (f32[2048,4]{0,1:T(4,128)S(1)}, f32[2048,4]{0,1:T(4,128)}, u32[]{:S(2)}) copy-start(f32[2048,4]{0,1:T(4,128)} %param.22) | copy-start | bytes 98308
  1148.9 23.7 %copy-start.33 = (f32[128]{0:T(128)S(1)}, f32[128]{0:T(128)}, u32[]{:S(2)}) copy-start(f32[128]{0:T(128)} %copy-done.32) | copy-start | bytes 1540
  1150.4 41.8 %copy-start.34 = (f32[128]{0:T(128)S(1)}, f32[128]{0:T(128)}, u32[]{:S(2)}) copy-start(f32[128]{0:T(128)} %get-tuple-element.81) | copy-start | bytes 1540
  1172.6 23.6 %copy-start.1 = (f32[2048,4]{0,1:T(4,128)S(1)}, f32[2048,4]{0,1:T(4,128)}, u32[]{:S(2)}) copy-start(f32[2048,4]{0,1:T(4,128)} %param.23) | copy-start | bytes 98308
  1175.1 4.3 collective-permute-start.5
  1179.4 1.3 collective-permute-start.6
  1180.8 4.3 collective-permute-start.7
  1185.1 5.5 collective-permute-start.8
  1190.7 4.3 collective-permute-start.9
  (14 other events, 37.6 us)
Sparse Core Ops, SparseCore 0:
  11.7 133.4 all-gather.4
  148.0 72.3 all-gather.6
  225.0 102.8 reduce-scatter.4
  331.5 74.7 all-gather.8
  604.4 104.4 reduce-scatter.6
  734.9 104.4 reduce-scatter.8
  843.7 76.1 all-gather.10
  989.8 110.0 reduce-scatter.10

commit v3 on v2

v3 whole, which is shorter than its diff:
```python
import functools
import math

import jax
import jax.numpy as jnp
from jax import lax
from jax.experimental import pallas as pl
from jax.experimental.pallas import tpu as pltpu
from jax.sharding import Mesh, PartitionSpec as P

HEADS = 16
HD = 128
TOP = 2


EPSILON = 1e-06
HIGHEST = lax.Precision.HIGHEST
MASKED = -1e30

GROUP = ("y", "c", "o")
EXPERT = ("y", "c")
ALL = ("y", "c", "o", "i")
OUTER = 4
F32 = jnp.float32
BF16 = jnp.bfloat16


def rope_tables(length):
    half_dim = HD // 2
    frequency = jnp.exp(jnp.arange(half_dim, dtype=F32) * (-2.0 * math.log(10000.0) / HD))
    angles = jnp.arange(length, dtype=F32)[:, None] * frequency[None, :]
    cosine, sine = jnp.cos(angles), jnp.sin(angles)
    return (
        jnp.concatenate([cosine, cosine], axis=1),
        jnp.concatenate([-sine, sine], axis=1),
    )


def norm_rows(stream, gain):
    inverse = lax.rsqrt(jnp.mean(stream * stream, axis=-1, keepdims=True) + EPSILON)
    return (stream * inverse * gain, inverse)


def norm_back(stream, inverse, gain, upstream):
    scaled = upstream * gain
    d_stream = inverse * scaled - stream * inverse**3 * jnp.mean(
        scaled * stream, axis=-1, keepdims=True
    )
    d_gain = jnp.sum(upstream * stream * inverse, axis=0)
    return (d_stream, d_gain)


def shift(value, axis):
    size = lax.axis_size(axis)
    return lax.ppermute(value, axis, [((k + 1) % size, k) for k in range(size)])


def ring_gather(value, axis):
    parts = [value]
    for _ in range(lax.axis_size(axis) - 1):
        parts.append(shift(parts[-1], axis))
    return parts


def ring_scatter(blocks, axis):
    size = lax.axis_size(axis)
    travelling = blocks[1].astype(BF16)
    for j in range(2, size):
        travelling = (shift(travelling, axis).astype(F32) + blocks[j]).astype(BF16)
    return shift(travelling, axis).astype(F32) + blocks[0]


def in_order(parts, axis, place=0):
    if len(parts) == 2:
        first = lax.axis_index(axis) == 0
        return jnp.stack([jnp.where(first, *parts), jnp.where(first, *parts[::-1])], axis=place)
    return jnp.roll(jnp.stack(parts, axis=place), lax.axis_index(axis), axis=place)


def from_order(parts, axis):
    if len(parts) == 2:
        first = lax.axis_index(axis) == 0
        return [jnp.where(first, *parts), jnp.where(first, *parts[::-1])]
    return list(jnp.roll(jnp.stack(parts), -lax.axis_index(axis), axis=0))


def sum_all(value):
    for axis in ALL:
        size = lax.axis_size(axis)
        step = 1
        while step < size:
            value = value + lax.ppermute(value, axis, [(k, k ^ step) for k in range(size)])
            step *= 2
    return value


def pair_gates(normed, router, route, experts):
    logits = jnp.dot(normed.astype(F32), router, precision=HIGHEST)
    onehot = (route[:, :, None] == jnp.arange(experts, dtype=jnp.int32)[None, None, :]).astype(F32)
    picked = jnp.sum(logits[:, None, :] * onehot, axis=-1)
    return (jax.nn.softmax(picked, axis=-1), onehot)


def gates_back(gates, onehot, d_gates, normed, router):
    d_picked = gates * (d_gates - jnp.sum(gates * d_gates, axis=-1, keepdims=True))
    d_logits = jnp.sum(d_picked[:, :, None] * onehot, axis=1)
    d_router = jnp.dot(d_logits.T, normed.astype(F32), precision=HIGHEST)
    d_normed = jnp.dot(d_logits, router.T, precision=HIGHEST)
    return (d_router, d_normed)


def to_experts(gates, onehot, extra):
    by_expert = jnp.sum(gates[:, :, None] * onehot, axis=1).T
    rows = jnp.repeat(by_expert, OUTER, axis=0)[:, None, :]
    if extra is not None:
        rows = jnp.concatenate(
            [rows, jnp.broadcast_to(extra[None, None, :], rows.shape)], axis=1
        )
    return lax.all_to_all(rows, GROUP, split_axis=0, concat_axis=0, tiled=True)


def from_experts(d_gates, onehot, experts):
    rows = lax.all_to_all(d_gates, GROUP, split_axis=0, concat_axis=0, tiled=True)
    by_expert = jnp.sum(rows.reshape(experts, OUTER, -1), axis=1)
    return jnp.einsum("tce,et->tc", onehot, by_expert, precision=HIGHEST)


def meet(rows):
    return lax.all_gather(rows, GROUP, axis=0, tiled=True)


def part(rows):
    return lax.psum_scatter(rows, GROUP, scatter_dimension=0, tiled=True)


def mm(form, first, second):
    return jnp.einsum(form, first, second, preferred_element_type=F32)


def head_columns(matrix):
    span = HEADS // OUTER * HD
    whole = HEADS * HD
    return [
        jnp.concatenate(
            [
                matrix[:, start + k * span : start + (k + 1) * span]
                for start in range(0, matrix.shape[1], whole)
            ],
            axis=1,
        )
        for k in range(OUTER)
    ]


def gather_heads(weight):
    return lax.all_to_all(
        jnp.stack(head_columns(weight)), "o", split_axis=0, concat_axis=0, tiled=True
    )


def gather_query(weight):
    parts = ring_gather(gather_heads(weight), "i")
    return in_order(parts, "i", 1).reshape(-1, parts[0].shape[2])


def scatter_rows(grad):
    inner = lax.axis_size("i")
    blocks = grad.reshape(OUTER, inner, -1, grad.shape[1])
    blocks = from_order([blocks[:, k] for k in range(inner)], "i")
    mine = ring_scatter(blocks, "i").astype(BF16)
    here = lax.all_to_all(mine, "o", split_axis=0, concat_axis=0, tiled=True).astype(F32)
    span = HEADS // OUTER * HD
    return jnp.concatenate(
        [
            here[k, :, start : start + span]
            for start in range(0, grad.shape[1], span)
            for k in range(OUTER)
        ],
        axis=1,
    )


def gather_kv(weight):
    here = ring_gather(gather_heads(weight), "y")
    here = ring_gather(jnp.stack(here), "i")
    here = ring_gather(jnp.stack(here), "c")
    whole = in_order([in_order([in_order(list(one), "y", 0) for one in two], "i", 2) for two in here], "c", 1)
    return whole.reshape(-1, whole.shape[-1])


def scatter_kv(grad):
    high = lax.axis_size("y")
    blocks = grad.reshape(high, 2, -1, grad.shape[1])
    mine = ring_scatter(from_order([blocks[:, 0], blocks[:, 1]], "c"), "c")
    mine = ring_scatter(from_order([mine[k] for k in range(high)], "y"), "y")
    return scatter_rows(mine)


def own_places():
    return jnp.stack([lax.axis_index(axis) for axis in GROUP]).astype(jnp.int32)


def add_low(first, second):
    return (first.astype(F32) + second.astype(F32)).astype(BF16)


def ring_low(blocks, axis):
    travelling = blocks[1]
    for j in range(2, lax.axis_size(axis)):
        travelling = add_low(shift(travelling, axis), blocks[j])
    return add_low(shift(travelling, axis), blocks[0])


def part_by_rings(rows):
    rows = ring_low([rows[k] for k in range(rows.shape[0])], "c")
    half = rows.shape[2] // 2
    first, second = rows[:, :, :half], rows[:, :, half:]
    first = ring_low([first[k] for k in range(first.shape[0])], "y")
    first = ring_low([first[k] for k in range(first.shape[0])], "o")
    second = ring_low([second[:, k] for k in range(second.shape[1])], "o")
    second = ring_low([second[k] for k in range(second.shape[0])], "y")
    return jnp.concatenate([first, second])


VMEM = 56 * 1024 * 1024
ROW_STEP = 256


def nn(first, second):
    return jnp.dot(first, second, preferred_element_type=F32)


def nt(first, second):
    return lax.dot_general(first, second, (((1,), (1,)), ((), ())), preferred_element_type=F32)


def tn(first, second):
    return lax.dot_general(first, second, (((0,), (0,)), ((), ())), preferred_element_type=F32)


def as_column(row, rows):
    return jnp.broadcast_to(row, (rows, rows)).T[:, :1]


def turn(head, cosine, sine):
    return head * cosine + pltpu.roll(head, HD // 2, 1) * sine


def turn_back(head, cosine, sine):
    return head * cosine - pltpu.roll(head, HD // 2, 1) * sine


def allowed_keys(segment, length):
    keys = jnp.broadcast_to(segment, (length, length))
    row = lax.broadcasted_iota(jnp.int32, (length, length), 0)
    column = lax.broadcasted_iota(jnp.int32, (length, length), 1)
    return (keys == keys.T) & (column <= row)


def heads_nt(first, second):
    return lax.dot_general(first, second, (((2,), (2,)), ((0,), (0,))), preferred_element_type=F32)


def heads_nn(first, second):
    return lax.dot_general(first, second, (((2,), (1,)), ((0,), (0,))), preferred_element_type=F32)


def heads_tn(first, second):
    return lax.dot_general(first, second, (((1,), (1,)), ((0,), (0,))), preferred_element_type=F32)


def softmax_rows(queries, keys, allowed):
    scores = jnp.where(allowed[None], heads_nt(queries, keys) * (1.0 / math.sqrt(HD)), MASKED)
    exponent = jnp.exp(scores - jnp.max(scores, axis=-1, keepdims=True))
    return exponent / jnp.sum(exponent, axis=-1, keepdims=True)


def place_rows(places_ref, part_ref, value, first, length):
    count = part_ref.shape[2]
    for seq in range(value.shape[0] // length):
        slot = lax.rem(first + seq - places_ref[2] + count, count)
        part_ref[0, 0, slot] = value[seq * length : (seq + 1) * length]


def attend_kernel(
    places_ref, x_ref, info_ref, cos_ref, sin_ref, slab_ref, out_ref, qkv_ref, gated_ref, part_ref
):
    length = cos_ref.shape[0]
    span = out_ref.shape[0]
    raw = nn(x_ref[...], slab_ref[...])
    cosine, sine = cos_ref[...], sin_ref[...]
    starts = range(0, span, HD)
    for seq in range(info_ref.shape[0]):
        rows = slice(seq * length, (seq + 1) * length)
        gate = as_column(info_ref[seq, 0:1, :], length)
        allowed = allowed_keys(info_ref[seq, 1:2, :], length)
        queries, keys, values = [], [], []
        for at in starts:
            head = raw[rows, at : at + HD].astype(BF16).astype(F32)
            queries.append(turn(head, cosine, sine).astype(BF16))
            keys.append(turn(raw[rows, span + at : span + at + HD], cosine, sine).astype(BF16))
            values.append(raw[rows, 2 * span + at : 2 * span + at + HD].astype(BF16))
            qkv_ref[rows, at : at + HD] = queries[-1]
            qkv_ref[rows, span + at : span + at + HD] = keys[-1]
            qkv_ref[rows, 2 * span + at : 2 * span + at + HD] = values[-1]
        probs = softmax_rows(jnp.stack(queries), jnp.stack(keys), allowed)
        gated = (heads_nn(probs.astype(BF16), jnp.stack(values)) * gate[None]).astype(BF16)
        for number, at in enumerate(starts):
            gated_ref[rows, at : at + HD] = gated[number]
    place_rows(places_ref, part_ref, nn(gated_ref[...], out_ref[...]).astype(BF16), 0, length)


def attend_back_kernel(
    places_ref,
    mid_ref,
    info_ref,
    cos_ref,
    sin_ref,
    qkv_ref,
    x_ref,
    slab_ref,
    out_ref,
    d_qkv_ref,
    part_ref,
    d_gate_ref,
    d_gain_ref,
):
    length = cos_ref.shape[0]
    span = out_ref.shape[0]
    scale = 1.0 / math.sqrt(HD)
    d_rows = nt(mid_ref[...], out_ref[...])
    cosine, sine = cos_ref[...], sin_ref[...]
    starts = range(0, span, HD)
    for seq in range(info_ref.shape[0]):
        rows = slice(seq * length, (seq + 1) * length)
        gate = as_column(info_ref[seq, 0:1, :], length)[None]
        allowed = allowed_keys(info_ref[seq, 1:2, :], length)
        queries = jnp.stack([qkv_ref[rows, at : at + HD] for at in starts])
        keys = jnp.stack([qkv_ref[rows, span + at : span + at + HD] for at in starts])
        values = jnp.stack([qkv_ref[rows, 2 * span + at : 2 * span + at + HD] for at in starts])
        d_heads = jnp.stack([d_rows[rows, at : at + HD] for at in starts])
        probs = softmax_rows(queries, keys, allowed)
        weighted = probs * heads_nt(d_heads.astype(BF16), values)
        sums = jnp.sum(weighted, axis=-1, keepdims=True)
        d_scores = ((weighted - probs * sums) * gate).astype(BF16)
        d_queries = heads_nn(d_scores, keys) * scale
        d_keys = heads_tn(d_scores, queries) * scale
        d_values = heads_tn(probs.astype(BF16), (d_heads * gate).astype(BF16))
        for number, at in enumerate(starts):
            d_qkv_ref[rows, at : at + HD] = turn_back(d_queries[number], cosine, sine).astype(BF16)
            d_qkv_ref[rows, span + at : span + at + HD] = turn_back(
                d_keys[number], cosine, sine
            ).astype(BF16)
            d_qkv_ref[rows, 2 * span + at : 2 * span + at + HD] = d_values[number].astype(BF16)
        total = jnp.broadcast_to(jnp.sum(sums, axis=0), (length, length))
        d_gate_ref[seq] = total.T[:1]
    d_input = nt(d_qkv_ref[...], slab_ref[...])

    @pl.when(pl.program_id(0) == 0)
    def _():
        d_gain_ref[...] = jnp.zeros_like(d_gain_ref)

    d_gain_ref[...] += jnp.sum(d_input * x_ref[...].astype(F32), axis=0, keepdims=True)
    place_rows(places_ref, part_ref, d_input.astype(BF16), 0, length)


def fixed(shape):
    return pl.BlockSpec(shape, lambda step, places: (0,) * len(shape))


def rows_spec(rows, columns):
    return pl.BlockSpec((rows, columns), lambda step, places: (step, 0))


def info_spec(seqs, kinds, length):
    return pl.BlockSpec((seqs, kinds, length), lambda step, places: (step, 0, 0))


def place_spec(high, length, width, steps):
    def index(step, places):
        pair = lax.div(step, steps)
        low = lax.rem(lax.rem(pair, 2) - places[1] + 2, 2)
        return (low, lax.rem(lax.div(pair, 2) - places[0] + high, high), 0, 0, 0)

    return pl.BlockSpec((1, 1, OUTER, length, width), index)


def shape(dims, dtype=BF16):
    return jax.ShapeDtypeStruct(dims, dtype)


def call(kernel, name, steps, in_specs, out_specs, out_shape, flops, moved, operands):
    return pl.pallas_call(
        kernel,
        grid_spec=pltpu.PrefetchScalarGridSpec(
            num_scalar_prefetch=1, grid=(steps,), in_specs=in_specs, out_specs=out_specs
        ),
        out_shape=out_shape,
        compiler_params=pltpu.CompilerParams(vmem_limit_bytes=VMEM),
        cost_estimate=pl.CostEstimate(flops=flops, bytes_accessed=moved, transcendentals=0),
        name=name,
    )(*operands)


def attend(places, rows, info, cosine, sine, slab, out_mat):
    count, width = rows.shape
    length = cosine.shape[0]
    step = OUTER * length
    span = out_mat.shape[0]
    high = count // (2 * step)
    return call(
        attend_kernel,
        "attend",
        count // step,
        [
            rows_spec(step, width),
            info_spec(OUTER, 2, length),
            fixed(cosine.shape),
            fixed(sine.shape),
            fixed(slab.shape),
            fixed(out_mat.shape),
        ],
        [rows_spec(step, 3 * span), rows_spec(step, span), place_spec(high, length, width, 1)],
        [shape((count, 3 * span)), shape((count, span)), shape((2, high, OUTER, length, width))],
        2 * count * width * 4 * span + 4 * count * length * span,
        4 * count * (width + 2 * span),
        (places, rows, info, cosine, sine, slab, out_mat),
    )


def attend_back(places, d_middle, info, cosine, sine, qkv, rows, slab, out_mat):
    count, width = d_middle.shape
    length = cosine.shape[0]
    step = OUTER * length
    span = out_mat.shape[0]
    high = count // (2 * step)
    return call(
        attend_back_kernel,
        "attend_back",
        count // step,
        [
            rows_spec(step, width),
            info_spec(OUTER, 2, length),
            fixed(cosine.shape),
            fixed(sine.shape),
            rows_spec(step, 3 * span),
            rows_spec(step, width),
            fixed(slab.shape),
            fixed(out_mat.shape),
        ],
        [
            rows_spec(step, 3 * span),
            place_spec(high, length, width, 1),
            info_spec(OUTER, 1, length),
            fixed((1, width)),
        ],
        [
            shape((count, 3 * span)),
            shape((2, high, OUTER, length, width)),
            shape((count // length, 1, length), F32),
            shape((1, width), F32),
        ],
        2 * count * width * 4 * span + 10 * count * length * span,
        4 * count * (2 * width + 3 * span),
        (places, d_middle, info, cosine, sine, qkv, rows, slab, out_mat),
    )


def units_kernel(parts, places_ref, x_ref, info_ref, *refs):
    d_units_refs, up_refs = refs[:parts], refs[parts : 3 * parts]
    d_both_refs, gated_refs = refs[3 * parts : 4 * parts], refs[4 * parts : 5 * parts]
    back_ref, d_gate_ref = refs[5 * parts :]
    length = info_ref.shape[2]
    seqs = info_ref.shape[0]
    rows = x_ref[...]
    gate = jnp.concatenate([as_column(info_ref[seq], length) for seq in range(seqs)], axis=0)
    back = jnp.zeros((seqs * length, back_ref.shape[-1]), F32)
    d_gate = jnp.zeros((seqs * length, 1), F32)
    for part in range(parts):
        first_ref, second_ref = up_refs[2 * part : 2 * part + 2]
        units = first_ref.shape[0]
        gate_in = nt(rows, first_ref[...])
        up_in = nt(rows, second_ref[...])
        sigma = jax.nn.sigmoid(gate_in)
        active = gate_in * sigma
        hidden_units = active * up_in
        d_units = d_units_refs[part][...].astype(F32)
        d_gate = d_gate + jnp.sum(hidden_units * d_units, axis=-1, keepdims=True)
        gated_refs[part][...] = (hidden_units * gate).astype(BF16)
        d_units = d_units * gate
        d_first = (d_units * up_in * (sigma + active * (1.0 - sigma))).astype(BF16)
        d_second = (d_units * active).astype(BF16)
        d_both_refs[part][:, :units] = d_first
        d_both_refs[part][:, units:] = d_second
        back = back + nn(d_first, first_ref[...]) + nn(d_second, second_ref[...])
    first = lax.rem(pl.program_id(0), OUTER // seqs) * seqs
    place_rows(places_ref, back_ref, back.astype(BF16), first, length)
    for seq in range(seqs):
        column = jnp.broadcast_to(d_gate[seq * length : (seq + 1) * length], (length, length))
        d_gate_ref[seq] = column.T[:1]


def run_units(places, rows, info, d_units, own_up, other_up):
    count, width = rows.shape
    length = info.shape[2]
    parts = 1 + len(other_up) // 2
    units = d_units[0].shape[1]
    seqs = ROW_STEP // length
    high = count // (2 * OUTER * length)
    own_specs = [
        pl.BlockSpec((units, width), lambda step, places, half=half: (half, 0)) for half in range(2)
    ]
    return call(
        functools.partial(units_kernel, parts),
        "units",
        count // ROW_STEP,
        [rows_spec(ROW_STEP, width), info_spec(seqs, 1, length)]
        + [rows_spec(ROW_STEP, units)] * parts
        + own_specs
        + [fixed(one.shape) for one in other_up],
        [rows_spec(ROW_STEP, 2 * units)] * parts
        + [rows_spec(ROW_STEP, units)] * parts
        + [place_spec(high, length, width, OUTER // seqs), info_spec(seqs, 1, length)],
        [shape((count, 2 * units))] * parts
        + [shape((count, units))] * parts
        + [
            shape((2, high, OUTER, length, width)),
            shape((count // length, 1, length), F32),
        ],
        8 * count * width * units * parts,
        4 * count * (width + 2 * units * parts),
        (places, rows, info, *d_units, own_up, own_up, *other_up),
    )


def shards(
    hidden_in,
    segment_ids,
    att_route,
    mlp_route,
    norm_gain1,
    norm_gain2,
    att_router,
    mlp_router,
    kv_weight,
    query_weight,
    out_weight,
    att_bias,
    up_weight,
    down_weight,
    mlp_bias,
    cotangent,
):
    experts = lax.axis_size(EXPERT)
    inner = lax.axis_size("i")
    tokens, width = hidden_in.shape
    span = HEADS // OUTER * HD
    cosine, sine_table = rope_tables(tokens)

    places = own_places()
    tie = lax.optimization_barrier

    kv_mat = gather_kv(kv_weight)
    query_mat = gather_query(query_weight[0])
    slab = jnp.concatenate([query_mat, kv_mat], axis=1)
    out_mat = in_order(ring_gather(out_weight[0], "i"), "i").reshape(span, width)
    own_up = up_weight[0].reshape(-1, width)
    down_source, _ = tie((down_weight[0], slab))
    down_parts = ring_gather(down_source, "i")

    residual = hidden_in.astype(F32)
    normed_one, inverse_one = norm_rows(residual, norm_gain1)
    attn_input = normed_one.astype(BF16)
    att_gate, att_onehot = pair_gates(attn_input, att_router, att_route, experts)
    info = to_experts(att_gate, att_onehot, segment_ids[0].astype(F32))
    all_attn = meet(attn_input)
    cot_low, all_attn = tie((cotangent.astype(BF16), all_attn))
    all_cot = meet(cot_low)
    qkv, gated, branch = attend(places, all_attn, info, cosine, sine_table, slab, out_mat)
    branch = part_by_rings(branch)

    branch, down_parts, all_cot = tie((branch, down_parts, all_cot))
    first_source, _ = tie((up_weight[0, 0], down_parts[-1]))
    first_parts = ring_gather(first_source, "i")
    middle = residual + branch.astype(F32) + att_bias
    normed_two, inverse_two = norm_rows(middle, norm_gain2)
    mlp_input = normed_two.astype(BF16)
    mlp_gate, mlp_onehot = pair_gates(mlp_input, mlp_router, mlp_route, experts)
    mlp_input, first_parts = tie((mlp_input, first_parts))
    second_source, _ = tie((up_weight[0, 1], first_parts[-1]))
    second_parts = ring_gather(second_source, "i")
    gate_m = to_experts(mlp_gate, mlp_onehot, None)
    all_mlp = meet(mlp_input)
    d_units = [mm("td,fd->tf", all_cot, down).astype(BF16) for down in down_parts]
    other_up = [one for pair in zip(first_parts[1:], second_parts[1:]) for one in pair]
    found = run_units(places, all_mlp, gate_m, d_units, own_up, other_up)
    d_both, gated_units = found[:inner], found[inner : 2 * inner]
    rows_back, d_gate_m = found[2 * inner :]
    d_mlp_gate = from_experts(d_gate_m[:, 0], mlp_onehot, experts)
    d_mlp_input = part_by_rings(rows_back).astype(F32)
    d_mlp_router, d_mlp_from_router = gates_back(
        mlp_gate, mlp_onehot, d_mlp_gate, mlp_input, mlp_router
    )
    d_norm_two, d_gain_two = norm_back(
        middle, inverse_two, norm_gain2, d_mlp_input + d_mlp_from_router
    )
    d_middle = cotangent + d_norm_two
    summed_one = sum_all(
        jnp.concatenate(
            [
                jnp.stack([d_gain_two, jnp.sum(d_middle, axis=0), jnp.sum(cotangent, axis=0)]),
                d_mlp_router,
            ]
        )
    )
    d_upper = ring_scatter([mm("tf,td->fd", d_here, all_mlp) for d_here in d_both], "i")
    d_upper = d_upper.reshape(up_weight.shape)
    d_lower = ring_scatter([mm("tf,td->fd", here, all_cot) for here in gated_units], "i")[None]
    rows_out = None
    for units_here, down in zip(gated_units, down_parts):
        ahead = mm("tf,fd->td", units_here, down)
        rows_out = ahead if rows_out is None else rows_out + ahead
    rows_out = rows_out.astype(BF16)

    all_mid = meet(d_middle.astype(BF16))
    rows_out, all_mid = tie((rows_out, all_mid))
    layer_out = middle + part(rows_out).astype(F32) + mlp_bias
    d_qkv, rows_one, d_gate_a, d_gain_a = attend_back(
        places, all_mid, info, cosine, sine_table, qkv, all_attn, slab, out_mat
    )
    d_att_gate = from_experts(d_gate_a[:, 0], att_onehot, experts)
    d_attn_input = part_by_rings(rows_one).astype(F32)
    d_out = mm("tf,td->fd", gated, all_mid).reshape(inner, -1, width)
    d_output = ring_scatter(from_order([d_out[k] for k in range(inner)], "i"), "i")[None]
    d_slab = mm("td,tf->df", all_attn, d_qkv)
    d_query = scatter_rows(d_slab[:, :span])[None]
    d_kv_weight = scatter_kv(d_slab[:, span:])
    d_att_router, d_att_from_router = gates_back(
        att_gate, att_onehot, d_att_gate, attn_input, att_router
    )
    d_norm_one, _ = norm_back(
        residual, inverse_one, norm_gain1, d_attn_input + d_att_from_router
    )
    d_gain_one = d_gain_a / norm_gain1 + jnp.sum(
        d_att_from_router * residual * inverse_one, axis=0, keepdims=True
    )
    d_input = d_middle + d_norm_one
    summed_two = sum_all(jnp.concatenate([d_gain_one, d_att_router]))
    return (
        layer_out,
        d_input,
        summed_two[0],
        summed_one[0],
        summed_two[1:].T,
        summed_one[3:].T,
        d_kv_weight,
        d_query,
        d_output,
        summed_one[1],
        d_upper,
        d_lower,
        summed_one[2],
    )


def solution(mesh):
    experts, fsdp = mesh.shape["expert"], mesh.shape["fsdp"]
    fine = Mesh(mesh.devices.reshape(experts // 2, 2, OUTER, fsdp // OUTER), ALL)
    shard = ("o", "i")
    rows = P(ALL, None)
    placed = (
        rows,
        rows,
        rows,
        rows,
        P(),
        P(),
        P(),
        P(),
        rows,
        P(EXPERT, shard, None),
        P(EXPERT, shard, None),
        P(),
        P(EXPERT, None, shard, None),
        P(EXPERT, shard, None),
        P(),
        rows,
    )
    return jax.shard_map(
        shards,
        mesh=fine,
        in_specs=placed,
        out_specs=(
            rows,
            rows,
            P(),
            P(),
            P(),
            P(),
            rows,
            P(EXPERT, shard, None),
            P(EXPERT, shard, None),
            P(),
            P(EXPERT, None, shard, None),
            P(EXPERT, shard, None),
            P(),
        ),
        check_vma=False,
    )
```

time: 1210 us -> 1100 us (0.909)
  waiting for transfers between devices: 721 us -> 532 us
  starting transfers between devices: 53.5 us -> 125 us
  Pallas kernels: 166 us -> 140 us
  other arithmetic: 64.1 us -> 85.6 us
  blocking collectives: 10.6 us -> 24.9 us
  local copies, waits for them, and re-layouts: 36.3 us -> 48.4 us
    reduce_scatter x4 -> x1, waiting for transfers between devices: 302 us -> 0.01 us  [part(): return lax.psum_scatter(rows, GROUP, scatter_dimension=0, tiled=True)]
    ppermute x10 -> x42, waiting for transfers between devices: 289 us -> 464 us  [shift(): return lax.ppermute(value, axis, [((k + 1) % size, k) for k in range(size)])]
    ppermute x10 -> x42, starting transfers between devices: 10.4 us -> 80 us  [shift(): return lax.ppermute(value, axis, [((k + 1) % size, k) for k in range(size)])]
    all_to_all x4, waiting for transfers between devices: 96 us -> 52.8 us  [the longest x2 34 us: gather_heads(): lax.all_to_all(jnp.stack(head_columns(weight)), 'o', split_axis=0, concat...]
    pallas_call x3, Pallas kernels: 166 us -> 140 us  [call(): pl.pallas_call(kernel, grid_spec=pltpu.PrefetchScalarGridSpec(num_scalar_...]
    convert_element_type x1 -> x31, other arithmetic: 3.8 us -> 24.5 us  [the longest x27 20.4 us: add_low(): return (first.astype(F32) + second.astype(F32)).astype(BF16)]
    squeeze x1 -> x17, local copies, waits for them, and re-layouts: 0.17 us -> 18 us  [the longest x3 10.7 us: part_by_rings(): rows = ring_low([rows[k] for k in range(rows.shape[0])], 'c')]
    all_gather x4, waiting for transfers between devices: 17.3 us -> 2.77 us  [meet(): return lax.all_gather(rows, GROUP, axis=0, tiled=True)]
  transfers between devices with their start and end apart: 35 -> 64, of which waited for: 21 -> 37; matrix products, arithmetic and copies ran while one was open for 16% -> 19% of each run, Pallas kernels for 8% -> 3%
where the time goes in v3:
time: 1100 us
  waiting for transfers between devices  532 us (48%)
  Pallas kernels  140 us (13%)
  matrix products  128 us (12%)
  starting transfers between devices  125 us (11%)
  other arithmetic  85.6 us (8%)
  local copies, waits for them, and re-layouts  48.4 us (4%)
  blocking collectives  24.9 us (2%)
  between operations  15.4 us (1%)
    ppermute x42, waiting for transfers between devices, shift(): return lax.ppermute(value, axis, [((k + 1) % size, k) for k in range(size)])  464 us
    pallas_call x3, Pallas kernels, call(): pl.pallas_call(kernel, grid_spec=pltpu.PrefetchScalarGridSpec(num_scalar_...  140 us
    dot_general x10, matrix products, mm(): return jnp.einsum(form, first, second, preferred_element_type=F32)  121 us
    ppermute x42, starting transfers between devices, shift(): return lax.ppermute(value, axis, [((k + 1) % size, k) for k in range(size)])  80 us
    all_to_all x2, waiting for transfers between devices, gather_heads(): lax.all_to_all(jnp.stack(head_columns(weight)), 'o', split_axis=0, concat...  34 us
    all_to_all x1, blocking collectives, from_experts(): lax.all_to_all(d_gates, GROUP, split_axis=0, concat_axis=0, tiled=True)  24.9 us
  transfers between devices with their start and end apart: 64, of which 37 were waited for; matrix products, arithmetic and copies ran while one was open for 19% of the time, Pallas kernels for 3%

profile of v3, /device:TPU:0, one launch (start us, length us, event | category | flops | bytes accessed | tf_op | source)
XLA Modules:
  0.0 1099.5 jit_solution(14938501983851733124)
XLA Ops:
  13.8 6.4 all-to-all-start.2
  23.5 22.9 %all-to-all-done.2 = bf16[4,64,1024]{2,1,0:T(8,128)(2,1)S(1)} async-done(((bf16[4,64,1024]{2,1,0:T(8,128)(2,1)}), bf16[4,64,1024]{2,1,0:T(8,128)(2,1)S(1)}, u32[]{:S(2)}, u32[]{:S(2)}) %all-to-all-start.2) | async-done | bytes 524320 | tf_op jit(solution)/shard_map/all_to_all | solution.py:156
  51.6 7.5 collective-permute-done.1
  65.4 14.8 %collective-permute-done.2 = bf16[2,4,64,1024]{3,2,1,0:T(8,128)(2,1)} collective-permute-done((bf16[2,4,64,1024]{3,2,1,0:T(8,128)(2,1)}, bf16[2,4,64,1024]{3,2,1,0:T(8,128)(2,1)}, u32[]{:S(2)}, u32[]{:S(2)}) %collective-permute-start.2) | collective-permute-done | bytes 1048608 | tf_op jit(solution)/shard_map/ppermute | solution.py:55
  83.8 11.1 %all-to-all-done.1 = bf16[4,256,512]{2,1,0:T(8,128)(2,1)S(1)} async-done(((bf16[4,256,512]{2,1,0:T(8,128)(2,1)}), bf16[4,256,512]{2,1,0:T(8,128)(2,1)S(1)}, u32[]{:S(2)}, u32[]{:S(2)}) %all-to-all-start.1) | async-done | bytes 1048608 | tf_op jit(solution)/shard_map/all_to_all | solution.py:156
  94.9 4.3 all-to-all-start
  107.0 17.9 %collective-permute-done = bf16[4,256,512]{2,1,0:T(8,128)(2,1)S(1)} collective-permute-done((bf16[4,256,512]{2,1,0:T(8,128)(2,1)S(1)}, bf16[4,256,512]{2,1,0:T(8,128)(2,1)S(1)}, u32[]{:S(2)}, u32[]{:S(2)}) %collective-permute-start) | collective-permute-done | bytes 1048608 | tf_op jit(solution)/shard_map/ppermute | solution.py:55
  137.6 33.6 %attend.1 = (bf16[2048,1536]{1,0:T(8,128)(2,1)}, bf16[2048,512]{1,0:T(8,128)(2,1)}, bf16[2,2,4,128,2048]{4,3,2,1,0:T(8,128)(2,1)}) custom-call(s32[3]{0:T(128)} %pad_add_fusion.places_ref, bf16[2048,2048]{1,0:T(8,128)(2,1)} %all-gather.5.cloned.1.call-done.x_ref, f32[16,2,128]{2,1,0:T(2,128)} %copy-done.36, f32[128,128]{1,0:T(8,128)} %get-tuple-element.123.cos_ref, ...), custom_call_target="tpu_custom_call" | custom-call | flops 17716740096 | bytes 25165824 | tf_op jit(solution)/shard_map/attend/pallas_call | solution.py:393
  173.9 7.1 collective-permute-done.5
  188.2 23.3 %collective-permute-done.10 = bf16[2,64,2048]{2,1,0:T(8,128)(2,1)S(1)} collective-permute-done((bf16[2,64,2048]{2,1,0:T(8,128)(2,1)S(1)}, bf16[2,64,2048]{2,1,0:T(8,128)(2,1)S(1)}, u32[]{:S(2)}, u32[]{:S(2)}) %collective-permute-start.10) | collective-permute-done | bytes 524320 | tf_op jit(solution)/shard_map/ppermute | solution.py:55
  211.8 13.5 %collective-permute-done.11 = bf16[2,64,2048]{2,1,0:T(8,128)(2,1)S(1)} collective-permute-done((bf16[2,64,2048]{2,1,0:T(8,128)(2,1)S(1)}, bf16[2,64,2048]{2,1,0:T(8,128)(2,1)S(1)}, u32[]{:S(2)}, u32[]{:S(2)}) %collective-permute-start.11) | collective-permute-done | bytes 524320 | tf_op jit(solution)/shard_map/ppermute | solution.py:55
  233.3 10.7 collective-permute-done.7
  244.1 4.1 collective-permute-start.8
  252.2 4.6 collective-permute-start.9
  256.9 3.8 collective-permute-done.9
  260.8 34.3 %collective-permute-done.14 = bf16[704,2048]{1,0:T(8,128)(2,1)} collective-permute-done((bf16[704,2048]{1,0:T(8,128)(2,1)S(1)}, bf16[704,2048]{1,0:T(8,128)(2,1)}, u32[]{:S(2)}, u32[]{:S(2)}) %collective-permute-start.14) | collective-permute-done | bytes 2883616 | tf_op jit(solution)/shard_map/ppermute | solution.py:55
  297.9 59.9 %collective-permute-done.15.refs_4_ = bf16[704,2048]{1,0:T(8,128)(2,1)} collective-permute-done((bf16[704,2048]{1,0:T(8,128)(2,1)}, bf16[704,2048]{1,0:T(8,128)(2,1)}, u32[]{:S(2)}, u32[]{:S(2)}) %collective-permute-start.15) | collective-permute-done | bytes 2883616 | tf_op jit(solution)/shard_map/ppermute | solution.py:55
  360.1 3.9 all-to-all-start.3
  365.6 11.4 %convolution_convert_fusion.2 = bf16[2048,704]{0,1:T(8,128)(2,1)} fusion(bf16[2048,2048]{1,0:T(8,128)(2,1)} %all-gather.7.cloned.1.call-done, bf16[704,2048]{1,0:T(8,128)(2,1)} %collective-permute-done.14), kind=kOutput, calls=%fused_computation.23 | convolution fusion | flops 5907021824 | bytes 14155776 | tf_op jit(solution)/shard_map/td,fd->tf/dot_general | solution.py:137
  377.1 7.5 convolution_convert_fusion.3
  384.6 4.6 copy.127.refs_0_
  389.2 4.6 copy.128.refs_1_
  393.8 35.5 %collective-permute-done.16.refs_5_ = bf16[704,2048]{1,0:T(8,128)(2,1)} collective-permute-done((bf16[704,2048]{1,0:T(8,128)(2,1)}, bf16[704,2048]{1,0:T(8,128)(2,1)}, u32[]{:S(2)}, u32[]{:S(2)}) %collective-permute-start.16) | collective-permute-done | bytes 2883616 | tf_op jit(solution)/shard_map/ppermute | solution.py:55
  432.1 66.2 %units.1 = (bf16[2048,1408]{1,0:T(8,128)(2,1)}, bf16[2048,1408]{1,0:T(8,128)(2,1)}, bf16[2048,704]{1,0:T(8,128)(2,1)}, bf16[2048,704]{1,0:T(8,128)(2,1)}, bf16[2...) custom-call(s32[3]{0:T(128)} %pad_add_fusion.places_ref, bf16[2048,2048]{1,0:T(8,128)(2,1)} %all-gather.9.cloned.1.call-done.x_ref, ...), custom_call_target="tpu_custom_call" | custom-call | flops 47244640256 | bytes 39845888 | tf_op jit(solution)/shard_map/units/pallas_call | solution.py:393
  501.2 6.9 collective-permute-done.17
  512.9 24.9 %all_to_all.42 = f32[16,1,128]{2,1,0:T(1,128)S(1)} all-to-all(f32[16,1,128]{2,1,0:T(1,128)S(1)} %copy-done.44), channel_id=1, replica_groups=mesh['y'=2,'c'=2,'o'=4,'i'=2] {'y','c','o'}, dimensions={0} | all-to-all | bytes 16384 | tf_op jit(solution)/shard_map/all_to_all | solution.py:123
  543.8 10.0 collective-permute-done.22
  562.8 8.1 collective-permute-done.23
  572.0 4.3 collective-permute-start.24
  576.4 4.4 collective-permute-start.21
  580.8 7.7 collective-permute-done.24
  592.3 3.8 collective-permute-done.25
  600.1 10.8 convolution_convert_fusion.1
  613.4 18.1 %convolution_convert_fusion = bf16[1408,2048]{1,0:T(8,128)(2,1)} fusion(bf16[2048,1408]{1,0:T(8,128)(2,1)} %get-tuple-element.63, bf16[2048,2048]{1,0:T(8,128)(2,1)} %all-gather.9.cloned.1.call-done.x_ref), kind=kOutput, calls=%fused_computation.8 | convolution fusion | flops 11814043648 | bytes 19922944 | tf_op jit(solution)/shard_map/tf,td->fd/dot_general | solution.py:137
  632.2 11.5 %fusion.72 = f32[2048,2048]{1,0:T(8,128)} fusion(bf16[2048,704]{1,0:T(8,128)(2,1)S(1)} %copy-done.57, bf16[704,2048]{1,0:T(8,128)(2,1)} %collective-permute-done.14), kind=kOutput, calls=%fused_computation.267 | convolution fusion | flops 5905580032 | bytes 22544384 | tf_op jit(solution)/shard_map/tf,fd->td/dot_general | solution.py:137
  643.9 12.5 %add_convert_fusion = bf16[2048,2048]{1,0:T(8,128)(2,1)} fusion(f32[2048,2048]{1,0:T(8,128)} %fusion.72, bf16[2048,704]{1,0:T(8,128)(2,1)S(1)} %copy-done.56, bf16[704,2048]{1,0:T(8,128)(2,1)S(1)} %bitcast.479), kind=kOutput, calls=%fused_computation | convolution fusion | flops 5913968640 | bytes 30932992 | tf_op jit(solution)/shard_map/tf,fd->td/dot_general | solution.py:137
  656.5 4.9 collective-permute-start.43
  661.3 15.3 %collective-permute-done.51 = bf16[704,2048]{1,0:T(8,128)(2,1)} collective-permute-done((bf16[704,2048]{1,0:T(8,128)(2,1)}, bf16[704,2048]{1,0:T(8,128)(2,1)}, u32[]{:S(2)}, u32[]{:S(2)}) %collective-permute-start.51) | collective-permute-done | bytes 2883616 | tf_op jit(solution)/shard_map/ppermute | solution.py:55
  676.6 10.7 add_bitcast_fusion
  688.8 107.3 %collective-permute-done.50 = bf16[1408,2048]{1,0:T(8,128)(2,1)} collective-permute-done((bf16[1408,2048]{1,0:T(8,128)(2,1)}, bf16[1408,2048]{1,0:T(8,128)(2,1)}, u32[]{:S(2)}, u32[]{:S(2)}) %collective-permute-start.50) | collective-permute-done | bytes 5767200 | tf_op jit(solution)/shard_map/ppermute | solution.py:55
  796.2 16.1 %convert_add_fusion = f32[1408,2048]{1,0:T(8,128)} fusion(bf16[1408,2048]{1,0:T(8,128)(2,1)} %collective-permute-done.50, bf16[2048,1408]{1,0:T(8,128)(2,1)S(1)} %bitcast.482, bf16[2048,2048]{1,0:T(8,128)(2,1)S(1)} %bitcast.474), kind=kOutput, calls=%fused_computation.1 | convolution fusion | flops 11816927232 | bytes 31457280 | tf_op jit(solution)/shard_map/tf,td->fd/dot_general | solution.py:137
  813.5 40.5 %attend_back.1 = (bf16[2048,1536]{1,0:T(8,128)(2,1)}, bf16[2,2,4,128,2048]{4,3,2,1,0:T(8,128)(2,1)}, f32[16,1,128]{2,1,0:T(1,128)}, f32[1,2048]{1,0:T(1,128)}) custom-call(s32[3]{0:T(128)} %pad_add_fusion.places_ref, bf16[2048,2048]{1,0:T(8,128)(2,1)} %all-gather.11.cloned.1.call-done.mid_ref, f32[16,2,128]{2,1,0:T(2,128)} %copy-done.36, ...), custom_call_target="tpu_custom_call" | custom-call | flops 18522046464 | bytes 46137344 | tf_op jit(solution)/shard_map/attend_back/pallas_call | solution.py:393
  854.0 17.8 %fusion.75 = f32[2048,1536]{1,0:T(8,128)S(1)} fusion(bf16[2048,2048]{1,0:T(8,128)(2,1)} %all-gather.5.cloned.1.call-done.x_ref, bf16[2048,1536]{1,0:T(8,128)(2,1)} %get-tuple-element.61), kind=kOutput, calls=%fused_computation.270 | convolution fusion | flops 12884901888 | bytes 27262976 | tf_op jit(solution)/shard_map/td,tf->df/dot_general | solution.py:137
  874.4 4.3 slice.428
  887.5 4.8 fusion.3
  892.5 5.4 slice_bitcast_fusion.3
  898.2 4.7 fusion.76
  906.8 5.8 bitcast_add_fusion
  918.5 4.5 all-to-all-start.7
  923.4 27.9 %collective-permute-done.46 = bf16[512,1024]{1,0:T(8,128)(2,1)} collective-permute-done((bf16[512,1024]{1,0:T(8,128)(2,1)S(1)}, bf16[512,1024]{1,0:T(8,128)(2,1)}, u32[]{:S(2)}, u32[]{:S(2)}) %collective-permute-start.46) | collective-permute-done | bytes 1048608 | tf_op jit(solution)/shard_map/ppermute | solution.py:55
  959.9 13.6 %all-to-all-done.7 = bf16[4,256,512]{2,1,0:T(8,128)(2,1)S(1)} async-done(((bf16[4,256,512]{2,1,0:T(8,128)(2,1)}), bf16[4,256,512]{2,1,0:T(8,128)(2,1)S(1)}, u32[]{:S(2)}, u32[]{:S(2)}) %all-to-all-start.7) | async-done | bytes 1048608 | tf_op jit(solution)/shard_map/all_to_all | solution.py:171
  980.7 4.4 fusion
  988.7 4.0 collective-permute-start.31
  992.7 5.2 all-to-all-done.6
  998.0 18.7 %collective-permute-done.27 = bf16[4,64,2048]{2,1,0:T(8,128)(2,1)} collective-permute-done((bf16[4,64,2048]{2,1,0:T(8,128)(2,1)}, bf16[4,64,2048]{2,1,0:T(8,128)(2,1)}, u32[]{:S(2)}, u32[]{:S(2)}) %collective-permute-start.27) | collective-permute-done | bytes 1048608 | tf_op jit(solution)/shard_map/ppermute | solution.py:55
  1018.7 3.8 collective-permute-start.28
  1024.4 4.9 collective-permute-done.28
  1029.4 4.3 collective-permute-start.29
  1033.7 6.8 collective-permute-done.32
  1041.7 4.3 collective-permute-start.33
  1046.2 4.2 collective-permute-start.30
  1050.4 7.0 collective-permute-done.33
  1060.7 4.5 collective-permute-done.34
  1074.3 3.8 collective-permute-done.37
  (381 shorter events, 187.9 us)
Async XLA Ops:
  7.2 122.0 %all-gather.5.cloned.1.call-start = ((), (), s32[]{:S(2)}) async-start(), calls=%async_computation.9 | async-start | bytes 8912896 | tf_op jit(solution)/shard_map/all_gather | solution.py:129
  13.8 32.6 %all-to-all-start.2 = ((bf16[4,64,1024]{2,1,0:T(8,128)(2,1)}), bf16[4,64,1024]{2,1,0:T(8,128)(2,1)S(1)}, u32[]{:S(2)}, u32[]{:S(2)}) async-start(bf16[4,64,1024]{2,1,0:T(8,128)(2,1)} %pad_maximum_fusion.13), calls=%async_computation.2 | async-start | bytes 1048576 | tf_op jit(solution)/shard_map/all_to_all | solution.py:156
  20.2 80.6 %collective-permute-start.4 = (bf16[256,2048]{1,0:T(8,128)(2,1)}, bf16[256,2048]{1,0:T(8,128)(2,1)}, u32[]{:S(2)}, u32[]{:S(2)}) collective-permute-start(bf16[256,2048]{1,0:T(8,128)(2,1)} %bitcast.45), channel_id=1, source_target_pairs={{1,0},{0,1},{3,2},{2,3},{5,4},{4,5},{7,6},{6,7},{9,8},{8,9},{11,10... | collective-permute-start | bytes 3145736 | tf_op jit(solution)/shard_map/ppermute | solution.py:55
  46.4 48.5 %all-to-all-start.1 = ((bf16[4,256,512]{2,1,0:T(8,128)(2,1)}), bf16[4,256,512]{2,1,0:T(8,128)(2,1)S(1)}, u32[]{:S(2)}, u32[]{:S(2)}) async-start(bf16[4,256,512]{2,1,0:T(8,128)(2,1)} %pad_maximum_fusion.7), calls=%async_computation.1 | async-start | bytes 2097152 | tf_op jit(solution)/shard_map/all_to_all | solution.py:156
  49.9 9.2 collective-permute-start.1
  60.6 19.5 %collective-permute-start.2 = (bf16[2,4,64,1024]{3,2,1,0:T(8,128)(2,1)}, bf16[2,4,64,1024]{3,2,1,0:T(8,128)(2,1)}, u32[]{:S(2)}, u32[]{:S(2)}) collective-permute-start(bf16[2,4,64,1024]{3,2,1,0:T(8,128)(2,1)} %get-tuple-element.100), channel_id=1, source_target_pairs={{1,0},{0,1},{3,2},{2,3},{5,4},{4,5},{7,6},{6,7},{9,8},{8,9},{11,10... | collective-permute-start | bytes 3145736 | tf_op jit(solution)/shard_map/ppermute | solution.py:55
  83.2 42.2 %collective-permute-start.3 = (bf16[2,2,4,64,1024]{4,3,2,1,0:T(8,128)(2,1)}, bf16[2,2,4,64,1024]{4,3,2,1,0:T(8,128)(2,1)}, u32[]{:S(2)}, u32[]{:S(2)}) collective-permute-start(bf16[2,2,4,64,1024]{4,3,2,1,0:T(8,128)(2,1)} %pad_maximum_fusion.4), channel_id=1, source_target_pairs={{8,0},{0,8},{9,1},{1,9},{10,2},{2,10},{11,3},{3,11},{12,4},{4,12},... | collective-permute-start | bytes 6291464 | tf_op jit(solution)/shard_map/ppermute | solution.py:55
  94.9 42.1 %all-to-all-start = ((f32[16,2,128]{2,1,0:T(2,128)}), f32[16,2,128]{2,1,0:T(2,128)S(1)}, u32[]{:S(2)}, u32[]{:S(2)}) async-start(f32[16,2,128]{2,1,0:T(2,128)} %pad_maximum_fusion.20), calls=%async_computation | async-start | bytes 32768 | tf_op jit(solution)/shard_map/all_to_all | solution.py:119
  99.2 195.9 %all-gather.7.cloned.1.call-start = ((), (), s32[]{:S(2)}) async-start(), calls=%async_computation.10 | async-start | bytes 8912896 | tf_op jit(solution)/shard_map/all_gather | solution.py:129
  99.3 25.6 %collective-permute-start = (bf16[4,256,512]{2,1,0:T(8,128)(2,1)S(1)}, bf16[4,256,512]{2,1,0:T(8,128)(2,1)S(1)}, u32[]{:S(2)}, u32[]{:S(2)}) collective-permute-start(bf16[4,256,512]{2,1,0:T(8,128)(2,1)S(1)} %all-to-all-done.1), channel_id=1, source_target_pairs={{1,0},{0,1},{3,2},{2,3},{5,4},{4,5},{7,6},{6,7},{9,8},{8,9},{11,10... | collective-permute-start | bytes 3145736 | tf_op jit(solution)/shard_map/ppermute | solution.py:55
  129.2 302.8 %all-gather.9.cloned.1.call-start = ((), (), s32[]{:S(2)}) async-start(), calls=%async_computation.11 | async-start | bytes 8912896 | tf_op jit(solution)/shard_map/all_gather | solution.py:129
  173.9 7.2 collective-permute-start.5
  183.0 28.5 %collective-permute-start.10 = (bf16[2,64,2048]{2,1,0:T(8,128)(2,1)S(1)}, bf16[2,64,2048]{2,1,0:T(8,128)(2,1)S(1)}, u32[]{:S(2)}, u32[]{:S(2)}) collective-permute-start(bf16[2,64,2048]{2,1,0:T(8,128)(2,1)S(1)} %slice_bitcast_fusion.33), channel_id=1, source_target_pairs={{2,0},{4,2},{6,4},{0,6},{3,1},{5,3},{7,5},{1,7},{10,8},{12,10},{14... | collective-permute-start | bytes 1572872 | tf_op jit(solution)/shard_map/ppermute | solution.py:55
  186.7 41.0 %collective-permute-start.6 = (bf16[4,64,2048]{2,1,0:T(8,128)(2,1)S(1)}, bf16[4,64,2048]{2,1,0:T(8,128)(2,1)S(1)}, u32[]{:S(2)}, u32[]{:S(2)}) collective-permute-start(bf16[4,64,2048]{2,1,0:T(8,128)(2,1)S(1)} %slice_bitcast_fusion.17), channel_id=1, source_target_pairs={{16,0},{0,16},{17,1},{1,17},{18,2},{2,18},{19,3},{3,19},{20,4},{4,... | collective-permute-start | bytes 3145736 | tf_op jit(solution)/shard_map/ppermute | solution.py:55
  211.7 13.7 %collective-permute-start.11 = (bf16[2,64,2048]{2,1,0:T(8,128)(2,1)S(1)}, bf16[2,64,2048]{2,1,0:T(8,128)(2,1)S(1)}, u32[]{:S(2)}, u32[]{:S(2)}) collective-permute-start(bf16[2,64,2048]{2,1,0:T(8,128)(2,1)S(1)} %fusion.30), channel_id=1, source_target_pairs={{2,0},{4,2},{6,4},{0,6},{3,1},{5,3},{7,5},{1,7},{10,8},{12,10},{14... | collective-permute-start | bytes 1572872 | tf_op jit(solution)/shard_map/ppermute | solution.py:55
  225.5 22.7 %collective-permute-start.12 = (bf16[2,64,2048]{2,1,0:T(8,128)(2,1)S(1)}, bf16[2,64,2048]{2,1,0:T(8,128)(2,1)S(1)}, u32[]{:S(2)}, u32[]{:S(2)}) collective-permute-start(bf16[2,64,2048]{2,1,0:T(8,128)(2,1)S(1)} %fusion.29), channel_id=1, source_target_pairs={{2,0},{4,2},{6,4},{0,6},{3,1},{5,3},{7,5},{1,7},{10,8},{12,10},{14... | collective-permute-start | bytes 1572872 | tf_op jit(solution)/shard_map/ppermute | solution.py:55
  228.1 15.9 %collective-permute-start.7 = (bf16[64,2048]{1,0:T(8,128)(2,1)S(1)}, bf16[64,2048]{1,0:T(8,128)(2,1)S(1)}, u32[]{:S(2)}, u32[]{:S(2)}) collective-permute-start(bf16[64,2048]{1,0:T(8,128)(2,1)S(1)} %slice_bitcast_fusion.51), channel_id=1, source_target_pairs={{2,0},{4,2},{6,4},{0,6},{3,1},{5,3},{7,5},{1,7},{10,8},{12,10},{14... | collective-permute-start | bytes 786440 | tf_op jit(solution)/shard_map/ppermute | solution.py:55
  231.7 63.4 %collective-permute-start.14 = (bf16[704,2048]{1,0:T(8,128)(2,1)S(1)}, bf16[704,2048]{1,0:T(8,128)(2,1)}, u32[]{:S(2)}, u32[]{:S(2)}) collective-permute-start(bf16[704,2048]{1,0:T(8,128)(2,1)S(1)} %bitcast.477), channel_id=1, source_target_pairs={{1,0},{0,1},{3,2},{2,3},{5,4},{4,5},{7,6},{6,7},{9,8},{8,9},{11,10... | collective-permute-start | bytes 8650760 | tf_op jit(solution)/shard_map/ppermute | solution.py:55
  244.1 8.1 collective-permute-start.8
  248.4 8.4 collective-permute-start.13
  252.2 8.5 collective-permute-start.9
  295.2 62.7 %collective-permute-start.15 = (bf16[704,2048]{1,0:T(8,128)(2,1)}, bf16[704,2048]{1,0:T(8,128)(2,1)}, u32[]{:S(2)}, u32[]{:S(2)}) collective-permute-start(bf16[704,2048]{1,0:T(8,128)(2,1)} %get-tuple-element.45), channel_id=1, source_target_pairs={{1,0},{0,1},{3,2},{2,3},{5,4},{4,5},{7,6},{6,7},{9,8},{8,9},{11,10... | collective-permute-start | bytes 8650760 | tf_op jit(solution)/shard_map/ppermute | solution.py:55
  360.1 33.7 %all-to-all-start.3 = ((f32[16,1,128]{2,1,0:T(1,128)}), f32[16,1,128]{2,1,0:T(1,128)S(1)}, u32[]{:S(2)}, u32[]{:S(2)}) async-start(f32[16,1,128]{2,1,0:T(1,128)} %bitcast.66), calls=%async_computation.3 | async-start | bytes 16384 | tf_op jit(solution)/shard_map/all_to_all | solution.py:119
  364.0 449.5 %all-gather.11.cloned.1.call-start = ((), (), s32[]{:S(2)}) async-start(), calls=%async_computation.12 | async-start | bytes 8912896 | tf_op jit(solution)/shard_map/all_gather | solution.py:129
  364.1 65.2 %collective-permute-start.16 = (bf16[704,2048]{1,0:T(8,128)(2,1)}, bf16[704,2048]{1,0:T(8,128)(2,1)}, u32[]{:S(2)}, u32[]{:S(2)}) collective-permute-start(bf16[704,2048]{1,0:T(8,128)(2,1)} %get-tuple-element.50), channel_id=1, source_target_pairs={{1,0},{0,1},{3,2},{2,3},{5,4},{4,5},{7,6},{6,7},{9,8},{8,9},{11,10... | collective-permute-start | bytes 8650760 | tf_op jit(solution)/shard_map/ppermute | solution.py:55
  500.9 7.2 collective-permute-start.17
  512.3 28.3 %collective-permute-start.18 = (bf16[4,64,2048]{2,1,0:T(8,128)(2,1)S(1)}, bf16[4,64,2048]{2,1,0:T(8,128)(2,1)S(1)}, u32[]{:S(2)}, u32[]{:S(2)}) collective-permute-start(bf16[4,64,2048]{2,1,0:T(8,128)(2,1)S(1)} %slice_bitcast_fusion.15), channel_id=1, source_target_pairs={{16,0},{0,16},{17,1},{1,17},{18,2},{2,18},{19,3},{3,19},{20,4},{4,... | collective-permute-start | bytes 3145736 | tf_op jit(solution)/shard_map/ppermute | solution.py:55
  539.0 14.8 %collective-permute-start.22 = (bf16[2,64,2048]{2,1,0:T(8,128)(2,1)S(1)}, bf16[2,64,2048]{2,1,0:T(8,128)(2,1)S(1)}, u32[]{:S(2)}, u32[]{:S(2)}) collective-permute-start(bf16[2,64,2048]{2,1,0:T(8,128)(2,1)S(1)} %slice_bitcast_fusion.29), channel_id=1, source_target_pairs={{2,0},{4,2},{6,4},{0,6},{3,1},{5,3},{7,5},{1,7},{10,8},{12,10},{14... | collective-permute-start | bytes 1572872 | tf_op jit(solution)/shard_map/ppermute | solution.py:55
  542.3 17.2 %collective-permute-start.19 = (bf16[64,2048]{1,0:T(8,128)(2,1)S(1)}, bf16[64,2048]{1,0:T(8,128)(2,1)S(1)}, u32[]{:S(2)}, u32[]{:S(2)}) collective-permute-start(bf16[64,2048]{1,0:T(8,128)(2,1)S(1)} %slice_bitcast_fusion.45), channel_id=1, source_target_pairs={{2,0},{4,2},{6,4},{0,6},{3,1},{5,3},{7,5},{1,7},{10,8},{12,10},{14... | collective-permute-start | bytes 786440 | tf_op jit(solution)/shard_map/ppermute | solution.py:55
  555.0 15.8 %collective-permute-start.23 = (bf16[2,64,2048]{2,1,0:T(8,128)(2,1)S(1)}, bf16[2,64,2048]{2,1,0:T(8,128)(2,1)S(1)}, u32[]{:S(2)}, u32[]{:S(2)}) collective-permute-start(bf16[2,64,2048]{2,1,0:T(8,128)(2,1)S(1)} %fusion.27), channel_id=1, source_target_pairs={{2,0},{4,2},{6,4},{0,6},{3,1},{5,3},{7,5},{1,7},{10,8},{12,10},{14... | collective-permute-start | bytes 1572872 | tf_op jit(solution)/shard_map/ppermute | solution.py:55
  559.5 16.8 %collective-permute-start.20 = (bf16[64,2048]{1,0:T(8,128)(2,1)S(1)}, bf16[64,2048]{1,0:T(8,128)(2,1)S(1)}, u32[]{:S(2)}, u32[]{:S(2)}) collective-permute-start(bf16[64,2048]{1,0:T(8,128)(2,1)S(1)} %fusion.41), channel_id=1, source_target_pairs={{2,0},{4,2},{6,4},{0,6},{3,1},{5,3},{7,5},{1,7},{10,8},{12,10},{14... | collective-permute-start | bytes 786440 | tf_op jit(solution)/shard_map/ppermute | solution.py:55
  572.0 16.5 %collective-permute-start.24 = (bf16[2,64,2048]{2,1,0:T(8,128)(2,1)S(1)}, bf16[2,64,2048]{2,1,0:T(8,128)(2,1)S(1)}, u32[]{:S(2)}, u32[]{:S(2)}) collective-permute-start(bf16[2,64,2048]{2,1,0:T(8,128)(2,1)S(1)} %fusion.26), channel_id=1, source_target_pairs={{2,0},{4,2},{6,4},{0,6},{3,1},{5,3},{7,5},{1,7},{10,8},{12,10},{14... | collective-permute-start | bytes 1572872 | tf_op jit(solution)/shard_map/ppermute | solution.py:55
  576.4 15.8 %collective-permute-start.21 = (bf16[64,2048]{1,0:T(8,128)(2,1)S(1)}, bf16[64,2048]{1,0:T(8,128)(2,1)S(1)}, u32[]{:S(2)}, u32[]{:S(2)}) collective-permute-start(bf16[64,2048]{1,0:T(8,128)(2,1)S(1)} %fusion.40), channel_id=1, source_target_pairs={{2,0},{4,2},{6,4},{0,6},{3,1},{5,3},{7,5},{1,7},{10,8},{12,10},{14... | collective-permute-start | bytes 786440 | tf_op jit(solution)/shard_map/ppermute | solution.py:55
  589.7 6.4 collective-permute-start.25
  600.0 489.4 %reduce-scatter.2.cloned.1.call-start = ((), (), s32[]{:S(2)}) async-start(), calls=%async_computation.13 | async-start | bytes 8912896 | tf_op jit(solution)/shard_map/reduce_scatter | solution.py:133
  610.9 65.7 %collective-permute-start.51 = (bf16[704,2048]{1,0:T(8,128)(2,1)}, bf16[704,2048]{1,0:T(8,128)(2,1)}, u32[]{:S(2)}, u32[]{:S(2)}) collective-permute-start(bf16[704,2048]{1,0:T(8,128)(2,1)} %convolution_convert_fusion.1), channel_id=1, source_target_pairs={{1,0},{0,1},{3,2},{2,3},{5,4},{4,5},{7,6},{6,7},{9,8},{8,9},{11,10... | collective-permute-start | bytes 8650760 | tf_op jit(solution)/shard_map/ppermute | solution.py:55
  612.7 19.3 %collective-permute-start.40 = (f32[7,2048]{1,0:T(8,128)S(1)}, f32[7,2048]{1,0:T(8,128)S(1)}, u32[]{:S(2)}, u32[]{:S(2)}) collective-permute-start(f32[7,2048]{1,0:T(8,128)S(1)} %pad_maximum_fusion.19), channel_id=1, source_target_pairs={{0,16},{16,0},{1,17},{17,1},{2,18},{18,2},{3,19},{19,3},{4,20},{20... | collective-permute-start | bytes 172040 | tf_op jit(solution)/shard_map/ppermute | solution.py:92
  631.4 164.7 %collective-permute-start.50 = (bf16[1408,2048]{1,0:T(8,128)(2,1)}, bf16[1408,2048]{1,0:T(8,128)(2,1)}, u32[]{:S(2)}, u32[]{:S(2)}) collective-permute-start(bf16[1408,2048]{1,0:T(8,128)(2,1)} %convolution_convert_fusion), channel_id=1, source_target_pairs={{1,0},{0,1},{3,2},{2,3},{5,4},{4,5},{7,6},{6,7},{9,8},{8,9},{11,10... | collective-permute-start | bytes 17301512 | tf_op jit(solution)/shard_map/ppermute | solution.py:55
  632.2 11.6 %collective-permute-start.41 = (f32[7,2048]{1,0:T(8,128)S(1)}, f32[7,2048]{1,0:T(8,128)S(1)}, u32[]{:S(2)}, u32[]{:S(2)}) collective-permute-start(f32[7,2048]{1,0:T(8,128)S(1)} %fusion.64), channel_id=1, source_target_pairs={{0,8},{8,0},{1,9},{9,1},{2,10},{10,2},{3,11},{11,3},{4,12},{12,4},... | collective-permute-start | bytes 172040 | tf_op jit(solution)/shard_map/ppermute | solution.py:92
  643.8 12.6 %collective-permute-start.42 = (f32[7,2048]{1,0:T(8,128)S(1)}, f32[7,2048]{1,0:T(8,128)S(1)}, u32[]{:S(2)}, u32[]{:S(2)}) collective-permute-start(f32[7,2048]{1,0:T(8,128)S(1)} %add.243), channel_id=1, source_target_pairs={{0,2},{2,0},{4,6},{6,4},{1,3},{3,1},{5,7},{7,5},{8,10},{10,8},{12,... | collective-permute-start | bytes 172040 | tf_op jit(solution)/shard_map/ppermute | solution.py:92
  656.5 30.9 %collective-permute-start.43 = (f32[7,2048]{1,0:T(8,128)S(1)}, f32[7,2048]{1,0:T(8,128)S(1)}, u32[]{:S(2)}, u32[]{:S(2)}) collective-permute-start(f32[7,2048]{1,0:T(8,128)S(1)} %add.244), channel_id=1, source_target_pairs={{0,4},{2,6},{4,0},{6,2},{1,5},{3,7},{5,1},{7,3},{8,12},{10,14},{12... | collective-permute-start | bytes 172040 | tf_op jit(solution)/shard_map/ppermute | solution.py:92
  687.4 124.9 %collective-permute-start.44 = (f32[7,2048]{1,0:T(8,128)S(1)}, f32[7,2048]{1,0:T(8,128)S(1)}, u32[]{:S(2)}, u32[]{:S(2)}) collective-permute-start(f32[7,2048]{1,0:T(8,128)S(1)} %add.245), channel_id=1, source_target_pairs={{0,1},{1,0},{2,3},{3,2},{4,5},{5,4},{6,7},{7,6},{8,9},{9,8},{10,11... | collective-permute-start | bytes 172040 | tf_op jit(solution)/shard_map/ppermute | solution.py:92
  878.7 28.0 %all-to-all-start.5 = ((f32[16,1,128]{2,1,0:T(1,128)}), f32[16,1,128]{2,1,0:T(1,128)S(1)}, u32[]{:S(2)}, u32[]{:S(2)}) async-start(f32[16,1,128]{2,1,0:T(1,128)} %get-tuple-element.59), calls=%async_computation.6 | async-start | bytes 16384 | tf_op jit(solution)/shard_map/all_to_all | solution.py:123
  886.1 30.9 %collective-permute-start.48 = (bf16[4,256,512]{2,1,0:T(8,128)(2,1)}, bf16[4,256,512]{2,1,0:T(8,128)(2,1)S(1)}, u32[]{:S(2)}, u32[]{:S(2)}) collective-permute-start(bf16[4,256,512]{2,1,0:T(8,128)(2,1)} %fusion.10), channel_id=1, source_target_pairs={{1,0},{0,1},{3,2},{2,3},{5,4},{4,5},{7,6},{6,7},{9,8},{8,9},{11,10... | collective-permute-start | bytes 3145736 | tf_op jit(solution)/shard_map/ppermute | solution.py:55
  892.3 14.5 %collective-permute-start.45 = (bf16[2,512,1024]{2,1,0:T(8,128)(2,1)S(1)}, bf16[2,512,1024]{2,1,0:T(8,128)(2,1)}, u32[]{:S(2)}, u32[]{:S(2)}) collective-permute-start(bf16[2,512,1024]{2,1,0:T(8,128)(2,1)S(1)} %fusion.3), channel_id=1, source_target_pairs={{8,0},{0,8},{9,1},{1,9},{10,2},{2,10},{11,3},{3,11},{12,4},{4,12},... | collective-permute-start | bytes 6291464 | tf_op jit(solution)/shard_map/ppermute | solution.py:55
  897.9 82.8 %collective-permute-start.26 = (bf16[2,4,128,2048]{3,2,0,1:T(8,128)(2,1)}, bf16[2,4,128,2048]{3,2,0,1:T(8,128)(2,1)}, u32[]{:S(2)}, u32[]{:S(2)}) collective-permute-start(bf16[2,4,128,2048]{3,2,0,1:T(8,128)(2,1)} %slice_bitcast_fusion.3), channel_id=1, source_target_pairs={{8,0},{0,8},{9,1},{1,9},{10,2},{2,10},{11,3},{3,11},{12,4},{4,12},... | collective-permute-start | bytes 12582920 | tf_op jit(solution)/shard_map/ppermute | solution.py:55
  906.1 50.8 %collective-permute-start.49 = (bf16[256,2048]{1,0:T(8,128)(2,1)}, bf16[256,2048]{1,0:T(8,128)(2,1)}, u32[]{:S(2)}, u32[]{:S(2)}) collective-permute-start(bf16[256,2048]{1,0:T(8,128)(2,1)} %select_convert_fusion.1), channel_id=1, source_target_pairs={{1,0},{0,1},{3,2},{2,3},{5,4},{4,5},{7,6},{6,7},{9,8},{8,9},{11,10... | collective-permute-start | bytes 3145736 | tf_op jit(solution)/shard_map/ppermute | solution.py:55
  914.7 36.6 %collective-permute-start.46 = (bf16[512,1024]{1,0:T(8,128)(2,1)S(1)}, bf16[512,1024]{1,0:T(8,128)(2,1)}, u32[]{:S(2)}, u32[]{:S(2)}) collective-permute-start(bf16[512,1024]{1,0:T(8,128)(2,1)S(1)} %fusion.9), channel_id=1, source_target_pairs={{16,0},{0,16},{17,1},{1,17},{18,2},{2,18},{19,3},{3,19},{20,4},{4,... | collective-permute-start | bytes 3145736 | tf_op jit(solution)/shard_map/ppermute | solution.py:55
  918.5 55.0 %all-to-all-start.7 = ((bf16[4,256,512]{2,1,0:T(8,128)(2,1)}), bf16[4,256,512]{2,1,0:T(8,128)(2,1)S(1)}, u32[]{:S(2)}, u32[]{:S(2)}) async-start(bf16[4,256,512]{2,1,0:T(8,128)(2,1)} %fusion.7), calls=%async_computation.8 | async-start | bytes 2097152 | tf_op jit(solution)/shard_map/all_to_all | solution.py:171
  955.4 19.7 %collective-permute-start.47 = (bf16[4,64,1024]{2,1,0:T(8,128)(2,1)}, bf16[4,64,1024]{2,1,0:T(8,128)(2,1)}, u32[]{:S(2)}, u32[]{:S(2)}) collective-permute-start(bf16[4,64,1024]{2,1,0:T(8,128)(2,1)} %fusion.33), channel_id=1, source_target_pairs={{1,0},{0,1},{3,2},{2,3},{5,4},{4,5},{7,6},{6,7},{9,8},{8,9},{11,10... | collective-permute-start | bytes 1572872 | tf_op jit(solution)/shard_map/ppermute | solution.py:55
  977.2 20.7 %all-to-all-start.6 = ((bf16[4,64,1024]{2,1,0:T(8,128)(2,1)}), bf16[4,64,1024]{2,1,0:T(8,128)(2,1)S(1)}, u32[]{:S(2)}, u32[]{:S(2)}) async-start(bf16[4,64,1024]{2,1,0:T(8,128)(2,1)} %fusion.31), calls=%async_computation.7 | async-start | bytes 1048576 | tf_op jit(solution)/shard_map/all_to_all | solution.py:171
  986.1 30.5 %collective-permute-start.27 = (bf16[4,64,2048]{2,1,0:T(8,128)(2,1)}, bf16[4,64,2048]{2,1,0:T(8,128)(2,1)}, u32[]{:S(2)}, u32[]{:S(2)}) collective-permute-start(bf16[4,64,2048]{2,1,0:T(8,128)(2,1)} %slice_bitcast_fusion.13), channel_id=1, source_target_pairs={{16,0},{0,16},{17,1},{1,17},{18,2},{2,18},{19,3},{3,19},{20,4},{4,... | collective-permute-start | bytes 3145736 | tf_op jit(solution)/shard_map/ppermute | solution.py:55
  988.7 33.8 %collective-permute-start.31 = (bf16[2,64,2048]{2,1,0:T(8,128)(2,1)S(1)}, bf16[2,64,2048]{2,1,0:T(8,128)(2,1)S(1)}, u32[]{:S(2)}, u32[]{:S(2)}) collective-permute-start(bf16[2,64,2048]{2,1,0:T(8,128)(2,1)S(1)} %slice_bitcast_fusion.25), channel_id=1, source_target_pairs={{2,0},{4,2},{6,4},{0,6},{3,1},{5,3},{7,5},{1,7},{10,8},{12,10},{14... | collective-permute-start | bytes 1572872 | tf_op jit(solution)/shard_map/ppermute | solution.py:55
  1018.7 10.6 collective-permute-start.28
  1023.7 16.8 %collective-permute-start.32 = (bf16[2,64,2048]{2,1,0:T(8,128)(2,1)S(1)}, bf16[2,64,2048]{2,1,0:T(8,128)(2,1)S(1)}, u32[]{:S(2)}, u32[]{:S(2)}) collective-permute-start(bf16[2,64,2048]{2,1,0:T(8,128)(2,1)S(1)} %fusion.24), channel_id=1, source_target_pairs={{2,0},{4,2},{6,4},{0,6},{3,1},{5,3},{7,5},{1,7},{10,8},{12,10},{14... | collective-permute-start | bytes 1572872 | tf_op jit(solution)/shard_map/ppermute | solution.py:55
  1029.4 16.7 %collective-permute-start.29 = (bf16[64,2048]{1,0:T(8,128)(2,1)S(1)}, bf16[64,2048]{1,0:T(8,128)(2,1)S(1)}, u32[]{:S(2)}, u32[]{:S(2)}) collective-permute-start(bf16[64,2048]{1,0:T(8,128)(2,1)S(1)} %fusion.37), channel_id=1, source_target_pairs={{2,0},{4,2},{6,4},{0,6},{3,1},{5,3},{7,5},{1,7},{10,8},{12,10},{14... | collective-permute-start | bytes 786440 | tf_op jit(solution)/shard_map/ppermute | solution.py:55
  1041.7 15.7 %collective-permute-start.33 = (bf16[2,64,2048]{2,1,0:T(8,128)(2,1)S(1)}, bf16[2,64,2048]{2,1,0:T(8,128)(2,1)S(1)}, u32[]{:S(2)}, u32[]{:S(2)}) collective-permute-start(bf16[2,64,2048]{2,1,0:T(8,128)(2,1)S(1)} %fusion.23), channel_id=1, source_target_pairs={{2,0},{4,2},{6,4},{0,6},{3,1},{5,3},{7,5},{1,7},{10,8},{12,10},{14... | collective-permute-start | bytes 1572872 | tf_op jit(solution)/shard_map/ppermute | solution.py:55
  1046.2 14.4 %collective-permute-start.30 = (bf16[64,2048]{1,0:T(8,128)(2,1)S(1)}, bf16[64,2048]{1,0:T(8,128)(2,1)S(1)}, u32[]{:S(2)}, u32[]{:S(2)}) collective-permute-start(bf16[64,2048]{1,0:T(8,128)(2,1)S(1)} %fusion.36), channel_id=1, source_target_pairs={{2,0},{4,2},{6,4},{0,6},{3,1},{5,3},{7,5},{1,7},{10,8},{12,10},{14... | collective-permute-start | bytes 786440 | tf_op jit(solution)/shard_map/ppermute | solution.py:55
  1058.6 6.6 collective-permute-start.34
  1067.6 4.8 collective-permute-start.35
  1072.4 1.3 collective-permute-start.36
  1073.8 4.3 collective-permute-start.37
  1078.1 5.8 collective-permute-start.38
  1083.9 4.3 collective-permute-start.39
  (68 other events, 2720.3 us)
Sparse Core Ops, SparseCore 0:
  11.8 98.2 all-gather.4
  129.4 83.2 all-gather.6
  358.0 74.0 all-gather.8
  600.2 77.9 all-gather.10
  878.8 144.1 reduce-scatter.1

commit v4 on v3

--- a/solution.py
+++ b/solution.py
@@ -62,12 +62,15 @@
     return parts
 
 
-def ring_scatter(blocks, axis):
+def ring_scatter(blocks, axis, after=None):
     size = lax.axis_size(axis)
     travelling = blocks[1].astype(BF16)
     for j in range(2, size):
         travelling = (shift(travelling, axis).astype(F32) + blocks[j]).astype(BF16)
-    return shift(travelling, axis).astype(F32) + blocks[0]
+    arrived = shift(travelling, axis)
+    if after is not None:
+        arrived, _ = lax.optimization_barrier((arrived, after))
+    return arrived.astype(F32) + blocks[0]
 
 
 def in_order(parts, axis, place=0):
@@ -153,14 +156,10 @@
 
 
 def gather_heads(weight):
-    return lax.all_to_all(
-        jnp.stack(head_columns(weight)), "o", split_axis=0, concat_axis=0, tiled=True
-    )
-
-
-def gather_query(weight):
-    parts = ring_gather(gather_heads(weight), "i")
-    return in_order(parts, "i", 1).reshape(-1, parts[0].shape[2])
+    parts = ring_gather(weight, "i")
+    sent = in_order([jnp.stack(head_columns(one)) for one in parts], "i", 1)
+    here = lax.all_to_all(sent, "o", split_axis=0, concat_axis=0, tiled=True)
+    return here.reshape(-1, here.shape[-1])
 
 
 def scatter_rows(grad):
@@ -180,11 +179,9 @@
     )
 
 
-def gather_kv(weight):
-    here = ring_gather(gather_heads(weight), "y")
-    here = ring_gather(jnp.stack(here), "i")
-    here = ring_gather(jnp.stack(here), "c")
-    whole = in_order([in_order([in_order(list(one), "y", 0) for one in two], "i", 2) for two in here], "c", 1)
+def gather_kv(rows):
+    here = ring_gather(jnp.stack(ring_gather(rows, "y")), "c")
+    whole = in_order([in_order(list(one), "y", 0) for one in here], "c", 1)
     return whole.reshape(-1, whole.shape[-1])
 
 
@@ -212,7 +209,6 @@
 
 
 def part_by_rings(rows):
-    rows = ring_low([rows[k] for k in range(rows.shape[0])], "c")
     half = rows.shape[2] // 2
     first, second = rows[:, :, :half], rows[:, :, half:]
     first = ring_low([first[k] for k in range(first.shape[0])], "y")
@@ -275,16 +271,17 @@
     return exponent / jnp.sum(exponent, axis=-1, keepdims=True)
 
 
-def place_rows(places_ref, part_ref, value, first, length):
+def place_rows(places_ref, part_ref, value, length):
     count = part_ref.shape[2]
-    for seq in range(value.shape[0] // length):
-        slot = lax.rem(first + seq - places_ref[2] + count, count)
+    for seq in range(count):
+        slot = lax.rem(seq - places_ref[2] + count, count)
         part_ref[0, 0, slot] = value[seq * length : (seq + 1) * length]
 
 
 def attend_kernel(
     places_ref, x_ref, info_ref, cos_ref, sin_ref, slab_ref, out_ref, qkv_ref, gated_ref, part_ref
 ):
+    del places_ref
     length = cos_ref.shape[0]
     span = out_ref.shape[0]
     raw = nn(x_ref[...], slab_ref[...])
@@ -307,7 +304,7 @@
         gated = (heads_nn(probs.astype(BF16), jnp.stack(values)) * gate[None]).astype(BF16)
         for number, at in enumerate(starts):
             gated_ref[rows, at : at + HD] = gated[number]
-    place_rows(places_ref, part_ref, nn(gated_ref[...], out_ref[...]).astype(BF16), 0, length)
+    part_ref[...] = nn(gated_ref[...], out_ref[...]).astype(BF16)
 
 
 def attend_back_kernel(
@@ -361,7 +358,7 @@
         d_gain_ref[...] = jnp.zeros_like(d_gain_ref)
 
     d_gain_ref[...] += jnp.sum(d_input * x_ref[...].astype(F32), axis=0, keepdims=True)
-    place_rows(places_ref, part_ref, d_input.astype(BF16), 0, length)
+    place_rows(places_ref, part_ref, d_input.astype(BF16), length)
 
 
 def fixed(shape):
@@ -376,11 +373,10 @@
     return pl.BlockSpec((seqs, kinds, length), lambda step, places: (step, 0, 0))
 
 
-def place_spec(high, length, width, steps):
+def place_spec(high, length, width):
     def index(step, places):
-        pair = lax.div(step, steps)
-        low = lax.rem(lax.rem(pair, 2) - places[1] + 2, 2)
-        return (low, lax.rem(lax.div(pair, 2) - places[0] + high, high), 0, 0, 0)
+        low = lax.rem(lax.rem(step, 2) - places[1] + 2, 2)
+        return (low, lax.rem(lax.div(step, 2) - places[0] + high, high), 0, 0, 0)
 
     return pl.BlockSpec((1, 1, OUTER, length, width), index)
 
@@ -407,7 +403,6 @@
     length = cosine.shape[0]
     step = OUTER * length
     span = out_mat.shape[0]
-    high = count // (2 * step)
     return call(
         attend_kernel,
         "attend",
@@ -420,8 +415,8 @@
             fixed(slab.shape),
             fixed(out_mat.shape),
         ],
-        [rows_spec(step, 3 * span), rows_spec(step, span), place_spec(high, length, width, 1)],
-        [shape((count, 3 * span)), shape((count, span)), shape((2, high, OUTER, length, width))],
+        [rows_spec(step, 3 * span), rows_spec(step, span), rows_spec(step, width)],
+        [shape((count, 3 * span)), shape((count, span)), shape((count, width))],
         2 * count * width * 4 * span + 4 * count * length * span,
         4 * count * (width + 2 * span),
         (places, rows, info, cosine, sine, slab, out_mat),
@@ -450,7 +445,7 @@
         ],
         [
             rows_spec(step, 3 * span),
-            place_spec(high, length, width, 1),
+            place_spec(high, length, width),
             info_spec(OUTER, 1, length),
             fixed((1, width)),
         ],
@@ -467,6 +462,7 @@
 
 
 def units_kernel(parts, places_ref, x_ref, info_ref, *refs):
+    del places_ref
     d_units_refs, up_refs = refs[:parts], refs[parts : 3 * parts]
     d_both_refs, gated_refs = refs[3 * parts : 4 * parts], refs[4 * parts : 5 * parts]
     back_ref, d_gate_ref = refs[5 * parts :]
@@ -493,8 +489,7 @@
         d_both_refs[part][:, :units] = d_first
         d_both_refs[part][:, units:] = d_second
         back = back + nn(d_first, first_ref[...]) + nn(d_second, second_ref[...])
-    first = lax.rem(pl.program_id(0), OUTER // seqs) * seqs
-    place_rows(places_ref, back_ref, back.astype(BF16), first, length)
+    back_ref[...] = back.astype(BF16)
     for seq in range(seqs):
         column = jnp.broadcast_to(d_gate[seq * length : (seq + 1) * length], (length, length))
         d_gate_ref[seq] = column.T[:1]
@@ -506,7 +501,6 @@
     parts = 1 + len(other_up) // 2
     units = d_units[0].shape[1]
     seqs = ROW_STEP // length
-    high = count // (2 * OUTER * length)
     own_specs = [
         pl.BlockSpec((units, width), lambda step, places, half=half: (half, 0)) for half in range(2)
     ]
@@ -520,13 +514,10 @@
         + [fixed(one.shape) for one in other_up],
         [rows_spec(ROW_STEP, 2 * units)] * parts
         + [rows_spec(ROW_STEP, units)] * parts
-        + [place_spec(high, length, width, OUTER // seqs), info_spec(seqs, 1, length)],
+        + [rows_spec(ROW_STEP, width), info_spec(seqs, 1, length)],
         [shape((count, 2 * units))] * parts
         + [shape((count, units))] * parts
-        + [
-            shape((2, high, OUTER, length, width)),
-            shape((count // length, 1, length), F32),
-        ],
+        + [shape((count, width)), shape((count // length, 1, length), F32)],
         8 * count * width * units * parts,
         4 * count * (width + 2 * units * parts),
         (places, rows, info, *d_units, own_up, own_up, *other_up),
@@ -560,12 +551,15 @@
     places = own_places()
     tie = lax.optimization_barrier
 
-    kv_mat = gather_kv(kv_weight)
-    query_mat = gather_query(query_weight[0])
+    kv_rows = gather_heads(kv_weight)
+    kv_mat = gather_kv(kv_rows)
+    query_mat = gather_heads(query_weight[0])
     slab = jnp.concatenate([query_mat, kv_mat], axis=1)
-    out_mat = in_order(ring_gather(out_weight[0], "i"), "i").reshape(span, width)
+    out_source, _ = tie((out_weight[0], kv_rows))
+    out_parts = ring_gather(out_source, "i")
+    out_mat = in_order(out_parts, "i").reshape(span, width)
     own_up = up_weight[0].reshape(-1, width)
-    down_source, _ = tie((down_weight[0], slab))
+    down_source, _ = tie((down_weight[0], out_parts[-1]))
     down_parts = ring_gather(down_source, "i")
 
     residual = hidden_in.astype(F32)
@@ -574,35 +568,44 @@
     att_gate, att_onehot = pair_gates(attn_input, att_router, att_route, experts)
     info = to_experts(att_gate, att_onehot, segment_ids[0].astype(F32))
     all_attn = meet(attn_input)
-    cot_low, all_attn = tie((cotangent.astype(BF16), all_attn))
+    cot_low, _ = tie((cotangent.astype(BF16), kv_rows))
     all_cot = meet(cot_low)
+    slab, down_parts = tie((slab, down_parts))
     qkv, gated, branch = attend(places, all_attn, info, cosine, sine_table, slab, out_mat)
-    branch = part_by_rings(branch)
-
-    branch, down_parts, all_cot = tie((branch, down_parts, all_cot))
-    first_source, _ = tie((up_weight[0, 0], down_parts[-1]))
+    first_source, branch = tie((up_weight[0, 0], branch))
     first_parts = ring_gather(first_source, "i")
+    branch = part(branch)
+
+    all_cot, first_parts = tie((all_cot, first_parts))
+    d_units = [mm("td,fd->tf", all_cot, down).astype(BF16) for down in down_parts]
+    branch, d_units = tie((branch, d_units))
     middle = residual + branch.astype(F32) + att_bias
     normed_two, inverse_two = norm_rows(middle, norm_gain2)
     mlp_input = normed_two.astype(BF16)
     mlp_gate, mlp_onehot = pair_gates(mlp_input, mlp_router, mlp_route, experts)
-    mlp_input, first_parts = tie((mlp_input, first_parts))
-    second_source, _ = tie((up_weight[0, 1], first_parts[-1]))
+    second_source, mlp_input = tie((up_weight[0, 1], mlp_input))
     second_parts = ring_gather(second_source, "i")
+    all_mlp = meet(mlp_input)
     gate_m = to_experts(mlp_gate, mlp_onehot, None)
-    all_mlp = meet(mlp_input)
-    d_units = [mm("td,fd->tf", all_cot, down).astype(BF16) for down in down_parts]
+    gate_m, second_parts = tie((gate_m, second_parts))
     other_up = [one for pair in zip(first_parts[1:], second_parts[1:]) for one in pair]
     found = run_units(places, all_mlp, gate_m, d_units, own_up, other_up)
     d_both, gated_units = found[:inner], found[inner : 2 * inner]
     rows_back, d_gate_m = found[2 * inner :]
+    d_mlp_input = part(rows_back)
     d_mlp_gate = from_experts(d_gate_m[:, 0], mlp_onehot, experts)
-    d_mlp_input = part_by_rings(rows_back).astype(F32)
+    grad_up = [mm("tf,td->fd", d_here, all_mlp) for d_here in d_both]
+    grad_down = [mm("tf,td->fd", here, all_cot) for here in gated_units]
+    rows_out = None
+    for units_here, down in zip(gated_units, down_parts):
+        ahead = mm("tf,fd->td", units_here, down)
+        rows_out = ahead if rows_out is None else rows_out + ahead
+    rows_out = rows_out.astype(BF16)
     d_mlp_router, d_mlp_from_router = gates_back(
         mlp_gate, mlp_onehot, d_mlp_gate, mlp_input, mlp_router
     )
     d_norm_two, d_gain_two = norm_back(
-        middle, inverse_two, norm_gain2, d_mlp_input + d_mlp_from_router
+        middle, inverse_two, norm_gain2, d_mlp_input.astype(F32) + d_mlp_from_router
     )
     d_middle = cotangent + d_norm_two
     summed_one = sum_all(
@@ -613,28 +616,25 @@
             ]
         )
     )
-    d_upper = ring_scatter([mm("tf,td->fd", d_here, all_mlp) for d_here in d_both], "i")
-    d_upper = d_upper.reshape(up_weight.shape)
-    d_lower = ring_scatter([mm("tf,td->fd", here, all_cot) for here in gated_units], "i")[None]
-    rows_out = None
-    for units_here, down in zip(gated_units, down_parts):
-        ahead = mm("tf,fd->td", units_here, down)
-        rows_out = ahead if rows_out is None else rows_out + ahead
-    rows_out = rows_out.astype(BF16)
 
     all_mid = meet(d_middle.astype(BF16))
     rows_out, all_mid = tie((rows_out, all_mid))
-    layer_out = middle + part(rows_out).astype(F32) + mlp_bias
     d_qkv, rows_one, d_gate_a, d_gain_a = attend_back(
         places, all_mid, info, cosine, sine_table, qkv, all_attn, slab, out_mat
     )
+    rows_one = ring_low([rows_one[0], rows_one[1]], "c")
+    d_qkv, rows_one = tie((d_qkv, rows_one))
+    d_attn_input = part_by_rings(rows_one).astype(F32)
     d_att_gate = from_experts(d_gate_a[:, 0], att_onehot, experts)
-    d_attn_input = part_by_rings(rows_one).astype(F32)
-    d_out = mm("tf,td->fd", gated, all_mid).reshape(inner, -1, width)
-    d_output = ring_scatter(from_order([d_out[k] for k in range(inner)], "i"), "i")[None]
     d_slab = mm("td,tf->df", all_attn, d_qkv)
     d_query = scatter_rows(d_slab[:, :span])[None]
     d_kv_weight = scatter_kv(d_slab[:, span:])
+    d_out = mm("tf,td->fd", gated, all_mid).reshape(inner, -1, width)
+    d_output = ring_scatter(from_order([d_out[k] for k in range(inner)], "i"), "i")[None]
+    layer_out = middle + part(rows_out).astype(F32) + mlp_bias
+    d_upper = ring_scatter(grad_up, "i", d_attn_input)
+    d_upper = d_upper.reshape(up_weight.shape)
+    d_lower = ring_scatter(grad_down, "i", d_attn_input)[None]
     d_att_router, d_att_from_router = gates_back(
         att_gate, att_onehot, d_att_gate, attn_input, att_router
     )

time: 1100 us -> 1110 us (level)
  waiting for transfers between devices: 532 us -> 605 us
  starting transfers between devices: 125 us -> 77.3 us
    ppermute x42 -> x24, waiting for transfers between devices: 464 us -> 235 us  [shift(): return lax.ppermute(value, axis, [((k + 1) % size, k) for k in range(size)])]
    ppermute x10, waiting for transfers between devices: 12.7 us -> 130 us  [sum_all(): lax.ppermute(value, axis, [(k, k ^ step) for k in range(size)])]
    reduce_scatter x1 -> x3, waiting for transfers between devices: 0.01 us -> 112 us  [part(): return lax.psum_scatter(rows, GROUP, scatter_dimension=0, tiled=True)]
    all_to_all x2, waiting for transfers between devices: 34 us -> 108 us  [gather_heads(): here = lax.all_to_all(sent, 'o', split_axis=0, concat_axis=0, tiled=True)]
    ppermute x42 -> x24, starting transfers between devices: 80 us -> 35.5 us  [shift(): return lax.ppermute(value, axis, [((k + 1) % size, k) for k in range(size)])]
    all_to_all x1, blocking collectives: 24.9 us -> 9.36 us  [from_experts(): lax.all_to_all(d_gates, GROUP, split_axis=0, concat_axis=0, tiled=True)]
    convert_element_type x27 -> x9, other arithmetic: 20.4 us -> 5.49 us  [add_low(): return (first.astype(F32) + second.astype(F32)).astype(BF16)]
    add x2 -> x3, other arithmetic: 8.97 us -> 22.1 us  [ring_scatter(): return arrived.astype(F32) + blocks[0]]
  transfers between devices with their start and end apart: 64 -> 47, of which waited for: 37 -> 23; matrix products, arithmetic and copies ran while one was open for 19% -> 20% of each run, Pallas kernels for 3% -> 7%
where the time goes in v4:
time: 1110 us; the launch traced here: 1100 us
  waiting for transfers between devices  605 us (55%)
  Pallas kernels  138 us (12%)
  matrix products  128 us (12%)
  starting transfers between devices  77.3 us (7%)
  other arithmetic  75.6 us (7%)
  local copies, waits for them, and re-layouts  40.7 us (4%)
  blocking collectives  20 us (2%)
  between operations  15.5 us (1%)
    ppermute x24, waiting for transfers between devices, shift(): return lax.ppermute(value, axis, [((k + 1) % size, k) for k in range(size)])  235 us
    pallas_call x3, Pallas kernels, call(): pl.pallas_call(kernel, grid_spec=pltpu.PrefetchScalarGridSpec(num_scalar_...  138 us
    ppermute x10, waiting for transfers between devices, sum_all(): lax.ppermute(value, axis, [(k, k ^ step) for k in range(size)])  130 us
    dot_general x10, matrix products, mm(): return jnp.einsum(form, first, second, preferred_element_type=F32)  121 us
    reduce_scatter x3, waiting for transfers between devices, part(): return lax.psum_scatter(rows, GROUP, scatter_dimension=0, tiled=True)  112 us
    all_to_all x2, waiting for transfers between devices, gather_heads(): here = lax.all_to_all(sent, 'o', split_axis=0, concat_axis=0, tiled=True)  108 us
    ppermute x24, starting transfers between devices, shift(): return lax.ppermute(value, axis, [((k + 1) % size, k) for k in range(size)])  35.5 us
  transfers between devices with their start and end apart: 47, of which 23 were waited for; matrix products, arithmetic and copies ran while one was open for 20% of the time, Pallas kernels for 7%

profile of v4, /device:TPU:0, one launch (start us, length us, event | category | flops | bytes accessed | tf_op | source)
XLA Modules:
  0.0 1100.3 jit_solution(2935180045812905117)
XLA Ops:
  11.1 3.0 collective-permute-start.1
  15.3 11.0 collective-permute-done.1
  27.6 5.1 all-to-all-start.2
  33.6 46.7 %all-to-all-done.2 = bf16[4,2,64,1024]{3,2,1,0:T(8,128)(2,1)S(1)} async-done(((bf16[4,2,64,1024]{3,2,1,0:T(8,128)(2,1)}), bf16[4,2,64,1024]{3,2,1,0:T(8,128)(2,1)S(1)}, u32[]{:S(2)}, u32[]{:S(2)}) %all-to-all-start.2) | async-done | bytes 1048608 | tf_op jit(solution)/shard_map/all_to_all | solution.py:161
  86.7 18.5 %collective-permute-done = bf16[256,2048]{1,0:T(8,128)(2,1)} collective-permute-done((bf16[256,2048]{1,0:T(8,128)(2,1)}, bf16[256,2048]{1,0:T(8,128)(2,1)}, u32[]{:S(2)}, u32[]{:S(2)}) %collective-permute-start) | collective-permute-done | bytes 1048608 | tf_op jit(solution)/shard_map/ppermute | solution.py:55
  109.8 4.5 all-to-all-start.1
  114.4 2.7 pad_maximum_fusion.4
  117.1 6.2 slice_bitcast_fusion.5
  123.3 7.3 collective-permute-done.4
  140.9 2.4 pad_maximum_fusion.1
  143.2 61.4 %all-to-all-done.1 = bf16[4,2,256,512]{3,2,1,0:T(8,128)(2,1)} async-done(((bf16[4,2,256,512]{3,2,1,0:T(8,128)(2,1)}), bf16[4,2,256,512]{3,2,1,0:T(8,128)(2,1)}, u32[]{:S(2)}, u32[]{:S(2)}) %all-to-all-start.1) | async-done | bytes 2097184 | tf_op jit(solution)/shard_map/all_to_all | solution.py:161
  204.7 3.5 all-to-all-start
  208.2 6.2 pad_maximum_fusion.slab_ref
  215.1 32.6 %attend.1 = (bf16[2048,1536]{1,0:T(8,128)(2,1)}, bf16[2048,512]{1,0:T(8,128)(2,1)}, bf16[2048,2048]{1,0:T(8,128)(2,1)}) custom-call(s32[3]{0:T(128)} %pad_add_fusion.places_ref, bf16[2048,2048]{1,0:T(8,128)(2,1)} %all-gather.5.cloned.1.call-done.x_ref, f32[16,2,128]{2,1,0:T(2,128)} %copy-done.23, f32[128,128]{1,0:T(8,128)} %get-tuple-element.149.cos_ref, ...), custom_call_target="tpu_custom_call" | custom-call | flops 17716740096 | bytes 25165824 | tf_op jit(solution)/shard_map/attend/pallas_call | solution.py:389
  249.9 63.4 %collective-permute-done.6.refs_4_ = bf16[704,2048]{1,0:T(8,128)(2,1)} collective-permute-done((bf16[704,2048]{1,0:T(8,128)(2,1)}, bf16[704,2048]{1,0:T(8,128)(2,1)}, u32[]{:S(2)}, u32[]{:S(2)}) %collective-permute-start.6) | collective-permute-done | bytes 2883616 | tf_op jit(solution)/shard_map/ppermute | solution.py:55
  313.2 11.2 %convolution_convert_fusion.1.refs_1_ = bf16[2048,704]{1,0:T(8,128)(2,1)} fusion(bf16[2048,2048]{1,0:T(8,128)(2,1)} %all-gather.7.cloned.1.call-done, bf16[704,2048]{1,0:T(8,128)(2,1)} %collective-permute-done.5), kind=kOutput, calls=%fused_computation.16 | convolution fusion | flops 5907021824 | bytes 14155776 | tf_op jit(solution)/shard_map/td,fd->tf/dot_general | solution.py:140
  324.4 10.1 convolution_convert_fusion.2.refs_0_
  334.5 19.0 %reduce-scatter.4.cloned.1.call-done = bf16[128,2048]{1,0:T(8,128)(2,1)} async-done(((bf16[2048,2048]{1,0:T(8,128)(2,1)}), bf16[128,2048]{1,0:T(8,128)(2,1)}) %reduce-scatter.4.cloned.1.call-update) | async-done | bytes 524304 | tf_op jit(solution)/shard_map/reduce_scatter | solution.py:136
  360.2 10.6 all_to_all.42.info_ref
  370.8 50.8 %collective-permute-done.7.refs_5_ = bf16[704,2048]{1,0:T(8,128)(2,1)} collective-permute-done((bf16[704,2048]{1,0:T(8,128)(2,1)}, bf16[704,2048]{1,0:T(8,128)(2,1)}, u32[]{:S(2)}, u32[]{:S(2)}) %collective-permute-start.7) | collective-permute-done | bytes 2883616 | tf_op jit(solution)/shard_map/ppermute | solution.py:55
  421.6 10.1 all-gather.9.cloned.1.call-done.x_ref
  431.8 65.0 %units.1 = (bf16[2048,1408]{1,0:T(8,128)(2,1)}, bf16[2048,1408]{1,0:T(8,128)(2,1)}, bf16[2048,704]{1,0:T(8,128)(2,1)}, bf16[2048,704]{1,0:T(8,128)(2,1)}, bf16[2...) custom-call(s32[3]{0:T(128)} %pad_add_fusion.places_ref, bf16[2048,2048]{1,0:T(8,128)(2,1)} %all-gather.9.cloned.1.call-done.x_ref, ...), custom_call_target="tpu_custom_call" | custom-call | flops 47244640256 | bytes 39845888 | tf_op jit(solution)/shard_map/units/pallas_call | solution.py:389
  497.5 9.4 all_to_all.43
  506.9 92.9 %reduce-scatter.6.cloned.1.call-done = bf16[128,2048]{1,0:T(8,128)(2,1)} async-done(((bf16[2048,2048]{1,0:T(8,128)(2,1)}), bf16[128,2048]{1,0:T(8,128)(2,1)}) %reduce-scatter.6.cloned.1.call-update) | async-done | bytes 524304 | tf_op jit(solution)/shard_map/reduce_scatter | solution.py:136
  599.8 2.5 multiply_reduce_fusion
  606.5 10.8 convolution_convert_fusion.3
  619.0 16.7 %convolution_convert_fusion = bf16[1408,2048]{1,0:T(8,128)(2,1)} fusion(bf16[2048,1408]{1,0:T(8,128)(2,1)S(1)} %bitcast.344, bf16[2048,2048]{1,0:T(8,128)(2,1)} %all-gather.9.cloned.1.call-done.x_ref), kind=kOutput, calls=%fused_computation.4 | convolution fusion | flops 11814043648 | bytes 19922944 | tf_op jit(solution)/shard_map/tf,td->fd/dot_general | solution.py:140
  638.1 15.6 %fusion.58 = f32[1408,2048]{1,0:T(8,128)} fusion(bf16[2048,1408]{1,0:T(8,128)(2,1)S(1)} %bitcast.342, bf16[2048,2048]{1,0:T(8,128)(2,1)S(1)} %bitcast.338), kind=kOutput, calls=%fused_computation.200 | convolution fusion | flops 11811160064 | bytes 25690112 | tf_op jit(solution)/shard_map/tf,td->fd/dot_general | solution.py:140
  654.8 11.4 %fusion.53 = f32[2048,2048]{1,0:T(8,128)} fusion(bf16[2048,704]{1,0:T(8,128)(2,1)S(1)} %copy-done.42, bf16[704,2048]{1,0:T(8,128)(2,1)} %collective-permute-done.5), kind=kOutput, calls=%fused_computation.195 | convolution fusion | flops 5905580032 | bytes 22544384 | tf_op jit(solution)/shard_map/tf,fd->td/dot_general | solution.py:140
  667.8 13.3 %add_convert_fusion = bf16[2048,2048]{1,0:T(8,128)(2,1)} fusion(f32[2048,2048]{1,0:T(8,128)} %fusion.53, bf16[2048,704]{1,0:T(8,128)(2,1)S(1)} %copy-done.40, bf16[704,2048]{1,0:T(8,128)(2,1)} %bitcast.39), kind=kOutput, calls=%fused_computation | convolution fusion | flops 5913968640 | bytes 30932992 | tf_op jit(solution)/shard_map/tf,fd->td/dot_general | solution.py:140
  681.1 125.5 %collective-permute-done.26 = f32[7,2048]{1,0:T(8,128)S(1)} collective-permute-done((f32[7,2048]{1,0:T(8,128)S(1)}, f32[7,2048]{1,0:T(8,128)S(1)}, u32[]{:S(2)}, u32[]{:S(2)}) %collective-permute-start.26) | collective-permute-done | bytes 57376 | tf_op jit(solution)/shard_map/ppermute | solution.py:95
  806.6 40.4 %attend_back.1 = (bf16[2048,1536]{1,0:T(8,128)(2,1)}, bf16[2,2,4,128,2048]{4,3,2,1,0:T(8,128)(2,1)}, f32[16,1,128]{2,1,0:T(1,128)}, f32[1,2048]{1,0:T(1,128)}) custom-call(s32[3]{0:T(128)} %pad_add_fusion.places_ref, bf16[2048,2048]{1,0:T(8,128)(2,1)} %all-gather.11.cloned.1.call-done.mid_ref, f32[16,2,128]{2,1,0:T(2,128)} %copy-done.23, ...), custom_call_target="tpu_custom_call" | custom-call | flops 18522046464 | bytes 46137344 | tf_op jit(solution)/shard_map/attend_back/pallas_call | solution.py:389
  847.1 4.9 slice_bitcast_fusion.3
  852.6 3.8 all-to-all-start.5
  856.5 6.9 fusion.57
  869.4 21.8 %collective-permute-done.31 = bf16[256,2048]{1,0:T(8,128)(2,1)S(1)} collective-permute-done((bf16[256,2048]{1,0:T(8,128)(2,1)S(1)}, bf16[256,2048]{1,0:T(8,128)(2,1)S(1)}, u32[]{:S(2)}, u32[]{:S(2)}) %collective-permute-start.31) | collective-permute-done | bytes 1048608 | tf_op jit(solution)/shard_map/ppermute | solution.py:55
  891.3 4.3 add_bitcast_fusion.1
  895.6 4.5 fusion
  900.2 3.7 collective-permute-start.13
  905.4 13.9 %fusion.56 = f32[2048,1536]{1,0:T(8,128)S(1)} fusion(bf16[2048,2048]{1,0:T(8,128)(2,1)S(1)} %bitcast.336, bf16[2048,1536]{1,0:T(8,128)(2,1)S(1)} %bitcast.340), kind=kOutput, calls=%fused_computation.198 | convolution fusion | flops 12884901888 | bytes 27262976 | tf_op jit(solution)/shard_map/td,tf->df/dot_general | solution.py:140
  919.3 4.5 copy-done.5
  924.3 4.3 slice.319
  930.5 6.6 collective-permute-done.13
  939.7 19.0 %collective-permute-done.14 = bf16[2,64,2048]{2,1,0:T(8,128)(2,1)S(1)} collective-permute-done((bf16[2,64,2048]{2,1,0:T(8,128)(2,1)S(1)}, bf16[2,64,2048]{2,1,0:T(8,128)(2,1)S(1)}, u32[]{:S(2)}, u32[]{:S(2)}) %collective-permute-start.14) | collective-permute-done | bytes 524320 | tf_op jit(solution)/shard_map/ppermute | solution.py:55
  958.9 2.6 collective-permute-start.15
  961.5 2.9 collective-permute-done.10
  964.4 2.6 collective-permute-start.11
  968.7 12.1 %collective-permute-done.11 = bf16[64,2048]{1,0:T(8,128)(2,1)S(1)} collective-permute-done((bf16[64,2048]{1,0:T(8,128)(2,1)S(1)}, bf16[64,2048]{1,0:T(8,128)(2,1)S(1)}, u32[]{:S(2)}, u32[]{:S(2)}) %collective-permute-start.11) | collective-permute-done | bytes 262176 | tf_op jit(solution)/shard_map/ppermute | solution.py:55
  981.0 2.4 collective-permute-start.12
  983.6 6.2 collective-permute-done.12
  991.3 6.4 collective-permute-done.16
  997.8 2.3 fusion.16
  1000.1 2.2 collective-permute-start.17
  1004.0 7.0 all-to-all-start.7
  1014.4 5.7 bitcast_add_fusion
  1022.4 13.4 %convert_add_fusion = f32[1408,2048]{1,0:T(8,128)} fusion(f32[1408,2048]{1,0:T(8,128)} %fusion.58, bf16[1408,2048]{1,0:T(8,128)(2,1)} %collective-permute-done.32), kind=kLoop, calls=%fused_computation.1 | loop fusion | flops 5767168 | bytes 28835840 | tf_op jit(solution)/shard_map/add | solution.py:73
  1035.8 2.4 collective-permute-start.20
  1038.2 9.2 collective-permute-done.28
  1047.4 3.1 bitcast_add_fusion.2
  1052.1 10.7 add_bitcast_fusion
  1063.5 3.6 collective-permute-done.21
  1068.3 3.6 all-to-all-start.6
  1075.2 9.1 all-to-all-done.6
  1089.7 3.3 fusion.13
  (287 shorter events, 85.8 us)
Async XLA Ops:
  7.2 351.4 %copy-start = (f32[2048,4]{0,1:T(4,128)S(1)}, f32[2048,4]{0,1:T(4,128)}, u32[]{:S(2)}) copy-start(f32[2048,4]{0,1:T(4,128)} %param.23) | copy-start | bytes 98308
  7.2 207.3 %all-gather.5.cloned.1.call-start = ((), (), s32[]{:S(2)}) async-start(), calls=%async_computation.11 | async-start | bytes 8912896 | tf_op jit(solution)/shard_map/all_gather | solution.py:132
  11.1 15.1 %collective-permute-start.1 = (bf16[64,4096]{1,0:T(8,128)(2,1)}, bf16[64,4096]{1,0:T(8,128)(2,1)S(1)}, u32[]{:S(2)}, u32[]{:S(2)}) collective-permute-start(bf16[64,4096]{1,0:T(8,128)(2,1)} %param.24), channel_id=1, source_target_pairs={{1,0},{0,1},{3,2},{2,3},{5,4},{4,5},{7,6},{6,7},{9,8},{8,9},{11,10... | collective-permute-start | bytes 1572872 | tf_op jit(solution)/shard_map/ppermute | solution.py:55
  26.4 55.6 %copy-start.9 = (bf16[128,2048]{1,0:T(8,128)(2,1)S(1)}, bf16[128,2048]{1,0:T(8,128)(2,1)}, u32[]{:S(2)}) copy-start(bf16[128,2048]{1,0:T(8,128)(2,1)} %fusion.9) | copy-start | bytes 1572868
  26.4 55.6 %copy-start.21 = (f32[2048,4]{0,1:T(4,128)S(1)}, f32[2048,4]{0,1:T(4,128)}, u32[]{:S(2)}) copy-start(f32[2048,4]{0,1:T(4,128)} %param.22) | copy-start | bytes 98308
  26.4 56.1 %copy-start.25 = (s32[128,2]{0,1:T(2,128)S(1)}, s32[128,2]{0,1:T(2,128)}, u32[]{:S(2)}) copy-start(s32[128,2]{0,1:T(2,128)} %param.18) | copy-start | bytes 3076
  26.4 59.0 %copy-start.38 = (s32[1,128]{1,0:T(1,128)S(1)}, s32[1,128]{1,0:T(1,128)}, u32[]{:S(2)}) copy-start(s32[1,128]{1,0:T(1,128)} %param.17) | copy-start | bytes 1540
  27.6 52.7 %all-to-all-start.2 = ((bf16[4,2,64,1024]{3,2,1,0:T(8,128)(2,1)}), bf16[4,2,64,1024]{3,2,1,0:T(8,128)(2,1)S(1)}, u32[]{:S(2)}, u32[]{:S(2)}) async-start(bf16[4,2,64,1024]{3,2,1,0:T(8,128)(2,1)} %pad_maximum_fusion.9), calls=%async_computation.2 | async-start | bytes 2097152 | tf_op jit(solution)/shard_map/all_to_all | solution.py:161
  32.8 217.1 %all-gather.7.cloned.1.call-start = ((), (), s32[]{:S(2)}) async-start(), calls=%async_computation.13 | async-start | bytes 8912896 | tf_op jit(solution)/shard_map/all_gather | solution.py:132
  80.4 24.8 %collective-permute-start = (bf16[256,2048]{1,0:T(8,128)(2,1)}, bf16[256,2048]{1,0:T(8,128)(2,1)}, u32[]{:S(2)}, u32[]{:S(2)}) collective-permute-start(bf16[256,2048]{1,0:T(8,128)(2,1)} %bitcast.313), channel_id=1, source_target_pairs={{1,0},{0,1},{3,2},{2,3},{5,4},{4,5},{7,6},{6,7},{9,8},{8,9},{11,10... | collective-permute-start | bytes 3145736 | tf_op jit(solution)/shard_map/ppermute | solution.py:55
  83.9 30.4 %collective-permute-start.2 = (bf16[512,1024]{1,0:T(8,128)(2,1)S(1)}, bf16[512,1024]{1,0:T(8,128)(2,1)}, u32[]{:S(2)}, u32[]{:S(2)}) collective-permute-start(bf16[512,1024]{1,0:T(8,128)(2,1)S(1)} %bitcast.307), channel_id=1, source_target_pairs={{16,0},{0,16},{17,1},{1,17},{18,2},{2,18},{19,3},{3,19},{20,4},{4,... | collective-permute-start | bytes 3145736 | tf_op jit(solution)/shard_map/ppermute | solution.py:55
  106.7 23.9 %collective-permute-start.4 = (bf16[256,2048]{1,0:T(8,128)(2,1)}, bf16[256,2048]{1,0:T(8,128)(2,1)}, u32[]{:S(2)}, u32[]{:S(2)}) collective-permute-start(bf16[256,2048]{1,0:T(8,128)(2,1)} %bitcast.40), channel_id=1, source_target_pairs={{1,0},{0,1},{3,2},{2,3},{5,4},{4,5},{7,6},{6,7},{9,8},{8,9},{11,10... | collective-permute-start | bytes 3145736 | tf_op jit(solution)/shard_map/ppermute | solution.py:55
  109.8 94.9 %all-to-all-start.1 = ((bf16[4,2,256,512]{3,2,1,0:T(8,128)(2,1)}), bf16[4,2,256,512]{3,2,1,0:T(8,128)(2,1)}, u32[]{:S(2)}, u32[]{:S(2)}) async-start(bf16[4,2,256,512]{3,2,1,0:T(8,128)(2,1)} %pad_maximum_fusion.2), calls=%async_computation.1 | async-start | bytes 4194304 | tf_op jit(solution)/shard_map/all_to_all | solution.py:161
  117.1 21.6 %collective-permute-start.3 = (bf16[2,512,1024]{2,1,0:T(8,128)(2,1)}, bf16[2,512,1024]{2,1,0:T(8,128)(2,1)}, u32[]{:S(2)}, u32[]{:S(2)}) collective-permute-start(bf16[2,512,1024]{2,1,0:T(8,128)(2,1)} %pad_maximum_fusion.4), channel_id=1, source_target_pairs={{8,0},{0,8},{9,1},{1,9},{10,2},{2,10},{11,3},{3,11},{12,4},{4,12},... | collective-permute-start | bytes 6291464 | tf_op jit(solution)/shard_map/ppermute | solution.py:55
  130.6 83.8 %collective-permute-start.5 = (bf16[704,2048]{1,0:T(8,128)(2,1)}, bf16[704,2048]{1,0:T(8,128)(2,1)}, u32[]{:S(2)}, u32[]{:S(2)}) collective-permute-start(bf16[704,2048]{1,0:T(8,128)(2,1)} %bitcast.39), channel_id=1, source_target_pairs={{1,0},{0,1},{3,2},{2,3},{5,4},{4,5},{7,6},{6,7},{9,8},{8,9},{11,10... | collective-permute-start | bytes 8650760 | tf_op jit(solution)/shard_map/ppermute | solution.py:55
  204.7 9.9 all-to-all-start
  208.2 145.3 %reduce-scatter.4.cloned.1.call-start = ((), (), s32[]{:S(2)}) async-start(), calls=%async_computation.12 | async-start | bytes 8912896 | tf_op jit(solution)/shard_map/reduce_scatter | solution.py:136
  247.8 183.9 %all-gather.9.cloned.1.call-start = ((), (), s32[]{:S(2)}) async-start(), calls=%async_computation.14 | async-start | bytes 8912896 | tf_op jit(solution)/shard_map/all_gather | solution.py:132
  248.3 64.9 %collective-permute-start.6 = (bf16[704,2048]{1,0:T(8,128)(2,1)}, bf16[704,2048]{1,0:T(8,128)(2,1)}, u32[]{:S(2)}, u32[]{:S(2)}) collective-permute-start(bf16[704,2048]{1,0:T(8,128)(2,1)} %get-tuple-element.55), channel_id=1, source_target_pairs={{1,0},{0,1},{3,2},{2,3},{5,4},{4,5},{7,6},{6,7},{9,8},{8,9},{11,10... | collective-permute-start | bytes 8650760 | tf_op jit(solution)/shard_map/ppermute | solution.py:55
  249.9 74.5 %copy-start.37 = (bf16[2048,2048]{1,0:T(8,128)(2,1)S(1)}, bf16[2048,2048]{1,0:T(8,128)(2,1)}, u32[]{:S(2)}) copy-start(bf16[2048,2048]{1,0:T(8,128)(2,1)} %all-gather.7.cloned.1.call-done) | copy-start | bytes 25165828
  324.4 30.4 %copy-start.20 = (f32[2048]{0:T(1024)S(1)}, f32[2048]{0:T(1024)}, u32[]{:S(2)}) copy-start(f32[2048]{0:T(1024)} %param.21) | copy-start | bytes 24580
  324.4 35.7 %copy-start.24 = (s32[128,2]{0,1:T(2,128)S(1)}, s32[128,2]{0,1:T(2,128)}, u32[]{:S(2)}) copy-start(s32[128,2]{0,1:T(2,128)} %param.19) | copy-start | bytes 3076
  357.0 242.8 %reduce-scatter.6.cloned.1.call-start = ((), (), s32[]{:S(2)}) async-start(), calls=%async_computation.15 | async-start | bytes 8912896 | tf_op jit(solution)/shard_map/reduce_scatter | solution.py:136
  357.0 64.6 %collective-permute-start.7 = (bf16[704,2048]{1,0:T(8,128)(2,1)}, bf16[704,2048]{1,0:T(8,128)(2,1)}, u32[]{:S(2)}, u32[]{:S(2)}) collective-permute-start(bf16[704,2048]{1,0:T(8,128)(2,1)} %get-tuple-element.61), channel_id=1, source_target_pairs={{1,0},{0,1},{3,2},{2,3},{5,4},{4,5},{7,6},{6,7},{9,8},{8,9},{11,10... | collective-permute-start | bytes 8650760 | tf_op jit(solution)/shard_map/ppermute | solution.py:55
  496.8 103.0 %copy-start.12 = (bf16[128,2048]{1,0:T(8,128)(2,1)S(1)}, bf16[128,2048]{1,0:T(8,128)(2,1)}, u32[]{:S(2)}) copy-start(bf16[128,2048]{1,0:T(8,128)(2,1)} %reduce-scatter.4.cloned.1.call-done) | copy-start | bytes 1572868
  496.8 309.8 %all-gather.11.cloned.1.call-start = ((), (), s32[]{:S(2)}) async-start(), calls=%async_computation.16 | async-start | bytes 8912896 | tf_op jit(solution)/shard_map/all_gather | solution.py:132
  506.9 97.7 %copy-start.11 = (bf16[128,2048]{1,0:T(8,128)(2,1)S(1)}, bf16[128,2048]{1,0:T(8,128)(2,1)}, u32[]{:S(2)}) copy-start(bf16[128,2048]{1,0:T(8,128)(2,1)} %multiply_convert_fusion) | copy-start | bytes 1572868
  605.0 13.8 %collective-permute-start.22 = (f32[7,2048]{1,0:T(8,128)S(1)}, f32[7,2048]{1,0:T(8,128)S(1)}, u32[]{:S(2)}, u32[]{:S(2)}) collective-permute-start(f32[7,2048]{1,0:T(8,128)S(1)} %pad_maximum_fusion.15), channel_id=1, source_target_pairs={{0,16},{16,0},{1,17},{17,1},{2,18},{18,2},{3,19},{19,3},{4,20},{20... | collective-permute-start | bytes 172040 | tf_op jit(solution)/shard_map/ppermute | solution.py:95
  606.5 31.5 %slice-start.2 = ((s8[8388608]{0:T(1024)(128)(4,1)}), s8[4194304]{0:T(1024)(128)(4,1)S(1)}, s32[]{:S(2)}) async-start(s8[8388608]{0:T(1024)(128)(4,1)} %bitcast.337), calls=%async_computation.20 | async-start | bytes 8388608
  606.5 31.5 %slice-start.6 = ((s8[5767168]{0:T(1024)(128)(4,1)}), s8[4194304]{0:T(1024)(128)(4,1)S(1)}, s32[]{:S(2)}) async-start(s8[5767168]{0:T(1024)(128)(4,1)} %bitcast.341), calls=%async_computation.24 | async-start | bytes 8388608
  617.4 418.4 %collective-permute-start.33 = (bf16[704,2048]{1,0:T(8,128)(2,1)}, bf16[704,2048]{1,0:T(8,128)(2,1)}, u32[]{:S(2)}, u32[]{:S(2)}) collective-permute-start(bf16[704,2048]{1,0:T(8,128)(2,1)} %convolution_convert_fusion.3), channel_id=1, source_target_pairs={{1,0},{0,1},{3,2},{2,3},{5,4},{4,5},{7,6},{6,7},{9,8},{8,9},{11,10... | collective-permute-start | bytes 8650760 | tf_op jit(solution)/shard_map/ppermute | solution.py:55
  618.9 17.4 %collective-permute-start.23 = (f32[7,2048]{1,0:T(8,128)S(1)}, f32[7,2048]{1,0:T(8,128)S(1)}, u32[]{:S(2)}, u32[]{:S(2)}) collective-permute-start(f32[7,2048]{1,0:T(8,128)S(1)} %fusion.45), channel_id=1, source_target_pairs={{0,8},{8,0},{1,9},{9,1},{2,10},{10,2},{3,11},{11,3},{4,12},{12,4},... | collective-permute-start | bytes 172040 | tf_op jit(solution)/shard_map/ppermute | solution.py:95
  635.7 375.4 %collective-permute-start.32 = (bf16[1408,2048]{1,0:T(8,128)(2,1)}, bf16[1408,2048]{1,0:T(8,128)(2,1)}, u32[]{:S(2)}, u32[]{:S(2)}) collective-permute-start(bf16[1408,2048]{1,0:T(8,128)(2,1)} %convolution_convert_fusion), channel_id=1, source_target_pairs={{1,0},{0,1},{3,2},{2,3},{5,4},{4,5},{7,6},{6,7},{9,8},{8,9},{11,10... | collective-permute-start | bytes 17301512 | tf_op jit(solution)/shard_map/ppermute | solution.py:55
  636.3 17.4 %collective-permute-start.24 = (f32[7,2048]{1,0:T(8,128)S(1)}, f32[7,2048]{1,0:T(8,128)S(1)}, u32[]{:S(2)}, u32[]{:S(2)}) collective-permute-start(f32[7,2048]{1,0:T(8,128)S(1)} %add.175), channel_id=1, source_target_pairs={{0,2},{2,0},{4,6},{6,4},{1,3},{3,1},{5,7},{7,5},{8,10},{10,8},{12,... | collective-permute-start | bytes 172040 | tf_op jit(solution)/shard_map/ppermute | solution.py:95
  653.7 12.5 %collective-permute-start.25 = (f32[7,2048]{1,0:T(8,128)S(1)}, f32[7,2048]{1,0:T(8,128)S(1)}, u32[]{:S(2)}, u32[]{:S(2)}) collective-permute-start(f32[7,2048]{1,0:T(8,128)S(1)} %add.176), channel_id=1, source_target_pairs={{0,4},{2,6},{4,0},{6,2},{1,5},{3,7},{5,1},{7,3},{8,12},{10,14},{12... | collective-permute-start | bytes 172040 | tf_op jit(solution)/shard_map/ppermute | solution.py:95
  666.2 140.4 %collective-permute-start.26 = (f32[7,2048]{1,0:T(8,128)S(1)}, f32[7,2048]{1,0:T(8,128)S(1)}, u32[]{:S(2)}, u32[]{:S(2)}) collective-permute-start(f32[7,2048]{1,0:T(8,128)S(1)} %add.177), channel_id=1, source_target_pairs={{0,1},{1,0},{2,3},{3,2},{4,5},{5,4},{6,7},{7,6},{8,9},{9,8},{10,11... | collective-permute-start | bytes 172040 | tf_op jit(solution)/shard_map/ppermute | solution.py:95
  852.0 43.6 %collective-permute-start.8 = (bf16[2,4,128,2048]{3,2,0,1:T(8,128)(2,1)}, bf16[2,4,128,2048]{3,2,0,1:T(8,128)(2,1)}, u32[]{:S(2)}, u32[]{:S(2)}) collective-permute-start(bf16[2,4,128,2048]{3,2,0,1:T(8,128)(2,1)} %slice_bitcast_fusion.3), channel_id=1, source_target_pairs={{8,0},{0,8},{9,1},{1,9},{10,2},{2,10},{11,3},{3,11},{12,4},{4,12},... | collective-permute-start | bytes 12582920 | tf_op jit(solution)/shard_map/ppermute | solution.py:55
  852.6 15.5 %all-to-all-start.5 = ((f32[16,1,128]{2,1,0:T(1,128)}), f32[16,1,128]{2,1,0:T(1,128)S(1)}, u32[]{:S(2)}, u32[]{:S(2)}) async-start(f32[16,1,128]{2,1,0:T(1,128)} %get-tuple-element.77), calls=%async_computation.8 | async-start | bytes 16384 | tf_op jit(solution)/shard_map/all_to_all | solution.py:126
  856.5 233.2 %reduce-scatter.8.cloned.1.call-start = ((), (), s32[]{:S(2)}) async-start(), calls=%async_computation.17 | async-start | bytes 8912896 | tf_op jit(solution)/shard_map/reduce_scatter | solution.py:136
  865.7 25.6 %collective-permute-start.31 = (bf16[256,2048]{1,0:T(8,128)(2,1)S(1)}, bf16[256,2048]{1,0:T(8,128)(2,1)S(1)}, u32[]{:S(2)}, u32[]{:S(2)}) collective-permute-start(bf16[256,2048]{1,0:T(8,128)(2,1)S(1)} %select_convert_fusion.1), channel_id=1, source_target_pairs={{1,0},{0,1},{3,2},{2,3},{5,4},{4,5},{7,6},{6,7},{9,8},{8,9},{11,10... | collective-permute-start | bytes 3145736 | tf_op jit(solution)/shard_map/ppermute | solution.py:55
  900.2 36.9 %collective-permute-start.13 = (bf16[2,64,2048]{2,1,0:T(8,128)(2,1)S(1)}, bf16[2,64,2048]{2,1,0:T(8,128)(2,1)S(1)}, u32[]{:S(2)}, u32[]{:S(2)}) collective-permute-start(bf16[2,64,2048]{2,1,0:T(8,128)(2,1)S(1)} %slice_bitcast_fusion.11), channel_id=1, source_target_pairs={{2,0},{4,2},{6,4},{0,6},{3,1},{5,3},{7,5},{1,7},{10,8},{12,10},{14... | collective-permute-start | bytes 1572872 | tf_op jit(solution)/shard_map/ppermute | solution.py:55
  903.9 33.4 %collective-permute-start.9 = (bf16[4,64,2048]{2,1,0:T(8,128)(2,1)S(1)}, bf16[4,64,2048]{2,1,0:T(8,128)(2,1)S(1)}, u32[]{:S(2)}, u32[]{:S(2)}) collective-permute-start(bf16[4,64,2048]{2,1,0:T(8,128)(2,1)S(1)} %slice_bitcast_fusion.6), channel_id=1, source_target_pairs={{16,0},{0,16},{17,1},{1,17},{18,2},{2,18},{19,3},{3,19},{20,4},{4,... | collective-permute-start | bytes 3145736 | tf_op jit(solution)/shard_map/ppermute | solution.py:55
  928.6 38.5 %copy-start.2 = (f32[2048,1024]{1,0:T(8,128)}, f32[2048,1024]{1,0:T(8,128)S(1)}, u32[]{:S(2)}) copy-start(f32[2048,1024]{1,0:T(8,128)S(1)} %slice.319) | copy-start | bytes 25165828
  928.8 73.5 %collective-permute-start.30 = (bf16[4,256,512]{2,1,0:T(8,128)(2,1)S(1)}, bf16[4,256,512]{2,1,0:T(8,128)(2,1)S(1)}, u32[]{:S(2)}, u32[]{:S(2)}) collective-permute-start(bf16[4,256,512]{2,1,0:T(8,128)(2,1)S(1)} %fusion.6), channel_id=1, source_target_pairs={{1,0},{0,1},{3,2},{2,3},{5,4},{4,5},{7,6},{6,7},{9,8},{8,9},{11,10... | collective-permute-start | bytes 3145736 | tf_op jit(solution)/shard_map/ppermute | solution.py:55
  937.2 21.5 %collective-permute-start.14 = (bf16[2,64,2048]{2,1,0:T(8,128)(2,1)S(1)}, bf16[2,64,2048]{2,1,0:T(8,128)(2,1)S(1)}, u32[]{:S(2)}, u32[]{:S(2)}) collective-permute-start(bf16[2,64,2048]{2,1,0:T(8,128)(2,1)S(1)} %fusion.20), channel_id=1, source_target_pairs={{2,0},{4,2},{6,4},{0,6},{3,1},{5,3},{7,5},{1,7},{10,8},{12,10},{14... | collective-permute-start | bytes 1572872 | tf_op jit(solution)/shard_map/ppermute | solution.py:55
  937.7 26.6 %collective-permute-start.10 = (bf16[64,2048]{1,0:T(8,128)(2,1)S(1)}, bf16[64,2048]{1,0:T(8,128)(2,1)S(1)}, u32[]{:S(2)}, u32[]{:S(2)}) collective-permute-start(bf16[64,2048]{1,0:T(8,128)(2,1)S(1)} %slice_bitcast_fusion.17), channel_id=1, source_target_pairs={{2,0},{4,2},{6,4},{0,6},{3,1},{5,3},{7,5},{1,7},{10,8},{12,10},{14... | collective-permute-start | bytes 786440 | tf_op jit(solution)/shard_map/ppermute | solution.py:55
  958.9 22.1 %collective-permute-start.15 = (bf16[2,64,2048]{2,1,0:T(8,128)(2,1)S(1)}, bf16[2,64,2048]{2,1,0:T(8,128)(2,1)S(1)}, u32[]{:S(2)}, u32[]{:S(2)}) collective-permute-start(bf16[2,64,2048]{2,1,0:T(8,128)(2,1)S(1)} %fusion.19), channel_id=1, source_target_pairs={{2,0},{4,2},{6,4},{0,6},{3,1},{5,3},{7,5},{1,7},{10,8},{12,10},{14... | collective-permute-start | bytes 1572872 | tf_op jit(solution)/shard_map/ppermute | solution.py:55
  964.4 16.5 %collective-permute-start.11 = (bf16[64,2048]{1,0:T(8,128)(2,1)S(1)}, bf16[64,2048]{1,0:T(8,128)(2,1)S(1)}, u32[]{:S(2)}, u32[]{:S(2)}) collective-permute-start(bf16[64,2048]{1,0:T(8,128)(2,1)S(1)} %fusion.26), channel_id=1, source_target_pairs={{2,0},{4,2},{6,4},{0,6},{3,1},{5,3},{7,5},{1,7},{10,8},{12,10},{14... | collective-permute-start | bytes 786440 | tf_op jit(solution)/shard_map/ppermute | solution.py:55
  967.1 30.7 %copy-start.17 = (f32[2048]{0:T(1024)S(1)}, f32[2048]{0:T(1024)}, u32[]{:S(2)}) copy-start(f32[2048]{0:T(1024)} %param.20) | copy-start | bytes 24580
  967.1 30.7 %copy-start.22 = (f32[2048,4]{0,1:T(4,128)S(1)}, f32[2048,4]{0,1:T(4,128)}, u32[]{:S(2)}) copy-start(f32[2048,4]{0,1:T(4,128)} %param.22) | copy-start | bytes 98308
  967.1 30.7 %copy-start.35 = (f32[128]{0:T(128)S(1)}, f32[128]{0:T(128)}, u32[]{:S(2)}) copy-start(f32[128]{0:T(128)} %copy-done.34) | copy-start | bytes 1540
  968.7 31.3 %copy-start.33 = (f32[1,2048]{1,0:T(1,128)S(1)}, f32[1,2048]{1,0:T(1,128)}, u32[]{:S(2)}) copy-start(f32[1,2048]{1,0:T(1,128)} %get-tuple-element.78) | copy-start | bytes 24580
  980.9 33.5 %collective-permute-start.27 = (bf16[2,512,1024]{2,1,0:T(8,128)(2,1)}, bf16[2,512,1024]{2,1,0:T(8,128)(2,1)}, u32[]{:S(2)}, u32[]{:S(2)}) collective-permute-start(bf16[2,512,1024]{2,1,0:T(8,128)(2,1)} %fusion.1), channel_id=1, source_target_pairs={{8,0},{0,8},{9,1},{1,9},{10,2},{2,10},{11,3},{3,11},{12,4},{4,12},... | collective-permute-start | bytes 6291464 | tf_op jit(solution)/shard_map/ppermute | solution.py:55
  981.0 8.8 collective-permute-start.12
  989.8 7.9 collective-permute-start.16
  1000.1 10.8 collective-permute-start.17
  1004.0 64.3 %all-to-all-start.7 = ((bf16[4,256,512]{2,1,0:T(8,128)(2,1)}), bf16[4,256,512]{2,1,0:T(8,128)(2,1)S(1)}, u32[]{:S(2)}, u32[]{:S(2)}) async-start(bf16[4,256,512]{2,1,0:T(8,128)(2,1)} %fusion.4), calls=%async_computation.10 | async-start | bytes 2097152 | tf_op jit(solution)/shard_map/all_to_all | solution.py:170
  1011.0 1.3 collective-permute-start.18
  1012.3 23.4 %collective-permute-start.19 = (f32[5,2048]{1,0:T(8,128)S(1)}, f32[5,2048]{1,0:T(8,128)S(1)}, u32[]{:S(2)}, u32[]{:S(2)}) collective-permute-start(f32[5,2048]{1,0:T(8,128)S(1)} %add.170), channel_id=1, source_target_pairs={{0,2},{2,0},{4,6},{6,4},{1,3},{3,1},{5,7},{7,5},{8,10},{10,8},{12,... | collective-permute-start | bytes 122888 | tf_op jit(solution)/shard_map/ppermute | solution.py:95
  1022.3 25.1 %collective-permute-start.28 = (bf16[512,1024]{1,0:T(8,128)(2,1)S(1)}, bf16[512,1024]{1,0:T(8,128)(2,1)}, u32[]{:S(2)}, u32[]{:S(2)}) collective-permute-start(bf16[512,1024]{1,0:T(8,128)(2,1)S(1)} %fusion.5), channel_id=1, source_target_pairs={{16,0},{0,16},{17,1},{1,17},{18,2},{2,18},{19,3},{3,19},{20,4},{4,... | collective-permute-start | bytes 3145736 | tf_op jit(solution)/shard_map/ppermute | solution.py:55
  1035.8 27.0 %collective-permute-start.20 = (f32[5,2048]{1,0:T(8,128)S(1)}, f32[5,2048]{1,0:T(8,128)S(1)}, u32[]{:S(2)}, u32[]{:S(2)}) collective-permute-start(f32[5,2048]{1,0:T(8,128)S(1)} %add.171), channel_id=1, source_target_pairs={{0,4},{2,6},{4,0},{6,2},{1,5},{3,7},{5,1},{7,3},{8,12},{10,14},{12... | collective-permute-start | bytes 122888 | tf_op jit(solution)/shard_map/ppermute | solution.py:95
  1050.6 16.5 %collective-permute-start.29 = (bf16[4,64,1024]{2,1,0:T(8,128)(2,1)S(1)}, bf16[4,64,1024]{2,1,0:T(8,128)(2,1)S(1)}, u32[]{:S(2)}, u32[]{:S(2)}) collective-permute-start(bf16[4,64,1024]{2,1,0:T(8,128)(2,1)S(1)} %fusion.22), channel_id=1, source_target_pairs={{1,0},{0,1},{3,2},{2,3},{5,4},{4,5},{7,6},{6,7},{9,8},{8,9},{11,10... | collective-permute-start | bytes 1572872 | tf_op jit(solution)/shard_map/ppermute | solution.py:55
  1062.8 4.3 collective-permute-start.21
  1068.3 16.0 %all-to-all-start.6 = ((bf16[4,64,1024]{2,1,0:T(8,128)(2,1)}), bf16[4,64,1024]{2,1,0:T(8,128)(2,1)S(1)}, u32[]{:S(2)}, u32[]{:S(2)}) async-start(bf16[4,64,1024]{2,1,0:T(8,128)(2,1)} %fusion.21), calls=%async_computation.9 | async-start | bytes 1048576 | tf_op jit(solution)/shard_map/all_to_all | solution.py:170
  (36 other events, 352.5 us)
Sparse Core Ops, SparseCore 0:
  11.3 90.0 all-gather.4
  104.1 108.6 all-gather.6
  247.9 105.5 reduce-scatter.3
  357.1 74.6 all-gather.8
  496.9 102.8 reduce-scatter.5
  604.7 75.1 all-gather.10
  868.2 156.6 reduce-scatter.7

commit v5 on v4

--- a/solution.py
+++ b/solution.py
@@ -140,61 +140,65 @@
     return jnp.einsum(form, first, second, preferred_element_type=F32)
 
 
-def head_columns(matrix):
+def head_blocks(matrix):
     span = HEADS // OUTER * HD
+    return jnp.stack([matrix[:, k * span : (k + 1) * span] for k in range(OUTER)])
+
+
+def join_blocks(blocks):
+    return jnp.concatenate([blocks[k] for k in range(OUTER)], axis=1)
+
+
+def exchange(blocks):
+    return lax.all_to_all(blocks, "o", split_axis=0, concat_axis=0, tiled=True)
+
+
+def gather_heads(places, query_weight, kv_weight):
     whole = HEADS * HD
-    return [
+    rows = query_weight.shape[0]
+    here = exchange(
         jnp.concatenate(
             [
-                matrix[:, start + k * span : start + (k + 1) * span]
-                for start in range(0, matrix.shape[1], whole)
+                head_blocks(query_weight),
+                head_blocks(kv_weight[:, :whole]),
+                head_blocks(kv_weight[:, whole:]),
             ],
             axis=1,
         )
-        for k in range(OUTER)
-    ]
-
-
-def gather_heads(weight):
-    parts = ring_gather(weight, "i")
-    sent = in_order([jnp.stack(head_columns(one)) for one in parts], "i", 1)
-    here = lax.all_to_all(sent, "o", split_axis=0, concat_axis=0, tiled=True)
-    return here.reshape(-1, here.shape[-1])
-
-
-def scatter_rows(grad):
+    )
+    span = here.shape[2]
+    kv = ring_gather(here[:, rows:].reshape(OUTER, 2, -1, span), "i")
+    query_source, _ = lax.optimization_barrier((here[:, :rows], kv[-1]))
+    query = in_order(ring_gather(query_source, "i"), "i", 1).reshape(-1, span)
+    kv = jnp.stack(ring_gather(jnp.stack(kv), "y"))
+    kv = jnp.stack(ring_gather(kv, "c"))
+    return query, arrange(places, kv)
+
+
+def scatter_query(grad):
     inner = lax.axis_size("i")
     blocks = grad.reshape(OUTER, inner, -1, grad.shape[1])
     blocks = from_order([blocks[:, k] for k in range(inner)], "i")
     mine = ring_scatter(blocks, "i").astype(BF16)
-    here = lax.all_to_all(mine, "o", split_axis=0, concat_axis=0, tiled=True).astype(F32)
-    span = HEADS // OUTER * HD
-    return jnp.concatenate(
-        [
-            here[k, :, start : start + span]
-            for start in range(0, grad.shape[1], span)
-            for k in range(OUTER)
-        ],
-        axis=1,
-    )
-
-
-def gather_kv(rows):
-    here = ring_gather(jnp.stack(ring_gather(rows, "y")), "c")
-    whole = in_order([in_order(list(one), "y", 0) for one in here], "c", 1)
-    return whole.reshape(-1, whole.shape[-1])
+    return join_blocks(exchange(mine)).astype(F32)
 
 
 def scatter_kv(grad):
-    high = lax.axis_size("y")
-    blocks = grad.reshape(high, 2, -1, grad.shape[1])
+    high, inner = lax.axis_size("y"), lax.axis_size("i")
+    wide = grad.shape[1]
+    blocks = grad.reshape(high, 2, OUTER, inner, -1, wide)
     mine = ring_scatter(from_order([blocks[:, 0], blocks[:, 1]], "c"), "c")
     mine = ring_scatter(from_order([mine[k] for k in range(high)], "y"), "y")
-    return scatter_rows(mine)
+    mine = ring_scatter(from_order([mine[:, k] for k in range(inner)], "i"), "i").astype(BF16)
+    here = exchange(mine)
+    half = wide // 2
+    return jnp.concatenate(
+        [join_blocks(here[:, :, :half]), join_blocks(here[:, :, half:])], axis=1
+    ).astype(F32)
 
 
 def own_places():
-    return jnp.stack([lax.axis_index(axis) for axis in GROUP]).astype(jnp.int32)
+    return jnp.stack([lax.axis_index(axis) for axis in ALL]).astype(jnp.int32)
 
 
 def add_low(first, second):
@@ -209,6 +213,7 @@
 
 
 def part_by_rings(rows):
+    rows = ring_low([rows[k] for k in range(rows.shape[0])], "c")
     half = rows.shape[2] // 2
     first, second = rows[:, :, :half], rows[:, :, half:]
     first = ring_low([first[k] for k in range(first.shape[0])], "y")
@@ -278,13 +283,32 @@
         part_ref[0, 0, slot] = value[seq * length : (seq + 1) * length]
 
 
+def arrange_kernel(places_ref, in_ref, out_ref):
+    del places_ref
+    half = in_ref.shape[-1]
+    for outer in range(OUTER):
+        out_ref[0, 0, outer, 0, :, :half] = in_ref[0, 0, 0, outer, 0]
+        out_ref[0, 0, outer, 0, :, half:] = in_ref[0, 0, 0, outer, 1]
+
+
 def attend_kernel(
-    places_ref, x_ref, info_ref, cos_ref, sin_ref, slab_ref, out_ref, qkv_ref, gated_ref, part_ref
+    places_ref,
+    x_ref,
+    info_ref,
+    cos_ref,
+    sin_ref,
+    query_ref,
+    kv_ref,
+    out_ref,
+    qkv_ref,
+    gated_ref,
+    part_ref,
 ):
     del places_ref
     length = cos_ref.shape[0]
     span = out_ref.shape[0]
-    raw = nn(x_ref[...], slab_ref[...])
+    raw_query = nn(x_ref[...], query_ref[...])
+    raw = nn(x_ref[...], kv_ref[...])
     cosine, sine = cos_ref[...], sin_ref[...]
     starts = range(0, span, HD)
     for seq in range(info_ref.shape[0]):
@@ -293,10 +317,10 @@
         allowed = allowed_keys(info_ref[seq, 1:2, :], length)
         queries, keys, values = [], [], []
         for at in starts:
-            head = raw[rows, at : at + HD].astype(BF16).astype(F32)
+            head = raw_query[rows, at : at + HD].astype(BF16).astype(F32)
             queries.append(turn(head, cosine, sine).astype(BF16))
-            keys.append(turn(raw[rows, span + at : span + at + HD], cosine, sine).astype(BF16))
-            values.append(raw[rows, 2 * span + at : 2 * span + at + HD].astype(BF16))
+            keys.append(turn(raw[rows, at : at + HD], cosine, sine).astype(BF16))
+            values.append(raw[rows, span + at : span + at + HD].astype(BF16))
             qkv_ref[rows, at : at + HD] = queries[-1]
             qkv_ref[rows, span + at : span + at + HD] = keys[-1]
             qkv_ref[rows, 2 * span + at : 2 * span + at + HD] = values[-1]
@@ -315,13 +339,16 @@
     sin_ref,
     qkv_ref,
     x_ref,
-    slab_ref,
+    query_ref,
+    kv_ref,
     out_ref,
-    d_qkv_ref,
+    d_query_ref,
+    d_kv_ref,
     part_ref,
     d_gate_ref,
     d_gain_ref,
 ):
+    del places_ref
     length = cos_ref.shape[0]
     span = out_ref.shape[0]
     scale = 1.0 / math.sqrt(HD)
@@ -344,21 +371,29 @@
         d_keys = heads_tn(d_scores, queries) * scale
         d_values = heads_tn(probs.astype(BF16), (d_heads * gate).astype(BF16))
         for number, at in enumerate(starts):
-            d_qkv_ref[rows, at : at + HD] = turn_back(d_queries[number], cosine, sine).astype(BF16)
-            d_qkv_ref[rows, span + at : span + at + HD] = turn_back(
-                d_keys[number], cosine, sine
-            ).astype(BF16)
-            d_qkv_ref[rows, 2 * span + at : 2 * span + at + HD] = d_values[number].astype(BF16)
+            cols = slice(at, at + HD)
+            d_query_ref[rows, cols] = turn_back(d_queries[number], cosine, sine).astype(BF16)
+            d_kv_ref[rows, cols] = turn_back(d_keys[number], cosine, sine).astype(BF16)
+            d_kv_ref[rows, span + at : span + at + HD] = d_values[number].astype(BF16)
         total = jnp.broadcast_to(jnp.sum(sums, axis=0), (length, length))
         d_gate_ref[seq] = total.T[:1]
-    d_input = nt(d_qkv_ref[...], slab_ref[...])
+    d_input = nt(d_query_ref[...], query_ref[...]) + nt(d_kv_ref[...], kv_ref[...])
 
     @pl.when(pl.program_id(0) == 0)
     def _():
         d_gain_ref[...] = jnp.zeros_like(d_gain_ref)
 
     d_gain_ref[...] += jnp.sum(d_input * x_ref[...].astype(F32), axis=0, keepdims=True)
-    place_rows(places_ref, part_ref, d_input.astype(BF16), length)
+    part_ref[...] = d_input.astype(BF16)
+
+
+def layer_rows_kernel(parts, places_ref, *refs):
+    gated_refs, down_refs, part_ref = refs[:parts], refs[parts : 2 * parts], refs[2 * parts]
+    length = part_ref.shape[3]
+    value = nn(gated_refs[0][...], down_refs[0][...])
+    for part in range(1, parts):
+        value = value + nn(gated_refs[part][...], down_refs[part][...])
+    place_rows(places_ref, part_ref, value.astype(BF16), length)
 
 
 def fixed(shape):
@@ -398,11 +433,53 @@
     )(*operands)
 
 
-def attend(places, rows, info, cosine, sine, slab, out_mat):
-    count, width = rows.shape
+def arrange(places, value):
+    low, high, inner, outer, kinds, rows, span = value.shape
+
+    def index(step, places):
+        y = lax.div(step, 2 * inner)
+        c = lax.rem(lax.div(step, inner), 2)
+        i = lax.rem(step, inner)
+        return (
+            lax.rem(c - places[1] + 2, 2),
+            lax.rem(y - places[0] + high, high),
+            lax.rem(i - places[3] + inner, inner),
+            0,
+            0,
+            0,
+            0,
+        )
+
+    def out_index(step, places):
+        return (
+            lax.div(step, 2 * inner),
+            lax.rem(lax.div(step, inner), 2),
+            0,
+            lax.rem(step, inner),
+            0,
+            0,
+        )
+
+    dims = (high, low, outer, inner, rows, kinds * span)
+    found = call(
+        arrange_kernel,
+        "arrange",
+        high * low * inner,
+        [pl.BlockSpec((1, 1, 1, outer, kinds, rows, span), index)],
+        pl.BlockSpec((1, 1, outer, 1, rows, kinds * span), out_index),
+        shape(dims),
+        0,
+        4 * value.size,
+        (places, value),
+    )
+    return found.reshape(-1, kinds * span)
+
+
+def attend(places, both, info, cosine, sine, query_mat, kv_mat, out_mat):
+    count = both.shape[0]
+    span, width = out_mat.shape
     length = cosine.shape[0]
     step = OUTER * length
-    span = out_mat.shape[0]
     return call(
         attend_kernel,
         "attend",
@@ -412,23 +489,23 @@
             info_spec(OUTER, 2, length),
             fixed(cosine.shape),
             fixed(sine.shape),
-            fixed(slab.shape),
+            fixed(query_mat.shape),
+            fixed(kv_mat.shape),
             fixed(out_mat.shape),
         ],
         [rows_spec(step, 3 * span), rows_spec(step, span), rows_spec(step, width)],
         [shape((count, 3 * span)), shape((count, span)), shape((count, width))],
         2 * count * width * 4 * span + 4 * count * length * span,
         4 * count * (width + 2 * span),
-        (places, rows, info, cosine, sine, slab, out_mat),
-    )
-
-
-def attend_back(places, d_middle, info, cosine, sine, qkv, rows, slab, out_mat):
+        (places, both, info, cosine, sine, query_mat, kv_mat, out_mat),
+    )
+
+
+def attend_back(places, d_middle, info, cosine, sine, qkv, both, query_mat, kv_mat, out_mat):
     count, width = d_middle.shape
     length = cosine.shape[0]
     step = OUTER * length
     span = out_mat.shape[0]
-    high = count // (2 * step)
     return call(
         attend_back_kernel,
         "attend_back",
@@ -440,24 +517,46 @@
             fixed(sine.shape),
             rows_spec(step, 3 * span),
             rows_spec(step, width),
-            fixed(slab.shape),
+            fixed(query_mat.shape),
+            fixed(kv_mat.shape),
             fixed(out_mat.shape),
         ],
         [
-            rows_spec(step, 3 * span),
-            place_spec(high, length, width),
+            rows_spec(step, span),
+            rows_spec(step, 2 * span),
+            rows_spec(step, width),
             info_spec(OUTER, 1, length),
             fixed((1, width)),
         ],
         [
-            shape((count, 3 * span)),
-            shape((2, high, OUTER, length, width)),
+            shape((count, span)),
+            shape((count, 2 * span)),
+            shape((count, width)),
             shape((count // length, 1, length), F32),
             shape((1, width), F32),
         ],
         2 * count * width * 4 * span + 10 * count * length * span,
         4 * count * (2 * width + 3 * span),
-        (places, d_middle, info, cosine, sine, qkv, rows, slab, out_mat),
+        (places, d_middle, info, cosine, sine, qkv, both, query_mat, kv_mat, out_mat),
+    )
+
+
+def layer_rows(places, gated_units, down_parts, length):
+    count, units = gated_units[0].shape
+    width = down_parts[0].shape[1]
+    parts = len(down_parts)
+    step = OUTER * length
+    high = count // (2 * step)
+    return call(
+        functools.partial(layer_rows_kernel, parts),
+        "layer_rows",
+        count // step,
+        [rows_spec(step, units)] * parts + [fixed(down.shape) for down in down_parts],
+        place_spec(high, length, width),
+        shape((2, high, OUTER, length, width)),
+        2 * count * width * units * parts,
+        4 * count * (width + units * parts),
+        (places, *gated_units, *down_parts),
     )
 
 
@@ -551,11 +650,8 @@
     places = own_places()
     tie = lax.optimization_barrier
 
-    kv_rows = gather_heads(kv_weight)
-    kv_mat = gather_kv(kv_rows)
-    query_mat = gather_heads(query_weight[0])
-    slab = jnp.concatenate([query_mat, kv_mat], axis=1)
-    out_source, _ = tie((out_weight[0], kv_rows))
+    query_mat, kv_mat = gather_heads(places, query_weight[0], kv_weight)
+    out_source, _ = tie((out_weight[0], query_mat[:16, :128]))
     out_parts = ring_gather(out_source, "i")
     out_mat = in_order(out_parts, "i").reshape(span, width)
     own_up = up_weight[0].reshape(-1, width)
@@ -567,16 +663,16 @@
     attn_input = normed_one.astype(BF16)
     att_gate, att_onehot = pair_gates(attn_input, att_router, att_route, experts)
     info = to_experts(att_gate, att_onehot, segment_ids[0].astype(F32))
-    all_attn = meet(attn_input)
-    cot_low, _ = tie((cotangent.astype(BF16), kv_rows))
-    all_cot = meet(cot_low)
-    slab, down_parts = tie((slab, down_parts))
-    qkv, gated, branch = attend(places, all_attn, info, cosine, sine_table, slab, out_mat)
-    first_source, branch = tie((up_weight[0, 0], branch))
+    both = meet(jnp.concatenate([attn_input, cotangent.astype(BF16)], axis=1))
+    qkv, gated, branch = attend(
+        places, both, info, cosine, sine_table, query_mat, kv_mat, out_mat
+    )
+    first_source, branch, both = tie((up_weight[0, 0], branch, both))
     first_parts = ring_gather(first_source, "i")
+    all_attn, all_cot = both[:, :width], both[:, width:]
     branch = part(branch)
 
-    all_cot, first_parts = tie((all_cot, first_parts))
+    all_cot, first_parts, down_parts = tie((all_cot, first_parts, down_parts))
     d_units = [mm("td,fd->tf", all_cot, down).astype(BF16) for down in down_parts]
     branch, d_units = tie((branch, d_units))
     middle = residual + branch.astype(F32) + att_bias
@@ -596,11 +692,11 @@
     d_mlp_gate = from_experts(d_gate_m[:, 0], mlp_onehot, experts)
     grad_up = [mm("tf,td->fd", d_here, all_mlp) for d_here in d_both]
     grad_down = [mm("tf,td->fd", here, all_cot) for here in gated_units]
-    rows_out = None
-    for units_here, down in zip(gated_units, down_parts):
-        ahead = mm("tf,fd->td", units_here, down)
-        rows_out = ahead if rows_out is None else rows_out + ahead
-    rows_out = rows_out.astype(BF16)
+    rows_out = layer_rows(places, gated_units, down_parts, tokens)
+    low_up = [one.astype(BF16) for one in grad_up[1:]]
+    low_down = [one.astype(BF16) for one in grad_down[1:]]
+    d_mlp_input, low_up, low_down, rows_out = tie((d_mlp_input, low_up, low_down, rows_out))
+    grad_up, grad_down = grad_up[:1] + low_up, grad_down[:1] + low_down
     d_mlp_router, d_mlp_from_router = gates_back(
         mlp_gate, mlp_onehot, d_mlp_gate, mlp_input, mlp_router
     )
@@ -608,58 +704,55 @@
         middle, inverse_two, norm_gain2, d_mlp_input.astype(F32) + d_mlp_from_router
     )
     d_middle = cotangent + d_norm_two
-    summed_one = sum_all(
-        jnp.concatenate(
-            [
-                jnp.stack([d_gain_two, jnp.sum(d_middle, axis=0), jnp.sum(cotangent, axis=0)]),
-                d_mlp_router,
-            ]
-        )
+    sums = jnp.concatenate(
+        [
+            jnp.stack([d_gain_two, jnp.sum(d_middle, axis=0), jnp.sum(cotangent, axis=0)]),
+            d_mlp_router,
+        ]
     )
 
     all_mid = meet(d_middle.astype(BF16))
-    rows_out, all_mid = tie((rows_out, all_mid))
-    d_qkv, rows_one, d_gate_a, d_gain_a = attend_back(
-        places, all_mid, info, cosine, sine_table, qkv, all_attn, slab, out_mat
-    )
-    rows_one = ring_low([rows_one[0], rows_one[1]], "c")
-    d_qkv, rows_one = tie((d_qkv, rows_one))
-    d_attn_input = part_by_rings(rows_one).astype(F32)
+    rows_out = part_by_rings(rows_out)
+    all_mid, rows_out = tie((all_mid, rows_out))
+    layer_out = middle + rows_out.astype(F32) + mlp_bias
+    d_heads, d_kv, rows_one, d_gate_a, d_gain_a = attend_back(
+        places, all_mid, info, cosine, sine_table, qkv, both, query_mat, kv_mat, out_mat
+    )
+    d_attn_input = part(rows_one)
     d_att_gate = from_experts(d_gate_a[:, 0], att_onehot, experts)
-    d_slab = mm("td,tf->df", all_attn, d_qkv)
-    d_query = scatter_rows(d_slab[:, :span])[None]
-    d_kv_weight = scatter_kv(d_slab[:, span:])
+    d_kv_weight = scatter_kv(mm("td,tf->df", all_attn, d_kv))
+    d_query = scatter_query(mm("td,tf->df", all_attn, d_heads))[None]
     d_out = mm("tf,td->fd", gated, all_mid).reshape(inner, -1, width)
     d_output = ring_scatter(from_order([d_out[k] for k in range(inner)], "i"), "i")[None]
-    layer_out = middle + part(rows_out).astype(F32) + mlp_bias
-    d_upper = ring_scatter(grad_up, "i", d_attn_input)
+    d_upper = ring_scatter(grad_up, "i", rows_one)
     d_upper = d_upper.reshape(up_weight.shape)
-    d_lower = ring_scatter(grad_down, "i", d_attn_input)[None]
+    d_lower = ring_scatter(grad_down, "i", rows_one)[None]
     d_att_router, d_att_from_router = gates_back(
         att_gate, att_onehot, d_att_gate, attn_input, att_router
     )
-    d_norm_one, _ = norm_back(
-        residual, inverse_one, norm_gain1, d_attn_input + d_att_from_router
-    )
     d_gain_one = d_gain_a / norm_gain1 + jnp.sum(
         d_att_from_router * residual * inverse_one, axis=0, keepdims=True
     )
+    summed = sum_all(jnp.concatenate([d_gain_one, sums, d_att_router]))
+    d_attn_input, summed = tie((d_attn_input, summed))
+    d_norm_one, _ = norm_back(
+        residual, inverse_one, norm_gain1, d_attn_input.astype(F32) + d_att_from_router
+    )
     d_input = d_middle + d_norm_one
-    summed_two = sum_all(jnp.concatenate([d_gain_one, d_att_router]))
     return (
         layer_out,
         d_input,
-        summed_two[0],
-        summed_one[0],
-        summed_two[1:].T,
-        summed_one[3:].T,
+        summed[0],
+        summed[1],
+        summed[4 + experts :].T,
+        summed[4 : 4 + experts].T,
         d_kv_weight,
         d_query,
         d_output,
-        summed_one[1],
+        summed[2],
         d_upper,
         d_lower,
-        summed_one[2],
+        summed[3],
     )
 
 

time: 1110 us -> 1020 us (0.919)
  waiting for transfers between devices: 605 us -> 449 us
  blocking collectives: 20 us -> 87 us
  Pallas kernels: 138 us -> 164 us
  starting transfers between devices: 77.3 us -> 64.9 us
    ppermute x24, waiting for transfers between devices: 235 us -> 378 us  [shift(): return lax.ppermute(value, axis, [((k + 1) % size, k) for k in range(size)])]
    ppermute x10 -> x5, waiting for transfers between devices: 130 us -> 2.34 us  [sum_all(): lax.ppermute(value, axis, [(k, k ^ step) for k in range(size)])]
    all_to_all x4 -> x2, waiting for transfers between devices: 117 us -> 5.56 us  [exchange(): return lax.all_to_all(blocks, 'o', split_axis=0, concat_axis=0, tiled=True)]
    all_to_all x1, blocking collectives: 9.36 us -> 75.1 us  [exchange(): return lax.all_to_all(blocks, 'o', split_axis=0, concat_axis=0, tiled=True)]
    reduce_scatter x3, waiting for transfers between devices: 112 us -> 51 us  [part(): return lax.psum_scatter(rows, GROUP, scatter_dimension=0, tiled=True)]
    pallas_call x3 -> x5, Pallas kernels: 138 us -> 164 us  [call(): pl.pallas_call(kernel, grid_spec=pltpu.PrefetchScalarGridSpec(num_scalar_...]
    all_to_all x4 -> x2, starting transfers between devices: 20.3 us -> 8.42 us  [exchange(): return lax.all_to_all(blocks, 'o', split_axis=0, concat_axis=0, tiled=True)]
    dot_general x10 -> x9, matrix products: 121 us -> 111 us  [mm(): return jnp.einsum(form, first, second, preferred_element_type=F32)]
  transfers between devices with their start and end apart: 47 -> 40, of which waited for: 23 -> 20; matrix products, arithmetic and copies ran while one was open for 20% -> 21% of each run, Pallas kernels for 7% -> 7%
where the time goes in v5:
time: 1020 us; the launch traced here: 1010 us
  waiting for transfers between devices  449 us (44%)
  Pallas kernels  164 us (16%)
  matrix products  118 us (12%)
  blocking collectives  87 us (9%)
  other arithmetic  77.7 us (8%)
  starting transfers between devices  64.9 us (6%)
  local copies, waits for them, and re-layouts  36.7 us (4%)
  between operations  15.2 us (1%)
    ppermute x24, waiting for transfers between devices, shift(): return lax.ppermute(value, axis, [((k + 1) % size, k) for k in range(size)])  378 us
    pallas_call x5, Pallas kernels, call(): pl.pallas_call(kernel, grid_spec=pltpu.PrefetchScalarGridSpec(num_scalar_...  164 us
    dot_general x9, matrix products, mm(): return jnp.einsum(form, first, second, preferred_element_type=F32)  111 us
    all_to_all x1, blocking collectives, exchange(): return lax.all_to_all(blocks, 'o', split_axis=0, concat_axis=0, tiled=True)  75.1 us
    reduce_scatter x3, waiting for transfers between devices, part(): return lax.psum_scatter(rows, GROUP, scatter_dimension=0, tiled=True)  51 us
    ppermute x24, starting transfers between devices, shift(): return lax.ppermute(value, axis, [((k + 1) % size, k) for k in range(size)])  34.3 us
  transfers between devices with their start and end apart: 40, of which 20 were waited for; matrix products, arithmetic and copies ran while one was open for 21% of the time, Pallas kernels for 7%

profile of v5, /device:TPU:0, one launch (start us, length us, event | category | flops | bytes accessed | tf_op | source)
XLA Modules:
  0.0 1012.4 jit_solution(16212336102309381375)
XLA Ops:
  9.7 2.6 fusion.51
  13.9 75.1 %all_to_all.37 = bf16[4,384,512]{2,1,0:T(8,128)(2,1)S(1)} all-to-all(bf16[4,384,512]{2,1,0:T(8,128)(2,1)S(1)} %maximum_maximum_fusion), channel_id=1, replica_groups=mesh['y'=2,'c'=2,'o'=4,'i'=2] {'o'}, dimensions={0} | all-to-all | bytes 3145728 | tf_op jit(solution)/shard_map/all_to_all | solution.py:153
  91.2 8.6 collective-permute-done
  100.6 2.3 fusion.46
  105.6 4.0 all-to-all-start
  111.5 38.8 %collective-permute-done.2 = bf16[2,4,2,64,512]{4,3,2,1,0:T(8,128)(2,1)} collective-permute-done((bf16[2,4,2,64,512]{4,3,2,1,0:T(8,128)(2,1)}, bf16[2,4,2,64,512]{4,3,2,1,0:T(8,128)(2,1)}, u32[]{:S(2)}, u32[]{:S(2)}) %collective-permute-start.2) | collective-permute-done | bytes 1048608 | tf_op jit(solution)/shard_map/ppermute | solution.py:55
  151.9 6.2 slice_bitcast_fusion.2
  163.9 19.8 %collective-permute-done.1 = bf16[4,256,512]{2,1,0:T(8,128)(2,1)S(1)} collective-permute-done((bf16[4,256,512]{2,1,0:T(8,128)(2,1)S(1)}, bf16[4,256,512]{2,1,0:T(8,128)(2,1)S(1)}, u32[]{:S(2)}, u32[]{:S(2)}) %collective-permute-start.1) | collective-permute-done | bytes 1048608 | tf_op jit(solution)/shard_map/ppermute | solution.py:55
  185.6 2.4 pad_maximum_fusion.in_ref
  188.0 7.4 arrange.1
  196.0 32.7 %attend.1 = (bf16[2048,1536]{1,0:T(8,128)(2,1)}, bf16[2048,512]{1,0:T(8,128)(2,1)}, bf16[2048,2048]{1,0:T(8,128)(2,1)}) custom-call(s32[4]{0:T(128)} %pad_add_fusion.places_ref, bf16[2048,4096]{1,0:T(8,128)(2,1)} %all-gather.4.cloned.1.call-done.x_ref, f32[16,2,128]{2,1,0:T(2,128)} %copy-done.32, f32[128,128]{1,0:T(8,128)} %get-tuple-element.146.cos_ref, ...), custom_call_target="tpu_custom_call" | custom-call | flops 17716740096 | bytes 25165824 | tf_op jit(solution)/shard_map/attend/pallas_call | solution.py:424
  232.0 9.1 slice.226
  241.1 53.6 %collective-permute-done.6.refs_3_ = bf16[704,2048]{1,0:T(8,128)(2,1)} collective-permute-done((bf16[704,2048]{1,0:T(8,128)(2,1)}, bf16[704,2048]{1,0:T(8,128)(2,1)}, u32[]{:S(2)}, u32[]{:S(2)}) %collective-permute-start.6) | collective-permute-done | bytes 2883616 | tf_op jit(solution)/shard_map/ppermute | solution.py:55
  294.7 60.6 %collective-permute-done.5.refs_4_ = bf16[704,2048]{1,0:T(8,128)(2,1)} collective-permute-done((bf16[704,2048]{1,0:T(8,128)(2,1)S(1)}, bf16[704,2048]{1,0:T(8,128)(2,1)}, u32[]{:S(2)}, u32[]{:S(2)}) %collective-permute-start.5) | collective-permute-done | bytes 2883616 | tf_op jit(solution)/shard_map/ppermute | solution.py:55
  355.4 10.3 %convolution_convert_fusion.2.refs_0_ = bf16[2048,704]{1,0:T(8,128)(2,1)} fusion(bf16[2048,2048]{1,0:T(8,128)(2,1)} %slice.226, bf16[704,2048]{1,0:T(8,128)(2,1)S(1)} %bitcast.285), kind=kOutput, calls=%fused_computation.15 | convolution fusion | flops 5907021824 | bytes 14155776 | tf_op jit(solution)/shard_map/td,fd->tf/dot_general | solution.py:140
  365.7 9.9 convolution_convert_fusion.1.refs_1_
  377.2 2.1 multiply_convert_fusion
  382.5 11.9 %all_to_all.38.info_ref = f32[16,1,128]{2,1,0:T(1,128)} all-to-all(f32[16,1,128]{2,1,0:T(1,128)S(1)} %bitcast.270), channel_id=1, replica_groups=mesh['y'=2,'c'=2,'o'=4,'i'=2] {'y','c','o'}, dimensions={0} | all-to-all | bytes 16384 | tf_op jit(solution)/shard_map/all_to_all | solution.py:122
  394.5 48.4 %collective-permute-done.7.refs_5_ = bf16[704,2048]{1,0:T(8,128)(2,1)} collective-permute-done((bf16[704,2048]{1,0:T(8,128)(2,1)S(1)}, bf16[704,2048]{1,0:T(8,128)(2,1)}, u32[]{:S(2)}, u32[]{:S(2)}) %collective-permute-start.7) | collective-permute-done | bytes 2883616 | tf_op jit(solution)/shard_map/ppermute | solution.py:55
  442.8 12.2 %all-gather.6.cloned.1.call-done.x_ref = bf16[2048,2048]{1,0:T(8,128)(2,1)} async-done(((bf16[128,2048]{1,0:T(8,128)(2,1)}), bf16[2048,2048]{1,0:T(8,128)(2,1)}) %all-gather.6.cloned.1.call-update) | async-done | bytes 8388624 | tf_op jit(solution)/shard_map/all_gather | solution.py:132
  455.1 65.0 %units.1 = (bf16[2048,1408]{1,0:T(8,128)(2,1)}, bf16[2048,1408]{1,0:T(8,128)(2,1)}, bf16[2048,704]{1,0:T(8,128)(2,1)}, bf16[2048,704]{1,0:T(8,128)(2,1)}, bf16[2...) custom-call(s32[4]{0:T(128)} %pad_add_fusion.places_ref, bf16[2048,2048]{1,0:T(8,128)(2,1)} %all-gather.6.cloned.1.call-done.x_ref, ...), custom_call_target="tpu_custom_call" | custom-call | flops 47244640256 | bytes 39845888 | tf_op jit(solution)/shard_map/units/pallas_call | solution.py:424
  520.1 3.5 all-to-all-start.3
  524.1 11.5 %convolution_convert_fusion.3 = bf16[704,2048]{1,0:T(8,128)(2,1)} fusion(bf16[2048,704]{1,0:T(8,128)(2,1)} %get-tuple-element.72.refs_1_, bf16[2048,2048]{1,0:T(8,128)(2,1)} %slice.226), kind=kOutput, calls=%fused_computation.16 | convolution fusion | flops 5907021824 | bytes 14155776 | tf_op jit(solution)/shard_map/tf,td->fd/dot_general | solution.py:140
  535.6 16.9 %convolution_convert_fusion = bf16[1408,2048]{1,0:T(8,128)(2,1)} fusion(bf16[2048,1408]{1,0:T(8,128)(2,1)S(1)} %copy-done.49, bf16[2048,2048]{1,0:T(8,128)(2,1)} %all-gather.6.cloned.1.call-done.x_ref), kind=kOutput, calls=%fused_computation.3 | convolution fusion | flops 11814043648 | bytes 19922944 | tf_op jit(solution)/shard_map/tf,td->fd/dot_general | solution.py:140
  552.5 19.4 %layer_rows.1 = bf16[2,2,4,128,2048]{4,3,2,1,0:T(8,128)(2,1)} custom-call(s32[4]{0:T(128)} %pad_add_fusion.places_ref, bf16[2048,704]{1,0:T(8,128)(2,1)} %get-tuple-element.73.refs_0_, bf16[2048,704]{1,0:T(8,128)(2,1)} %get-tuple-element.72.refs_1_, bf16[704,2048]{1,0:T(8,128)(2,1)} %bitcast.284, bf16[704,2048]{1,0:T(8,128)(2,1)} %collective-permute-done.6.refs_3_), custom_call_target="tpu_custom_call" | custom-call | flops 11811160064 | bytes 28311552 | tf_op jit(solution)/shard_map/layer_rows/pallas_call | solution.py:424
  572.1 51.0 %reduce-scatter.6.cloned.1.call-done = bf16[128,2048]{1,0:T(8,128)(2,1)} async-done(((bf16[2048,2048]{1,0:T(8,128)(2,1)}), bf16[128,2048]{1,0:T(8,128)(2,1)}) %reduce-scatter.6.cloned.1.call-update) | async-done | bytes 524304 | tf_op jit(solution)/shard_map/reduce_scatter | solution.py:136
  623.1 2.5 multiply_reduce_fusion
  627.0 2.7 slice_bitcast_fusion.1
  629.8 7.1 collective-permute-done.8
  636.9 2.0 fusion
  641.8 2.2 collective-permute-start.13
  644.0 22.2 %collective-permute-done.13 = bf16[2,64,2048]{2,1,0:T(8,128)(2,1)} collective-permute-done((bf16[2,64,2048]{2,1,0:T(8,128)(2,1)}, bf16[2,64,2048]{2,1,0:T(8,128)(2,1)}, u32[]{:S(2)}, u32[]{:S(2)}) %collective-permute-start.13) | collective-permute-done | bytes 524320 | tf_op jit(solution)/shard_map/ppermute | solution.py:55
  667.5 2.2 collective-permute-start.14
  669.7 2.2 fusion.6
  673.4 18.9 %fusion.58 = f32[1408,2048]{1,0:T(8,128)} fusion(bf16[2048,1408]{1,0:T(8,128)(2,1)} %get-tuple-element.90, bf16[2048,2048]{1,0:T(8,128)(2,1)} %all-gather.6.cloned.1.call-done.x_ref), kind=kOutput, calls=%fused_computation.180 | convolution fusion | flops 11811160064 | bytes 25690112 | tf_op jit(solution)/shard_map/tf,td->fd/dot_general | solution.py:140
  692.3 24.8 %collective-permute-done.10 = bf16[64,2048]{1,0:T(8,128)(2,1)S(1)} collective-permute-done((bf16[64,2048]{1,0:T(8,128)(2,1)S(1)}, bf16[64,2048]{1,0:T(8,128)(2,1)S(1)}, u32[]{:S(2)}, u32[]{:S(2)}) %collective-permute-start.10) | collective-permute-done | bytes 262176 | tf_op jit(solution)/shard_map/ppermute | solution.py:55
  721.9 5.8 collective-permute-done.11
  727.8 4.5 collective-permute-start.12
  732.3 6.6 collective-permute-done.15
  740.1 1.8 collective-permute-start.16
  743.2 3.3 collective-permute-done.16
  747.5 39.7 %attend_back.1 = (bf16[2048,512]{1,0:T(8,128)(2,1)}, bf16[2048,1024]{1,0:T(8,128)(2,1)}, bf16[2048,2048]{1,0:T(8,128)(2,1)}, f32[16,1,128]{2,1,0:T(1,128)}, f32[1,2048]{1,0:T(1,128)}) custom-call(s32[4]{0:T(128)} %pad_add_fusion.places_ref, bf16[2048,2048]{1,0:T(8,128)(2,1)} %all-gather.8.cloned.1.call-done.mid_ref, f32[16,2,128]{2,1,0:T(2,128)} %copy-done.32, ...), custom_call_target="tpu_custom_call" | custom-call | flops 18522046464 | bytes 46137344 | tf_op jit(solution)/shard_map/attend_back/pallas_call | solution.py:424
  787.2 7.2 all-to-all-start.4
  794.4 13.5 %fusion.3 = f32[2048,1024]{1,0:T(8,128)S(1)} fusion(bf16[2048,1024]{1,0:T(8,128)(2,1)} %get-tuple-element.85, bf16[2048,4096]{1,0:T(8,128)(2,1)} %all-gather.4.cloned.1.call-done.x_ref), kind=kOutput, calls=%fused_computation.6 | convolution fusion | flops 8589934592 | bytes 20971520 | tf_op jit(solution)/shard_map/td,tf->df/dot_general | solution.py:140
  809.7 12.4 %fusion.57 = f32[512,2048]{1,0:T(8,128)} fusion(bf16[2048,512]{1,0:T(8,128)(2,1)S(1)} %copy-done.47, bf16[2048,2048]{1,0:T(8,128)(2,1)} %all-gather.8.cloned.1.call-done.mid_ref), kind=kOutput, calls=%fused_computation.179 | convolution fusion | flops 4294967296 | bytes 14680064 | tf_op jit(solution)/shard_map/tf,td->fd/dot_general | solution.py:140
  826.2 1.8 collective-permute-start.17
  828.0 3.4 select_convert_fusion.1
  832.9 2.3 collective-permute-done.17
  835.3 7.3 fusion.1
  842.7 1.8 collective-permute-start.19
  845.6 63.6 %collective-permute-done.27 = bf16[1408,2048]{1,0:T(8,128)(2,1)} collective-permute-done((bf16[1408,2048]{1,0:T(8,128)(2,1)}, bf16[1408,2048]{1,0:T(8,128)(2,1)}, u32[]{:S(2)}, u32[]{:S(2)}) %collective-permute-start.27) | collective-permute-done | bytes 5767200 | tf_op jit(solution)/shard_map/ppermute | solution.py:55
  910.6 2.5 collective-permute-start.20
  913.2 3.2 bitcast_add_fusion
  916.4 2.0 copy-done.7
  921.0 13.3 %convert_add_fusion = f32[1408,2048]{1,0:T(8,128)} fusion(f32[1408,2048]{1,0:T(8,128)} %fusion.58, bf16[1408,2048]{1,0:T(8,128)(2,1)} %collective-permute-done.27), kind=kLoop, calls=%fused_computation | loop fusion | flops 5767168 | bytes 28835840 | tf_op jit(solution)/shard_map/add | solution.py:73
  935.9 12.9 %collective-permute-done.25 = bf16[4,256,512]{2,1,0:T(8,128)(2,1)} collective-permute-done((bf16[4,256,512]{2,1,0:T(8,128)(2,1)}, bf16[4,256,512]{2,1,0:T(8,128)(2,1)}, u32[]{:S(2)}, u32[]{:S(2)}) %collective-permute-start.25) | collective-permute-done | bytes 1048608 | tf_op jit(solution)/shard_map/ppermute | solution.py:55
  948.8 4.1 fusion.7
  952.9 4.3 all-to-all-start.6
  957.2 3.3 bitcast_add_fusion.2
  962.1 10.7 %add_bitcast_fusion = f32[1,704,2048]{2,1,0:T(8,128)} fusion(bf16[704,2048]{1,0:T(8,128)(2,1)} %collective-permute-done.28, bf16[2048,704]{1,0:T(8,128)(2,1)S(1)} %copy-done.48, bf16[2048,2048]{1,0:T(8,128)(2,1)} %slice.226), kind=kOutput, calls=%fused_computation.8 | convolution fusion | flops 5908463616 | bytes 19922944 | tf_op jit(solution)/shard_map/tf,td->fd/dot_general | solution.py:140
  976.2 4.2 all-to-all-start.5
  980.3 4.5 add_bitcast_fusion.1
  987.7 4.2 all-to-all-done.5
  1002.3 3.1 fusion.18
  (250 shorter events, 77.6 us)
Async XLA Ops:
  7.2 373.7 %copy-start = (f32[2048,4]{0,1:T(4,128)S(1)}, f32[2048,4]{0,1:T(4,128)}, u32[]{:S(2)}) copy-start(f32[2048,4]{0,1:T(4,128)} %param.23) | copy-start | bytes 98308
  7.2 188.2 %all-gather.4.cloned.1.call-start = ((), (), s32[]{:S(2)}) async-start(), calls=%async_computation.10 | async-start | bytes 17825792 | tf_op jit(solution)/shard_map/all_gather | solution.py:132
  12.3 78.3 %copy-start.13 = (bf16[128,2048]{1,0:T(8,128)(2,1)}, bf16[128,2048]{1,0:T(8,128)(2,1)S(1)}, u32[]{:S(2)}) copy-start(bf16[128,2048]{1,0:T(8,128)(2,1)S(1)} %get-tuple-element.145) | copy-start | bytes 1572868
  13.7 77.0 %copy-start.26 = (f32[2048,4]{0,1:T(4,128)S(1)}, f32[2048,4]{0,1:T(4,128)}, u32[]{:S(2)}) copy-start(f32[2048,4]{0,1:T(4,128)} %param.22) | copy-start | bytes 98308
  13.9 77.3 %copy-start.34 = (s32[128,2]{0,1:T(2,128)S(1)}, s32[128,2]{0,1:T(2,128)}, u32[]{:S(2)}) copy-start(s32[128,2]{0,1:T(2,128)} %param.18) | copy-start | bytes 3076
  89.0 15.5 %copy-start.46 = (s32[1,128]{1,0:T(1,128)S(1)}, s32[1,128]{1,0:T(1,128)}, u32[]{:S(2)}) copy-start(s32[1,128]{1,0:T(1,128)} %param.17) | copy-start | bytes 1540
  89.0 10.8 %copy-start.19 = (bf16[4,128,512]{2,1,0:T(8,128)(2,1)}, bf16[4,128,512]{2,1,0:T(8,128)(2,1)S(1)}, u32[]{:S(2)}) copy-start(bf16[4,128,512]{2,1,0:T(8,128)(2,1)S(1)} %slice.276) | copy-start | bytes 1572868
  89.1 10.8 %collective-permute-start = (bf16[4,2,64,512]{3,2,1,0:T(8,128)(2,1)S(1)}, bf16[4,2,64,512]{3,2,1,0:T(8,128)(2,1)S(1)}, u32[]{:S(2)}, u32[]{:S(2)}) collective-permute-start(bf16[4,2,64,512]{3,2,1,0:T(8,128)(2,1)S(1)} %bitcast.259), channel_id=1, source_target_pairs={{1,0},{0,1},{3,2},{2,3},{5,4},{4,5},{7,6},{6,7},{9,8},{8,9},{11,10... | collective-permute-start | bytes 1572872 | tf_op jit(solution)/shard_map/ppermute | solution.py:55
  91.2 60.6 %copy-start.28 = (f32[128,2]{0,1:T(2,128)}, f32[128,2]{0,1:T(2,128)S(1)}, u32[]{:S(2)}) copy-start(f32[128,2]{0,1:T(2,128)S(1)} %select_reduce_fusion.7) | copy-start | bytes 3076
  91.2 13.3 %copy-start.36 = (f32[128]{0:T(128)}, f32[128]{0:T(128)S(1)}, u32[]{:S(2)}) copy-start(f32[128]{0:T(128)S(1)} %reduce_max.18) | copy-start | bytes 1540
  102.9 47.4 %collective-permute-start.2 = (bf16[2,4,2,64,512]{4,3,2,1,0:T(8,128)(2,1)}, bf16[2,4,2,64,512]{4,3,2,1,0:T(8,128)(2,1)}, u32[]{:S(2)}, u32[]{:S(2)}) collective-permute-start(bf16[2,4,2,64,512]{4,3,2,1,0:T(8,128)(2,1)} %get-tuple-element.114), channel_id=1, source_target_pairs={{16,0},{0,16},{17,1},{1,17},{18,2},{2,18},{19,3},{3,19},{20,4},{4,... | collective-permute-start | bytes 3145736 | tf_op jit(solution)/shard_map/ppermute | solution.py:55
  105.6 89.8 %all-to-all-start = ((f32[16,2,128]{2,1,0:T(2,128)}), f32[16,2,128]{2,1,0:T(2,128)S(1)}, u32[]{:S(2)}, u32[]{:S(2)}) async-start(f32[16,2,128]{2,1,0:T(2,128)} %pad_maximum_fusion.9), calls=%async_computation | async-start | bytes 32768 | tf_op jit(solution)/shard_map/all_to_all | solution.py:122
  109.6 266.1 %reduce-scatter.4.cloned.1.call-start = ((), (), s32[]{:S(2)}) async-start(), calls=%async_computation.11 | async-start | bytes 8912896 | tf_op jit(solution)/shard_map/reduce_scatter | solution.py:136
  109.6 51.4 %collective-permute-start.4 = (bf16[256,2048]{1,0:T(8,128)(2,1)}, bf16[256,2048]{1,0:T(8,128)(2,1)}, u32[]{:S(2)}, u32[]{:S(2)}) collective-permute-start(bf16[256,2048]{1,0:T(8,128)(2,1)} %bitcast.262), channel_id=1, source_target_pairs={{1,0},{0,1},{3,2},{2,3},{5,4},{4,5},{7,6},{6,7},{9,8},{8,9},{11,10... | collective-permute-start | bytes 3145736 | tf_op jit(solution)/shard_map/ppermute | solution.py:55
  151.8 33.8 %collective-permute-start.3 = (bf16[2,2,4,2,64,512]{5,4,3,2,1,0:T(8,128)(2,1)S(1)}, bf16[2,2,4,2,64,512]{5,4,3,2,1,0:T(8,128)(2,1)S(1)}, u32[]{:S(2)}, u32[]{:S(2)}) collective-permute-start(bf16[2,2,4,2,64,512]{5,4,3,2,1,0:T(8,128)(2,1)S(1)} %get-tuple-element.104), channel_id=1, source_target_pairs={{8,0},{0,8},{9,1},{1,9},{10,2},{2,10},{11,3},{3,11},{12,4},{4,12},... | collective-permute-start | bytes 6291464 | tf_op jit(solution)/shard_map/ppermute | solution.py:55
  158.1 25.6 %collective-permute-start.1 = (bf16[4,256,512]{2,1,0:T(8,128)(2,1)S(1)}, bf16[4,256,512]{2,1,0:T(8,128)(2,1)S(1)}, u32[]{:S(2)}, u32[]{:S(2)}) collective-permute-start(bf16[4,256,512]{2,1,0:T(8,128)(2,1)S(1)} %slice.275), channel_id=1, source_target_pairs={{1,0},{0,1},{3,2},{2,3},{5,4},{4,5},{7,6},{6,7},{9,8},{8,9},{11,10... | collective-permute-start | bytes 3145736 | tf_op jit(solution)/shard_map/ppermute | solution.py:55
  228.8 226.3 %all-gather.6.cloned.1.call-start = ((), (), s32[]{:S(2)}) async-start(), calls=%async_computation.12 | async-start | bytes 8912896 | tf_op jit(solution)/shard_map/all_gather | solution.py:132
  229.0 126.4 %copy-start.45 = (bf16[1,704,2048]{2,1,0:T(8,128)(2,1)S(1)}, bf16[1,704,2048]{2,1,0:T(8,128)(2,1)}, u32[]{:S(2)}) copy-start(bf16[1,704,2048]{2,1,0:T(8,128)(2,1)} %param.29) | copy-start | bytes 8650756
  229.0 65.8 %collective-permute-start.6 = (bf16[704,2048]{1,0:T(8,128)(2,1)}, bf16[704,2048]{1,0:T(8,128)(2,1)}, u32[]{:S(2)}, u32[]{:S(2)}) collective-permute-start(bf16[704,2048]{1,0:T(8,128)(2,1)} %bitcast.283), channel_id=1, source_target_pairs={{1,0},{0,1},{3,2},{2,3},{5,4},{4,5},{7,6},{6,7},{9,8},{8,9},{11,10... | collective-permute-start | bytes 8650760 | tf_op jit(solution)/shard_map/ppermute | solution.py:55
  230.5 124.8 %collective-permute-start.5 = (bf16[704,2048]{1,0:T(8,128)(2,1)S(1)}, bf16[704,2048]{1,0:T(8,128)(2,1)}, u32[]{:S(2)}, u32[]{:S(2)}) collective-permute-start(bf16[704,2048]{1,0:T(8,128)(2,1)S(1)} %copy-done.18), channel_id=1, source_target_pairs={{1,0},{0,1},{3,2},{2,3},{5,4},{4,5},{7,6},{6,7},{9,8},{8,9},{11,10... | collective-permute-start | bytes 8650760 | tf_op jit(solution)/shard_map/ppermute | solution.py:55
  241.1 124.5 %copy-start.11 = (bf16[2048,2048]{1,0:T(8,128)(2,1)S(1)}, bf16[2048,2048]{1,0:T(8,128)(2,1)}, u32[]{:S(2)}) copy-start(bf16[2048,2048]{1,0:T(8,128)(2,1)} %slice.226) | copy-start | bytes 25165828
  365.7 10.0 copy-start.6
  365.7 10.0 copy-start.24
  365.7 11.5 %copy-start.30 = (f32[2048]{0:T(1024)S(1)}, f32[2048]{0:T(1024)}, u32[]{:S(2)}) copy-start(f32[2048]{0:T(1024)} %param.21) | copy-start | bytes 24580
  379.3 243.8 %reduce-scatter.6.cloned.1.call-start = ((), (), s32[]{:S(2)}) async-start(), calls=%async_computation.13 | async-start | bytes 8912896 | tf_op jit(solution)/shard_map/reduce_scatter | solution.py:136
  379.3 63.5 %collective-permute-start.7 = (bf16[704,2048]{1,0:T(8,128)(2,1)S(1)}, bf16[704,2048]{1,0:T(8,128)(2,1)}, u32[]{:S(2)}, u32[]{:S(2)}) collective-permute-start(bf16[704,2048]{1,0:T(8,128)(2,1)S(1)} %copy-done.17), channel_id=1, source_target_pairs={{1,0},{0,1},{3,2},{2,3},{5,4},{4,5},{7,6},{6,7},{9,8},{8,9},{11,10... | collective-permute-start | bytes 8650760 | tf_op jit(solution)/shard_map/ppermute | solution.py:55
  520.1 51.8 %all-to-all-start.3 = ((f32[16,1,128]{2,1,0:T(1,128)}), f32[16,1,128]{2,1,0:T(1,128)S(1)}, u32[]{:S(2)}, u32[]{:S(2)}) async-start(f32[16,1,128]{2,1,0:T(1,128)} %get-tuple-element.75), calls=%async_computation.5 | async-start | bytes 16384 | tf_op jit(solution)/shard_map/all_to_all | solution.py:126
  523.6 223.9 %all-gather.8.cloned.1.call-start = ((), (), s32[]{:S(2)}) async-start(), calls=%async_computation.14 | async-start | bytes 8912896 | tf_op jit(solution)/shard_map/all_gather | solution.py:132
  524.1 11.5 %copy-start.49 = (bf16[2048,1408]{1,0:T(8,128)(2,1)S(1)}, bf16[2048,1408]{1,0:T(8,128)(2,1)}, u32[]{:S(2)}) copy-start(bf16[2048,1408]{1,0:T(8,128)(2,1)} %get-tuple-element.71) | copy-start | bytes 17301508
  552.5 70.6 %copy-start.15 = (bf16[128,2048]{1,0:T(8,128)(2,1)S(1)}, bf16[128,2048]{1,0:T(8,128)(2,1)}, u32[]{:S(2)}) copy-start(bf16[128,2048]{1,0:T(8,128)(2,1)} %reduce-scatter.4.cloned.1.call-done) | copy-start | bytes 1572868
  571.9 53.7 %copy-start.16 = (f32[128,2048]{1,0:T(8,128)S(1)}, f32[128,2048]{1,0:T(8,128)}, u32[]{:S(2)}) copy-start(f32[128,2048]{1,0:T(8,128)} %param.31) | copy-start | bytes 3145732
  627.0 372.7 %reduce-scatter.8.cloned.1.call-start = ((), (), s32[]{:S(2)}) async-start(), calls=%async_computation.15 | async-start | bytes 8912896 | tf_op jit(solution)/shard_map/reduce_scatter | solution.py:136
  629.7 7.2 collective-permute-start.8
  639.1 30.6 %collective-permute-start.9 = (bf16[4,64,2048]{2,1,0:T(8,128)(2,1)S(1)}, bf16[4,64,2048]{2,1,0:T(8,128)(2,1)}, u32[]{:S(2)}, u32[]{:S(2)}) collective-permute-start(bf16[4,64,2048]{2,1,0:T(8,128)(2,1)S(1)} %slice_bitcast_fusion.7), channel_id=1, source_target_pairs={{16,0},{0,16},{17,1},{1,17},{18,2},{2,18},{19,3},{3,19},{20,4},{4,... | collective-permute-start | bytes 3145736 | tf_op jit(solution)/shard_map/ppermute | solution.py:55
  641.8 24.3 %collective-permute-start.13 = (bf16[2,64,2048]{2,1,0:T(8,128)(2,1)}, bf16[2,64,2048]{2,1,0:T(8,128)(2,1)}, u32[]{:S(2)}, u32[]{:S(2)}) collective-permute-start(bf16[2,64,2048]{2,1,0:T(8,128)(2,1)} %slice_bitcast_fusion.11), channel_id=1, source_target_pairs={{2,0},{4,2},{6,4},{0,6},{3,1},{5,3},{7,5},{1,7},{10,8},{12,10},{14... | collective-permute-start | bytes 1572872 | tf_op jit(solution)/shard_map/ppermute | solution.py:55
  667.5 49.7 %collective-permute-start.14 = (bf16[2,64,2048]{2,1,0:T(8,128)(2,1)S(1)}, bf16[2,64,2048]{2,1,0:T(8,128)(2,1)S(1)}, u32[]{:S(2)}, u32[]{:S(2)}) collective-permute-start(bf16[2,64,2048]{2,1,0:T(8,128)(2,1)S(1)} %fusion.22), channel_id=1, source_target_pairs={{2,0},{4,2},{6,4},{0,6},{3,1},{5,3},{7,5},{1,7},{10,8},{12,10},{14... | collective-permute-start | bytes 1572872 | tf_op jit(solution)/shard_map/ppermute | solution.py:55
  672.0 45.1 %collective-permute-start.10 = (bf16[64,2048]{1,0:T(8,128)(2,1)S(1)}, bf16[64,2048]{1,0:T(8,128)(2,1)S(1)}, u32[]{:S(2)}, u32[]{:S(2)}) collective-permute-start(bf16[64,2048]{1,0:T(8,128)(2,1)S(1)} %slice_bitcast_fusion.17), channel_id=1, source_target_pairs={{2,0},{4,2},{6,4},{0,6},{3,1},{5,3},{7,5},{1,7},{10,8},{12,10},{14... | collective-permute-start | bytes 786440 | tf_op jit(solution)/shard_map/ppermute | solution.py:55
  673.4 46.1 %copy-start.12 = (bf16[128,2048]{1,0:T(8,128)(2,1)S(1)}, bf16[128,2048]{1,0:T(8,128)(2,1)}, u32[]{:S(2)}) copy-start(bf16[128,2048]{1,0:T(8,128)(2,1)} %multiply_convert_fusion) | copy-start | bytes 1572868
  717.1 10.6 %collective-permute-start.11 = (bf16[64,2048]{1,0:T(8,128)(2,1)S(1)}, bf16[64,2048]{1,0:T(8,128)(2,1)S(1)}, u32[]{:S(2)}, u32[]{:S(2)}) collective-permute-start(bf16[64,2048]{1,0:T(8,128)(2,1)S(1)} %fusion.28), channel_id=1, source_target_pairs={{2,0},{4,2},{6,4},{0,6},{3,1},{5,3},{7,5},{1,7},{10,8},{12,10},{14... | collective-permute-start | bytes 786440 | tf_op jit(solution)/shard_map/ppermute | solution.py:55
  718.4 20.5 %collective-permute-start.15 = (bf16[2,64,2048]{2,1,0:T(8,128)(2,1)S(1)}, bf16[2,64,2048]{2,1,0:T(8,128)(2,1)S(1)}, u32[]{:S(2)}, u32[]{:S(2)}) collective-permute-start(bf16[2,64,2048]{2,1,0:T(8,128)(2,1)S(1)} %fusion.21), channel_id=1, source_target_pairs={{2,0},{4,2},{6,4},{0,6},{3,1},{5,3},{7,5},{1,7},{10,8},{12,10},{14... | collective-permute-start | bytes 1572872 | tf_op jit(solution)/shard_map/ppermute | solution.py:55
  719.8 214.6 %collective-permute-start.28 = (bf16[704,2048]{1,0:T(8,128)(2,1)}, bf16[704,2048]{1,0:T(8,128)(2,1)}, u32[]{:S(2)}, u32[]{:S(2)}) collective-permute-start(bf16[704,2048]{1,0:T(8,128)(2,1)} %convolution_convert_fusion.3), channel_id=1, source_target_pairs={{1,0},{0,1},{3,2},{2,3},{5,4},{4,5},{7,6},{6,7},{9,8},{8,9},{11,10... | collective-permute-start | bytes 8650760 | tf_op jit(solution)/shard_map/ppermute | solution.py:55
  721.3 187.9 %collective-permute-start.27 = (bf16[1408,2048]{1,0:T(8,128)(2,1)}, bf16[1408,2048]{1,0:T(8,128)(2,1)}, u32[]{:S(2)}, u32[]{:S(2)}) collective-permute-start(bf16[1408,2048]{1,0:T(8,128)(2,1)} %convolution_convert_fusion), channel_id=1, source_target_pairs={{1,0},{0,1},{3,2},{2,3},{5,4},{4,5},{7,6},{6,7},{9,8},{8,9},{11,10... | collective-permute-start | bytes 17301512 | tf_op jit(solution)/shard_map/ppermute | solution.py:55
  727.8 15.4 %collective-permute-start.12 = (bf16[64,2048]{1,0:T(8,128)(2,1)S(1)}, bf16[64,2048]{1,0:T(8,128)(2,1)S(1)}, u32[]{:S(2)}, u32[]{:S(2)}) collective-permute-start(bf16[64,2048]{1,0:T(8,128)(2,1)S(1)} %fusion.27), channel_id=1, source_target_pairs={{2,0},{4,2},{6,4},{0,6},{3,1},{5,3},{7,5},{1,7},{10,8},{12,10},{14... | collective-permute-start | bytes 786440 | tf_op jit(solution)/shard_map/ppermute | solution.py:55
  740.1 6.4 collective-permute-start.16
  787.2 37.3 %all-to-all-start.4 = ((f32[16,1,128]{2,1,0:T(1,128)}), f32[16,1,128]{2,1,0:T(1,128)S(1)}, u32[]{:S(2)}, u32[]{:S(2)}) async-start(f32[16,1,128]{2,1,0:T(1,128)} %get-tuple-element.82), calls=%async_computation.7 | async-start | bytes 16384 | tf_op jit(solution)/shard_map/all_to_all | solution.py:126
  809.6 12.5 %copy-start.2 = (f32[2,1,4,2,64,1024]{5,4,3,2,1,0:T(8,128)}, f32[2,1,4,2,64,1024]{5,4,3,2,1,0:T(8,128)S(1)}, u32[]{:S(2)}) copy-start(f32[2,1,4,2,64,1024]{5,4,3,2,1,0:T(8,128)S(1)} %get-tuple-element.97) | copy-start | bytes 12582916
  809.7 12.5 %copy-start.4 = (f32[2,1,4,2,64,1024]{5,4,3,2,1,0:T(8,128)}, f32[2,1,4,2,64,1024]{5,4,3,2,1,0:T(8,128)S(1)}, u32[]{:S(2)}) copy-start(f32[2,1,4,2,64,1024]{5,4,3,2,1,0:T(8,128)S(1)} %get-tuple-element.98) | copy-start | bytes 12582916
  823.9 89.3 %collective-permute-start.22 = (bf16[2,4,2,64,1024]{4,3,1,2,0:T(8,128)(2,1)}, bf16[2,4,2,64,1024]{4,3,1,2,0:T(8,128)(2,1)}, u32[]{:S(2)}, u32[]{:S(2)}) collective-permute-start(bf16[2,4,2,64,1024]{4,3,1,2,0:T(8,128)(2,1)} %fusion.5), channel_id=1, source_target_pairs={{8,0},{0,8},{9,1},{1,9},{10,2},{2,10},{11,3},{3,11},{12,4},{4,12},... | collective-permute-start | bytes 6291464 | tf_op jit(solution)/shard_map/ppermute | solution.py:55
  826.2 9.0 collective-permute-start.17
  831.4 148.9 %collective-permute-start.26 = (bf16[256,2048]{1,0:T(8,128)(2,1)}, bf16[256,2048]{1,0:T(8,128)(2,1)}, u32[]{:S(2)}, u32[]{:S(2)}) collective-permute-start(bf16[256,2048]{1,0:T(8,128)(2,1)} %select_convert_fusion.1), channel_id=1, source_target_pairs={{1,0},{0,1},{3,2},{2,3},{5,4},{4,5},{7,6},{6,7},{9,8},{8,9},{11,10... | collective-permute-start | bytes 3145736 | tf_op jit(solution)/shard_map/ppermute | solution.py:55
  835.2 7.4 collective-permute-start.18
  835.3 77.9 %copy-start.3 = (f32[2,1,4,2,64,1024]{5,4,3,2,1,0:T(8,128)S(1)}, f32[2,1,4,2,64,1024]{5,4,3,2,1,0:T(8,128)}, u32[]{:S(2)}) copy-start(f32[2,1,4,2,64,1024]{5,4,3,2,1,0:T(8,128)} %copy-done.2) | copy-start | bytes 12582916
  835.3 77.9 %copy-start.5 = (f32[2,1,4,2,64,1024]{5,4,3,2,1,0:T(8,128)S(1)}, f32[2,1,4,2,64,1024]{5,4,3,2,1,0:T(8,128)}, u32[]{:S(2)}) copy-start(f32[2,1,4,2,64,1024]{5,4,3,2,1,0:T(8,128)} %copy-done.4) | copy-start | bytes 12582916
  842.6 70.5 %copy-start.9 = (f32[2048,512]{1,0:T(8,128)}, f32[2048,512]{1,0:T(8,128)S(1)}, u32[]{:S(2)}) copy-start(f32[2048,512]{1,0:T(8,128)S(1)} %fusion.1) | copy-start | bytes 12582916
  842.7 68.0 %collective-permute-start.19 = (f32[12,2048]{1,0:T(8,128)S(1)}, f32[12,2048]{1,0:T(8,128)S(1)}, u32[]{:S(2)}, u32[]{:S(2)}) collective-permute-start(f32[12,2048]{1,0:T(8,128)S(1)} %add.149), channel_id=1, source_target_pairs={{0,2},{2,0},{4,6},{6,4},{1,3},{3,1},{5,7},{7,5},{8,10},{10,8},{12,... | collective-permute-start | bytes 294920 | tf_op jit(solution)/shard_map/ppermute | solution.py:95
  909.2 39.6 %collective-permute-start.25 = (bf16[4,256,512]{2,1,0:T(8,128)(2,1)}, bf16[4,256,512]{2,1,0:T(8,128)(2,1)}, u32[]{:S(2)}, u32[]{:S(2)}) collective-permute-start(bf16[4,256,512]{2,1,0:T(8,128)(2,1)} %fusion.9), channel_id=1, source_target_pairs={{1,0},{0,1},{3,2},{2,3},{5,4},{4,5},{7,6},{6,7},{9,8},{8,9},{11,10... | collective-permute-start | bytes 3145736 | tf_op jit(solution)/shard_map/ppermute | solution.py:55
  910.6 23.7 %collective-permute-start.20 = (f32[12,2048]{1,0:T(8,128)S(1)}, f32[12,2048]{1,0:T(8,128)}, u32[]{:S(2)}, u32[]{:S(2)}) collective-permute-start(f32[12,2048]{1,0:T(8,128)S(1)} %add.150), channel_id=1, source_target_pairs={{0,4},{2,6},{4,0},{6,2},{1,5},{3,7},{5,1},{7,3},{8,12},{10,14},{12... | collective-permute-start | bytes 294920 | tf_op jit(solution)/shard_map/ppermute | solution.py:95
  919.6 37.7 %collective-permute-start.23 = (bf16[4,2,64,1024]{3,2,0,1:T(8,128)(2,1)}, bf16[4,2,64,1024]{3,2,0,1:T(8,128)(2,1)}, u32[]{:S(2)}, u32[]{:S(2)}) collective-permute-start(bf16[4,2,64,1024]{3,2,0,1:T(8,128)(2,1)} %fusion.8), channel_id=1, source_target_pairs={{16,0},{0,16},{17,1},{1,17},{18,2},{2,18},{19,3},{3,19},{20,4},{4,... | collective-permute-start | bytes 3145736 | tf_op jit(solution)/shard_map/ppermute | solution.py:55
  935.3 37.5 %collective-permute-start.21 = (f32[12,2048]{1,0:T(8,128)S(1)}, f32[12,2048]{1,0:T(8,128)}, u32[]{:S(2)}, u32[]{:S(2)}) collective-permute-start(f32[12,2048]{1,0:T(8,128)S(1)} %add.151), channel_id=1, source_target_pairs={{0,1},{1,0},{2,3},{3,2},{4,5},{5,4},{6,7},{7,6},{8,9},{9,8},{10,11... | collective-permute-start | bytes 294920 | tf_op jit(solution)/shard_map/ppermute | solution.py:95
  952.9 23.2 %all-to-all-start.6 = ((bf16[4,256,512]{2,1,0:T(8,128)(2,1)}), bf16[4,256,512]{2,1,0:T(8,128)(2,1)}, u32[]{:S(2)}, u32[]{:S(2)}) async-start(bf16[4,256,512]{2,1,0:T(8,128)(2,1)} %fusion.7), calls=%async_computation.9 | async-start | bytes 2097152 | tf_op jit(solution)/shard_map/all_to_all | solution.py:153
  960.6 13.1 %collective-permute-start.24 = (bf16[4,64,1024]{2,1,0:T(8,128)(2,1)S(1)}, bf16[4,64,1024]{2,1,0:T(8,128)(2,1)S(1)}, u32[]{:S(2)}, u32[]{:S(2)}) collective-permute-start(bf16[4,64,1024]{2,1,0:T(8,128)(2,1)S(1)} %fusion.24), channel_id=1, source_target_pairs={{1,0},{0,1},{3,2},{2,3},{5,4},{4,5},{7,6},{6,7},{9,8},{8,9},{11,10... | collective-permute-start | bytes 1572872 | tf_op jit(solution)/shard_map/ppermute | solution.py:55
  976.2 15.7 %all-to-all-start.5 = ((bf16[4,64,1024]{2,1,0:T(8,128)(2,1)}), bf16[4,64,1024]{2,1,0:T(8,128)(2,1)}, u32[]{:S(2)}, u32[]{:S(2)}) async-start(bf16[4,64,1024]{2,1,0:T(8,128)(2,1)} %fusion.23), calls=%async_computation.8 | async-start | bytes 1048576 | tf_op jit(solution)/shard_map/all_to_all | solution.py:153
  987.6 14.6 %copy-start.38 = (f32[2048]{0:T(1024)S(1)}, f32[2048]{0:T(1024)}, u32[]{:S(2)}) copy-start(f32[2048]{0:T(1024)} %param.30) | copy-start | bytes 24580
  987.6 14.6 %copy-start.44 = (f32[128]{0:T(128)S(1)}, f32[128]{0:T(128)}, u32[]{:S(2)}) copy-start(f32[128]{0:T(128)} %get-tuple-element.135) | copy-start | bytes 1540
  (27 other events, 89.9 us)
Sparse Core Ops, SparseCore 0:
  13.6 180.1 all-gather.3
  228.9 105.2 reduce-scatter.3
  379.4 75.6 all-gather.5
  520.2 102.8 reduce-scatter.5
  627.1 98.9 all-gather.7
  787.3 108.7 reduce-scatter.7

commit v6 on v5

--- a/solution.py
+++ b/solution.py
@@ -153,7 +153,7 @@
     return lax.all_to_all(blocks, "o", split_axis=0, concat_axis=0, tiled=True)
 
 
-def gather_heads(places, query_weight, kv_weight):
+def gather_heads(places, query_weight, kv_weight, beside):
     whole = HEADS * HD
     rows = query_weight.shape[0]
     here = exchange(
@@ -166,13 +166,15 @@
             axis=1,
         )
     )
+    here, beside = lax.optimization_barrier((here, beside()))
     span = here.shape[2]
     kv = ring_gather(here[:, rows:].reshape(OUTER, 2, -1, span), "i")
     query_source, _ = lax.optimization_barrier((here[:, :rows], kv[-1]))
     query = in_order(ring_gather(query_source, "i"), "i", 1).reshape(-1, span)
-    kv = jnp.stack(ring_gather(jnp.stack(kv), "y"))
-    kv = jnp.stack(ring_gather(kv, "c"))
-    return query, arrange(places, kv)
+    kv = ring_gather(jnp.stack(kv), "y")
+    seen = kv[-1][0, 0, 0, 0]
+    kv = jnp.stack(ring_gather(jnp.stack(kv), "c"))
+    return query, arrange(places, kv), beside, seen
 
 
 def scatter_query(grad):
@@ -212,13 +214,20 @@
     return add_low(shift(travelling, axis), blocks[0])
 
 
-def part_by_rings(rows):
-    rows = ring_low([rows[k] for k in range(rows.shape[0])], "c")
+def part_low(rows):
+    return ring_low([rows[k] for k in range(rows.shape[0])], "c")
+
+
+def part_first(rows):
     half = rows.shape[2] // 2
     first, second = rows[:, :, :half], rows[:, :, half:]
     first = ring_low([first[k] for k in range(first.shape[0])], "y")
+    second = ring_low([second[:, k] for k in range(second.shape[1])], "o")
+    return first, second
+
+
+def part_second(first, second):
     first = ring_low([first[k] for k in range(first.shape[0])], "o")
-    second = ring_low([second[:, k] for k in range(second.shape[1])], "o")
     second = ring_low([second[k] for k in range(second.shape[0])], "y")
     return jnp.concatenate([first, second])
 
@@ -304,7 +313,6 @@
     gated_ref,
     part_ref,
 ):
-    del places_ref
     length = cos_ref.shape[0]
     span = out_ref.shape[0]
     raw_query = nn(x_ref[...], query_ref[...])
@@ -328,7 +336,7 @@
         gated = (heads_nn(probs.astype(BF16), jnp.stack(values)) * gate[None]).astype(BF16)
         for number, at in enumerate(starts):
             gated_ref[rows, at : at + HD] = gated[number]
-    part_ref[...] = nn(gated_ref[...], out_ref[...]).astype(BF16)
+    place_rows(places_ref, part_ref, nn(gated_ref[...], out_ref[...]).astype(BF16), length)
 
 
 def attend_back_kernel(
@@ -475,11 +483,12 @@
     return found.reshape(-1, kinds * span)
 
 
-def attend(places, both, info, cosine, sine, query_mat, kv_mat, out_mat):
-    count = both.shape[0]
-    span, width = out_mat.shape
+def attend(places, rows, info, cosine, sine, query_mat, kv_mat, out_mat):
+    count, width = rows.shape
+    span = out_mat.shape[0]
     length = cosine.shape[0]
     step = OUTER * length
+    high = count // (2 * step)
     return call(
         attend_kernel,
         "attend",
@@ -493,15 +502,15 @@
             fixed(kv_mat.shape),
             fixed(out_mat.shape),
         ],
-        [rows_spec(step, 3 * span), rows_spec(step, span), rows_spec(step, width)],
-        [shape((count, 3 * span)), shape((count, span)), shape((count, width))],
+        [rows_spec(step, 3 * span), rows_spec(step, span), place_spec(high, length, width)],
+        [shape((count, 3 * span)), shape((count, span)), shape((2, high, OUTER, length, width))],
         2 * count * width * 4 * span + 4 * count * length * span,
         4 * count * (width + 2 * span),
-        (places, both, info, cosine, sine, query_mat, kv_mat, out_mat),
-    )
-
-
-def attend_back(places, d_middle, info, cosine, sine, qkv, both, query_mat, kv_mat, out_mat):
+        (places, rows, info, cosine, sine, query_mat, kv_mat, out_mat),
+    )
+
+
+def attend_back(places, d_middle, info, cosine, sine, qkv, rows, query_mat, kv_mat, out_mat):
     count, width = d_middle.shape
     length = cosine.shape[0]
     step = OUTER * length
@@ -537,7 +546,7 @@
         ],
         2 * count * width * 4 * span + 10 * count * length * span,
         4 * count * (2 * width + 3 * span),
-        (places, d_middle, info, cosine, sine, qkv, both, query_mat, kv_mat, out_mat),
+        (places, d_middle, info, cosine, sine, qkv, rows, query_mat, kv_mat, out_mat),
     )
 
 
@@ -560,66 +569,68 @@
     )
 
 
-def units_kernel(parts, places_ref, x_ref, info_ref, *refs):
+def units_kernel(places_ref, x_ref, info_ref, d_units_ref, first_ref, second_ref, *refs):
     del places_ref
-    d_units_refs, up_refs = refs[:parts], refs[parts : 3 * parts]
-    d_both_refs, gated_refs = refs[3 * parts : 4 * parts], refs[4 * parts : 5 * parts]
-    back_ref, d_gate_ref = refs[5 * parts :]
+    sums_refs, (d_both_ref, gated_ref, back_ref, d_gate_ref) = refs[:-4], refs[-4:]
     length = info_ref.shape[2]
     seqs = info_ref.shape[0]
+    units = first_ref.shape[0]
     rows = x_ref[...]
     gate = jnp.concatenate([as_column(info_ref[seq], length) for seq in range(seqs)], axis=0)
-    back = jnp.zeros((seqs * length, back_ref.shape[-1]), F32)
-    d_gate = jnp.zeros((seqs * length, 1), F32)
-    for part in range(parts):
-        first_ref, second_ref = up_refs[2 * part : 2 * part + 2]
-        units = first_ref.shape[0]
-        gate_in = nt(rows, first_ref[...])
-        up_in = nt(rows, second_ref[...])
-        sigma = jax.nn.sigmoid(gate_in)
-        active = gate_in * sigma
-        hidden_units = active * up_in
-        d_units = d_units_refs[part][...].astype(F32)
-        d_gate = d_gate + jnp.sum(hidden_units * d_units, axis=-1, keepdims=True)
-        gated_refs[part][...] = (hidden_units * gate).astype(BF16)
-        d_units = d_units * gate
-        d_first = (d_units * up_in * (sigma + active * (1.0 - sigma))).astype(BF16)
-        d_second = (d_units * active).astype(BF16)
-        d_both_refs[part][:, :units] = d_first
-        d_both_refs[part][:, units:] = d_second
-        back = back + nn(d_first, first_ref[...]) + nn(d_second, second_ref[...])
-    back_ref[...] = back.astype(BF16)
+    gate_in = nt(rows, first_ref[...])
+    up_in = nt(rows, second_ref[...])
+    sigma = jax.nn.sigmoid(gate_in)
+    active = gate_in * sigma
+    hidden_units = active * up_in
+    d_units = d_units_ref[...].astype(F32)
+    d_gate = jnp.sum(hidden_units * d_units, axis=-1, keepdims=True)
+    gated_ref[...] = (hidden_units * gate).astype(BF16)
+    d_units = d_units * gate
+    d_first = (d_units * up_in * (sigma + active * (1.0 - sigma))).astype(BF16)
+    d_second = (d_units * active).astype(BF16)
+    d_both_ref[:, :units] = d_first
+    d_both_ref[:, units:] = d_second
+    back = nn(d_first, first_ref[...]) + nn(d_second, second_ref[...])
+    if sums_refs:
+        back = back + sums_refs[0][...]
+    back_ref[...] = back.astype(back_ref.dtype)
     for seq in range(seqs):
         column = jnp.broadcast_to(d_gate[seq * length : (seq + 1) * length], (length, length))
         d_gate_ref[seq] = column.T[:1]
 
 
-def run_units(places, rows, info, d_units, own_up, other_up):
+def run_units(places, rows, info, d_units, first, second, sums, last):
     count, width = rows.shape
     length = info.shape[2]
-    parts = 1 + len(other_up) // 2
-    units = d_units[0].shape[1]
+    units = d_units.shape[1]
     seqs = ROW_STEP // length
-    own_specs = [
-        pl.BlockSpec((units, width), lambda step, places, half=half: (half, 0)) for half in range(2)
-    ]
+
+    def weight_spec(block):
+        return pl.BlockSpec((units, width), lambda step, places: (block, 0))
+
+    extra = [] if sums is None else [sums]
     return call(
-        functools.partial(units_kernel, parts),
+        units_kernel,
         "units",
         count // ROW_STEP,
-        [rows_spec(ROW_STEP, width), info_spec(seqs, 1, length)]
-        + [rows_spec(ROW_STEP, units)] * parts
-        + own_specs
-        + [fixed(one.shape) for one in other_up],
-        [rows_spec(ROW_STEP, 2 * units)] * parts
-        + [rows_spec(ROW_STEP, units)] * parts
-        + [rows_spec(ROW_STEP, width), info_spec(seqs, 1, length)],
-        [shape((count, 2 * units))] * parts
-        + [shape((count, units))] * parts
-        + [shape((count, width)), shape((count // length, 1, length), F32)],
-        8 * count * width * units * parts,
-        4 * count * (width + 2 * units * parts),
-        (places, rows, info, *d_units, own_up, own_up, *other_up),
+        [rows_spec(ROW_STEP, width), info_spec(seqs, 1, length), rows_spec(ROW_STEP, units)]
+        + [weight_spec(first[1]), weight_spec(second[1])]
+        + [rows_spec(ROW_STEP, width) for _ in extra],
+        [
+            rows_spec(ROW_STEP, 2 * units),
+            rows_spec(ROW_STEP, units),
+            rows_spec(ROW_STEP, width),
+            info_spec(seqs, 1, length),
+        ],
+        [
+            shape((count, 2 * units)),
+            shape((count, units)),
+            shape((count, width), BF16 if last else F32),
+            shape((count // length, 1, length), F32),
+        ],
+        0,
+        0,
+        (places, rows, info, d_units, first[0], second[0], *extra),
     )
 
 
@@ -650,44 +661,53 @@
     places = own_places()
     tie = lax.optimization_barrier
 
-    query_mat, kv_mat = gather_heads(places, query_weight[0], kv_weight)
-    out_source, _ = tie((out_weight[0], query_mat[:16, :128]))
-    out_parts = ring_gather(out_source, "i")
-    out_mat = in_order(out_parts, "i").reshape(span, width)
+    query_mat, kv_mat, down_parts, seen = gather_heads(
+        places, query_weight[0], kv_weight, lambda: ring_gather(down_weight[0], "i")
+    )
+    out_source, _ = tie((out_weight[0], seen))
+    out_mat = in_order(ring_gather(out_source, "i"), "i").reshape(span, width)
     own_up = up_weight[0].reshape(-1, width)
-    down_source, _ = tie((down_weight[0], out_parts[-1]))
-    down_parts = ring_gather(down_source, "i")
 
     residual = hidden_in.astype(F32)
     normed_one, inverse_one = norm_rows(residual, norm_gain1)
     attn_input = normed_one.astype(BF16)
     att_gate, att_onehot = pair_gates(attn_input, att_router, att_route, experts)
     info = to_experts(att_gate, att_onehot, segment_ids[0].astype(F32))
-    both = meet(jnp.concatenate([attn_input, cotangent.astype(BF16)], axis=1))
+    all_attn = meet(attn_input)
+    cot_low, _ = tie((cotangent.astype(BF16), seen))
+    all_cot = meet(cot_low)
     qkv, gated, branch = attend(
-        places, both, info, cosine, sine_table, query_mat, kv_mat, out_mat
-    )
-    first_source, branch, both = tie((up_weight[0, 0], branch, both))
-    first_parts = ring_gather(first_source, "i")
-    all_attn, all_cot = both[:, :width], both[:, width:]
-    branch = part(branch)
-
-    all_cot, first_parts, down_parts = tie((all_cot, first_parts, down_parts))
+        places, all_attn, info, cosine, sine_table, query_mat, kv_mat, out_mat
+    )
+    up_source, branch = tie((own_up, branch))
+    branch = part_second(*part_first(part_low(branch)))
+
     d_units = [mm("td,fd->tf", all_cot, down).astype(BF16) for down in down_parts]
     branch, d_units = tie((branch, d_units))
     middle = residual + branch.astype(F32) + att_bias
     normed_two, inverse_two = norm_rows(middle, norm_gain2)
     mlp_input = normed_two.astype(BF16)
     mlp_gate, mlp_onehot = pair_gates(mlp_input, mlp_router, mlp_route, experts)
-    second_source, mlp_input = tie((up_weight[0, 1], mlp_input))
-    second_parts = ring_gather(second_source, "i")
+    up_parts = ring_gather(up_source, "i")
     all_mlp = meet(mlp_input)
     gate_m = to_experts(mlp_gate, mlp_onehot, None)
-    gate_m, second_parts = tie((gate_m, second_parts))
-    other_up = [one for pair in zip(first_parts[1:], second_parts[1:]) for one in pair]
-    found = run_units(places, all_mlp, gate_m, d_units, own_up, other_up)
-    d_both, gated_units = found[:inner], found[inner : 2 * inner]
-    rows_back, d_gate_m = found[2 * inner :]
+    d_both, gated_units, rows_back, d_gate_m = [], [], None, None
+    for number, up in enumerate(up_parts):
+        source = own_up if number == 0 else up
+        found = run_units(
+            places,
+            all_mlp,
+            gate_m,
+            d_units[number],
+            (source, 0),
+            (source, 1),
+            rows_back,
+            number == inner - 1,
+        )
+        d_both.append(found[0])
+        gated_units.append(found[1])
+        rows_back = found[2]
+        d_gate_m = found[3] if d_gate_m is None else d_gate_m + found[3]
     d_mlp_input = part(rows_back)
     d_mlp_gate = from_experts(d_gate_m[:, 0], mlp_onehot, experts)
     grad_up = [mm("tf,td->fd", d_here, all_mlp) for d_here in d_both]
@@ -712,21 +732,21 @@
     )
 
     all_mid = meet(d_middle.astype(BF16))
-    rows_out = part_by_rings(rows_out)
-    all_mid, rows_out = tie((all_mid, rows_out))
+    rows_out, all_mid = tie((part_first(part_low(rows_out)), all_mid))
+    rows_out = part_second(*rows_out)
+    d_heads, d_kv, rows_one, d_gate_a, d_gain_a = attend_back(
+        places, all_mid, info, cosine, sine_table, qkv, all_attn, query_mat, kv_mat, out_mat
+    )
     layer_out = middle + rows_out.astype(F32) + mlp_bias
-    d_heads, d_kv, rows_one, d_gate_a, d_gain_a = attend_back(
-        places, all_mid, info, cosine, sine_table, qkv, both, query_mat, kv_mat, out_mat
-    )
     d_attn_input = part(rows_one)
     d_att_gate = from_experts(d_gate_a[:, 0], att_onehot, experts)
     d_kv_weight = scatter_kv(mm("td,tf->df", all_attn, d_kv))
     d_query = scatter_query(mm("td,tf->df", all_attn, d_heads))[None]
     d_out = mm("tf,td->fd", gated, all_mid).reshape(inner, -1, width)
     d_output = ring_scatter(from_order([d_out[k] for k in range(inner)], "i"), "i")[None]
-    d_upper = ring_scatter(grad_up, "i", rows_one)
+    d_upper = ring_scatter(grad_up, "i", d_attn_input)
     d_upper = d_upper.reshape(up_weight.shape)
-    d_lower = ring_scatter(grad_down, "i", rows_one)[None]
+    d_lower = ring_scatter(grad_down, "i", d_attn_input)[None]
     d_att_router, d_att_from_router = gates_back(
         att_gate, att_onehot, d_att_gate, attn_input, att_router
     )

time: 1020 us -> 932 us (0.914)
  waiting for transfers between devices: 449 us -> 344 us
  starting transfers between devices: 64.9 us -> 87.1 us
  blocking collectives: 87 us -> 71.2 us
  other arithmetic: 77.7 us -> 90.5 us
    ppermute x24 -> x32, waiting for transfers between devices: 378 us -> 205 us  [shift(): return lax.ppermute(value, axis, [((k + 1) % size, k) for k in range(size)])]
    all_gather x3 -> x4, waiting for transfers between devices: 12.3 us -> 73.6 us  [meet(): return lax.all_gather(rows, GROUP, axis=0, tiled=True)]
    ppermute x24 -> x32, starting transfers between devices: 34.3 us -> 55.1 us  [shift(): return lax.ppermute(value, axis, [((k + 1) % size, k) for k in range(size)])]
    all_to_all x1, blocking collectives: 75.1 us -> 58.9 us  [exchange(): return lax.all_to_all(blocks, 'o', split_axis=0, concat_axis=0, tiled=True)]
    pallas_call x5 -> x6, Pallas kernels: 164 us -> 171 us  [call(): pl.pallas_call(kernel, grid_spec=pltpu.PrefetchScalarGridSpec(num_scalar_...]
    reduce_scatter x3 -> x2, waiting for transfers between devices: 51 us -> 50.1 us  [part(): return lax.psum_scatter(rows, GROUP, scatter_dimension=0, tiled=True)]
  transfers between devices with their start and end apart: 40 -> 48, of which waited for: 20 -> 26; matrix products, arithmetic and copies ran while one was open for 21% -> 22% of each run, Pallas kernels for 7% -> 15%
where the time goes in v6:
time: 932 us; the launch traced here: 928 us
  waiting for transfers between devices  344 us (37%)
  Pallas kernels  171 us (18%)
  matrix products  119 us (13%)
  other arithmetic  90.5 us (10%)
  starting transfers between devices  87.1 us (9%)
  blocking collectives  71.2 us (8%)
  local copies, waits for them, and re-layouts  30.1 us (3%)
  between operations  15.4 us (2%)
    ppermute x32, waiting for transfers between devices, shift(): return lax.ppermute(value, axis, [((k + 1) % size, k) for k in range(size)])  205 us
    pallas_call x6, Pallas kernels, call(): pl.pallas_call(kernel, grid_spec=pltpu.PrefetchScalarGridSpec(num_scalar_...  171 us
    dot_general x9, matrix products, mm(): return jnp.einsum(form, first, second, preferred_element_type=F32)  112 us
    all_gather x4, waiting for transfers between devices, meet(): return lax.all_gather(rows, GROUP, axis=0, tiled=True)  73.6 us
    all_to_all x1, blocking collectives, exchange(): return lax.all_to_all(blocks, 'o', split_axis=0, concat_axis=0, tiled=True)  58.9 us
    ppermute x32, starting transfers between devices, shift(): return lax.ppermute(value, axis, [((k + 1) % size, k) for k in range(size)])  55.1 us
    reduce_scatter x2, waiting for transfers between devices, part(): return lax.psum_scatter(rows, GROUP, scatter_dimension=0, tiled=True)  50.1 us
    add x3, other arithmetic, ring_scatter(): return arrived.astype(F32) + blocks[0]  20.9 us
  transfers between devices with their start and end apart: 48, of which 26 were waited for; matrix products, arithmetic and copies ran while one was open for 22% of the time, Pallas kernels for 15%

profile of v6, /device:TPU:0, one launch (start us, length us, event | category | flops | bytes accessed | tf_op | source)
XLA Modules:
  0.0 927.6 jit_solution(562213601541546581)
XLA Ops:
  11.2 3.0 collective-permute-start
  15.7 58.9 %all_to_all.37 = bf16[4,384,512]{2,1,0:T(8,128)(2,1)S(1)} all-to-all(bf16[4,384,512]{2,1,0:T(8,128)(2,1)S(1)} %maximum_maximum_fusion), channel_id=1, replica_groups=mesh['y'=2,'c'=2,'o'=4,'i'=2] {'o'}, dimensions={0} | all-to-all | bytes 3145728 | tf_op jit(solution)/shard_map/all_to_all | solution.py:153
  78.8 11.4 %collective-permute-done.1 = bf16[4,2,64,512]{3,2,1,0:T(8,128)(2,1)S(1)} collective-permute-done((bf16[4,2,64,512]{3,2,1,0:T(8,128)(2,1)S(1)}, bf16[4,2,64,512]{3,2,1,0:T(8,128)(2,1)S(1)}, u32[]{:S(2)}, u32[]{:S(2)}) %collective-permute-start.1) | collective-permute-done | bytes 524320 | tf_op jit(solution)/shard_map/ppermute | solution.py:55
  94.2 23.6 %collective-permute-done.3 = bf16[2,4,2,64,512]{4,3,2,1,0:T(8,128)(2,1)S(1)} collective-permute-done((bf16[2,4,2,64,512]{4,3,2,1,0:T(8,128)(2,1)S(1)}, bf16[2,4,2,64,512]{4,3,2,1,0:T(8,128)(2,1)S(1)}, u32[]{:S(2)}, u32[]{:S(2)}) %collective-permute-start.3) | collective-permute-done | bytes 1048608 | tf_op jit(solution)/shard_map/ppermute | solution.py:55
  120.9 3.1 fusion.52
  124.8 4.8 all-to-all-start
  132.1 13.8 %collective-permute-done.2 = bf16[4,256,512]{2,1,0:T(8,128)(2,1)} collective-permute-done((bf16[4,256,512]{2,1,0:T(8,128)(2,1)}, bf16[4,256,512]{2,1,0:T(8,128)(2,1)}, u32[]{:S(2)}, u32[]{:S(2)}) %collective-permute-start.2) | collective-permute-done | bytes 1048608 | tf_op jit(solution)/shard_map/ppermute | solution.py:55
  149.3 17.2 %collective-permute-done.5 = bf16[256,2048]{1,0:T(8,128)(2,1)S(1)} collective-permute-done((bf16[256,2048]{1,0:T(8,128)(2,1)}, bf16[256,2048]{1,0:T(8,128)(2,1)S(1)}, u32[]{:S(2)}, u32[]{:S(2)}) %collective-permute-start.5) | collective-permute-done | bytes 1048608 | tf_op jit(solution)/shard_map/ppermute | solution.py:55
  168.1 4.0 pad_maximum_fusion.in_ref
  172.1 7.4 arrange.1
  180.2 33.3 %attend.1 = (bf16[2048,1536]{1,0:T(8,128)(2,1)}, bf16[2048,512]{1,0:T(8,128)(2,1)}, bf16[2,2,4,128,2048]{4,3,2,1,0:T(8,128)(2,1)}) custom-call(s32[4]{0:T(128)} %pad_add_fusion.places_ref, bf16[2048,2048]{1,0:T(8,128)(2,1)} %all-gather.5.cloned.1.call-done.x_ref, f32[16,2,128]{2,1,0:T(2,128)} %copy-done.32, f32[128,128]{1,0:T(8,128)} %get-tuple-element.139.cos_ref, ...), custom_call_target="tpu_custom_call" | custom-call | flops 17716740096 | bytes 25165824 | tf_op jit(solution)/shard_map/attend/pallas_call | solution.py:432
  216.2 7.1 collective-permute-done.6
  225.4 3.4 collective-permute-start.11
  229.6 10.8 %collective-permute-done.11 = bf16[2,64,2048]{2,1,0:T(8,128)(2,1)S(1)} collective-permute-done((bf16[2,64,2048]{2,1,0:T(8,128)(2,1)S(1)}, bf16[2,64,2048]{2,1,0:T(8,128)(2,1)S(1)}, u32[]{:S(2)}, u32[]{:S(2)}) %collective-permute-start.11) | collective-permute-done | bytes 524320 | tf_op jit(solution)/shard_map/ppermute | solution.py:55
  240.5 4.5 collective-permute-start.12
  245.0 11.3 %convolution_convert_fusion.1.d_units_ref = bf16[2048,704]{1,0:T(8,128)(2,1)} fusion(bf16[2048,2048]{1,0:T(8,128)(2,1)} %all-gather.7.cloned.1.call-done, bf16[704,2048]{1,0:T(8,128)(2,1)} %collective-permute-done.refs_3_), kind=kOutput, calls=%fused_computation.14 | convolution fusion | flops 5907021824 | bytes 14155776 | tf_op jit(solution)/shard_map/td,fd->tf/dot_general | solution.py:140
  256.5 3.7 collective-permute-start.13
  260.7 8.1 convolution_convert_fusion.2.d_units_ref
  268.8 6.8 collective-permute-done.8
  275.6 4.3 collective-permute-start.9
  280.7 3.1 collective-permute-done.9
  283.9 4.3 collective-permute-start.10
  288.3 3.8 collective-permute-done.10
  296.9 12.3 %all_to_all.38.info_ref = f32[16,1,128]{2,1,0:T(1,128)} all-to-all(f32[16,1,128]{2,1,0:T(1,128)S(1)} %bitcast.318), channel_id=1, replica_groups=mesh['y'=2,'c'=2,'o'=4,'i'=2] {'y','c','o'}, dimensions={0} | all-to-all | bytes 16384 | tf_op jit(solution)/shard_map/all_to_all | solution.py:122
  309.2 60.4 %all-gather.9.cloned.1.call-done.x_ref = bf16[2048,2048]{1,0:T(8,128)(2,1)} async-done(((bf16[128,2048]{1,0:T(8,128)(2,1)}), bf16[2048,2048]{1,0:T(8,128)(2,1)}) %all-gather.9.cloned.1.call-update) | async-done | bytes 8388624 | tf_op jit(solution)/shard_map/all_gather | solution.py:132
  369.6 35.5 %units.2 = (bf16[2048,1408]{1,0:T(8,128)(2,1)}, bf16[2048,704]{1,0:T(8,128)(2,1)}, f32[2048,2048]{1,0:T(8,128)}, f32[16,1,128]{2,1,0:T(1,128)}) custom-call(s32[4]{0:T(128)} %pad_add_fusion.places_ref, bf16[2048,2048]{1,0:T(8,128)(2,1)} %all-gather.9.cloned.1.call-done.x_ref, f32[16,1,128]{2,1,0:T(1,128)} %all_to_all.38.info_ref, ...), custom_call_target="tpu_custom_call" | custom-call | tf_op jit(solution)/shard_map/units/pallas_call | solution.py:432
  405.1 10.6 %collective-permute-done.15.first_ref.second_ref = bf16[1408,2048]{1,0:T(8,128)(2,1)} collective-permute-done((bf16[1408,2048]{1,0:T(8,128)(2,1)}, bf16[1408,2048]{1,0:T(8,128)(2,1)}, u32[]{:S(2)}, u32[]{:S(2)}) %collective-permute-start.15) | collective-permute-done | bytes 5767200 | tf_op jit(solution)/shard_map/ppermute | solution.py:55
  415.7 35.9 %units.3 = (bf16[2048,1408]{1,0:T(8,128)(2,1)}, bf16[2048,704]{1,0:T(8,128)(2,1)}, bf16[2048,2048]{1,0:T(8,128)(2,1)}, f32[16,1,128]{2,1,0:T(1,128)}) custom-call(s32[4]{0:T(128)} %pad_add_fusion.places_ref, bf16[2048,2048]{1,0:T(8,128)(2,1)} %all-gather.9.cloned.1.call-done.x_ref, f32[16,1,128]{2,1,0:T(1,128)} %all_to_all.38.info_ref, ...), custom_call_target="tpu_custom_call" | custom-call | tf_op jit(solution)/shard_map/units/pallas_call | solution.py:432
  452.9 5.4 all-to-all-start.3
  458.8 11.7 %convolution_convert_fusion.3 = bf16[704,2048]{1,0:T(8,128)(2,1)} fusion(bf16[2048,704]{1,0:T(8,128)(2,1)} %get-tuple-element.66.refs_1_, bf16[2048,2048]{1,0:T(8,128)(2,1)} %all-gather.7.cloned.1.call-done), kind=kOutput, calls=%fused_computation.16 | convolution fusion | flops 5907021824 | bytes 14155776 | tf_op jit(solution)/shard_map/tf,td->fd/dot_general | solution.py:140
  470.4 16.9 %convolution_convert_fusion = bf16[1408,2048]{1,0:T(8,128)(2,1)} fusion(bf16[2048,1408]{1,0:T(8,128)(2,1)S(1)} %copy-done.48, bf16[2048,2048]{1,0:T(8,128)(2,1)} %all-gather.9.cloned.1.call-done.x_ref), kind=kOutput, calls=%fused_computation.5 | convolution fusion | flops 11814043648 | bytes 19922944 | tf_op jit(solution)/shard_map/tf,td->fd/dot_general | solution.py:140
  487.4 19.4 %layer_rows.1 = bf16[2,2,4,128,2048]{4,3,2,1,0:T(8,128)(2,1)} custom-call(s32[4]{0:T(128)} %pad_add_fusion.places_ref, bf16[2048,704]{1,0:T(8,128)(2,1)} %get-tuple-element.67.refs_0_, bf16[2048,704]{1,0:T(8,128)(2,1)} %get-tuple-element.66.refs_1_, bf16[704,2048]{1,0:T(8,128)(2,1)} %bitcast.334, bf16[704,2048]{1,0:T(8,128)(2,1)} %collective-permute-done.refs_3_), custom_call_target="tpu_custom_call" | custom-call | flops 11811160064 | bytes 28311552 | tf_op jit(solution)/shard_map/layer_rows/pallas_call | solution.py:432
  506.9 50.1 %reduce-scatter.3.cloned.1.call-done = bf16[128,2048]{1,0:T(8,128)(2,1)} async-done(((bf16[2048,2048]{1,0:T(8,128)(2,1)}), bf16[128,2048]{1,0:T(8,128)(2,1)}) %reduce-scatter.3.cloned.1.call-update) | async-done | bytes 524304 | tf_op jit(solution)/shard_map/reduce_scatter | solution.py:136
  560.9 4.8 slice_bitcast_fusion.1
  565.7 7.5 collective-permute-done.16
  573.2 4.5 fusion
  580.0 19.0 %fusion.65 = f32[1408,2048]{1,0:T(8,128)} fusion(bf16[2048,1408]{1,0:T(8,128)(2,1)} %get-tuple-element.86, bf16[2048,2048]{1,0:T(8,128)(2,1)} %all-gather.9.cloned.1.call-done.x_ref), kind=kOutput, calls=%fused_computation.204 | convolution fusion | flops 11811160064 | bytes 25690112 | tf_op jit(solution)/shard_map/tf,td->fd/dot_general | solution.py:140
  602.3 8.3 fusion.66
  612.7 19.5 %collective-permute-done.19 = bf16[2,64,2048]{2,1,0:T(8,128)(2,1)S(1)} collective-permute-done((bf16[2,64,2048]{2,1,0:T(8,128)(2,1)S(1)}, bf16[2,64,2048]{2,1,0:T(8,128)(2,1)S(1)}, u32[]{:S(2)}, u32[]{:S(2)}) %collective-permute-start.19) | collective-permute-done | bytes 524320 | tf_op jit(solution)/shard_map/ppermute | solution.py:55
  632.4 10.9 %collective-permute-done.17 = bf16[4,64,2048]{2,1,0:T(8,128)(2,1)S(1)} collective-permute-done((bf16[4,64,2048]{2,1,0:T(8,128)(2,1)S(1)}, bf16[4,64,2048]{2,1,0:T(8,128)(2,1)S(1)}, u32[]{:S(2)}, u32[]{:S(2)}) %collective-permute-start.17) | collective-permute-done | bytes 1048608 | tf_op jit(solution)/shard_map/ppermute | solution.py:55
  643.7 4.3 collective-permute-done.20
  648.9 13.2 %all-gather.11.cloned.1.call-done.mid_ref = bf16[2048,2048]{1,0:T(8,128)(2,1)} async-done(((bf16[128,2048]{1,0:T(8,128)(2,1)}), bf16[2048,2048]{1,0:T(8,128)(2,1)}) %all-gather.11.cloned.1.call-update) | async-done | bytes 8388624 | tf_op jit(solution)/shard_map/all_gather | solution.py:132
  662.1 39.7 %attend_back.1 = (bf16[2048,512]{1,0:T(8,128)(2,1)}, bf16[2048,1024]{1,0:T(8,128)(2,1)}, bf16[2048,2048]{1,0:T(8,128)(2,1)}, f32[16,1,128]{2,1,0:T(1,128)}, f32[1,2048]{1,0:T(1,128)}) custom-call(s32[4]{0:T(128)} %pad_add_fusion.places_ref, bf16[2048,2048]{1,0:T(8,128)(2,1)} %all-gather.11.cloned.1.call-done.mid_ref, f32[16,2,128]{2,1,0:T(2,128)} %copy-done.32, ...), custom_call_target="tpu_custom_call" | custom-call | flops 18522046464 | bytes 46137344 | tf_op jit(solution)/shard_map/attend_back/pallas_call | solution.py:432
  701.8 5.1 all-to-all-start.4
  707.7 3.7 collective-permute-start.21
  711.4 14.6 %fusion.62 = f32[2048,1024]{1,0:T(8,128)S(1)} fusion(bf16[2048,2048]{1,0:T(8,128)(2,1)} %all-gather.5.cloned.1.call-done.x_ref, bf16[2048,1024]{1,0:T(8,128)(2,1)} %get-tuple-element.81), kind=kOutput, calls=%fused_computation.201 | convolution fusion | flops 8589934592 | bytes 20971520 | tf_op jit(solution)/shard_map/td,tf->df/dot_general | solution.py:140
  726.0 9.4 %fusion.64 = f32[512,2048]{1,0:T(8,128)} fusion(bf16[2048,512]{1,0:T(8,128)(2,1)S(1)} %copy-done.52, bf16[2048,2048]{1,0:T(8,128)(2,1)} %all-gather.11.cloned.1.call-done.mid_ref), kind=kOutput, calls=%fused_computation.203 | convolution fusion | flops 4294967296 | bytes 14680064 | tf_op jit(solution)/shard_map/tf,td->fd/dot_general | solution.py:140
  737.2 12.8 %fusion.63 = f32[2048,512]{1,0:T(8,128)} fusion(bf16[2048,2048]{1,0:T(8,128)(2,1)} %all-gather.5.cloned.1.call-done.x_ref, bf16[2048,512]{1,0:T(8,128)(2,1)S(1)} %copy-done.53), kind=kOutput, calls=%fused_computation.202 | convolution fusion | flops 4294967296 | bytes 14680064 | tf_op jit(solution)/shard_map/td,tf->df/dot_general | solution.py:140
  755.1 3.5 select_convert_fusion.1
  766.2 6.4 collective-permute-done.27
  773.3 4.4 bitcast_add_fusion
  791.1 4.2 all-to-all-start.6
  795.4 17.5 %collective-permute-done.31 = bf16[4,2,64,1024]{3,2,0,1:T(8,128)(2,1)} collective-permute-done((bf16[4,2,64,1024]{3,2,0,1:T(8,128)(2,1)}, bf16[4,2,64,1024]{3,2,0,1:T(8,128)(2,1)}, u32[]{:S(2)}, u32[]{:S(2)}) %collective-permute-start.31) | collective-permute-done | bytes 1048608 | tf_op jit(solution)/shard_map/ppermute | solution.py:55
  815.1 3.1 bitcast_add_fusion.2
  819.1 2.9 collective-permute-start.32
  824.7 5.6 collective-permute-done.23
  832.0 2.8 collective-permute-done.32
  835.9 7.9 all-to-all-start.5
  843.8 4.5 add_bitcast_fusion.1
  851.1 7.4 all-to-all-done.5
  866.3 26.0 %collective-permute-done.36 = bf16[704,2048]{1,0:T(8,128)(2,1)} collective-permute-done((bf16[704,2048]{1,0:T(8,128)(2,1)}, bf16[704,2048]{1,0:T(8,128)(2,1)}, u32[]{:S(2)}, u32[]{:S(2)}) %collective-permute-start.36) | collective-permute-done | bytes 2883616 | tf_op jit(solution)/shard_map/ppermute | solution.py:55
  896.8 7.4 add_bitcast_fusion
  904.1 13.3 %convert_add_fusion = f32[1408,2048]{1,0:T(8,128)} fusion(f32[1408,2048]{1,0:T(8,128)} %fusion.65, bf16[1408,2048]{1,0:T(8,128)(2,1)} %collective-permute-done.35), kind=kLoop, calls=%fused_computation | loop fusion | flops 5767168 | bytes 28835840 | tf_op jit(solution)/shard_map/add | solution.py:73
  917.5 3.0 fusion.16
  (292 shorter events, 105.1 us)
Async XLA Ops:
  7.2 288.0 %copy-start = (f32[2048,4]{0,1:T(4,128)S(1)}, f32[2048,4]{0,1:T(4,128)}, u32[]{:S(2)}) copy-start(f32[2048,4]{0,1:T(4,128)} %param.23) | copy-start | bytes 98308
  7.2 172.4 %all-gather.5.cloned.1.call-start = ((), (), s32[]{:S(2)}) async-start(), calls=%async_computation.9 | async-start | bytes 8912896 | tf_op jit(solution)/shard_map/all_gather | solution.py:132
  11.1 233.9 %all-gather.7.cloned.1.call-start = ((), (), s32[]{:S(2)}) async-start(), calls=%async_computation.10 | async-start | bytes 8912896 | tf_op jit(solution)/shard_map/all_gather | solution.py:132
  11.2 65.8 %collective-permute-start = (bf16[704,2048]{1,0:T(8,128)(2,1)}, bf16[704,2048]{1,0:T(8,128)(2,1)}, u32[]{:S(2)}, u32[]{:S(2)}) collective-permute-start(bf16[704,2048]{1,0:T(8,128)(2,1)} %bitcast.333), channel_id=1, source_target_pairs={{1,0},{0,1},{3,2},{2,3},{5,4},{4,5},{7,6},{6,7},{9,8},{8,9},{11,10... | collective-permute-start | bytes 8650760 | tf_op jit(solution)/shard_map/ppermute | solution.py:55
  15.7 77.1 %copy-start.16 = (f32[128,2048]{1,0:T(8,128)S(1)}, f32[128,2048]{1,0:T(8,128)}, u32[]{:S(2)}) copy-start(f32[128,2048]{1,0:T(8,128)} %param.31) | copy-start | bytes 3145732
  15.7 102.1 %copy-start.11 = (bf16[128,2048]{1,0:T(8,128)(2,1)S(1)}, bf16[128,2048]{1,0:T(8,128)(2,1)}, u32[]{:S(2)}) copy-start(bf16[128,2048]{1,0:T(8,128)(2,1)} %fusion.10) | copy-start | bytes 1572868
  15.7 102.1 %copy-start.26 = (f32[2048,4]{0,1:T(4,128)S(1)}, f32[2048,4]{0,1:T(4,128)}, u32[]{:S(2)}) copy-start(f32[2048,4]{0,1:T(4,128)} %param.22) | copy-start | bytes 98308
  74.6 43.7 %copy-start.34 = (s32[128,2]{0,1:T(2,128)S(1)}, s32[128,2]{0,1:T(2,128)}, u32[]{:S(2)}) copy-start(s32[128,2]{0,1:T(2,128)} %param.18) | copy-start | bytes 3076
  77.0 43.9 %copy-start.51 = (s32[1,128]{1,0:T(1,128)S(1)}, s32[1,128]{1,0:T(1,128)}, u32[]{:S(2)}) copy-start(s32[1,128]{1,0:T(1,128)} %param.17) | copy-start | bytes 1540
  77.0 13.2 %collective-permute-start.1 = (bf16[4,2,64,512]{3,2,1,0:T(8,128)(2,1)S(1)}, bf16[4,2,64,512]{3,2,1,0:T(8,128)(2,1)S(1)}, u32[]{:S(2)}, u32[]{:S(2)}) collective-permute-start(bf16[4,2,64,512]{3,2,1,0:T(8,128)(2,1)S(1)} %bitcast.307), channel_id=1, source_target_pairs={{1,0},{0,1},{3,2},{2,3},{5,4},{4,5},{7,6},{6,7},{9,8},{8,9},{11,10... | collective-permute-start | bytes 1572872 | tf_op jit(solution)/shard_map/ppermute | solution.py:55
  91.3 26.5 %collective-permute-start.3 = (bf16[2,4,2,64,512]{4,3,2,1,0:T(8,128)(2,1)S(1)}, bf16[2,4,2,64,512]{4,3,2,1,0:T(8,128)(2,1)S(1)}, u32[]{:S(2)}, u32[]{:S(2)}) collective-permute-start(bf16[2,4,2,64,512]{4,3,2,1,0:T(8,128)(2,1)S(1)} %get-tuple-element.108), channel_id=1, source_target_pairs={{16,0},{0,16},{17,1},{1,17},{18,2},{2,18},{19,3},{3,19},{20,4},{4,... | collective-permute-start | bytes 3145736 | tf_op jit(solution)/shard_map/ppermute | solution.py:55
  119.5 26.4 %collective-permute-start.2 = (bf16[4,256,512]{2,1,0:T(8,128)(2,1)}, bf16[4,256,512]{2,1,0:T(8,128)(2,1)}, u32[]{:S(2)}, u32[]{:S(2)}) collective-permute-start(bf16[4,256,512]{2,1,0:T(8,128)(2,1)} %slice.263), channel_id=1, source_target_pairs={{1,0},{0,1},{3,2},{2,3},{5,4},{4,5},{7,6},{6,7},{9,8},{8,9},{11,10... | collective-permute-start | bytes 3145736 | tf_op jit(solution)/shard_map/ppermute | solution.py:55
  124.1 44.1 %collective-permute-start.4 = (bf16[2,2,4,2,64,512]{5,4,3,2,1,0:T(8,128)(2,1)}, bf16[2,2,4,2,64,512]{5,4,3,2,1,0:T(8,128)(2,1)}, u32[]{:S(2)}, u32[]{:S(2)}) collective-permute-start(bf16[2,2,4,2,64,512]{5,4,3,2,1,0:T(8,128)(2,1)} %get-tuple-element.98), channel_id=1, source_target_pairs={{8,0},{0,8},{9,1},{1,9},{10,2},{2,10},{11,3},{3,11},{12,4},{4,12},... | collective-permute-start | bytes 6291464 | tf_op jit(solution)/shard_map/ppermute | solution.py:55
  124.8 54.7 %all-to-all-start = ((f32[16,2,128]{2,1,0:T(2,128)}), f32[16,2,128]{2,1,0:T(2,128)S(1)}, u32[]{:S(2)}, u32[]{:S(2)}) async-start(f32[16,2,128]{2,1,0:T(2,128)} %pad_maximum_fusion.8), calls=%async_computation | async-start | bytes 32768 | tf_op jit(solution)/shard_map/all_to_all | solution.py:122
  129.6 240.0 %all-gather.9.cloned.1.call-start = ((), (), s32[]{:S(2)}) async-start(), calls=%async_computation.11 | async-start | bytes 8912896 | tf_op jit(solution)/shard_map/all_gather | solution.py:132
  129.9 36.6 %collective-permute-start.5 = (bf16[256,2048]{1,0:T(8,128)(2,1)}, bf16[256,2048]{1,0:T(8,128)(2,1)S(1)}, u32[]{:S(2)}, u32[]{:S(2)}) collective-permute-start(bf16[256,2048]{1,0:T(8,128)(2,1)} %bitcast.309), channel_id=1, source_target_pairs={{1,0},{0,1},{3,2},{2,3},{5,4},{4,5},{7,6},{6,7},{9,8},{8,9},{11,10... | collective-permute-start | bytes 3145736 | tf_op jit(solution)/shard_map/ppermute | solution.py:55
  216.1 7.2 collective-permute-start.6
  225.4 14.9 %collective-permute-start.11 = (bf16[2,64,2048]{2,1,0:T(8,128)(2,1)S(1)}, bf16[2,64,2048]{2,1,0:T(8,128)(2,1)S(1)}, u32[]{:S(2)}, u32[]{:S(2)}) collective-permute-start(bf16[2,64,2048]{2,1,0:T(8,128)(2,1)S(1)} %slice_bitcast_fusion.17), channel_id=1, source_target_pairs={{2,0},{4,2},{6,4},{0,6},{3,1},{5,3},{7,5},{1,7},{10,8},{12,10},{14... | collective-permute-start | bytes 1572872 | tf_op jit(solution)/shard_map/ppermute | solution.py:55
  229.0 31.2 %collective-permute-start.7 = (bf16[4,64,2048]{2,1,0:T(8,128)(2,1)S(1)}, bf16[4,64,2048]{2,1,0:T(8,128)(2,1)S(1)}, u32[]{:S(2)}, u32[]{:S(2)}) collective-permute-start(bf16[4,64,2048]{2,1,0:T(8,128)(2,1)S(1)} %slice_bitcast_fusion.9), channel_id=1, source_target_pairs={{16,0},{0,16},{17,1},{1,17},{18,2},{2,18},{19,3},{3,19},{20,4},{4,... | collective-permute-start | bytes 3145736 | tf_op jit(solution)/shard_map/ppermute | solution.py:55
  240.5 15.8 %collective-permute-start.12 = (bf16[2,64,2048]{2,1,0:T(8,128)(2,1)S(1)}, bf16[2,64,2048]{2,1,0:T(8,128)(2,1)S(1)}, u32[]{:S(2)}, u32[]{:S(2)}) collective-permute-start(bf16[2,64,2048]{2,1,0:T(8,128)(2,1)S(1)} %fusion.23), channel_id=1, source_target_pairs={{2,0},{4,2},{6,4},{0,6},{3,1},{5,3},{7,5},{1,7},{10,8},{12,10},{14... | collective-permute-start | bytes 1572872 | tf_op jit(solution)/shard_map/ppermute | solution.py:55
  256.5 23.4 %collective-permute-start.13 = (bf16[2,64,2048]{2,1,0:T(8,128)(2,1)S(1)}, bf16[2,64,2048]{2,1,0:T(8,128)(2,1)S(1)}, u32[]{:S(2)}, u32[]{:S(2)}) collective-permute-start(bf16[2,64,2048]{2,1,0:T(8,128)(2,1)S(1)} %fusion.22), channel_id=1, source_target_pairs={{2,0},{4,2},{6,4},{0,6},{3,1},{5,3},{7,5},{1,7},{10,8},{12,10},{14... | collective-permute-start | bytes 1572872 | tf_op jit(solution)/shard_map/ppermute | solution.py:55
  260.6 14.9 %collective-permute-start.8 = (bf16[64,2048]{1,0:T(8,128)(2,1)S(1)}, bf16[64,2048]{1,0:T(8,128)(2,1)S(1)}, u32[]{:S(2)}, u32[]{:S(2)}) collective-permute-start(bf16[64,2048]{1,0:T(8,128)(2,1)S(1)} %slice_bitcast_fusion.23), channel_id=1, source_target_pairs={{2,0},{4,2},{6,4},{0,6},{3,1},{5,3},{7,5},{1,7},{10,8},{12,10},{14... | collective-permute-start | bytes 786440 | tf_op jit(solution)/shard_map/ppermute | solution.py:55
  268.8 23.5 %copy-start.5 = (bf16[128,2048]{1,0:T(8,128)(2,1)S(1)}, bf16[128,2048]{1,0:T(8,128)(2,1)}, u32[]{:S(2)}) copy-start(bf16[128,2048]{1,0:T(8,128)(2,1)} %param.16) | copy-start | bytes 1572868
  268.8 23.5 %copy-start.24 = (f32[2048]{0:T(1024)S(1)}, f32[2048]{0:T(1024)}, u32[]{:S(2)}) copy-start(f32[2048]{0:T(1024)} %param.27) | copy-start | bytes 24580
  268.8 23.8 %copy-start.30 = (f32[2048]{0:T(1024)S(1)}, f32[2048]{0:T(1024)}, u32[]{:S(2)}) copy-start(f32[2048]{0:T(1024)} %param.21) | copy-start | bytes 24580
  275.6 8.2 collective-permute-start.9
  280.1 8.1 collective-permute-start.14
  283.9 8.2 collective-permute-start.10
  293.6 263.4 %reduce-scatter.3.cloned.1.call-start = ((), (), s32[]{:S(2)}) async-start(), calls=%async_computation.12 | async-start | bytes 8912896 | tf_op jit(solution)/shard_map/reduce_scatter | solution.py:136
  293.7 122.0 %collective-permute-start.15 = (bf16[1408,2048]{1,0:T(8,128)(2,1)}, bf16[1408,2048]{1,0:T(8,128)(2,1)}, u32[]{:S(2)}, u32[]{:S(2)}) collective-permute-start(bf16[1408,2048]{1,0:T(8,128)(2,1)} %bitcast.294), channel_id=1, source_target_pairs={{1,0},{0,1},{3,2},{2,3},{5,4},{4,5},{7,6},{6,7},{9,8},{8,9},{11,10... | collective-permute-start | bytes 17301512 | tf_op jit(solution)/shard_map/ppermute | solution.py:55
  452.9 53.9 %all-to-all-start.3 = ((f32[16,1,128]{2,1,0:T(1,128)}), f32[16,1,128]{2,1,0:T(1,128)S(1)}, u32[]{:S(2)}, u32[]{:S(2)}) async-start(f32[16,1,128]{2,1,0:T(1,128)} %add.175), calls=%async_computation.4 | async-start | bytes 16384 | tf_op jit(solution)/shard_map/all_to_all | solution.py:126
  458.3 203.8 %all-gather.11.cloned.1.call-start = ((), (), s32[]{:S(2)}) async-start(), calls=%async_computation.13 | async-start | bytes 8912896 | tf_op jit(solution)/shard_map/all_gather | solution.py:132
  487.4 72.1 %copy-start.17 = (f32[128,2048]{1,0:T(8,128)S(1)}, f32[128,2048]{1,0:T(8,128)}, u32[]{:S(2)}) copy-start(f32[128,2048]{1,0:T(8,128)} %param.31) | copy-start | bytes 3145732
  560.9 331.4 %reduce-scatter.5.cloned.1.call-start = ((), (), s32[]{:S(2)}) async-start(), calls=%async_computation.14 | async-start | bytes 8912896 | tf_op jit(solution)/shard_map/reduce_scatter | solution.py:136
  565.7 7.5 collective-permute-start.16
  573.2 29.1 %slice-start = ((s8[8388608]{0:T(1024)(128)(4,1)}), s8[4194304]{0:T(1024)(128)(4,1)S(1)}, s32[]{:S(2)}) async-start(s8[8388608]{0:T(1024)(128)(4,1)} %bitcast.331), calls=%async_computation.15 | async-start | bytes 8388608
  577.7 22.9 %collective-permute-start.18 = (bf16[2,64,2048]{2,1,0:T(8,128)(2,1)S(1)}, bf16[2,64,2048]{2,1,0:T(8,128)(2,1)S(1)}, u32[]{:S(2)}, u32[]{:S(2)}) collective-permute-start(bf16[2,64,2048]{2,1,0:T(8,128)(2,1)S(1)} %slice_bitcast_fusion.13), channel_id=1, source_target_pairs={{2,0},{4,2},{6,4},{0,6},{3,1},{5,3},{7,5},{1,7},{10,8},{12,10},{14... | collective-permute-start | bytes 1572872 | tf_op jit(solution)/shard_map/ppermute | solution.py:55
  580.0 22.4 %slice-start.1 = ((s8[8388608]{0:T(1024)(128)(4,1)}), s8[4194304]{0:T(1024)(128)(4,1)S(1)}, s32[]{:S(2)}) async-start(s8[8388608]{0:T(1024)(128)(4,1)} %bitcast.331), calls=%async_computation.16 | async-start | bytes 8388608
  580.0 22.4 %copy-start.49 = (bf16[2048,704]{1,0:T(8,128)(2,1)S(1)}, bf16[2048,704]{1,0:T(8,128)(2,1)}, u32[]{:S(2)}) copy-start(bf16[2048,704]{1,0:T(8,128)(2,1)} %get-tuple-element.67.refs_0_) | copy-start | bytes 8650756
  599.1 44.2 %collective-permute-start.17 = (bf16[4,64,2048]{2,1,0:T(8,128)(2,1)S(1)}, bf16[4,64,2048]{2,1,0:T(8,128)(2,1)S(1)}, u32[]{:S(2)}, u32[]{:S(2)}) collective-permute-start(bf16[4,64,2048]{2,1,0:T(8,128)(2,1)S(1)} %slice_bitcast_fusion.7), channel_id=1, source_target_pairs={{16,0},{0,16},{17,1},{1,17},{18,2},{2,18},{19,3},{3,19},{20,4},{4,... | collective-permute-start | bytes 3145736 | tf_op jit(solution)/shard_map/ppermute | solution.py:55
  600.8 31.4 %collective-permute-start.19 = (bf16[2,64,2048]{2,1,0:T(8,128)(2,1)S(1)}, bf16[2,64,2048]{2,1,0:T(8,128)(2,1)S(1)}, u32[]{:S(2)}, u32[]{:S(2)}) collective-permute-start(bf16[2,64,2048]{2,1,0:T(8,128)(2,1)S(1)} %fusion.20), channel_id=1, source_target_pairs={{2,0},{4,2},{6,4},{0,6},{3,1},{5,3},{7,5},{1,7},{10,8},{12,10},{14... | collective-permute-start | bytes 1572872 | tf_op jit(solution)/shard_map/ppermute | solution.py:55
  611.0 285.8 %collective-permute-start.35 = (bf16[1408,2048]{1,0:T(8,128)(2,1)}, bf16[1408,2048]{1,0:T(8,128)(2,1)}, u32[]{:S(2)}, u32[]{:S(2)}) collective-permute-start(bf16[1408,2048]{1,0:T(8,128)(2,1)} %convolution_convert_fusion), channel_id=1, source_target_pairs={{1,0},{0,1},{3,2},{2,3},{5,4},{4,5},{7,6},{6,7},{9,8},{8,9},{11,10... | collective-permute-start | bytes 17301512 | tf_op jit(solution)/shard_map/ppermute | solution.py:55
  632.3 15.7 %collective-permute-start.20 = (bf16[2,64,2048]{2,1,0:T(8,128)(2,1)S(1)}, bf16[2,64,2048]{2,1,0:T(8,128)(2,1)S(1)}, u32[]{:S(2)}, u32[]{:S(2)}) collective-permute-start(bf16[2,64,2048]{2,1,0:T(8,128)(2,1)S(1)} %fusion.19), channel_id=1, source_target_pairs={{2,0},{4,2},{6,4},{0,6},{3,1},{5,3},{7,5},{1,7},{10,8},{12,10},{14... | collective-permute-start | bytes 1572872 | tf_op jit(solution)/shard_map/ppermute | solution.py:55
  643.7 63.3 %copy-start.14 = (bf16[4,64,2048]{2,1,0:T(8,128)(2,1)}, bf16[4,64,2048]{2,1,0:T(8,128)(2,1)S(1)}, u32[]{:S(2)}) copy-start(bf16[4,64,2048]{2,1,0:T(8,128)(2,1)S(1)} %fusion.3) | copy-start | bytes 3145732
  701.8 50.0 %all-to-all-start.4 = ((f32[16,1,128]{2,1,0:T(1,128)}), f32[16,1,128]{2,1,0:T(1,128)S(1)}, u32[]{:S(2)}, u32[]{:S(2)}) async-start(f32[16,1,128]{2,1,0:T(1,128)} %get-tuple-element.78), calls=%async_computation.6 | async-start | bytes 16384 | tf_op jit(solution)/shard_map/all_to_all | solution.py:126
  707.7 56.0 %collective-permute-start.21 = (bf16[64,2048]{1,0:T(8,128)(2,1)}, bf16[64,2048]{1,0:T(8,128)(2,1)}, u32[]{:S(2)}, u32[]{:S(2)}) collective-permute-start(bf16[64,2048]{1,0:T(8,128)(2,1)} %slice_bitcast_fusion.29), channel_id=1, source_target_pairs={{2,0},{4,2},{6,4},{0,6},{3,1},{5,3},{7,5},{1,7},{10,8},{12,10},{14... | collective-permute-start | bytes 786440 | tf_op jit(solution)/shard_map/ppermute | solution.py:55
  751.8 21.5 %collective-permute-start.30 = (bf16[2,4,2,64,1024]{4,3,1,2,0:T(8,128)(2,1)}, bf16[2,4,2,64,1024]{4,3,1,2,0:T(8,128)(2,1)}, u32[]{:S(2)}, u32[]{:S(2)}) collective-permute-start(bf16[2,4,2,64,1024]{4,3,1,2,0:T(8,128)(2,1)} %fusion.2), channel_id=1, source_target_pairs={{8,0},{0,8},{9,1},{1,9},{10,2},{2,10},{11,3},{3,11},{12,4},{4,12},... | collective-permute-start | bytes 6291464 | tf_op jit(solution)/shard_map/ppermute | solution.py:55
  753.6 19.7 %copy-start.3 = (f32[2,1,4,2,64,1024]{5,4,3,2,1,0:T(8,128)S(1)}, f32[2,1,4,2,64,1024]{5,4,3,2,1,0:T(8,128)}, u32[]{:S(2)}) copy-start(f32[2,1,4,2,64,1024]{5,4,3,2,1,0:T(8,128)} %copy-done.2) | copy-start | bytes 12582916
  753.6 6.0 collective-permute-start.25
  759.6 4.0 collective-permute-start.26
  762.1 26.0 %collective-permute-start.33 = (bf16[4,256,512]{2,1,0:T(8,128)(2,1)S(1)}, bf16[4,256,512]{2,1,0:T(8,128)(2,1)S(1)}, u32[]{:S(2)}, u32[]{:S(2)}) collective-permute-start(bf16[4,256,512]{2,1,0:T(8,128)(2,1)S(1)} %fusion.7), channel_id=1, source_target_pairs={{1,0},{0,1},{3,2},{2,3},{5,4},{4,5},{7,6},{6,7},{9,8},{8,9},{11,10... | collective-permute-start | bytes 3145736 | tf_op jit(solution)/shard_map/ppermute | solution.py:55
  763.6 8.9 collective-permute-start.27
  764.8 19.5 %collective-permute-start.22 = (bf16[64,2048]{1,0:T(8,128)(2,1)S(1)}, bf16[64,2048]{1,0:T(8,128)(2,1)S(1)}, u32[]{:S(2)}, u32[]{:S(2)}) collective-permute-start(bf16[64,2048]{1,0:T(8,128)(2,1)S(1)} %fusion.29), channel_id=1, source_target_pairs={{2,0},{4,2},{6,4},{0,6},{3,1},{5,3},{7,5},{1,7},{10,8},{12,10},{14... | collective-permute-start | bytes 786440 | tf_op jit(solution)/shard_map/ppermute | solution.py:55
  772.6 10.6 %collective-permute-start.28 = (f32[12,2048]{1,0:T(8,128)S(1)}, f32[12,2048]{1,0:T(8,128)S(1)}, u32[]{:S(2)}, u32[]{:S(2)}) collective-permute-start(f32[12,2048]{1,0:T(8,128)S(1)} %add.188), channel_id=1, source_target_pairs={{0,4},{2,6},{4,0},{6,2},{1,5},{3,7},{5,1},{7,3},{8,12},{10,14},{12... | collective-permute-start | bytes 294920 | tf_op jit(solution)/shard_map/ppermute | solution.py:95
  780.9 32.0 %collective-permute-start.31 = (bf16[4,2,64,1024]{3,2,0,1:T(8,128)(2,1)}, bf16[4,2,64,1024]{3,2,0,1:T(8,128)(2,1)}, u32[]{:S(2)}, u32[]{:S(2)}) collective-permute-start(bf16[4,2,64,1024]{3,2,0,1:T(8,128)(2,1)} %fusion.6), channel_id=1, source_target_pairs={{16,0},{0,16},{17,1},{1,17},{18,2},{2,18},{19,3},{3,19},{20,4},{4,... | collective-permute-start | bytes 3145736 | tf_op jit(solution)/shard_map/ppermute | solution.py:55
  783.2 35.2 %collective-permute-start.24 = (bf16[64,2048]{1,0:T(8,128)(2,1)}, bf16[64,2048]{1,0:T(8,128)(2,1)S(1)}, u32[]{:S(2)}, u32[]{:S(2)}) collective-permute-start(bf16[64,2048]{1,0:T(8,128)(2,1)} %slice_bitcast_fusion.28), channel_id=1, source_target_pairs={{16,0},{0,16},{17,1},{1,17},{18,2},{2,18},{19,3},{3,19},{20,4},{4,... | collective-permute-start | bytes 786440 | tf_op jit(solution)/shard_map/ppermute | solution.py:55
  784.3 59.5 %collective-permute-start.34 = (bf16[256,2048]{1,0:T(8,128)(2,1)}, bf16[256,2048]{1,0:T(8,128)(2,1)}, u32[]{:S(2)}, u32[]{:S(2)}) collective-permute-start(bf16[256,2048]{1,0:T(8,128)(2,1)} %select_convert_fusion.1), channel_id=1, source_target_pairs={{1,0},{0,1},{3,2},{2,3},{5,4},{4,5},{7,6},{6,7},{9,8},{8,9},{11,10... | collective-permute-start | bytes 3145736 | tf_op jit(solution)/shard_map/ppermute | solution.py:55
  788.2 34.9 %collective-permute-start.29 = (f32[12,2048]{1,0:T(8,128)}, f32[12,2048]{1,0:T(8,128)}, u32[]{:S(2)}, u32[]{:S(2)}) collective-permute-start(f32[12,2048]{1,0:T(8,128)} %add.189), channel_id=1, source_target_pairs={{0,1},{1,0},{2,3},{3,2},{4,5},{5,4},{6,7},{7,6},{8,9},{9,8},{10,11... | collective-permute-start | bytes 294920 | tf_op jit(solution)/shard_map/ppermute | solution.py:95
  791.1 44.8 %all-to-all-start.6 = ((bf16[4,256,512]{2,1,0:T(8,128)(2,1)}), bf16[4,256,512]{2,1,0:T(8,128)(2,1)}, u32[]{:S(2)}, u32[]{:S(2)}) async-start(bf16[4,256,512]{2,1,0:T(8,128)(2,1)} %fusion.5), calls=%async_computation.8 | async-start | bytes 2097152 | tf_op jit(solution)/shard_map/all_to_all | solution.py:153
  795.4 26.6 %copy-start.19 = (bf16[2,64,2048]{2,1,0:T(8,128)(2,1)S(1)}, bf16[2,64,2048]{2,1,0:T(8,128)(2,1)}, u32[]{:S(2)}) copy-start(bf16[2,64,2048]{2,1,0:T(8,128)(2,1)} %fusion.18) | copy-start | bytes 1572868
  812.9 17.4 %collective-permute-start.23 = (bf16[64,2048]{1,0:T(8,128)(2,1)}, bf16[64,2048]{1,0:T(8,128)(2,1)S(1)}, u32[]{:S(2)}, u32[]{:S(2)}) collective-permute-start(bf16[64,2048]{1,0:T(8,128)(2,1)} %fusion.28), channel_id=1, source_target_pairs={{2,0},{4,2},{6,4},{0,6},{3,1},{5,3},{7,5},{1,7},{10,8},{12,10},{14... | collective-permute-start | bytes 786440 | tf_op jit(solution)/shard_map/ppermute | solution.py:55
  819.1 15.7 %collective-permute-start.32 = (bf16[4,64,1024]{2,1,0:T(8,128)(2,1)S(1)}, bf16[4,64,1024]{2,1,0:T(8,128)(2,1)S(1)}, u32[]{:S(2)}, u32[]{:S(2)}) collective-permute-start(bf16[4,64,1024]{2,1,0:T(8,128)(2,1)S(1)} %fusion.25), channel_id=1, source_target_pairs={{1,0},{0,1},{3,2},{2,3},{5,4},{4,5},{7,6},{6,7},{9,8},{8,9},{11,10... | collective-permute-start | bytes 1572872 | tf_op jit(solution)/shard_map/ppermute | solution.py:55
  823.0 69.3 %collective-permute-start.36 = (bf16[704,2048]{1,0:T(8,128)(2,1)}, bf16[704,2048]{1,0:T(8,128)(2,1)}, u32[]{:S(2)}, u32[]{:S(2)}) collective-permute-start(bf16[704,2048]{1,0:T(8,128)(2,1)} %convolution_convert_fusion.3), channel_id=1, source_target_pairs={{1,0},{0,1},{3,2},{2,3},{5,4},{4,5},{7,6},{6,7},{9,8},{8,9},{11,10... | collective-permute-start | bytes 8650760 | tf_op jit(solution)/shard_map/ppermute | solution.py:55
  835.9 22.6 %all-to-all-start.5 = ((bf16[4,64,1024]{2,1,0:T(8,128)(2,1)}), bf16[4,64,1024]{2,1,0:T(8,128)(2,1)}, u32[]{:S(2)}, u32[]{:S(2)}) async-start(bf16[4,64,1024]{2,1,0:T(8,128)(2,1)} %fusion.24), calls=%async_computation.7 | async-start | bytes 1048576 | tf_op jit(solution)/shard_map/all_to_all | solution.py:153
  (40 other events, 290.2 us)
Sparse Core Ops, SparseCore 0:
  11.2 102.2 all-gather.4
  117.9 75.1 all-gather.6
  293.7 75.8 all-gather.8
  451.7 105.2 reduce-scatter.2
  561.0 101.0 all-gather.10
  701.9 122.1 reduce-scatter.4

commit v7 on v6

--- a/solution.py
+++ b/solution.py
@@ -55,6 +55,30 @@
     return lax.ppermute(value, axis, [((k + 1) % size, k) for k in range(size)])
 
 
+def shift_far(value):
+    size = lax.axis_size("i")
+    pairs = [
+        (low * size + (k + 1) % size, (1 - low) * size + k) for k in range(size) for low in range(2)
+    ]
+    return shift(lax.ppermute(value, ("c", "i"), pairs), "c")
+
+
+def far_gather(value):
+    parts = [value]
+    for _ in range(lax.axis_size("i") - 1):
+        parts.append(shift_far(parts[-1]))
+    return parts
+
+
+def far_scatter(blocks, after):
+    size = lax.axis_size("i")
+    travelling = blocks[1].astype(BF16)
+    for j in range(2, size):
+        travelling = (shift_far(travelling).astype(F32) + blocks[j]).astype(BF16)
+    arrived, _ = lax.optimization_barrier((shift_far(travelling), after))
+    return arrived.astype(F32) + blocks[0]
+
+
 def ring_gather(value, axis):
     parts = [value]
     for _ in range(lax.axis_size(axis) - 1):
@@ -62,15 +86,12 @@
     return parts
 
 
-def ring_scatter(blocks, axis, after=None):
+def ring_scatter(blocks, axis):
     size = lax.axis_size(axis)
     travelling = blocks[1].astype(BF16)
     for j in range(2, size):
         travelling = (shift(travelling, axis).astype(F32) + blocks[j]).astype(BF16)
-    arrived = shift(travelling, axis)
-    if after is not None:
-        arrived, _ = lax.optimization_barrier((arrived, after))
-    return arrived.astype(F32) + blocks[0]
+    return shift(travelling, axis).astype(F32) + blocks[0]
 
 
 def in_order(parts, axis, place=0):
@@ -170,8 +191,10 @@
     span = here.shape[2]
     kv = ring_gather(here[:, rows:].reshape(OUTER, 2, -1, span), "i")
     query_source, _ = lax.optimization_barrier((here[:, :rows], kv[-1]))
-    query = in_order(ring_gather(query_source, "i"), "i", 1).reshape(-1, span)
+    query = ring_gather(query_source, "i")
     kv = ring_gather(jnp.stack(kv), "y")
+    query, kv = lax.optimization_barrier((query, kv))
+    query = in_order(query, "i", 1).reshape(-1, span)
     seen = kv[-1][0, 0, 0, 0]
     kv = jnp.stack(ring_gather(jnp.stack(kv), "c"))
     return query, arrange(places, kv), beside, seen
@@ -185,11 +208,11 @@
     return join_blocks(exchange(mine)).astype(F32)
 
 
-def scatter_kv(grad):
+def scatter_kv(kept, sent):
+    mine = lax.ppermute(sent, "c", [(0, 1), (1, 0)]).astype(F32) + kept
     high, inner = lax.axis_size("y"), lax.axis_size("i")
-    wide = grad.shape[1]
-    blocks = grad.reshape(high, 2, OUTER, inner, -1, wide)
-    mine = ring_scatter(from_order([blocks[:, 0], blocks[:, 1]], "c"), "c")
+    wide = kept.shape[-1]
+    mine = mine.reshape(high, OUTER, inner, -1, wide)
     mine = ring_scatter(from_order([mine[k] for k in range(high)], "y"), "y")
     mine = ring_scatter(from_order([mine[:, k] for k in range(inner)], "i"), "i").astype(BF16)
     here = exchange(mine)
@@ -688,7 +711,7 @@
     normed_two, inverse_two = norm_rows(middle, norm_gain2)
     mlp_input = normed_two.astype(BF16)
     mlp_gate, mlp_onehot = pair_gates(mlp_input, mlp_router, mlp_route, experts)
-    up_parts = ring_gather(up_source, "i")
+    up_parts = far_gather(up_source)
     all_mlp = meet(mlp_input)
     gate_m = to_experts(mlp_gate, mlp_onehot, None)
     d_both, gated_units, rows_back, d_gate_m = [], [], None, None
@@ -712,11 +735,13 @@
     d_mlp_gate = from_experts(d_gate_m[:, 0], mlp_onehot, experts)
     grad_up = [mm("tf,td->fd", d_here, all_mlp) for d_here in d_both]
     grad_down = [mm("tf,td->fd", here, all_cot) for here in gated_units]
-    rows_out = layer_rows(places, gated_units, down_parts, tokens)
     low_up = [one.astype(BF16) for one in grad_up[1:]]
     low_down = [one.astype(BF16) for one in grad_down[1:]]
-    d_mlp_input, low_up, low_down, rows_out = tie((d_mlp_input, low_up, low_down, rows_out))
-    grad_up, grad_down = grad_up[:1] + low_up, grad_down[:1] + low_down
+    rows_out = part_low(layer_rows(places, gated_units, down_parts, tokens))
+    half = tokens // 2
+    rows_first, rows_second = rows_out[:, :, :half], rows_out[:, :, half:]
+    rows_first = ring_low([rows_first[k] for k in range(rows_first.shape[0])], "y")
+    d_mlp_input, rows_first, low_up, low_down = tie((d_mlp_input, rows_first, low_up, low_down))
     d_mlp_router, d_mlp_from_router = gates_back(
         mlp_gate, mlp_onehot, d_mlp_gate, mlp_input, mlp_router
     )
@@ -732,21 +757,24 @@
     )
 
     all_mid = meet(d_middle.astype(BF16))
-    rows_out, all_mid = tie((part_first(part_low(rows_out)), all_mid))
-    rows_out = part_second(*rows_out)
+    rows_second = ring_low([rows_second[:, k] for k in range(OUTER)], "o")
+    all_mid, rows_second = tie((all_mid, rows_second))
     d_heads, d_kv, rows_one, d_gate_a, d_gain_a = attend_back(
         places, all_mid, info, cosine, sine_table, qkv, all_attn, query_mat, kv_mat, out_mat
     )
-    layer_out = middle + rows_out.astype(F32) + mlp_bias
+    rows_first, rows_second, d_heads = tie((rows_first, rows_second, d_heads))
+    layer_out = middle + part_second(rows_first, rows_second).astype(F32) + mlp_bias
     d_attn_input = part(rows_one)
     d_att_gate = from_experts(d_gate_a[:, 0], att_onehot, experts)
-    d_kv_weight = scatter_kv(mm("td,tf->df", all_attn, d_kv))
+    d_kv_mat = mm("td,tf->df", all_attn, d_kv).reshape(experts // 2, 2, -1, 2 * span)
+    d_kv_mat = from_order([d_kv_mat[:, 0], d_kv_mat[:, 1]], "c")
+    d_kv_sent, d_heads, all_mid = tie((d_kv_mat[1].astype(BF16), d_heads, all_mid))
+    d_kv_weight = scatter_kv(d_kv_mat[0], d_kv_sent)
     d_query = scatter_query(mm("td,tf->df", all_attn, d_heads))[None]
     d_out = mm("tf,td->fd", gated, all_mid).reshape(inner, -1, width)
     d_output = ring_scatter(from_order([d_out[k] for k in range(inner)], "i"), "i")[None]
-    d_upper = ring_scatter(grad_up, "i", d_attn_input)
-    d_upper = d_upper.reshape(up_weight.shape)
-    d_lower = ring_scatter(grad_down, "i", d_attn_input)[None]
+    d_upper = far_scatter(grad_up[:1] + low_up, d_attn_input).reshape(up_weight.shape)
+    d_lower = far_scatter(grad_down[:1] + low_down, d_attn_input)[None]
     d_att_router, d_att_from_router = gates_back(
         att_gate, att_onehot, d_att_gate, attn_input, att_router
     )

time: 932 us -> 995 us (1.068)
  waiting for transfers between devices: 344 us -> 398 us
    ppermute x0 -> x4, waiting for transfers between devices: none -> 172 us  [the longest x3 172 us: shift_far(): return shift(lax.ppermute(value, ('c', 'i'), pairs), 'c')]
    all_gather x4, waiting for transfers between devices: 73.6 us -> 0.02 us  [meet(): return lax.all_gather(rows, GROUP, axis=0, tiled=True)]
    reduce_scatter x2, waiting for transfers between devices: 50.1 us -> 18.1 us  [part(): return lax.psum_scatter(rows, GROUP, scatter_dimension=0, tiled=True)]
    ppermute x32 -> x31, waiting for transfers between devices: 205 us -> 178 us  [shift(): return lax.ppermute(value, axis, [((k + 1) % size, k) for k in range(size)])]
    ppermute x5, waiting for transfers between devices: 7.34 us -> 22.6 us  [sum_all(): lax.ppermute(value, axis, [(k, k ^ step) for k in range(size)])]
    ppermute x32 -> x31, starting transfers between devices: 55.1 us -> 54.5 us  [shift(): return lax.ppermute(value, axis, [((k + 1) % size, k) for k in range(size)])]
  transfers between devices with their start and end apart: 48 -> 51, of which waited for: 26 -> 23; matrix products, arithmetic and copies ran while one was open for 22% -> 21% of each run, Pallas kernels for 15% -> 14%
where the time goes in v7:
time: 995 us; the launch traced here: 991 us
  waiting for transfers between devices  398 us (40%)
  Pallas kernels  171 us (17%)
  matrix products  117 us (12%)
  other arithmetic  96.8 us (10%)
  starting transfers between devices  81.9 us (8%)
  blocking collectives  71.9 us (7%)
  local copies, waits for them, and re-layouts  38.6 us (4%)
  between operations  15.4 us (2%)
    ppermute x31, waiting for transfers between devices, shift(): return lax.ppermute(value, axis, [((k + 1) % size, k) for k in range(size)])  178 us
    ppermute x3, waiting for transfers between devices, shift_far(): return shift(lax.ppermute(value, ('c', 'i'), pairs), 'c')  172 us
    pallas_call x6, Pallas kernels, call(): pl.pallas_call(kernel, grid_spec=pltpu.PrefetchScalarGridSpec(num_scalar_...  171 us
    dot_general x9, matrix products, mm(): return jnp.einsum(form, first, second, preferred_element_type=F32)  109 us
    all_to_all x1, blocking collectives, exchange(): return lax.all_to_all(blocks, 'o', split_axis=0, concat_axis=0, tiled=True)  58.9 us
    ppermute x31, starting transfers between devices, shift(): return lax.ppermute(value, axis, [((k + 1) % size, k) for k in range(size)])  54.5 us
    ppermute x5, waiting for transfers between devices, sum_all(): lax.ppermute(value, axis, [(k, k ^ step) for k in range(size)])  22.6 us
  transfers between devices with their start and end apart: 51, of which 23 were waited for; matrix products, arithmetic and copies ran while one was open for 21% of the time, Pallas kernels for 14%

profile of v7, /device:TPU:0, one launch (start us, length us, event | category | flops | bytes accessed | tf_op | source)
XLA Modules:
  0.0 990.9 jit_solution(16456262571824537324)
XLA Ops:
  11.3 3.0 collective-permute-start
  15.8 58.9 %all_to_all.37 = bf16[4,384,512]{2,1,0:T(8,128)(2,1)S(1)} all-to-all(bf16[4,384,512]{2,1,0:T(8,128)(2,1)S(1)} %maximum_maximum_fusion), channel_id=1, replica_groups=mesh['y'=2,'c'=2,'o'=4,'i'=2] {'o'}, dimensions={0} | all-to-all | bytes 3145728 | tf_op jit(solution)/shard_map/all_to_all | solution.py:174
  80.4 11.4 %collective-permute-done.1 = bf16[4,2,64,512]{3,2,1,0:T(8,128)(2,1)S(1)} collective-permute-done((bf16[4,2,64,512]{3,2,1,0:T(8,128)(2,1)S(1)}, bf16[4,2,64,512]{3,2,1,0:T(8,128)(2,1)S(1)}, u32[]{:S(2)}, u32[]{:S(2)}) %collective-permute-start.1) | collective-permute-done | bytes 524320 | tf_op jit(solution)/shard_map/ppermute | solution.py:55
  96.4 21.5 %collective-permute-done.3 = bf16[2,4,2,64,512]{4,3,2,1,0:T(8,128)(2,1)S(1)} collective-permute-done((bf16[2,4,2,64,512]{4,3,2,1,0:T(8,128)(2,1)S(1)}, bf16[2,4,2,64,512]{4,3,2,1,0:T(8,128)(2,1)S(1)}, u32[]{:S(2)}, u32[]{:S(2)}) %collective-permute-start.3) | collective-permute-done | bytes 1048608 | tf_op jit(solution)/shard_map/ppermute | solution.py:55
  119.6 3.1 fusion.51
  123.4 4.8 all-to-all-start
  135.3 19.1 %collective-permute-done.5 = bf16[256,2048]{1,0:T(8,128)(2,1)S(1)} collective-permute-done((bf16[256,2048]{1,0:T(8,128)(2,1)}, bf16[256,2048]{1,0:T(8,128)(2,1)S(1)}, u32[]{:S(2)}, u32[]{:S(2)}) %collective-permute-start.5) | collective-permute-done | bytes 1048608 | tf_op jit(solution)/shard_map/ppermute | solution.py:55
  156.0 4.0 pad_maximum_fusion.in_ref
  159.9 7.3 arrange.1
  167.9 33.3 %attend.1 = (bf16[2048,1536]{1,0:T(8,128)(2,1)}, bf16[2048,512]{1,0:T(8,128)(2,1)}, bf16[2,2,4,128,2048]{4,3,2,1,0:T(8,128)(2,1)}) custom-call(s32[4]{0:T(128)} %pad_add_fusion.places_ref, bf16[2048,2048]{1,0:T(8,128)(2,1)} %all-gather.5.cloned.1.call-done.x_ref, f32[16,2,128]{2,1,0:T(2,128)} %copy-done.33, f32[128,128]{1,0:T(8,128)} %get-tuple-element.155.cos_ref, ...), custom_call_target="tpu_custom_call" | custom-call | flops 17716740096 | bytes 25165824 | tf_op jit(solution)/shard_map/attend/pallas_call | solution.py:455
  201.1 2.7 slice_bitcast_fusion.3
  203.9 7.1 collective-permute-done.6
  213.1 3.5 collective-permute-start.11
  218.3 9.8 collective-permute-done.11
  228.3 4.9 collective-permute-start.12
  233.1 11.3 %convolution_convert_fusion.1.d_units_ref = bf16[2048,704]{1,0:T(8,128)(2,1)} fusion(bf16[2048,2048]{1,0:T(8,128)(2,1)} %all-gather.7.cloned.1.call-done, bf16[704,2048]{1,0:T(8,128)(2,1)} %copy-done.52), kind=kOutput, calls=%fused_computation.16 | convolution fusion | flops 5907021824 | bytes 14155776 | tf_op jit(solution)/shard_map/td,fd->tf/dot_general | solution.py:161
  244.6 3.7 collective-permute-start.13
  248.7 8.1 convolution_convert_fusion.2.d_units_ref
  256.8 6.8 collective-permute-done.8
  263.7 4.3 collective-permute-start.9
  272.0 4.3 collective-permute-start.10
  276.4 3.8 collective-permute-done.10
  281.8 126.9 %collective-permute-done.15 = bf16[1408,2048]{1,0:T(8,128)(2,1)} collective-permute-done((bf16[1408,2048]{1,0:T(8,128)(2,1)}, bf16[1408,2048]{1,0:T(8,128)(2,1)}, u32[]{:S(2)}, u32[]{:S(2)}) %collective-permute-start.15) | collective-permute-done | bytes 5767200 | tf_op jit(solution)/shard_map/ppermute | solution.py:63
  410.5 13.0 %all_to_all.38.info_ref = f32[16,1,128]{2,1,0:T(1,128)} all-to-all(f32[16,1,128]{2,1,0:T(1,128)S(1)} %bitcast.349), channel_id=1, replica_groups=mesh['y'=2,'c'=2,'o'=4,'i'=2] {'y','c','o'}, dimensions={0} | all-to-all | bytes 16384 | tf_op jit(solution)/shard_map/all_to_all | solution.py:143
  423.5 35.5 %units.2 = (bf16[2048,1408]{1,0:T(8,128)(2,1)}, bf16[2048,704]{1,0:T(8,128)(2,1)}, f32[2048,2048]{1,0:T(8,128)}, f32[16,1,128]{2,1,0:T(1,128)}) custom-call(s32[4]{0:T(128)} %pad_add_fusion.places_ref, bf16[2048,2048]{1,0:T(8,128)(2,1)} %all-gather.9.cloned.1.call-done.x_ref, f32[16,1,128]{2,1,0:T(1,128)} %all_to_all.38.info_ref, ...), custom_call_target="tpu_custom_call" | custom-call | tf_op jit(solution)/shard_map/units/pallas_call | solution.py:455
  459.0 35.9 %units.3 = (bf16[2048,1408]{1,0:T(8,128)(2,1)}, bf16[2048,704]{1,0:T(8,128)(2,1)}, bf16[2048,2048]{1,0:T(8,128)(2,1)}, f32[16,1,128]{2,1,0:T(1,128)}) custom-call(s32[4]{0:T(128)} %pad_add_fusion.places_ref, bf16[2048,2048]{1,0:T(8,128)(2,1)} %all-gather.9.cloned.1.call-done.x_ref, f32[16,1,128]{2,1,0:T(1,128)} %all_to_all.38.info_ref, ...), custom_call_target="tpu_custom_call" | custom-call | tf_op jit(solution)/shard_map/units/pallas_call | solution.py:455
  494.9 19.6 %layer_rows.1 = bf16[2,2,4,128,2048]{4,3,2,1,0:T(8,128)(2,1)} custom-call(s32[4]{0:T(128)} %pad_add_fusion.places_ref, bf16[2048,704]{1,0:T(8,128)(2,1)} %get-tuple-element.78.refs_0_, bf16[2048,704]{1,0:T(8,128)(2,1)} %get-tuple-element.79.refs_1_, bf16[704,2048]{1,0:T(8,128)(2,1)} %bitcast.365, bf16[704,2048]{1,0:T(8,128)(2,1)} %copy-done.52), custom_call_target="tpu_custom_call" | custom-call | flops 11811160064 | bytes 28311552 | tf_op jit(solution)/shard_map/layer_rows/pallas_call | solution.py:455
  514.5 5.3 fusion.53
  522.8 3.5 all-to-all-start.3
  526.6 18.1 %convolution_convert_fusion = bf16[1408,2048]{1,0:T(8,128)(2,1)} fusion(bf16[2048,1408]{1,0:T(8,128)(2,1)} %get-tuple-element.80, bf16[2048,2048]{1,0:T(8,128)(2,1)} %all-gather.9.cloned.1.call-done.x_ref), kind=kOutput, calls=%fused_computation.5 | convolution fusion | flops 11814043648 | bytes 19922944 | tf_op jit(solution)/shard_map/tf,td->fd/dot_general | solution.py:161
  544.7 4.3 fusion
  553.0 10.3 %convolution_convert_fusion.3 = bf16[704,2048]{1,0:T(8,128)(2,1)} fusion(bf16[2048,704]{1,0:T(8,128)(2,1)S(1)} %copy-done.50, bf16[2048,2048]{1,0:T(8,128)(2,1)} %all-gather.7.cloned.1.call-done), kind=kOutput, calls=%fused_computation.18 | convolution fusion | flops 5907021824 | bytes 14155776 | tf_op jit(solution)/shard_map/tf,td->fd/dot_general | solution.py:161
  563.4 24.5 %collective-permute-done.18 = bf16[4,64,2048]{2,1,0:T(8,128)(2,1)S(1)} collective-permute-done((bf16[4,64,2048]{2,1,0:T(8,128)(2,1)S(1)}, bf16[4,64,2048]{2,1,0:T(8,128)(2,1)S(1)}, u32[]{:S(2)}, u32[]{:S(2)}) %collective-permute-start.18) | collective-permute-done | bytes 1048608 | tf_op jit(solution)/shard_map/ppermute | solution.py:55
  589.6 18.1 %reduce-scatter.3.cloned.1.call-done = bf16[128,2048]{1,0:T(8,128)(2,1)} async-done(((bf16[2048,2048]{1,0:T(8,128)(2,1)}), bf16[128,2048]{1,0:T(8,128)(2,1)}) %reduce-scatter.3.cloned.1.call-update) | async-done | bytes 524304 | tf_op jit(solution)/shard_map/reduce_scatter | solution.py:157
  617.7 22.6 %collective-permute-done.19 = bf16[2,64,2048]{2,1,0:T(8,128)(2,1)} collective-permute-done((bf16[2,64,2048]{2,1,0:T(8,128)(2,1)}, bf16[2,64,2048]{2,1,0:T(8,128)(2,1)}, u32[]{:S(2)}, u32[]{:S(2)}) %collective-permute-start.19) | collective-permute-done | bytes 524320 | tf_op jit(solution)/shard_map/ppermute | solution.py:55
  641.8 19.0 %fusion.64 = f32[1408,2048]{1,0:T(8,128)} fusion(bf16[2048,1408]{1,0:T(8,128)(2,1)} %get-tuple-element.104, bf16[2048,2048]{1,0:T(8,128)(2,1)} %all-gather.9.cloned.1.call-done.x_ref), kind=kOutput, calls=%fused_computation.206 | convolution fusion | flops 11811160064 | bytes 25690112 | tf_op jit(solution)/shard_map/tf,td->fd/dot_general | solution.py:161
  663.3 10.4 %fusion.65 = f32[704,2048]{1,0:T(8,128)} fusion(bf16[2048,704]{1,0:T(8,128)(2,1)S(1)} %copy-done.49, bf16[2048,2048]{1,0:T(8,128)(2,1)} %all-gather.7.cloned.1.call-done), kind=kOutput, calls=%fused_computation.207 | convolution fusion | flops 5905580032 | bytes 17039360 | tf_op jit(solution)/shard_map/tf,td->fd/dot_general | solution.py:161
  674.0 22.8 %collective-permute-done.21 = bf16[2,64,2048]{2,1,0:T(8,128)(2,1)S(1)} collective-permute-done((bf16[2,64,2048]{2,1,0:T(8,128)(2,1)S(1)}, bf16[2,64,2048]{2,1,0:T(8,128)(2,1)S(1)}, u32[]{:S(2)}, u32[]{:S(2)}) %collective-permute-start.21) | collective-permute-done | bytes 524320 | tf_op jit(solution)/shard_map/ppermute | solution.py:55
  698.8 44.9 %collective-permute-done.36 = bf16[1408,2048]{1,0:T(8,128)(2,1)} collective-permute-done((bf16[1408,2048]{1,0:T(8,128)(2,1)}, bf16[1408,2048]{1,0:T(8,128)(2,1)}, u32[]{:S(2)}, u32[]{:S(2)}) %collective-permute-start.36) | collective-permute-done | bytes 5767200 | tf_op jit(solution)/shard_map/ppermute | solution.py:63
  743.9 39.7 %attend_back.1 = (bf16[2048,512]{1,0:T(8,128)(2,1)}, bf16[2048,1024]{1,0:T(8,128)(2,1)}, bf16[2048,2048]{1,0:T(8,128)(2,1)}, f32[16,1,128]{2,1,0:T(1,128)}, f32[1,2048]{1,0:T(1,128)}) custom-call(s32[4]{0:T(128)} %pad_add_fusion.places_ref, bf16[2048,2048]{1,0:T(8,128)(2,1)} %all-gather.11.cloned.1.call-done.mid_ref, f32[16,2,128]{2,1,0:T(2,128)} %copy-done.33, ...), custom_call_target="tpu_custom_call" | custom-call | flops 18522046464 | bytes 46137344 | tf_op jit(solution)/shard_map/attend_back/pallas_call | solution.py:455
  783.7 3.8 all-to-all-start.4
  788.1 3.7 collective-permute-start.22
  791.9 14.0 %fusion.61 = f32[2048,1024]{1,0:T(8,128)S(1)} fusion(bf16[2048,2048]{1,0:T(8,128)(2,1)} %all-gather.5.cloned.1.call-done.x_ref, bf16[2048,1024]{1,0:T(8,128)(2,1)} %get-tuple-element.96), kind=kOutput, calls=%fused_computation.203 | convolution fusion | flops 8589934592 | bytes 20971520 | tf_op jit(solution)/shard_map/td,tf->df/dot_general | solution.py:161
  809.0 12.3 %fusion.62 = f32[2048,512]{1,0:T(8,128)} fusion(bf16[2048,2048]{1,0:T(8,128)(2,1)} %all-gather.5.cloned.1.call-done.x_ref, bf16[2048,512]{1,0:T(8,128)(2,1)S(1)} %copy-done.55), kind=kOutput, calls=%fused_computation.204 | convolution fusion | flops 4294967296 | bytes 14680064 | tf_op jit(solution)/shard_map/td,tf->df/dot_general | solution.py:161
  821.4 6.1 fusion.63
  831.6 4.0 select_convert_fusion.1
  840.0 11.5 %collective-permute-done.28 = f32[12,2048]{1,0:T(8,128)S(1)} collective-permute-done((f32[12,2048]{1,0:T(8,128)S(1)}, f32[12,2048]{1,0:T(8,128)S(1)}, u32[]{:S(2)}, u32[]{:S(2)}) %collective-permute-start.28) | collective-permute-done | bytes 98336 | tf_op jit(solution)/shard_map/ppermute | solution.py:116
  854.2 6.8 collective-permute-done.29
  863.1 2.5 collective-permute-start.23
  865.7 3.4 bitcast_add_fusion
  874.6 11.5 %collective-permute-done.34 = bf16[4,256,512]{2,1,0:T(8,128)(2,1)S(1)} collective-permute-done((bf16[4,256,512]{2,1,0:T(8,128)(2,1)S(1)}, bf16[4,256,512]{2,1,0:T(8,128)(2,1)S(1)}, u32[]{:S(2)}, u32[]{:S(2)}) %collective-permute-start.34) | collective-permute-done | bytes 1048608 | tf_op jit(solution)/shard_map/ppermute | solution.py:55
  889.1 4.3 all-to-all-start.6
  893.4 2.6 slice_select_fusion
  896.0 6.7 collective-permute-done.32
  905.1 2.6 collective-permute-start.24
  910.9 4.3 collective-permute-done.30
  916.8 3.2 collective-permute-done.24
  921.7 3.0 collective-permute-done.33
  925.7 7.4 all-to-all-start.5
  933.1 4.5 add_bitcast_fusion.1
  940.4 7.3 all-to-all-done.5
  960.0 7.4 add_bitcast_fusion
  967.4 13.3 %convert_add_fusion = f32[1408,2048]{1,0:T(8,128)} fusion(f32[1408,2048]{1,0:T(8,128)} %fusion.64, bf16[1408,2048]{1,0:T(8,128)(2,1)} %collective-permute-done.37), kind=kLoop, calls=%fused_computation | loop fusion | flops 5767168 | bytes 28835840 | tf_op jit(solution)/shard_map/add | solution.py:79
  980.7 3.0 fusion.15
  (303 shorter events, 115.5 us)
Async XLA Ops:
  7.2 401.6 %copy-start = (f32[2048,4]{0,1:T(4,128)S(1)}, f32[2048,4]{0,1:T(4,128)}, u32[]{:S(2)}) copy-start(f32[2048,4]{0,1:T(4,128)} %param.23) | copy-start | bytes 98308
  7.2 160.1 %all-gather.5.cloned.1.call-start = ((), (), s32[]{:S(2)}) async-start(), calls=%async_computation.9 | async-start | bytes 8912896 | tf_op jit(solution)/shard_map/all_gather | solution.py:153
  11.2 221.9 %all-gather.7.cloned.1.call-start = ((), (), s32[]{:S(2)}) async-start(), calls=%async_computation.10 | async-start | bytes 8912896 | tf_op jit(solution)/shard_map/all_gather | solution.py:153
  11.3 65.7 %collective-permute-start = (bf16[704,2048]{1,0:T(8,128)(2,1)}, bf16[704,2048]{1,0:T(8,128)(2,1)S(1)}, u32[]{:S(2)}, u32[]{:S(2)}) collective-permute-start(bf16[704,2048]{1,0:T(8,128)(2,1)} %bitcast.364), channel_id=1, source_target_pairs={{1,0},{0,1},{3,2},{2,3},{5,4},{4,5},{7,6},{6,7},{9,8},{8,9},{11,10... | collective-permute-start | bytes 8650760 | tf_op jit(solution)/shard_map/ppermute | solution.py:55
  15.8 79.1 %copy-start.15 = (f32[128,2048]{1,0:T(8,128)S(1)}, f32[128,2048]{1,0:T(8,128)}, u32[]{:S(2)}) copy-start(f32[128,2048]{1,0:T(8,128)} %param.31) | copy-start | bytes 3145732
  74.7 44.2 %copy-start.12 = (bf16[128,2048]{1,0:T(8,128)(2,1)S(1)}, bf16[128,2048]{1,0:T(8,128)(2,1)}, u32[]{:S(2)}) copy-start(bf16[128,2048]{1,0:T(8,128)(2,1)} %fusion.9) | copy-start | bytes 1572868
  74.7 44.2 %copy-start.27 = (f32[2048,4]{0,1:T(4,128)S(1)}, f32[2048,4]{0,1:T(4,128)}, u32[]{:S(2)}) copy-start(f32[2048,4]{0,1:T(4,128)} %param.22) | copy-start | bytes 98308
  74.7 44.8 %copy-start.35 = (s32[128,2]{0,1:T(2,128)S(1)}, s32[128,2]{0,1:T(2,128)}, u32[]{:S(2)}) copy-start(s32[128,2]{0,1:T(2,128)} %param.18) | copy-start | bytes 3076
  74.7 44.9 %copy-start.53 = (s32[1,128]{1,0:T(1,128)S(1)}, s32[1,128]{1,0:T(1,128)}, u32[]{:S(2)}) copy-start(s32[1,128]{1,0:T(1,128)} %param.17) | copy-start | bytes 1540
  78.6 13.2 %collective-permute-start.1 = (bf16[4,2,64,512]{3,2,1,0:T(8,128)(2,1)S(1)}, bf16[4,2,64,512]{3,2,1,0:T(8,128)(2,1)S(1)}, u32[]{:S(2)}, u32[]{:S(2)}) collective-permute-start(bf16[4,2,64,512]{3,2,1,0:T(8,128)(2,1)S(1)} %bitcast.338), channel_id=1, source_target_pairs={{1,0},{0,1},{3,2},{2,3},{5,4},{4,5},{7,6},{6,7},{9,8},{8,9},{11,10... | collective-permute-start | bytes 1572872 | tf_op jit(solution)/shard_map/ppermute | solution.py:55
  91.9 27.7 %copy-start.17 = (bf16[2,4,2,64,512]{4,3,2,1,0:T(8,128)(2,1)}, bf16[2,4,2,64,512]{4,3,2,1,0:T(8,128)(2,1)S(1)}, u32[]{:S(2)}) copy-start(bf16[2,4,2,64,512]{4,3,2,1,0:T(8,128)(2,1)S(1)} %pad_maximum_fusion.4) | copy-start | bytes 3145732
  91.9 26.0 %collective-permute-start.3 = (bf16[2,4,2,64,512]{4,3,2,1,0:T(8,128)(2,1)S(1)}, bf16[2,4,2,64,512]{4,3,2,1,0:T(8,128)(2,1)S(1)}, u32[]{:S(2)}, u32[]{:S(2)}) collective-permute-start(bf16[2,4,2,64,512]{4,3,2,1,0:T(8,128)(2,1)S(1)} %pad_maximum_fusion.4), channel_id=1, source_target_pairs={{16,0},{0,16},{17,1},{1,17},{18,2},{2,18},{19,3},{3,19},{20,4},{4,... | collective-permute-start | bytes 3145736 | tf_op jit(solution)/shard_map/ppermute | solution.py:55
  93.4 24.4 %collective-permute-start.2 = (bf16[4,256,512]{2,1,0:T(8,128)(2,1)S(1)}, bf16[4,256,512]{2,1,0:T(8,128)(2,1)S(1)}, u32[]{:S(2)}, u32[]{:S(2)}) collective-permute-start(bf16[4,256,512]{2,1,0:T(8,128)(2,1)S(1)} %slice.265), channel_id=1, source_target_pairs={{1,0},{0,1},{3,2},{2,3},{5,4},{4,5},{7,6},{6,7},{9,8},{8,9},{11,10... | collective-permute-start | bytes 3145736 | tf_op jit(solution)/shard_map/ppermute | solution.py:55
  122.7 33.2 %collective-permute-start.4 = (bf16[2,2,4,2,64,512]{5,4,3,2,1,0:T(8,128)(2,1)}, bf16[2,2,4,2,64,512]{5,4,3,2,1,0:T(8,128)(2,1)}, u32[]{:S(2)}, u32[]{:S(2)}) collective-permute-start(bf16[2,2,4,2,64,512]{5,4,3,2,1,0:T(8,128)(2,1)} %get-tuple-element.116), channel_id=1, source_target_pairs={{8,0},{0,8},{9,1},{1,9},{10,2},{2,10},{11,3},{3,11},{12,4},{4,12},... | collective-permute-start | bytes 6291464 | tf_op jit(solution)/shard_map/ppermute | solution.py:55
  123.4 43.9 %all-to-all-start = ((f32[16,2,128]{2,1,0:T(2,128)}), f32[16,2,128]{2,1,0:T(2,128)S(1)}, u32[]{:S(2)}, u32[]{:S(2)}) async-start(f32[16,2,128]{2,1,0:T(2,128)} %pad_maximum_fusion.8), calls=%async_computation | async-start | bytes 32768 | tf_op jit(solution)/shard_map/all_to_all | solution.py:143
  128.2 295.3 %all-gather.9.cloned.1.call-start = ((), (), s32[]{:S(2)}) async-start(), calls=%async_computation.11 | async-start | bytes 8912896 | tf_op jit(solution)/shard_map/all_gather | solution.py:153
  128.5 25.8 %collective-permute-start.5 = (bf16[256,2048]{1,0:T(8,128)(2,1)}, bf16[256,2048]{1,0:T(8,128)(2,1)S(1)}, u32[]{:S(2)}, u32[]{:S(2)}) collective-permute-start(bf16[256,2048]{1,0:T(8,128)(2,1)} %bitcast.340), channel_id=1, source_target_pairs={{1,0},{0,1},{3,2},{2,3},{5,4},{4,5},{7,6},{6,7},{9,8},{8,9},{11,10... | collective-permute-start | bytes 3145736 | tf_op jit(solution)/shard_map/ppermute | solution.py:55
  203.8 7.2 collective-permute-start.6
  213.1 15.0 %collective-permute-start.11 = (bf16[2,64,2048]{2,1,0:T(8,128)(2,1)S(1)}, bf16[2,64,2048]{2,1,0:T(8,128)(2,1)S(1)}, u32[]{:S(2)}, u32[]{:S(2)}) collective-permute-start(bf16[2,64,2048]{2,1,0:T(8,128)(2,1)S(1)} %slice_bitcast_fusion.17), channel_id=1, source_target_pairs={{2,0},{4,2},{6,4},{0,6},{3,1},{5,3},{7,5},{1,7},{10,8},{12,10},{14... | collective-permute-start | bytes 1572872 | tf_op jit(solution)/shard_map/ppermute | solution.py:55
  216.7 31.5 %collective-permute-start.7 = (bf16[4,64,2048]{2,1,0:T(8,128)(2,1)S(1)}, bf16[4,64,2048]{2,1,0:T(8,128)(2,1)S(1)}, u32[]{:S(2)}, u32[]{:S(2)}) collective-permute-start(bf16[4,64,2048]{2,1,0:T(8,128)(2,1)S(1)} %slice_bitcast_fusion.9), channel_id=1, source_target_pairs={{16,0},{0,16},{17,1},{1,17},{18,2},{2,18},{19,3},{3,19},{20,4},{4,... | collective-permute-start | bytes 3145736 | tf_op jit(solution)/shard_map/ppermute | solution.py:55
  228.3 16.2 %collective-permute-start.12 = (bf16[2,64,2048]{2,1,0:T(8,128)(2,1)S(1)}, bf16[2,64,2048]{2,1,0:T(8,128)(2,1)S(1)}, u32[]{:S(2)}, u32[]{:S(2)}) collective-permute-start(bf16[2,64,2048]{2,1,0:T(8,128)(2,1)S(1)} %fusion.23), channel_id=1, source_target_pairs={{2,0},{4,2},{6,4},{0,6},{3,1},{5,3},{7,5},{1,7},{10,8},{12,10},{14... | collective-permute-start | bytes 1572872 | tf_op jit(solution)/shard_map/ppermute | solution.py:55
  244.6 23.4 %collective-permute-start.13 = (bf16[2,64,2048]{2,1,0:T(8,128)(2,1)S(1)}, bf16[2,64,2048]{2,1,0:T(8,128)(2,1)S(1)}, u32[]{:S(2)}, u32[]{:S(2)}) collective-permute-start(bf16[2,64,2048]{2,1,0:T(8,128)(2,1)S(1)} %fusion.22), channel_id=1, source_target_pairs={{2,0},{4,2},{6,4},{0,6},{3,1},{5,3},{7,5},{1,7},{10,8},{12,10},{14... | collective-permute-start | bytes 1572872 | tf_op jit(solution)/shard_map/ppermute | solution.py:55
  248.7 14.9 %collective-permute-start.8 = (bf16[64,2048]{1,0:T(8,128)(2,1)S(1)}, bf16[64,2048]{1,0:T(8,128)(2,1)S(1)}, u32[]{:S(2)}, u32[]{:S(2)}) collective-permute-start(bf16[64,2048]{1,0:T(8,128)(2,1)S(1)} %slice_bitcast_fusion.23), channel_id=1, source_target_pairs={{2,0},{4,2},{6,4},{0,6},{3,1},{5,3},{7,5},{1,7},{10,8},{12,10},{14... | collective-permute-start | bytes 786440 | tf_op jit(solution)/shard_map/ppermute | solution.py:55
  256.8 23.5 %copy-start.2 = (bf16[128,2048]{1,0:T(8,128)(2,1)S(1)}, bf16[128,2048]{1,0:T(8,128)(2,1)}, u32[]{:S(2)}) copy-start(bf16[128,2048]{1,0:T(8,128)(2,1)} %param.16) | copy-start | bytes 1572868
  256.8 23.5 %copy-start.25 = (f32[2048]{0:T(1024)S(1)}, f32[2048]{0:T(1024)}, u32[]{:S(2)}) copy-start(f32[2048]{0:T(1024)} %param.27) | copy-start | bytes 24580
  256.8 23.8 %copy-start.31 = (f32[2048]{0:T(1024)S(1)}, f32[2048]{0:T(1024)}, u32[]{:S(2)}) copy-start(f32[2048]{0:T(1024)} %param.21) | copy-start | bytes 24580
  263.7 8.2 collective-permute-start.9
  268.1 142.2 %copy-start.34 = (s32[128,2]{0,1:T(2,128)S(1)}, s32[128,2]{0,1:T(2,128)}, u32[]{:S(2)}) copy-start(s32[128,2]{0,1:T(2,128)} %param.19) | copy-start | bytes 3076
  268.2 8.1 collective-permute-start.14
  272.0 8.2 collective-permute-start.10
  281.7 326.0 %reduce-scatter.3.cloned.1.call-start = ((), (), s32[]{:S(2)}) async-start(), calls=%async_computation.12 | async-start | bytes 8912896 | tf_op jit(solution)/shard_map/reduce_scatter | solution.py:157
  281.7 126.9 %collective-permute-start.15 = (bf16[1408,2048]{1,0:T(8,128)(2,1)}, bf16[1408,2048]{1,0:T(8,128)(2,1)}, u32[]{:S(2)}, u32[]{:S(2)}) collective-permute-start(bf16[1408,2048]{1,0:T(8,128)(2,1)} %bitcast.322), channel_id=1, source_target_pairs={{1,8},{9,0},{0,9},{8,1},{3,10},{11,2},{2,11},{10,3},{5,12},{13,4},... | collective-permute-start | bytes 17301512 | tf_op jit(solution)/shard_map/ppermute | solution.py:63
  408.7 50.3 %collective-permute-start.16 = (bf16[1408,2048]{1,0:T(8,128)(2,1)}, bf16[1408,2048]{1,0:T(8,128)(2,1)}, u32[]{:S(2)}, u32[]{:S(2)}) collective-permute-start(bf16[1408,2048]{1,0:T(8,128)(2,1)} %collective-permute-done.15), channel_id=1, source_target_pairs={{8,0},{0,8},{9,1},{1,9},{10,2},{2,10},{11,3},{3,11},{12,4},{4,12},... | collective-permute-start | bytes 17301512 | tf_op jit(solution)/shard_map/ppermute | solution.py:55
  522.2 22.5 %collective-permute-start.17 = (bf16[2,4,128,2048]{3,2,0,1:T(8,128)(2,1)}, bf16[2,4,128,2048]{3,2,0,1:T(8,128)(2,1)}, u32[]{:S(2)}, u32[]{:S(2)}) collective-permute-start(bf16[2,4,128,2048]{3,2,0,1:T(8,128)(2,1)} %bitcast.321), channel_id=1, source_target_pairs={{8,0},{0,8},{9,1},{1,9},{10,2},{2,10},{11,3},{3,11},{12,4},{4,12},... | collective-permute-start | bytes 12582920 | tf_op jit(solution)/shard_map/ppermute | solution.py:55
  522.8 40.5 %all-to-all-start.3 = ((f32[16,1,128]{2,1,0:T(1,128)}), f32[16,1,128]{2,1,0:T(1,128)S(1)}, u32[]{:S(2)}, u32[]{:S(2)}) async-start(f32[16,1,128]{2,1,0:T(1,128)} %add.172), calls=%async_computation.4 | async-start | bytes 16384 | tf_op jit(solution)/shard_map/all_to_all | solution.py:147
  526.3 217.6 %all-gather.11.cloned.1.call-start = ((), (), s32[]{:S(2)}) async-start(), calls=%async_computation.13 | async-start | bytes 8912896 | tf_op jit(solution)/shard_map/all_gather | solution.py:153
  551.1 36.8 %collective-permute-start.18 = (bf16[4,64,2048]{2,1,0:T(8,128)(2,1)S(1)}, bf16[4,64,2048]{2,1,0:T(8,128)(2,1)S(1)}, u32[]{:S(2)}, u32[]{:S(2)}) collective-permute-start(bf16[4,64,2048]{2,1,0:T(8,128)(2,1)S(1)} %slice_bitcast_fusion.7), channel_id=1, source_target_pairs={{16,0},{0,16},{17,1},{1,17},{18,2},{2,18},{19,3},{3,19},{20,4},{4,... | collective-permute-start | bytes 3145736 | tf_op jit(solution)/shard_map/ppermute | solution.py:55
  589.5 197.9 %copy-start.14 = (bf16[4,64,2048]{2,1,0:T(8,128)(2,1)}, bf16[4,64,2048]{2,1,0:T(8,128)(2,1)S(1)}, u32[]{:S(2)}) copy-start(bf16[4,64,2048]{2,1,0:T(8,128)(2,1)S(1)} %fusion.3) | copy-start | bytes 3145732
  612.8 342.8 %reduce-scatter.5.cloned.1.call-start = ((), (), s32[]{:S(2)}) async-start(), calls=%async_computation.14 | async-start | bytes 8912896 | tf_op jit(solution)/shard_map/reduce_scatter | solution.py:157
  614.7 25.6 %collective-permute-start.19 = (bf16[2,64,2048]{2,1,0:T(8,128)(2,1)}, bf16[2,64,2048]{2,1,0:T(8,128)(2,1)}, u32[]{:S(2)}, u32[]{:S(2)}) collective-permute-start(bf16[2,64,2048]{2,1,0:T(8,128)(2,1)} %slice_bitcast_fusion.13), channel_id=1, source_target_pairs={{2,0},{4,2},{6,4},{0,6},{3,1},{5,3},{7,5},{1,7},{10,8},{12,10},{14... | collective-permute-start | bytes 1572872 | tf_op jit(solution)/shard_map/ppermute | solution.py:55
  616.9 126.8 %collective-permute-start.36 = (bf16[1408,2048]{1,0:T(8,128)(2,1)}, bf16[1408,2048]{1,0:T(8,128)(2,1)}, u32[]{:S(2)}, u32[]{:S(2)}) collective-permute-start(bf16[1408,2048]{1,0:T(8,128)(2,1)} %convolution_convert_fusion), channel_id=1, source_target_pairs={{1,8},{9,0},{0,9},{8,1},{3,10},{11,2},{2,11},{10,3},{5,12},{13,4},... | collective-permute-start | bytes 17301512 | tf_op jit(solution)/shard_map/ppermute | solution.py:63
  641.6 19.2 %collective-permute-start.20 = (bf16[2,64,2048]{2,1,0:T(8,128)(2,1)S(1)}, bf16[2,64,2048]{2,1,0:T(8,128)(2,1)S(1)}, u32[]{:S(2)}, u32[]{:S(2)}) collective-permute-start(bf16[2,64,2048]{2,1,0:T(8,128)(2,1)S(1)} %fusion.20), channel_id=1, source_target_pairs={{2,0},{4,2},{6,4},{0,6},{3,1},{5,3},{7,5},{1,7},{10,8},{12,10},{14... | collective-permute-start | bytes 1572872 | tf_op jit(solution)/shard_map/ppermute | solution.py:55
  662.0 34.8 %collective-permute-start.21 = (bf16[2,64,2048]{2,1,0:T(8,128)(2,1)S(1)}, bf16[2,64,2048]{2,1,0:T(8,128)(2,1)S(1)}, u32[]{:S(2)}, u32[]{:S(2)}) collective-permute-start(bf16[2,64,2048]{2,1,0:T(8,128)(2,1)S(1)} %fusion.19), channel_id=1, source_target_pairs={{2,0},{4,2},{6,4},{0,6},{3,1},{5,3},{7,5},{1,7},{10,8},{12,10},{14... | collective-permute-start | bytes 1572872 | tf_op jit(solution)/shard_map/ppermute | solution.py:55
  698.8 206.2 %collective-permute-start.38 = (bf16[704,2048]{1,0:T(8,128)(2,1)}, bf16[704,2048]{1,0:T(8,128)(2,1)}, u32[]{:S(2)}, u32[]{:S(2)}) collective-permute-start(bf16[704,2048]{1,0:T(8,128)(2,1)} %convolution_convert_fusion.3), channel_id=1, source_target_pairs={{1,8},{9,0},{0,9},{8,1},{3,10},{11,2},{2,11},{10,3},{5,12},{13,4},... | collective-permute-start | bytes 8650760 | tf_op jit(solution)/shard_map/ppermute | solution.py:63
  743.7 216.3 %collective-permute-start.37 = (bf16[1408,2048]{1,0:T(8,128)(2,1)}, bf16[1408,2048]{1,0:T(8,128)(2,1)}, u32[]{:S(2)}, u32[]{:S(2)}) collective-permute-start(bf16[1408,2048]{1,0:T(8,128)(2,1)} %collective-permute-done.36), channel_id=1, source_target_pairs={{8,0},{0,8},{9,1},{1,9},{10,2},{2,10},{11,3},{3,11},{12,4},{4,12},... | collective-permute-start | bytes 17301512 | tf_op jit(solution)/shard_map/ppermute | solution.py:55
  783.7 43.8 %all-to-all-start.4 = ((f32[16,1,128]{2,1,0:T(1,128)}), f32[16,1,128]{2,1,0:T(1,128)S(1)}, u32[]{:S(2)}, u32[]{:S(2)}) async-start(f32[16,1,128]{2,1,0:T(1,128)} %get-tuple-element.93), calls=%async_computation.6 | async-start | bytes 16384 | tf_op jit(solution)/shard_map/all_to_all | solution.py:147
  788.1 64.9 %collective-permute-start.22 = (bf16[64,2048]{1,0:T(8,128)(2,1)}, bf16[64,2048]{1,0:T(8,128)(2,1)}, u32[]{:S(2)}, u32[]{:S(2)}) collective-permute-start(bf16[64,2048]{1,0:T(8,128)(2,1)} %slice_bitcast_fusion.29), channel_id=1, source_target_pairs={{2,0},{4,2},{6,4},{0,6},{3,1},{5,3},{7,5},{1,7},{10,8},{12,10},{14... | collective-permute-start | bytes 786440 | tf_op jit(solution)/shard_map/ppermute | solution.py:55
  807.6 55.6 %collective-permute-start.31 = (bf16[2,512,1024]{2,1,0:T(8,128)(2,1)}, bf16[2,512,1024]{2,1,0:T(8,128)(2,1)}, u32[]{:S(2)}, u32[]{:S(2)}) collective-permute-start(bf16[2,512,1024]{2,1,0:T(8,128)(2,1)} %fusion.2), channel_id=1, source_target_pairs={{0,8},{8,0},{1,9},{9,1},{2,10},{10,2},{3,11},{11,3},{4,12},{12,4},... | collective-permute-start | bytes 6291464 | tf_op jit(solution)/shard_map/ppermute | solution.py:212
  830.2 35.4 %copy-start.5 = (f32[2048,1024]{1,0:T(8,128)S(1)}, f32[2048,1024]{1,0:T(8,128)}, u32[]{:S(2)}) copy-start(f32[2048,1024]{1,0:T(8,128)} %copy-done.4) | copy-start | bytes 25165828
  830.2 5.4 collective-permute-start.26
  835.6 1.8 collective-permute-start.27
  837.4 14.1 %collective-permute-start.28 = (f32[12,2048]{1,0:T(8,128)S(1)}, f32[12,2048]{1,0:T(8,128)S(1)}, u32[]{:S(2)}, u32[]{:S(2)}) collective-permute-start(f32[12,2048]{1,0:T(8,128)S(1)} %add.187), channel_id=1, source_target_pairs={{0,2},{2,0},{4,6},{6,4},{1,3},{3,1},{5,7},{7,5},{8,10},{10,8},{12,... | collective-permute-start | bytes 294920 | tf_op jit(solution)/shard_map/ppermute | solution.py:116
  851.5 56.2 %collective-permute-start.25 = (bf16[64,2048]{1,0:T(8,128)(2,1)}, bf16[64,2048]{1,0:T(8,128)(2,1)S(1)}, u32[]{:S(2)}, u32[]{:S(2)}) collective-permute-start(bf16[64,2048]{1,0:T(8,128)(2,1)} %slice_bitcast_fusion.28), channel_id=1, source_target_pairs={{16,0},{0,16},{17,1},{1,17},{18,2},{2,18},{19,3},{3,19},{20,4},{4,... | collective-permute-start | bytes 786440 | tf_op jit(solution)/shard_map/ppermute | solution.py:55
  853.0 8.0 collective-permute-start.29
  861.0 25.1 %collective-permute-start.34 = (bf16[4,256,512]{2,1,0:T(8,128)(2,1)S(1)}, bf16[4,256,512]{2,1,0:T(8,128)(2,1)S(1)}, u32[]{:S(2)}, u32[]{:S(2)}) collective-permute-start(bf16[4,256,512]{2,1,0:T(8,128)(2,1)S(1)} %fusion.6), channel_id=1, source_target_pairs={{1,0},{0,1},{3,2},{2,3},{5,4},{4,5},{7,6},{6,7},{9,8},{8,9},{11,10... | collective-permute-start | bytes 3145736 | tf_op jit(solution)/shard_map/ppermute | solution.py:55
  863.1 9.1 collective-permute-start.23
  872.3 30.5 %collective-permute-start.32 = (bf16[4,2,64,1024]{3,2,1,0:T(8,128)(2,1)}, bf16[4,2,64,1024]{3,2,1,0:T(8,128)(2,1)}, u32[]{:S(2)}, u32[]{:S(2)}) collective-permute-start(bf16[4,2,64,1024]{3,2,1,0:T(8,128)(2,1)} %bitcast.85), channel_id=1, source_target_pairs={{16,0},{0,16},{17,1},{1,17},{18,2},{2,18},{19,3},{3,19},{20,4},{4,... | collective-permute-start | bytes 3145736 | tf_op jit(solution)/shard_map/ppermute | solution.py:55
  886.1 47.0 %collective-permute-start.35 = (bf16[256,2048]{1,0:T(8,128)(2,1)}, bf16[256,2048]{1,0:T(8,128)(2,1)}, u32[]{:S(2)}, u32[]{:S(2)}) collective-permute-start(bf16[256,2048]{1,0:T(8,128)(2,1)} %select_convert_fusion.1), channel_id=1, source_target_pairs={{1,0},{0,1},{3,2},{2,3},{5,4},{4,5},{7,6},{6,7},{9,8},{8,9},{11,10... | collective-permute-start | bytes 3145736 | tf_op jit(solution)/shard_map/ppermute | solution.py:55
  889.1 36.6 %all-to-all-start.6 = ((bf16[4,256,512]{2,1,0:T(8,128)(2,1)}), bf16[4,256,512]{2,1,0:T(8,128)(2,1)}, u32[]{:S(2)}, u32[]{:S(2)}) async-start(bf16[4,256,512]{2,1,0:T(8,128)(2,1)} %fusion.5), calls=%async_computation.8 | async-start | bytes 2097152 | tf_op jit(solution)/shard_map/all_to_all | solution.py:174
  902.7 12.5 %collective-permute-start.30 = (f32[12,2048]{1,0:T(8,128)}, f32[12,2048]{1,0:T(8,128)S(1)}, u32[]{:S(2)}, u32[]{:S(2)}) collective-permute-start(f32[12,2048]{1,0:T(8,128)} %add.189), channel_id=1, source_target_pairs={{0,1},{1,0},{2,3},{3,2},{4,5},{5,4},{6,7},{7,6},{8,9},{9,8},{10,11... | collective-permute-start | bytes 294920 | tf_op jit(solution)/shard_map/ppermute | solution.py:116
  905.1 14.8 %collective-permute-start.24 = (bf16[64,2048]{1,0:T(8,128)(2,1)S(1)}, bf16[64,2048]{1,0:T(8,128)(2,1)S(1)}, u32[]{:S(2)}, u32[]{:S(2)}) collective-permute-start(bf16[64,2048]{1,0:T(8,128)(2,1)S(1)} %copy-done.24), channel_id=1, source_target_pairs={{2,0},{4,2},{6,4},{0,6},{3,1},{5,3},{7,5},{1,7},{10,8},{12,10},{14... | collective-permute-start | bytes 786440 | tf_op jit(solution)/shard_map/ppermute | solution.py:55
  908.4 16.3 %collective-permute-start.33 = (bf16[4,64,1024]{2,1,0:T(8,128)(2,1)S(1)}, bf16[4,64,1024]{2,1,0:T(8,128)(2,1)S(1)}, u32[]{:S(2)}, u32[]{:S(2)}) collective-permute-start(bf16[4,64,1024]{2,1,0:T(8,128)(2,1)S(1)} %fusion.25), channel_id=1, source_target_pairs={{1,0},{0,1},{3,2},{2,3},{5,4},{4,5},{7,6},{6,7},{9,8},{8,9},{11,10... | collective-permute-start | bytes 1572872 | tf_op jit(solution)/shard_map/ppermute | solution.py:55
  915.2 40.4 %collective-permute-start.39 = (bf16[704,2048]{1,0:T(8,128)(2,1)}, bf16[704,2048]{1,0:T(8,128)(2,1)}, u32[]{:S(2)}, u32[]{:S(2)}) collective-permute-start(bf16[704,2048]{1,0:T(8,128)(2,1)} %collective-permute-done.38), channel_id=1, source_target_pairs={{8,0},{0,8},{9,1},{1,9},{10,2},{2,10},{11,3},{3,11},{12,4},{4,12},... | collective-permute-start | bytes 8650760 | tf_op jit(solution)/shard_map/ppermute | solution.py:55
  925.7 22.0 %all-to-all-start.5 = ((bf16[4,64,1024]{2,1,0:T(8,128)(2,1)}), bf16[4,64,1024]{2,1,0:T(8,128)(2,1)}, u32[]{:S(2)}, u32[]{:S(2)}) async-start(bf16[4,64,1024]{2,1,0:T(8,128)(2,1)} %fusion.24), calls=%async_computation.7 | async-start | bytes 1048576 | tf_op jit(solution)/shard_map/all_to_all | solution.py:174
  (45 other events, 418.5 us)
Sparse Core Ops, SparseCore 0:
  11.3 101.6 all-gather.4
  119.0 75.1 all-gather.6
  281.8 76.7 all-gather.8
  495.0 112.6 reduce-scatter.2
  612.9 95.4 all-gather.10
  783.8 125.2 reduce-scatter.4

commit v8 on v7

--- a/solution.py
+++ b/solution.py
@@ -55,28 +55,9 @@
     return lax.ppermute(value, axis, [((k + 1) % size, k) for k in range(size)])
 
 
-def shift_far(value):
-    size = lax.axis_size("i")
-    pairs = [
-        (low * size + (k + 1) % size, (1 - low) * size + k) for k in range(size) for low in range(2)
-    ]
-    return shift(lax.ppermute(value, ("c", "i"), pairs), "c")
-
-
-def far_gather(value):
-    parts = [value]
-    for _ in range(lax.axis_size("i") - 1):
-        parts.append(shift_far(parts[-1]))
-    return parts
-
-
-def far_scatter(blocks, after):
-    size = lax.axis_size("i")
-    travelling = blocks[1].astype(BF16)
-    for j in range(2, size):
-        travelling = (shift_far(travelling).astype(F32) + blocks[j]).astype(BF16)
-    arrived, _ = lax.optimization_barrier((shift_far(travelling), after))
-    return arrived.astype(F32) + blocks[0]
+def after(value, *others):
+    token, _ = lax.optimization_barrier((lax.create_token(), others))
+    return lax.optimization_barrier((token, value))[1]
 
 
 def ring_gather(value, axis):
@@ -86,12 +67,19 @@
     return parts
 
 
-def ring_scatter(blocks, axis):
+def ring_open(blocks, axis):
     size = lax.axis_size(axis)
     travelling = blocks[1].astype(BF16)
     for j in range(2, size):
         travelling = (shift(travelling, axis).astype(F32) + blocks[j]).astype(BF16)
-    return shift(travelling, axis).astype(F32) + blocks[0]
+    return blocks[0], shift(travelling, axis)
+
+
+def ring_scatter(blocks, axis, *others):
+    own, arrived = ring_open(blocks, axis)
+    if others:
+        arrived = after(arrived, *others)
+    return arrived.astype(F32) + own
 
 
 def in_order(parts, axis, place=0):
@@ -187,17 +175,16 @@
             axis=1,
         )
     )
-    here, beside = lax.optimization_barrier((here, beside()))
+    here = after(here, *beside)
     span = here.shape[2]
     kv = ring_gather(here[:, rows:].reshape(OUTER, 2, -1, span), "i")
-    query_source, _ = lax.optimization_barrier((here[:, :rows], kv[-1]))
-    query = ring_gather(query_source, "i")
+    query = ring_gather(after(here[:, :rows], kv[-1]), "i")
     kv = ring_gather(jnp.stack(kv), "y")
-    query, kv = lax.optimization_barrier((query, kv))
+    kv = after(kv, query)
     query = in_order(query, "i", 1).reshape(-1, span)
     seen = kv[-1][0, 0, 0, 0]
     kv = jnp.stack(ring_gather(jnp.stack(kv), "c"))
-    return query, arrange(places, kv), beside, seen
+    return query, arrange(places, kv), seen
 
 
 def scatter_query(grad):
@@ -331,13 +318,12 @@
     sin_ref,
     query_ref,
     kv_ref,
-    out_ref,
     qkv_ref,
     gated_ref,
-    part_ref,
 ):
+    del places_ref
     length = cos_ref.shape[0]
-    span = out_ref.shape[0]
+    span = query_ref.shape[1]
     raw_query = nn(x_ref[...], query_ref[...])
     raw = nn(x_ref[...], kv_ref[...])
     cosine, sine = cos_ref[...], sin_ref[...]
@@ -359,7 +345,6 @@
         gated = (heads_nn(probs.astype(BF16), jnp.stack(values)) * gate[None]).astype(BF16)
         for number, at in enumerate(starts):
             gated_ref[rows, at : at + HD] = gated[number]
-    place_rows(places_ref, part_ref, nn(gated_ref[...], out_ref[...]).astype(BF16), length)
 
 
 def attend_back_kernel(
@@ -418,7 +403,7 @@
     part_ref[...] = d_input.astype(BF16)
 
 
-def layer_rows_kernel(parts, places_ref, *refs):
+def rows_kernel(parts, places_ref, *refs):
     gated_refs, down_refs, part_ref = refs[:parts], refs[parts : 2 * parts], refs[2 * parts]
     length = part_ref.shape[3]
     value = nn(gated_refs[0][...], down_refs[0][...])
@@ -506,12 +491,11 @@
     return found.reshape(-1, kinds * span)
 
 
-def attend(places, rows, info, cosine, sine, query_mat, kv_mat, out_mat):
+def attend(places, rows, info, cosine, sine, query_mat, kv_mat):
     count, width = rows.shape
-    span = out_mat.shape[0]
+    span = query_mat.shape[1]
     length = cosine.shape[0]
     step = OUTER * length
-    high = count // (2 * step)
     return call(
         attend_kernel,
         "attend",
@@ -523,13 +507,12 @@
             fixed(sine.shape),
             fixed(query_mat.shape),
             fixed(kv_mat.shape),
-            fixed(out_mat.shape),
         ],
-        [rows_spec(step, 3 * span), rows_spec(step, span), place_spec(high, length, width)],
-        [shape((count, 3 * span)), shape((count, span)), shape((2, high, OUTER, length, width))],
-        2 * count * width * 4 * span + 4 * count * length * span,
+        [rows_spec(step, 3 * span), rows_spec(step, span)],
+        [shape((count, 3 * span)), shape((count, span))],
+        2 * count * width * 3 * span + 4 * count * length * span,
         4 * count * (width + 2 * span),
-        (places, rows, info, cosine, sine, query_mat, kv_mat, out_mat),
+        (places, rows, info, cosine, sine, query_mat, kv_mat),
     )
 
 
@@ -573,15 +556,15 @@
     )
 
 
-def layer_rows(places, gated_units, down_parts, length):
+def ring_rows(places, gated_units, down_parts, length):
     count, units = gated_units[0].shape
     width = down_parts[0].shape[1]
     parts = len(down_parts)
     step = OUTER * length
     high = count // (2 * step)
     return call(
-        functools.partial(layer_rows_kernel, parts),
-        "layer_rows",
+        functools.partial(rows_kernel, parts),
+        "rows",
         count // step,
         [rows_spec(step, units)] * parts + [fixed(down.shape) for down in down_parts],
         place_spec(high, length, width),
@@ -682,13 +665,12 @@
     cosine, sine_table = rope_tables(tokens)
 
     places = own_places()
-    tie = lax.optimization_barrier
-
-    query_mat, kv_mat, down_parts, seen = gather_heads(
-        places, query_weight[0], kv_weight, lambda: ring_gather(down_weight[0], "i")
-    )
-    out_source, _ = tie((out_weight[0], seen))
-    out_mat = in_order(ring_gather(out_source, "i"), "i").reshape(span, width)
+
+    down_parts = ring_gather(down_weight[0], "i")
+    query_mat, kv_mat, seen = gather_heads(
+        places, query_weight[0], kv_weight, down_parts[1:]
+    )
+    out_mat = in_order(ring_gather(after(out_weight[0], seen), "i"), "i").reshape(span, width)
     own_up = up_weight[0].reshape(-1, width)
 
     residual = hidden_in.astype(F32)
@@ -697,21 +679,18 @@
     att_gate, att_onehot = pair_gates(attn_input, att_router, att_route, experts)
     info = to_experts(att_gate, att_onehot, segment_ids[0].astype(F32))
     all_attn = meet(attn_input)
-    cot_low, _ = tie((cotangent.astype(BF16), seen))
-    all_cot = meet(cot_low)
-    qkv, gated, branch = attend(
-        places, all_attn, info, cosine, sine_table, query_mat, kv_mat, out_mat
-    )
-    up_source, branch = tie((own_up, branch))
-    branch = part_second(*part_first(part_low(branch)))
+    all_cot = meet(after(cotangent.astype(BF16), seen))
+    qkv, gated = attend(places, all_attn, info, cosine, sine_table, query_mat, kv_mat)
+    branch = part_low(ring_rows(places, [gated], [out_mat], tokens))
+    branch = part_second(*part_first(branch))
 
     d_units = [mm("td,fd->tf", all_cot, down).astype(BF16) for down in down_parts]
-    branch, d_units = tie((branch, d_units))
+    branch = after(branch, d_units)
     middle = residual + branch.astype(F32) + att_bias
     normed_two, inverse_two = norm_rows(middle, norm_gain2)
     mlp_input = normed_two.astype(BF16)
     mlp_gate, mlp_onehot = pair_gates(mlp_input, mlp_router, mlp_route, experts)
-    up_parts = far_gather(up_source)
+    up_parts = ring_gather(after(own_up, branch), "i")
     all_mlp = meet(mlp_input)
     gate_m = to_experts(mlp_gate, mlp_onehot, None)
     d_both, gated_units, rows_back, d_gate_m = [], [], None, None
@@ -737,11 +716,12 @@
     grad_down = [mm("tf,td->fd", here, all_cot) for here in gated_units]
     low_up = [one.astype(BF16) for one in grad_up[1:]]
     low_down = [one.astype(BF16) for one in grad_down[1:]]
-    rows_out = part_low(layer_rows(places, gated_units, down_parts, tokens))
+    rows_out = part_low(ring_rows(places, gated_units, down_parts, tokens))
     half = tokens // 2
     rows_first, rows_second = rows_out[:, :, :half], rows_out[:, :, half:]
     rows_first = ring_low([rows_first[k] for k in range(rows_first.shape[0])], "y")
-    d_mlp_input, rows_first, low_up, low_down = tie((d_mlp_input, rows_first, low_up, low_down))
+    d_lower, last = ring_open(grad_down[:1] + low_down, "i")
+    d_mlp_input = after(d_mlp_input, rows_first, low_up, last)
     d_mlp_router, d_mlp_from_router = gates_back(
         mlp_gate, mlp_onehot, d_mlp_gate, mlp_input, mlp_router
     )
@@ -758,23 +738,24 @@
 
     all_mid = meet(d_middle.astype(BF16))
     rows_second = ring_low([rows_second[:, k] for k in range(OUTER)], "o")
-    all_mid, rows_second = tie((all_mid, rows_second))
+    all_mid = after(all_mid, rows_second)
     d_heads, d_kv, rows_one, d_gate_a, d_gain_a = attend_back(
         places, all_mid, info, cosine, sine_table, qkv, all_attn, query_mat, kv_mat, out_mat
     )
-    rows_first, rows_second, d_heads = tie((rows_first, rows_second, d_heads))
-    layer_out = middle + part_second(rows_first, rows_second).astype(F32) + mlp_bias
+    rows_out = part_second(after(rows_first, d_heads), after(rows_second, d_heads))
+    layer_out = middle + rows_out.astype(F32) + mlp_bias
     d_attn_input = part(rows_one)
     d_att_gate = from_experts(d_gate_a[:, 0], att_onehot, experts)
     d_kv_mat = mm("td,tf->df", all_attn, d_kv).reshape(experts // 2, 2, -1, 2 * span)
     d_kv_mat = from_order([d_kv_mat[:, 0], d_kv_mat[:, 1]], "c")
-    d_kv_sent, d_heads, all_mid = tie((d_kv_mat[1].astype(BF16), d_heads, all_mid))
+    d_kv_sent = d_kv_mat[1].astype(BF16)
+    d_heads, all_mid = after((d_heads, all_mid), d_kv_sent)
     d_kv_weight = scatter_kv(d_kv_mat[0], d_kv_sent)
     d_query = scatter_query(mm("td,tf->df", all_attn, d_heads))[None]
     d_out = mm("tf,td->fd", gated, all_mid).reshape(inner, -1, width)
     d_output = ring_scatter(from_order([d_out[k] for k in range(inner)], "i"), "i")[None]
-    d_upper = far_scatter(grad_up[:1] + low_up, d_attn_input).reshape(up_weight.shape)
-    d_lower = far_scatter(grad_down[:1] + low_down, d_attn_input)[None]
+    d_upper = ring_scatter(grad_up[:1] + low_up, "i", d_attn_input).reshape(up_weight.shape)
+    d_lower = (after(last, d_attn_input).astype(F32) + d_lower)[None]
     d_att_router, d_att_from_router = gates_back(
         att_gate, att_onehot, d_att_gate, attn_input, att_router
     )
@@ -782,7 +763,7 @@
         d_att_from_router * residual * inverse_one, axis=0, keepdims=True
     )
     summed = sum_all(jnp.concatenate([d_gain_one, sums, d_att_router]))
-    d_attn_input, summed = tie((d_attn_input, summed))
+    d_attn_input = after(d_attn_input, summed)
     d_norm_one, _ = norm_back(
         residual, inverse_one, norm_gain1, d_attn_input.astype(F32) + d_att_from_router
     )

time: 995 us -> 936 us (0.941)
  blocking collectives: 71.9 us -> 13.1 us
    ppermute x3 -> x0, waiting for transfers between devices: 172 us -> none  [shift_far(): return shift(lax.ppermute(value, ('c', 'i'), pairs), 'c')]
    ppermute x31, waiting for transfers between devices: 178 us -> 250 us  [shift(): return lax.ppermute(value, axis, [((k + 1) % size, k) for k in range(size)])]
    all_gather x4, waiting for transfers between devices: 0.02 us -> 70.1 us  [meet(): return lax.all_gather(rows, GROUP, axis=0, tiled=True)]
    all_to_all x1 -> x0, blocking collectives: 58.9 us -> none  [exchange(): return lax.all_to_all(blocks, 'o', split_axis=0, concat_axis=0, tiled=True)]
    ppermute x5, waiting for transfers between devices: 22.6 us -> 59 us  [sum_all(): lax.ppermute(value, axis, [(k, k ^ step) for k in range(size)])]
    reduce_scatter x2, waiting for transfers between devices: 18.1 us -> 6.73 us  [part(): return lax.psum_scatter(rows, GROUP, scatter_dimension=0, tiled=True)]
    pallas_call x6 -> x7, Pallas kernels: 171 us -> 172 us  [call(): pl.pallas_call(kernel, grid_spec=pltpu.PrefetchScalarGridSpec(num_scalar_...]
  transfers between devices with their start and end apart: 51 -> 49, of which waited for: 23 -> 25; matrix products, arithmetic and copies ran while one was open for 21% -> 22% of each run, Pallas kernels for 14% -> 15%
where the time goes in v8:
time: 936 us; the launch traced here: 931 us
  waiting for transfers between devices  391 us (42%)
  Pallas kernels  172 us (18%)
  matrix products  116 us (12%)
  other arithmetic  93.1 us (10%)
  starting transfers between devices  90.3 us (10%)
  local copies, waits for them, and re-layouts  40.3 us (4%)
  between operations  15.4 us (2%)
  blocking collectives  13.1 us (1%)
    ppermute x31, waiting for transfers between devices, shift(): return lax.ppermute(value, axis, [((k + 1) % size, k) for k in range(size)])  250 us
    pallas_call x7, Pallas kernels, call(): pl.pallas_call(kernel, grid_spec=pltpu.PrefetchScalarGridSpec(num_scalar_...  172 us
    dot_general x9, matrix products, mm(): return jnp.einsum(form, first, second, preferred_element_type=F32)  110 us
    all_gather x4, waiting for transfers between devices, meet(): return lax.all_gather(rows, GROUP, axis=0, tiled=True)  70.1 us
    ppermute x5, waiting for transfers between devices, sum_all(): lax.ppermute(value, axis, [(k, k ^ step) for k in range(size)])  59 us
    ppermute x31, starting transfers between devices, shift(): return lax.ppermute(value, axis, [((k + 1) % size, k) for k in range(size)])  56.3 us
  transfers between devices with their start and end apart: 49, of which 25 were waited for; matrix products, arithmetic and copies ran while one was open for 22% of the time, Pallas kernels for 15%

profile of v8, /device:TPU:0, one launch (start us, length us, event | category | flops | bytes accessed | tf_op | source)
XLA Modules:
  0.0 931.1 jit_solution(15149650466559229349)
XLA Ops:
  17.3 4.9 all-to-all-start
  22.2 55.3 %collective-permute-done.refs_3_ = bf16[704,2048]{1,0:T(8,128)(2,1)} collective-permute-done((bf16[704,2048]{1,0:T(8,128)(2,1)}, bf16[704,2048]{1,0:T(8,128)(2,1)}, u32[]{:S(2)}, u32[]{:S(2)}) %collective-permute-start) | collective-permute-done | bytes 2883616 | tf_op jit(solution)/shard_map/ppermute | solution.py:55
  79.5 11.3 %collective-permute-done.1 = bf16[4,2,64,512]{3,2,1,0:T(8,128)(2,1)S(1)} collective-permute-done((bf16[4,2,64,512]{3,2,1,0:T(8,128)(2,1)S(1)}, bf16[4,2,64,512]{3,2,1,0:T(8,128)(2,1)S(1)}, u32[]{:S(2)}, u32[]{:S(2)}) %collective-permute-start.1) | collective-permute-done | bytes 524320 | tf_op jit(solution)/shard_map/ppermute | solution.py:55
  93.9 3.0 fusion.57
  96.9 17.4 %collective-permute-done.2 = bf16[4,256,512]{2,1,0:T(8,128)(2,1)S(1)} collective-permute-done((bf16[4,256,512]{2,1,0:T(8,128)(2,1)S(1)}, bf16[4,256,512]{2,1,0:T(8,128)(2,1)S(1)}, u32[]{:S(2)}, u32[]{:S(2)}) %collective-permute-start.2) | collective-permute-done | bytes 1048608 | tf_op jit(solution)/shard_map/ppermute | solution.py:55
  114.3 6.3 collective-permute-done.3
  121.9 3.1 fusion.52
  125.7 4.8 all-to-all-start.1
  137.2 19.5 %collective-permute-done.5 = bf16[256,2048]{1,0:T(8,128)(2,1)S(1)} collective-permute-done((bf16[256,2048]{1,0:T(8,128)(2,1)}, bf16[256,2048]{1,0:T(8,128)(2,1)S(1)}, u32[]{:S(2)}, u32[]{:S(2)}) %collective-permute-start.5) | collective-permute-done | bytes 1048608 | tf_op jit(solution)/shard_map/ppermute | solution.py:55
  158.3 4.0 pad_maximum_fusion.in_ref
  162.3 7.3 arrange.1
  170.2 25.4 %attend.1 = (bf16[2048,1536]{1,0:T(8,128)(2,1)}, bf16[2048,512]{1,0:T(8,128)(2,1)}) custom-call(s32[4]{0:T(128)} %pad_add_fusion.places_ref, bf16[2048,2048]{1,0:T(8,128)(2,1)} %all-gather.7.cloned.1.call-done.x_ref, f32[16,2,128]{2,1,0:T(2,128)} %copy-done.33, f32[128,128]{1,0:T(8,128)} %get-tuple-element.157.cos_ref, ...), custom_call_target="tpu_custom_call" | custom-call | flops 13421772800 | bytes 25165824 | tf_op jit(solution)/shard_map/attend/pallas_call | solution.py:440
  195.6 9.2 rows.2
  204.8 3.8 fusion.55
  209.3 7.1 collective-permute-done.6
  218.8 3.5 collective-permute-start.11
  224.0 9.8 %collective-permute-done.11 = bf16[2,64,2048]{2,1,0:T(8,128)(2,1)S(1)} collective-permute-done((bf16[2,64,2048]{2,1,0:T(8,128)(2,1)S(1)}, bf16[2,64,2048]{2,1,0:T(8,128)(2,1)S(1)}, u32[]{:S(2)}, u32[]{:S(2)}) %collective-permute-start.11) | collective-permute-done | bytes 524320 | tf_op jit(solution)/shard_map/ppermute | solution.py:55
  233.9 4.9 collective-permute-start.12
  238.8 11.3 %convolution_convert_fusion.1.d_units_ref = bf16[2048,704]{1,0:T(8,128)(2,1)} fusion(bf16[2048,2048]{1,0:T(8,128)(2,1)} %all-gather.5.cloned.1.call-done, bf16[704,2048]{1,0:T(8,128)(2,1)} %collective-permute-done.refs_3_), kind=kOutput, calls=%fused_computation.16 | convolution fusion | flops 5907021824 | bytes 14155776 | tf_op jit(solution)/shard_map/td,fd->tf/dot_general | solution.py:149
  250.2 3.7 collective-permute-start.13
  254.4 8.1 convolution_convert_fusion.2.d_units_ref
  262.5 6.8 collective-permute-done.8
  269.3 4.3 collective-permute-start.9
  277.6 4.3 collective-permute-start.10
  282.0 3.8 collective-permute-done.10
  290.6 13.1 %all_to_all.37.info_ref = f32[16,1,128]{2,1,0:T(1,128)} all-to-all(f32[16,1,128]{2,1,0:T(1,128)S(1)} %bitcast.352), channel_id=1, replica_groups=mesh['y'=2,'c'=2,'o'=4,'i'=2] {'y','c','o'}, dimensions={0} | all-to-all | bytes 16384 | tf_op jit(solution)/shard_map/all_to_all | solution.py:131
  303.7 60.6 %all-gather.9.cloned.1.call-done.x_ref = bf16[2048,2048]{1,0:T(8,128)(2,1)} async-done(((bf16[128,2048]{1,0:T(8,128)(2,1)}), bf16[2048,2048]{1,0:T(8,128)(2,1)}) %all-gather.9.cloned.1.call-update) | async-done | bytes 8388624 | tf_op jit(solution)/shard_map/all_gather | solution.py:141
  364.4 35.5 %units.2 = (bf16[2048,1408]{1,0:T(8,128)(2,1)}, bf16[2048,704]{1,0:T(8,128)(2,1)}, f32[2048,2048]{1,0:T(8,128)}, f32[16,1,128]{2,1,0:T(1,128)}) custom-call(s32[4]{0:T(128)} %pad_add_fusion.places_ref, bf16[2048,2048]{1,0:T(8,128)(2,1)} %all-gather.9.cloned.1.call-done.x_ref, f32[16,1,128]{2,1,0:T(1,128)} %all_to_all.37.info_ref, ...), custom_call_target="tpu_custom_call" | custom-call | tf_op jit(solution)/shard_map/units/pallas_call | solution.py:440
  399.9 9.6 %collective-permute-done.15.first_ref.second_ref = bf16[1408,2048]{1,0:T(8,128)(2,1)} collective-permute-done((bf16[1408,2048]{1,0:T(8,128)(2,1)}, bf16[1408,2048]{1,0:T(8,128)(2,1)}, u32[]{:S(2)}, u32[]{:S(2)}) %collective-permute-start.15) | collective-permute-done | bytes 5767200 | tf_op jit(solution)/shard_map/ppermute | solution.py:55
  409.5 35.9 %units.3 = (bf16[2048,1408]{1,0:T(8,128)(2,1)}, bf16[2048,704]{1,0:T(8,128)(2,1)}, bf16[2048,2048]{1,0:T(8,128)(2,1)}, f32[16,1,128]{2,1,0:T(1,128)}) custom-call(s32[4]{0:T(128)} %pad_add_fusion.places_ref, bf16[2048,2048]{1,0:T(8,128)(2,1)} %all-gather.9.cloned.1.call-done.x_ref, f32[16,1,128]{2,1,0:T(1,128)} %all_to_all.37.info_ref, ...), custom_call_target="tpu_custom_call" | custom-call | tf_op jit(solution)/shard_map/units/pallas_call | solution.py:440
  445.4 19.2 %rows.3 = bf16[2,2,4,128,2048]{4,3,2,1,0:T(8,128)(2,1)} custom-call(s32[4]{0:T(128)} %pad_add_fusion.places_ref, bf16[2048,704]{1,0:T(8,128)(2,1)} %get-tuple-element.74.refs_0_, bf16[2048,704]{1,0:T(8,128)(2,1)} %get-tuple-element.78.refs_1_, bf16[704,2048]{1,0:T(8,128)(2,1)} %bitcast.366, bf16[704,2048]{1,0:T(8,128)(2,1)} %collective-permute-done.refs_3_), custom_call_target="tpu_custom_call" | custom-call | flops 11811160064 | bytes 28311552 | tf_op jit(solution)/shard_map/rows/pallas_call | solution.py:440
  464.5 6.4 fusion.54
  473.8 6.4 all-to-all-start.3
  480.5 10.8 %convolution_convert_fusion.3 = bf16[704,2048]{1,0:T(8,128)(2,1)} fusion(bf16[2048,704]{1,0:T(8,128)(2,1)} %get-tuple-element.78.refs_1_, bf16[2048,2048]{1,0:T(8,128)(2,1)} %all-gather.5.cloned.1.call-done), kind=kOutput, calls=%fused_computation.18 | convolution fusion | flops 5907021824 | bytes 14155776 | tf_op jit(solution)/shard_map/tf,td->fd/dot_general | solution.py:149
  492.8 4.1 fusion
  501.1 18.5 %convolution_convert_fusion = bf16[1408,2048]{1,0:T(8,128)(2,1)} fusion(bf16[2048,1408]{1,0:T(8,128)(2,1)} %get-tuple-element.80, bf16[2048,2048]{1,0:T(8,128)(2,1)} %all-gather.9.cloned.1.call-done.x_ref), kind=kOutput, calls=%fused_computation.5 | convolution fusion | flops 11814043648 | bytes 19922944 | tf_op jit(solution)/shard_map/tf,td->fd/dot_general | solution.py:149
  519.6 16.0 %collective-permute-done.20 = bf16[4,64,2048]{2,1,0:T(8,128)(2,1)S(1)} collective-permute-done((bf16[4,64,2048]{2,1,0:T(8,128)(2,1)S(1)}, bf16[4,64,2048]{2,1,0:T(8,128)(2,1)S(1)}, u32[]{:S(2)}, u32[]{:S(2)}) %collective-permute-start.20) | collective-permute-done | bytes 1048608 | tf_op jit(solution)/shard_map/ppermute | solution.py:55
  537.3 19.2 %collective-permute-done.21 = bf16[704,2048]{1,0:T(8,128)(2,1)} collective-permute-done((bf16[704,2048]{1,0:T(8,128)(2,1)}, bf16[704,2048]{1,0:T(8,128)(2,1)}, u32[]{:S(2)}, u32[]{:S(2)}) %collective-permute-start.21) | collective-permute-done | bytes 2883616 | tf_op jit(solution)/shard_map/ppermute | solution.py:55
  556.5 6.7 reduce-scatter.3.cloned.1.call-done
  573.9 22.0 %collective-permute-done.17 = bf16[2,64,2048]{2,1,0:T(8,128)(2,1)} collective-permute-done((bf16[2,64,2048]{2,1,0:T(8,128)(2,1)}, bf16[2,64,2048]{2,1,0:T(8,128)(2,1)}, u32[]{:S(2)}, u32[]{:S(2)}) %collective-permute-start.17) | collective-permute-done | bytes 524320 | tf_op jit(solution)/shard_map/ppermute | solution.py:55
  597.3 19.0 %fusion.66 = f32[1408,2048]{1,0:T(8,128)} fusion(bf16[2048,1408]{1,0:T(8,128)(2,1)} %get-tuple-element.104, bf16[2048,2048]{1,0:T(8,128)(2,1)} %all-gather.9.cloned.1.call-done.x_ref), kind=kOutput, calls=%fused_computation.208 | convolution fusion | flops 11811160064 | bytes 25690112 | tf_op jit(solution)/shard_map/tf,td->fd/dot_general | solution.py:149
  618.8 10.4 %fusion.67 = f32[704,2048]{1,0:T(8,128)} fusion(bf16[2048,704]{1,0:T(8,128)(2,1)S(1)} %copy-done.49, bf16[2048,2048]{1,0:T(8,128)(2,1)} %all-gather.5.cloned.1.call-done), kind=kOutput, calls=%fused_computation.209 | convolution fusion | flops 5905580032 | bytes 17039360 | tf_op jit(solution)/shard_map/tf,td->fd/dot_general | solution.py:149
  629.5 22.9 %collective-permute-done.19 = bf16[2,64,2048]{2,1,0:T(8,128)(2,1)S(1)} collective-permute-done((bf16[2,64,2048]{2,1,0:T(8,128)(2,1)S(1)}, bf16[2,64,2048]{2,1,0:T(8,128)(2,1)S(1)}, u32[]{:S(2)}, u32[]{:S(2)}) %collective-permute-start.19) | collective-permute-done | bytes 524320 | tf_op jit(solution)/shard_map/ppermute | solution.py:55
  654.4 9.5 %all-gather.11.cloned.1.call-done.mid_ref = bf16[2048,2048]{1,0:T(8,128)(2,1)} async-done(((bf16[128,2048]{1,0:T(8,128)(2,1)}), bf16[2048,2048]{1,0:T(8,128)(2,1)}) %all-gather.11.cloned.1.call-update) | async-done | bytes 8388624 | tf_op jit(solution)/shard_map/all_gather | solution.py:141
  663.9 39.7 %attend_back.1 = (bf16[2048,512]{1,0:T(8,128)(2,1)}, bf16[2048,1024]{1,0:T(8,128)(2,1)}, bf16[2048,2048]{1,0:T(8,128)(2,1)}, f32[16,1,128]{2,1,0:T(1,128)}, f32[1,2048]{1,0:T(1,128)}) custom-call(s32[4]{0:T(128)} %pad_add_fusion.places_ref, bf16[2048,2048]{1,0:T(8,128)(2,1)} %all-gather.11.cloned.1.call-done.mid_ref, f32[16,2,128]{2,1,0:T(2,128)} %copy-done.33, ...), custom_call_target="tpu_custom_call" | custom-call | flops 18522046464 | bytes 46137344 | tf_op jit(solution)/shard_map/attend_back/pallas_call | solution.py:440
  703.6 6.5 all-to-all-start.4
  714.4 3.3 collective-permute-start.22
  717.6 14.0 %fusion.63 = f32[2048,1024]{1,0:T(8,128)S(1)} fusion(bf16[2048,2048]{1,0:T(8,128)(2,1)} %all-gather.7.cloned.1.call-done.x_ref, bf16[2048,1024]{1,0:T(8,128)(2,1)} %get-tuple-element.98), kind=kOutput, calls=%fused_computation.205 | convolution fusion | flops 8589934592 | bytes 20971520 | tf_op jit(solution)/shard_map/td,tf->df/dot_general | solution.py:149
  731.7 3.5 copy-done.4
  737.0 10.1 %fusion.64 = f32[2048,512]{1,0:T(8,128)} fusion(bf16[2048,2048]{1,0:T(8,128)(2,1)} %all-gather.7.cloned.1.call-done.x_ref, bf16[2048,512]{1,0:T(8,128)(2,1)S(1)} %copy-done.52), kind=kOutput, calls=%fused_computation.206 | convolution fusion | flops 4294967296 | bytes 14680064 | tf_op jit(solution)/shard_map/td,tf->df/dot_general | solution.py:149
  750.1 7.7 fusion.65
  759.6 14.1 %collective-permute-done.28 = f32[12,2048]{1,0:T(8,128)S(1)} collective-permute-done((f32[12,2048]{1,0:T(8,128)S(1)}, f32[12,2048]{1,0:T(8,128)S(1)}, u32[]{:S(2)}, u32[]{:S(2)}) %collective-permute-start.28) | collective-permute-done | bytes 98336 | tf_op jit(solution)/shard_map/ppermute | solution.py:104
  776.3 6.8 collective-permute-done.29
  786.3 37.9 %collective-permute-done.30 = f32[12,2048]{1,0:T(8,128)S(1)} collective-permute-done((f32[12,2048]{1,0:T(8,128)S(1)}, f32[12,2048]{1,0:T(8,128)S(1)}, u32[]{:S(2)}, u32[]{:S(2)}) %collective-permute-start.30) | collective-permute-done | bytes 98336 | tf_op jit(solution)/shard_map/ppermute | solution.py:104
  826.2 5.7 bitcast_add_fusion
  839.3 4.2 all-to-all-start.6
  846.2 13.4 %collective-permute-done.32 = bf16[4,2,64,1024]{3,2,1,0:T(8,128)(2,1)} collective-permute-done((bf16[4,2,64,1024]{3,2,1,0:T(8,128)(2,1)}, bf16[4,2,64,1024]{3,2,1,0:T(8,128)(2,1)}, u32[]{:S(2)}, u32[]{:S(2)}) %collective-permute-start.32) | collective-permute-done | bytes 1048608 | tf_op jit(solution)/shard_map/ppermute | solution.py:55
  866.4 7.2 collective-permute-done.33
  874.6 4.1 all-to-all-start.5
  878.8 4.5 add_bitcast_fusion.1
  886.1 5.0 all-to-all-done.5
  900.3 7.4 add_bitcast_fusion
  907.6 13.3 %convert_add_fusion = f32[1408,2048]{1,0:T(8,128)} fusion(f32[1408,2048]{1,0:T(8,128)} %fusion.66, bf16[1408,2048]{1,0:T(8,128)(2,1)} %collective-permute-done.36), kind=kLoop, calls=%fused_computation | loop fusion | flops 5767168 | bytes 28835840 | tf_op jit(solution)/shard_map/add | solution.py:82
  921.0 3.0 fusion.15
  (289 shorter events, 115.7 us)
Async XLA Ops:
  7.2 281.8 %copy-start = (f32[2048,4]{0,1:T(4,128)S(1)}, f32[2048,4]{0,1:T(4,128)}, u32[]{:S(2)}) copy-start(f32[2048,4]{0,1:T(4,128)} %param.23) | copy-start | bytes 98308
  7.2 162.4 %all-gather.7.cloned.1.call-start = ((), (), s32[]{:S(2)}) async-start(), calls=%async_computation.10 | async-start | bytes 8912896 | tf_op jit(solution)/shard_map/all_gather | solution.py:141
  11.8 65.8 %collective-permute-start = (bf16[704,2048]{1,0:T(8,128)(2,1)}, bf16[704,2048]{1,0:T(8,128)(2,1)}, u32[]{:S(2)}, u32[]{:S(2)}) collective-permute-start(bf16[704,2048]{1,0:T(8,128)(2,1)} %bitcast.365), channel_id=1, source_target_pairs={{1,0},{0,1},{3,2},{2,3},{5,4},{4,5},{7,6},{6,7},{9,8},{8,9},{11,10... | collective-permute-start | bytes 8650760 | tf_op jit(solution)/shard_map/ppermute | solution.py:55
  17.3 60.3 %all-to-all-start = ((bf16[4,384,512]{2,1,0:T(8,128)(2,1)}), bf16[4,384,512]{2,1,0:T(8,128)(2,1)S(1)}, u32[]{:S(2)}, u32[]{:S(2)}) async-start(bf16[4,384,512]{2,1,0:T(8,128)(2,1)} %maximum_maximum_fusion), calls=%async_computation | async-start | bytes 3145728 | tf_op jit(solution)/shard_map/all_to_all | solution.py:162
  22.2 98.5 %copy-start.11 = (bf16[128,2048]{1,0:T(8,128)(2,1)S(1)}, bf16[128,2048]{1,0:T(8,128)(2,1)}, u32[]{:S(2)}) copy-start(bf16[128,2048]{1,0:T(8,128)(2,1)} %fusion.9) | copy-start | bytes 1572868
  22.2 98.5 %copy-start.27 = (f32[2048,4]{0,1:T(4,128)S(1)}, f32[2048,4]{0,1:T(4,128)}, u32[]{:S(2)}) copy-start(f32[2048,4]{0,1:T(4,128)} %param.22) | copy-start | bytes 98308
  22.2 99.0 %copy-start.35 = (s32[128,2]{0,1:T(2,128)S(1)}, s32[128,2]{0,1:T(2,128)}, u32[]{:S(2)}) copy-start(s32[128,2]{0,1:T(2,128)} %param.18) | copy-start | bytes 3076
  22.2 99.1 %copy-start.51 = (s32[1,128]{1,0:T(1,128)S(1)}, s32[1,128]{1,0:T(1,128)}, u32[]{:S(2)}) copy-start(s32[1,128]{1,0:T(1,128)} %param.17) | copy-start | bytes 1540
  22.2 216.6 %all-gather.5.cloned.1.call-start = ((), (), s32[]{:S(2)}) async-start(), calls=%async_computation.9 | async-start | bytes 8912896 | tf_op jit(solution)/shard_map/all_gather | solution.py:141
  77.6 13.2 %collective-permute-start.1 = (bf16[4,2,64,512]{3,2,1,0:T(8,128)(2,1)S(1)}, bf16[4,2,64,512]{3,2,1,0:T(8,128)(2,1)S(1)}, u32[]{:S(2)}, u32[]{:S(2)}) collective-permute-start(bf16[4,2,64,512]{3,2,1,0:T(8,128)(2,1)S(1)} %bitcast.341), channel_id=1, source_target_pairs={{1,0},{0,1},{3,2},{2,3},{5,4},{4,5},{7,6},{6,7},{9,8},{8,9},{11,10... | collective-permute-start | bytes 1572872 | tf_op jit(solution)/shard_map/ppermute | solution.py:55
  90.8 23.5 %collective-permute-start.2 = (bf16[4,256,512]{2,1,0:T(8,128)(2,1)S(1)}, bf16[4,256,512]{2,1,0:T(8,128)(2,1)S(1)}, u32[]{:S(2)}, u32[]{:S(2)}) collective-permute-start(bf16[4,256,512]{2,1,0:T(8,128)(2,1)S(1)} %slice.266), channel_id=1, source_target_pairs={{1,0},{0,1},{3,2},{2,3},{5,4},{4,5},{7,6},{6,7},{9,8},{8,9},{11,10... | collective-permute-start | bytes 3145736 | tf_op jit(solution)/shard_map/ppermute | solution.py:55
  92.3 29.0 %copy-start.17 = (bf16[2,4,2,64,512]{4,3,2,1,0:T(8,128)(2,1)}, bf16[2,4,2,64,512]{4,3,2,1,0:T(8,128)(2,1)S(1)}, u32[]{:S(2)}) copy-start(bf16[2,4,2,64,512]{4,3,2,1,0:T(8,128)(2,1)S(1)} %pad_maximum_fusion.4) | copy-start | bytes 3145732
  92.3 28.3 %collective-permute-start.3 = (bf16[2,4,2,64,512]{4,3,2,1,0:T(8,128)(2,1)S(1)}, bf16[2,4,2,64,512]{4,3,2,1,0:T(8,128)(2,1)S(1)}, u32[]{:S(2)}, u32[]{:S(2)}) collective-permute-start(bf16[2,4,2,64,512]{4,3,2,1,0:T(8,128)(2,1)S(1)} %pad_maximum_fusion.4), channel_id=1, source_target_pairs={{16,0},{0,16},{17,1},{1,17},{18,2},{2,18},{19,3},{3,19},{20,4},{4,... | collective-permute-start | bytes 3145736 | tf_op jit(solution)/shard_map/ppermute | solution.py:55
  125.0 33.3 %collective-permute-start.4 = (bf16[2,2,4,2,64,512]{5,4,3,2,1,0:T(8,128)(2,1)}, bf16[2,2,4,2,64,512]{5,4,3,2,1,0:T(8,128)(2,1)}, u32[]{:S(2)}, u32[]{:S(2)}) collective-permute-start(bf16[2,2,4,2,64,512]{5,4,3,2,1,0:T(8,128)(2,1)} %get-tuple-element.118), channel_id=1, source_target_pairs={{8,0},{0,8},{9,1},{1,9},{10,2},{2,10},{11,3},{3,11},{12,4},{4,12},... | collective-permute-start | bytes 6291464 | tf_op jit(solution)/shard_map/ppermute | solution.py:55
  125.7 43.9 %all-to-all-start.1 = ((f32[16,2,128]{2,1,0:T(2,128)}), f32[16,2,128]{2,1,0:T(2,128)S(1)}, u32[]{:S(2)}, u32[]{:S(2)}) async-start(f32[16,2,128]{2,1,0:T(2,128)} %pad_maximum_fusion.8), calls=%async_computation.1 | async-start | bytes 32768 | tf_op jit(solution)/shard_map/all_to_all | solution.py:131
  130.5 233.9 %all-gather.9.cloned.1.call-start = ((), (), s32[]{:S(2)}) async-start(), calls=%async_computation.11 | async-start | bytes 8912896 | tf_op jit(solution)/shard_map/all_gather | solution.py:141
  130.8 25.8 %collective-permute-start.5 = (bf16[256,2048]{1,0:T(8,128)(2,1)}, bf16[256,2048]{1,0:T(8,128)(2,1)S(1)}, u32[]{:S(2)}, u32[]{:S(2)}) collective-permute-start(bf16[256,2048]{1,0:T(8,128)(2,1)} %bitcast.343), channel_id=1, source_target_pairs={{1,0},{0,1},{3,2},{2,3},{5,4},{4,5},{7,6},{6,7},{9,8},{8,9},{11,10... | collective-permute-start | bytes 3145736 | tf_op jit(solution)/shard_map/ppermute | solution.py:55
  135.4 21.2 %copy-start.19 = (bf16[1,256,2048]{2,1,0:T(8,128)(2,1)S(1)}, bf16[1,256,2048]{2,1,0:T(8,128)(2,1)}, u32[]{:S(2)}) copy-start(bf16[1,256,2048]{2,1,0:T(8,128)(2,1)} %param.26) | copy-start | bytes 3145732
  209.2 7.2 collective-permute-start.6
  218.8 15.0 %collective-permute-start.11 = (bf16[2,64,2048]{2,1,0:T(8,128)(2,1)S(1)}, bf16[2,64,2048]{2,1,0:T(8,128)(2,1)S(1)}, u32[]{:S(2)}, u32[]{:S(2)}) collective-permute-start(bf16[2,64,2048]{2,1,0:T(8,128)(2,1)S(1)} %slice_bitcast_fusion.15), channel_id=1, source_target_pairs={{2,0},{4,2},{6,4},{0,6},{3,1},{5,3},{7,5},{1,7},{10,8},{12,10},{14... | collective-permute-start | bytes 1572872 | tf_op jit(solution)/shard_map/ppermute | solution.py:55
  222.4 31.5 %collective-permute-start.7 = (bf16[4,64,2048]{2,1,0:T(8,128)(2,1)S(1)}, bf16[4,64,2048]{2,1,0:T(8,128)(2,1)S(1)}, u32[]{:S(2)}, u32[]{:S(2)}) collective-permute-start(bf16[4,64,2048]{2,1,0:T(8,128)(2,1)S(1)} %slice_bitcast_fusion.7), channel_id=1, source_target_pairs={{16,0},{0,16},{17,1},{1,17},{18,2},{2,18},{19,3},{3,19},{20,4},{4,... | collective-permute-start | bytes 3145736 | tf_op jit(solution)/shard_map/ppermute | solution.py:55
  233.9 16.2 %collective-permute-start.12 = (bf16[2,64,2048]{2,1,0:T(8,128)(2,1)S(1)}, bf16[2,64,2048]{2,1,0:T(8,128)(2,1)S(1)}, u32[]{:S(2)}, u32[]{:S(2)}) collective-permute-start(bf16[2,64,2048]{2,1,0:T(8,128)(2,1)S(1)} %fusion.23), channel_id=1, source_target_pairs={{2,0},{4,2},{6,4},{0,6},{3,1},{5,3},{7,5},{1,7},{10,8},{12,10},{14... | collective-permute-start | bytes 1572872 | tf_op jit(solution)/shard_map/ppermute | solution.py:55
  250.2 23.4 %collective-permute-start.13 = (bf16[2,64,2048]{2,1,0:T(8,128)(2,1)S(1)}, bf16[2,64,2048]{2,1,0:T(8,128)(2,1)S(1)}, u32[]{:S(2)}, u32[]{:S(2)}) collective-permute-start(bf16[2,64,2048]{2,1,0:T(8,128)(2,1)S(1)} %fusion.22), channel_id=1, source_target_pairs={{2,0},{4,2},{6,4},{0,6},{3,1},{5,3},{7,5},{1,7},{10,8},{12,10},{14... | collective-permute-start | bytes 1572872 | tf_op jit(solution)/shard_map/ppermute | solution.py:55
  254.3 14.9 %collective-permute-start.8 = (bf16[64,2048]{1,0:T(8,128)(2,1)S(1)}, bf16[64,2048]{1,0:T(8,128)(2,1)S(1)}, u32[]{:S(2)}, u32[]{:S(2)}) collective-permute-start(bf16[64,2048]{1,0:T(8,128)(2,1)S(1)} %slice_bitcast_fusion.21), channel_id=1, source_target_pairs={{2,0},{4,2},{6,4},{0,6},{3,1},{5,3},{7,5},{1,7},{10,8},{12,10},{14... | collective-permute-start | bytes 786440 | tf_op jit(solution)/shard_map/ppermute | solution.py:55
  262.5 23.5 %copy-start.2 = (bf16[128,2048]{1,0:T(8,128)(2,1)S(1)}, bf16[128,2048]{1,0:T(8,128)(2,1)}, u32[]{:S(2)}) copy-start(bf16[128,2048]{1,0:T(8,128)(2,1)} %param.16) | copy-start | bytes 1572868
  262.5 23.5 %copy-start.25 = (f32[2048]{0:T(1024)S(1)}, f32[2048]{0:T(1024)}, u32[]{:S(2)}) copy-start(f32[2048]{0:T(1024)} %param.27) | copy-start | bytes 24580
  262.5 23.8 %copy-start.31 = (f32[2048]{0:T(1024)S(1)}, f32[2048]{0:T(1024)}, u32[]{:S(2)}) copy-start(f32[2048]{0:T(1024)} %param.21) | copy-start | bytes 24580
  269.3 8.2 collective-permute-start.9
  273.9 8.1 collective-permute-start.14
  277.6 8.2 collective-permute-start.10
  287.4 275.8 %reduce-scatter.3.cloned.1.call-start = ((), (), s32[]{:S(2)}) async-start(), calls=%async_computation.12 | async-start | bytes 8912896 | tf_op jit(solution)/shard_map/reduce_scatter | solution.py:145
  287.4 122.0 %collective-permute-start.15 = (bf16[1408,2048]{1,0:T(8,128)(2,1)}, bf16[1408,2048]{1,0:T(8,128)(2,1)}, u32[]{:S(2)}, u32[]{:S(2)}) collective-permute-start(bf16[1408,2048]{1,0:T(8,128)(2,1)} %bitcast.324), channel_id=1, source_target_pairs={{1,0},{0,1},{3,2},{2,3},{5,4},{4,5},{7,6},{6,7},{9,8},{8,9},{11,10... | collective-permute-start | bytes 17301512 | tf_op jit(solution)/shard_map/ppermute | solution.py:55
  473.2 19.6 %collective-permute-start.16 = (bf16[2,4,128,2048]{3,2,0,1:T(8,128)(2,1)}, bf16[2,4,128,2048]{3,2,0,1:T(8,128)(2,1)}, u32[]{:S(2)}, u32[]{:S(2)}) collective-permute-start(bf16[2,4,128,2048]{3,2,0,1:T(8,128)(2,1)} %bitcast.322), channel_id=1, source_target_pairs={{8,0},{0,8},{9,1},{1,9},{10,2},{2,10},{11,3},{3,11},{12,4},{4,12},... | collective-permute-start | bytes 12582920 | tf_op jit(solution)/shard_map/ppermute | solution.py:55
  473.8 45.7 %all-to-all-start.3 = ((f32[16,1,128]{2,1,0:T(1,128)}), f32[16,1,128]{2,1,0:T(1,128)S(1)}, u32[]{:S(2)}, u32[]{:S(2)}) async-start(f32[16,1,128]{2,1,0:T(1,128)} %add.175), calls=%async_computation.4 | async-start | bytes 16384 | tf_op jit(solution)/shard_map/all_to_all | solution.py:135
  480.2 183.6 %all-gather.11.cloned.1.call-start = ((), (), s32[]{:S(2)}) async-start(), calls=%async_computation.13 | async-start | bytes 8912896 | tf_op jit(solution)/shard_map/all_gather | solution.py:141
  491.3 65.1 %collective-permute-start.21 = (bf16[704,2048]{1,0:T(8,128)(2,1)}, bf16[704,2048]{1,0:T(8,128)(2,1)}, u32[]{:S(2)}, u32[]{:S(2)}) collective-permute-start(bf16[704,2048]{1,0:T(8,128)(2,1)} %convolution_convert_fusion.3), channel_id=1, source_target_pairs={{1,0},{0,1},{3,2},{2,3},{5,4},{4,5},{7,6},{6,7},{9,8},{8,9},{11,10... | collective-permute-start | bytes 8650760 | tf_op jit(solution)/shard_map/ppermute | solution.py:55
  499.0 36.5 %collective-permute-start.20 = (bf16[4,64,2048]{2,1,0:T(8,128)(2,1)S(1)}, bf16[4,64,2048]{2,1,0:T(8,128)(2,1)S(1)}, u32[]{:S(2)}, u32[]{:S(2)}) collective-permute-start(bf16[4,64,2048]{2,1,0:T(8,128)(2,1)S(1)} %slice_bitcast_fusion.5), channel_id=1, source_target_pairs={{16,0},{0,16},{17,1},{1,17},{18,2},{2,18},{19,3},{3,19},{20,4},{4,... | collective-permute-start | bytes 3145736 | tf_op jit(solution)/shard_map/ppermute | solution.py:55
  537.2 172.8 %copy-start.14 = (bf16[4,64,2048]{2,1,0:T(8,128)(2,1)}, bf16[4,64,2048]{2,1,0:T(8,128)(2,1)S(1)}, u32[]{:S(2)}) copy-start(bf16[4,64,2048]{2,1,0:T(8,128)(2,1)S(1)} %fusion.3) | copy-start | bytes 3145732
  568.3 330.7 %reduce-scatter.5.cloned.1.call-start = ((), (), s32[]{:S(2)}) async-start(), calls=%async_computation.14 | async-start | bytes 8912896 | tf_op jit(solution)/shard_map/reduce_scatter | solution.py:145
  570.2 25.6 %collective-permute-start.17 = (bf16[2,64,2048]{2,1,0:T(8,128)(2,1)}, bf16[2,64,2048]{2,1,0:T(8,128)(2,1)}, u32[]{:S(2)}, u32[]{:S(2)}) collective-permute-start(bf16[2,64,2048]{2,1,0:T(8,128)(2,1)} %slice_bitcast_fusion.11), channel_id=1, source_target_pairs={{2,0},{4,2},{6,4},{0,6},{3,1},{5,3},{7,5},{1,7},{10,8},{12,10},{14... | collective-permute-start | bytes 1572872 | tf_op jit(solution)/shard_map/ppermute | solution.py:55
  572.3 327.9 %collective-permute-start.36 = (bf16[1408,2048]{1,0:T(8,128)(2,1)}, bf16[1408,2048]{1,0:T(8,128)(2,1)}, u32[]{:S(2)}, u32[]{:S(2)}) collective-permute-start(bf16[1408,2048]{1,0:T(8,128)(2,1)} %convolution_convert_fusion), channel_id=1, source_target_pairs={{1,0},{0,1},{3,2},{2,3},{5,4},{4,5},{7,6},{6,7},{9,8},{8,9},{11,10... | collective-permute-start | bytes 17301512 | tf_op jit(solution)/shard_map/ppermute | solution.py:55
  597.2 19.1 %collective-permute-start.18 = (bf16[2,64,2048]{2,1,0:T(8,128)(2,1)S(1)}, bf16[2,64,2048]{2,1,0:T(8,128)(2,1)S(1)}, u32[]{:S(2)}, u32[]{:S(2)}) collective-permute-start(bf16[2,64,2048]{2,1,0:T(8,128)(2,1)S(1)} %fusion.20), channel_id=1, source_target_pairs={{2,0},{4,2},{6,4},{0,6},{3,1},{5,3},{7,5},{1,7},{10,8},{12,10},{14... | collective-permute-start | bytes 1572872 | tf_op jit(solution)/shard_map/ppermute | solution.py:55
  597.3 21.5 %copy-start.49 = (bf16[2048,704]{1,0:T(8,128)(2,1)S(1)}, bf16[2048,704]{1,0:T(8,128)(2,1)}, u32[]{:S(2)}) copy-start(bf16[2048,704]{1,0:T(8,128)(2,1)} %get-tuple-element.74.refs_0_) | copy-start | bytes 8650756
  617.5 34.9 %collective-permute-start.19 = (bf16[2,64,2048]{2,1,0:T(8,128)(2,1)S(1)}, bf16[2,64,2048]{2,1,0:T(8,128)(2,1)S(1)}, u32[]{:S(2)}, u32[]{:S(2)}) collective-permute-start(bf16[2,64,2048]{2,1,0:T(8,128)(2,1)S(1)} %fusion.19), channel_id=1, source_target_pairs={{2,0},{4,2},{6,4},{0,6},{3,1},{5,3},{7,5},{1,7},{10,8},{12,10},{14... | collective-permute-start | bytes 1572872 | tf_op jit(solution)/shard_map/ppermute | solution.py:55
  703.6 43.6 %all-to-all-start.4 = ((f32[16,1,128]{2,1,0:T(1,128)}), f32[16,1,128]{2,1,0:T(1,128)S(1)}, u32[]{:S(2)}, u32[]{:S(2)}) async-start(f32[16,1,128]{2,1,0:T(1,128)} %get-tuple-element.94), calls=%async_computation.5 | async-start | bytes 16384 | tf_op jit(solution)/shard_map/all_to_all | solution.py:135
  712.4 62.8 %collective-permute-start.25 = (bf16[64,2048]{1,0:T(8,128)(2,1)}, bf16[64,2048]{1,0:T(8,128)(2,1)}, u32[]{:S(2)}, u32[]{:S(2)}) collective-permute-start(bf16[64,2048]{1,0:T(8,128)(2,1)} %slice_bitcast_fusion.26), channel_id=1, source_target_pairs={{16,0},{0,16},{17,1},{1,17},{18,2},{2,18},{19,3},{3,19},{20,4},{4,... | collective-permute-start | bytes 786440 | tf_op jit(solution)/shard_map/ppermute | solution.py:55
  714.4 70.1 %collective-permute-start.22 = (bf16[64,2048]{1,0:T(8,128)(2,1)}, bf16[64,2048]{1,0:T(8,128)(2,1)}, u32[]{:S(2)}, u32[]{:S(2)}) collective-permute-start(bf16[64,2048]{1,0:T(8,128)(2,1)} %slice_bitcast_fusion.27), channel_id=1, source_target_pairs={{2,0},{4,2},{6,4},{0,6},{3,1},{5,3},{7,5},{1,7},{10,8},{12,10},{14... | collective-permute-start | bytes 786440 | tf_op jit(solution)/shard_map/ppermute | solution.py:55
  736.9 89.3 %collective-permute-start.31 = (bf16[2,512,1024]{2,1,0:T(8,128)(2,1)}, bf16[2,512,1024]{2,1,0:T(8,128)(2,1)}, u32[]{:S(2)}, u32[]{:S(2)}) collective-permute-start(bf16[2,512,1024]{2,1,0:T(8,128)(2,1)} %fusion.2), channel_id=1, source_target_pairs={{0,8},{8,0},{1,9},{9,1},{2,10},{10,2},{3,11},{11,3},{4,12},{12,4},... | collective-permute-start | bytes 6291464 | tf_op jit(solution)/shard_map/ppermute | solution.py:199
  748.9 8.9 collective-permute-start.26
  757.8 26.7 %copy-start.10 = (f32[512,2048]{1,0:T(8,128)}, f32[512,2048]{1,0:T(8,128)S(1)}, u32[]{:S(2)}) copy-start(f32[512,2048]{1,0:T(8,128)S(1)} %fusion.65) | copy-start | bytes 12582916
  757.8 17.5 %copy-start.18 = (bf16[2,64,2048]{2,1,0:T(8,128)(2,1)S(1)}, bf16[2,64,2048]{2,1,0:T(8,128)(2,1)}, u32[]{:S(2)}) copy-start(bf16[2,64,2048]{2,1,0:T(8,128)(2,1)} %fusion.18) | copy-start | bytes 1572868
  757.9 27.4 %copy-start.15 = (bf16[4,64,2048]{2,1,0:T(8,128)(2,1)S(1)}, bf16[4,64,2048]{2,1,0:T(8,128)(2,1)}, u32[]{:S(2)}) copy-start(bf16[4,64,2048]{2,1,0:T(8,128)(2,1)} %copy-done.14) | copy-start | bytes 3145732
  757.9 1.4 collective-permute-start.27
  759.3 14.4 %collective-permute-start.28 = (f32[12,2048]{1,0:T(8,128)S(1)}, f32[12,2048]{1,0:T(8,128)S(1)}, u32[]{:S(2)}, u32[]{:S(2)}) collective-permute-start(f32[12,2048]{1,0:T(8,128)S(1)} %add.187), channel_id=1, source_target_pairs={{0,2},{2,0},{4,6},{6,4},{1,3},{3,1},{5,7},{7,5},{8,10},{10,8},{12,... | collective-permute-start | bytes 294920 | tf_op jit(solution)/shard_map/ppermute | solution.py:104
  773.7 64.0 %collective-permute-start.34 = (bf16[4,256,512]{2,1,0:T(8,128)(2,1)S(1)}, bf16[4,256,512]{2,1,0:T(8,128)(2,1)S(1)}, u32[]{:S(2)}, u32[]{:S(2)}) collective-permute-start(bf16[4,256,512]{2,1,0:T(8,128)(2,1)S(1)} %fusion.6), channel_id=1, source_target_pairs={{1,0},{0,1},{3,2},{2,3},{5,4},{4,5},{7,6},{6,7},{9,8},{8,9},{11,10... | collective-permute-start | bytes 3145736 | tf_op jit(solution)/shard_map/ppermute | solution.py:55
  775.2 7.9 collective-permute-start.29
  783.1 95.6 %collective-permute-start.35 = (bf16[256,2048]{1,0:T(8,128)(2,1)}, bf16[256,2048]{1,0:T(8,128)(2,1)}, u32[]{:S(2)}, u32[]{:S(2)}) collective-permute-start(bf16[256,2048]{1,0:T(8,128)(2,1)} %select_convert_fusion.1), channel_id=1, source_target_pairs={{1,0},{0,1},{3,2},{2,3},{5,4},{4,5},{7,6},{6,7},{9,8},{8,9},{11,10... | collective-permute-start | bytes 3145736 | tf_op jit(solution)/shard_map/ppermute | solution.py:55
  784.5 39.7 %collective-permute-start.30 = (f32[12,2048]{1,0:T(8,128)S(1)}, f32[12,2048]{1,0:T(8,128)S(1)}, u32[]{:S(2)}, u32[]{:S(2)}) collective-permute-start(f32[12,2048]{1,0:T(8,128)S(1)} %add.189), channel_id=1, source_target_pairs={{0,1},{1,0},{2,3},{3,2},{4,5},{5,4},{6,7},{7,6},{8,9},{9,8},{10,11... | collective-permute-start | bytes 294920 | tf_op jit(solution)/shard_map/ppermute | solution.py:104
  824.2 12.8 %collective-permute-start.23 = (bf16[64,2048]{1,0:T(8,128)(2,1)S(1)}, bf16[64,2048]{1,0:T(8,128)(2,1)S(1)}, u32[]{:S(2)}, u32[]{:S(2)}) collective-permute-start(bf16[64,2048]{1,0:T(8,128)(2,1)S(1)} %fusion.29), channel_id=1, source_target_pairs={{2,0},{4,2},{6,4},{0,6},{3,1},{5,3},{7,5},{1,7},{10,8},{12,10},{14... | collective-permute-start | bytes 786440 | tf_op jit(solution)/shard_map/ppermute | solution.py:55
  835.0 24.6 %collective-permute-start.32 = (bf16[4,2,64,1024]{3,2,1,0:T(8,128)(2,1)}, bf16[4,2,64,1024]{3,2,1,0:T(8,128)(2,1)}, u32[]{:S(2)}, u32[]{:S(2)}) collective-permute-start(bf16[4,2,64,1024]{3,2,1,0:T(8,128)(2,1)} %bitcast.85), channel_id=1, source_target_pairs={{16,0},{0,16},{17,1},{1,17},{18,2},{2,18},{19,3},{3,19},{20,4},{4,... | collective-permute-start | bytes 3145736 | tf_op jit(solution)/shard_map/ppermute | solution.py:55
  837.7 26.8 %collective-permute-start.24 = (bf16[64,2048]{1,0:T(8,128)(2,1)}, bf16[64,2048]{1,0:T(8,128)(2,1)}, u32[]{:S(2)}, u32[]{:S(2)}) collective-permute-start(bf16[64,2048]{1,0:T(8,128)(2,1)} %fusion.28), channel_id=1, source_target_pairs={{2,0},{4,2},{6,4},{0,6},{3,1},{5,3},{7,5},{1,7},{10,8},{12,10},{14... | collective-permute-start | bytes 786440 | tf_op jit(solution)/shard_map/ppermute | solution.py:55
  839.3 35.3 %all-to-all-start.6 = ((bf16[4,256,512]{2,1,0:T(8,128)(2,1)}), bf16[4,256,512]{2,1,0:T(8,128)(2,1)}, u32[]{:S(2)}, u32[]{:S(2)}) async-start(bf16[4,256,512]{2,1,0:T(8,128)(2,1)} %fusion.5), calls=%async_computation.8 | async-start | bytes 2097152 | tf_op jit(solution)/shard_map/all_to_all | solution.py:162
  861.4 12.2 %collective-permute-start.33 = (bf16[4,64,1024]{2,1,0:T(8,128)(2,1)S(1)}, bf16[4,64,1024]{2,1,0:T(8,128)(2,1)S(1)}, u32[]{:S(2)}, u32[]{:S(2)}) collective-permute-start(bf16[4,64,1024]{2,1,0:T(8,128)(2,1)S(1)} %fusion.25), channel_id=1, source_target_pairs={{1,0},{0,1},{3,2},{2,3},{5,4},{4,5},{7,6},{6,7},{9,8},{8,9},{11,10... | collective-permute-start | bytes 1572872 | tf_op jit(solution)/shard_map/ppermute | solution.py:55
  874.6 16.5 %all-to-all-start.5 = ((bf16[4,64,1024]{2,1,0:T(8,128)(2,1)}), bf16[4,64,1024]{2,1,0:T(8,128)(2,1)}, u32[]{:S(2)}, u32[]{:S(2)}) async-start(bf16[4,64,1024]{2,1,0:T(8,128)(2,1)} %fusion.24), calls=%async_computation.7 | async-start | bytes 1048576 | tf_op jit(solution)/shard_map/all_to_all | solution.py:162
  (38 other events, 342.3 us)
Sparse Core Ops, SparseCore 0:
  11.9 106.3 all-gather.6
  120.8 75.1 all-gather.4
  287.5 76.8 all-gather.8
  445.5 117.6 reduce-scatter.2
  568.4 95.4 all-gather.10
  703.7 110.0 reduce-scatter.4

commit v9 on v8

--- a/solution.py
+++ b/solution.py
@@ -96,8 +96,8 @@
     return list(jnp.roll(jnp.stack(parts), -lax.axis_index(axis), axis=0))
 
 
-def sum_all(value):
-    for axis in ALL:
+def sum_over(value, axes):
+    for axis in axes:
         size = lax.axis_size(axis)
         step = 1
         while step < size:
@@ -187,11 +187,11 @@
     return query, arrange(places, kv), seen
 
 
-def scatter_query(grad):
+def scatter_query(grad, *others):
     inner = lax.axis_size("i")
     blocks = grad.reshape(OUTER, inner, -1, grad.shape[1])
     blocks = from_order([blocks[:, k] for k in range(inner)], "i")
-    mine = ring_scatter(blocks, "i").astype(BF16)
+    mine = ring_scatter(blocks[:1] + list(after(blocks[1:], *others)), "i").astype(BF16)
     return join_blocks(exchange(mine)).astype(F32)
 
 
@@ -200,13 +200,15 @@
     high, inner = lax.axis_size("y"), lax.axis_size("i")
     wide = kept.shape[-1]
     mine = mine.reshape(high, OUTER, inner, -1, wide)
-    mine = ring_scatter(from_order([mine[k] for k in range(high)], "y"), "y")
+    own, arrived = ring_open(from_order([mine[k] for k in range(high)], "y"), "y")
+    mine = arrived.astype(F32) + own
     mine = ring_scatter(from_order([mine[:, k] for k in range(inner)], "i"), "i").astype(BF16)
     here = exchange(mine)
     half = wide // 2
-    return jnp.concatenate(
+    whole = jnp.concatenate(
         [join_blocks(here[:, :, :half]), join_blocks(here[:, :, half:])], axis=1
-    ).astype(F32)
+    )
+    return whole.astype(F32), arrived
 
 
 def own_places():
@@ -217,11 +219,14 @@
     return (first.astype(F32) + second.astype(F32)).astype(BF16)
 
 
-def ring_low(blocks, axis):
+def ring_low(blocks, axis, *others):
     travelling = blocks[1]
     for j in range(2, lax.axis_size(axis)):
         travelling = add_low(shift(travelling, axis), blocks[j])
-    return add_low(shift(travelling, axis), blocks[0])
+    arrived = shift(travelling, axis)
+    if others:
+        arrived = after(arrived, *others)
+    return add_low(arrived, blocks[0])
 
 
 def part_low(rows):
@@ -670,7 +675,7 @@
     query_mat, kv_mat, seen = gather_heads(
         places, query_weight[0], kv_weight, down_parts[1:]
     )
-    out_mat = in_order(ring_gather(after(out_weight[0], seen), "i"), "i").reshape(span, width)
+    out_parts = ring_gather(after(out_weight[0], seen), "i")
     own_up = up_weight[0].reshape(-1, width)
 
     residual = hidden_in.astype(F32)
@@ -681,6 +686,8 @@
     all_attn = meet(attn_input)
     all_cot = meet(after(cotangent.astype(BF16), seen))
     qkv, gated = attend(places, all_attn, info, cosine, sine_table, query_mat, kv_mat)
+    out_parts = out_parts[:1] + list(after(out_parts[1:], gated))
+    out_mat = in_order(out_parts, "i").reshape(span, width)
     branch = part_low(ring_rows(places, [gated], [out_mat], tokens))
     branch = part_second(*part_first(branch))
 
@@ -719,9 +726,9 @@
     rows_out = part_low(ring_rows(places, gated_units, down_parts, tokens))
     half = tokens // 2
     rows_first, rows_second = rows_out[:, :, :half], rows_out[:, :, half:]
-    rows_first = ring_low([rows_first[k] for k in range(rows_first.shape[0])], "y")
-    d_lower, last = ring_open(grad_down[:1] + low_down, "i")
-    d_mlp_input = after(d_mlp_input, rows_first, low_up, last)
+    lower_own, lower_last = ring_open(grad_down[:1] + low_down, "i")
+    upper_own, upper_last = ring_open(grad_up[:1] + low_up, "i")
+    d_mlp_input = after(d_mlp_input, rows_out, low_up, lower_last)
     d_mlp_router, d_mlp_from_router = gates_back(
         mlp_gate, mlp_onehot, d_mlp_gate, mlp_input, mlp_router
     )
@@ -742,7 +749,9 @@
     d_heads, d_kv, rows_one, d_gate_a, d_gain_a = attend_back(
         places, all_mid, info, cosine, sine_table, qkv, all_attn, query_mat, kv_mat, out_mat
     )
-    rows_out = part_second(after(rows_first, d_heads), after(rows_second, d_heads))
+    rows_first = after(rows_first, all_mid)
+    rows_first = [rows_first[k] for k in range(rows_first.shape[0])]
+    rows_out = part_second(ring_low(rows_first, "y", d_heads), after(rows_second, d_heads))
     layer_out = middle + rows_out.astype(F32) + mlp_bias
     d_attn_input = part(rows_one)
     d_att_gate = from_experts(d_gate_a[:, 0], att_onehot, experts)
@@ -750,19 +759,21 @@
     d_kv_mat = from_order([d_kv_mat[:, 0], d_kv_mat[:, 1]], "c")
     d_kv_sent = d_kv_mat[1].astype(BF16)
     d_heads, all_mid = after((d_heads, all_mid), d_kv_sent)
-    d_kv_weight = scatter_kv(d_kv_mat[0], d_kv_sent)
-    d_query = scatter_query(mm("td,tf->df", all_attn, d_heads))[None]
-    d_out = mm("tf,td->fd", gated, all_mid).reshape(inner, -1, width)
-    d_output = ring_scatter(from_order([d_out[k] for k in range(inner)], "i"), "i")[None]
-    d_upper = ring_scatter(grad_up[:1] + low_up, "i", d_attn_input).reshape(up_weight.shape)
-    d_lower = (after(last, d_attn_input).astype(F32) + d_lower)[None]
+    d_kv_weight, kv_arrived = scatter_kv(d_kv_mat[0], d_kv_sent)
     d_att_router, d_att_from_router = gates_back(
         att_gate, att_onehot, d_att_gate, attn_input, att_router
     )
     d_gain_one = d_gain_a / norm_gain1 + jnp.sum(
         d_att_from_router * residual * inverse_one, axis=0, keepdims=True
     )
-    summed = sum_all(jnp.concatenate([d_gain_one, sums, d_att_router]))
+    summed = sum_over(jnp.concatenate([d_gain_one, sums, d_att_router]), ("i",))
+    d_query = scatter_query(mm("td,tf->df", all_attn, d_heads), summed)[None]
+    d_out = mm("tf,td->fd", gated, all_mid).reshape(inner, -1, width)
+    d_out = from_order([d_out[k] for k in range(inner)], "i")
+    d_output = ring_scatter(d_out[:1] + list(after(d_out[1:], summed)), "i")[None]
+    d_upper = (after(upper_last, d_kv_sent).astype(F32) + upper_own).reshape(up_weight.shape)
+    d_lower = (lower_last.astype(F32) + lower_own)[None]
+    summed = sum_over(after(summed, kv_arrived), ("c", "o", "y"))
     d_attn_input = after(d_attn_input, summed)
     d_norm_one, _ = norm_back(
         residual, inverse_one, norm_gain1, d_attn_input.astype(F32) + d_att_from_router

time: 936 us -> 892 us (0.953)
  waiting for transfers between devices: 391 us -> 340 us
  starting transfers between devices: 90.3 us -> 113 us
    ppermute x5, waiting for transfers between devices: 59 us -> 15.4 us  [sum_over(): lax.ppermute(value, axis, [(k, k ^ step) for k in range(size)])]
    ppermute x31, starting transfers between devices: 56.3 us -> 75.5 us  [shift(): return lax.ppermute(value, axis, [((k + 1) % size, k) for k in range(size)])]
    ppermute x31, waiting for transfers between devices: 250 us -> 239 us  [shift(): return lax.ppermute(value, axis, [((k + 1) % size, k) for k in range(size)])]
  transfers between devices with their start and end apart: 49 -> 49, of which waited for: 25 -> 27; matrix products, arithmetic and copies ran while one was open for 22% -> 24% of each run, Pallas kernels for 15% -> 15%
where the time goes in v9:
time: 892 us
  waiting for transfers between devices  340 us (38%)
  Pallas kernels  173 us (19%)
  matrix products  114 us (13%)
  starting transfers between devices  113 us (13%)
  other arithmetic  84.8 us (10%)
  local copies, waits for them, and re-layouts  40.2 us (5%)
  between operations  15.2 us (2%)
  blocking collectives  11.8 us (1%)
    ppermute x31, waiting for transfers between devices, shift(): return lax.ppermute(value, axis, [((k + 1) % size, k) for k in range(size)])  239 us
    pallas_call x7, Pallas kernels, call(): pl.pallas_call(kernel, grid_spec=pltpu.PrefetchScalarGridSpec(num_scalar_...  173 us
    dot_general x9, matrix products, mm(): return jnp.einsum(form, first, second, preferred_element_type=F32)  106 us
    ppermute x31, starting transfers between devices, shift(): return lax.ppermute(value, axis, [((k + 1) % size, k) for k in range(size)])  75.5 us
    all_gather x4, waiting for transfers between devices, meet(): return lax.all_gather(rows, GROUP, axis=0, tiled=True)  75 us
    unnamed x129, local copies, waits for them, and re-layouts  18.5 us
  transfers between devices with their start and end apart: 49, of which 27 were waited for; matrix products, arithmetic and copies ran while one was open for 24% of the time, Pallas kernels for 15%

profile of v9, /device:TPU:0, one launch (start us, length us, event | category | flops | bytes accessed | tf_op | source)
XLA Modules:
  0.0 892.3 jit_solution(2088209085881574625)
XLA Ops:
  17.4 4.9 all-to-all-start
  22.2 55.4 %collective-permute-done.refs_3_ = bf16[704,2048]{1,0:T(8,128)(2,1)} collective-permute-done((bf16[704,2048]{1,0:T(8,128)(2,1)}, bf16[704,2048]{1,0:T(8,128)(2,1)}, u32[]{:S(2)}, u32[]{:S(2)}) %collective-permute-start) | collective-permute-done | bytes 2883616 | tf_op jit(solution)/shard_map/ppermute | solution.py:55
  79.6 11.3 %collective-permute-done.1 = bf16[4,2,64,512]{3,2,1,0:T(8,128)(2,1)S(1)} collective-permute-done((bf16[4,2,64,512]{3,2,1,0:T(8,128)(2,1)S(1)}, bf16[4,2,64,512]{3,2,1,0:T(8,128)(2,1)S(1)}, u32[]{:S(2)}, u32[]{:S(2)}) %collective-permute-start.1) | collective-permute-done | bytes 524320 | tf_op jit(solution)/shard_map/ppermute | solution.py:55
  95.5 18.9 %collective-permute-done.2 = bf16[4,256,512]{2,1,0:T(8,128)(2,1)S(1)} collective-permute-done((bf16[4,256,512]{2,1,0:T(8,128)(2,1)S(1)}, bf16[4,256,512]{2,1,0:T(8,128)(2,1)S(1)}, u32[]{:S(2)}, u32[]{:S(2)}) %collective-permute-start.2) | collective-permute-done | bytes 1048608 | tf_op jit(solution)/shard_map/ppermute | solution.py:55
  114.4 6.3 collective-permute-done.3
  121.8 3.2 fusion.51
  126.8 4.8 all-to-all-start.1
  138.6 4.0 pad_maximum_fusion.in_ref
  142.6 7.4 arrange.1
  150.6 25.6 %attend.1 = (bf16[2048,1536]{1,0:T(8,128)(2,1)}, bf16[2048,512]{1,0:T(8,128)(2,1)}) custom-call(s32[4]{0:T(128)} %pad_add_fusion.places_ref, bf16[2048,2048]{1,0:T(8,128)(2,1)} %all-gather.7.cloned.1.call-done.x_ref, f32[16,2,128]{2,1,0:T(2,128)} %copy-done.35, f32[128,128]{1,0:T(8,128)} %get-tuple-element.173.cos_ref, ...), custom_call_target="tpu_custom_call" | custom-call | flops 13421772800 | bytes 25165824 | tf_op jit(solution)/shard_map/attend/pallas_call | solution.py:445
  177.8 9.2 %rows.2 = bf16[2,2,4,128,2048]{4,3,2,1,0:T(8,128)(2,1)} custom-call(s32[4]{0:T(128)} %pad_add_fusion.places_ref, bf16[2048,512]{1,0:T(8,128)(2,1)} %get-tuple-element.78.refs_0_, bf16[512,2048]{1,0:T(8,128)(2,1)} %bitcast.339), custom_call_target="tpu_custom_call" | custom-call | flops 4294967296 | bytes 20971520 | tf_op jit(solution)/shard_map/rows/pallas_call | solution.py:445
  187.0 3.9 fusion.54
  191.7 7.6 collective-permute-done.6
  201.7 3.2 collective-permute-start.11
  207.0 9.4 %collective-permute-done.11 = bf16[2,64,2048]{2,1,0:T(8,128)(2,1)S(1)} collective-permute-done((bf16[2,64,2048]{2,1,0:T(8,128)(2,1)S(1)}, bf16[2,64,2048]{2,1,0:T(8,128)(2,1)S(1)}, u32[]{:S(2)}, u32[]{:S(2)}) %collective-permute-start.11) | collective-permute-done | bytes 524320 | tf_op jit(solution)/shard_map/ppermute | solution.py:55
  216.5 15.1 %collective-permute-start.12 = (bf16[2,64,2048]{2,1,0:T(8,128)(2,1)S(1)}, bf16[2,64,2048]{2,1,0:T(8,128)(2,1)S(1)}, u32[]{:S(2)}, u32[]{:S(2)}) collective-permute-start(bf16[2,64,2048]{2,1,0:T(8,128)(2,1)S(1)} %fusion.22), channel_id=1, source_target_pairs={{2,0},{4,2},{6,4},{0,6},{3,1},{5,3},{7,5},{1,7},{10,8},{12,10},{14... | collective-permute-start | bytes 1572872 | tf_op jit(solution)/shard_map/ppermute | solution.py:55
  231.6 11.3 %convolution_convert_fusion.1.d_units_ref = bf16[2048,704]{1,0:T(8,128)(2,1)} fusion(bf16[2048,2048]{1,0:T(8,128)(2,1)} %all-gather.5.cloned.1.call-done, bf16[704,2048]{1,0:T(8,128)(2,1)} %collective-permute-done.refs_3_), kind=kOutput, calls=%fused_computation.16 | convolution fusion | flops 5907021824 | bytes 14155776 | tf_op jit(solution)/shard_map/td,fd->tf/dot_general | solution.py:149
  243.0 3.7 collective-permute-start.13
  247.2 8.1 convolution_convert_fusion.2.d_units_ref
  255.3 6.8 collective-permute-done.8
  262.2 4.3 collective-permute-start.9
  270.5 4.3 collective-permute-start.10
  274.9 3.8 collective-permute-done.10
  284.1 11.8 %all_to_all.37.info_ref = f32[16,1,128]{2,1,0:T(1,128)} all-to-all(f32[16,1,128]{2,1,0:T(1,128)S(1)} %bitcast.353), channel_id=1, replica_groups=mesh['y'=2,'c'=2,'o'=4,'i'=2] {'y','c','o'}, dimensions={0} | all-to-all | bytes 16384 | tf_op jit(solution)/shard_map/all_to_all | solution.py:131
  295.9 61.0 %all-gather.9.cloned.1.call-done.x_ref = bf16[2048,2048]{1,0:T(8,128)(2,1)} async-done(((bf16[128,2048]{1,0:T(8,128)(2,1)}), bf16[2048,2048]{1,0:T(8,128)(2,1)}) %all-gather.9.cloned.1.call-update) | async-done | bytes 8388624 | tf_op jit(solution)/shard_map/all_gather | solution.py:141
  356.9 35.5 %units.2 = (bf16[2048,1408]{1,0:T(8,128)(2,1)}, bf16[2048,704]{1,0:T(8,128)(2,1)}, f32[2048,2048]{1,0:T(8,128)}, f32[16,1,128]{2,1,0:T(1,128)}) custom-call(s32[4]{0:T(128)} %pad_add_fusion.places_ref, bf16[2048,2048]{1,0:T(8,128)(2,1)} %all-gather.9.cloned.1.call-done.x_ref, f32[16,1,128]{2,1,0:T(1,128)} %all_to_all.37.info_ref, ...), custom_call_target="tpu_custom_call" | custom-call | tf_op jit(solution)/shard_map/units/pallas_call | solution.py:445
  392.4 10.5 %collective-permute-done.15.first_ref.second_ref = bf16[1408,2048]{1,0:T(8,128)(2,1)} collective-permute-done((bf16[1408,2048]{1,0:T(8,128)(2,1)}, bf16[1408,2048]{1,0:T(8,128)(2,1)}, u32[]{:S(2)}, u32[]{:S(2)}) %collective-permute-start.15) | collective-permute-done | bytes 5767200 | tf_op jit(solution)/shard_map/ppermute | solution.py:55
  402.9 35.8 %units.3 = (bf16[2048,1408]{1,0:T(8,128)(2,1)}, bf16[2048,704]{1,0:T(8,128)(2,1)}, bf16[2048,2048]{1,0:T(8,128)(2,1)}, f32[16,1,128]{2,1,0:T(1,128)}) custom-call(s32[4]{0:T(128)} %pad_add_fusion.places_ref, bf16[2048,2048]{1,0:T(8,128)(2,1)} %all-gather.9.cloned.1.call-done.x_ref, f32[16,1,128]{2,1,0:T(1,128)} %all_to_all.37.info_ref, ...), custom_call_target="tpu_custom_call" | custom-call | tf_op jit(solution)/shard_map/units/pallas_call | solution.py:445
  440.0 6.2 all-to-all-start.3
  446.6 19.9 %rows.3 = bf16[2,2,4,128,2048]{4,3,2,1,0:T(8,128)(2,1)} custom-call(s32[4]{0:T(128)} %pad_add_fusion.places_ref, bf16[2048,704]{1,0:T(8,128)(2,1)} %get-tuple-element.84.refs_0_, bf16[2048,704]{1,0:T(8,128)(2,1)} %get-tuple-element.88.refs_1_, bf16[704,2048]{1,0:T(8,128)(2,1)} %bitcast.369, bf16[704,2048]{1,0:T(8,128)(2,1)} %collective-permute-done.refs_3_), custom_call_target="tpu_custom_call" | custom-call | flops 11811160064 | bytes 28311552 | tf_op jit(solution)/shard_map/rows/pallas_call | solution.py:445
  466.6 5.3 fusion.53
  475.3 10.3 %convolution_convert_fusion.3 = bf16[704,2048]{1,0:T(8,128)(2,1)} fusion(bf16[2048,704]{1,0:T(8,128)(2,1)S(1)} %copy-done.52, bf16[2048,2048]{1,0:T(8,128)(2,1)} %all-gather.5.cloned.1.call-done), kind=kOutput, calls=%fused_computation.18 | convolution fusion | flops 5907021824 | bytes 14155776 | tf_op jit(solution)/shard_map/tf,td->fd/dot_general | solution.py:149
  486.9 14.2 %convolution_convert_fusion = bf16[1408,2048]{1,0:T(8,128)(2,1)} fusion(bf16[2048,1408]{1,0:T(8,128)(2,1)S(1)} %bitcast.367, bf16[2048,2048]{1,0:T(8,128)(2,1)S(1)} %bitcast.323), kind=kOutput, calls=%fused_computation.5 | convolution fusion | flops 11814043648 | bytes 19922944 | tf_op jit(solution)/shard_map/tf,td->fd/dot_general | solution.py:149
  501.3 7.9 fusion
  509.1 41.5 %collective-permute-done.20 = bf16[704,2048]{1,0:T(8,128)(2,1)} collective-permute-done((bf16[704,2048]{1,0:T(8,128)(2,1)}, bf16[704,2048]{1,0:T(8,128)(2,1)}, u32[]{:S(2)}, u32[]{:S(2)}) %collective-permute-start.20) | collective-permute-done | bytes 2883616 | tf_op jit(solution)/shard_map/ppermute | solution.py:55
  555.7 3.8 collective-permute-start.17
  560.6 17.1 %collective-permute-done.17 = bf16[2,64,2048]{2,1,0:T(8,128)(2,1)S(1)} collective-permute-done((bf16[2,64,2048]{2,1,0:T(8,128)(2,1)S(1)}, bf16[2,64,2048]{2,1,0:T(8,128)(2,1)S(1)}, u32[]{:S(2)}, u32[]{:S(2)}) %collective-permute-start.17) | collective-permute-done | bytes 524320 | tf_op jit(solution)/shard_map/ppermute | solution.py:55
  578.9 4.3 collective-permute-start.18
  583.2 19.0 %fusion.65 = f32[1408,2048]{1,0:T(8,128)} fusion(bf16[2048,1408]{1,0:T(8,128)(2,1)} %get-tuple-element.122, bf16[2048,2048]{1,0:T(8,128)(2,1)} %all-gather.9.cloned.1.call-done.x_ref), kind=kOutput, calls=%fused_computation.209 | convolution fusion | flops 11811160064 | bytes 25690112 | tf_op jit(solution)/shard_map/tf,td->fd/dot_general | solution.py:149
  602.9 11.1 %add_bitcast_fusion = f32[1,704,2048]{2,1,0:T(8,128)} fusion(bf16[704,2048]{1,0:T(8,128)(2,1)} %collective-permute-done.20, bf16[2048,704]{1,0:T(8,128)(2,1)S(1)} %copy-done.51, bf16[2048,2048]{1,0:T(8,128)(2,1)} %all-gather.5.cloned.1.call-done), kind=kOutput, calls=%fused_computation.6 | convolution fusion | flops 5908463616 | bytes 19922944 | tf_op jit(solution)/shard_map/tf,td->fd/dot_general | solution.py:149
  614.3 18.5 %collective-permute-done.19 = bf16[2,64,2048]{2,1,0:T(8,128)(2,1)S(1)} collective-permute-done((bf16[2,64,2048]{2,1,0:T(8,128)(2,1)S(1)}, bf16[2,64,2048]{2,1,0:T(8,128)(2,1)S(1)}, u32[]{:S(2)}, u32[]{:S(2)}) %collective-permute-start.19) | collective-permute-done | bytes 524320 | tf_op jit(solution)/shard_map/ppermute | solution.py:55
  633.7 13.9 %all-gather.11.cloned.1.call-done.mid_ref = bf16[2048,2048]{1,0:T(8,128)(2,1)} async-done(((bf16[128,2048]{1,0:T(8,128)(2,1)}), bf16[2048,2048]{1,0:T(8,128)(2,1)}) %all-gather.11.cloned.1.call-update) | async-done | bytes 8388624 | tf_op jit(solution)/shard_map/all_gather | solution.py:141
  647.7 39.7 %attend_back.1 = (bf16[2048,512]{1,0:T(8,128)(2,1)}, bf16[2048,1024]{1,0:T(8,128)(2,1)}, bf16[2048,2048]{1,0:T(8,128)(2,1)}, f32[16,1,128]{2,1,0:T(1,128)}, f32[1,2048]{1,0:T(1,128)}) custom-call(s32[4]{0:T(128)} %pad_add_fusion.places_ref, bf16[2048,2048]{1,0:T(8,128)(2,1)} %all-gather.11.cloned.1.call-done.mid_ref, f32[16,2,128]{2,1,0:T(2,128)} %copy-done.35, ...), custom_call_target="tpu_custom_call" | custom-call | flops 18522046464 | bytes 46137344 | tf_op jit(solution)/shard_map/attend_back/pallas_call | solution.py:445
  687.4 7.5 all-to-all-start.4
  699.6 13.8 %fusion.60 = f32[2048,1024]{1,0:T(8,128)S(1)} fusion(bf16[2048,2048]{1,0:T(8,128)(2,1)} %all-gather.7.cloned.1.call-done.x_ref, bf16[2048,1024]{1,0:T(8,128)(2,1)} %get-tuple-element.105), kind=kOutput, calls=%fused_computation.204 | convolution fusion | flops 8589934592 | bytes 20971520 | tf_op jit(solution)/shard_map/td,tf->df/dot_general | solution.py:149
  713.4 3.3 copy-done.3
  718.4 14.1 %convert_add_fusion = f32[1408,2048]{1,0:T(8,128)} fusion(f32[1408,2048]{1,0:T(8,128)} %fusion.65, bf16[1408,2048]{1,0:T(8,128)(2,1)} %collective-permute-done.36), kind=kLoop, calls=%fused_computation | loop fusion | flops 5767168 | bytes 28835840 | tf_op jit(solution)/shard_map/add | solution.py:774
  732.4 10.8 %fusion.63 = f32[2048,512]{1,0:T(8,128)} fusion(bf16[2048,2048]{1,0:T(8,128)(2,1)} %all-gather.7.cloned.1.call-done.x_ref, bf16[2048,512]{1,0:T(8,128)(2,1)} %get-tuple-element.115), kind=kOutput, calls=%fused_computation.207 | convolution fusion | flops 4294967296 | bytes 14680064 | tf_op jit(solution)/shard_map/td,tf->df/dot_general | solution.py:149
  743.3 7.1 fusion.64
  767.9 3.8 collective-permute-start.22
  772.7 9.0 %collective-permute-done.22 = bf16[64,2048]{1,0:T(8,128)(2,1)S(1)} collective-permute-done((bf16[64,2048]{1,0:T(8,128)(2,1)S(1)}, bf16[64,2048]{1,0:T(8,128)(2,1)S(1)}, u32[]{:S(2)}, u32[]{:S(2)}) %collective-permute-start.22) | collective-permute-done | bytes 262176 | tf_op jit(solution)/shard_map/ppermute | solution.py:55
  781.8 4.3 collective-permute-start.23
  786.1 4.1 collective-permute-done.34
  791.8 5.1 all-to-all-start.6
  798.1 3.2 collective-permute-start.24
  801.3 5.8 bitcast_add_fusion
  808.4 3.3 collective-permute-done.35
  811.7 3.2 add_bitcast_fusion.1
  814.9 6.7 collective-permute-done.24
  822.8 6.1 collective-permute-done.27
  837.8 7.5 collective-permute-done.31
  854.4 4.3 all-to-all-start.5
  861.8 10.9 %all-to-all-done.5 = bf16[4,64,1024]{2,1,0:T(8,128)(2,1)} async-done(((bf16[4,64,1024]{2,1,0:T(8,128)(2,1)}), bf16[4,64,1024]{2,1,0:T(8,128)(2,1)}, u32[]{:S(2)}, u32[]{:S(2)}) %all-to-all-start.5) | async-done | bytes 524320 | tf_op jit(solution)/shard_map/all_to_all | solution.py:162
  882.2 3.0 fusion.14
  (305 shorter events, 120.6 us)
Async XLA Ops:
  7.2 275.2 %copy-start = (f32[2048,4]{0,1:T(4,128)S(1)}, f32[2048,4]{0,1:T(4,128)}, u32[]{:S(2)}) copy-start(f32[2048,4]{0,1:T(4,128)} %param.23) | copy-start | bytes 98308
  7.2 142.8 %all-gather.7.cloned.1.call-start = ((), (), s32[]{:S(2)}) async-start(), calls=%async_computation.10 | async-start | bytes 8912896 | tf_op jit(solution)/shard_map/all_gather | solution.py:141
  11.8 65.8 %collective-permute-start = (bf16[704,2048]{1,0:T(8,128)(2,1)}, bf16[704,2048]{1,0:T(8,128)(2,1)}, u32[]{:S(2)}, u32[]{:S(2)}) collective-permute-start(bf16[704,2048]{1,0:T(8,128)(2,1)} %bitcast.368), channel_id=1, source_target_pairs={{1,0},{0,1},{3,2},{2,3},{5,4},{4,5},{7,6},{6,7},{9,8},{8,9},{11,10... | collective-permute-start | bytes 8650760 | tf_op jit(solution)/shard_map/ppermute | solution.py:55
  17.4 60.3 %all-to-all-start = ((bf16[4,384,512]{2,1,0:T(8,128)(2,1)}), bf16[4,384,512]{2,1,0:T(8,128)(2,1)S(1)}, u32[]{:S(2)}, u32[]{:S(2)}) async-start(bf16[4,384,512]{2,1,0:T(8,128)(2,1)} %maximum_maximum_fusion), calls=%async_computation | async-start | bytes 3145728 | tf_op jit(solution)/shard_map/all_to_all | solution.py:162
  22.2 71.7 %copy-start.17 = (f32[128,2048]{1,0:T(8,128)S(1)}, f32[128,2048]{1,0:T(8,128)}, u32[]{:S(2)}) copy-start(f32[128,2048]{1,0:T(8,128)} %param.31) | copy-start | bytes 3145732
  22.2 209.4 %all-gather.5.cloned.1.call-start = ((), (), s32[]{:S(2)}) async-start(), calls=%async_computation.9 | async-start | bytes 8912896 | tf_op jit(solution)/shard_map/all_gather | solution.py:141
  77.7 13.2 %collective-permute-start.1 = (bf16[4,2,64,512]{3,2,1,0:T(8,128)(2,1)S(1)}, bf16[4,2,64,512]{3,2,1,0:T(8,128)(2,1)S(1)}, u32[]{:S(2)}, u32[]{:S(2)}) collective-permute-start(bf16[4,2,64,512]{3,2,1,0:T(8,128)(2,1)S(1)} %bitcast.341), channel_id=1, source_target_pairs={{1,0},{0,1},{3,2},{2,3},{5,4},{4,5},{7,6},{6,7},{9,8},{8,9},{11,10... | collective-permute-start | bytes 1572872 | tf_op jit(solution)/shard_map/ppermute | solution.py:55
  90.8 23.5 %collective-permute-start.2 = (bf16[4,256,512]{2,1,0:T(8,128)(2,1)S(1)}, bf16[4,256,512]{2,1,0:T(8,128)(2,1)S(1)}, u32[]{:S(2)}, u32[]{:S(2)}) collective-permute-start(bf16[4,256,512]{2,1,0:T(8,128)(2,1)S(1)} %slice.266), channel_id=1, source_target_pairs={{1,0},{0,1},{3,2},{2,3},{5,4},{4,5},{7,6},{6,7},{9,8},{8,9},{11,10... | collective-permute-start | bytes 3145736 | tf_op jit(solution)/shard_map/ppermute | solution.py:55
  92.4 29.3 %copy-start.20 = (bf16[2,4,2,64,512]{4,3,2,1,0:T(8,128)(2,1)}, bf16[2,4,2,64,512]{4,3,2,1,0:T(8,128)(2,1)S(1)}, u32[]{:S(2)}) copy-start(bf16[2,4,2,64,512]{4,3,2,1,0:T(8,128)(2,1)S(1)} %pad_maximum_fusion.4) | copy-start | bytes 3145732
  92.4 28.3 %collective-permute-start.3 = (bf16[2,4,2,64,512]{4,3,2,1,0:T(8,128)(2,1)S(1)}, bf16[2,4,2,64,512]{4,3,2,1,0:T(8,128)(2,1)S(1)}, u32[]{:S(2)}, u32[]{:S(2)}) collective-permute-start(bf16[2,4,2,64,512]{4,3,2,1,0:T(8,128)(2,1)S(1)} %pad_maximum_fusion.4), channel_id=1, source_target_pairs={{16,0},{0,16},{17,1},{1,17},{18,2},{2,18},{19,3},{3,19},{20,4},{4,... | collective-permute-start | bytes 3145736 | tf_op jit(solution)/shard_map/ppermute | solution.py:55
  124.9 13.6 %collective-permute-start.4 = (bf16[2,2,4,2,64,512]{5,4,3,2,1,0:T(8,128)(2,1)}, bf16[2,2,4,2,64,512]{5,4,3,2,1,0:T(8,128)(2,1)}, u32[]{:S(2)}, u32[]{:S(2)}) collective-permute-start(bf16[2,2,4,2,64,512]{5,4,3,2,1,0:T(8,128)(2,1)} %get-tuple-element.134), channel_id=1, source_target_pairs={{8,0},{0,8},{9,1},{1,9},{10,2},{2,10},{11,3},{3,11},{12,4},{4,12},... | collective-permute-start | bytes 6291464 | tf_op jit(solution)/shard_map/ppermute | solution.py:55
  126.8 23.2 %all-to-all-start.1 = ((f32[16,2,128]{2,1,0:T(2,128)}), f32[16,2,128]{2,1,0:T(2,128)S(1)}, u32[]{:S(2)}, u32[]{:S(2)}) async-start(f32[16,2,128]{2,1,0:T(2,128)} %pad_maximum_fusion.8), calls=%async_computation.1 | async-start | bytes 32768 | tf_op jit(solution)/shard_map/all_to_all | solution.py:131
  131.6 225.3 %all-gather.9.cloned.1.call-start = ((), (), s32[]{:S(2)}) async-start(), calls=%async_computation.11 | async-start | bytes 8912896 | tf_op jit(solution)/shard_map/all_gather | solution.py:141
  133.7 42.5 %collective-permute-start.5 = (bf16[256,2048]{1,0:T(8,128)(2,1)}, bf16[256,2048]{1,0:T(8,128)(2,1)S(1)}, u32[]{:S(2)}, u32[]{:S(2)}) collective-permute-start(bf16[256,2048]{1,0:T(8,128)(2,1)} %bitcast.343), channel_id=1, source_target_pairs={{1,0},{0,1},{3,2},{2,3},{5,4},{4,5},{7,6},{6,7},{9,8},{8,9},{11,10... | collective-permute-start | bytes 3145736 | tf_op jit(solution)/shard_map/ppermute | solution.py:55
  150.6 25.6 %copy-start.22 = (bf16[1,256,2048]{2,1,0:T(8,128)(2,1)S(1)}, bf16[1,256,2048]{2,1,0:T(8,128)(2,1)}, u32[]{:S(2)}) copy-start(bf16[1,256,2048]{2,1,0:T(8,128)(2,1)} %param.26) | copy-start | bytes 3145732
  191.5 7.8 collective-permute-start.6
  201.7 14.7 %collective-permute-start.11 = (bf16[2,64,2048]{2,1,0:T(8,128)(2,1)S(1)}, bf16[2,64,2048]{2,1,0:T(8,128)(2,1)S(1)}, u32[]{:S(2)}, u32[]{:S(2)}) collective-permute-start(bf16[2,64,2048]{2,1,0:T(8,128)(2,1)S(1)} %slice_bitcast_fusion.14), channel_id=1, source_target_pairs={{2,0},{4,2},{6,4},{0,6},{3,1},{5,3},{7,5},{1,7},{10,8},{12,10},{14... | collective-permute-start | bytes 1572872 | tf_op jit(solution)/shard_map/ppermute | solution.py:55
  205.0 41.7 %collective-permute-start.7 = (bf16[4,64,2048]{2,1,0:T(8,128)(2,1)S(1)}, bf16[4,64,2048]{2,1,0:T(8,128)(2,1)S(1)}, u32[]{:S(2)}, u32[]{:S(2)}) collective-permute-start(bf16[4,64,2048]{2,1,0:T(8,128)(2,1)S(1)} %slice_bitcast_fusion.6), channel_id=1, source_target_pairs={{16,0},{0,16},{17,1},{1,17},{18,2},{2,18},{19,3},{3,19},{20,4},{4,... | collective-permute-start | bytes 3145736 | tf_op jit(solution)/shard_map/ppermute | solution.py:55
  216.5 26.4 %collective-permute-start.12 = (bf16[2,64,2048]{2,1,0:T(8,128)(2,1)S(1)}, bf16[2,64,2048]{2,1,0:T(8,128)(2,1)S(1)}, u32[]{:S(2)}, u32[]{:S(2)}) collective-permute-start(bf16[2,64,2048]{2,1,0:T(8,128)(2,1)S(1)} %fusion.22), channel_id=1, source_target_pairs={{2,0},{4,2},{6,4},{0,6},{3,1},{5,3},{7,5},{1,7},{10,8},{12,10},{14... | collective-permute-start | bytes 1572872 | tf_op jit(solution)/shard_map/ppermute | solution.py:55
  243.0 23.5 %collective-permute-start.13 = (bf16[2,64,2048]{2,1,0:T(8,128)(2,1)S(1)}, bf16[2,64,2048]{2,1,0:T(8,128)(2,1)S(1)}, u32[]{:S(2)}, u32[]{:S(2)}) collective-permute-start(bf16[2,64,2048]{2,1,0:T(8,128)(2,1)S(1)} %fusion.21), channel_id=1, source_target_pairs={{2,0},{4,2},{6,4},{0,6},{3,1},{5,3},{7,5},{1,7},{10,8},{12,10},{14... | collective-permute-start | bytes 1572872 | tf_op jit(solution)/shard_map/ppermute | solution.py:55
  247.1 14.9 %collective-permute-start.8 = (bf16[64,2048]{1,0:T(8,128)(2,1)S(1)}, bf16[64,2048]{1,0:T(8,128)(2,1)S(1)}, u32[]{:S(2)}, u32[]{:S(2)}) collective-permute-start(bf16[64,2048]{1,0:T(8,128)(2,1)S(1)} %slice_bitcast_fusion.24), channel_id=1, source_target_pairs={{2,0},{4,2},{6,4},{0,6},{3,1},{5,3},{7,5},{1,7},{10,8},{12,10},{14... | collective-permute-start | bytes 786440 | tf_op jit(solution)/shard_map/ppermute | solution.py:55
  255.3 23.5 %copy-start.2 = (bf16[128,2048]{1,0:T(8,128)(2,1)S(1)}, bf16[128,2048]{1,0:T(8,128)(2,1)}, u32[]{:S(2)}) copy-start(bf16[128,2048]{1,0:T(8,128)(2,1)} %param.16) | copy-start | bytes 1572868
  255.3 23.5 %copy-start.27 = (f32[2048]{0:T(1024)S(1)}, f32[2048]{0:T(1024)}, u32[]{:S(2)}) copy-start(f32[2048]{0:T(1024)} %param.27) | copy-start | bytes 24580
  262.2 8.2 collective-permute-start.9
  266.7 8.1 collective-permute-start.14
  270.5 8.2 collective-permute-start.10
  280.2 270.4 %reduce-scatter.3.cloned.1.call-start = ((), (), s32[]{:S(2)}) async-start(), calls=%async_computation.12 | async-start | bytes 8912896 | tf_op jit(solution)/shard_map/reduce_scatter | solution.py:145
  280.3 122.6 %collective-permute-start.15 = (bf16[1408,2048]{1,0:T(8,128)(2,1)}, bf16[1408,2048]{1,0:T(8,128)(2,1)}, u32[]{:S(2)}, u32[]{:S(2)}) collective-permute-start(bf16[1408,2048]{1,0:T(8,128)(2,1)} %bitcast.324), channel_id=1, source_target_pairs={{1,0},{0,1},{3,2},{2,3},{5,4},{4,5},{7,6},{6,7},{9,8},{8,9},{11,10... | collective-permute-start | bytes 17301512 | tf_op jit(solution)/shard_map/ppermute | solution.py:55
  440.0 61.2 %all-to-all-start.3 = ((f32[16,1,128]{2,1,0:T(1,128)}), f32[16,1,128]{2,1,0:T(1,128)S(1)}, u32[]{:S(2)}, u32[]{:S(2)}) async-start(f32[16,1,128]{2,1,0:T(1,128)} %add.174), calls=%async_computation.4 | async-start | bytes 16384 | tf_op jit(solution)/shard_map/all_to_all | solution.py:135
  446.2 201.5 %all-gather.11.cloned.1.call-start = ((), (), s32[]{:S(2)}) async-start(), calls=%async_computation.13 | async-start | bytes 8912896 | tf_op jit(solution)/shard_map/all_gather | solution.py:141
  474.3 27.0 %collective-permute-start.16 = (bf16[2,4,128,2048]{3,2,0,1:T(8,128)(2,1)}, bf16[2,4,128,2048]{3,2,0,1:T(8,128)(2,1)}, u32[]{:S(2)}, u32[]{:S(2)}) collective-permute-start(bf16[2,4,128,2048]{3,2,0,1:T(8,128)(2,1)} %bitcast.320), channel_id=1, source_target_pairs={{8,0},{0,8},{9,1},{1,9},{10,2},{2,10},{11,3},{3,11},{12,4},{4,12},... | collective-permute-start | bytes 12582920 | tf_op jit(solution)/shard_map/ppermute | solution.py:55
  485.6 65.0 %collective-permute-start.20 = (bf16[704,2048]{1,0:T(8,128)(2,1)}, bf16[704,2048]{1,0:T(8,128)(2,1)}, u32[]{:S(2)}, u32[]{:S(2)}) collective-permute-start(bf16[704,2048]{1,0:T(8,128)(2,1)} %convolution_convert_fusion.3), channel_id=1, source_target_pairs={{1,0},{0,1},{3,2},{2,3},{5,4},{4,5},{7,6},{6,7},{9,8},{8,9},{11,10... | collective-permute-start | bytes 8650760 | tf_op jit(solution)/shard_map/ppermute | solution.py:55
  509.1 44.0 %copy-start.18 = (f32[128,2048]{1,0:T(8,128)S(1)}, f32[128,2048]{1,0:T(8,128)}, u32[]{:S(2)}) copy-start(f32[128,2048]{1,0:T(8,128)} %param.31) | copy-start | bytes 3145732
  553.6 48.6 %copy-start.10 = (f32[128,2048]{1,0:T(8,128)}, f32[128,2048]{1,0:T(8,128)S(1)}, u32[]{:S(2)}) copy-start(f32[128,2048]{1,0:T(8,128)S(1)} %get-tuple-element.126) | copy-start | bytes 3145732
  554.6 325.9 %reduce-scatter.5.cloned.1.call-start = ((), (), s32[]{:S(2)}) async-start(), calls=%async_computation.14 | async-start | bytes 8912896 | tf_op jit(solution)/shard_map/reduce_scatter | solution.py:145
  555.7 22.0 %collective-permute-start.17 = (bf16[2,64,2048]{2,1,0:T(8,128)(2,1)S(1)}, bf16[2,64,2048]{2,1,0:T(8,128)(2,1)S(1)}, u32[]{:S(2)}, u32[]{:S(2)}) collective-permute-start(bf16[2,64,2048]{2,1,0:T(8,128)(2,1)S(1)} %slice_bitcast_fusion.10), channel_id=1, source_target_pairs={{2,0},{4,2},{6,4},{0,6},{3,1},{5,3},{7,5},{1,7},{10,8},{12,10},{14... | collective-permute-start | bytes 1572872 | tf_op jit(solution)/shard_map/ppermute | solution.py:55
  559.5 158.8 %collective-permute-start.36 = (bf16[1408,2048]{1,0:T(8,128)(2,1)}, bf16[1408,2048]{1,0:T(8,128)(2,1)}, u32[]{:S(2)}, u32[]{:S(2)}) collective-permute-start(bf16[1408,2048]{1,0:T(8,128)(2,1)} %convolution_convert_fusion), channel_id=1, source_target_pairs={{1,0},{0,1},{3,2},{2,3},{5,4},{4,5},{7,6},{6,7},{9,8},{8,9},{11,10... | collective-permute-start | bytes 17301512 | tf_op jit(solution)/shard_map/ppermute | solution.py:55
  578.9 23.7 %collective-permute-start.18 = (bf16[2,64,2048]{2,1,0:T(8,128)(2,1)S(1)}, bf16[2,64,2048]{2,1,0:T(8,128)(2,1)S(1)}, u32[]{:S(2)}, u32[]{:S(2)}) collective-permute-start(bf16[2,64,2048]{2,1,0:T(8,128)(2,1)S(1)} %fusion.19), channel_id=1, source_target_pairs={{2,0},{4,2},{6,4},{0,6},{3,1},{5,3},{7,5},{1,7},{10,8},{12,10},{14... | collective-permute-start | bytes 1572872 | tf_op jit(solution)/shard_map/ppermute | solution.py:55
  583.2 19.3 %copy-start.6 = (bf16[2,4,128,2048]{3,2,0,1:T(8,128)(2,1)S(1)}, bf16[2,4,128,2048]{3,2,0,1:T(8,128)(2,1)}, u32[]{:S(2)}) copy-start(bf16[2,4,128,2048]{3,2,0,1:T(8,128)(2,1)} %fusion) | copy-start | bytes 12582916
  583.2 19.7 %copy-start.51 = (bf16[2048,704]{1,0:T(8,128)(2,1)S(1)}, bf16[2048,704]{1,0:T(8,128)(2,1)}, u32[]{:S(2)}) copy-start(bf16[2048,704]{1,0:T(8,128)(2,1)} %get-tuple-element.84.refs_0_) | copy-start | bytes 8650756
  602.7 30.1 %collective-permute-start.19 = (bf16[2,64,2048]{2,1,0:T(8,128)(2,1)S(1)}, bf16[2,64,2048]{2,1,0:T(8,128)(2,1)S(1)}, u32[]{:S(2)}, u32[]{:S(2)}) collective-permute-start(bf16[2,64,2048]{2,1,0:T(8,128)(2,1)S(1)} %fusion.18), channel_id=1, source_target_pairs={{2,0},{4,2},{6,4},{0,6},{3,1},{5,3},{7,5},{1,7},{10,8},{12,10},{14... | collective-permute-start | bytes 1572872 | tf_op jit(solution)/shard_map/ppermute | solution.py:55
  687.4 66.3 %all-to-all-start.4 = ((f32[16,1,128]{2,1,0:T(1,128)}), f32[16,1,128]{2,1,0:T(1,128)S(1)}, u32[]{:S(2)}, u32[]{:S(2)}) async-start(f32[16,1,128]{2,1,0:T(1,128)} %get-tuple-element.108), calls=%async_computation.5 | async-start | bytes 16384 | tf_op jit(solution)/shard_map/all_to_all | solution.py:135
  696.6 75.1 %collective-permute-start.25 = (bf16[64,2048]{1,0:T(8,128)(2,1)}, bf16[64,2048]{1,0:T(8,128)(2,1)}, u32[]{:S(2)}, u32[]{:S(2)}) collective-permute-start(bf16[64,2048]{1,0:T(8,128)(2,1)} %slice_bitcast_fusion.29), channel_id=1, source_target_pairs={{16,0},{0,16},{17,1},{1,17},{18,2},{2,18},{19,3},{3,19},{20,4},{4,... | collective-permute-start | bytes 786440 | tf_op jit(solution)/shard_map/ppermute | solution.py:55
  699.6 66.6 %collective-permute-start.21 = (bf16[4,64,2048]{2,1,0:T(8,128)(2,1)}, bf16[4,64,2048]{2,1,0:T(8,128)(2,1)}, u32[]{:S(2)}, u32[]{:S(2)}) collective-permute-start(bf16[4,64,2048]{2,1,0:T(8,128)(2,1)} %slice_bitcast_fusion.4), channel_id=1, source_target_pairs={{16,0},{0,16},{17,1},{1,17},{18,2},{2,18},{19,3},{3,19},{20,4},{4,... | collective-permute-start | bytes 3145736 | tf_op jit(solution)/shard_map/ppermute | solution.py:55
  718.4 82.9 %collective-permute-start.26 = (bf16[2,512,1024]{2,1,0:T(8,128)(2,1)}, bf16[2,512,1024]{2,1,0:T(8,128)(2,1)}, u32[]{:S(2)}, u32[]{:S(2)}) collective-permute-start(bf16[2,512,1024]{2,1,0:T(8,128)(2,1)} %fusion.2), channel_id=1, source_target_pairs={{0,8},{8,0},{1,9},{9,1},{2,10},{10,2},{3,11},{11,3},{4,12},{12,4},... | collective-permute-start | bytes 6291464 | tf_op jit(solution)/shard_map/ppermute | solution.py:199
  757.5 6.0 collective-permute-start.28
  761.3 28.9 %copy-start.7 = (f32[2048,512]{1,0:T(8,128)S(1)}, f32[2048,512]{1,0:T(8,128)}, u32[]{:S(2)}) copy-start(f32[2048,512]{1,0:T(8,128)} %fusion.63) | copy-start | bytes 12582916
  764.2 26.0 %collective-permute-start.34 = (bf16[4,256,512]{2,1,0:T(8,128)(2,1)S(1)}, bf16[4,256,512]{2,1,0:T(8,128)(2,1)S(1)}, u32[]{:S(2)}, u32[]{:S(2)}) collective-permute-start(bf16[4,256,512]{2,1,0:T(8,128)(2,1)S(1)} %select_bitcast_fusion), channel_id=1, source_target_pairs={{1,0},{0,1},{3,2},{2,3},{5,4},{4,5},{7,6},{6,7},{9,8},{8,9},{11,10... | collective-permute-start | bytes 3145736 | tf_op jit(solution)/shard_map/ppermute | solution.py:55
  765.4 46.3 %collective-permute-start.35 = (bf16[256,2048]{1,0:T(8,128)(2,1)}, bf16[256,2048]{1,0:T(8,128)(2,1)}, u32[]{:S(2)}, u32[]{:S(2)}) collective-permute-start(bf16[256,2048]{1,0:T(8,128)(2,1)} %slice_select_fusion), channel_id=1, source_target_pairs={{1,0},{0,1},{3,2},{2,3},{5,4},{4,5},{7,6},{6,7},{9,8},{8,9},{11,10... | collective-permute-start | bytes 3145736 | tf_op jit(solution)/shard_map/ppermute | solution.py:55
  767.9 13.8 %collective-permute-start.22 = (bf16[64,2048]{1,0:T(8,128)(2,1)S(1)}, bf16[64,2048]{1,0:T(8,128)(2,1)S(1)}, u32[]{:S(2)}, u32[]{:S(2)}) collective-permute-start(bf16[64,2048]{1,0:T(8,128)(2,1)S(1)} %slice_bitcast_fusion.18), channel_id=1, source_target_pairs={{2,0},{4,2},{6,4},{0,6},{3,1},{5,3},{7,5},{1,7},{10,8},{12,10},{14... | collective-permute-start | bytes 786440 | tf_op jit(solution)/shard_map/ppermute | solution.py:55
  781.8 16.2 %collective-permute-start.23 = (bf16[64,2048]{1,0:T(8,128)(2,1)S(1)}, bf16[64,2048]{1,0:T(8,128)(2,1)S(1)}, u32[]{:S(2)}, u32[]{:S(2)}) collective-permute-start(bf16[64,2048]{1,0:T(8,128)(2,1)S(1)} %fusion.28), channel_id=1, source_target_pairs={{2,0},{4,2},{6,4},{0,6},{3,1},{5,3},{7,5},{1,7},{10,8},{12,10},{14... | collective-permute-start | bytes 786440 | tf_op jit(solution)/shard_map/ppermute | solution.py:55
  791.8 44.8 %all-to-all-start.6 = ((bf16[4,256,512]{2,1,0:T(8,128)(2,1)}), bf16[4,256,512]{2,1,0:T(8,128)(2,1)}, u32[]{:S(2)}, u32[]{:S(2)}) async-start(bf16[4,256,512]{2,1,0:T(8,128)(2,1)} %fusion.5), calls=%async_computation.8 | async-start | bytes 2097152 | tf_op jit(solution)/shard_map/all_to_all | solution.py:162
  798.1 23.5 %collective-permute-start.24 = (bf16[64,2048]{1,0:T(8,128)(2,1)S(1)}, bf16[64,2048]{1,0:T(8,128)(2,1)S(1)}, u32[]{:S(2)}, u32[]{:S(2)}) collective-permute-start(bf16[64,2048]{1,0:T(8,128)(2,1)S(1)} %fusion.27), channel_id=1, source_target_pairs={{2,0},{4,2},{6,4},{0,6},{3,1},{5,3},{7,5},{1,7},{10,8},{12,10},{14... | collective-permute-start | bytes 786440 | tf_op jit(solution)/shard_map/ppermute | solution.py:55
  807.3 21.6 %collective-permute-start.27 = (bf16[4,2,64,1024]{3,2,1,0:T(8,128)(2,1)S(1)}, bf16[4,2,64,1024]{3,2,1,0:T(8,128)(2,1)S(1)}, u32[]{:S(2)}, u32[]{:S(2)}) collective-permute-start(bf16[4,2,64,1024]{3,2,1,0:T(8,128)(2,1)S(1)} %bitcast.346), channel_id=1, source_target_pairs={{16,0},{0,16},{17,1},{1,17},{18,2},{2,18},{19,3},{3,19},{20,4},{4,... | collective-permute-start | bytes 3145736 | tf_op jit(solution)/shard_map/ppermute | solution.py:55
  828.9 1.3 collective-permute-start.29
  830.3 5.6 collective-permute-start.30
  831.9 20.4 %collective-permute-start.33 = (bf16[4,64,1024]{2,1,0:T(8,128)(2,1)}, bf16[4,64,1024]{2,1,0:T(8,128)(2,1)}, u32[]{:S(2)}, u32[]{:S(2)}) collective-permute-start(bf16[4,64,1024]{2,1,0:T(8,128)(2,1)} %fusion.24), channel_id=1, source_target_pairs={{1,0},{0,1},{3,2},{2,3},{5,4},{4,5},{7,6},{6,7},{9,8},{8,9},{11,10... | collective-permute-start | bytes 1572872 | tf_op jit(solution)/shard_map/ppermute | solution.py:55
  836.6 8.7 collective-permute-start.31
  846.3 5.3 collective-permute-start.32
  854.4 27.8 %copy-start.11 = (f32[128,2048]{1,0:T(8,128)S(1)}, f32[128,2048]{1,0:T(8,128)}, u32[]{:S(2)}) copy-start(f32[128,2048]{1,0:T(8,128)} %copy-done.10) | copy-start | bytes 3145732
  854.4 27.8 %copy-start.12 = (f32[128,2048]{1,0:T(8,128)S(1)}, f32[128,2048]{1,0:T(8,128)}, u32[]{:S(2)}) copy-start(f32[128,2048]{1,0:T(8,128)} %get-tuple-element.172) | copy-start | bytes 3145732
  854.4 27.8 %copy-start.41 = (f32[2048]{0:T(1024)S(1)}, f32[2048]{0:T(1024)}, u32[]{:S(2)}) copy-start(f32[2048]{0:T(1024)} %param.30) | copy-start | bytes 24580
  854.4 27.8 %copy-start.49 = (f32[128]{0:T(128)S(1)}, f32[128]{0:T(128)}, u32[]{:S(2)}) copy-start(f32[128]{0:T(128)} %get-tuple-element.163) | copy-start | bytes 1540
  854.4 18.3 %all-to-all-start.5 = ((bf16[4,64,1024]{2,1,0:T(8,128)(2,1)}), bf16[4,64,1024]{2,1,0:T(8,128)(2,1)}, u32[]{:S(2)}, u32[]{:S(2)}) async-start(bf16[4,64,1024]{2,1,0:T(8,128)(2,1)} %fusion.23), calls=%async_computation.7 | async-start | bytes 1048576 | tf_op jit(solution)/shard_map/all_to_all | solution.py:162
  (45 other events, 320.2 us)
Sparse Core Ops, SparseCore 0:
  11.9 106.4 all-gather.6
  121.8 78.0 all-gather.4
  280.3 76.5 all-gather.8
  438.9 105.6 reduce-scatter.2
  554.7 92.9 all-gather.10
  687.5 115.3 reduce-scatter.4

commit v10 on v9

--- a/solution.py
+++ b/solution.py
@@ -71,7 +71,7 @@
     size = lax.axis_size(axis)
     travelling = blocks[1].astype(BF16)
     for j in range(2, size):
-        travelling = (shift(travelling, axis).astype(F32) + blocks[j]).astype(BF16)
+        travelling = (shift(travelling, axis).astype(F32) + blocks[j].astype(F32)).astype(BF16)
     return blocks[0], shift(travelling, axis)
 
 
@@ -200,7 +200,9 @@
     high, inner = lax.axis_size("y"), lax.axis_size("i")
     wide = kept.shape[-1]
     mine = mine.reshape(high, OUTER, inner, -1, wide)
-    own, arrived = ring_open(from_order([mine[k] for k in range(high)], "y"), "y")
+    blocks = from_order([mine[k] for k in range(high)], "y")
+    sent = blocks[1].astype(BF16)
+    own, arrived = ring_open([blocks[0], sent] + blocks[2:], "y")
     mine = arrived.astype(F32) + own
     mine = ring_scatter(from_order([mine[:, k] for k in range(inner)], "i"), "i").astype(BF16)
     here = exchange(mine)
@@ -208,7 +210,7 @@
     whole = jnp.concatenate(
         [join_blocks(here[:, :, :half]), join_blocks(here[:, :, half:])], axis=1
     )
-    return whole.astype(F32), arrived
+    return whole.astype(F32), sent, arrived
 
 
 def own_places():
@@ -219,14 +221,11 @@
     return (first.astype(F32) + second.astype(F32)).astype(BF16)
 
 
-def ring_low(blocks, axis, *others):
+def ring_low(blocks, axis):
     travelling = blocks[1]
     for j in range(2, lax.axis_size(axis)):
         travelling = add_low(shift(travelling, axis), blocks[j])
-    arrived = shift(travelling, axis)
-    if others:
-        arrived = after(arrived, *others)
-    return add_low(arrived, blocks[0])
+    return add_low(shift(travelling, axis), blocks[0])
 
 
 def part_low(rows):
@@ -697,7 +696,7 @@
     normed_two, inverse_two = norm_rows(middle, norm_gain2)
     mlp_input = normed_two.astype(BF16)
     mlp_gate, mlp_onehot = pair_gates(mlp_input, mlp_router, mlp_route, experts)
-    up_parts = ring_gather(after(own_up, branch), "i")
+    up_parts = ring_gather(after(own_up, gated), "i")
     all_mlp = meet(mlp_input)
     gate_m = to_experts(mlp_gate, mlp_onehot, None)
     d_both, gated_units, rows_back, d_gate_m = [], [], None, None
@@ -751,15 +750,14 @@
     )
     rows_first = after(rows_first, all_mid)
     rows_first = [rows_first[k] for k in range(rows_first.shape[0])]
-    rows_out = part_second(ring_low(rows_first, "y", d_heads), after(rows_second, d_heads))
-    layer_out = middle + rows_out.astype(F32) + mlp_bias
-    d_attn_input = part(rows_one)
+    rows_first = ring_low(rows_first, "y")
+    d_attn_input = part(after(rows_one, rows_first))
     d_att_gate = from_experts(d_gate_a[:, 0], att_onehot, experts)
     d_kv_mat = mm("td,tf->df", all_attn, d_kv).reshape(experts // 2, 2, -1, 2 * span)
     d_kv_mat = from_order([d_kv_mat[:, 0], d_kv_mat[:, 1]], "c")
     d_kv_sent = d_kv_mat[1].astype(BF16)
-    d_heads, all_mid = after((d_heads, all_mid), d_kv_sent)
-    d_kv_weight, kv_arrived = scatter_kv(d_kv_mat[0], d_kv_sent)
+    d_kv_weight, kv_sent, kv_arrived = scatter_kv(d_kv_mat[0], d_kv_sent)
+    d_heads, all_mid = after((d_heads, all_mid), kv_sent)
     d_att_router, d_att_from_router = gates_back(
         att_gate, att_onehot, d_att_gate, attn_input, att_router
     )
@@ -770,8 +768,10 @@
     d_query = scatter_query(mm("td,tf->df", all_attn, d_heads), summed)[None]
     d_out = mm("tf,td->fd", gated, all_mid).reshape(inner, -1, width)
     d_out = from_order([d_out[k] for k in range(inner)], "i")
-    d_output = ring_scatter(d_out[:1] + list(after(d_out[1:], summed)), "i")[None]
-    d_upper = (after(upper_last, d_kv_sent).astype(F32) + upper_own).reshape(up_weight.shape)
+    d_output = ring_scatter(d_out[:1] + list(after(d_out[1:], kv_arrived)), "i")[None]
+    rows_out = part_second(*after((rows_first, rows_second), kv_sent))
+    layer_out = middle + rows_out.astype(F32) + mlp_bias
+    d_upper = (after(upper_last, kv_sent).astype(F32) + upper_own).reshape(up_weight.shape)
     d_lower = (lower_last.astype(F32) + lower_own)[None]
     summed = sum_over(after(summed, kv_arrived), ("c", "o", "y"))
     d_attn_input = after(d_attn_input, summed)

time: 892 us -> 898 us (level)
  starting transfers between devices: 113 us -> 99.9 us
  waiting for transfers between devices: 340 us -> 352 us
    ppermute x31, starting transfers between devices: 75.5 us -> 59.9 us  [shift(): return lax.ppermute(value, axis, [((k + 1) % size, k) for k in range(size)])]
    ppermute x31, waiting for transfers between devices: 239 us -> 250 us  [shift(): return lax.ppermute(value, axis, [((k + 1) % size, k) for k in range(size)])]
    ppermute x5, waiting for transfers between devices: 15.4 us -> 6.23 us  [sum_over(): lax.ppermute(value, axis, [(k, k ^ step) for k in range(size)])]
    unnamed x129 -> x135, local copies, waits for them, and re-layouts: 18.5 us -> 18.5 us
  transfers between devices with their start and end apart: 49 -> 49, of which waited for: 27 -> 24; matrix products, arithmetic and copies ran while one was open for 24% -> 24% of each run, Pallas kernels for 15% -> 15%
where the time goes in v10:
time: 898 us; the launch traced here: 894 us
  waiting for transfers between devices  352 us (39%)
  Pallas kernels  173 us (19%)
  matrix products  109 us (12%)
  starting transfers between devices  99.9 us (11%)
  other arithmetic  87.9 us (10%)
  local copies, waits for them, and re-layouts  44.5 us (5%)
  between operations  15.4 us (2%)
  blocking collectives  11.9 us (1%)
    ppermute x31, waiting for transfers between devices, shift(): return lax.ppermute(value, axis, [((k + 1) % size, k) for k in range(size)])  250 us
    pallas_call x7, Pallas kernels, call(): pl.pallas_call(kernel, grid_spec=pltpu.PrefetchScalarGridSpec(num_scalar_...  173 us
    dot_general x9, matrix products, mm(): return jnp.einsum(form, first, second, preferred_element_type=F32)  102 us
    all_gather x4, waiting for transfers between devices, meet(): return lax.all_gather(rows, GROUP, axis=0, tiled=True)  78.9 us
    ppermute x31, starting transfers between devices, shift(): return lax.ppermute(value, axis, [((k + 1) % size, k) for k in range(size)])  59.9 us
    convert_element_type x18, other arithmetic, add_low(): return (first.astype(F32) + second.astype(F32)).astype(BF16)  19 us
    unnamed x135, local copies, waits for them, and re-layouts  18.5 us
  transfers between devices with their start and end apart: 49, of which 24 were waited for; matrix products, arithmetic and copies ran while one was open for 24% of the time, Pallas kernels for 15%

profile of v10, /device:TPU:0, one launch (start us, length us, event | category | flops | bytes accessed | tf_op | source)
XLA Modules:
  0.0 893.7 jit_solution(15278024731780500493)
XLA Ops:
  11.8 3.0 collective-permute-start
  17.3 4.9 all-to-all-start
  22.2 55.4 %collective-permute-done.refs_3_ = bf16[704,2048]{1,0:T(8,128)(2,1)} collective-permute-done((bf16[704,2048]{1,0:T(8,128)(2,1)}, bf16[704,2048]{1,0:T(8,128)(2,1)}, u32[]{:S(2)}, u32[]{:S(2)}) %collective-permute-start) | collective-permute-done | bytes 2883616 | tf_op jit(solution)/shard_map/ppermute | solution.py:55
  79.5 11.3 %collective-permute-done.1 = bf16[4,2,64,512]{3,2,1,0:T(8,128)(2,1)S(1)} collective-permute-done((bf16[4,2,64,512]{3,2,1,0:T(8,128)(2,1)S(1)}, bf16[4,2,64,512]{3,2,1,0:T(8,128)(2,1)S(1)}, u32[]{:S(2)}, u32[]{:S(2)}) %collective-permute-start.1) | collective-permute-done | bytes 524320 | tf_op jit(solution)/shard_map/ppermute | solution.py:55
  95.4 18.9 %collective-permute-done.2 = bf16[4,256,512]{2,1,0:T(8,128)(2,1)S(1)} collective-permute-done((bf16[4,256,512]{2,1,0:T(8,128)(2,1)S(1)}, bf16[4,256,512]{2,1,0:T(8,128)(2,1)S(1)}, u32[]{:S(2)}, u32[]{:S(2)}) %collective-permute-start.2) | collective-permute-done | bytes 1048608 | tf_op jit(solution)/shard_map/ppermute | solution.py:55
  114.3 6.3 collective-permute-done.3
  121.7 3.2 fusion.51
  126.7 4.8 all-to-all-start.1
  138.4 4.0 pad_maximum_fusion.in_ref
  142.4 7.3 arrange.1
  150.3 25.6 %attend.1 = (bf16[2048,1536]{1,0:T(8,128)(2,1)}, bf16[2048,512]{1,0:T(8,128)(2,1)}) custom-call(s32[4]{0:T(128)} %pad_add_fusion.places_ref, bf16[2048,2048]{1,0:T(8,128)(2,1)} %all-gather.7.cloned.1.call-done.x_ref, f32[16,2,128]{2,1,0:T(2,128)} %copy-done.36, f32[128,128]{1,0:T(8,128)} %get-tuple-element.175.cos_ref, ...), custom_call_target="tpu_custom_call" | custom-call | flops 13421772800 | bytes 25165824 | tf_op jit(solution)/shard_map/attend/pallas_call | solution.py:444
  177.6 9.2 %rows.2 = bf16[2,2,4,128,2048]{4,3,2,1,0:T(8,128)(2,1)} custom-call(s32[4]{0:T(128)} %pad_add_fusion.places_ref, bf16[2048,512]{1,0:T(8,128)(2,1)} %get-tuple-element.79.refs_0_, bf16[512,2048]{1,0:T(8,128)(2,1)} %bitcast.333), custom_call_target="tpu_custom_call" | custom-call | flops 4294967296 | bytes 20971520 | tf_op jit(solution)/shard_map/rows/pallas_call | solution.py:444
  186.7 3.9 fusion.54
  191.5 7.0 collective-permute-done.6
  200.8 3.8 collective-permute-start.11
  206.7 9.4 %collective-permute-done.11 = bf16[2,64,2048]{2,1,0:T(8,128)(2,1)S(1)} collective-permute-done((bf16[2,64,2048]{2,1,0:T(8,128)(2,1)S(1)}, bf16[2,64,2048]{2,1,0:T(8,128)(2,1)S(1)}, u32[]{:S(2)}, u32[]{:S(2)}) %collective-permute-start.11) | collective-permute-done | bytes 524320 | tf_op jit(solution)/shard_map/ppermute | solution.py:55
  216.3 4.9 collective-permute-start.12
  221.2 11.3 %convolution_convert_fusion.1.d_units_ref = bf16[2048,704]{1,0:T(8,128)(2,1)} fusion(bf16[2048,2048]{1,0:T(8,128)(2,1)} %all-gather.5.cloned.1.call-done, bf16[704,2048]{1,0:T(8,128)(2,1)} %collective-permute-done.refs_3_), kind=kOutput, calls=%fused_computation.16 | convolution fusion | flops 5907021824 | bytes 14155776 | tf_op jit(solution)/shard_map/td,fd->tf/dot_general | solution.py:149
  232.6 3.8 collective-permute-start.13
  236.9 8.1 convolution_convert_fusion.2.d_units_ref
  245.0 6.8 collective-permute-done.8
  251.9 4.3 collective-permute-start.9
  260.2 4.3 collective-permute-start.10
  264.6 3.8 collective-permute-done.10
  273.1 11.9 %all_to_all.37.info_ref = f32[16,1,128]{2,1,0:T(1,128)} all-to-all(f32[16,1,128]{2,1,0:T(1,128)S(1)} %bitcast.346), channel_id=1, replica_groups=mesh['y'=2,'c'=2,'o'=4,'i'=2] {'y','c','o'}, dimensions={0} | all-to-all | bytes 16384 | tf_op jit(solution)/shard_map/all_to_all | solution.py:131
  285.0 61.3 %all-gather.9.cloned.1.call-done.x_ref = bf16[2048,2048]{1,0:T(8,128)(2,1)} async-done(((bf16[128,2048]{1,0:T(8,128)(2,1)}), bf16[2048,2048]{1,0:T(8,128)(2,1)}) %all-gather.9.cloned.1.call-update) | async-done | bytes 8388624 | tf_op jit(solution)/shard_map/all_gather | solution.py:141
  346.3 35.5 %units.2 = (bf16[2048,1408]{1,0:T(8,128)(2,1)}, bf16[2048,704]{1,0:T(8,128)(2,1)}, f32[2048,2048]{1,0:T(8,128)}, f32[16,1,128]{2,1,0:T(1,128)}) custom-call(s32[4]{0:T(128)} %pad_add_fusion.places_ref, bf16[2048,2048]{1,0:T(8,128)(2,1)} %all-gather.9.cloned.1.call-done.x_ref, f32[16,1,128]{2,1,0:T(1,128)} %all_to_all.37.info_ref, ...), custom_call_target="tpu_custom_call" | custom-call | tf_op jit(solution)/shard_map/units/pallas_call | solution.py:444
  381.8 10.3 %collective-permute-done.15.first_ref.second_ref = bf16[1408,2048]{1,0:T(8,128)(2,1)} collective-permute-done((bf16[1408,2048]{1,0:T(8,128)(2,1)}, bf16[1408,2048]{1,0:T(8,128)(2,1)}, u32[]{:S(2)}, u32[]{:S(2)}) %collective-permute-start.15) | collective-permute-done | bytes 5767200 | tf_op jit(solution)/shard_map/ppermute | solution.py:55
  392.1 35.8 %units.3 = (bf16[2048,1408]{1,0:T(8,128)(2,1)}, bf16[2048,704]{1,0:T(8,128)(2,1)}, bf16[2048,2048]{1,0:T(8,128)(2,1)}, f32[16,1,128]{2,1,0:T(1,128)}) custom-call(s32[4]{0:T(128)} %pad_add_fusion.places_ref, bf16[2048,2048]{1,0:T(8,128)(2,1)} %all-gather.9.cloned.1.call-done.x_ref, f32[16,1,128]{2,1,0:T(1,128)} %all_to_all.37.info_ref, ...), custom_call_target="tpu_custom_call" | custom-call | tf_op jit(solution)/shard_map/units/pallas_call | solution.py:444
  429.2 6.5 all-to-all-start.3
  436.0 19.9 %rows.3 = bf16[2,2,4,128,2048]{4,3,2,1,0:T(8,128)(2,1)} custom-call(s32[4]{0:T(128)} %pad_add_fusion.places_ref, bf16[2048,704]{1,0:T(8,128)(2,1)} %get-tuple-element.85.refs_0_, bf16[2048,704]{1,0:T(8,128)(2,1)} %get-tuple-element.89.refs_1_, bf16[704,2048]{1,0:T(8,128)(2,1)} %bitcast.364, bf16[704,2048]{1,0:T(8,128)(2,1)} %collective-permute-done.refs_3_), custom_call_target="tpu_custom_call" | custom-call | flops 11811160064 | bytes 28311552 | tf_op jit(solution)/shard_map/rows/pallas_call | solution.py:444
  455.9 5.3 fusion.53
  464.6 10.2 %convolution_convert_fusion.3 = bf16[704,2048]{1,0:T(8,128)(2,1)} fusion(bf16[2048,704]{1,0:T(8,128)(2,1)S(1)} %copy-done.52, bf16[2048,2048]{1,0:T(8,128)(2,1)} %all-gather.5.cloned.1.call-done), kind=kOutput, calls=%fused_computation.18 | convolution fusion | flops 5907021824 | bytes 14155776 | tf_op jit(solution)/shard_map/tf,td->fd/dot_general | solution.py:149
  475.6 14.2 %convolution_convert_fusion = bf16[1408,2048]{1,0:T(8,128)(2,1)} fusion(bf16[2048,1408]{1,0:T(8,128)(2,1)S(1)} %bitcast.362, bf16[2048,2048]{1,0:T(8,128)(2,1)S(1)} %bitcast.317), kind=kOutput, calls=%fused_computation.5 | convolution fusion | flops 11814043648 | bytes 19922944 | tf_op jit(solution)/shard_map/tf,td->fd/dot_general | solution.py:149
  489.9 7.9 fusion
  497.8 42.0 %collective-permute-done.20 = bf16[704,2048]{1,0:T(8,128)(2,1)} collective-permute-done((bf16[704,2048]{1,0:T(8,128)(2,1)}, bf16[704,2048]{1,0:T(8,128)(2,1)}, u32[]{:S(2)}, u32[]{:S(2)}) %collective-permute-start.20) | collective-permute-done | bytes 2883616 | tf_op jit(solution)/shard_map/ppermute | solution.py:55
  544.8 4.0 collective-permute-start.17
  548.8 19.0 %collective-permute-done.17 = bf16[2,64,2048]{2,1,0:T(8,128)(2,1)S(1)} collective-permute-done((bf16[2,64,2048]{2,1,0:T(8,128)(2,1)S(1)}, bf16[2,64,2048]{2,1,0:T(8,128)(2,1)S(1)}, u32[]{:S(2)}, u32[]{:S(2)}) %collective-permute-start.17) | collective-permute-done | bytes 524320 | tf_op jit(solution)/shard_map/ppermute | solution.py:55
  568.9 4.0 collective-permute-start.18
  573.0 14.7 %collective-permute-done.18 = bf16[2,64,2048]{2,1,0:T(8,128)(2,1)S(1)} collective-permute-done((bf16[2,64,2048]{2,1,0:T(8,128)(2,1)S(1)}, bf16[2,64,2048]{2,1,0:T(8,128)(2,1)S(1)}, u32[]{:S(2)}, u32[]{:S(2)}) %collective-permute-start.18) | collective-permute-done | bytes 524320 | tf_op jit(solution)/shard_map/ppermute | solution.py:55
  588.8 4.4 collective-permute-start.19
  593.2 19.6 %fusion.65 = f32[1408,2048]{1,0:T(8,128)} fusion(bf16[2048,1408]{1,0:T(8,128)(2,1)} %get-tuple-element.124, bf16[2048,2048]{1,0:T(8,128)(2,1)} %all-gather.9.cloned.1.call-done.x_ref), kind=kOutput, calls=%fused_computation.206 | convolution fusion | flops 11811160064 | bytes 25690112 | tf_op jit(solution)/shard_map/tf,td->fd/dot_general | solution.py:149
  614.5 3.7 collective-permute-done.19
  619.2 17.7 %all-gather.11.cloned.1.call-done.mid_ref = bf16[2048,2048]{1,0:T(8,128)(2,1)} async-done(((bf16[128,2048]{1,0:T(8,128)(2,1)}), bf16[2048,2048]{1,0:T(8,128)(2,1)}) %all-gather.11.cloned.1.call-update) | async-done | bytes 8388624 | tf_op jit(solution)/shard_map/all_gather | solution.py:141
  636.8 39.7 %attend_back.1 = (bf16[2048,512]{1,0:T(8,128)(2,1)}, bf16[2048,1024]{1,0:T(8,128)(2,1)}, bf16[2048,2048]{1,0:T(8,128)(2,1)}, f32[16,1,128]{2,1,0:T(1,128)}, f32[1,2048]{1,0:T(1,128)}) custom-call(s32[4]{0:T(128)} %pad_add_fusion.places_ref, bf16[2048,2048]{1,0:T(8,128)(2,1)} %all-gather.11.cloned.1.call-done.mid_ref, f32[16,2,128]{2,1,0:T(2,128)} %copy-done.36, ...), custom_call_target="tpu_custom_call" | custom-call | flops 18522046464 | bytes 46137344 | tf_op jit(solution)/shard_map/attend_back/pallas_call | solution.py:444
  676.5 8.2 all-to-all-start.4
  689.0 13.1 %fusion.60 = f32[2048,1024]{1,0:T(8,128)S(1)} fusion(bf16[2048,2048]{1,0:T(8,128)(2,1)} %all-gather.7.cloned.1.call-done.x_ref, bf16[2048,1024]{1,0:T(8,128)(2,1)} %get-tuple-element.99), kind=kOutput, calls=%fused_computation.201 | convolution fusion | flops 8589934592 | bytes 20971520 | tf_op jit(solution)/shard_map/td,tf->df/dot_general | solution.py:149
  702.2 3.3 copy-done.4
  709.9 11.6 %add_bitcast_fusion = f32[1,704,2048]{2,1,0:T(8,128)} fusion(bf16[704,2048]{1,0:T(8,128)(2,1)} %collective-permute-done.20, bf16[2048,704]{1,0:T(8,128)(2,1)} %get-tuple-element.85.refs_0_, bf16[2048,2048]{1,0:T(8,128)(2,1)} %all-gather.5.cloned.1.call-done), kind=kOutput, calls=%fused_computation.6 | convolution fusion | flops 5908463616 | bytes 19922944 | tf_op jit(solution)/shard_map/tf,td->fd/dot_general | solution.py:149
  724.7 5.8 bitcast_add_fusion
  732.0 3.7 slice_bitcast_fusion.26
  735.7 3.4 collective-permute-start.23
  740.5 8.3 fusion.63
  753.3 6.1 fusion.64
  759.4 13.3 %convert_add_fusion = f32[1408,2048]{1,0:T(8,128)} fusion(f32[1408,2048]{1,0:T(8,128)} %fusion.65, bf16[1408,2048]{1,0:T(8,128)(2,1)} %collective-permute-done.36), kind=kLoop, calls=%fused_computation | loop fusion | flops 5767168 | bytes 28835840 | tf_op jit(solution)/shard_map/add | solution.py:774
  777.7 18.8 %collective-permute-done.24 = bf16[64,2048]{1,0:T(8,128)(2,1)S(1)} collective-permute-done((bf16[64,2048]{1,0:T(8,128)(2,1)S(1)}, bf16[64,2048]{1,0:T(8,128)(2,1)S(1)}, u32[]{:S(2)}, u32[]{:S(2)}) %collective-permute-start.24) | collective-permute-done | bytes 262176 | tf_op jit(solution)/shard_map/ppermute | solution.py:55
  797.8 5.5 collective-permute-done.25
  818.1 3.1 fusion.5
  827.6 4.1 all-to-all-start.5
  833.4 12.5 %collective-permute-done.35 = bf16[256,2048]{1,0:T(8,128)(2,1)} collective-permute-done((bf16[256,2048]{1,0:T(8,128)(2,1)}, bf16[256,2048]{1,0:T(8,128)(2,1)}, u32[]{:S(2)}, u32[]{:S(2)}) %collective-permute-start.35) | collective-permute-done | bytes 1048608 | tf_op jit(solution)/shard_map/ppermute | solution.py:55
  845.9 4.5 add_bitcast_fusion.1
  850.4 4.3 all-to-all-start.6
  862.5 16.9 %all-to-all-done.6 = bf16[4,256,512]{2,1,0:T(8,128)(2,1)} async-done(((bf16[4,256,512]{2,1,0:T(8,128)(2,1)}), bf16[4,256,512]{2,1,0:T(8,128)(2,1)}, u32[]{:S(2)}, u32[]{:S(2)}) %all-to-all-start.6) | async-done | bytes 1048608 | tf_op jit(solution)/shard_map/all_to_all | solution.py:162
  883.6 3.0 fusion.14
  (312 shorter events, 116.1 us)
Async XLA Ops:
  7.2 264.2 %copy-start = (f32[2048,4]{0,1:T(4,128)S(1)}, f32[2048,4]{0,1:T(4,128)}, u32[]{:S(2)}) copy-start(f32[2048,4]{0,1:T(4,128)} %param.23) | copy-start | bytes 98308
  7.2 142.5 %all-gather.7.cloned.1.call-start = ((), (), s32[]{:S(2)}) async-start(), calls=%async_computation.10 | async-start | bytes 8912896 | tf_op jit(solution)/shard_map/all_gather | solution.py:141
  11.8 65.8 %collective-permute-start = (bf16[704,2048]{1,0:T(8,128)(2,1)}, bf16[704,2048]{1,0:T(8,128)(2,1)}, u32[]{:S(2)}, u32[]{:S(2)}) collective-permute-start(bf16[704,2048]{1,0:T(8,128)(2,1)} %bitcast.363), channel_id=1, source_target_pairs={{1,0},{0,1},{3,2},{2,3},{5,4},{4,5},{7,6},{6,7},{9,8},{8,9},{11,10... | collective-permute-start | bytes 8650760 | tf_op jit(solution)/shard_map/ppermute | solution.py:55
  17.3 60.3 %all-to-all-start = ((bf16[4,384,512]{2,1,0:T(8,128)(2,1)}), bf16[4,384,512]{2,1,0:T(8,128)(2,1)S(1)}, u32[]{:S(2)}, u32[]{:S(2)}) async-start(bf16[4,384,512]{2,1,0:T(8,128)(2,1)} %maximum_maximum_fusion), calls=%async_computation | async-start | bytes 3145728 | tf_op jit(solution)/shard_map/all_to_all | solution.py:162
  22.2 71.7 %copy-start.16 = (f32[128,2048]{1,0:T(8,128)S(1)}, f32[128,2048]{1,0:T(8,128)}, u32[]{:S(2)}) copy-start(f32[128,2048]{1,0:T(8,128)} %param.31) | copy-start | bytes 3145732
  22.2 199.0 %all-gather.5.cloned.1.call-start = ((), (), s32[]{:S(2)}) async-start(), calls=%async_computation.9 | async-start | bytes 8912896 | tf_op jit(solution)/shard_map/all_gather | solution.py:141
  77.6 13.2 %collective-permute-start.1 = (bf16[4,2,64,512]{3,2,1,0:T(8,128)(2,1)S(1)}, bf16[4,2,64,512]{3,2,1,0:T(8,128)(2,1)S(1)}, u32[]{:S(2)}, u32[]{:S(2)}) collective-permute-start(bf16[4,2,64,512]{3,2,1,0:T(8,128)(2,1)S(1)} %bitcast.335), channel_id=1, source_target_pairs={{1,0},{0,1},{3,2},{2,3},{5,4},{4,5},{7,6},{6,7},{9,8},{8,9},{11,10... | collective-permute-start | bytes 1572872 | tf_op jit(solution)/shard_map/ppermute | solution.py:55
  79.5 15.9 %copy-start.18 = (bf16[4,256,512]{2,1,0:T(8,128)(2,1)}, bf16[4,256,512]{2,1,0:T(8,128)(2,1)S(1)}, u32[]{:S(2)}) copy-start(bf16[4,256,512]{2,1,0:T(8,128)(2,1)S(1)} %slice.266) | copy-start | bytes 3145732
  90.8 23.5 %collective-permute-start.2 = (bf16[4,256,512]{2,1,0:T(8,128)(2,1)S(1)}, bf16[4,256,512]{2,1,0:T(8,128)(2,1)S(1)}, u32[]{:S(2)}, u32[]{:S(2)}) collective-permute-start(bf16[4,256,512]{2,1,0:T(8,128)(2,1)S(1)} %slice.266), channel_id=1, source_target_pairs={{1,0},{0,1},{3,2},{2,3},{5,4},{4,5},{7,6},{6,7},{9,8},{8,9},{11,10... | collective-permute-start | bytes 3145736 | tf_op jit(solution)/shard_map/ppermute | solution.py:55
  92.3 29.3 %copy-start.19 = (bf16[2,4,2,64,512]{4,3,2,1,0:T(8,128)(2,1)}, bf16[2,4,2,64,512]{4,3,2,1,0:T(8,128)(2,1)S(1)}, u32[]{:S(2)}) copy-start(bf16[2,4,2,64,512]{4,3,2,1,0:T(8,128)(2,1)S(1)} %pad_maximum_fusion.4) | copy-start | bytes 3145732
  92.3 28.3 %collective-permute-start.3 = (bf16[2,4,2,64,512]{4,3,2,1,0:T(8,128)(2,1)S(1)}, bf16[2,4,2,64,512]{4,3,2,1,0:T(8,128)(2,1)S(1)}, u32[]{:S(2)}, u32[]{:S(2)}) collective-permute-start(bf16[2,4,2,64,512]{4,3,2,1,0:T(8,128)(2,1)S(1)} %pad_maximum_fusion.4), channel_id=1, source_target_pairs={{16,0},{0,16},{17,1},{1,17},{18,2},{2,18},{19,3},{3,19},{20,4},{4,... | collective-permute-start | bytes 3145736 | tf_op jit(solution)/shard_map/ppermute | solution.py:55
  124.9 13.5 %collective-permute-start.4 = (bf16[2,2,4,2,64,512]{5,4,3,2,1,0:T(8,128)(2,1)}, bf16[2,2,4,2,64,512]{5,4,3,2,1,0:T(8,128)(2,1)}, u32[]{:S(2)}, u32[]{:S(2)}) collective-permute-start(bf16[2,2,4,2,64,512]{5,4,3,2,1,0:T(8,128)(2,1)} %get-tuple-element.136), channel_id=1, source_target_pairs={{8,0},{0,8},{9,1},{1,9},{10,2},{2,10},{11,3},{3,11},{12,4},{4,12},... | collective-permute-start | bytes 6291464 | tf_op jit(solution)/shard_map/ppermute | solution.py:55
  126.7 23.0 %all-to-all-start.1 = ((f32[16,2,128]{2,1,0:T(2,128)}), f32[16,2,128]{2,1,0:T(2,128)S(1)}, u32[]{:S(2)}, u32[]{:S(2)}) async-start(f32[16,2,128]{2,1,0:T(2,128)} %pad_maximum_fusion.8), calls=%async_computation.1 | async-start | bytes 32768 | tf_op jit(solution)/shard_map/all_to_all | solution.py:131
  131.5 214.7 %all-gather.9.cloned.1.call-start = ((), (), s32[]{:S(2)}) async-start(), calls=%async_computation.11 | async-start | bytes 8912896 | tf_op jit(solution)/shard_map/all_gather | solution.py:141
  133.5 42.4 %collective-permute-start.5 = (bf16[256,2048]{1,0:T(8,128)(2,1)}, bf16[256,2048]{1,0:T(8,128)(2,1)S(1)}, u32[]{:S(2)}, u32[]{:S(2)}) collective-permute-start(bf16[256,2048]{1,0:T(8,128)(2,1)} %bitcast.337), channel_id=1, source_target_pairs={{1,0},{0,1},{3,2},{2,3},{5,4},{4,5},{7,6},{6,7},{9,8},{8,9},{11,10... | collective-permute-start | bytes 3145736 | tf_op jit(solution)/shard_map/ppermute | solution.py:55
  150.3 25.6 %copy-start.22 = (bf16[1,256,2048]{2,1,0:T(8,128)(2,1)S(1)}, bf16[1,256,2048]{2,1,0:T(8,128)(2,1)}, u32[]{:S(2)}) copy-start(bf16[1,256,2048]{2,1,0:T(8,128)(2,1)} %param.26) | copy-start | bytes 3145732
  191.2 7.2 collective-permute-start.6
  200.8 15.4 %collective-permute-start.11 = (bf16[2,64,2048]{2,1,0:T(8,128)(2,1)S(1)}, bf16[2,64,2048]{2,1,0:T(8,128)(2,1)S(1)}, u32[]{:S(2)}, u32[]{:S(2)}) collective-permute-start(bf16[2,64,2048]{2,1,0:T(8,128)(2,1)S(1)} %slice_bitcast_fusion.14), channel_id=1, source_target_pairs={{2,0},{4,2},{6,4},{0,6},{3,1},{5,3},{7,5},{1,7},{10,8},{12,10},{14... | collective-permute-start | bytes 1572872 | tf_op jit(solution)/shard_map/ppermute | solution.py:55
  204.7 31.7 %collective-permute-start.7 = (bf16[4,64,2048]{2,1,0:T(8,128)(2,1)S(1)}, bf16[4,64,2048]{2,1,0:T(8,128)(2,1)S(1)}, u32[]{:S(2)}, u32[]{:S(2)}) collective-permute-start(bf16[4,64,2048]{2,1,0:T(8,128)(2,1)S(1)} %slice_bitcast_fusion.6), channel_id=1, source_target_pairs={{16,0},{0,16},{17,1},{1,17},{18,2},{2,18},{19,3},{3,19},{20,4},{4,... | collective-permute-start | bytes 3145736 | tf_op jit(solution)/shard_map/ppermute | solution.py:55
  216.3 16.1 %collective-permute-start.12 = (bf16[2,64,2048]{2,1,0:T(8,128)(2,1)S(1)}, bf16[2,64,2048]{2,1,0:T(8,128)(2,1)S(1)}, u32[]{:S(2)}, u32[]{:S(2)}) collective-permute-start(bf16[2,64,2048]{2,1,0:T(8,128)(2,1)S(1)} %fusion.22), channel_id=1, source_target_pairs={{2,0},{4,2},{6,4},{0,6},{3,1},{5,3},{7,5},{1,7},{10,8},{12,10},{14... | collective-permute-start | bytes 1572872 | tf_op jit(solution)/shard_map/ppermute | solution.py:55
  232.6 23.6 %collective-permute-start.13 = (bf16[2,64,2048]{2,1,0:T(8,128)(2,1)S(1)}, bf16[2,64,2048]{2,1,0:T(8,128)(2,1)S(1)}, u32[]{:S(2)}, u32[]{:S(2)}) collective-permute-start(bf16[2,64,2048]{2,1,0:T(8,128)(2,1)S(1)} %fusion.21), channel_id=1, source_target_pairs={{2,0},{4,2},{6,4},{0,6},{3,1},{5,3},{7,5},{1,7},{10,8},{12,10},{14... | collective-permute-start | bytes 1572872 | tf_op jit(solution)/shard_map/ppermute | solution.py:55
  236.8 15.0 %collective-permute-start.8 = (bf16[64,2048]{1,0:T(8,128)(2,1)S(1)}, bf16[64,2048]{1,0:T(8,128)(2,1)S(1)}, u32[]{:S(2)}, u32[]{:S(2)}) collective-permute-start(bf16[64,2048]{1,0:T(8,128)(2,1)S(1)} %slice_bitcast_fusion.20), channel_id=1, source_target_pairs={{2,0},{4,2},{6,4},{0,6},{3,1},{5,3},{7,5},{1,7},{10,8},{12,10},{14... | collective-permute-start | bytes 786440 | tf_op jit(solution)/shard_map/ppermute | solution.py:55
  245.0 23.6 %copy-start.2 = (bf16[128,2048]{1,0:T(8,128)(2,1)S(1)}, bf16[128,2048]{1,0:T(8,128)(2,1)}, u32[]{:S(2)}) copy-start(bf16[128,2048]{1,0:T(8,128)(2,1)} %param.16) | copy-start | bytes 1572868
  245.0 23.6 %copy-start.28 = (f32[2048]{0:T(1024)S(1)}, f32[2048]{0:T(1024)}, u32[]{:S(2)}) copy-start(f32[2048]{0:T(1024)} %param.27) | copy-start | bytes 24580
  251.9 17.0 %copy-start.34 = (f32[2048]{0:T(1024)S(1)}, f32[2048]{0:T(1024)}, u32[]{:S(2)}) copy-start(f32[2048]{0:T(1024)} %param.21) | copy-start | bytes 24580
  251.9 8.2 collective-permute-start.9
  256.4 8.1 collective-permute-start.14
  260.2 8.2 collective-permute-start.10
  269.9 269.9 %reduce-scatter.3.cloned.1.call-start = ((), (), s32[]{:S(2)}) async-start(), calls=%async_computation.12 | async-start | bytes 8912896 | tf_op jit(solution)/shard_map/reduce_scatter | solution.py:145
  270.0 122.1 %collective-permute-start.15 = (bf16[1408,2048]{1,0:T(8,128)(2,1)}, bf16[1408,2048]{1,0:T(8,128)(2,1)}, u32[]{:S(2)}, u32[]{:S(2)}) collective-permute-start(bf16[1408,2048]{1,0:T(8,128)(2,1)} %bitcast.318), channel_id=1, source_target_pairs={{1,0},{0,1},{3,2},{2,3},{5,4},{4,5},{7,6},{6,7},{9,8},{8,9},{11,10... | collective-permute-start | bytes 17301512 | tf_op jit(solution)/shard_map/ppermute | solution.py:55
  429.2 60.6 %all-to-all-start.3 = ((f32[16,1,128]{2,1,0:T(1,128)}), f32[16,1,128]{2,1,0:T(1,128)S(1)}, u32[]{:S(2)}, u32[]{:S(2)}) async-start(f32[16,1,128]{2,1,0:T(1,128)} %add.174), calls=%async_computation.4 | async-start | bytes 16384 | tf_op jit(solution)/shard_map/all_to_all | solution.py:135
  435.7 201.1 %all-gather.11.cloned.1.call-start = ((), (), s32[]{:S(2)}) async-start(), calls=%async_computation.13 | async-start | bytes 8912896 | tf_op jit(solution)/shard_map/all_gather | solution.py:141
  463.6 26.3 %collective-permute-start.16 = (bf16[2,4,128,2048]{3,2,0,1:T(8,128)(2,1)}, bf16[2,4,128,2048]{3,2,0,1:T(8,128)(2,1)}, u32[]{:S(2)}, u32[]{:S(2)}) collective-permute-start(bf16[2,4,128,2048]{3,2,0,1:T(8,128)(2,1)} %bitcast.314), channel_id=1, source_target_pairs={{8,0},{0,8},{9,1},{1,9},{10,2},{2,10},{11,3},{3,11},{12,4},{4,12},... | collective-permute-start | bytes 12582920 | tf_op jit(solution)/shard_map/ppermute | solution.py:55
  474.8 65.0 %collective-permute-start.20 = (bf16[704,2048]{1,0:T(8,128)(2,1)}, bf16[704,2048]{1,0:T(8,128)(2,1)}, u32[]{:S(2)}, u32[]{:S(2)}) collective-permute-start(bf16[704,2048]{1,0:T(8,128)(2,1)} %convolution_convert_fusion.3), channel_id=1, source_target_pairs={{1,0},{0,1},{3,2},{2,3},{5,4},{4,5},{7,6},{6,7},{9,8},{8,9},{11,10... | collective-permute-start | bytes 8650760 | tf_op jit(solution)/shard_map/ppermute | solution.py:55
  497.8 44.5 %copy-start.17 = (f32[128,2048]{1,0:T(8,128)S(1)}, f32[128,2048]{1,0:T(8,128)}, u32[]{:S(2)}) copy-start(f32[128,2048]{1,0:T(8,128)} %param.31) | copy-start | bytes 3145732
  544.8 23.0 %collective-permute-start.17 = (bf16[2,64,2048]{2,1,0:T(8,128)(2,1)S(1)}, bf16[2,64,2048]{2,1,0:T(8,128)(2,1)S(1)}, u32[]{:S(2)}, u32[]{:S(2)}) collective-permute-start(bf16[2,64,2048]{2,1,0:T(8,128)(2,1)S(1)} %slice_bitcast_fusion.10), channel_id=1, source_target_pairs={{2,0},{4,2},{6,4},{0,6},{3,1},{5,3},{7,5},{1,7},{10,8},{12,10},{14... | collective-permute-start | bytes 1572872 | tf_op jit(solution)/shard_map/ppermute | solution.py:55
  568.9 18.7 %collective-permute-start.18 = (bf16[2,64,2048]{2,1,0:T(8,128)(2,1)S(1)}, bf16[2,64,2048]{2,1,0:T(8,128)(2,1)S(1)}, u32[]{:S(2)}, u32[]{:S(2)}) collective-permute-start(bf16[2,64,2048]{2,1,0:T(8,128)(2,1)S(1)} %fusion.19), channel_id=1, source_target_pairs={{2,0},{4,2},{6,4},{0,6},{3,1},{5,3},{7,5},{1,7},{10,8},{12,10},{14... | collective-permute-start | bytes 1572872 | tf_op jit(solution)/shard_map/ppermute | solution.py:55
  573.0 180.3 %collective-permute-start.36 = (bf16[1408,2048]{1,0:T(8,128)(2,1)}, bf16[1408,2048]{1,0:T(8,128)(2,1)}, u32[]{:S(2)}, u32[]{:S(2)}) collective-permute-start(bf16[1408,2048]{1,0:T(8,128)(2,1)} %convolution_convert_fusion), channel_id=1, source_target_pairs={{1,0},{0,1},{3,2},{2,3},{5,4},{4,5},{7,6},{6,7},{9,8},{8,9},{11,10... | collective-permute-start | bytes 17301512 | tf_op jit(solution)/shard_map/ppermute | solution.py:55
  588.8 29.4 %collective-permute-start.19 = (bf16[2,64,2048]{2,1,0:T(8,128)(2,1)S(1)}, bf16[2,64,2048]{2,1,0:T(8,128)(2,1)S(1)}, u32[]{:S(2)}, u32[]{:S(2)}) collective-permute-start(bf16[2,64,2048]{2,1,0:T(8,128)(2,1)S(1)} %fusion.18), channel_id=1, source_target_pairs={{2,0},{4,2},{6,4},{0,6},{3,1},{5,3},{7,5},{1,7},{10,8},{12,10},{14... | collective-permute-start | bytes 1572872 | tf_op jit(solution)/shard_map/ppermute | solution.py:55
  593.2 19.6 %copy-start.14 = (bf16[128,2048]{1,0:T(8,128)(2,1)S(1)}, bf16[128,2048]{1,0:T(8,128)(2,1)}, u32[]{:S(2)}) copy-start(bf16[128,2048]{1,0:T(8,128)(2,1)} %multiply_convert_fusion) | copy-start | bytes 1572868
  593.2 19.9 %copy-start.7 = (bf16[2,4,128,2048]{3,2,0,1:T(8,128)(2,1)S(1)}, bf16[2,4,128,2048]{3,2,0,1:T(8,128)(2,1)}, u32[]{:S(2)}) copy-start(bf16[2,4,128,2048]{3,2,0,1:T(8,128)(2,1)} %fusion) | copy-start | bytes 12582916
  676.5 30.7 %all-to-all-start.4 = ((f32[16,1,128]{2,1,0:T(1,128)}), f32[16,1,128]{2,1,0:T(1,128)S(1)}, u32[]{:S(2)}, u32[]{:S(2)}) async-start(f32[16,1,128]{2,1,0:T(1,128)} %get-tuple-element.107), calls=%async_computation.5 | async-start | bytes 16384 | tf_op jit(solution)/shard_map/all_to_all | solution.py:135
  684.8 197.5 %reduce-scatter.5.cloned.1.call-start = ((), (), s32[]{:S(2)}) async-start(), calls=%async_computation.14 | async-start | bytes 8912896 | tf_op jit(solution)/shard_map/reduce_scatter | solution.py:145
  687.1 35.0 %collective-permute-start.22 = (bf16[4,64,2048]{2,1,0:T(8,128)(2,1)}, bf16[4,64,2048]{2,1,0:T(8,128)(2,1)}, u32[]{:S(2)}, u32[]{:S(2)}) collective-permute-start(bf16[4,64,2048]{2,1,0:T(8,128)(2,1)} %slice_bitcast_fusion.4), channel_id=1, source_target_pairs={{16,0},{0,16},{17,1},{1,17},{18,2},{2,18},{19,3},{3,19},{20,4},{4,... | collective-permute-start | bytes 3145736 | tf_op jit(solution)/shard_map/ppermute | solution.py:55
  707.2 17.5 %collective-permute-start.21 = (bf16[2,512,1024]{2,1,0:T(8,128)(2,1)}, bf16[2,512,1024]{2,1,0:T(8,128)(2,1)}, u32[]{:S(2)}, u32[]{:S(2)}) collective-permute-start(bf16[2,512,1024]{2,1,0:T(8,128)(2,1)} %fusion.2), channel_id=1, source_target_pairs={{0,8},{8,0},{1,9},{9,1},{2,10},{10,2},{3,11},{11,3},{4,12},{12,4},... | collective-permute-start | bytes 6291464 | tf_op jit(solution)/shard_map/ppermute | solution.py:199
  709.0 12.4 %collective-permute-start.28 = (f32[12,2048]{1,0:T(8,128)S(1)}, f32[12,2048]{1,0:T(8,128)S(1)}, u32[]{:S(2)}, u32[]{:S(2)}) collective-permute-start(f32[12,2048]{1,0:T(8,128)S(1)} %concatenate.40), channel_id=1, source_target_pairs={{0,1},{1,0},{2,3},{3,2},{4,5},{5,4},{6,7},{7,6},{8,9},{9,8},{10,11... | collective-permute-start | bytes 294920 | tf_op jit(solution)/shard_map/ppermute | solution.py:104
  730.6 18.2 %copy-start.3 = (f32[2,512,1024]{2,1,0:T(8,128)}, f32[2,512,1024]{2,1,0:T(8,128)S(1)}, u32[]{:S(2)}) copy-start(f32[2,512,1024]{2,1,0:T(8,128)S(1)} %bitcast_add_fusion) | copy-start | bytes 12582916
  730.6 22.7 %slice-start.2 = ((s8[8388608]{0:T(1024)(128)(4,1)}), s8[4194304]{0:T(1024)(128)(4,1)S(1)}, s32[]{:S(2)}) async-start(s8[8388608]{0:T(1024)(128)(4,1)} %bitcast.359), calls=%async_computation.17 | async-start | bytes 8388608
  731.7 66.0 %collective-permute-start.27 = (bf16[4,2,64,1024]{3,2,1,0:T(8,128)(2,1)}, bf16[4,2,64,1024]{3,2,1,0:T(8,128)(2,1)}, u32[]{:S(2)}, u32[]{:S(2)}) collective-permute-start(bf16[4,2,64,1024]{3,2,1,0:T(8,128)(2,1)} %bitcast.67), channel_id=1, source_target_pairs={{16,0},{0,16},{17,1},{1,17},{18,2},{2,18},{19,3},{3,19},{20,4},{4,... | collective-permute-start | bytes 3145736 | tf_op jit(solution)/shard_map/ppermute | solution.py:55
  735.7 39.9 %collective-permute-start.23 = (bf16[64,2048]{1,0:T(8,128)(2,1)}, bf16[64,2048]{1,0:T(8,128)(2,1)S(1)}, u32[]{:S(2)}, u32[]{:S(2)}) collective-permute-start(bf16[64,2048]{1,0:T(8,128)(2,1)} %slice_bitcast_fusion.26), channel_id=1, source_target_pairs={{2,0},{4,2},{6,4},{0,6},{3,1},{5,3},{7,5},{1,7},{10,8},{12,10},{14... | collective-permute-start | bytes 786440 | tf_op jit(solution)/shard_map/ppermute | solution.py:55
  739.8 56.9 %collective-permute-start.26 = (bf16[64,2048]{1,0:T(8,128)(2,1)}, bf16[64,2048]{1,0:T(8,128)(2,1)}, u32[]{:S(2)}, u32[]{:S(2)}) collective-permute-start(bf16[64,2048]{1,0:T(8,128)(2,1)} %slice_bitcast_fusion.25), channel_id=1, source_target_pairs={{16,0},{0,16},{17,1},{1,17},{18,2},{2,18},{19,3},{3,19},{20,4},{4,... | collective-permute-start | bytes 786440 | tf_op jit(solution)/shard_map/ppermute | solution.py:55
  752.1 66.1 %collective-permute-start.34 = (bf16[4,256,512]{2,1,0:T(8,128)(2,1)}, bf16[4,256,512]{2,1,0:T(8,128)(2,1)}, u32[]{:S(2)}, u32[]{:S(2)}) collective-permute-start(bf16[4,256,512]{2,1,0:T(8,128)(2,1)} %select_bitcast_fusion), channel_id=1, source_target_pairs={{1,0},{0,1},{3,2},{2,3},{5,4},{4,5},{7,6},{6,7},{9,8},{8,9},{11,10... | collective-permute-start | bytes 3145736 | tf_op jit(solution)/shard_map/ppermute | solution.py:55
  775.6 21.1 %copy-start.21 = (bf16[2,64,2048]{2,1,0:T(8,128)(2,1)S(1)}, bf16[2,64,2048]{2,1,0:T(8,128)(2,1)}, u32[]{:S(2)}) copy-start(bf16[2,64,2048]{2,1,0:T(8,128)(2,1)} %fusion.17) | copy-start | bytes 1572868
  775.6 22.1 %copy-start.25 = (f32[12,2048]{1,0:T(8,128)S(1)}, f32[12,2048]{1,0:T(8,128)}, u32[]{:S(2)}) copy-start(f32[12,2048]{1,0:T(8,128)} %add.187) | copy-start | bytes 294916
  775.7 20.8 %collective-permute-start.24 = (bf16[64,2048]{1,0:T(8,128)(2,1)S(1)}, bf16[64,2048]{1,0:T(8,128)(2,1)S(1)}, u32[]{:S(2)}, u32[]{:S(2)}) collective-permute-start(bf16[64,2048]{1,0:T(8,128)(2,1)S(1)} %fusion.28), channel_id=1, source_target_pairs={{2,0},{4,2},{6,4},{0,6},{3,1},{5,3},{7,5},{1,7},{10,8},{12,10},{14... | collective-permute-start | bytes 786440 | tf_op jit(solution)/shard_map/ppermute | solution.py:55
  796.6 6.7 collective-permute-start.25
  797.7 6.3 collective-permute-start.29
  804.1 5.0 collective-permute-start.30
  809.1 7.3 collective-permute-start.31
  811.6 14.9 %collective-permute-start.33 = (bf16[4,64,1024]{2,1,0:T(8,128)(2,1)S(1)}, bf16[4,64,1024]{2,1,0:T(8,128)(2,1)S(1)}, u32[]{:S(2)}, u32[]{:S(2)}) collective-permute-start(bf16[4,64,1024]{2,1,0:T(8,128)(2,1)S(1)} %fusion.24), channel_id=1, source_target_pairs={{1,0},{0,1},{3,2},{2,3},{5,4},{4,5},{7,6},{6,7},{9,8},{8,9},{11,10... | collective-permute-start | bytes 1572872 | tf_op jit(solution)/shard_map/ppermute | solution.py:55
  813.1 32.8 %collective-permute-start.35 = (bf16[256,2048]{1,0:T(8,128)(2,1)}, bf16[256,2048]{1,0:T(8,128)(2,1)}, u32[]{:S(2)}, u32[]{:S(2)}) collective-permute-start(bf16[256,2048]{1,0:T(8,128)(2,1)} %slice_select_fusion), channel_id=1, source_target_pairs={{1,0},{0,1},{3,2},{2,3},{5,4},{4,5},{7,6},{6,7},{9,8},{8,9},{11,10... | collective-permute-start | bytes 3145736 | tf_op jit(solution)/shard_map/ppermute | solution.py:55
  816.5 6.6 collective-permute-start.32
  827.6 22.8 %all-to-all-start.5 = ((bf16[4,64,1024]{2,1,0:T(8,128)(2,1)}), bf16[4,64,1024]{2,1,0:T(8,128)(2,1)}, u32[]{:S(2)}, u32[]{:S(2)}) async-start(bf16[4,64,1024]{2,1,0:T(8,128)(2,1)} %fusion.23), calls=%async_computation.7 | async-start | bytes 1048576 | tf_op jit(solution)/shard_map/all_to_all | solution.py:162
  850.4 29.0 %all-to-all-start.6 = ((bf16[4,256,512]{2,1,0:T(8,128)(2,1)}), bf16[4,256,512]{2,1,0:T(8,128)(2,1)}, u32[]{:S(2)}, u32[]{:S(2)}) async-start(bf16[4,256,512]{2,1,0:T(8,128)(2,1)} %fusion.5), calls=%async_computation.8 | async-start | bytes 2097152 | tf_op jit(solution)/shard_map/all_to_all | solution.py:162
  (48 other events, 276.8 us)
Sparse Core Ops, SparseCore 0:
  11.9 106.4 all-gather.6
  121.8 77.8 all-gather.4
  270.1 76.1 all-gather.8
  428.1 105.4 reduce-scatter.2
  543.8 92.9 all-gather.10
  724.8 122.4 reduce-scatter.4

commit v11 on v10

--- a/solution.py
+++ b/solution.py
@@ -192,7 +192,7 @@
     blocks = grad.reshape(OUTER, inner, -1, grad.shape[1])
     blocks = from_order([blocks[:, k] for k in range(inner)], "i")
     mine = ring_scatter(blocks[:1] + list(after(blocks[1:], *others)), "i").astype(BF16)
-    return join_blocks(exchange(mine)).astype(F32)
+    return exchange(mine)
 
 
 def scatter_kv(kept, sent):
@@ -210,7 +210,7 @@
     whole = jnp.concatenate(
         [join_blocks(here[:, :, :half]), join_blocks(here[:, :, half:])], axis=1
     )
-    return whole.astype(F32), sent, arrived
+    return whole.astype(F32), sent, arrived, mine
 
 
 def own_places():
@@ -751,12 +751,12 @@
     rows_first = after(rows_first, all_mid)
     rows_first = [rows_first[k] for k in range(rows_first.shape[0])]
     rows_first = ring_low(rows_first, "y")
-    d_attn_input = part(after(rows_one, rows_first))
+    d_attn_input = part(rows_one)
     d_att_gate = from_experts(d_gate_a[:, 0], att_onehot, experts)
     d_kv_mat = mm("td,tf->df", all_attn, d_kv).reshape(experts // 2, 2, -1, 2 * span)
     d_kv_mat = from_order([d_kv_mat[:, 0], d_kv_mat[:, 1]], "c")
     d_kv_sent = d_kv_mat[1].astype(BF16)
-    d_kv_weight, kv_sent, kv_arrived = scatter_kv(d_kv_mat[0], d_kv_sent)
+    d_kv_weight, kv_sent, kv_arrived, kv_last = scatter_kv(d_kv_mat[0], d_kv_sent)
     d_heads, all_mid = after((d_heads, all_mid), kv_sent)
     d_att_router, d_att_from_router = gates_back(
         att_gate, att_onehot, d_att_gate, attn_input, att_router
@@ -765,15 +765,17 @@
         d_att_from_router * residual * inverse_one, axis=0, keepdims=True
     )
     summed = sum_over(jnp.concatenate([d_gain_one, sums, d_att_router]), ("i",))
-    d_query = scatter_query(mm("td,tf->df", all_attn, d_heads), summed)[None]
+    d_query = scatter_query(mm("td,tf->df", all_attn, d_heads), summed)
     d_out = mm("tf,td->fd", gated, all_mid).reshape(inner, -1, width)
     d_out = from_order([d_out[k] for k in range(inner)], "i")
-    d_output = ring_scatter(d_out[:1] + list(after(d_out[1:], kv_arrived)), "i")[None]
-    rows_out = part_second(*after((rows_first, rows_second), kv_sent))
+    d_out = d_out[:1] + list(after(d_out[1:], kv_arrived))
+    d_output = ring_scatter(d_out, "i", d_query)[None]
+    d_query = join_blocks(d_query).astype(F32)[None]
+    rows_out = part_second(*after((rows_first, rows_second), kv_arrived))
     layer_out = middle + rows_out.astype(F32) + mlp_bias
     d_upper = (after(upper_last, kv_sent).astype(F32) + upper_own).reshape(up_weight.shape)
     d_lower = (lower_last.astype(F32) + lower_own)[None]
-    summed = sum_over(after(summed, kv_arrived), ("c", "o", "y"))
+    summed = sum_over(after(summed, kv_last), ("c", "o", "y"))
     d_attn_input = after(d_attn_input, summed)
     d_norm_one, _ = norm_back(
         residual, inverse_one, norm_gain1, d_attn_input.astype(F32) + d_att_from_router

time: 898 us -> 892 us (level)
  waiting for transfers between devices: 352 us -> 335 us
  starting transfers between devices: 99.9 us -> 111 us
    ppermute x31, waiting for transfers between devices: 250 us -> 220 us  [shift(): return lax.ppermute(value, axis, [((k + 1) % size, k) for k in range(size)])]
    unnamed x135 -> x125, local copies, waits for them, and re-layouts: 18.5 us -> 22.6 us
  transfers between devices with their start and end apart: 49 -> 49, of which waited for: 24 -> 22; matrix products, arithmetic and copies ran while one was open for 24% -> 24% of each run, Pallas kernels for 15% -> 15%
where the time goes in v11:
time: 892 us; the launch traced here: 888 us
  waiting for transfers between devices  335 us (38%)
  Pallas kernels  173 us (19%)
  starting transfers between devices  111 us (12%)
  matrix products  110 us (12%)
  other arithmetic  87.4 us (10%)
  local copies, waits for them, and re-layouts  43.4 us (5%)
  between operations  15.3 us (2%)
  blocking collectives  11.9 us (1%)
    ppermute x31, waiting for transfers between devices, shift(): return lax.ppermute(value, axis, [((k + 1) % size, k) for k in range(size)])  220 us
    pallas_call x7, Pallas kernels, call(): pl.pallas_call(kernel, grid_spec=pltpu.PrefetchScalarGridSpec(num_scalar_...  173 us
    dot_general x9, matrix products, mm(): return jnp.einsum(form, first, second, preferred_element_type=F32)  104 us
    all_gather x4, waiting for transfers between devices, meet(): return lax.all_gather(rows, GROUP, axis=0, tiled=True)  80.8 us
    ppermute x31, starting transfers between devices, shift(): return lax.ppermute(value, axis, [((k + 1) % size, k) for k in range(size)])  62.4 us
    unnamed x125, local copies, waits for them, and re-layouts  22.6 us
    all_to_all x3, waiting for transfers between devices, exchange(): return lax.all_to_all(blocks, 'o', split_axis=0, concat_axis=0, tiled=True)  22.6 us
    convert_element_type x18, other arithmetic, add_low(): return (first.astype(F32) + second.astype(F32)).astype(BF16)  20.1 us
  transfers between devices with their start and end apart: 49, of which 22 were waited for; matrix products, arithmetic and copies ran while one was open for 24% of the time, Pallas kernels for 15%

profile of v11, /device:TPU:0, one launch (start us, length us, event | category | flops | bytes accessed | tf_op | source)
XLA Modules:
  0.0 887.9 jit_solution(8621801650726387416)
XLA Ops:
  11.8 3.0 collective-permute-start
  17.3 4.9 all-to-all-start
  22.2 55.4 %collective-permute-done.refs_3_ = bf16[704,2048]{1,0:T(8,128)(2,1)} collective-permute-done((bf16[704,2048]{1,0:T(8,128)(2,1)}, bf16[704,2048]{1,0:T(8,128)(2,1)}, u32[]{:S(2)}, u32[]{:S(2)}) %collective-permute-start) | collective-permute-done | bytes 2883616 | tf_op jit(solution)/shard_map/ppermute | solution.py:55
  79.5 11.3 %collective-permute-done.1 = bf16[4,2,64,512]{3,2,1,0:T(8,128)(2,1)S(1)} collective-permute-done((bf16[4,2,64,512]{3,2,1,0:T(8,128)(2,1)S(1)}, bf16[4,2,64,512]{3,2,1,0:T(8,128)(2,1)S(1)}, u32[]{:S(2)}, u32[]{:S(2)}) %collective-permute-start.1) | collective-permute-done | bytes 524320 | tf_op jit(solution)/shard_map/ppermute | solution.py:55
  95.4 18.9 %collective-permute-done.2 = bf16[4,256,512]{2,1,0:T(8,128)(2,1)S(1)} collective-permute-done((bf16[4,256,512]{2,1,0:T(8,128)(2,1)S(1)}, bf16[4,256,512]{2,1,0:T(8,128)(2,1)S(1)}, u32[]{:S(2)}, u32[]{:S(2)}) %collective-permute-start.2) | collective-permute-done | bytes 1048608 | tf_op jit(solution)/shard_map/ppermute | solution.py:55
  114.3 6.3 collective-permute-done.3
  121.7 3.2 fusion.51
  126.8 4.8 all-to-all-start.1
  138.5 4.0 pad_maximum_fusion.in_ref
  142.5 7.3 arrange.1
  150.5 25.6 %attend.1 = (bf16[2048,1536]{1,0:T(8,128)(2,1)}, bf16[2048,512]{1,0:T(8,128)(2,1)}) custom-call(s32[4]{0:T(128)} %pad_add_fusion.places_ref, bf16[2048,2048]{1,0:T(8,128)(2,1)} %all-gather.7.cloned.1.call-done.x_ref, f32[16,2,128]{2,1,0:T(2,128)} %copy-done.34, f32[128,128]{1,0:T(8,128)} %get-tuple-element.175.cos_ref, ...), custom_call_target="tpu_custom_call" | custom-call | flops 13421772800 | bytes 25165824 | tf_op jit(solution)/shard_map/attend/pallas_call | solution.py:444
  177.7 9.2 %rows.2 = bf16[2,2,4,128,2048]{4,3,2,1,0:T(8,128)(2,1)} custom-call(s32[4]{0:T(128)} %pad_add_fusion.places_ref, bf16[2048,512]{1,0:T(8,128)(2,1)} %get-tuple-element.79.refs_0_, bf16[512,2048]{1,0:T(8,128)(2,1)} %bitcast.333), custom_call_target="tpu_custom_call" | custom-call | flops 4294967296 | bytes 20971520 | tf_op jit(solution)/shard_map/rows/pallas_call | solution.py:444
  186.9 3.9 fusion.54
  191.6 7.2 collective-permute-done.6
  201.1 3.6 collective-permute-start.11
  206.9 9.4 %collective-permute-done.11 = bf16[2,64,2048]{2,1,0:T(8,128)(2,1)S(1)} collective-permute-done((bf16[2,64,2048]{2,1,0:T(8,128)(2,1)S(1)}, bf16[2,64,2048]{2,1,0:T(8,128)(2,1)S(1)}, u32[]{:S(2)}, u32[]{:S(2)}) %collective-permute-start.11) | collective-permute-done | bytes 524320 | tf_op jit(solution)/shard_map/ppermute | solution.py:55
  216.4 4.9 collective-permute-start.12
  221.3 11.3 %convolution_convert_fusion.1.d_units_ref = bf16[2048,704]{1,0:T(8,128)(2,1)} fusion(bf16[2048,2048]{1,0:T(8,128)(2,1)} %all-gather.5.cloned.1.call-done, bf16[704,2048]{1,0:T(8,128)(2,1)} %collective-permute-done.refs_3_), kind=kOutput, calls=%fused_computation.16 | convolution fusion | flops 5907021824 | bytes 14155776 | tf_op jit(solution)/shard_map/td,fd->tf/dot_general | solution.py:149
  232.7 3.7 collective-permute-start.13
  236.9 8.1 convolution_convert_fusion.2.d_units_ref
  245.0 6.8 collective-permute-done.8
  251.8 4.3 collective-permute-start.9
  260.1 4.3 collective-permute-start.10
  264.5 3.8 collective-permute-done.10
  273.7 11.9 %all_to_all.37.info_ref = f32[16,1,128]{2,1,0:T(1,128)} all-to-all(f32[16,1,128]{2,1,0:T(1,128)S(1)} %bitcast.346), channel_id=1, replica_groups=mesh['y'=2,'c'=2,'o'=4,'i'=2] {'y','c','o'}, dimensions={0} | all-to-all | bytes 16384 | tf_op jit(solution)/shard_map/all_to_all | solution.py:131
  285.7 60.9 %all-gather.9.cloned.1.call-done.x_ref = bf16[2048,2048]{1,0:T(8,128)(2,1)} async-done(((bf16[128,2048]{1,0:T(8,128)(2,1)}), bf16[2048,2048]{1,0:T(8,128)(2,1)}) %all-gather.9.cloned.1.call-update) | async-done | bytes 8388624 | tf_op jit(solution)/shard_map/all_gather | solution.py:141
  346.5 35.5 %units.2 = (bf16[2048,1408]{1,0:T(8,128)(2,1)}, bf16[2048,704]{1,0:T(8,128)(2,1)}, f32[2048,2048]{1,0:T(8,128)}, f32[16,1,128]{2,1,0:T(1,128)}) custom-call(s32[4]{0:T(128)} %pad_add_fusion.places_ref, bf16[2048,2048]{1,0:T(8,128)(2,1)} %all-gather.9.cloned.1.call-done.x_ref, f32[16,1,128]{2,1,0:T(1,128)} %all_to_all.37.info_ref, ...), custom_call_target="tpu_custom_call" | custom-call | tf_op jit(solution)/shard_map/units/pallas_call | solution.py:444
  382.1 10.5 %collective-permute-done.15.first_ref.second_ref = bf16[1408,2048]{1,0:T(8,128)(2,1)} collective-permute-done((bf16[1408,2048]{1,0:T(8,128)(2,1)}, bf16[1408,2048]{1,0:T(8,128)(2,1)}, u32[]{:S(2)}, u32[]{:S(2)}) %collective-permute-start.15) | collective-permute-done | bytes 5767200 | tf_op jit(solution)/shard_map/ppermute | solution.py:55
  392.5 35.8 %units.3 = (bf16[2048,1408]{1,0:T(8,128)(2,1)}, bf16[2048,704]{1,0:T(8,128)(2,1)}, bf16[2048,2048]{1,0:T(8,128)(2,1)}, f32[16,1,128]{2,1,0:T(1,128)}) custom-call(s32[4]{0:T(128)} %pad_add_fusion.places_ref, bf16[2048,2048]{1,0:T(8,128)(2,1)} %all-gather.9.cloned.1.call-done.x_ref, f32[16,1,128]{2,1,0:T(1,128)} %all_to_all.37.info_ref, ...), custom_call_target="tpu_custom_call" | custom-call | tf_op jit(solution)/shard_map/units/pallas_call | solution.py:444
  429.7 6.2 all-to-all-start.3
  436.1 19.9 %rows.3 = bf16[2,2,4,128,2048]{4,3,2,1,0:T(8,128)(2,1)} custom-call(s32[4]{0:T(128)} %pad_add_fusion.places_ref, bf16[2048,704]{1,0:T(8,128)(2,1)} %get-tuple-element.85.refs_0_, bf16[2048,704]{1,0:T(8,128)(2,1)} %get-tuple-element.89.refs_1_, bf16[704,2048]{1,0:T(8,128)(2,1)} %bitcast.362, bf16[704,2048]{1,0:T(8,128)(2,1)} %collective-permute-done.refs_3_), custom_call_target="tpu_custom_call" | custom-call | flops 11811160064 | bytes 28311552 | tf_op jit(solution)/shard_map/rows/pallas_call | solution.py:444
  456.0 5.3 fusion.53
  464.8 10.3 %convolution_convert_fusion.3 = bf16[704,2048]{1,0:T(8,128)(2,1)} fusion(bf16[2048,704]{1,0:T(8,128)(2,1)S(1)} %copy-done.50, bf16[2048,2048]{1,0:T(8,128)(2,1)} %all-gather.5.cloned.1.call-done), kind=kOutput, calls=%fused_computation.18 | convolution fusion | flops 5907021824 | bytes 14155776 | tf_op jit(solution)/shard_map/tf,td->fd/dot_general | solution.py:149
  476.5 14.2 %convolution_convert_fusion = bf16[1408,2048]{1,0:T(8,128)(2,1)} fusion(bf16[2048,1408]{1,0:T(8,128)(2,1)S(1)} %bitcast.360, bf16[2048,2048]{1,0:T(8,128)(2,1)S(1)} %bitcast.317), kind=kOutput, calls=%fused_computation.5 | convolution fusion | flops 11814043648 | bytes 19922944 | tf_op jit(solution)/shard_map/tf,td->fd/dot_general | solution.py:149
  490.8 7.9 fusion
  498.7 41.5 %collective-permute-done.20 = bf16[704,2048]{1,0:T(8,128)(2,1)} collective-permute-done((bf16[704,2048]{1,0:T(8,128)(2,1)}, bf16[704,2048]{1,0:T(8,128)(2,1)}, u32[]{:S(2)}, u32[]{:S(2)}) %collective-permute-start.20) | collective-permute-done | bytes 2883616 | tf_op jit(solution)/shard_map/ppermute | solution.py:55
  545.1 4.0 collective-permute-start.17
  549.0 18.0 %collective-permute-done.17 = bf16[2,64,2048]{2,1,0:T(8,128)(2,1)S(1)} collective-permute-done((bf16[2,64,2048]{2,1,0:T(8,128)(2,1)S(1)}, bf16[2,64,2048]{2,1,0:T(8,128)(2,1)S(1)}, u32[]{:S(2)}, u32[]{:S(2)}) %collective-permute-start.17) | collective-permute-done | bytes 524320 | tf_op jit(solution)/shard_map/ppermute | solution.py:55
  568.2 4.3 collective-permute-start.18
  573.4 14.4 %collective-permute-done.18 = bf16[2,64,2048]{2,1,0:T(8,128)(2,1)S(1)} collective-permute-done((bf16[2,64,2048]{2,1,0:T(8,128)(2,1)S(1)}, bf16[2,64,2048]{2,1,0:T(8,128)(2,1)S(1)}, u32[]{:S(2)}, u32[]{:S(2)}) %collective-permute-start.18) | collective-permute-done | bytes 524320 | tf_op jit(solution)/shard_map/ppermute | solution.py:55
  588.9 4.4 collective-permute-start.19
  593.3 20.0 %fusion.65 = f32[1408,2048]{1,0:T(8,128)} fusion(bf16[2048,1408]{1,0:T(8,128)(2,1)} %get-tuple-element.124, bf16[2048,2048]{1,0:T(8,128)(2,1)} %all-gather.9.cloned.1.call-done.x_ref), kind=kOutput, calls=%fused_computation.206 | convolution fusion | flops 11811160064 | bytes 25690112 | tf_op jit(solution)/shard_map/tf,td->fd/dot_general | solution.py:149
  616.9 19.9 %all-gather.11.cloned.1.call-done.mid_ref = bf16[2048,2048]{1,0:T(8,128)(2,1)} async-done(((bf16[128,2048]{1,0:T(8,128)(2,1)}), bf16[2048,2048]{1,0:T(8,128)(2,1)}) %all-gather.11.cloned.1.call-update) | async-done | bytes 8388624 | tf_op jit(solution)/shard_map/all_gather | solution.py:141
  636.9 39.7 %attend_back.1 = (bf16[2048,512]{1,0:T(8,128)(2,1)}, bf16[2048,1024]{1,0:T(8,128)(2,1)}, bf16[2048,2048]{1,0:T(8,128)(2,1)}, f32[16,1,128]{2,1,0:T(1,128)}, f32[1,2048]{1,0:T(1,128)}) custom-call(s32[4]{0:T(128)} %pad_add_fusion.places_ref, bf16[2048,2048]{1,0:T(8,128)(2,1)} %all-gather.11.cloned.1.call-done.mid_ref, f32[16,2,128]{2,1,0:T(2,128)} %copy-done.34, ...), custom_call_target="tpu_custom_call" | custom-call | flops 18522046464 | bytes 46137344 | tf_op jit(solution)/shard_map/attend_back/pallas_call | solution.py:444
  676.6 8.4 all-to-all-start.4
  689.3 13.1 %fusion.60 = f32[2048,1024]{1,0:T(8,128)S(1)} fusion(bf16[2048,2048]{1,0:T(8,128)(2,1)} %all-gather.7.cloned.1.call-done.x_ref, bf16[2048,1024]{1,0:T(8,128)(2,1)} %get-tuple-element.99), kind=kOutput, calls=%fused_computation.201 | convolution fusion | flops 8589934592 | bytes 20971520 | tf_op jit(solution)/shard_map/td,tf->df/dot_general | solution.py:149
  702.4 3.3 copy-done.5
  710.6 11.6 %add_bitcast_fusion = f32[1,704,2048]{2,1,0:T(8,128)} fusion(bf16[704,2048]{1,0:T(8,128)(2,1)} %collective-permute-done.20, bf16[2048,704]{1,0:T(8,128)(2,1)} %get-tuple-element.85.refs_0_, bf16[2048,2048]{1,0:T(8,128)(2,1)} %all-gather.5.cloned.1.call-done), kind=kOutput, calls=%fused_computation.6 | convolution fusion | flops 5908463616 | bytes 19922944 | tf_op jit(solution)/shard_map/tf,td->fd/dot_general | solution.py:149
  723.1 2.9 fusion.3
  726.0 6.6 bitcast_add_fusion
  736.0 7.5 fusion.63
  747.2 13.3 %convert_add_fusion = f32[1408,2048]{1,0:T(8,128)} fusion(f32[1408,2048]{1,0:T(8,128)} %fusion.65, bf16[1408,2048]{1,0:T(8,128)(2,1)} %collective-permute-done.36), kind=kLoop, calls=%fused_computation | loop fusion | flops 5767168 | bytes 28835840 | tf_op jit(solution)/shard_map/add | solution.py:776
  760.5 7.8 fusion.64
  771.9 3.2 collective-permute-start.24
  779.5 12.8 %collective-permute-done.24 = bf16[64,2048]{1,0:T(8,128)(2,1)S(1)} collective-permute-done((bf16[64,2048]{1,0:T(8,128)(2,1)S(1)}, bf16[64,2048]{1,0:T(8,128)(2,1)S(1)}, u32[]{:S(2)}, u32[]{:S(2)}) %collective-permute-start.24) | collective-permute-done | bytes 262176 | tf_op jit(solution)/shard_map/ppermute | solution.py:55
  793.5 2.9 fusion.5
  806.1 4.1 all-to-all-start.5
  810.3 10.1 %collective-permute-done.32 = f32[12,2048]{1,0:T(8,128)} collective-permute-done((f32[12,2048]{1,0:T(8,128)}, f32[12,2048]{1,0:T(8,128)}, u32[]{:S(2)}, u32[]{:S(2)}) %collective-permute-start.32) | collective-permute-done | bytes 98336 | tf_op jit(solution)/shard_map/ppermute | solution.py:104
  821.4 7.5 collective-permute-start.33
  833.1 4.8 all-to-all-done.5
  837.9 7.0 all-to-all-start.6
  852.7 17.8 %all-to-all-done.6 = bf16[4,256,512]{2,1,0:T(8,128)(2,1)} async-done(((bf16[4,256,512]{2,1,0:T(8,128)(2,1)}), bf16[4,256,512]{2,1,0:T(8,128)(2,1)}, u32[]{:S(2)}, u32[]{:S(2)}) %all-to-all-start.6) | async-done | bytes 1048608 | tf_op jit(solution)/shard_map/all_to_all | solution.py:162
  873.4 3.1 add_bitcast_fusion.1
  877.8 3.0 fusion.14
  (301 shorter events, 112.3 us)
Async XLA Ops:
  7.2 264.9 %copy-start = (f32[2048,4]{0,1:T(4,128)S(1)}, f32[2048,4]{0,1:T(4,128)}, u32[]{:S(2)}) copy-start(f32[2048,4]{0,1:T(4,128)} %param.23) | copy-start | bytes 98308
  7.2 142.7 %all-gather.7.cloned.1.call-start = ((), (), s32[]{:S(2)}) async-start(), calls=%async_computation.10 | async-start | bytes 8912896 | tf_op jit(solution)/shard_map/all_gather | solution.py:141
  11.8 65.8 %collective-permute-start = (bf16[704,2048]{1,0:T(8,128)(2,1)}, bf16[704,2048]{1,0:T(8,128)(2,1)}, u32[]{:S(2)}, u32[]{:S(2)}) collective-permute-start(bf16[704,2048]{1,0:T(8,128)(2,1)} %bitcast.361), channel_id=1, source_target_pairs={{1,0},{0,1},{3,2},{2,3},{5,4},{4,5},{7,6},{6,7},{9,8},{8,9},{11,10... | collective-permute-start | bytes 8650760 | tf_op jit(solution)/shard_map/ppermute | solution.py:55
  17.3 60.3 %all-to-all-start = ((bf16[4,384,512]{2,1,0:T(8,128)(2,1)}), bf16[4,384,512]{2,1,0:T(8,128)(2,1)S(1)}, u32[]{:S(2)}, u32[]{:S(2)}) async-start(bf16[4,384,512]{2,1,0:T(8,128)(2,1)} %maximum_maximum_fusion), calls=%async_computation | async-start | bytes 3145728 | tf_op jit(solution)/shard_map/all_to_all | solution.py:162
  22.2 71.7 %copy-start.17 = (f32[128,2048]{1,0:T(8,128)S(1)}, f32[128,2048]{1,0:T(8,128)}, u32[]{:S(2)}) copy-start(f32[128,2048]{1,0:T(8,128)} %param.31) | copy-start | bytes 3145732
  22.2 199.1 %all-gather.5.cloned.1.call-start = ((), (), s32[]{:S(2)}) async-start(), calls=%async_computation.9 | async-start | bytes 8912896 | tf_op jit(solution)/shard_map/all_gather | solution.py:141
  77.6 13.2 %collective-permute-start.1 = (bf16[4,2,64,512]{3,2,1,0:T(8,128)(2,1)S(1)}, bf16[4,2,64,512]{3,2,1,0:T(8,128)(2,1)S(1)}, u32[]{:S(2)}, u32[]{:S(2)}) collective-permute-start(bf16[4,2,64,512]{3,2,1,0:T(8,128)(2,1)S(1)} %bitcast.335), channel_id=1, source_target_pairs={{1,0},{0,1},{3,2},{2,3},{5,4},{4,5},{7,6},{6,7},{9,8},{8,9},{11,10... | collective-permute-start | bytes 1572872 | tf_op jit(solution)/shard_map/ppermute | solution.py:55
  79.5 15.9 %copy-start.19 = (bf16[4,256,512]{2,1,0:T(8,128)(2,1)}, bf16[4,256,512]{2,1,0:T(8,128)(2,1)S(1)}, u32[]{:S(2)}) copy-start(bf16[4,256,512]{2,1,0:T(8,128)(2,1)S(1)} %slice.266) | copy-start | bytes 3145732
  90.8 23.5 %collective-permute-start.2 = (bf16[4,256,512]{2,1,0:T(8,128)(2,1)S(1)}, bf16[4,256,512]{2,1,0:T(8,128)(2,1)S(1)}, u32[]{:S(2)}, u32[]{:S(2)}) collective-permute-start(bf16[4,256,512]{2,1,0:T(8,128)(2,1)S(1)} %slice.266), channel_id=1, source_target_pairs={{1,0},{0,1},{3,2},{2,3},{5,4},{4,5},{7,6},{6,7},{9,8},{8,9},{11,10... | collective-permute-start | bytes 3145736 | tf_op jit(solution)/shard_map/ppermute | solution.py:55
  92.3 29.3 %copy-start.20 = (bf16[2,4,2,64,512]{4,3,2,1,0:T(8,128)(2,1)}, bf16[2,4,2,64,512]{4,3,2,1,0:T(8,128)(2,1)S(1)}, u32[]{:S(2)}) copy-start(bf16[2,4,2,64,512]{4,3,2,1,0:T(8,128)(2,1)S(1)} %pad_maximum_fusion.4) | copy-start | bytes 3145732
  92.3 28.3 %collective-permute-start.3 = (bf16[2,4,2,64,512]{4,3,2,1,0:T(8,128)(2,1)S(1)}, bf16[2,4,2,64,512]{4,3,2,1,0:T(8,128)(2,1)S(1)}, u32[]{:S(2)}, u32[]{:S(2)}) collective-permute-start(bf16[2,4,2,64,512]{4,3,2,1,0:T(8,128)(2,1)S(1)} %pad_maximum_fusion.4), channel_id=1, source_target_pairs={{16,0},{0,16},{17,1},{1,17},{18,2},{2,18},{19,3},{3,19},{20,4},{4,... | collective-permute-start | bytes 3145736 | tf_op jit(solution)/shard_map/ppermute | solution.py:55
  124.9 13.6 %collective-permute-start.4 = (bf16[2,2,4,2,64,512]{5,4,3,2,1,0:T(8,128)(2,1)}, bf16[2,2,4,2,64,512]{5,4,3,2,1,0:T(8,128)(2,1)}, u32[]{:S(2)}, u32[]{:S(2)}) collective-permute-start(bf16[2,2,4,2,64,512]{5,4,3,2,1,0:T(8,128)(2,1)} %get-tuple-element.136), channel_id=1, source_target_pairs={{8,0},{0,8},{9,1},{1,9},{10,2},{2,10},{11,3},{3,11},{12,4},{4,12},... | collective-permute-start | bytes 6291464 | tf_op jit(solution)/shard_map/ppermute | solution.py:55
  126.8 23.1 %all-to-all-start.1 = ((f32[16,2,128]{2,1,0:T(2,128)}), f32[16,2,128]{2,1,0:T(2,128)S(1)}, u32[]{:S(2)}, u32[]{:S(2)}) async-start(f32[16,2,128]{2,1,0:T(2,128)} %pad_maximum_fusion.8), calls=%async_computation.1 | async-start | bytes 32768 | tf_op jit(solution)/shard_map/all_to_all | solution.py:131
  131.6 214.9 %all-gather.9.cloned.1.call-start = ((), (), s32[]{:S(2)}) async-start(), calls=%async_computation.11 | async-start | bytes 8912896 | tf_op jit(solution)/shard_map/all_gather | solution.py:141
  133.6 42.4 %collective-permute-start.5 = (bf16[256,2048]{1,0:T(8,128)(2,1)}, bf16[256,2048]{1,0:T(8,128)(2,1)S(1)}, u32[]{:S(2)}, u32[]{:S(2)}) collective-permute-start(bf16[256,2048]{1,0:T(8,128)(2,1)} %bitcast.337), channel_id=1, source_target_pairs={{1,0},{0,1},{3,2},{2,3},{5,4},{4,5},{7,6},{6,7},{9,8},{8,9},{11,10... | collective-permute-start | bytes 3145736 | tf_op jit(solution)/shard_map/ppermute | solution.py:55
  150.5 25.6 %copy-start.22 = (bf16[1,256,2048]{2,1,0:T(8,128)(2,1)S(1)}, bf16[1,256,2048]{2,1,0:T(8,128)(2,1)}, u32[]{:S(2)}) copy-start(bf16[1,256,2048]{2,1,0:T(8,128)(2,1)} %param.26) | copy-start | bytes 3145732
  191.4 7.4 collective-permute-start.6
  201.1 15.2 %copy-start.6 = (bf16[2,4,128,2048]{3,2,0,1:T(8,128)(2,1)}, bf16[2,4,128,2048]{3,2,0,1:T(8,128)(2,1)S(1)}, u32[]{:S(2)}) copy-start(bf16[2,4,128,2048]{3,2,0,1:T(8,128)(2,1)S(1)} %fusion.1) | copy-start | bytes 12582916
  201.1 15.1 %collective-permute-start.11 = (bf16[2,64,2048]{2,1,0:T(8,128)(2,1)S(1)}, bf16[2,64,2048]{2,1,0:T(8,128)(2,1)S(1)}, u32[]{:S(2)}, u32[]{:S(2)}) collective-permute-start(bf16[2,64,2048]{2,1,0:T(8,128)(2,1)S(1)} %slice_bitcast_fusion.14), channel_id=1, source_target_pairs={{2,0},{4,2},{6,4},{0,6},{3,1},{5,3},{7,5},{1,7},{10,8},{12,10},{14... | collective-permute-start | bytes 1572872 | tf_op jit(solution)/shard_map/ppermute | solution.py:55
  204.9 31.5 %collective-permute-start.7 = (bf16[4,64,2048]{2,1,0:T(8,128)(2,1)S(1)}, bf16[4,64,2048]{2,1,0:T(8,128)(2,1)S(1)}, u32[]{:S(2)}, u32[]{:S(2)}) collective-permute-start(bf16[4,64,2048]{2,1,0:T(8,128)(2,1)S(1)} %slice_bitcast_fusion.6), channel_id=1, source_target_pairs={{16,0},{0,16},{17,1},{1,17},{18,2},{2,18},{19,3},{3,19},{20,4},{4,... | collective-permute-start | bytes 3145736 | tf_op jit(solution)/shard_map/ppermute | solution.py:55
  216.4 16.2 %collective-permute-start.12 = (bf16[2,64,2048]{2,1,0:T(8,128)(2,1)S(1)}, bf16[2,64,2048]{2,1,0:T(8,128)(2,1)S(1)}, u32[]{:S(2)}, u32[]{:S(2)}) collective-permute-start(bf16[2,64,2048]{2,1,0:T(8,128)(2,1)S(1)} %fusion.22), channel_id=1, source_target_pairs={{2,0},{4,2},{6,4},{0,6},{3,1},{5,3},{7,5},{1,7},{10,8},{12,10},{14... | collective-permute-start | bytes 1572872 | tf_op jit(solution)/shard_map/ppermute | solution.py:55
  221.3 15.6 %copy-start.49 = (bf16[2048,2048]{1,0:T(8,128)(2,1)S(1)}, bf16[2048,2048]{1,0:T(8,128)(2,1)}, u32[]{:S(2)}) copy-start(bf16[2048,2048]{1,0:T(8,128)(2,1)} %all-gather.5.cloned.1.call-done) | copy-start | bytes 25165828
  232.7 23.4 %collective-permute-start.13 = (bf16[2,64,2048]{2,1,0:T(8,128)(2,1)S(1)}, bf16[2,64,2048]{2,1,0:T(8,128)(2,1)S(1)}, u32[]{:S(2)}, u32[]{:S(2)}) collective-permute-start(bf16[2,64,2048]{2,1,0:T(8,128)(2,1)S(1)} %fusion.21), channel_id=1, source_target_pairs={{2,0},{4,2},{6,4},{0,6},{3,1},{5,3},{7,5},{1,7},{10,8},{12,10},{14... | collective-permute-start | bytes 1572872 | tf_op jit(solution)/shard_map/ppermute | solution.py:55
  236.8 14.9 %collective-permute-start.8 = (bf16[64,2048]{1,0:T(8,128)(2,1)S(1)}, bf16[64,2048]{1,0:T(8,128)(2,1)S(1)}, u32[]{:S(2)}, u32[]{:S(2)}) collective-permute-start(bf16[64,2048]{1,0:T(8,128)(2,1)S(1)} %slice_bitcast_fusion.20), channel_id=1, source_target_pairs={{2,0},{4,2},{6,4},{0,6},{3,1},{5,3},{7,5},{1,7},{10,8},{12,10},{14... | collective-permute-start | bytes 786440 | tf_op jit(solution)/shard_map/ppermute | solution.py:55
  245.0 23.5 %copy-start.2 = (bf16[128,2048]{1,0:T(8,128)(2,1)S(1)}, bf16[128,2048]{1,0:T(8,128)(2,1)}, u32[]{:S(2)}) copy-start(bf16[128,2048]{1,0:T(8,128)(2,1)} %param.16) | copy-start | bytes 1572868
  245.0 23.5 %copy-start.26 = (f32[2048]{0:T(1024)S(1)}, f32[2048]{0:T(1024)}, u32[]{:S(2)}) copy-start(f32[2048]{0:T(1024)} %param.27) | copy-start | bytes 24580
  251.8 17.0 %copy-start.32 = (f32[2048]{0:T(1024)S(1)}, f32[2048]{0:T(1024)}, u32[]{:S(2)}) copy-start(f32[2048]{0:T(1024)} %param.21) | copy-start | bytes 24580
  251.8 8.2 collective-permute-start.9
  256.3 8.1 collective-permute-start.14
  260.1 13.5 %copy-start.35 = (s32[128,2]{0,1:T(2,128)S(1)}, s32[128,2]{0,1:T(2,128)}, u32[]{:S(2)}) copy-start(s32[128,2]{0,1:T(2,128)} %param.19) | copy-start | bytes 3076
  260.1 8.2 collective-permute-start.10
  269.9 270.3 %reduce-scatter.3.cloned.1.call-start = ((), (), s32[]{:S(2)}) async-start(), calls=%async_computation.12 | async-start | bytes 8912896 | tf_op jit(solution)/shard_map/reduce_scatter | solution.py:145
  269.9 122.6 %collective-permute-start.15 = (bf16[1408,2048]{1,0:T(8,128)(2,1)}, bf16[1408,2048]{1,0:T(8,128)(2,1)}, u32[]{:S(2)}, u32[]{:S(2)}) collective-permute-start(bf16[1408,2048]{1,0:T(8,128)(2,1)} %bitcast.318), channel_id=1, source_target_pairs={{1,0},{0,1},{3,2},{2,3},{5,4},{4,5},{7,6},{6,7},{9,8},{8,9},{11,10... | collective-permute-start | bytes 17301512 | tf_op jit(solution)/shard_map/ppermute | solution.py:55
  429.7 61.0 %all-to-all-start.3 = ((f32[16,1,128]{2,1,0:T(1,128)}), f32[16,1,128]{2,1,0:T(1,128)S(1)}, u32[]{:S(2)}, u32[]{:S(2)}) async-start(f32[16,1,128]{2,1,0:T(1,128)} %add.174), calls=%async_computation.4 | async-start | bytes 16384 | tf_op jit(solution)/shard_map/all_to_all | solution.py:135
  435.9 201.0 %all-gather.11.cloned.1.call-start = ((), (), s32[]{:S(2)}) async-start(), calls=%async_computation.13 | async-start | bytes 8912896 | tf_op jit(solution)/shard_map/all_gather | solution.py:141
  463.8 27.0 %collective-permute-start.16 = (bf16[2,4,128,2048]{3,2,0,1:T(8,128)(2,1)}, bf16[2,4,128,2048]{3,2,0,1:T(8,128)(2,1)}, u32[]{:S(2)}, u32[]{:S(2)}) collective-permute-start(bf16[2,4,128,2048]{3,2,0,1:T(8,128)(2,1)} %bitcast.314), channel_id=1, source_target_pairs={{8,0},{0,8},{9,1},{1,9},{10,2},{2,10},{11,3},{3,11},{12,4},{4,12},... | collective-permute-start | bytes 12582920 | tf_op jit(solution)/shard_map/ppermute | solution.py:55
  475.1 65.1 %collective-permute-start.20 = (bf16[704,2048]{1,0:T(8,128)(2,1)}, bf16[704,2048]{1,0:T(8,128)(2,1)}, u32[]{:S(2)}, u32[]{:S(2)}) collective-permute-start(bf16[704,2048]{1,0:T(8,128)(2,1)} %convolution_convert_fusion.3), channel_id=1, source_target_pairs={{1,0},{0,1},{3,2},{2,3},{5,4},{4,5},{7,6},{6,7},{9,8},{8,9},{11,10... | collective-permute-start | bytes 8650760 | tf_op jit(solution)/shard_map/ppermute | solution.py:55
  498.7 44.0 %copy-start.18 = (f32[128,2048]{1,0:T(8,128)S(1)}, f32[128,2048]{1,0:T(8,128)}, u32[]{:S(2)}) copy-start(f32[128,2048]{1,0:T(8,128)} %param.31) | copy-start | bytes 3145732
  545.1 22.0 %collective-permute-start.17 = (bf16[2,64,2048]{2,1,0:T(8,128)(2,1)S(1)}, bf16[2,64,2048]{2,1,0:T(8,128)(2,1)S(1)}, u32[]{:S(2)}, u32[]{:S(2)}) collective-permute-start(bf16[2,64,2048]{2,1,0:T(8,128)(2,1)S(1)} %slice_bitcast_fusion.10), channel_id=1, source_target_pairs={{2,0},{4,2},{6,4},{0,6},{3,1},{5,3},{7,5},{1,7},{10,8},{12,10},{14... | collective-permute-start | bytes 1572872 | tf_op jit(solution)/shard_map/ppermute | solution.py:55
  568.2 19.5 %collective-permute-start.18 = (bf16[2,64,2048]{2,1,0:T(8,128)(2,1)S(1)}, bf16[2,64,2048]{2,1,0:T(8,128)(2,1)S(1)}, u32[]{:S(2)}, u32[]{:S(2)}) collective-permute-start(bf16[2,64,2048]{2,1,0:T(8,128)(2,1)S(1)} %fusion.19), channel_id=1, source_target_pairs={{2,0},{4,2},{6,4},{0,6},{3,1},{5,3},{7,5},{1,7},{10,8},{12,10},{14... | collective-permute-start | bytes 1572872 | tf_op jit(solution)/shard_map/ppermute | solution.py:55
  572.6 174.6 %collective-permute-start.36 = (bf16[1408,2048]{1,0:T(8,128)(2,1)}, bf16[1408,2048]{1,0:T(8,128)(2,1)}, u32[]{:S(2)}, u32[]{:S(2)}) collective-permute-start(bf16[1408,2048]{1,0:T(8,128)(2,1)} %convolution_convert_fusion), channel_id=1, source_target_pairs={{1,0},{0,1},{3,2},{2,3},{5,4},{4,5},{7,6},{6,7},{9,8},{8,9},{11,10... | collective-permute-start | bytes 17301512 | tf_op jit(solution)/shard_map/ppermute | solution.py:55
  588.9 27.1 %collective-permute-start.19 = (bf16[2,64,2048]{2,1,0:T(8,128)(2,1)S(1)}, bf16[2,64,2048]{2,1,0:T(8,128)(2,1)S(1)}, u32[]{:S(2)}, u32[]{:S(2)}) collective-permute-start(bf16[2,64,2048]{2,1,0:T(8,128)(2,1)S(1)} %fusion.18), channel_id=1, source_target_pairs={{2,0},{4,2},{6,4},{0,6},{3,1},{5,3},{7,5},{1,7},{10,8},{12,10},{14... | collective-permute-start | bytes 1572872 | tf_op jit(solution)/shard_map/ppermute | solution.py:55
  593.3 20.0 %copy-start.15 = (bf16[128,2048]{1,0:T(8,128)(2,1)S(1)}, bf16[128,2048]{1,0:T(8,128)(2,1)}, u32[]{:S(2)}) copy-start(bf16[128,2048]{1,0:T(8,128)(2,1)} %multiply_convert_fusion) | copy-start | bytes 1572868
  593.3 20.3 %copy-start.8 = (bf16[2,4,128,2048]{3,2,0,1:T(8,128)(2,1)S(1)}, bf16[2,4,128,2048]{3,2,0,1:T(8,128)(2,1)}, u32[]{:S(2)}) copy-start(bf16[2,4,128,2048]{3,2,0,1:T(8,128)(2,1)} %fusion) | copy-start | bytes 12582916
  676.6 30.9 %all-to-all-start.4 = ((f32[16,1,128]{2,1,0:T(1,128)}), f32[16,1,128]{2,1,0:T(1,128)S(1)}, u32[]{:S(2)}, u32[]{:S(2)}) async-start(f32[16,1,128]{2,1,0:T(1,128)} %get-tuple-element.107), calls=%async_computation.5 | async-start | bytes 16384 | tf_op jit(solution)/shard_map/all_to_all | solution.py:135
  685.0 191.5 %reduce-scatter.5.cloned.1.call-start = ((), (), s32[]{:S(2)}) async-start(), calls=%async_computation.14 | async-start | bytes 8912896 | tf_op jit(solution)/shard_map/reduce_scatter | solution.py:145
  687.4 35.7 %collective-permute-start.23 = (bf16[4,64,2048]{2,1,0:T(8,128)(2,1)}, bf16[4,64,2048]{2,1,0:T(8,128)(2,1)}, u32[]{:S(2)}, u32[]{:S(2)}) collective-permute-start(bf16[4,64,2048]{2,1,0:T(8,128)(2,1)} %slice_bitcast_fusion.4), channel_id=1, source_target_pairs={{16,0},{0,16},{17,1},{1,17},{18,2},{2,18},{19,3},{3,19},{20,4},{4,... | collective-permute-start | bytes 3145736 | tf_op jit(solution)/shard_map/ppermute | solution.py:55
  707.5 18.6 %collective-permute-start.21 = (bf16[2,512,1024]{2,1,0:T(8,128)(2,1)}, bf16[2,512,1024]{2,1,0:T(8,128)(2,1)}, u32[]{:S(2)}, u32[]{:S(2)}) collective-permute-start(bf16[2,512,1024]{2,1,0:T(8,128)(2,1)} %fusion.2), channel_id=1, source_target_pairs={{0,8},{8,0},{1,9},{9,1},{2,10},{10,2},{3,11},{11,3},{4,12},{12,4},... | collective-permute-start | bytes 6291464 | tf_op jit(solution)/shard_map/ppermute | solution.py:199
  709.2 13.0 %collective-permute-start.29 = (f32[12,2048]{1,0:T(8,128)S(1)}, f32[12,2048]{1,0:T(8,128)}, u32[]{:S(2)}, u32[]{:S(2)}) collective-permute-start(f32[12,2048]{1,0:T(8,128)S(1)} %concatenate.40), channel_id=1, source_target_pairs={{0,1},{1,0},{2,3},{3,2},{4,5},{5,4},{6,7},{7,6},{8,9},{9,8},{10,11... | collective-permute-start | bytes 294920 | tf_op jit(solution)/shard_map/ppermute | solution.py:104
  733.8 37.8 %collective-permute-start.22 = (bf16[4,2,64,1024]{3,2,1,0:T(8,128)(2,1)}, bf16[4,2,64,1024]{3,2,1,0:T(8,128)(2,1)}, u32[]{:S(2)}, u32[]{:S(2)}) collective-permute-start(bf16[4,2,64,1024]{3,2,1,0:T(8,128)(2,1)} %bitcast.67), channel_id=1, source_target_pairs={{16,0},{0,16},{17,1},{1,17},{18,2},{2,18},{19,3},{3,19},{20,4},{4,... | collective-permute-start | bytes 3145736 | tf_op jit(solution)/shard_map/ppermute | solution.py:55
  746.7 46.8 %collective-permute-start.34 = (bf16[4,256,512]{2,1,0:T(8,128)(2,1)}, bf16[4,256,512]{2,1,0:T(8,128)(2,1)}, u32[]{:S(2)}, u32[]{:S(2)}) collective-permute-start(bf16[4,256,512]{2,1,0:T(8,128)(2,1)} %select_bitcast_fusion), channel_id=1, source_target_pairs={{1,0},{0,1},{3,2},{2,3},{5,4},{4,5},{7,6},{6,7},{9,8},{8,9},{11,10... | collective-permute-start | bytes 3145736 | tf_op jit(solution)/shard_map/ppermute | solution.py:55
  771.9 20.4 %collective-permute-start.24 = (bf16[64,2048]{1,0:T(8,128)(2,1)S(1)}, bf16[64,2048]{1,0:T(8,128)(2,1)S(1)}, u32[]{:S(2)}, u32[]{:S(2)}) collective-permute-start(bf16[64,2048]{1,0:T(8,128)(2,1)S(1)} %slice_bitcast_fusion.26), channel_id=1, source_target_pairs={{2,0},{4,2},{6,4},{0,6},{3,1},{5,3},{7,5},{1,7},{10,8},{12,10},{14... | collective-permute-start | bytes 786440 | tf_op jit(solution)/shard_map/ppermute | solution.py:55
  776.8 16.7 %copy-start.10 = (f32[2048,512]{1,0:T(8,128)S(1)}, f32[2048,512]{1,0:T(8,128)}, u32[]{:S(2)}) copy-start(f32[2048,512]{1,0:T(8,128)} %copy-done.9) | copy-start | bytes 12582916
  776.9 15.5 %collective-permute-start.28 = (bf16[4,64,1024]{2,1,0:T(8,128)(2,1)S(1)}, bf16[4,64,1024]{2,1,0:T(8,128)(2,1)S(1)}, u32[]{:S(2)}, u32[]{:S(2)}) collective-permute-start(bf16[4,64,1024]{2,1,0:T(8,128)(2,1)S(1)} %fusion.24), channel_id=1, source_target_pairs={{1,0},{0,1},{3,2},{2,3},{5,4},{4,5},{7,6},{6,7},{9,8},{8,9},{11,10... | collective-permute-start | bytes 1572872 | tf_op jit(solution)/shard_map/ppermute | solution.py:55
  778.8 27.3 %collective-permute-start.27 = (bf16[64,2048]{1,0:T(8,128)(2,1)S(1)}, bf16[64,2048]{1,0:T(8,128)(2,1)S(1)}, u32[]{:S(2)}, u32[]{:S(2)}) collective-permute-start(bf16[64,2048]{1,0:T(8,128)(2,1)S(1)} %slice_bitcast_fusion.25), channel_id=1, source_target_pairs={{16,0},{0,16},{17,1},{1,17},{18,2},{2,18},{19,3},{3,19},{20,4},{4,... | collective-permute-start | bytes 786440 | tf_op jit(solution)/shard_map/ppermute | solution.py:55
  779.1 91.4 %collective-permute-start.35 = (bf16[256,2048]{1,0:T(8,128)(2,1)}, bf16[256,2048]{1,0:T(8,128)(2,1)}, u32[]{:S(2)}, u32[]{:S(2)}) collective-permute-start(bf16[256,2048]{1,0:T(8,128)(2,1)} %slice_select_fusion), channel_id=1, source_target_pairs={{1,0},{0,1},{3,2},{2,3},{5,4},{4,5},{7,6},{6,7},{9,8},{8,9},{11,10... | collective-permute-start | bytes 3145736 | tf_op jit(solution)/shard_map/ppermute | solution.py:55
  792.4 7.9 collective-permute-start.25
  793.5 3.0 collective-permute-start.30
  796.5 6.9 collective-permute-start.31
  801.0 27.9 %collective-permute-start.26 = (bf16[64,2048]{1,0:T(8,128)(2,1)}, bf16[64,2048]{1,0:T(8,128)(2,1)}, u32[]{:S(2)}, u32[]{:S(2)}) collective-permute-start(bf16[64,2048]{1,0:T(8,128)(2,1)} %fusion.27), channel_id=1, source_target_pairs={{2,0},{4,2},{6,4},{0,6},{3,1},{5,3},{7,5},{1,7},{10,8},{12,10},{14... | collective-permute-start | bytes 786440 | tf_op jit(solution)/shard_map/ppermute | solution.py:55
  804.0 16.4 %collective-permute-start.32 = (f32[12,2048]{1,0:T(8,128)}, f32[12,2048]{1,0:T(8,128)}, u32[]{:S(2)}, u32[]{:S(2)}) collective-permute-start(f32[12,2048]{1,0:T(8,128)} %add.191), channel_id=1, source_target_pairs={{0,4},{2,6},{4,0},{6,2},{1,5},{3,7},{5,1},{7,3},{8,12},{10,14},{12... | collective-permute-start | bytes 294920 | tf_op jit(solution)/shard_map/ppermute | solution.py:104
  806.1 31.8 %all-to-all-start.5 = ((bf16[4,64,1024]{2,1,0:T(8,128)(2,1)}), bf16[4,64,1024]{2,1,0:T(8,128)(2,1)}, u32[]{:S(2)}, u32[]{:S(2)}) async-start(bf16[4,64,1024]{2,1,0:T(8,128)(2,1)} %fusion.23), calls=%async_computation.7 | async-start | bytes 1048576 | tf_op jit(solution)/shard_map/all_to_all | solution.py:162
  821.4 10.4 %collective-permute-start.33 = (f32[12,2048]{1,0:T(8,128)S(1)}, f32[12,2048]{1,0:T(8,128)S(1)}, u32[]{:S(2)}, u32[]{:S(2)}) collective-permute-start(f32[12,2048]{1,0:T(8,128)S(1)} %add.192), channel_id=1, source_target_pairs={{0,16},{16,0},{1,17},{17,1},{2,18},{18,2},{3,19},{19,3},{4,20},{20... | collective-permute-start | bytes 294920 | tf_op jit(solution)/shard_map/ppermute | solution.py:104
  837.9 32.5 %all-to-all-start.6 = ((bf16[4,256,512]{2,1,0:T(8,128)(2,1)}), bf16[4,256,512]{2,1,0:T(8,128)(2,1)}, u32[]{:S(2)}, u32[]{:S(2)}) async-start(bf16[4,256,512]{2,1,0:T(8,128)(2,1)} %fusion.5), calls=%async_computation.8 | async-start | bytes 2097152 | tf_op jit(solution)/shard_map/all_to_all | solution.py:162
  (43 other events, 193.1 us)
Sparse Core Ops, SparseCore 0:
  11.9 106.4 all-gather.6
  121.8 77.9 all-gather.4
  270.0 76.5 all-gather.8
  428.5 105.5 reduce-scatter.2
  544.1 92.7 all-gather.10
  722.3 121.9 reduce-scatter.4

commit v12 on v11

--- a/solution.py
+++ b/solution.py
@@ -162,7 +162,7 @@
     return lax.all_to_all(blocks, "o", split_axis=0, concat_axis=0, tiled=True)
 
 
-def gather_heads(places, query_weight, kv_weight, beside):
+def gather_heads(query_weight, kv_weight, beside):
     whole = HEADS * HD
     rows = query_weight.shape[0]
     here = exchange(
@@ -183,34 +183,37 @@
     kv = after(kv, query)
     query = in_order(query, "i", 1).reshape(-1, span)
     seen = kv[-1][0, 0, 0, 0]
-    kv = jnp.stack(ring_gather(jnp.stack(kv), "c"))
-    return query, arrange(places, kv), seen
+    return query, ring_gather(jnp.stack(kv), "c"), seen
 
 
 def scatter_query(grad, *others):
     inner = lax.axis_size("i")
     blocks = grad.reshape(OUTER, inner, -1, grad.shape[1])
     blocks = from_order([blocks[:, k] for k in range(inner)], "i")
-    mine = ring_scatter(blocks[:1] + list(after(blocks[1:], *others)), "i").astype(BF16)
-    return exchange(mine)
+    return ring_scatter(blocks[:1] + list(after(blocks[1:], *others)), "i").astype(BF16)
 
 
 def scatter_kv(kept, sent):
     mine = lax.ppermute(sent, "c", [(0, 1), (1, 0)]).astype(F32) + kept
     high, inner = lax.axis_size("y"), lax.axis_size("i")
-    wide = kept.shape[-1]
-    mine = mine.reshape(high, OUTER, inner, -1, wide)
+    mine = mine.reshape(high, OUTER, inner, -1, kept.shape[-1])
     blocks = from_order([mine[k] for k in range(high)], "y")
     sent = blocks[1].astype(BF16)
     own, arrived = ring_open([blocks[0], sent] + blocks[2:], "y")
     mine = arrived.astype(F32) + own
     mine = ring_scatter(from_order([mine[:, k] for k in range(inner)], "i"), "i").astype(BF16)
-    here = exchange(mine)
-    half = wide // 2
-    whole = jnp.concatenate(
-        [join_blocks(here[:, :, :half]), join_blocks(here[:, :, half:])], axis=1
-    )
-    return whole.astype(F32), sent, arrived, mine
+    return mine, sent, arrived
+
+
+def scatter_heads(query, kv, *others):
+    half = kv.shape[2] // 2
+    rows, kv_rows = query.shape[1], kv.shape[1]
+    sent = jnp.concatenate([query, kv[:, :, :half], kv[:, :, half:]], axis=1)
+    here = exchange(after(sent, *others)).astype(F32)
+    whole = [
+        join_blocks(here[:, rows + k * kv_rows : rows + (k + 1) * kv_rows]) for k in range(2)
+    ]
+    return join_blocks(here[:, :rows]), jnp.concatenate(whole, axis=1)
 
 
 def own_places():
@@ -228,8 +231,8 @@
     return add_low(shift(travelling, axis), blocks[0])
 
 
-def part_low(rows):
-    return ring_low([rows[k] for k in range(rows.shape[0])], "c")
+def part_low(own, other):
+    return ring_low([own, other], "c")
 
 
 def part_first(rows):
@@ -300,18 +303,26 @@
 
 
 def place_rows(places_ref, part_ref, value, length):
-    count = part_ref.shape[2]
+    count = part_ref.shape[1]
     for seq in range(count):
         slot = lax.rem(seq - places_ref[2] + count, count)
-        part_ref[0, 0, slot] = value[seq * length : (seq + 1) * length]
-
-
-def arrange_kernel(places_ref, in_ref, out_ref):
-    del places_ref
-    half = in_ref.shape[-1]
-    for outer in range(OUTER):
-        out_ref[0, 0, outer, 0, :, :half] = in_ref[0, 0, 0, outer, 0]
-        out_ref[0, 0, outer, 0, :, half:] = in_ref[0, 0, 0, outer, 1]
+        part_ref[0, slot] = value[seq * length : (seq + 1) * length]
+
+
+def arrange(places_ref, part_refs, out_ref):
+    high, inner, outer, kinds, rows, span = part_refs[0].shape
+    for low, part_ref in enumerate(part_refs):
+        c = lax.rem(low + places_ref[1], 2)
+        for first in range(high):
+            y = lax.rem(first + places_ref[0], high)
+            for second in range(inner):
+                i = lax.rem(second + places_ref[3], inner)
+                for o in range(outer):
+                    start = (((y * 2 + c) * outer + o) * inner + i) * rows
+                    for kind in range(kinds):
+                        out_ref[
+                            pl.ds(pl.multiple_of(start, 16), rows), kind * span : (kind + 1) * span
+                        ] = part_ref[first, second, o, kind]
 
 
 def attend_kernel(
@@ -321,11 +332,16 @@
     cos_ref,
     sin_ref,
     query_ref,
-    kv_ref,
+    own_ref,
+    other_ref,
     qkv_ref,
     gated_ref,
+    kv_ref,
 ):
-    del places_ref
+    @pl.when(pl.program_id(0) == 0)
+    def _():
+        arrange(places_ref, (own_ref, other_ref), kv_ref)
+
     length = cos_ref.shape[0]
     span = query_ref.shape[1]
     raw_query = nn(x_ref[...], query_ref[...])
@@ -408,12 +424,21 @@
 
 
 def rows_kernel(parts, places_ref, *refs):
-    gated_refs, down_refs, part_ref = refs[:parts], refs[parts : 2 * parts], refs[2 * parts]
-    length = part_ref.shape[3]
+    gated_refs, down_refs, (own_ref, other_ref) = refs[:parts], refs[parts : 2 * parts], refs[2 * parts :]
+    length = own_ref.shape[2]
     value = nn(gated_refs[0][...], down_refs[0][...])
     for part in range(1, parts):
         value = value + nn(gated_refs[part][...], down_refs[part][...])
-    place_rows(places_ref, part_ref, value.astype(BF16), length)
+    value = value.astype(BF16)
+    other_first = pl.num_programs(0) // 2
+
+    @pl.when(pl.program_id(0) < other_first)
+    def _():
+        place_rows(places_ref, other_ref, value, length)
+
+    @pl.when(pl.program_id(0) >= other_first)
+    def _():
+        place_rows(places_ref, own_ref, value, length)
 
 
 def fixed(shape):
@@ -426,14 +451,6 @@
 
 def info_spec(seqs, kinds, length):
     return pl.BlockSpec((seqs, kinds, length), lambda step, places: (step, 0, 0))
-
-
-def place_spec(high, length, width):
-    def index(step, places):
-        low = lax.rem(lax.rem(step, 2) - places[1] + 2, 2)
-        return (low, lax.rem(lax.div(step, 2) - places[0] + high, high), 0, 0, 0)
-
-    return pl.BlockSpec((1, 1, OUTER, length, width), index)
 
 
 def shape(dims, dtype=BF16):
@@ -453,49 +470,7 @@
     )(*operands)
 
 
-def arrange(places, value):
-    low, high, inner, outer, kinds, rows, span = value.shape
-
-    def index(step, places):
-        y = lax.div(step, 2 * inner)
-        c = lax.rem(lax.div(step, inner), 2)
-        i = lax.rem(step, inner)
-        return (
-            lax.rem(c - places[1] + 2, 2),
-            lax.rem(y - places[0] + high, high),
-            lax.rem(i - places[3] + inner, inner),
-            0,
-            0,
-            0,
-            0,
-        )
-
-    def out_index(step, places):
-        return (
-            lax.div(step, 2 * inner),
-            lax.rem(lax.div(step, inner), 2),
-            0,
-            lax.rem(step, inner),
-            0,
-            0,
-        )
-
-    dims = (high, low, outer, inner, rows, kinds * span)
-    found = call(
-        arrange_kernel,
-        "arrange",
-        high * low * inner,
-        [pl.BlockSpec((1, 1, 1, outer, kinds, rows, span), index)],
-        pl.BlockSpec((1, 1, outer, 1, rows, kinds * span), out_index),
-        shape(dims),
-        0,
-        4 * value.size,
-        (places, value),
-    )
-    return found.reshape(-1, kinds * span)
-
-
-def attend(places, rows, info, cosine, sine, query_mat, kv_mat):
+def attend(places, rows, info, cosine, sine, query_mat, kv_parts):
     count, width = rows.shape
     span = query_mat.shape[1]
     length = cosine.shape[0]
@@ -510,13 +485,13 @@
             fixed(cosine.shape),
             fixed(sine.shape),
             fixed(query_mat.shape),
-            fixed(kv_mat.shape),
+            *[fixed(one.shape) for one in kv_parts],
         ],
-        [rows_spec(step, 3 * span), rows_spec(step, span)],
-        [shape((count, 3 * span)), shape((count, span))],
+        [rows_spec(step, 3 * span), rows_spec(step, span), fixed((width, 2 * span))],
+        [shape((count, 3 * span)), shape((count, span)), shape((width, 2 * span))],
         2 * count * width * 3 * span + 4 * count * length * span,
         4 * count * (width + 2 * span),
-        (places, rows, info, cosine, sine, query_mat, kv_mat),
+        (places, rows, info, cosine, sine, query_mat, *kv_parts),
     )
 
 
@@ -560,22 +535,31 @@
     )
 
 
-def ring_rows(places, gated_units, down_parts, length):
-    count, units = gated_units[0].shape
-    width = down_parts[0].shape[1]
-    parts = len(down_parts)
+def ring_rows(places, gated, mats, length):
+    count, units = gated[0].shape
+    width = mats[0].shape[1]
+    parts = len(mats)
     step = OUTER * length
     high = count // (2 * step)
+
+    def pair(number, places):
+        c = lax.rem(lax.div(number, high) + 1 + places[1], 2)
+        return (lax.rem(lax.rem(number, high) + places[0], high) * 2 + c, 0)
+
+    block = (1, OUTER, length, width)
     return call(
         functools.partial(rows_kernel, parts),
         "rows",
         count // step,
-        [rows_spec(step, units)] * parts + [fixed(down.shape) for down in down_parts],
-        place_spec(high, length, width),
-        shape((2, high, OUTER, length, width)),
+        [pl.BlockSpec((step, units), pair)] * parts + [fixed(one.shape) for one in mats],
+        [
+            pl.BlockSpec(block, lambda number, places: (lax.max(number - high, 0), 0, 0, 0)),
+            pl.BlockSpec(block, lambda number, places: (lax.min(number, high - 1), 0, 0, 0)),
+        ],
+        [shape((high, OUTER, length, width))] * 2,
         2 * count * width * units * parts,
         4 * count * (width + units * parts),
-        (places, *gated_units, *down_parts),
+        (places, *gated, *mats),
     )
 
 
@@ -671,9 +655,7 @@
     places = own_places()
 
     down_parts = ring_gather(down_weight[0], "i")
-    query_mat, kv_mat, seen = gather_heads(
-        places, query_weight[0], kv_weight, down_parts[1:]
-    )
+    query_mat, kv_parts, seen = gather_heads(query_weight[0], kv_weight, down_parts[1:])
     out_parts = ring_gather(after(out_weight[0], seen), "i")
     own_up = up_weight[0].reshape(-1, width)
 
@@ -684,10 +666,12 @@
     info = to_experts(att_gate, att_onehot, segment_ids[0].astype(F32))
     all_attn = meet(attn_input)
     all_cot = meet(after(cotangent.astype(BF16), seen))
-    qkv, gated = attend(places, all_attn, info, cosine, sine_table, query_mat, kv_mat)
+    qkv, gated, kv_mat = attend(
+        places, all_attn, info, cosine, sine_table, query_mat, kv_parts
+    )
     out_parts = out_parts[:1] + list(after(out_parts[1:], gated))
     out_mat = in_order(out_parts, "i").reshape(span, width)
-    branch = part_low(ring_rows(places, [gated], [out_mat], tokens))
+    branch = part_low(*ring_rows(places, [gated], [out_mat], tokens))
     branch = part_second(*part_first(branch))
 
     d_units = [mm("td,fd->tf", all_cot, down).astype(BF16) for down in down_parts]
@@ -722,7 +706,7 @@
     grad_down = [mm("tf,td->fd", here, all_cot) for here in gated_units]
     low_up = [one.astype(BF16) for one in grad_up[1:]]
     low_down = [one.astype(BF16) for one in grad_down[1:]]
-    rows_out = part_low(ring_rows(places, gated_units, down_parts, tokens))
+    rows_out = part_low(*ring_rows(places, gated_units, down_parts, tokens))
     half = tokens // 2
     rows_first, rows_second = rows_out[:, :, :half], rows_out[:, :, half:]
     lower_own, lower_last = ring_open(grad_down[:1] + low_down, "i")
@@ -756,7 +740,7 @@
     d_kv_mat = mm("td,tf->df", all_attn, d_kv).reshape(experts // 2, 2, -1, 2 * span)
     d_kv_mat = from_order([d_kv_mat[:, 0], d_kv_mat[:, 1]], "c")
     d_kv_sent = d_kv_mat[1].astype(BF16)
-    d_kv_weight, kv_sent, kv_arrived, kv_last = scatter_kv(d_kv_mat[0], d_kv_sent)
+    d_kv_last, kv_sent, kv_arrived = scatter_kv(d_kv_mat[0], d_kv_sent)
     d_heads, all_mid = after((d_heads, all_mid), kv_sent)
     d_att_router, d_att_from_router = gates_back(
         att_gate, att_onehot, d_att_gate, attn_input, att_router
@@ -765,17 +749,18 @@
         d_att_from_router * residual * inverse_one, axis=0, keepdims=True
     )
     summed = sum_over(jnp.concatenate([d_gain_one, sums, d_att_router]), ("i",))
-    d_query = scatter_query(mm("td,tf->df", all_attn, d_heads), summed)
+    d_query_last = scatter_query(mm("td,tf->df", all_attn, d_heads), summed)
+    d_query, d_kv_weight = scatter_heads(d_query_last, d_kv_last, d_attn_input)
+    d_query = d_query[None]
     d_out = mm("tf,td->fd", gated, all_mid).reshape(inner, -1, width)
     d_out = from_order([d_out[k] for k in range(inner)], "i")
     d_out = d_out[:1] + list(after(d_out[1:], kv_arrived))
     d_output = ring_scatter(d_out, "i", d_query)[None]
-    d_query = join_blocks(d_query).astype(F32)[None]
     rows_out = part_second(*after((rows_first, rows_second), kv_arrived))
     layer_out = middle + rows_out.astype(F32) + mlp_bias
     d_upper = (after(upper_last, kv_sent).astype(F32) + upper_own).reshape(up_weight.shape)
     d_lower = (lower_last.astype(F32) + lower_own)[None]
-    summed = sum_over(after(summed, kv_last), ("c", "o", "y"))
+    summed = sum_over(after(summed, d_kv_last), ("c", "o", "y"))
     d_attn_input = after(d_attn_input, summed)
     d_norm_one, _ = norm_back(
         residual, inverse_one, norm_gain1, d_attn_input.astype(F32) + d_att_from_router

time: 892 us -> 881 us (0.988)
  waiting for transfers between devices: 335 us -> 348 us
  local copies, waits for them, and re-layouts: 43.4 us -> 31.5 us
    ppermute x31, starting transfers between devices: 62.4 us -> 77.2 us  [shift(): return lax.ppermute(value, axis, [((k + 1) % size, k) for k in range(size)])]
    slice x3 -> x1, local copies, waits for them, and re-layouts: 10.6 us -> 0.04 us  [scatter_heads(): sent = jnp.concatenate([query, kv[:, :, :half], kv[:, :, half:]], axis=1)]
    ppermute x5, starting transfers between devices: 12.9 us -> 2.39 us  [sum_over(): lax.ppermute(value, axis, [(k, k ^ step) for k in range(size)])]
    unnamed x125 -> x133, local copies, waits for them, and re-layouts: 22.6 us -> 13.2 us
    all_to_all x3 -> x2, waiting for transfers between devices: 22.6 us -> 30.1 us  [exchange(): return lax.all_to_all(blocks, 'o', split_axis=0, concat_axis=0, tiled=True)]
    pallas_call x7 -> x6, Pallas kernels: 173 us -> 170 us  [call(): pl.pallas_call(kernel, grid_spec=pltpu.PrefetchScalarGridSpec(num_scalar_...]
  transfers between devices with their start and end apart: 49 -> 48, of which waited for: 22 -> 23; matrix products, arithmetic and copies ran while one was open for 24% -> 23% of each run, Pallas kernels for 15% -> 15%
where the time goes in v12:
time: 881 us; the launch traced here: 877 us
  waiting for transfers between devices  348 us (40%)
  Pallas kernels  170 us (19%)
  matrix products  110 us (12%)
  starting transfers between devices  108 us (12%)
  other arithmetic  81.4 us (9%)
  local copies, waits for them, and re-layouts  31.5 us (4%)
  between operations  15.4 us (2%)
  blocking collectives  13 us (1%)
    ppermute x31, waiting for transfers between devices, shift(): return lax.ppermute(value, axis, [((k + 1) % size, k) for k in range(size)])  227 us
    pallas_call x6, Pallas kernels, call(): pl.pallas_call(kernel, grid_spec=pltpu.PrefetchScalarGridSpec(num_scalar_...  170 us
    dot_general x9, matrix products, mm(): return jnp.einsum(form, first, second, preferred_element_type=F32)  104 us
    all_gather x4, waiting for transfers between devices, meet(): return lax.all_gather(rows, GROUP, axis=0, tiled=True)  78.6 us
    ppermute x31, starting transfers between devices, shift(): return lax.ppermute(value, axis, [((k + 1) % size, k) for k in range(size)])  77.2 us
    all_to_all x2, waiting for transfers between devices, exchange(): return lax.all_to_all(blocks, 'o', split_axis=0, concat_axis=0, tiled=True)  30.1 us
    convert_element_type x18, other arithmetic, add_low(): return (first.astype(F32) + second.astype(F32)).astype(BF16)  19.2 us
  transfers between devices with their start and end apart: 48, of which 23 were waited for; matrix products, arithmetic and copies ran while one was open for 23% of the time, Pallas kernels for 15%

profile of v12, /device:TPU:0, one launch (start us, length us, event | category | flops | bytes accessed | tf_op | source)
XLA Modules:
  0.0 877.5 jit_solution(1802802230417358446)
XLA Ops:
  11.2 3.0 collective-permute-start
  16.8 4.9 all-to-all-start
  21.6 55.4 %collective-permute-done.refs_3_ = bf16[704,2048]{1,0:T(8,128)(2,1)} collective-permute-done((bf16[704,2048]{1,0:T(8,128)(2,1)}, bf16[704,2048]{1,0:T(8,128)(2,1)}, u32[]{:S(2)}, u32[]{:S(2)}) %collective-permute-start) | collective-permute-done | bytes 2883616 | tf_op jit(solution)/shard_map/ppermute | solution.py:55
  79.0 11.3 %collective-permute-done.1 = bf16[4,2,64,512]{3,2,1,0:T(8,128)(2,1)S(1)} collective-permute-done((bf16[4,2,64,512]{3,2,1,0:T(8,128)(2,1)S(1)}, bf16[4,2,64,512]{3,2,1,0:T(8,128)(2,1)S(1)}, u32[]{:S(2)}, u32[]{:S(2)}) %collective-permute-start.1) | collective-permute-done | bytes 524320 | tf_op jit(solution)/shard_map/ppermute | solution.py:55
  94.9 18.9 %collective-permute-done.2 = bf16[4,256,512]{2,1,0:T(8,128)(2,1)S(1)} collective-permute-done((bf16[4,256,512]{2,1,0:T(8,128)(2,1)S(1)}, bf16[4,256,512]{2,1,0:T(8,128)(2,1)S(1)}, u32[]{:S(2)}, u32[]{:S(2)}) %collective-permute-start.2) | collective-permute-done | bytes 1048608 | tf_op jit(solution)/shard_map/ppermute | solution.py:55
  113.8 6.3 collective-permute-done.3
  121.1 3.1 pad_maximum_fusion.1.own_ref
  126.0 4.8 all-to-all-start.1
  137.9 26.2 %attend.1 = (bf16[2048,1536]{1,0:T(8,128)(2,1)}, bf16[2048,512]{1,0:T(8,128)(2,1)}, bf16[2048,1024]{1,0:T(8,128)(2,1)}) custom-call(s32[4]{0:T(128)} %pad_add_fusion.places_ref, bf16[2048,2048]{1,0:T(8,128)(2,1)} %all-gather.7.cloned.1.call-done.x_ref, f32[16,2,128]{2,1,0:T(2,128)} %copy-done.39, f32[128,128]{1,0:T(8,128)} %get-tuple-element.185.cos_ref, ...), custom_call_target="tpu_custom_call" | custom-call | flops 13421772800 | bytes 25165824 | tf_op jit(solution)/shard_map/attend/pallas_call | solution.py:461
  167.0 10.5 %rows.2 = (bf16[2,4,128,2048]{3,2,1,0:T(8,128)(2,1)}, bf16[2,4,128,2048]{3,2,1,0:T(8,128)(2,1)}) custom-call(s32[4]{0:T(128)} %pad_add_fusion.places_ref, bf16[2048,512]{1,0:T(8,128)(2,1)} %get-tuple-element.86.refs_0_, bf16[512,2048]{1,0:T(8,128)(2,1)} %bitcast.320), custom_call_target="tpu_custom_call" | custom-call | flops 4294967296 | bytes 20971520 | tf_op jit(solution)/shard_map/rows/pallas_call | solution.py:461
  177.6 2.7 copy.72
  180.4 7.3 collective-permute-done.6
  190.1 14.4 %collective-permute-start.11 = (bf16[2,64,2048]{2,1,0:T(8,128)(2,1)S(1)}, bf16[2,64,2048]{2,1,0:T(8,128)(2,1)S(1)}, u32[]{:S(2)}, u32[]{:S(2)}) collective-permute-start(bf16[2,64,2048]{2,1,0:T(8,128)(2,1)S(1)} %slice_bitcast_fusion.18), channel_id=1, source_target_pairs={{2,0},{4,2},{6,4},{0,6},{3,1},{5,3},{7,5},{1,7},{10,8},{12,10},{14... | collective-permute-start | bytes 1572872 | tf_op jit(solution)/shard_map/ppermute | solution.py:55
  206.9 9.3 %collective-permute-done.11 = bf16[2,64,2048]{2,1,0:T(8,128)(2,1)S(1)} collective-permute-done((bf16[2,64,2048]{2,1,0:T(8,128)(2,1)S(1)}, bf16[2,64,2048]{2,1,0:T(8,128)(2,1)S(1)}, u32[]{:S(2)}, u32[]{:S(2)}) %collective-permute-start.11) | collective-permute-done | bytes 524320 | tf_op jit(solution)/shard_map/ppermute | solution.py:55
  216.3 4.3 collective-permute-start.12
  220.7 11.3 %convolution_convert_fusion.1.d_units_ref = bf16[2048,704]{1,0:T(8,128)(2,1)} fusion(bf16[2048,2048]{1,0:T(8,128)(2,1)} %all-gather.5.cloned.1.call-done, bf16[704,2048]{1,0:T(8,128)(2,1)} %collective-permute-done.refs_3_), kind=kOutput, calls=%fused_computation.9 | convolution fusion | flops 5907021824 | bytes 14155776 | tf_op jit(solution)/shard_map/td,fd->tf/dot_general | solution.py:149
  232.1 3.9 collective-permute-start.13
  236.6 8.1 convolution_convert_fusion.2.d_units_ref
  244.6 7.0 collective-permute-done.8
  251.7 4.3 collective-permute-start.9
  256.9 3.1 collective-permute-done.9
  260.0 4.3 collective-permute-start.10
  264.4 3.8 collective-permute-done.10
  272.0 13.0 %all_to_all.32.info_ref = f32[16,1,128]{2,1,0:T(1,128)} all-to-all(f32[16,1,128]{2,1,0:T(1,128)S(1)} %bitcast.333), channel_id=1, replica_groups=mesh['y'=2,'c'=2,'o'=4,'i'=2] {'y','c','o'}, dimensions={0} | all-to-all | bytes 16384 | tf_op jit(solution)/shard_map/all_to_all | solution.py:131
  285.0 60.8 %all-gather.9.cloned.1.call-done.x_ref = bf16[2048,2048]{1,0:T(8,128)(2,1)} async-done(((bf16[128,2048]{1,0:T(8,128)(2,1)}), bf16[2048,2048]{1,0:T(8,128)(2,1)}) %all-gather.9.cloned.1.call-update) | async-done | bytes 8388624 | tf_op jit(solution)/shard_map/all_gather | solution.py:141
  345.8 35.5 %units.2 = (bf16[2048,1408]{1,0:T(8,128)(2,1)}, bf16[2048,704]{1,0:T(8,128)(2,1)}, f32[2048,2048]{1,0:T(8,128)}, f32[16,1,128]{2,1,0:T(1,128)}) custom-call(s32[4]{0:T(128)} %pad_add_fusion.places_ref, bf16[2048,2048]{1,0:T(8,128)(2,1)} %all-gather.9.cloned.1.call-done.x_ref, f32[16,1,128]{2,1,0:T(1,128)} %all_to_all.32.info_ref, ...), custom_call_target="tpu_custom_call" | custom-call | tf_op jit(solution)/shard_map/units/pallas_call | solution.py:461
  381.3 10.8 %collective-permute-done.15.first_ref.second_ref = bf16[1408,2048]{1,0:T(8,128)(2,1)} collective-permute-done((bf16[1408,2048]{1,0:T(8,128)(2,1)}, bf16[1408,2048]{1,0:T(8,128)(2,1)}, u32[]{:S(2)}, u32[]{:S(2)}) %collective-permute-start.15) | collective-permute-done | bytes 5767200 | tf_op jit(solution)/shard_map/ppermute | solution.py:55
  392.1 35.9 %units.3 = (bf16[2048,1408]{1,0:T(8,128)(2,1)}, bf16[2048,704]{1,0:T(8,128)(2,1)}, bf16[2048,2048]{1,0:T(8,128)(2,1)}, f32[16,1,128]{2,1,0:T(1,128)}) custom-call(s32[4]{0:T(128)} %pad_add_fusion.places_ref, bf16[2048,2048]{1,0:T(8,128)(2,1)} %all-gather.9.cloned.1.call-done.x_ref, f32[16,1,128]{2,1,0:T(1,128)} %all_to_all.32.info_ref, ...), custom_call_target="tpu_custom_call" | custom-call | tf_op jit(solution)/shard_map/units/pallas_call | solution.py:461
  429.3 5.4 all-to-all-start.3
  435.1 21.9 %rows.3 = (bf16[2,4,128,2048]{3,2,1,0:T(8,128)(2,1)}, bf16[2,4,128,2048]{3,2,1,0:T(8,128)(2,1)}) custom-call(s32[4]{0:T(128)} %pad_add_fusion.places_ref, bf16[2048,704]{1,0:T(8,128)(2,1)} %get-tuple-element.94.refs_0_, bf16[2048,704]{1,0:T(8,128)(2,1)} %get-tuple-element.98.refs_1_, bf16[704,2048]{1,0:T(8,128)(2,1)} %bitcast.349, ...), custom_call_target="tpu_custom_call" | custom-call | flops 11811160064 | bytes 28311552 | tf_op jit(solution)/shard_map/rows/pallas_call | solution.py:461
  457.1 5.1 copy.75
  462.6 10.4 %convolution_convert_fusion.3 = bf16[704,2048]{1,0:T(8,128)(2,1)} fusion(bf16[2048,704]{1,0:T(8,128)(2,1)S(1)} %copy-done.55, bf16[2048,2048]{1,0:T(8,128)(2,1)} %all-gather.5.cloned.1.call-done), kind=kOutput, calls=%fused_computation.11 | convolution fusion | flops 5907021824 | bytes 14155776 | tf_op jit(solution)/shard_map/tf,td->fd/dot_general | solution.py:149
  474.1 14.2 %convolution_convert_fusion = bf16[1408,2048]{1,0:T(8,128)(2,1)} fusion(bf16[2048,1408]{1,0:T(8,128)(2,1)S(1)} %bitcast.347, bf16[2048,2048]{1,0:T(8,128)(2,1)S(1)} %bitcast.307), kind=kOutput, calls=%fused_computation.3 | convolution fusion | flops 11814043648 | bytes 19922944 | tf_op jit(solution)/shard_map/tf,td->fd/dot_general | solution.py:149
  488.5 7.9 add_convert_fusion
  496.4 41.3 %collective-permute-done.20 = bf16[704,2048]{1,0:T(8,128)(2,1)} collective-permute-done((bf16[704,2048]{1,0:T(8,128)(2,1)}, bf16[704,2048]{1,0:T(8,128)(2,1)}, u32[]{:S(2)}, u32[]{:S(2)}) %collective-permute-start.20) | collective-permute-done | bytes 2883616 | tf_op jit(solution)/shard_map/ppermute | solution.py:55
  537.7 2.5 multiply_reduce_fusion
  542.8 3.8 collective-permute-start.17
  546.7 18.1 %collective-permute-done.17 = bf16[2,64,2048]{2,1,0:T(8,128)(2,1)S(1)} collective-permute-done((bf16[2,64,2048]{2,1,0:T(8,128)(2,1)S(1)}, bf16[2,64,2048]{2,1,0:T(8,128)(2,1)S(1)}, u32[]{:S(2)}, u32[]{:S(2)}) %collective-permute-start.17) | collective-permute-done | bytes 524320 | tf_op jit(solution)/shard_map/ppermute | solution.py:55
  565.9 4.3 collective-permute-start.18
  571.3 14.4 %collective-permute-done.18 = bf16[2,64,2048]{2,1,0:T(8,128)(2,1)S(1)} collective-permute-done((bf16[2,64,2048]{2,1,0:T(8,128)(2,1)S(1)}, bf16[2,64,2048]{2,1,0:T(8,128)(2,1)S(1)}, u32[]{:S(2)}, u32[]{:S(2)}) %collective-permute-start.18) | collective-permute-done | bytes 524320 | tf_op jit(solution)/shard_map/ppermute | solution.py:55
  586.9 4.4 collective-permute-start.19
  591.3 19.5 %fusion.60 = f32[1408,2048]{1,0:T(8,128)} fusion(bf16[2048,1408]{1,0:T(8,128)(2,1)} %get-tuple-element.138, bf16[2048,2048]{1,0:T(8,128)(2,1)} %all-gather.9.cloned.1.call-done.x_ref), kind=kOutput, calls=%fused_computation.201 | convolution fusion | flops 11811160064 | bytes 25690112 | tf_op jit(solution)/shard_map/tf,td->fd/dot_general | solution.py:149
  612.5 3.9 collective-permute-done.19
  617.4 17.8 %all-gather.11.cloned.1.call-done.mid_ref = bf16[2048,2048]{1,0:T(8,128)(2,1)} async-done(((bf16[128,2048]{1,0:T(8,128)(2,1)}), bf16[2048,2048]{1,0:T(8,128)(2,1)}) %all-gather.11.cloned.1.call-update) | async-done | bytes 8388624 | tf_op jit(solution)/shard_map/all_gather | solution.py:141
  635.3 39.7 %attend_back.1 = (bf16[2048,512]{1,0:T(8,128)(2,1)}, bf16[2048,1024]{1,0:T(8,128)(2,1)}, bf16[2048,2048]{1,0:T(8,128)(2,1)}, f32[16,1,128]{2,1,0:T(1,128)}, f32[1,2048]{1,0:T(1,128)}) custom-call(s32[4]{0:T(128)} %pad_add_fusion.places_ref, bf16[2048,2048]{1,0:T(8,128)(2,1)} %all-gather.11.cloned.1.call-done.mid_ref, f32[16,2,128]{2,1,0:T(2,128)} %copy-done.39, ...), custom_call_target="tpu_custom_call" | custom-call | flops 18522046464 | bytes 46137344 | tf_op jit(solution)/shard_map/attend_back/pallas_call | solution.py:461
  675.0 8.5 all-to-all-start.4
  687.9 13.8 %fusion.55 = f32[2048,1024]{1,0:T(8,128)S(1)} fusion(bf16[2048,2048]{1,0:T(8,128)(2,1)} %all-gather.7.cloned.1.call-done.x_ref, bf16[2048,1024]{1,0:T(8,128)(2,1)} %get-tuple-element.111), kind=kOutput, calls=%fused_computation.196 | convolution fusion | flops 8589934592 | bytes 20971520 | tf_op jit(solution)/shard_map/td,tf->df/dot_general | solution.py:149
  701.7 3.3 copy-done.5
  710.1 11.7 %add_bitcast_fusion = f32[1,704,2048]{2,1,0:T(8,128)} fusion(bf16[704,2048]{1,0:T(8,128)(2,1)} %collective-permute-done.20, bf16[2048,704]{1,0:T(8,128)(2,1)} %get-tuple-element.94.refs_0_, bf16[2048,2048]{1,0:T(8,128)(2,1)} %all-gather.5.cloned.1.call-done), kind=kOutput, calls=%fused_computation.4 | convolution fusion | flops 5908463616 | bytes 19922944 | tf_op jit(solution)/shard_map/tf,td->fd/dot_general | solution.py:149
  722.5 2.6 fusion.1
  725.1 5.7 bitcast_add_fusion
  734.0 7.1 fusion.58
  745.5 13.5 %convert_add_fusion = f32[1408,2048]{1,0:T(8,128)} fusion(f32[1408,2048]{1,0:T(8,128)} %fusion.60, bf16[1408,2048]{1,0:T(8,128)(2,1)} %collective-permute-done.36), kind=kLoop, calls=%fused_computation | loop fusion | flops 5767168 | bytes 28835840 | tf_op jit(solution)/shard_map/add | solution.py:761
  759.0 7.7 fusion.59
  770.4 3.2 collective-permute-start.24
  780.2 4.8 collective-permute-done.24
  785.0 4.4 collective-permute-start.25
  791.4 9.9 %collective-permute-done.25 = bf16[64,2048]{1,0:T(8,128)(2,1)S(1)} collective-permute-done((bf16[64,2048]{1,0:T(8,128)(2,1)S(1)}, bf16[64,2048]{1,0:T(8,128)(2,1)S(1)}, u32[]{:S(2)}, u32[]{:S(2)}) %collective-permute-start.25) | collective-permute-done | bytes 262176 | tf_op jit(solution)/shard_map/ppermute | solution.py:55
  802.1 4.3 collective-permute-start.26
  806.5 7.6 collective-permute-done.31
  815.9 4.1 collective-permute-done.32
  820.8 4.4 all-to-all-start.5
  831.9 30.1 %all-to-all-done.5 = bf16[4,384,512]{2,1,0:T(8,128)(2,1)} async-done(((bf16[4,384,512]{2,1,0:T(8,128)(2,1)}), bf16[4,384,512]{2,1,0:T(8,128)(2,1)}, u32[]{:S(2)}, u32[]{:S(2)}) %all-to-all-start.5) | async-done | bytes 1572896 | tf_op jit(solution)/shard_map/all_to_all | solution.py:162
  867.4 3.0 add_bitcast_fusion.1
  (307 shorter events, 93.5 us)
Async XLA Ops:
  7.2 263.1 %copy-start = (f32[2048,4]{0,1:T(4,128)S(1)}, f32[2048,4]{0,1:T(4,128)}, u32[]{:S(2)}) copy-start(f32[2048,4]{0,1:T(4,128)} %param.23) | copy-start | bytes 98308
  7.2 130.1 %all-gather.7.cloned.1.call-start = ((), (), s32[]{:S(2)}) async-start(), calls=%async_computation.9 | async-start | bytes 8912896 | tf_op jit(solution)/shard_map/all_gather | solution.py:141
  11.2 65.8 %collective-permute-start = (bf16[704,2048]{1,0:T(8,128)(2,1)}, bf16[704,2048]{1,0:T(8,128)(2,1)}, u32[]{:S(2)}, u32[]{:S(2)}) collective-permute-start(bf16[704,2048]{1,0:T(8,128)(2,1)} %bitcast.348), channel_id=1, source_target_pairs={{1,0},{0,1},{3,2},{2,3},{5,4},{4,5},{7,6},{6,7},{9,8},{8,9},{11,10... | collective-permute-start | bytes 8650760 | tf_op jit(solution)/shard_map/ppermute | solution.py:55
  16.8 60.3 %all-to-all-start = ((bf16[4,384,512]{2,1,0:T(8,128)(2,1)}), bf16[4,384,512]{2,1,0:T(8,128)(2,1)S(1)}, u32[]{:S(2)}, u32[]{:S(2)}) async-start(bf16[4,384,512]{2,1,0:T(8,128)(2,1)} %maximum_maximum_fusion), calls=%async_computation | async-start | bytes 3145728 | tf_op jit(solution)/shard_map/all_to_all | solution.py:162
  21.6 71.8 %copy-start.19 = (f32[128,2048]{1,0:T(8,128)S(1)}, f32[128,2048]{1,0:T(8,128)}, u32[]{:S(2)}) copy-start(f32[128,2048]{1,0:T(8,128)} %param.31) | copy-start | bytes 3145732
  21.6 199.0 %all-gather.5.cloned.1.call-start = ((), (), s32[]{:S(2)}) async-start(), calls=%async_computation.8 | async-start | bytes 8912896 | tf_op jit(solution)/shard_map/all_gather | solution.py:141
  77.1 13.2 %collective-permute-start.1 = (bf16[4,2,64,512]{3,2,1,0:T(8,128)(2,1)S(1)}, bf16[4,2,64,512]{3,2,1,0:T(8,128)(2,1)S(1)}, u32[]{:S(2)}, u32[]{:S(2)}) collective-permute-start(bf16[4,2,64,512]{3,2,1,0:T(8,128)(2,1)S(1)} %bitcast.322), channel_id=1, source_target_pairs={{1,0},{0,1},{3,2},{2,3},{5,4},{4,5},{7,6},{6,7},{9,8},{8,9},{11,10... | collective-permute-start | bytes 1572872 | tf_op jit(solution)/shard_map/ppermute | solution.py:55
  90.2 23.5 %collective-permute-start.2 = (bf16[4,256,512]{2,1,0:T(8,128)(2,1)S(1)}, bf16[4,256,512]{2,1,0:T(8,128)(2,1)S(1)}, u32[]{:S(2)}, u32[]{:S(2)}) collective-permute-start(bf16[4,256,512]{2,1,0:T(8,128)(2,1)S(1)} %slice.265), channel_id=1, source_target_pairs={{1,0},{0,1},{3,2},{2,3},{5,4},{4,5},{7,6},{6,7},{9,8},{8,9},{11,10... | collective-permute-start | bytes 3145736 | tf_op jit(solution)/shard_map/ppermute | solution.py:55
  91.8 22.0 %copy-start.22 = (bf16[2,4,2,64,512]{4,3,2,1,0:T(8,128)(2,1)}, bf16[2,4,2,64,512]{4,3,2,1,0:T(8,128)(2,1)S(1)}, u32[]{:S(2)}) copy-start(bf16[2,4,2,64,512]{4,3,2,1,0:T(8,128)(2,1)S(1)} %pad_maximum_fusion.4) | copy-start | bytes 3145732
  91.8 32.4 %copy-start.14 = (bf16[128,2048]{1,0:T(8,128)(2,1)S(1)}, bf16[128,2048]{1,0:T(8,128)(2,1)}, u32[]{:S(2)}) copy-start(bf16[128,2048]{1,0:T(8,128)(2,1)} %fusion.6) | copy-start | bytes 1572868
  91.8 32.4 %copy-start.32 = (f32[2048,4]{0,1:T(4,128)S(1)}, f32[2048,4]{0,1:T(4,128)}, u32[]{:S(2)}) copy-start(f32[2048,4]{0,1:T(4,128)} %param.22) | copy-start | bytes 98308
  91.8 32.9 %copy-start.41 = (s32[128,2]{0,1:T(2,128)S(1)}, s32[128,2]{0,1:T(2,128)}, u32[]{:S(2)}) copy-start(s32[128,2]{0,1:T(2,128)} %param.18) | copy-start | bytes 3076
  91.8 33.5 %copy-start.57 = (s32[1,128]{1,0:T(1,128)S(1)}, s32[1,128]{1,0:T(1,128)}, u32[]{:S(2)}) copy-start(s32[1,128]{1,0:T(1,128)} %param.17) | copy-start | bytes 1540
  91.8 28.3 %collective-permute-start.3 = (bf16[2,4,2,64,512]{4,3,2,1,0:T(8,128)(2,1)S(1)}, bf16[2,4,2,64,512]{4,3,2,1,0:T(8,128)(2,1)S(1)}, u32[]{:S(2)}, u32[]{:S(2)}) collective-permute-start(bf16[2,4,2,64,512]{4,3,2,1,0:T(8,128)(2,1)S(1)} %pad_maximum_fusion.4), channel_id=1, source_target_pairs={{16,0},{0,16},{17,1},{1,17},{18,2},{2,18},{19,3},{3,19},{20,4},{4,... | collective-permute-start | bytes 3145736 | tf_op jit(solution)/shard_map/ppermute | solution.py:55
  94.9 39.0 %copy-start.21 = (bf16[4,256,512]{2,1,0:T(8,128)(2,1)S(1)}, bf16[4,256,512]{2,1,0:T(8,128)(2,1)}, u32[]{:S(2)}) copy-start(bf16[4,256,512]{2,1,0:T(8,128)(2,1)} %copy-done.20) | copy-start | bytes 3145732
  124.1 13.2 %collective-permute-start.4 = (bf16[2,2,4,2,64,512]{5,4,3,2,1,0:T(8,128)(2,1)}, bf16[2,2,4,2,64,512]{5,4,3,2,1,0:T(8,128)(2,1)}, u32[]{:S(2)}, u32[]{:S(2)}) collective-permute-start(bf16[2,2,4,2,64,512]{5,4,3,2,1,0:T(8,128)(2,1)} %pad_maximum_fusion.1.own_ref), channel_id=1, source_target_pairs={{8,0},{0,8},{9,1},{1,9},{10,2},{2,10},{11,3},{3,11},{12,4},{4,12},... | collective-permute-start | bytes 6291464 | tf_op jit(solution)/shard_map/ppermute | solution.py:55
  126.0 11.4 %all-to-all-start.1 = ((f32[16,2,128]{2,1,0:T(2,128)}), f32[16,2,128]{2,1,0:T(2,128)S(1)}, u32[]{:S(2)}, u32[]{:S(2)}) async-start(f32[16,2,128]{2,1,0:T(2,128)} %pad_maximum_fusion.8), calls=%async_computation.1 | async-start | bytes 32768 | tf_op jit(solution)/shard_map/all_to_all | solution.py:131
  130.8 215.0 %all-gather.9.cloned.1.call-start = ((), (), s32[]{:S(2)}) async-start(), calls=%async_computation.10 | async-start | bytes 8912896 | tf_op jit(solution)/shard_map/all_gather | solution.py:141
  132.4 31.7 %collective-permute-start.5 = (bf16[256,2048]{1,0:T(8,128)(2,1)}, bf16[256,2048]{1,0:T(8,128)(2,1)}, u32[]{:S(2)}, u32[]{:S(2)}) collective-permute-start(bf16[256,2048]{1,0:T(8,128)(2,1)} %bitcast.324), channel_id=1, source_target_pairs={{1,0},{0,1},{3,2},{2,3},{5,4},{4,5},{7,6},{6,7},{9,8},{8,9},{11,10... | collective-permute-start | bytes 3145736 | tf_op jit(solution)/shard_map/ppermute | solution.py:55
  137.9 26.2 %copy-start.25 = (bf16[1,256,2048]{2,1,0:T(8,128)(2,1)S(1)}, bf16[1,256,2048]{2,1,0:T(8,128)(2,1)}, u32[]{:S(2)}) copy-start(bf16[1,256,2048]{2,1,0:T(8,128)(2,1)} %param.26) | copy-start | bytes 3145732
  180.2 7.5 collective-permute-start.6
  190.1 26.1 %copy-start.6 = (bf16[2,4,128,2048]{3,2,0,1:T(8,128)(2,1)}, bf16[2,4,128,2048]{3,2,0,1:T(8,128)(2,1)S(1)}, u32[]{:S(2)}) copy-start(bf16[2,4,128,2048]{3,2,0,1:T(8,128)(2,1)S(1)} %add_convert_fusion.1) | copy-start | bytes 12582916
  190.1 26.1 %collective-permute-start.11 = (bf16[2,64,2048]{2,1,0:T(8,128)(2,1)S(1)}, bf16[2,64,2048]{2,1,0:T(8,128)(2,1)S(1)}, u32[]{:S(2)}, u32[]{:S(2)}) collective-permute-start(bf16[2,64,2048]{2,1,0:T(8,128)(2,1)S(1)} %slice_bitcast_fusion.18), channel_id=1, source_target_pairs={{2,0},{4,2},{6,4},{0,6},{3,1},{5,3},{7,5},{1,7},{10,8},{12,10},{14... | collective-permute-start | bytes 1572872 | tf_op jit(solution)/shard_map/ppermute | solution.py:55
  205.5 30.5 %collective-permute-start.7 = (bf16[4,64,2048]{2,1,0:T(8,128)(2,1)}, bf16[4,64,2048]{2,1,0:T(8,128)(2,1)S(1)}, u32[]{:S(2)}, u32[]{:S(2)}) collective-permute-start(bf16[4,64,2048]{2,1,0:T(8,128)(2,1)} %slice_bitcast_fusion.6), channel_id=1, source_target_pairs={{16,0},{0,16},{17,1},{1,17},{18,2},{2,18},{19,3},{3,19},{20,4},{4,... | collective-permute-start | bytes 3145736 | tf_op jit(solution)/shard_map/ppermute | solution.py:55
  216.3 15.6 %collective-permute-start.12 = (bf16[2,64,2048]{2,1,0:T(8,128)(2,1)S(1)}, bf16[2,64,2048]{2,1,0:T(8,128)(2,1)S(1)}, u32[]{:S(2)}, u32[]{:S(2)}) collective-permute-start(bf16[2,64,2048]{2,1,0:T(8,128)(2,1)S(1)} %fusion.20), channel_id=1, source_target_pairs={{2,0},{4,2},{6,4},{0,6},{3,1},{5,3},{7,5},{1,7},{10,8},{12,10},{14... | collective-permute-start | bytes 1572872 | tf_op jit(solution)/shard_map/ppermute | solution.py:55
  232.1 24.0 %collective-permute-start.13 = (bf16[2,64,2048]{2,1,0:T(8,128)(2,1)S(1)}, bf16[2,64,2048]{2,1,0:T(8,128)(2,1)S(1)}, u32[]{:S(2)}, u32[]{:S(2)}) collective-permute-start(bf16[2,64,2048]{2,1,0:T(8,128)(2,1)S(1)} %fusion.19), channel_id=1, source_target_pairs={{2,0},{4,2},{6,4},{0,6},{3,1},{5,3},{7,5},{1,7},{10,8},{12,10},{14... | collective-permute-start | bytes 1572872 | tf_op jit(solution)/shard_map/ppermute | solution.py:55
  236.5 15.2 %collective-permute-start.8 = (bf16[64,2048]{1,0:T(8,128)(2,1)S(1)}, bf16[64,2048]{1,0:T(8,128)(2,1)S(1)}, u32[]{:S(2)}, u32[]{:S(2)}) collective-permute-start(bf16[64,2048]{1,0:T(8,128)(2,1)S(1)} %slice_bitcast_fusion.24), channel_id=1, source_target_pairs={{2,0},{4,2},{6,4},{0,6},{3,1},{5,3},{7,5},{1,7},{10,8},{12,10},{14... | collective-permute-start | bytes 786440 | tf_op jit(solution)/shard_map/ppermute | solution.py:55
  244.6 23.8 %copy-start.2 = (bf16[128,2048]{1,0:T(8,128)(2,1)S(1)}, bf16[128,2048]{1,0:T(8,128)(2,1)}, u32[]{:S(2)}) copy-start(bf16[128,2048]{1,0:T(8,128)(2,1)} %param.16) | copy-start | bytes 1572868
  244.6 23.8 %copy-start.30 = (f32[2048]{0:T(1024)S(1)}, f32[2048]{0:T(1024)}, u32[]{:S(2)}) copy-start(f32[2048]{0:T(1024)} %param.27) | copy-start | bytes 24580
  251.7 8.2 collective-permute-start.9
  256.2 8.1 collective-permute-start.14
  260.0 8.2 collective-permute-start.10
  269.8 267.9 %reduce-scatter.3.cloned.1.call-start = ((), (), s32[]{:S(2)}) async-start(), calls=%async_computation.11 | async-start | bytes 8912896 | tf_op jit(solution)/shard_map/reduce_scatter | solution.py:145
  269.8 122.3 %collective-permute-start.15 = (bf16[1408,2048]{1,0:T(8,128)(2,1)}, bf16[1408,2048]{1,0:T(8,128)(2,1)}, u32[]{:S(2)}, u32[]{:S(2)}) collective-permute-start(bf16[1408,2048]{1,0:T(8,128)(2,1)} %bitcast.308), channel_id=1, source_target_pairs={{1,0},{0,1},{3,2},{2,3},{5,4},{4,5},{7,6},{6,7},{9,8},{8,9},{11,10... | collective-permute-start | bytes 17301512 | tf_op jit(solution)/shard_map/ppermute | solution.py:55
  429.3 59.1 %all-to-all-start.3 = ((f32[16,1,128]{2,1,0:T(1,128)}), f32[16,1,128]{2,1,0:T(1,128)S(1)}, u32[]{:S(2)}, u32[]{:S(2)}) async-start(f32[16,1,128]{2,1,0:T(1,128)} %add.174), calls=%async_computation.4 | async-start | bytes 16384 | tf_op jit(solution)/shard_map/all_to_all | solution.py:135
  434.7 200.6 %all-gather.11.cloned.1.call-start = ((), (), s32[]{:S(2)}) async-start(), calls=%async_computation.12 | async-start | bytes 8912896 | tf_op jit(solution)/shard_map/all_gather | solution.py:141
  435.1 27.4 %copy-start.55 = (bf16[2048,704]{1,0:T(8,128)(2,1)S(1)}, bf16[2048,704]{1,0:T(8,128)(2,1)}, u32[]{:S(2)}) copy-start(bf16[2048,704]{1,0:T(8,128)(2,1)} %get-tuple-element.98.refs_1_) | copy-start | bytes 8650756
  457.1 17.0 %slice-start.2 = ((s8[5767168]{0:T(1024)(128)(4,1)}), s8[4194304]{0:T(1024)(128)(4,1)S(1)}, s32[]{:S(2)}) async-start(s8[5767168]{0:T(1024)(128)(4,1)} %bitcast.346), calls=%async_computation.16 | async-start | bytes 8388608
  462.2 26.3 %collective-permute-start.16 = (bf16[2,4,128,2048]{3,2,0,1:T(8,128)(2,1)}, bf16[2,4,128,2048]{3,2,0,1:T(8,128)(2,1)}, u32[]{:S(2)}, u32[]{:S(2)}) collective-permute-start(bf16[2,4,128,2048]{3,2,0,1:T(8,128)(2,1)} %copy.75), channel_id=1, source_target_pairs={{8,0},{0,8},{9,1},{1,9},{10,2},{2,10},{11,3},{3,11},{12,4},{4,12},... | collective-permute-start | bytes 12582920 | tf_op jit(solution)/shard_map/ppermute | solution.py:55
  472.9 64.7 %collective-permute-start.20 = (bf16[704,2048]{1,0:T(8,128)(2,1)}, bf16[704,2048]{1,0:T(8,128)(2,1)}, u32[]{:S(2)}, u32[]{:S(2)}) collective-permute-start(bf16[704,2048]{1,0:T(8,128)(2,1)} %convolution_convert_fusion.3), channel_id=1, source_target_pairs={{1,0},{0,1},{3,2},{2,3},{5,4},{4,5},{7,6},{6,7},{9,8},{8,9},{11,10... | collective-permute-start | bytes 8650760 | tf_op jit(solution)/shard_map/ppermute | solution.py:55
  541.5 279.3 %reduce-scatter.5.cloned.1.call-start = ((), (), s32[]{:S(2)}) async-start(), calls=%async_computation.13 | async-start | bytes 8912896 | tf_op jit(solution)/shard_map/reduce_scatter | solution.py:145
  542.8 21.9 %collective-permute-start.17 = (bf16[2,64,2048]{2,1,0:T(8,128)(2,1)S(1)}, bf16[2,64,2048]{2,1,0:T(8,128)(2,1)S(1)}, u32[]{:S(2)}, u32[]{:S(2)}) collective-permute-start(bf16[2,64,2048]{2,1,0:T(8,128)(2,1)S(1)} %slice_bitcast_fusion.14), channel_id=1, source_target_pairs={{2,0},{4,2},{6,4},{0,6},{3,1},{5,3},{7,5},{1,7},{10,8},{12,10},{14... | collective-permute-start | bytes 1572872 | tf_op jit(solution)/shard_map/ppermute | solution.py:55
  565.9 19.8 %collective-permute-start.18 = (bf16[2,64,2048]{2,1,0:T(8,128)(2,1)S(1)}, bf16[2,64,2048]{2,1,0:T(8,128)(2,1)S(1)}, u32[]{:S(2)}, u32[]{:S(2)}) collective-permute-start(bf16[2,64,2048]{2,1,0:T(8,128)(2,1)S(1)} %fusion.17), channel_id=1, source_target_pairs={{2,0},{4,2},{6,4},{0,6},{3,1},{5,3},{7,5},{1,7},{10,8},{12,10},{14... | collective-permute-start | bytes 1572872 | tf_op jit(solution)/shard_map/ppermute | solution.py:55
  570.3 175.2 %collective-permute-start.36 = (bf16[1408,2048]{1,0:T(8,128)(2,1)}, bf16[1408,2048]{1,0:T(8,128)(2,1)}, u32[]{:S(2)}, u32[]{:S(2)}) collective-permute-start(bf16[1408,2048]{1,0:T(8,128)(2,1)} %convolution_convert_fusion), channel_id=1, source_target_pairs={{1,0},{0,1},{3,2},{2,3},{5,4},{4,5},{7,6},{6,7},{9,8},{8,9},{11,10... | collective-permute-start | bytes 17301512 | tf_op jit(solution)/shard_map/ppermute | solution.py:55
  586.9 29.5 %collective-permute-start.19 = (bf16[2,64,2048]{2,1,0:T(8,128)(2,1)S(1)}, bf16[2,64,2048]{2,1,0:T(8,128)(2,1)S(1)}, u32[]{:S(2)}, u32[]{:S(2)}) collective-permute-start(bf16[2,64,2048]{2,1,0:T(8,128)(2,1)S(1)} %fusion.16), channel_id=1, source_target_pairs={{2,0},{4,2},{6,4},{0,6},{3,1},{5,3},{7,5},{1,7},{10,8},{12,10},{14... | collective-permute-start | bytes 1572872 | tf_op jit(solution)/shard_map/ppermute | solution.py:55
  591.3 19.5 %copy-start.16 = (bf16[128,2048]{1,0:T(8,128)(2,1)S(1)}, bf16[128,2048]{1,0:T(8,128)(2,1)}, u32[]{:S(2)}) copy-start(bf16[128,2048]{1,0:T(8,128)(2,1)} %multiply_convert_fusion) | copy-start | bytes 1572868
  591.3 19.8 %copy-start.8 = (bf16[2,4,128,2048]{3,2,0,1:T(8,128)(2,1)S(1)}, bf16[2,4,128,2048]{3,2,0,1:T(8,128)(2,1)}, u32[]{:S(2)}) copy-start(bf16[2,4,128,2048]{3,2,0,1:T(8,128)(2,1)} %add_convert_fusion) | copy-start | bytes 12582916
  675.0 31.8 %all-to-all-start.4 = ((f32[16,1,128]{2,1,0:T(1,128)}), f32[16,1,128]{2,1,0:T(1,128)S(1)}, u32[]{:S(2)}, u32[]{:S(2)}) async-start(f32[16,1,128]{2,1,0:T(1,128)} %get-tuple-element.119), calls=%async_computation.5 | async-start | bytes 16384 | tf_op jit(solution)/shard_map/all_to_all | solution.py:135
  685.9 36.6 %collective-permute-start.23 = (bf16[4,64,2048]{2,1,0:T(8,128)(2,1)}, bf16[4,64,2048]{2,1,0:T(8,128)(2,1)}, u32[]{:S(2)}, u32[]{:S(2)}) collective-permute-start(bf16[4,64,2048]{2,1,0:T(8,128)(2,1)} %slice_bitcast_fusion.4), channel_id=1, source_target_pairs={{16,0},{0,16},{17,1},{1,17},{18,2},{2,18},{19,3},{3,19},{20,4},{4,... | collective-permute-start | bytes 3145736 | tf_op jit(solution)/shard_map/ppermute | solution.py:55
  706.8 18.4 %collective-permute-start.21 = (bf16[2,512,1024]{2,1,0:T(8,128)(2,1)}, bf16[2,512,1024]{2,1,0:T(8,128)(2,1)}, u32[]{:S(2)}, u32[]{:S(2)}) collective-permute-start(bf16[2,512,1024]{2,1,0:T(8,128)(2,1)} %fusion), channel_id=1, source_target_pairs={{0,8},{8,0},{1,9},{9,1},{2,10},{10,2},{3,11},{11,3},{4,12},{12,4},... | collective-permute-start | bytes 6291464 | tf_op jit(solution)/shard_map/ppermute | solution.py:197
  708.5 13.3 %collective-permute-start.29 = (f32[12,2048]{1,0:T(8,128)S(1)}, f32[12,2048]{1,0:T(8,128)S(1)}, u32[]{:S(2)}, u32[]{:S(2)}) collective-permute-start(f32[12,2048]{1,0:T(8,128)S(1)} %concatenate.36), channel_id=1, source_target_pairs={{0,1},{1,0},{2,3},{3,2},{4,5},{5,4},{6,7},{7,6},{8,9},{9,8},{10,11... | collective-permute-start | bytes 294920 | tf_op jit(solution)/shard_map/ppermute | solution.py:104
  732.0 38.0 %collective-permute-start.22 = (bf16[4,2,64,1024]{3,2,1,0:T(8,128)(2,1)}, bf16[4,2,64,1024]{3,2,1,0:T(8,128)(2,1)}, u32[]{:S(2)}, u32[]{:S(2)}) collective-permute-start(bf16[4,2,64,1024]{3,2,1,0:T(8,128)(2,1)} %bitcast.60), channel_id=1, source_target_pairs={{16,0},{0,16},{17,1},{1,17},{18,2},{2,18},{19,3},{3,19},{20,4},{4,... | collective-permute-start | bytes 3145736 | tf_op jit(solution)/shard_map/ppermute | solution.py:55
  744.3 34.0 %collective-permute-start.34 = (bf16[4,256,512]{2,1,0:T(8,128)(2,1)}, bf16[4,256,512]{2,1,0:T(8,128)(2,1)}, u32[]{:S(2)}, u32[]{:S(2)}) collective-permute-start(bf16[4,256,512]{2,1,0:T(8,128)(2,1)} %select_bitcast_fusion), channel_id=1, source_target_pairs={{1,0},{0,1},{3,2},{2,3},{5,4},{4,5},{7,6},{6,7},{9,8},{8,9},{11,10... | collective-permute-start | bytes 3145736 | tf_op jit(solution)/shard_map/ppermute | solution.py:55
  770.4 14.6 %collective-permute-start.24 = (bf16[64,2048]{1,0:T(8,128)(2,1)S(1)}, bf16[64,2048]{1,0:T(8,128)(2,1)S(1)}, u32[]{:S(2)}, u32[]{:S(2)}) collective-permute-start(bf16[64,2048]{1,0:T(8,128)(2,1)S(1)} %slice_bitcast_fusion.30), channel_id=1, source_target_pairs={{2,0},{4,2},{6,4},{0,6},{3,1},{5,3},{7,5},{1,7},{10,8},{12,10},{14... | collective-permute-start | bytes 786440 | tf_op jit(solution)/shard_map/ppermute | solution.py:55
  773.6 15.8 %collective-permute-start.27 = (bf16[64,2048]{1,0:T(8,128)(2,1)S(1)}, bf16[64,2048]{1,0:T(8,128)(2,1)S(1)}, u32[]{:S(2)}, u32[]{:S(2)}) collective-permute-start(bf16[64,2048]{1,0:T(8,128)(2,1)S(1)} %slice_bitcast_fusion.29), channel_id=1, source_target_pairs={{16,0},{0,16},{17,1},{1,17},{18,2},{2,18},{19,3},{3,19},{20,4},{4,... | collective-permute-start | bytes 786440 | tf_op jit(solution)/shard_map/ppermute | solution.py:55
  776.2 14.9 %collective-permute-start.28 = (bf16[4,64,1024]{2,1,0:T(8,128)(2,1)S(1)}, bf16[4,64,1024]{2,1,0:T(8,128)(2,1)S(1)}, u32[]{:S(2)}, u32[]{:S(2)}) collective-permute-start(bf16[4,64,1024]{2,1,0:T(8,128)(2,1)S(1)} %fusion.22), channel_id=1, source_target_pairs={{1,0},{0,1},{3,2},{2,3},{5,4},{4,5},{7,6},{6,7},{9,8},{8,9},{11,10... | collective-permute-start | bytes 1572872 | tf_op jit(solution)/shard_map/ppermute | solution.py:55
  777.7 88.0 %collective-permute-start.35 = (bf16[256,2048]{1,0:T(8,128)(2,1)}, bf16[256,2048]{1,0:T(8,128)(2,1)}, u32[]{:S(2)}, u32[]{:S(2)}) collective-permute-start(bf16[256,2048]{1,0:T(8,128)(2,1)} %slice_select_fusion), channel_id=1, source_target_pairs={{1,0},{0,1},{3,2},{2,3},{5,4},{4,5},{7,6},{6,7},{9,8},{8,9},{11,10... | collective-permute-start | bytes 3145736 | tf_op jit(solution)/shard_map/ppermute | solution.py:55
  785.0 16.3 %collective-permute-start.25 = (bf16[64,2048]{1,0:T(8,128)(2,1)S(1)}, bf16[64,2048]{1,0:T(8,128)(2,1)S(1)}, u32[]{:S(2)}, u32[]{:S(2)}) collective-permute-start(bf16[64,2048]{1,0:T(8,128)(2,1)S(1)} %fusion.26), channel_id=1, source_target_pairs={{2,0},{4,2},{6,4},{0,6},{3,1},{5,3},{7,5},{1,7},{10,8},{12,10},{14... | collective-permute-start | bytes 786440 | tf_op jit(solution)/shard_map/ppermute | solution.py:55
  791.4 15.0 %collective-permute-start.30 = (f32[12,2048]{1,0:T(8,128)S(1)}, f32[12,2048]{1,0:T(8,128)S(1)}, u32[]{:S(2)}, u32[]{:S(2)}) collective-permute-start(f32[12,2048]{1,0:T(8,128)S(1)} %copy-done.28), channel_id=1, source_target_pairs={{0,8},{8,0},{1,9},{9,1},{2,10},{10,2},{3,11},{11,3},{4,12},{12,4},... | collective-permute-start | bytes 294920 | tf_op jit(solution)/shard_map/ppermute | solution.py:104
  802.1 23.1 %collective-permute-start.26 = (bf16[64,2048]{1,0:T(8,128)(2,1)}, bf16[64,2048]{1,0:T(8,128)(2,1)}, u32[]{:S(2)}, u32[]{:S(2)}) collective-permute-start(bf16[64,2048]{1,0:T(8,128)(2,1)} %fusion.25), channel_id=1, source_target_pairs={{2,0},{4,2},{6,4},{0,6},{3,1},{5,3},{7,5},{1,7},{10,8},{12,10},{14... | collective-permute-start | bytes 786440 | tf_op jit(solution)/shard_map/ppermute | solution.py:55
  806.4 7.7 collective-permute-start.31
  814.1 5.9 collective-permute-start.32
  820.7 5.7 collective-permute-start.33
  820.8 41.2 %all-to-all-start.5 = ((bf16[4,384,512]{2,1,0:T(8,128)(2,1)}), bf16[4,384,512]{2,1,0:T(8,128)(2,1)}, u32[]{:S(2)}, u32[]{:S(2)}) async-start(bf16[4,384,512]{2,1,0:T(8,128)(2,1)} %pad_maximum_fusion.3), calls=%async_computation.7 | async-start | bytes 3145728 | tf_op jit(solution)/shard_map/all_to_all | solution.py:162
  (47 other events, 288.1 us)
Sparse Core Ops, SparseCore 0:
  11.3 106.3 all-gather.6
  121.2 75.1 all-gather.4
  269.9 75.8 all-gather.8
  428.2 105.1 reduce-scatter.2
  541.7 93.5 all-gather.10
  675.1 127.8 reduce-scatter.4

commit v13 on v12

--- a/solution.py
+++ b/solution.py
@@ -209,11 +209,12 @@
     half = kv.shape[2] // 2
     rows, kv_rows = query.shape[1], kv.shape[1]
     sent = jnp.concatenate([query, kv[:, :, :half], kv[:, :, half:]], axis=1)
-    here = exchange(after(sent, *others)).astype(F32)
+    sent = after(sent, *others)
+    here = exchange(sent).astype(F32)
     whole = [
         join_blocks(here[:, rows + k * kv_rows : rows + (k + 1) * kv_rows]) for k in range(2)
     ]
-    return join_blocks(here[:, :rows]), jnp.concatenate(whole, axis=1)
+    return join_blocks(here[:, :rows]), jnp.concatenate(whole, axis=1), sent
 
 
 def own_places():
@@ -706,7 +707,7 @@
     grad_down = [mm("tf,td->fd", here, all_cot) for here in gated_units]
     low_up = [one.astype(BF16) for one in grad_up[1:]]
     low_down = [one.astype(BF16) for one in grad_down[1:]]
-    rows_out = part_low(*ring_rows(places, gated_units, down_parts, tokens))
+    rows_out = part_low(*ring_rows(places, after(gated_units, low_down), down_parts, tokens))
     half = tokens // 2
     rows_first, rows_second = rows_out[:, :, :half], rows_out[:, :, half:]
     lower_own, lower_last = ring_open(grad_down[:1] + low_down, "i")
@@ -750,7 +751,7 @@
     )
     summed = sum_over(jnp.concatenate([d_gain_one, sums, d_att_router]), ("i",))
     d_query_last = scatter_query(mm("td,tf->df", all_attn, d_heads), summed)
-    d_query, d_kv_weight = scatter_heads(d_query_last, d_kv_last, d_attn_input)
+    d_query, d_kv_weight, heads_sent = scatter_heads(d_query_last, d_kv_last, d_attn_input)
     d_query = d_query[None]
     d_out = mm("tf,td->fd", gated, all_mid).reshape(inner, -1, width)
     d_out = from_order([d_out[k] for k in range(inner)], "i")
@@ -760,8 +761,8 @@
     layer_out = middle + rows_out.astype(F32) + mlp_bias
     d_upper = (after(upper_last, kv_sent).astype(F32) + upper_own).reshape(up_weight.shape)
     d_lower = (lower_last.astype(F32) + lower_own)[None]
-    summed = sum_over(after(summed, d_kv_last), ("c", "o", "y"))
     d_attn_input = after(d_attn_input, summed)
+    summed = sum_over(after(summed, heads_sent), ("c", "o", "y"))
     d_norm_one, _ = norm_back(
         residual, inverse_one, norm_gain1, d_attn_input.astype(F32) + d_att_from_router
     )

time: 881 us -> 869 us (0.986)
  waiting for transfers between devices: 348 us -> 336 us
    all_to_all x2, waiting for transfers between devices: 30.1 us -> 0.01 us  [exchange(): return lax.all_to_all(blocks, 'o', split_axis=0, concat_axis=0, tiled=True)]
    ppermute x5, waiting for transfers between devices: 11.7 us -> 32.5 us  [sum_over(): lax.ppermute(value, axis, [(k, k ^ step) for k in range(size)])]
    ppermute x31, starting transfers between devices: 77.2 us -> 60.8 us  [shift(): return lax.ppermute(value, axis, [((k + 1) % size, k) for k in range(size)])]
  transfers between devices with their start and end apart: 48 -> 48, of which waited for: 23 -> 24; matrix products, arithmetic and copies ran while one was open for 23% -> 23% of each run, Pallas kernels for 15% -> 16%
where the time goes in v13:
time: 869 us; the launch traced here: 860 us
  waiting for transfers between devices  336 us (39%)
  Pallas kernels  170 us (20%)
  matrix products  115 us (13%)
  starting transfers between devices  99.5 us (11%)
  other arithmetic  80.6 us (9%)
  local copies, waits for them, and re-layouts  30.7 us (4%)
  between operations  15.6 us (2%)
  blocking collectives  13.3 us (2%)
    ppermute x31, waiting for transfers between devices, shift(): return lax.ppermute(value, axis, [((k + 1) % size, k) for k in range(size)])  222 us
    pallas_call x6, Pallas kernels, call(): pl.pallas_call(kernel, grid_spec=pltpu.PrefetchScalarGridSpec(num_scalar_...  170 us
    dot_general x9, matrix products, mm(): return jnp.einsum(form, first, second, preferred_element_type=F32)  108 us
    all_gather x4, waiting for transfers between devices, meet(): return lax.all_gather(rows, GROUP, axis=0, tiled=True)  78.3 us
    ppermute x31, starting transfers between devices, shift(): return lax.ppermute(value, axis, [((k + 1) % size, k) for k in range(size)])  60.8 us
    ppermute x5, waiting for transfers between devices, sum_over(): lax.ppermute(value, axis, [(k, k ^ step) for k in range(size)])  32.5 us
    convert_element_type x18, other arithmetic, add_low(): return (first.astype(F32) + second.astype(F32)).astype(BF16)  19.2 us
  transfers between devices with their start and end apart: 48, of which 24 were waited for; matrix products, arithmetic and copies ran while one was open for 23% of the time, Pallas kernels for 16%

profile of v13, /device:TPU:0, one launch (start us, length us, event | category | flops | bytes accessed | tf_op | source)
XLA Modules:
  0.0 859.5 jit_solution(15787147002837954663)
XLA Ops:
  11.2 3.0 collective-permute-start
  16.8 4.9 all-to-all-start
  21.6 55.4 %collective-permute-done.refs_3_ = bf16[704,2048]{1,0:T(8,128)(2,1)} collective-permute-done((bf16[704,2048]{1,0:T(8,128)(2,1)}, bf16[704,2048]{1,0:T(8,128)(2,1)}, u32[]{:S(2)}, u32[]{:S(2)}) %collective-permute-start) | collective-permute-done | bytes 2883616 | tf_op jit(solution)/shard_map/ppermute | solution.py:55
  78.9 11.3 %collective-permute-done.1 = bf16[4,2,64,512]{3,2,1,0:T(8,128)(2,1)S(1)} collective-permute-done((bf16[4,2,64,512]{3,2,1,0:T(8,128)(2,1)S(1)}, bf16[4,2,64,512]{3,2,1,0:T(8,128)(2,1)S(1)}, u32[]{:S(2)}, u32[]{:S(2)}) %collective-permute-start.1) | collective-permute-done | bytes 524320 | tf_op jit(solution)/shard_map/ppermute | solution.py:55
  94.9 18.9 %collective-permute-done.2 = bf16[4,256,512]{2,1,0:T(8,128)(2,1)S(1)} collective-permute-done((bf16[4,256,512]{2,1,0:T(8,128)(2,1)S(1)}, bf16[4,256,512]{2,1,0:T(8,128)(2,1)S(1)}, u32[]{:S(2)}, u32[]{:S(2)}) %collective-permute-start.2) | collective-permute-done | bytes 1048608 | tf_op jit(solution)/shard_map/ppermute | solution.py:55
  113.8 6.3 collective-permute-done.3
  121.1 3.1 pad_maximum_fusion.1.own_ref
  125.9 4.8 all-to-all-start.1
  137.9 26.2 %attend.1 = (bf16[2048,1536]{1,0:T(8,128)(2,1)}, bf16[2048,512]{1,0:T(8,128)(2,1)}, bf16[2048,1024]{1,0:T(8,128)(2,1)}) custom-call(s32[4]{0:T(128)} %pad_add_fusion.places_ref, bf16[2048,2048]{1,0:T(8,128)(2,1)} %all-gather.7.cloned.1.call-done.x_ref, f32[16,2,128]{2,1,0:T(2,128)} %copy-done.38, f32[128,128]{1,0:T(8,128)} %get-tuple-element.191.cos_ref, ...), custom_call_target="tpu_custom_call" | custom-call | flops 13421772800 | bytes 25165824 | tf_op jit(solution)/shard_map/attend/pallas_call | solution.py:462
  167.0 10.5 %rows.2 = (bf16[2,4,128,2048]{3,2,1,0:T(8,128)(2,1)}, bf16[2,4,128,2048]{3,2,1,0:T(8,128)(2,1)}) custom-call(s32[4]{0:T(128)} %pad_add_fusion.places_ref, bf16[2048,512]{1,0:T(8,128)(2,1)} %get-tuple-element.89.refs_0_, bf16[512,2048]{1,0:T(8,128)(2,1)} %bitcast.318), custom_call_target="tpu_custom_call" | custom-call | flops 4294967296 | bytes 20971520 | tf_op jit(solution)/shard_map/rows/pallas_call | solution.py:462
  177.5 2.7 copy.72
  180.4 7.4 collective-permute-done.6
  190.1 3.6 collective-permute-start.11
  196.0 9.3 %collective-permute-done.11 = bf16[2,64,2048]{2,1,0:T(8,128)(2,1)S(1)} collective-permute-done((bf16[2,64,2048]{2,1,0:T(8,128)(2,1)S(1)}, bf16[2,64,2048]{2,1,0:T(8,128)(2,1)S(1)}, u32[]{:S(2)}, u32[]{:S(2)}) %collective-permute-start.11) | collective-permute-done | bytes 524320 | tf_op jit(solution)/shard_map/ppermute | solution.py:55
  205.5 4.3 collective-permute-start.12
  209.9 11.3 %convolution_convert_fusion.1.d_units_ref = bf16[2048,704]{1,0:T(8,128)(2,1)} fusion(bf16[2048,2048]{1,0:T(8,128)(2,1)} %all-gather.5.cloned.1.call-done, bf16[704,2048]{1,0:T(8,128)(2,1)} %collective-permute-done.refs_3_), kind=kOutput, calls=%fused_computation.9 | convolution fusion | flops 5907021824 | bytes 14155776 | tf_op jit(solution)/shard_map/td,fd->tf/dot_general | solution.py:149
  221.3 3.9 collective-permute-start.13
  225.7 8.1 convolution_convert_fusion.2.d_units_ref
  233.8 7.0 collective-permute-done.8
  240.9 4.3 collective-permute-start.9
  246.1 3.1 collective-permute-done.9
  249.2 4.3 collective-permute-start.10
  253.6 3.8 collective-permute-done.10
  261.2 13.3 %all_to_all.32.info_ref = f32[16,1,128]{2,1,0:T(1,128)} all-to-all(f32[16,1,128]{2,1,0:T(1,128)S(1)} %bitcast.331), channel_id=1, replica_groups=mesh['y'=2,'c'=2,'o'=4,'i'=2] {'y','c','o'}, dimensions={0} | all-to-all | bytes 16384 | tf_op jit(solution)/shard_map/all_to_all | solution.py:131
  274.5 60.5 %all-gather.9.cloned.1.call-done.x_ref = bf16[2048,2048]{1,0:T(8,128)(2,1)} async-done(((bf16[128,2048]{1,0:T(8,128)(2,1)}), bf16[2048,2048]{1,0:T(8,128)(2,1)}) %all-gather.9.cloned.1.call-update) | async-done | bytes 8388624 | tf_op jit(solution)/shard_map/all_gather | solution.py:141
  334.9 35.5 %units.2 = (bf16[2048,1408]{1,0:T(8,128)(2,1)}, bf16[2048,704]{1,0:T(8,128)(2,1)}, f32[2048,2048]{1,0:T(8,128)}, f32[16,1,128]{2,1,0:T(1,128)}) custom-call(s32[4]{0:T(128)} %pad_add_fusion.places_ref, bf16[2048,2048]{1,0:T(8,128)(2,1)} %all-gather.9.cloned.1.call-done.x_ref, f32[16,1,128]{2,1,0:T(1,128)} %all_to_all.32.info_ref, ...), custom_call_target="tpu_custom_call" | custom-call | tf_op jit(solution)/shard_map/units/pallas_call | solution.py:462
  370.5 10.8 %collective-permute-done.15.first_ref.second_ref = bf16[1408,2048]{1,0:T(8,128)(2,1)} collective-permute-done((bf16[1408,2048]{1,0:T(8,128)(2,1)}, bf16[1408,2048]{1,0:T(8,128)(2,1)}, u32[]{:S(2)}, u32[]{:S(2)}) %collective-permute-start.15) | collective-permute-done | bytes 5767200 | tf_op jit(solution)/shard_map/ppermute | solution.py:55
  381.3 35.9 %units.3 = (bf16[2048,1408]{1,0:T(8,128)(2,1)}, bf16[2048,704]{1,0:T(8,128)(2,1)}, bf16[2048,2048]{1,0:T(8,128)(2,1)}, f32[16,1,128]{2,1,0:T(1,128)}) custom-call(s32[4]{0:T(128)} %pad_add_fusion.places_ref, bf16[2048,2048]{1,0:T(8,128)(2,1)} %all-gather.9.cloned.1.call-done.x_ref, f32[16,1,128]{2,1,0:T(1,128)} %all_to_all.32.info_ref, ...), custom_call_target="tpu_custom_call" | custom-call | tf_op jit(solution)/shard_map/units/pallas_call | solution.py:462
  417.2 10.7 %convolution_convert_fusion.3 = bf16[704,2048]{1,0:T(8,128)(2,1)} fusion(bf16[2048,704]{1,0:T(8,128)(2,1)} %get-tuple-element.104.refs_1_, bf16[2048,2048]{1,0:T(8,128)(2,1)} %all-gather.5.cloned.1.call-done), kind=kOutput, calls=%fused_computation.11 | convolution fusion | flops 5907021824 | bytes 14155776 | tf_op jit(solution)/shard_map/tf,td->fd/dot_general | solution.py:149
  427.9 21.8 %rows.3 = (bf16[2,4,128,2048]{3,2,1,0:T(8,128)(2,1)}, bf16[2,4,128,2048]{3,2,1,0:T(8,128)(2,1)}) custom-call(s32[4]{0:T(128)} %pad_add_fusion.places_ref, bf16[2048,704]{1,0:T(8,128)(2,1)} %get-tuple-element.103.refs_0_, bf16[2048,704]{1,0:T(8,128)(2,1)} %get-tuple-element.104.refs_1_, bf16[704,2048]{1,0:T(8,128)(2,1)} %bitcast.345, ...), custom_call_target="tpu_custom_call" | custom-call | flops 11811160064 | bytes 28311552 | tf_op jit(solution)/shard_map/rows/pallas_call | solution.py:462
  449.7 4.9 copy.75
  456.2 6.2 all-to-all-start.3
  462.5 18.0 %convolution_convert_fusion = bf16[1408,2048]{1,0:T(8,128)(2,1)} fusion(bf16[2048,1408]{1,0:T(8,128)(2,1)} %get-tuple-element.108, bf16[2048,2048]{1,0:T(8,128)(2,1)} %all-gather.9.cloned.1.call-done.x_ref), kind=kOutput, calls=%fused_computation.3 | convolution fusion | flops 11814043648 | bytes 19922944 | tf_op jit(solution)/shard_map/tf,td->fd/dot_general | solution.py:149
  480.6 7.9 add_convert_fusion
  488.5 31.3 %collective-permute-done.20 = bf16[704,2048]{1,0:T(8,128)(2,1)} collective-permute-done((bf16[704,2048]{1,0:T(8,128)(2,1)}, bf16[704,2048]{1,0:T(8,128)(2,1)}, u32[]{:S(2)}, u32[]{:S(2)}) %collective-permute-start.20) | collective-permute-done | bytes 2883616 | tf_op jit(solution)/shard_map/ppermute | solution.py:55
  519.8 2.9 reduce-scatter.3.cloned.1.call-done
  522.7 2.5 multiply_reduce_fusion
  529.9 21.3 %collective-permute-done.17 = bf16[2,64,2048]{2,1,0:T(8,128)(2,1)S(1)} collective-permute-done((bf16[2,64,2048]{2,1,0:T(8,128)(2,1)S(1)}, bf16[2,64,2048]{2,1,0:T(8,128)(2,1)S(1)}, u32[]{:S(2)}, u32[]{:S(2)}) %collective-permute-start.17) | collective-permute-done | bytes 524320 | tf_op jit(solution)/shard_map/ppermute | solution.py:55
  554.9 14.7 %collective-permute-done.18 = bf16[2,64,2048]{2,1,0:T(8,128)(2,1)S(1)} collective-permute-done((bf16[2,64,2048]{2,1,0:T(8,128)(2,1)S(1)}, bf16[2,64,2048]{2,1,0:T(8,128)(2,1)S(1)}, u32[]{:S(2)}, u32[]{:S(2)}) %collective-permute-start.18) | collective-permute-done | bytes 524320 | tf_op jit(solution)/shard_map/ppermute | solution.py:55
  570.7 4.1 collective-permute-start.19
  574.9 19.6 %fusion.60 = f32[1408,2048]{1,0:T(8,128)} fusion(bf16[2048,1408]{1,0:T(8,128)(2,1)} %get-tuple-element.144, bf16[2048,2048]{1,0:T(8,128)(2,1)} %all-gather.9.cloned.1.call-done.x_ref), kind=kOutput, calls=%fused_computation.201 | convolution fusion | flops 11811160064 | bytes 25690112 | tf_op jit(solution)/shard_map/tf,td->fd/dot_general | solution.py:149
  596.3 4.4 collective-permute-done.19
  601.6 17.8 %all-gather.11.cloned.1.call-done.mid_ref = bf16[2048,2048]{1,0:T(8,128)(2,1)} async-done(((bf16[128,2048]{1,0:T(8,128)(2,1)}), bf16[2048,2048]{1,0:T(8,128)(2,1)}) %all-gather.11.cloned.1.call-update) | async-done | bytes 8388624 | tf_op jit(solution)/shard_map/all_gather | solution.py:141
  619.4 39.7 %attend_back.1 = (bf16[2048,512]{1,0:T(8,128)(2,1)}, bf16[2048,1024]{1,0:T(8,128)(2,1)}, bf16[2048,2048]{1,0:T(8,128)(2,1)}, f32[16,1,128]{2,1,0:T(1,128)}, f32[1,2048]{1,0:T(1,128)}) custom-call(s32[4]{0:T(128)} %pad_add_fusion.places_ref, bf16[2048,2048]{1,0:T(8,128)(2,1)} %all-gather.11.cloned.1.call-done.mid_ref, f32[16,2,128]{2,1,0:T(2,128)} %copy-done.38, ...), custom_call_target="tpu_custom_call" | custom-call | flops 18522046464 | bytes 46137344 | tf_op jit(solution)/shard_map/attend_back/pallas_call | solution.py:462
  659.1 8.6 all-to-all-start.4
  672.1 13.8 %fusion.55 = f32[2048,1024]{1,0:T(8,128)S(1)} fusion(bf16[2048,2048]{1,0:T(8,128)(2,1)} %all-gather.7.cloned.1.call-done.x_ref, bf16[2048,1024]{1,0:T(8,128)(2,1)} %get-tuple-element.117), kind=kOutput, calls=%fused_computation.196 | convolution fusion | flops 8589934592 | bytes 20971520 | tf_op jit(solution)/shard_map/td,tf->df/dot_general | solution.py:149
  685.9 3.3 copy-done.5
  694.2 11.8 %add_bitcast_fusion = f32[1,704,2048]{2,1,0:T(8,128)} fusion(bf16[704,2048]{1,0:T(8,128)(2,1)} %collective-permute-done.20, bf16[2048,704]{1,0:T(8,128)(2,1)} %get-tuple-element.103.refs_0_, bf16[2048,2048]{1,0:T(8,128)(2,1)} %all-gather.5.cloned.1.call-done), kind=kOutput, calls=%fused_computation.4 | convolution fusion | flops 5908463616 | bytes 19922944 | tf_op jit(solution)/shard_map/tf,td->fd/dot_general | solution.py:149
  706.7 2.6 fusion.1
  709.3 5.7 bitcast_add_fusion
  718.2 7.2 fusion.58
  729.7 13.5 %convert_add_fusion = f32[1408,2048]{1,0:T(8,128)} fusion(f32[1408,2048]{1,0:T(8,128)} %fusion.60, bf16[1408,2048]{1,0:T(8,128)(2,1)} %collective-permute-done.36), kind=kLoop, calls=%fused_computation | loop fusion | flops 5767168 | bytes 28835840 | tf_op jit(solution)/shard_map/add | solution.py:762
  743.2 7.7 fusion.59
  754.6 3.2 collective-permute-start.24
  764.4 4.8 collective-permute-done.24
  769.3 4.4 collective-permute-start.25
  773.8 11.8 %collective-permute-done.25 = bf16[64,2048]{1,0:T(8,128)(2,1)S(1)} collective-permute-done((bf16[64,2048]{1,0:T(8,128)(2,1)S(1)}, bf16[64,2048]{1,0:T(8,128)(2,1)S(1)}, u32[]{:S(2)}, u32[]{:S(2)}) %collective-permute-start.25) | collective-permute-done | bytes 262176 | tf_op jit(solution)/shard_map/ppermute | solution.py:55
  786.3 4.3 collective-permute-start.26
  792.2 4.5 all-to-all-start.5
  802.5 20.7 %collective-permute-done.32 = f32[12,2048]{1,0:T(8,128)S(1)} collective-permute-done((f32[12,2048]{1,0:T(8,128)S(1)}, f32[12,2048]{1,0:T(8,128)S(1)}, u32[]{:S(2)}, u32[]{:S(2)}) %collective-permute-start.32) | collective-permute-done | bytes 98336 | tf_op jit(solution)/shard_map/ppermute | solution.py:104
  823.2 5.8 collective-permute-start.33
  829.0 8.4 collective-permute-done.33
  839.5 3.0 collective-permute-done.34
  849.2 3.0 add_bitcast_fusion.1
  (293 shorter events, 94.5 us)
Async XLA Ops:
  7.2 252.3 %copy-start = (f32[2048,4]{0,1:T(4,128)S(1)}, f32[2048,4]{0,1:T(4,128)}, u32[]{:S(2)}) copy-start(f32[2048,4]{0,1:T(4,128)} %param.23) | copy-start | bytes 98308
  7.2 130.1 %all-gather.7.cloned.1.call-start = ((), (), s32[]{:S(2)}) async-start(), calls=%async_computation.9 | async-start | bytes 8912896 | tf_op jit(solution)/shard_map/all_gather | solution.py:141
  11.2 65.8 %collective-permute-start = (bf16[704,2048]{1,0:T(8,128)(2,1)}, bf16[704,2048]{1,0:T(8,128)(2,1)}, u32[]{:S(2)}, u32[]{:S(2)}) collective-permute-start(bf16[704,2048]{1,0:T(8,128)(2,1)} %bitcast.344), channel_id=1, source_target_pairs={{1,0},{0,1},{3,2},{2,3},{5,4},{4,5},{7,6},{6,7},{9,8},{8,9},{11,10... | collective-permute-start | bytes 8650760 | tf_op jit(solution)/shard_map/ppermute | solution.py:55
  16.8 60.3 %all-to-all-start = ((bf16[4,384,512]{2,1,0:T(8,128)(2,1)}), bf16[4,384,512]{2,1,0:T(8,128)(2,1)S(1)}, u32[]{:S(2)}, u32[]{:S(2)}) async-start(bf16[4,384,512]{2,1,0:T(8,128)(2,1)} %maximum_maximum_fusion), calls=%async_computation | async-start | bytes 3145728 | tf_op jit(solution)/shard_map/all_to_all | solution.py:162
  21.6 71.8 %copy-start.19 = (f32[128,2048]{1,0:T(8,128)S(1)}, f32[128,2048]{1,0:T(8,128)}, u32[]{:S(2)}) copy-start(f32[128,2048]{1,0:T(8,128)} %param.31) | copy-start | bytes 3145732
  21.6 188.2 %all-gather.5.cloned.1.call-start = ((), (), s32[]{:S(2)}) async-start(), calls=%async_computation.8 | async-start | bytes 8912896 | tf_op jit(solution)/shard_map/all_gather | solution.py:141
  77.0 13.2 %collective-permute-start.1 = (bf16[4,2,64,512]{3,2,1,0:T(8,128)(2,1)S(1)}, bf16[4,2,64,512]{3,2,1,0:T(8,128)(2,1)S(1)}, u32[]{:S(2)}, u32[]{:S(2)}) collective-permute-start(bf16[4,2,64,512]{3,2,1,0:T(8,128)(2,1)S(1)} %bitcast.320), channel_id=1, source_target_pairs={{1,0},{0,1},{3,2},{2,3},{5,4},{4,5},{7,6},{6,7},{9,8},{8,9},{11,10... | collective-permute-start | bytes 1572872 | tf_op jit(solution)/shard_map/ppermute | solution.py:55
  90.2 23.5 %collective-permute-start.2 = (bf16[4,256,512]{2,1,0:T(8,128)(2,1)S(1)}, bf16[4,256,512]{2,1,0:T(8,128)(2,1)S(1)}, u32[]{:S(2)}, u32[]{:S(2)}) collective-permute-start(bf16[4,256,512]{2,1,0:T(8,128)(2,1)S(1)} %slice.265), channel_id=1, source_target_pairs={{1,0},{0,1},{3,2},{2,3},{5,4},{4,5},{7,6},{6,7},{9,8},{8,9},{11,10... | collective-permute-start | bytes 3145736 | tf_op jit(solution)/shard_map/ppermute | solution.py:55
  91.7 22.0 %copy-start.22 = (bf16[2,4,2,64,512]{4,3,2,1,0:T(8,128)(2,1)}, bf16[2,4,2,64,512]{4,3,2,1,0:T(8,128)(2,1)S(1)}, u32[]{:S(2)}) copy-start(bf16[2,4,2,64,512]{4,3,2,1,0:T(8,128)(2,1)S(1)} %pad_maximum_fusion.4) | copy-start | bytes 3145732
  91.8 32.4 %copy-start.14 = (bf16[128,2048]{1,0:T(8,128)(2,1)S(1)}, bf16[128,2048]{1,0:T(8,128)(2,1)}, u32[]{:S(2)}) copy-start(bf16[128,2048]{1,0:T(8,128)(2,1)} %fusion.6) | copy-start | bytes 1572868
  91.8 32.4 %copy-start.31 = (f32[2048,4]{0,1:T(4,128)S(1)}, f32[2048,4]{0,1:T(4,128)}, u32[]{:S(2)}) copy-start(f32[2048,4]{0,1:T(4,128)} %param.22) | copy-start | bytes 98308
  91.8 32.9 %copy-start.40 = (s32[128,2]{0,1:T(2,128)S(1)}, s32[128,2]{0,1:T(2,128)}, u32[]{:S(2)}) copy-start(s32[128,2]{0,1:T(2,128)} %param.18) | copy-start | bytes 3076
  91.8 33.5 %copy-start.55 = (s32[1,128]{1,0:T(1,128)S(1)}, s32[1,128]{1,0:T(1,128)}, u32[]{:S(2)}) copy-start(s32[1,128]{1,0:T(1,128)} %param.17) | copy-start | bytes 1540
  91.8 28.3 %collective-permute-start.3 = (bf16[2,4,2,64,512]{4,3,2,1,0:T(8,128)(2,1)S(1)}, bf16[2,4,2,64,512]{4,3,2,1,0:T(8,128)(2,1)S(1)}, u32[]{:S(2)}, u32[]{:S(2)}) collective-permute-start(bf16[2,4,2,64,512]{4,3,2,1,0:T(8,128)(2,1)S(1)} %pad_maximum_fusion.4), channel_id=1, source_target_pairs={{16,0},{0,16},{17,1},{1,17},{18,2},{2,18},{19,3},{3,19},{20,4},{4,... | collective-permute-start | bytes 3145736 | tf_op jit(solution)/shard_map/ppermute | solution.py:55
  94.9 39.0 %copy-start.21 = (bf16[4,256,512]{2,1,0:T(8,128)(2,1)S(1)}, bf16[4,256,512]{2,1,0:T(8,128)(2,1)}, u32[]{:S(2)}) copy-start(bf16[4,256,512]{2,1,0:T(8,128)(2,1)} %copy-done.20) | copy-start | bytes 3145732
  124.1 13.2 %collective-permute-start.4 = (bf16[2,2,4,2,64,512]{5,4,3,2,1,0:T(8,128)(2,1)}, bf16[2,2,4,2,64,512]{5,4,3,2,1,0:T(8,128)(2,1)}, u32[]{:S(2)}, u32[]{:S(2)}) collective-permute-start(bf16[2,2,4,2,64,512]{5,4,3,2,1,0:T(8,128)(2,1)} %pad_maximum_fusion.1.own_ref), channel_id=1, source_target_pairs={{8,0},{0,8},{9,1},{1,9},{10,2},{2,10},{11,3},{3,11},{12,4},{4,12},... | collective-permute-start | bytes 6291464 | tf_op jit(solution)/shard_map/ppermute | solution.py:55
  125.9 11.4 %all-to-all-start.1 = ((f32[16,2,128]{2,1,0:T(2,128)}), f32[16,2,128]{2,1,0:T(2,128)S(1)}, u32[]{:S(2)}, u32[]{:S(2)}) async-start(f32[16,2,128]{2,1,0:T(2,128)} %pad_maximum_fusion.8), calls=%async_computation.1 | async-start | bytes 32768 | tf_op jit(solution)/shard_map/all_to_all | solution.py:131
  130.8 204.2 %all-gather.9.cloned.1.call-start = ((), (), s32[]{:S(2)}) async-start(), calls=%async_computation.10 | async-start | bytes 8912896 | tf_op jit(solution)/shard_map/all_gather | solution.py:141
  132.4 31.7 %collective-permute-start.5 = (bf16[256,2048]{1,0:T(8,128)(2,1)}, bf16[256,2048]{1,0:T(8,128)(2,1)}, u32[]{:S(2)}, u32[]{:S(2)}) collective-permute-start(bf16[256,2048]{1,0:T(8,128)(2,1)} %bitcast.322), channel_id=1, source_target_pairs={{1,0},{0,1},{3,2},{2,3},{5,4},{4,5},{7,6},{6,7},{9,8},{8,9},{11,10... | collective-permute-start | bytes 3145736 | tf_op jit(solution)/shard_map/ppermute | solution.py:55
  137.9 26.2 %copy-start.25 = (bf16[1,256,2048]{2,1,0:T(8,128)(2,1)S(1)}, bf16[1,256,2048]{2,1,0:T(8,128)(2,1)}, u32[]{:S(2)}) copy-start(bf16[1,256,2048]{2,1,0:T(8,128)(2,1)} %param.26) | copy-start | bytes 3145732
  180.2 7.6 collective-permute-start.6
  190.1 15.3 %collective-permute-start.11 = (bf16[2,64,2048]{2,1,0:T(8,128)(2,1)S(1)}, bf16[2,64,2048]{2,1,0:T(8,128)(2,1)S(1)}, u32[]{:S(2)}, u32[]{:S(2)}) collective-permute-start(bf16[2,64,2048]{2,1,0:T(8,128)(2,1)S(1)} %slice_bitcast_fusion.18), channel_id=1, source_target_pairs={{2,0},{4,2},{6,4},{0,6},{3,1},{5,3},{7,5},{1,7},{10,8},{12,10},{14... | collective-permute-start | bytes 1572872 | tf_op jit(solution)/shard_map/ppermute | solution.py:55
  194.7 30.5 %collective-permute-start.7 = (bf16[4,64,2048]{2,1,0:T(8,128)(2,1)}, bf16[4,64,2048]{2,1,0:T(8,128)(2,1)S(1)}, u32[]{:S(2)}, u32[]{:S(2)}) collective-permute-start(bf16[4,64,2048]{2,1,0:T(8,128)(2,1)} %slice_bitcast_fusion.6), channel_id=1, source_target_pairs={{16,0},{0,16},{17,1},{1,17},{18,2},{2,18},{19,3},{3,19},{20,4},{4,... | collective-permute-start | bytes 3145736 | tf_op jit(solution)/shard_map/ppermute | solution.py:55
  205.5 15.6 %collective-permute-start.12 = (bf16[2,64,2048]{2,1,0:T(8,128)(2,1)S(1)}, bf16[2,64,2048]{2,1,0:T(8,128)(2,1)S(1)}, u32[]{:S(2)}, u32[]{:S(2)}) collective-permute-start(bf16[2,64,2048]{2,1,0:T(8,128)(2,1)S(1)} %fusion.20), channel_id=1, source_target_pairs={{2,0},{4,2},{6,4},{0,6},{3,1},{5,3},{7,5},{1,7},{10,8},{12,10},{14... | collective-permute-start | bytes 1572872 | tf_op jit(solution)/shard_map/ppermute | solution.py:55
  221.3 24.0 %collective-permute-start.13 = (bf16[2,64,2048]{2,1,0:T(8,128)(2,1)S(1)}, bf16[2,64,2048]{2,1,0:T(8,128)(2,1)S(1)}, u32[]{:S(2)}, u32[]{:S(2)}) collective-permute-start(bf16[2,64,2048]{2,1,0:T(8,128)(2,1)S(1)} %fusion.19), channel_id=1, source_target_pairs={{2,0},{4,2},{6,4},{0,6},{3,1},{5,3},{7,5},{1,7},{10,8},{12,10},{14... | collective-permute-start | bytes 1572872 | tf_op jit(solution)/shard_map/ppermute | solution.py:55
  225.6 15.2 %collective-permute-start.8 = (bf16[64,2048]{1,0:T(8,128)(2,1)S(1)}, bf16[64,2048]{1,0:T(8,128)(2,1)S(1)}, u32[]{:S(2)}, u32[]{:S(2)}) collective-permute-start(bf16[64,2048]{1,0:T(8,128)(2,1)S(1)} %slice_bitcast_fusion.24), channel_id=1, source_target_pairs={{2,0},{4,2},{6,4},{0,6},{3,1},{5,3},{7,5},{1,7},{10,8},{12,10},{14... | collective-permute-start | bytes 786440 | tf_op jit(solution)/shard_map/ppermute | solution.py:55
  233.8 23.8 %copy-start.2 = (bf16[128,2048]{1,0:T(8,128)(2,1)S(1)}, bf16[128,2048]{1,0:T(8,128)(2,1)}, u32[]{:S(2)}) copy-start(bf16[128,2048]{1,0:T(8,128)(2,1)} %param.16) | copy-start | bytes 1572868
  233.8 23.8 %copy-start.29 = (f32[2048]{0:T(1024)S(1)}, f32[2048]{0:T(1024)}, u32[]{:S(2)}) copy-start(f32[2048]{0:T(1024)} %param.27) | copy-start | bytes 24580
  240.9 8.2 collective-permute-start.9
  245.4 8.1 collective-permute-start.14
  249.2 8.2 collective-permute-start.10
  259.0 263.8 %reduce-scatter.3.cloned.1.call-start = ((), (), s32[]{:S(2)}) async-start(), calls=%async_computation.11 | async-start | bytes 8912896 | tf_op jit(solution)/shard_map/reduce_scatter | solution.py:145
  259.0 122.3 %collective-permute-start.15 = (bf16[1408,2048]{1,0:T(8,128)(2,1)}, bf16[1408,2048]{1,0:T(8,128)(2,1)}, u32[]{:S(2)}, u32[]{:S(2)}) collective-permute-start(bf16[1408,2048]{1,0:T(8,128)(2,1)} %bitcast.306), channel_id=1, source_target_pairs={{1,0},{0,1},{3,2},{2,3},{5,4},{4,5},{7,6},{6,7},{9,8},{8,9},{11,10... | collective-permute-start | bytes 17301512 | tf_op jit(solution)/shard_map/ppermute | solution.py:55
  454.6 26.0 %collective-permute-start.16 = (bf16[2,4,128,2048]{3,2,0,1:T(8,128)(2,1)}, bf16[2,4,128,2048]{3,2,0,1:T(8,128)(2,1)}, u32[]{:S(2)}, u32[]{:S(2)}) collective-permute-start(bf16[2,4,128,2048]{3,2,0,1:T(8,128)(2,1)} %copy.75), channel_id=1, source_target_pairs={{8,0},{0,8},{9,1},{1,9},{10,2},{2,10},{11,3},{3,11},{12,4},{4,12},... | collective-permute-start | bytes 12582920 | tf_op jit(solution)/shard_map/ppermute | solution.py:55
  454.6 65.2 %collective-permute-start.20 = (bf16[704,2048]{1,0:T(8,128)(2,1)}, bf16[704,2048]{1,0:T(8,128)(2,1)}, u32[]{:S(2)}, u32[]{:S(2)}) collective-permute-start(bf16[704,2048]{1,0:T(8,128)(2,1)} %convolution_convert_fusion.3), channel_id=1, source_target_pairs={{1,0},{0,1},{3,2},{2,3},{5,4},{4,5},{7,6},{6,7},{9,8},{8,9},{11,10... | collective-permute-start | bytes 8650760 | tf_op jit(solution)/shard_map/ppermute | solution.py:55
  456.2 24.3 %all-to-all-start.3 = ((f32[16,1,128]{2,1,0:T(1,128)}), f32[16,1,128]{2,1,0:T(1,128)S(1)}, u32[]{:S(2)}, u32[]{:S(2)}) async-start(f32[16,1,128]{2,1,0:T(1,128)} %add.174), calls=%async_computation.4 | async-start | bytes 16384 | tf_op jit(solution)/shard_map/all_to_all | solution.py:135
  462.4 157.0 %all-gather.11.cloned.1.call-start = ((), (), s32[]{:S(2)}) async-start(), calls=%async_computation.12 | async-start | bytes 8912896 | tf_op jit(solution)/shard_map/all_gather | solution.py:141
  526.6 265.6 %reduce-scatter.5.cloned.1.call-start = ((), (), s32[]{:S(2)}) async-start(), calls=%async_computation.13 | async-start | bytes 8912896 | tf_op jit(solution)/shard_map/reduce_scatter | solution.py:145
  527.7 23.5 %collective-permute-start.17 = (bf16[2,64,2048]{2,1,0:T(8,128)(2,1)S(1)}, bf16[2,64,2048]{2,1,0:T(8,128)(2,1)S(1)}, u32[]{:S(2)}, u32[]{:S(2)}) collective-permute-start(bf16[2,64,2048]{2,1,0:T(8,128)(2,1)S(1)} %slice_bitcast_fusion.14), channel_id=1, source_target_pairs={{2,0},{4,2},{6,4},{0,6},{3,1},{5,3},{7,5},{1,7},{10,8},{12,10},{14... | collective-permute-start | bytes 1572872 | tf_op jit(solution)/shard_map/ppermute | solution.py:55
  552.3 17.2 %collective-permute-start.18 = (bf16[2,64,2048]{2,1,0:T(8,128)(2,1)S(1)}, bf16[2,64,2048]{2,1,0:T(8,128)(2,1)S(1)}, u32[]{:S(2)}, u32[]{:S(2)}) collective-permute-start(bf16[2,64,2048]{2,1,0:T(8,128)(2,1)S(1)} %fusion.17), channel_id=1, source_target_pairs={{2,0},{4,2},{6,4},{0,6},{3,1},{5,3},{7,5},{1,7},{10,8},{12,10},{14... | collective-permute-start | bytes 1572872 | tf_op jit(solution)/shard_map/ppermute | solution.py:55
  553.5 176.2 %collective-permute-start.36 = (bf16[1408,2048]{1,0:T(8,128)(2,1)}, bf16[1408,2048]{1,0:T(8,128)(2,1)}, u32[]{:S(2)}, u32[]{:S(2)}) collective-permute-start(bf16[1408,2048]{1,0:T(8,128)(2,1)} %convolution_convert_fusion), channel_id=1, source_target_pairs={{1,0},{0,1},{3,2},{2,3},{5,4},{4,5},{7,6},{6,7},{9,8},{8,9},{11,10... | collective-permute-start | bytes 17301512 | tf_op jit(solution)/shard_map/ppermute | solution.py:55
  570.7 29.9 %collective-permute-start.19 = (bf16[2,64,2048]{2,1,0:T(8,128)(2,1)S(1)}, bf16[2,64,2048]{2,1,0:T(8,128)(2,1)S(1)}, u32[]{:S(2)}, u32[]{:S(2)}) collective-permute-start(bf16[2,64,2048]{2,1,0:T(8,128)(2,1)S(1)} %fusion.16), channel_id=1, source_target_pairs={{2,0},{4,2},{6,4},{0,6},{3,1},{5,3},{7,5},{1,7},{10,8},{12,10},{14... | collective-permute-start | bytes 1572872 | tf_op jit(solution)/shard_map/ppermute | solution.py:55
  574.9 19.6 %copy-start.16 = (bf16[128,2048]{1,0:T(8,128)(2,1)S(1)}, bf16[128,2048]{1,0:T(8,128)(2,1)}, u32[]{:S(2)}) copy-start(bf16[128,2048]{1,0:T(8,128)(2,1)} %multiply_convert_fusion) | copy-start | bytes 1572868
  574.9 20.0 %copy-start.8 = (bf16[2,4,128,2048]{3,2,0,1:T(8,128)(2,1)S(1)}, bf16[2,4,128,2048]{3,2,0,1:T(8,128)(2,1)}, u32[]{:S(2)}) copy-start(bf16[2,4,128,2048]{3,2,0,1:T(8,128)(2,1)} %add_convert_fusion) | copy-start | bytes 12582916
  659.1 31.8 %all-to-all-start.4 = ((f32[16,1,128]{2,1,0:T(1,128)}), f32[16,1,128]{2,1,0:T(1,128)S(1)}, u32[]{:S(2)}, u32[]{:S(2)}) async-start(f32[16,1,128]{2,1,0:T(1,128)} %get-tuple-element.124), calls=%async_computation.5 | async-start | bytes 16384 | tf_op jit(solution)/shard_map/all_to_all | solution.py:135
  670.1 36.6 %collective-permute-start.23 = (bf16[4,64,2048]{2,1,0:T(8,128)(2,1)}, bf16[4,64,2048]{2,1,0:T(8,128)(2,1)}, u32[]{:S(2)}, u32[]{:S(2)}) collective-permute-start(bf16[4,64,2048]{2,1,0:T(8,128)(2,1)} %slice_bitcast_fusion.4), channel_id=1, source_target_pairs={{16,0},{0,16},{17,1},{1,17},{18,2},{2,18},{19,3},{3,19},{20,4},{4,... | collective-permute-start | bytes 3145736 | tf_op jit(solution)/shard_map/ppermute | solution.py:55
  690.9 18.4 %collective-permute-start.21 = (bf16[2,512,1024]{2,1,0:T(8,128)(2,1)}, bf16[2,512,1024]{2,1,0:T(8,128)(2,1)}, u32[]{:S(2)}, u32[]{:S(2)}) collective-permute-start(bf16[2,512,1024]{2,1,0:T(8,128)(2,1)} %fusion), channel_id=1, source_target_pairs={{0,8},{8,0},{1,9},{9,1},{2,10},{10,2},{3,11},{11,3},{4,12},{12,4},... | collective-permute-start | bytes 6291464 | tf_op jit(solution)/shard_map/ppermute | solution.py:197
  692.7 13.3 %collective-permute-start.28 = (f32[12,2048]{1,0:T(8,128)S(1)}, f32[12,2048]{1,0:T(8,128)S(1)}, u32[]{:S(2)}, u32[]{:S(2)}) collective-permute-start(f32[12,2048]{1,0:T(8,128)S(1)} %concatenate.36), channel_id=1, source_target_pairs={{0,1},{1,0},{2,3},{3,2},{4,5},{5,4},{6,7},{7,6},{8,9},{9,8},{10,11... | collective-permute-start | bytes 294920 | tf_op jit(solution)/shard_map/ppermute | solution.py:104
  716.2 38.0 %collective-permute-start.22 = (bf16[4,2,64,1024]{3,2,1,0:T(8,128)(2,1)}, bf16[4,2,64,1024]{3,2,1,0:T(8,128)(2,1)}, u32[]{:S(2)}, u32[]{:S(2)}) collective-permute-start(bf16[4,2,64,1024]{3,2,1,0:T(8,128)(2,1)} %bitcast.60), channel_id=1, source_target_pairs={{16,0},{0,16},{17,1},{1,17},{18,2},{2,18},{19,3},{3,19},{20,4},{4,... | collective-permute-start | bytes 3145736 | tf_op jit(solution)/shard_map/ppermute | solution.py:55
  728.5 33.9 %collective-permute-start.29 = (bf16[4,256,512]{2,1,0:T(8,128)(2,1)}, bf16[4,256,512]{2,1,0:T(8,128)(2,1)}, u32[]{:S(2)}, u32[]{:S(2)}) collective-permute-start(bf16[4,256,512]{2,1,0:T(8,128)(2,1)} %select_bitcast_fusion), channel_id=1, source_target_pairs={{1,0},{0,1},{3,2},{2,3},{5,4},{4,5},{7,6},{6,7},{9,8},{8,9},{11,10... | collective-permute-start | bytes 3145736 | tf_op jit(solution)/shard_map/ppermute | solution.py:55
  754.6 14.7 %collective-permute-start.24 = (bf16[64,2048]{1,0:T(8,128)(2,1)S(1)}, bf16[64,2048]{1,0:T(8,128)(2,1)S(1)}, u32[]{:S(2)}, u32[]{:S(2)}) collective-permute-start(bf16[64,2048]{1,0:T(8,128)(2,1)S(1)} %slice_bitcast_fusion.30), channel_id=1, source_target_pairs={{2,0},{4,2},{6,4},{0,6},{3,1},{5,3},{7,5},{1,7},{10,8},{12,10},{14... | collective-permute-start | bytes 786440 | tf_op jit(solution)/shard_map/ppermute | solution.py:55
  757.8 15.9 %collective-permute-start.27 = (bf16[64,2048]{1,0:T(8,128)(2,1)S(1)}, bf16[64,2048]{1,0:T(8,128)(2,1)S(1)}, u32[]{:S(2)}, u32[]{:S(2)}) collective-permute-start(bf16[64,2048]{1,0:T(8,128)(2,1)S(1)} %slice_bitcast_fusion.29), channel_id=1, source_target_pairs={{16,0},{0,16},{17,1},{1,17},{18,2},{2,18},{19,3},{3,19},{20,4},{4,... | collective-permute-start | bytes 786440 | tf_op jit(solution)/shard_map/ppermute | solution.py:55
  760.4 30.2 %collective-permute-start.30 = (bf16[4,64,1024]{2,1,0:T(8,128)(2,1)S(1)}, bf16[4,64,1024]{2,1,0:T(8,128)(2,1)S(1)}, u32[]{:S(2)}, u32[]{:S(2)}) collective-permute-start(bf16[4,64,1024]{2,1,0:T(8,128)(2,1)S(1)} %fusion.22), channel_id=1, source_target_pairs={{1,0},{0,1},{3,2},{2,3},{5,4},{4,5},{7,6},{6,7},{9,8},{8,9},{11,10... | collective-permute-start | bytes 1572872 | tf_op jit(solution)/shard_map/ppermute | solution.py:55
  761.9 85.6 %collective-permute-start.35 = (bf16[256,2048]{1,0:T(8,128)(2,1)}, bf16[256,2048]{1,0:T(8,128)(2,1)}, u32[]{:S(2)}, u32[]{:S(2)}) collective-permute-start(bf16[256,2048]{1,0:T(8,128)(2,1)} %slice_select_fusion), channel_id=1, source_target_pairs={{1,0},{0,1},{3,2},{2,3},{5,4},{4,5},{7,6},{6,7},{9,8},{8,9},{11,10... | collective-permute-start | bytes 3145736 | tf_op jit(solution)/shard_map/ppermute | solution.py:55
  769.3 16.2 %collective-permute-start.25 = (bf16[64,2048]{1,0:T(8,128)(2,1)S(1)}, bf16[64,2048]{1,0:T(8,128)(2,1)S(1)}, u32[]{:S(2)}, u32[]{:S(2)}) collective-permute-start(bf16[64,2048]{1,0:T(8,128)(2,1)S(1)} %fusion.26), channel_id=1, source_target_pairs={{2,0},{4,2},{6,4},{0,6},{3,1},{5,3},{7,5},{1,7},{10,8},{12,10},{14... | collective-permute-start | bytes 786440 | tf_op jit(solution)/shard_map/ppermute | solution.py:55
  786.3 10.5 %collective-permute-start.26 = (bf16[64,2048]{1,0:T(8,128)(2,1)}, bf16[64,2048]{1,0:T(8,128)(2,1)}, u32[]{:S(2)}, u32[]{:S(2)}) collective-permute-start(bf16[64,2048]{1,0:T(8,128)(2,1)} %fusion.25), channel_id=1, source_target_pairs={{2,0},{4,2},{6,4},{0,6},{3,1},{5,3},{7,5},{1,7},{10,8},{12,10},{14... | collective-permute-start | bytes 786440 | tf_op jit(solution)/shard_map/ppermute | solution.py:55
  792.2 45.4 %copy-start.44 = (f32[2048]{0:T(1024)S(1)}, f32[2048]{0:T(1024)}, u32[]{:S(2)}) copy-start(f32[2048]{0:T(1024)} %param.30) | copy-start | bytes 24580
  792.2 45.4 %copy-start.52 = (f32[128]{0:T(128)S(1)}, f32[128]{0:T(128)}, u32[]{:S(2)}) copy-start(f32[128]{0:T(128)} %get-tuple-element.181) | copy-start | bytes 1540
  792.2 51.6 %all-to-all-start.5 = ((bf16[4,384,512]{2,1,0:T(8,128)(2,1)}), bf16[4,384,512]{2,1,0:T(8,128)(2,1)}, u32[]{:S(2)}, u32[]{:S(2)}) async-start(bf16[4,384,512]{2,1,0:T(8,128)(2,1)} %pad_maximum_fusion.3), calls=%async_computation.7 | async-start | bytes 3145728 | tf_op jit(solution)/shard_map/all_to_all | solution.py:162
  796.7 40.9 %copy-start.24 = (bf16[128,2048]{1,0:T(8,128)(2,1)S(1)}, bf16[128,2048]{1,0:T(8,128)(2,1)}, u32[]{:S(2)}) copy-start(bf16[128,2048]{1,0:T(8,128)(2,1)} %reduce-scatter.5.cloned.1.call-done) | copy-start | bytes 1572868
  796.7 1.6 collective-permute-start.31
  799.2 24.0 %collective-permute-start.32 = (f32[12,2048]{1,0:T(8,128)S(1)}, f32[12,2048]{1,0:T(8,128)S(1)}, u32[]{:S(2)}, u32[]{:S(2)}) collective-permute-start(f32[12,2048]{1,0:T(8,128)S(1)} %add.193), channel_id=1, source_target_pairs={{0,2},{2,0},{4,6},{6,4},{1,3},{3,1},{5,7},{7,5},{8,10},{10,8},{12,... | collective-permute-start | bytes 294920 | tf_op jit(solution)/shard_map/ppermute | solution.py:104
  823.2 14.3 %collective-permute-start.33 = (f32[12,2048]{1,0:T(8,128)S(1)}, f32[12,2048]{1,0:T(8,128)S(1)}, u32[]{:S(2)}, u32[]{:S(2)}) collective-permute-start(f32[12,2048]{1,0:T(8,128)S(1)} %add.194), channel_id=1, source_target_pairs={{0,4},{2,6},{4,0},{6,2},{1,5},{3,7},{5,1},{7,3},{8,12},{10,14},{12... | collective-permute-start | bytes 294920 | tf_op jit(solution)/shard_map/ppermute | solution.py:104
  837.5 5.0 collective-permute-start.34
  (41 other events, 238.4 us)
Sparse Core Ops, SparseCore 0:
  11.3 106.3 all-gather.6
  121.2 75.4 all-gather.4
  259.1 75.8 all-gather.8
  417.3 105.3 reduce-scatter.2
  526.7 92.6 all-gather.10
  659.2 127.9 reduce-scatter.4

commit v14 on v13

--- a/solution.py
+++ b/solution.py
@@ -164,24 +164,18 @@
 
 def gather_heads(query_weight, kv_weight, beside):
     whole = HEADS * HD
-    rows = query_weight.shape[0]
-    here = exchange(
+    kv = exchange(
         jnp.concatenate(
-            [
-                head_blocks(query_weight),
-                head_blocks(kv_weight[:, :whole]),
-                head_blocks(kv_weight[:, whole:]),
-            ],
-            axis=1,
+            [head_blocks(kv_weight[:, :whole]), head_blocks(kv_weight[:, whole:])], axis=1
         )
     )
-    here = after(here, *beside)
-    span = here.shape[2]
-    kv = ring_gather(here[:, rows:].reshape(OUTER, 2, -1, span), "i")
-    query = ring_gather(after(here[:, :rows], kv[-1]), "i")
+    span = kv.shape[2]
+    query = exchange(after(head_blocks(query_weight), kv))
+    kv = ring_gather(kv.reshape(OUTER, 2, -1, span), "i")
+    query = ring_gather(after(query, kv[-1]), "i")
+    query = in_order(query, "i", 1).reshape(-1, span)
     kv = ring_gather(jnp.stack(kv), "y")
-    kv = after(kv, query)
-    query = in_order(query, "i", 1).reshape(-1, span)
+    kv = after(kv, *beside)
     seen = kv[-1][0, 0, 0, 0]
     return query, ring_gather(jnp.stack(kv), "c"), seen
 
@@ -210,11 +204,11 @@
     rows, kv_rows = query.shape[1], kv.shape[1]
     sent = jnp.concatenate([query, kv[:, :, :half], kv[:, :, half:]], axis=1)
     sent = after(sent, *others)
-    here = exchange(sent).astype(F32)
+    here = exchange(sent)
     whole = [
         join_blocks(here[:, rows + k * kv_rows : rows + (k + 1) * kv_rows]) for k in range(2)
     ]
-    return join_blocks(here[:, :rows]), jnp.concatenate(whole, axis=1), sent
+    return join_blocks(here[:, :rows]).astype(F32), jnp.concatenate(whole, axis=1).astype(F32), sent
 
 
 def own_places():
@@ -755,14 +749,14 @@
     d_query = d_query[None]
     d_out = mm("tf,td->fd", gated, all_mid).reshape(inner, -1, width)
     d_out = from_order([d_out[k] for k in range(inner)], "i")
-    d_out = d_out[:1] + list(after(d_out[1:], kv_arrived))
-    d_output = ring_scatter(d_out, "i", d_query)[None]
+    d_out = d_out[:1] + list(after(d_out[1:], d_kv_last))
+    d_output = ring_scatter(d_out, "i", heads_sent)[None]
     rows_out = part_second(*after((rows_first, rows_second), kv_arrived))
     layer_out = middle + rows_out.astype(F32) + mlp_bias
     d_upper = (after(upper_last, kv_sent).astype(F32) + upper_own).reshape(up_weight.shape)
     d_lower = (lower_last.astype(F32) + lower_own)[None]
     d_attn_input = after(d_attn_input, summed)
-    summed = sum_over(after(summed, heads_sent), ("c", "o", "y"))
+    summed = sum_over(after(summed, heads_sent), ("c", "y", "o"))
     d_norm_one, _ = norm_back(
         residual, inverse_one, norm_gain1, d_attn_input.astype(F32) + d_att_from_router
     )

time: 869 us -> 912 us (1.049)
  blocking collectives: 13.3 us -> 44.7 us
  waiting for transfers between devices: 336 us -> 357 us
    all_to_all x2, waiting for transfers between devices: 0.01 us -> 37.2 us  [exchange(): return lax.all_to_all(blocks, 'o', split_axis=0, concat_axis=0, tiled=True)]
    all_to_all x0 -> x1, blocking collectives: none -> 31.2 us  [exchange(): return lax.all_to_all(blocks, 'o', split_axis=0, concat_axis=0, tiled=True)]
    ppermute x5, waiting for transfers between devices: 32.5 us -> 22.1 us  [sum_over(): lax.ppermute(value, axis, [(k, k ^ step) for k in range(size)])]
  transfers between devices with their start and end apart: 48 -> 48, of which waited for: 24 -> 25; matrix products, arithmetic and copies ran while one was open for 23% -> 22% of each run, Pallas kernels for 16% -> 15%
where the time goes in v14:
time: 912 us; the launch traced here: 907 us
  waiting for transfers between devices  357 us (39%)
  Pallas kernels  169 us (19%)
  matrix products  112 us (12%)
  starting transfers between devices  92.6 us (10%)
  other arithmetic  80.5 us (9%)
  blocking collectives  44.7 us (5%)
  local copies, waits for them, and re-layouts  36.1 us (4%)
  between operations  15.3 us (2%)
    ppermute x31, waiting for transfers between devices, shift(): return lax.ppermute(value, axis, [((k + 1) % size, k) for k in range(size)])  216 us
    pallas_call x6, Pallas kernels, call(): pl.pallas_call(kernel, grid_spec=pltpu.PrefetchScalarGridSpec(num_scalar_...  169 us
    dot_general x9, matrix products, mm(): return jnp.einsum(form, first, second, preferred_element_type=F32)  106 us
    all_gather x4, waiting for transfers between devices, meet(): return lax.all_gather(rows, GROUP, axis=0, tiled=True)  78 us
    ppermute x31, starting transfers between devices, shift(): return lax.ppermute(value, axis, [((k + 1) % size, k) for k in range(size)])  53.7 us
    all_to_all x2, waiting for transfers between devices, exchange(): return lax.all_to_all(blocks, 'o', split_axis=0, concat_axis=0, tiled=True)  37.2 us
    all_to_all x1, blocking collectives, exchange(): return lax.all_to_all(blocks, 'o', split_axis=0, concat_axis=0, tiled=True)  31.2 us
    ppermute x5, waiting for transfers between devices, sum_over(): lax.ppermute(value, axis, [(k, k ^ step) for k in range(size)])  22.1 us
  transfers between devices with their start and end apart: 48, of which 25 were waited for; matrix products, arithmetic and copies ran while one was open for 22% of the time, Pallas kernels for 15%

profile of v14, /device:TPU:0, one launch (start us, length us, event | category | flops | bytes accessed | tf_op | source)
XLA Modules:
  0.0 907.3 jit_solution(16042000168696145690)
XLA Ops:
  11.3 3.0 collective-permute-start
  15.5 31.2 %all_to_all.37 = bf16[4,128,512]{2,1,0:T(8,128)(2,1)S(1)} all-to-all(bf16[4,128,512]{2,1,0:T(8,128)(2,1)S(1)} %maximum_maximum_fusion), channel_id=1, replica_groups=mesh['y'=2,'c'=2,'o'=4,'i'=2] {'o'}, dimensions={0} | all-to-all | bytes 1048576 | tf_op jit(solution)/shard_map/all_to_all | solution.py:162
  46.6 41.6 %collective-permute-done.1 = bf16[4,2,64,512]{3,2,1,0:T(8,128)(2,1)S(1)} collective-permute-done((bf16[4,2,64,512]{3,2,1,0:T(8,128)(2,1)S(1)}, bf16[4,2,64,512]{3,2,1,0:T(8,128)(2,1)S(1)}, u32[]{:S(2)}, u32[]{:S(2)}) %collective-permute-start.1) | collective-permute-done | bytes 524320 | tf_op jit(solution)/shard_map/ppermute | solution.py:55
  92.5 21.2 %collective-permute-done.2 = bf16[2,4,2,64,512]{4,3,2,1,0:T(8,128)(2,1)S(1)} collective-permute-done((bf16[2,4,2,64,512]{4,3,2,1,0:T(8,128)(2,1)S(1)}, bf16[2,4,2,64,512]{4,3,2,1,0:T(8,128)(2,1)S(1)}, u32[]{:S(2)}, u32[]{:S(2)}) %collective-permute-start.2) | collective-permute-done | bytes 1048608 | tf_op jit(solution)/shard_map/ppermute | solution.py:55
  116.0 4.8 all-to-all-start.2
  120.8 3.1 pad_maximum_fusion.1.own_ref
  124.5 37.2 %all-to-all-done.2 = bf16[4,256,512]{2,1,0:T(8,128)(2,1)S(1)} async-done(((bf16[4,256,512]{2,1,0:T(8,128)(2,1)}), bf16[4,256,512]{2,1,0:T(8,128)(2,1)S(1)}, u32[]{:S(2)}, u32[]{:S(2)}) %all-to-all-start.2) | async-done | bytes 1048608 | tf_op jit(solution)/shard_map/all_to_all | solution.py:162
  163.9 3.8 all-to-all-start.1
  170.2 17.7 %collective-permute-done.3 = bf16[4,256,512]{2,1,0:T(8,128)(2,1)} collective-permute-done((bf16[4,256,512]{2,1,0:T(8,128)(2,1)S(1)}, bf16[4,256,512]{2,1,0:T(8,128)(2,1)}, u32[]{:S(2)}, u32[]{:S(2)}) %collective-permute-start.3) | collective-permute-done | bytes 1048608 | tf_op jit(solution)/shard_map/ppermute | solution.py:55
  191.6 26.2 %attend.1 = (bf16[2048,1536]{1,0:T(8,128)(2,1)}, bf16[2048,512]{1,0:T(8,128)(2,1)}, bf16[2048,1024]{1,0:T(8,128)(2,1)}) custom-call(s32[4]{0:T(128)} %pad_add_fusion.places_ref, bf16[2048,2048]{1,0:T(8,128)(2,1)} %all-gather.7.cloned.1.call-done.x_ref, f32[16,2,128]{2,1,0:T(2,128)} %copy-done.33, f32[128,128]{1,0:T(8,128)} %get-tuple-element.191.cos_ref, ...), custom_call_target="tpu_custom_call" | custom-call | flops 13421772800 | bytes 25165824 | tf_op jit(solution)/shard_map/attend/pallas_call | solution.py:456
  220.7 10.5 %rows.2 = (bf16[2,4,128,2048]{3,2,1,0:T(8,128)(2,1)}, bf16[2,4,128,2048]{3,2,1,0:T(8,128)(2,1)}) custom-call(s32[4]{0:T(128)} %pad_add_fusion.places_ref, bf16[2048,512]{1,0:T(8,128)(2,1)} %get-tuple-element.89.refs_0_, bf16[512,2048]{1,0:T(8,128)(2,1)} %bitcast.308), custom_call_target="tpu_custom_call" | custom-call | flops 4294967296 | bytes 20971520 | tf_op jit(solution)/shard_map/rows/pallas_call | solution.py:456
  231.2 2.7 copy.72
  234.0 7.1 collective-permute-done.6
  246.3 11.2 %collective-permute-done.11 = bf16[2,64,2048]{2,1,0:T(8,128)(2,1)S(1)} collective-permute-done((bf16[2,64,2048]{2,1,0:T(8,128)(2,1)S(1)}, bf16[2,64,2048]{2,1,0:T(8,128)(2,1)S(1)}, u32[]{:S(2)}, u32[]{:S(2)}) %collective-permute-start.11) | collective-permute-done | bytes 524320 | tf_op jit(solution)/shard_map/ppermute | solution.py:55
  260.1 11.3 %convolution_convert_fusion.1.d_units_ref = bf16[2048,704]{1,0:T(8,128)(2,1)} fusion(bf16[2048,2048]{1,0:T(8,128)(2,1)} %all-gather.5.cloned.1.call-done, bf16[704,2048]{1,0:T(8,128)(2,1)} %copy-done.50), kind=kOutput, calls=%fused_computation.9 | convolution fusion | flops 5907021824 | bytes 14155776 | tf_op jit(solution)/shard_map/td,fd->tf/dot_general | solution.py:149
  271.5 4.0 collective-permute-start.13
  276.0 8.1 convolution_convert_fusion.2.d_units_ref
  284.1 7.1 collective-permute-done.8
  291.3 4.3 collective-permute-start.9
  299.6 4.3 collective-permute-start.10
  304.0 3.8 collective-permute-done.10
  312.6 13.5 %all_to_all.38.info_ref = f32[16,1,128]{2,1,0:T(1,128)} all-to-all(f32[16,1,128]{2,1,0:T(1,128)S(1)} %bitcast.321), channel_id=1, replica_groups=mesh['y'=2,'c'=2,'o'=4,'i'=2] {'y','c','o'}, dimensions={0} | all-to-all | bytes 16384 | tf_op jit(solution)/shard_map/all_to_all | solution.py:131
  326.1 60.2 %all-gather.9.cloned.1.call-done.x_ref = bf16[2048,2048]{1,0:T(8,128)(2,1)} async-done(((bf16[128,2048]{1,0:T(8,128)(2,1)}), bf16[2048,2048]{1,0:T(8,128)(2,1)}) %all-gather.9.cloned.1.call-update) | async-done | bytes 8388624 | tf_op jit(solution)/shard_map/all_gather | solution.py:141
  386.3 35.5 %units.2 = (bf16[2048,1408]{1,0:T(8,128)(2,1)}, bf16[2048,704]{1,0:T(8,128)(2,1)}, f32[2048,2048]{1,0:T(8,128)}, f32[16,1,128]{2,1,0:T(1,128)}) custom-call(s32[4]{0:T(128)} %pad_add_fusion.places_ref, bf16[2048,2048]{1,0:T(8,128)(2,1)} %all-gather.9.cloned.1.call-done.x_ref, f32[16,1,128]{2,1,0:T(1,128)} %all_to_all.38.info_ref, ...), custom_call_target="tpu_custom_call" | custom-call | tf_op jit(solution)/shard_map/units/pallas_call | solution.py:456
  421.8 9.9 %collective-permute-done.15.first_ref.second_ref = bf16[1408,2048]{1,0:T(8,128)(2,1)} collective-permute-done((bf16[1408,2048]{1,0:T(8,128)(2,1)}, bf16[1408,2048]{1,0:T(8,128)(2,1)}, u32[]{:S(2)}, u32[]{:S(2)}) %collective-permute-start.15) | collective-permute-done | bytes 5767200 | tf_op jit(solution)/shard_map/ppermute | solution.py:55
  431.7 35.8 %units.3 = (bf16[2048,1408]{1,0:T(8,128)(2,1)}, bf16[2048,704]{1,0:T(8,128)(2,1)}, bf16[2048,2048]{1,0:T(8,128)(2,1)}, f32[16,1,128]{2,1,0:T(1,128)}) custom-call(s32[4]{0:T(128)} %pad_add_fusion.places_ref, bf16[2048,2048]{1,0:T(8,128)(2,1)} %all-gather.9.cloned.1.call-done.x_ref, f32[16,1,128]{2,1,0:T(1,128)} %all_to_all.38.info_ref, ...), custom_call_target="tpu_custom_call" | custom-call | tf_op jit(solution)/shard_map/units/pallas_call | solution.py:456
  467.6 10.7 %convolution_convert_fusion.3 = bf16[704,2048]{1,0:T(8,128)(2,1)} fusion(bf16[2048,704]{1,0:T(8,128)(2,1)} %get-tuple-element.104.refs_1_, bf16[2048,2048]{1,0:T(8,128)(2,1)} %all-gather.5.cloned.1.call-done), kind=kOutput, calls=%fused_computation.11 | convolution fusion | flops 5907021824 | bytes 14155776 | tf_op jit(solution)/shard_map/tf,td->fd/dot_general | solution.py:149
  478.3 21.6 %rows.3 = (bf16[2,4,128,2048]{3,2,1,0:T(8,128)(2,1)}, bf16[2,4,128,2048]{3,2,1,0:T(8,128)(2,1)}) custom-call(s32[4]{0:T(128)} %pad_add_fusion.places_ref, bf16[2048,704]{1,0:T(8,128)(2,1)} %get-tuple-element.103.refs_0_, bf16[2048,704]{1,0:T(8,128)(2,1)} %get-tuple-element.104.refs_1_, bf16[704,2048]{1,0:T(8,128)(2,1)} %bitcast.337, bf16[704,2048]{1,0:T(8,128)(2,1)} %copy-done.50), custom_call_target="tpu_custom_call" | custom-call | flops 11811160064 | bytes 28311552 | tf_op jit(solution)/shard_map/rows/pallas_call | solution.py:456
  499.9 5.6 copy.75
  507.6 6.2 all-to-all-start.4
  513.9 18.0 %convolution_convert_fusion = bf16[1408,2048]{1,0:T(8,128)(2,1)} fusion(bf16[2048,1408]{1,0:T(8,128)(2,1)} %get-tuple-element.108, bf16[2048,2048]{1,0:T(8,128)(2,1)} %all-gather.9.cloned.1.call-done.x_ref), kind=kOutput, calls=%fused_computation.3 | convolution fusion | flops 11814043648 | bytes 19922944 | tf_op jit(solution)/shard_map/tf,td->fd/dot_general | solution.py:149
  532.1 8.0 add_convert_fusion
  540.0 30.7 %collective-permute-done.20 = bf16[704,2048]{1,0:T(8,128)(2,1)} collective-permute-done((bf16[704,2048]{1,0:T(8,128)(2,1)}, bf16[704,2048]{1,0:T(8,128)(2,1)}, u32[]{:S(2)}, u32[]{:S(2)}) %collective-permute-start.20) | collective-permute-done | bytes 2883616 | tf_op jit(solution)/shard_map/ppermute | solution.py:55
  570.8 3.4 reduce-scatter.3.cloned.1.call-done
  574.2 2.5 multiply_reduce_fusion
  581.4 21.1 %collective-permute-done.17 = bf16[2,64,2048]{2,1,0:T(8,128)(2,1)S(1)} collective-permute-done((bf16[2,64,2048]{2,1,0:T(8,128)(2,1)S(1)}, bf16[2,64,2048]{2,1,0:T(8,128)(2,1)S(1)}, u32[]{:S(2)}, u32[]{:S(2)}) %collective-permute-start.17) | collective-permute-done | bytes 524320 | tf_op jit(solution)/shard_map/ppermute | solution.py:55
  606.3 14.7 %collective-permute-done.18 = bf16[2,64,2048]{2,1,0:T(8,128)(2,1)S(1)} collective-permute-done((bf16[2,64,2048]{2,1,0:T(8,128)(2,1)S(1)}, bf16[2,64,2048]{2,1,0:T(8,128)(2,1)S(1)}, u32[]{:S(2)}, u32[]{:S(2)}) %collective-permute-start.18) | collective-permute-done | bytes 524320 | tf_op jit(solution)/shard_map/ppermute | solution.py:55
  622.2 4.1 collective-permute-start.19
  626.3 19.7 %fusion.61 = f32[1408,2048]{1,0:T(8,128)} fusion(bf16[2048,1408]{1,0:T(8,128)(2,1)} %get-tuple-element.144, bf16[2048,2048]{1,0:T(8,128)(2,1)} %all-gather.9.cloned.1.call-done.x_ref), kind=kOutput, calls=%fused_computation.199 | convolution fusion | flops 11811160064 | bytes 25690112 | tf_op jit(solution)/shard_map/tf,td->fd/dot_general | solution.py:149
  647.8 4.3 collective-permute-done.19
  653.1 17.8 %all-gather.11.cloned.1.call-done.mid_ref = bf16[2048,2048]{1,0:T(8,128)(2,1)} async-done(((bf16[128,2048]{1,0:T(8,128)(2,1)}), bf16[2048,2048]{1,0:T(8,128)(2,1)}) %all-gather.11.cloned.1.call-update) | async-done | bytes 8388624 | tf_op jit(solution)/shard_map/all_gather | solution.py:141
  670.9 39.8 %attend_back.1 = (bf16[2048,512]{1,0:T(8,128)(2,1)}, bf16[2048,1024]{1,0:T(8,128)(2,1)}, bf16[2048,2048]{1,0:T(8,128)(2,1)}, f32[16,1,128]{2,1,0:T(1,128)}, f32[1,2048]{1,0:T(1,128)}) custom-call(s32[4]{0:T(128)} %pad_add_fusion.places_ref, bf16[2048,2048]{1,0:T(8,128)(2,1)} %all-gather.11.cloned.1.call-done.mid_ref, f32[16,2,128]{2,1,0:T(2,128)} %copy-done.33, ...), custom_call_target="tpu_custom_call" | custom-call | flops 18522046464 | bytes 46137344 | tf_op jit(solution)/shard_map/attend_back/pallas_call | solution.py:456
  710.8 8.8 all-to-all-start.5
  723.9 13.8 %fusion.56 = f32[2048,1024]{1,0:T(8,128)S(1)} fusion(bf16[2048,2048]{1,0:T(8,128)(2,1)} %all-gather.7.cloned.1.call-done.x_ref, bf16[2048,1024]{1,0:T(8,128)(2,1)} %get-tuple-element.117), kind=kOutput, calls=%fused_computation.194 | convolution fusion | flops 8589934592 | bytes 20971520 | tf_op jit(solution)/shard_map/td,tf->df/dot_general | solution.py:149
  737.8 3.2 copy-done.5
  746.0 11.9 %add_bitcast_fusion = f32[1,704,2048]{2,1,0:T(8,128)} fusion(bf16[704,2048]{1,0:T(8,128)(2,1)} %collective-permute-done.20, bf16[2048,704]{1,0:T(8,128)(2,1)} %get-tuple-element.103.refs_0_, bf16[2048,2048]{1,0:T(8,128)(2,1)} %all-gather.5.cloned.1.call-done), kind=kOutput, calls=%fused_computation.4 | convolution fusion | flops 5908463616 | bytes 19922944 | tf_op jit(solution)/shard_map/tf,td->fd/dot_general | solution.py:149
  758.5 2.8 fusion.1
  761.3 5.9 bitcast_add_fusion
  769.4 4.6 fusion.59
  777.6 13.6 %convert_add_fusion = f32[1408,2048]{1,0:T(8,128)} fusion(f32[1408,2048]{1,0:T(8,128)} %fusion.61, bf16[1408,2048]{1,0:T(8,128)(2,1)} %collective-permute-done.36), kind=kLoop, calls=%fused_computation | loop fusion | flops 5767168 | bytes 28835840 | tf_op jit(solution)/shard_map/add | solution.py:756
  791.2 7.7 fusion.60
  802.1 3.4 collective-permute-done.22
  805.5 3.6 collective-permute-start.24
  814.2 5.5 collective-permute-done.24
  819.8 4.6 collective-permute-start.25
  824.5 12.1 %collective-permute-done.25 = bf16[64,2048]{1,0:T(8,128)(2,1)S(1)} collective-permute-done((bf16[64,2048]{1,0:T(8,128)(2,1)S(1)}, bf16[64,2048]{1,0:T(8,128)(2,1)S(1)}, u32[]{:S(2)}, u32[]{:S(2)}) %collective-permute-start.25) | collective-permute-done | bytes 262176 | tf_op jit(solution)/shard_map/ppermute | solution.py:55
  836.6 3.2 collective-permute-start.26
  844.5 5.5 all-to-all-start.6
  852.7 5.7 collective-permute-done.32
  860.5 3.0 fusion.12
  863.5 11.1 %collective-permute-done.33 = f32[12,2048]{1,0:T(8,128)S(1)} collective-permute-done((f32[12,2048]{1,0:T(8,128)S(1)}, f32[12,2048]{1,0:T(8,128)S(1)}, u32[]{:S(2)}, u32[]{:S(2)}) %collective-permute-start.33) | collective-permute-done | bytes 98336 | tf_op jit(solution)/shard_map/ppermute | solution.py:104
  874.7 5.5 collective-permute-start.34
  880.2 3.0 add_bitcast_fusion.1
  883.2 5.1 collective-permute-done.34
  (290 shorter events, 101.0 us)
Async XLA Ops:
  7.2 303.8 %copy-start = (f32[2048,4]{0,1:T(4,128)S(1)}, f32[2048,4]{0,1:T(4,128)}, u32[]{:S(2)}) copy-start(f32[2048,4]{0,1:T(4,128)} %param.23) | copy-start | bytes 98308
  7.2 83.9 %copy-start.19 = (f32[128,2048]{1,0:T(8,128)S(1)}, f32[128,2048]{1,0:T(8,128)}, u32[]{:S(2)}) copy-start(f32[128,2048]{1,0:T(8,128)} %param.31) | copy-start | bytes 3145732
  7.2 183.8 %all-gather.7.cloned.1.call-start = ((), (), s32[]{:S(2)}) async-start(), calls=%async_computation.10 | async-start | bytes 8912896 | tf_op jit(solution)/shard_map/all_gather | solution.py:141
  11.2 103.5 %copy-start.23 = (bf16[1,256,2048]{2,1,0:T(8,128)(2,1)S(1)}, bf16[1,256,2048]{2,1,0:T(8,128)(2,1)}, u32[]{:S(2)}) copy-start(bf16[1,256,2048]{2,1,0:T(8,128)(2,1)} %param.25) | copy-start | bytes 3145732
  11.2 248.9 %all-gather.5.cloned.1.call-start = ((), (), s32[]{:S(2)}) async-start(), calls=%async_computation.9 | async-start | bytes 8912896 | tf_op jit(solution)/shard_map/all_gather | solution.py:141
  11.3 81.2 %collective-permute-start = (bf16[704,2048]{1,0:T(8,128)(2,1)}, bf16[704,2048]{1,0:T(8,128)(2,1)S(1)}, u32[]{:S(2)}, u32[]{:S(2)}) collective-permute-start(bf16[704,2048]{1,0:T(8,128)(2,1)} %bitcast.336), channel_id=1, source_target_pairs={{1,0},{0,1},{3,2},{2,3},{5,4},{4,5},{7,6},{6,7},{9,8},{8,9},{11,10... | collective-permute-start | bytes 8650760 | tf_op jit(solution)/shard_map/ppermute | solution.py:55
  46.6 41.6 %collective-permute-start.1 = (bf16[4,2,64,512]{3,2,1,0:T(8,128)(2,1)S(1)}, bf16[4,2,64,512]{3,2,1,0:T(8,128)(2,1)S(1)}, u32[]{:S(2)}, u32[]{:S(2)}) collective-permute-start(bf16[4,2,64,512]{3,2,1,0:T(8,128)(2,1)S(1)} %bitcast.310), channel_id=1, source_target_pairs={{1,0},{0,1},{3,2},{2,3},{5,4},{4,5},{7,6},{6,7},{9,8},{8,9},{11,10... | collective-permute-start | bytes 1572872 | tf_op jit(solution)/shard_map/ppermute | solution.py:55
  89.3 24.5 %collective-permute-start.2 = (bf16[2,4,2,64,512]{4,3,2,1,0:T(8,128)(2,1)S(1)}, bf16[2,4,2,64,512]{4,3,2,1,0:T(8,128)(2,1)S(1)}, u32[]{:S(2)}, u32[]{:S(2)}) collective-permute-start(bf16[2,4,2,64,512]{4,3,2,1,0:T(8,128)(2,1)S(1)} %pad_maximum_fusion.4), channel_id=1, source_target_pairs={{16,0},{0,16},{17,1},{1,17},{18,2},{2,18},{19,3},{3,19},{20,4},{4,... | collective-permute-start | bytes 3145736 | tf_op jit(solution)/shard_map/ppermute | solution.py:55
  92.5 21.2 %copy-start.50 = (bf16[704,2048]{1,0:T(8,128)(2,1)}, bf16[704,2048]{1,0:T(8,128)(2,1)S(1)}, u32[]{:S(2)}) copy-start(bf16[704,2048]{1,0:T(8,128)(2,1)S(1)} %collective-permute-done.refs_3_) | copy-start | bytes 8650756
  114.9 48.3 %copy-start.51 = (s32[1,128]{1,0:T(1,128)S(1)}, s32[1,128]{1,0:T(1,128)}, u32[]{:S(2)}) copy-start(s32[1,128]{1,0:T(1,128)} %param.17) | copy-start | bytes 1540
  116.0 45.7 %all-to-all-start.2 = ((bf16[4,256,512]{2,1,0:T(8,128)(2,1)}), bf16[4,256,512]{2,1,0:T(8,128)(2,1)S(1)}, u32[]{:S(2)}, u32[]{:S(2)}) async-start(bf16[4,256,512]{2,1,0:T(8,128)(2,1)} %pad_maximum_fusion.5), calls=%async_computation.2 | async-start | bytes 2097152 | tf_op jit(solution)/shard_map/all_to_all | solution.py:162
  123.9 67.2 %collective-permute-start.4 = (bf16[2,2,4,2,64,512]{5,4,3,2,1,0:T(8,128)(2,1)}, bf16[2,2,4,2,64,512]{5,4,3,2,1,0:T(8,128)(2,1)}, u32[]{:S(2)}, u32[]{:S(2)}) collective-permute-start(bf16[2,2,4,2,64,512]{5,4,3,2,1,0:T(8,128)(2,1)} %pad_maximum_fusion.1.own_ref), channel_id=1, source_target_pairs={{8,0},{0,8},{9,1},{1,9},{10,2},{2,10},{11,3},{3,11},{12,4},{4,12},... | collective-permute-start | bytes 6291464 | tf_op jit(solution)/shard_map/ppermute | solution.py:55
  124.4 43.6 %copy-start.29 = (f32[128,2]{0,1:T(2,128)}, f32[128,2]{0,1:T(2,128)S(1)}, u32[]{:S(2)}) copy-start(f32[128,2]{0,1:T(2,128)S(1)} %select_reduce_fusion.7) | copy-start | bytes 3076
  124.4 65.0 %copy-start.37 = (f32[128]{0:T(128)}, f32[128]{0:T(128)S(1)}, u32[]{:S(2)}) copy-start(f32[128]{0:T(128)S(1)} %reduce_max.18) | copy-start | bytes 1540
  124.5 38.7 %copy-start.42 = (f32[128]{0:T(128)}, f32[128]{0:T(128)S(1)}, u32[]{:S(2)}) copy-start(f32[128]{0:T(128)S(1)} %fusion.45) | copy-start | bytes 1540
  161.7 26.2 %collective-permute-start.3 = (bf16[4,256,512]{2,1,0:T(8,128)(2,1)S(1)}, bf16[4,256,512]{2,1,0:T(8,128)(2,1)}, u32[]{:S(2)}, u32[]{:S(2)}) collective-permute-start(bf16[4,256,512]{2,1,0:T(8,128)(2,1)S(1)} %all-to-all-done.2), channel_id=1, source_target_pairs={{1,0},{0,1},{3,2},{2,3},{5,4},{4,5},{7,6},{6,7},{9,8},{8,9},{11,10... | collective-permute-start | bytes 3145736 | tf_op jit(solution)/shard_map/ppermute | solution.py:55
  163.9 27.1 %all-to-all-start.1 = ((f32[16,2,128]{2,1,0:T(2,128)}), f32[16,2,128]{2,1,0:T(2,128)S(1)}, u32[]{:S(2)}, u32[]{:S(2)}) async-start(f32[16,2,128]{2,1,0:T(2,128)} %pad_maximum_fusion.9), calls=%async_computation.1 | async-start | bytes 32768 | tf_op jit(solution)/shard_map/all_to_all | solution.py:131
  167.7 218.6 %all-gather.9.cloned.1.call-start = ((), (), s32[]{:S(2)}) async-start(), calls=%async_computation.11 | async-start | bytes 8912896 | tf_op jit(solution)/shard_map/all_gather | solution.py:141
  169.7 48.2 %collective-permute-start.5 = (bf16[256,2048]{1,0:T(8,128)(2,1)}, bf16[256,2048]{1,0:T(8,128)(2,1)}, u32[]{:S(2)}, u32[]{:S(2)}) collective-permute-start(bf16[256,2048]{1,0:T(8,128)(2,1)} %bitcast.312), channel_id=1, source_target_pairs={{1,0},{0,1},{3,2},{2,3},{5,4},{4,5},{7,6},{6,7},{9,8},{8,9},{11,10... | collective-permute-start | bytes 3145736 | tf_op jit(solution)/shard_map/ppermute | solution.py:55
  191.6 26.2 %copy-start.22 = (bf16[1,256,2048]{2,1,0:T(8,128)(2,1)S(1)}, bf16[1,256,2048]{2,1,0:T(8,128)(2,1)}, u32[]{:S(2)}) copy-start(bf16[1,256,2048]{2,1,0:T(8,128)(2,1)} %param.26) | copy-start | bytes 3145732
  233.9 7.2 collective-permute-start.6
  243.5 14.0 %collective-permute-start.11 = (bf16[2,64,2048]{2,1,0:T(8,128)(2,1)S(1)}, bf16[2,64,2048]{2,1,0:T(8,128)(2,1)S(1)}, u32[]{:S(2)}, u32[]{:S(2)}) collective-permute-start(bf16[2,64,2048]{2,1,0:T(8,128)(2,1)S(1)} %slice_bitcast_fusion.14), channel_id=1, source_target_pairs={{2,0},{4,2},{6,4},{0,6},{3,1},{5,3},{7,5},{1,7},{10,8},{12,10},{14... | collective-permute-start | bytes 1572872 | tf_op jit(solution)/shard_map/ppermute | solution.py:55
  244.8 30.8 %collective-permute-start.7 = (bf16[4,64,2048]{2,1,0:T(8,128)(2,1)}, bf16[4,64,2048]{2,1,0:T(8,128)(2,1)S(1)}, u32[]{:S(2)}, u32[]{:S(2)}) collective-permute-start(bf16[4,64,2048]{2,1,0:T(8,128)(2,1)} %slice_bitcast_fusion.6), channel_id=1, source_target_pairs={{16,0},{0,16},{17,1},{1,17},{18,2},{2,18},{19,3},{3,19},{20,4},{4,... | collective-permute-start | bytes 3145736 | tf_op jit(solution)/shard_map/ppermute | solution.py:55
  257.6 13.8 %collective-permute-start.12 = (bf16[2,64,2048]{2,1,0:T(8,128)(2,1)S(1)}, bf16[2,64,2048]{2,1,0:T(8,128)(2,1)S(1)}, u32[]{:S(2)}, u32[]{:S(2)}) collective-permute-start(bf16[2,64,2048]{2,1,0:T(8,128)(2,1)S(1)} %fusion.20), channel_id=1, source_target_pairs={{2,0},{4,2},{6,4},{0,6},{3,1},{5,3},{7,5},{1,7},{10,8},{12,10},{14... | collective-permute-start | bytes 1572872 | tf_op jit(solution)/shard_map/ppermute | solution.py:55
  271.5 24.1 %collective-permute-start.13 = (bf16[2,64,2048]{2,1,0:T(8,128)(2,1)S(1)}, bf16[2,64,2048]{2,1,0:T(8,128)(2,1)S(1)}, u32[]{:S(2)}, u32[]{:S(2)}) collective-permute-start(bf16[2,64,2048]{2,1,0:T(8,128)(2,1)S(1)} %fusion.19), channel_id=1, source_target_pairs={{2,0},{4,2},{6,4},{0,6},{3,1},{5,3},{7,5},{1,7},{10,8},{12,10},{14... | collective-permute-start | bytes 1572872 | tf_op jit(solution)/shard_map/ppermute | solution.py:55
  276.0 15.3 %collective-permute-start.8 = (bf16[64,2048]{1,0:T(8,128)(2,1)S(1)}, bf16[64,2048]{1,0:T(8,128)(2,1)S(1)}, u32[]{:S(2)}, u32[]{:S(2)}) collective-permute-start(bf16[64,2048]{1,0:T(8,128)(2,1)S(1)} %slice_bitcast_fusion.20), channel_id=1, source_target_pairs={{2,0},{4,2},{6,4},{0,6},{3,1},{5,3},{7,5},{1,7},{10,8},{12,10},{14... | collective-permute-start | bytes 786440 | tf_op jit(solution)/shard_map/ppermute | solution.py:55
  284.1 23.8 %copy-start.2 = (bf16[128,2048]{1,0:T(8,128)(2,1)S(1)}, bf16[128,2048]{1,0:T(8,128)(2,1)}, u32[]{:S(2)}) copy-start(bf16[128,2048]{1,0:T(8,128)(2,1)} %param.16) | copy-start | bytes 1572868
  284.1 23.8 %copy-start.25 = (f32[2048]{0:T(1024)S(1)}, f32[2048]{0:T(1024)}, u32[]{:S(2)}) copy-start(f32[2048]{0:T(1024)} %param.27) | copy-start | bytes 24580
  284.1 24.1 %copy-start.31 = (f32[2048]{0:T(1024)S(1)}, f32[2048]{0:T(1024)}, u32[]{:S(2)}) copy-start(f32[2048]{0:T(1024)} %param.21) | copy-start | bytes 24580
  291.3 8.2 collective-permute-start.9
  295.8 8.1 collective-permute-start.14
  299.6 8.2 collective-permute-start.10
  309.3 264.9 %reduce-scatter.3.cloned.1.call-start = ((), (), s32[]{:S(2)}) async-start(), calls=%async_computation.12 | async-start | bytes 8912896 | tf_op jit(solution)/shard_map/reduce_scatter | solution.py:145
  309.4 122.4 %collective-permute-start.15 = (bf16[1408,2048]{1,0:T(8,128)(2,1)}, bf16[1408,2048]{1,0:T(8,128)(2,1)}, u32[]{:S(2)}, u32[]{:S(2)}) collective-permute-start(bf16[1408,2048]{1,0:T(8,128)(2,1)} %bitcast.296), channel_id=1, source_target_pairs={{1,0},{0,1},{3,2},{2,3},{5,4},{4,5},{7,6},{6,7},{9,8},{8,9},{11,10... | collective-permute-start | bytes 17301512 | tf_op jit(solution)/shard_map/ppermute | solution.py:55
  505.5 26.5 %collective-permute-start.16 = (bf16[2,4,128,2048]{3,2,0,1:T(8,128)(2,1)}, bf16[2,4,128,2048]{3,2,0,1:T(8,128)(2,1)}, u32[]{:S(2)}, u32[]{:S(2)}) collective-permute-start(bf16[2,4,128,2048]{3,2,0,1:T(8,128)(2,1)} %copy.75), channel_id=1, source_target_pairs={{8,0},{0,8},{9,1},{1,9},{10,2},{2,10},{11,3},{3,11},{12,4},{4,12},... | collective-permute-start | bytes 12582920 | tf_op jit(solution)/shard_map/ppermute | solution.py:55
  505.5 65.2 %collective-permute-start.20 = (bf16[704,2048]{1,0:T(8,128)(2,1)}, bf16[704,2048]{1,0:T(8,128)(2,1)}, u32[]{:S(2)}, u32[]{:S(2)}) collective-permute-start(bf16[704,2048]{1,0:T(8,128)(2,1)} %convolution_convert_fusion.3), channel_id=1, source_target_pairs={{1,0},{0,1},{3,2},{2,3},{5,4},{4,5},{7,6},{6,7},{9,8},{8,9},{11,10... | collective-permute-start | bytes 8650760 | tf_op jit(solution)/shard_map/ppermute | solution.py:55
  507.6 24.3 %all-to-all-start.4 = ((f32[16,1,128]{2,1,0:T(1,128)}), f32[16,1,128]{2,1,0:T(1,128)S(1)}, u32[]{:S(2)}, u32[]{:S(2)}) async-start(f32[16,1,128]{2,1,0:T(1,128)} %add.174), calls=%async_computation.5 | async-start | bytes 16384 | tf_op jit(solution)/shard_map/all_to_all | solution.py:135
  513.9 157.0 %all-gather.11.cloned.1.call-start = ((), (), s32[]{:S(2)}) async-start(), calls=%async_computation.13 | async-start | bytes 8912896 | tf_op jit(solution)/shard_map/all_gather | solution.py:141
  578.0 266.4 %reduce-scatter.5.cloned.1.call-start = ((), (), s32[]{:S(2)}) async-start(), calls=%async_computation.14 | async-start | bytes 8912896 | tf_op jit(solution)/shard_map/reduce_scatter | solution.py:145
  579.2 23.3 %collective-permute-start.17 = (bf16[2,64,2048]{2,1,0:T(8,128)(2,1)S(1)}, bf16[2,64,2048]{2,1,0:T(8,128)(2,1)S(1)}, u32[]{:S(2)}, u32[]{:S(2)}) collective-permute-start(bf16[2,64,2048]{2,1,0:T(8,128)(2,1)S(1)} %slice_bitcast_fusion.10), channel_id=1, source_target_pairs={{2,0},{4,2},{6,4},{0,6},{3,1},{5,3},{7,5},{1,7},{10,8},{12,10},{14... | collective-permute-start | bytes 1572872 | tf_op jit(solution)/shard_map/ppermute | solution.py:55
  603.7 17.4 %collective-permute-start.18 = (bf16[2,64,2048]{2,1,0:T(8,128)(2,1)S(1)}, bf16[2,64,2048]{2,1,0:T(8,128)(2,1)S(1)}, u32[]{:S(2)}, u32[]{:S(2)}) collective-permute-start(bf16[2,64,2048]{2,1,0:T(8,128)(2,1)S(1)} %fusion.17), channel_id=1, source_target_pairs={{2,0},{4,2},{6,4},{0,6},{3,1},{5,3},{7,5},{1,7},{10,8},{12,10},{14... | collective-permute-start | bytes 1572872 | tf_op jit(solution)/shard_map/ppermute | solution.py:55
  605.0 172.6 %collective-permute-start.36 = (bf16[1408,2048]{1,0:T(8,128)(2,1)}, bf16[1408,2048]{1,0:T(8,128)(2,1)}, u32[]{:S(2)}, u32[]{:S(2)}) collective-permute-start(bf16[1408,2048]{1,0:T(8,128)(2,1)} %convolution_convert_fusion), channel_id=1, source_target_pairs={{1,0},{0,1},{3,2},{2,3},{5,4},{4,5},{7,6},{6,7},{9,8},{8,9},{11,10... | collective-permute-start | bytes 17301512 | tf_op jit(solution)/shard_map/ppermute | solution.py:55
  622.2 29.9 %collective-permute-start.19 = (bf16[2,64,2048]{2,1,0:T(8,128)(2,1)S(1)}, bf16[2,64,2048]{2,1,0:T(8,128)(2,1)S(1)}, u32[]{:S(2)}, u32[]{:S(2)}) collective-permute-start(bf16[2,64,2048]{2,1,0:T(8,128)(2,1)S(1)} %fusion.16), channel_id=1, source_target_pairs={{2,0},{4,2},{6,4},{0,6},{3,1},{5,3},{7,5},{1,7},{10,8},{12,10},{14... | collective-permute-start | bytes 1572872 | tf_op jit(solution)/shard_map/ppermute | solution.py:55
  626.3 19.7 %copy-start.16 = (bf16[128,2048]{1,0:T(8,128)(2,1)S(1)}, bf16[128,2048]{1,0:T(8,128)(2,1)}, u32[]{:S(2)}) copy-start(bf16[128,2048]{1,0:T(8,128)(2,1)} %multiply_convert_fusion) | copy-start | bytes 1572868
  626.3 20.0 %copy-start.8 = (bf16[2,4,128,2048]{3,2,0,1:T(8,128)(2,1)S(1)}, bf16[2,4,128,2048]{3,2,0,1:T(8,128)(2,1)}, u32[]{:S(2)}) copy-start(bf16[2,4,128,2048]{3,2,0,1:T(8,128)(2,1)} %add_convert_fusion) | copy-start | bytes 12582916
  710.8 31.9 %all-to-all-start.5 = ((f32[16,1,128]{2,1,0:T(1,128)}), f32[16,1,128]{2,1,0:T(1,128)S(1)}, u32[]{:S(2)}, u32[]{:S(2)}) async-start(f32[16,1,128]{2,1,0:T(1,128)} %get-tuple-element.124), calls=%async_computation.6 | async-start | bytes 16384 | tf_op jit(solution)/shard_map/all_to_all | solution.py:135
  721.9 36.6 %collective-permute-start.23 = (bf16[4,64,2048]{2,1,0:T(8,128)(2,1)}, bf16[4,64,2048]{2,1,0:T(8,128)(2,1)}, u32[]{:S(2)}, u32[]{:S(2)}) collective-permute-start(bf16[4,64,2048]{2,1,0:T(8,128)(2,1)} %slice_bitcast_fusion.4), channel_id=1, source_target_pairs={{16,0},{0,16},{17,1},{1,17},{18,2},{2,18},{19,3},{3,19},{20,4},{4,... | collective-permute-start | bytes 3145736 | tf_op jit(solution)/shard_map/ppermute | solution.py:55
  742.6 18.7 %collective-permute-start.21 = (bf16[2,512,1024]{2,1,0:T(8,128)(2,1)}, bf16[2,512,1024]{2,1,0:T(8,128)(2,1)}, u32[]{:S(2)}, u32[]{:S(2)}) collective-permute-start(bf16[2,512,1024]{2,1,0:T(8,128)(2,1)} %fusion), channel_id=1, source_target_pairs={{0,8},{8,0},{1,9},{9,1},{2,10},{10,2},{3,11},{11,3},{4,12},{12,4},... | collective-permute-start | bytes 6291464 | tf_op jit(solution)/shard_map/ppermute | solution.py:191
  744.4 13.5 %collective-permute-start.28 = (f32[12,2048]{1,0:T(8,128)S(1)}, f32[12,2048]{1,0:T(8,128)S(1)}, u32[]{:S(2)}, u32[]{:S(2)}) collective-permute-start(f32[12,2048]{1,0:T(8,128)S(1)} %concatenate.43), channel_id=1, source_target_pairs={{0,1},{1,0},{2,3},{3,2},{4,5},{5,4},{6,7},{7,6},{8,9},{9,8},{10,11... | collective-permute-start | bytes 294920 | tf_op jit(solution)/shard_map/ppermute | solution.py:104
  768.6 36.9 %collective-permute-start.22 = (bf16[4,2,64,1024]{3,2,1,0:T(8,128)(2,1)}, bf16[4,2,64,1024]{3,2,1,0:T(8,128)(2,1)}, u32[]{:S(2)}, u32[]{:S(2)}) collective-permute-start(bf16[4,2,64,1024]{3,2,1,0:T(8,128)(2,1)} %bitcast.60), channel_id=1, source_target_pairs={{16,0},{0,16},{17,1},{1,17},{18,2},{2,18},{19,3},{3,19},{20,4},{4,... | collective-permute-start | bytes 3145736 | tf_op jit(solution)/shard_map/ppermute | solution.py:55
  777.1 35.2 %collective-permute-start.29 = (bf16[4,256,512]{2,1,0:T(8,128)(2,1)}, bf16[4,256,512]{2,1,0:T(8,128)(2,1)}, u32[]{:S(2)}, u32[]{:S(2)}) collective-permute-start(bf16[4,256,512]{2,1,0:T(8,128)(2,1)} %select_bitcast_fusion), channel_id=1, source_target_pairs={{1,0},{0,1},{3,2},{2,3},{5,4},{4,5},{7,6},{6,7},{9,8},{8,9},{11,10... | collective-permute-start | bytes 3145736 | tf_op jit(solution)/shard_map/ppermute | solution.py:55
  805.5 14.3 %collective-permute-start.24 = (bf16[64,2048]{1,0:T(8,128)(2,1)S(1)}, bf16[64,2048]{1,0:T(8,128)(2,1)S(1)}, u32[]{:S(2)}, u32[]{:S(2)}) collective-permute-start(bf16[64,2048]{1,0:T(8,128)(2,1)S(1)} %slice_bitcast_fusion.26), channel_id=1, source_target_pairs={{2,0},{4,2},{6,4},{0,6},{3,1},{5,3},{7,5},{1,7},{10,8},{12,10},{14... | collective-permute-start | bytes 786440 | tf_op jit(solution)/shard_map/ppermute | solution.py:55
  809.0 15.4 %collective-permute-start.27 = (bf16[64,2048]{1,0:T(8,128)(2,1)S(1)}, bf16[64,2048]{1,0:T(8,128)(2,1)S(1)}, u32[]{:S(2)}, u32[]{:S(2)}) collective-permute-start(bf16[64,2048]{1,0:T(8,128)(2,1)S(1)} %slice_bitcast_fusion.25), channel_id=1, source_target_pairs={{16,0},{0,16},{17,1},{1,17},{18,2},{2,18},{19,3},{3,19},{20,4},{4,... | collective-permute-start | bytes 786440 | tf_op jit(solution)/shard_map/ppermute | solution.py:55
  811.7 28.1 %collective-permute-start.30 = (bf16[4,64,1024]{2,1,0:T(8,128)(2,1)S(1)}, bf16[4,64,1024]{2,1,0:T(8,128)(2,1)S(1)}, u32[]{:S(2)}, u32[]{:S(2)}) collective-permute-start(bf16[4,64,1024]{2,1,0:T(8,128)(2,1)S(1)} %fusion.22), channel_id=1, source_target_pairs={{1,0},{0,1},{3,2},{2,3},{5,4},{4,5},{7,6},{6,7},{9,8},{8,9},{11,10... | collective-permute-start | bytes 1572872 | tf_op jit(solution)/shard_map/ppermute | solution.py:55
  819.8 16.8 %collective-permute-start.25 = (bf16[64,2048]{1,0:T(8,128)(2,1)S(1)}, bf16[64,2048]{1,0:T(8,128)(2,1)S(1)}, u32[]{:S(2)}, u32[]{:S(2)}) collective-permute-start(bf16[64,2048]{1,0:T(8,128)(2,1)S(1)} %fusion.26), channel_id=1, source_target_pairs={{2,0},{4,2},{6,4},{0,6},{3,1},{5,3},{7,5},{1,7},{10,8},{12,10},{14... | collective-permute-start | bytes 786440 | tf_op jit(solution)/shard_map/ppermute | solution.py:55
  836.6 7.0 collective-permute-start.26
  840.1 23.4 %collective-permute-start.35 = (bf16[256,2048]{1,0:T(8,128)(2,1)}, bf16[256,2048]{1,0:T(8,128)(2,1)}, u32[]{:S(2)}, u32[]{:S(2)}) collective-permute-start(bf16[256,2048]{1,0:T(8,128)(2,1)} %slice_select_fusion), channel_id=1, source_target_pairs={{1,0},{0,1},{3,2},{2,3},{5,4},{4,5},{7,6},{6,7},{9,8},{8,9},{11,10... | collective-permute-start | bytes 3145736 | tf_op jit(solution)/shard_map/ppermute | solution.py:55
  844.5 45.2 %all-to-all-start.6 = ((bf16[4,384,512]{2,1,0:T(8,128)(2,1)}), bf16[4,384,512]{2,1,0:T(8,128)(2,1)}, u32[]{:S(2)}, u32[]{:S(2)}) async-start(bf16[4,384,512]{2,1,0:T(8,128)(2,1)} %pad_maximum_fusion.3), calls=%async_computation.8 | async-start | bytes 3145728 | tf_op jit(solution)/shard_map/all_to_all | solution.py:162
  850.0 1.6 collective-permute-start.31
  851.3 28.9 %copy-start.12 = (f32[512,2048]{1,0:T(8,128)S(1)}, f32[512,2048]{1,0:T(8,128)}, u32[]{:S(2)}) copy-start(f32[512,2048]{1,0:T(8,128)} %copy-done.11) | copy-start | bytes 12582916
  852.6 5.8 collective-permute-start.32
  858.4 16.2 %collective-permute-start.33 = (f32[12,2048]{1,0:T(8,128)S(1)}, f32[12,2048]{1,0:T(8,128)S(1)}, u32[]{:S(2)}, u32[]{:S(2)}) collective-permute-start(f32[12,2048]{1,0:T(8,128)S(1)} %add.194), channel_id=1, source_target_pairs={{0,2},{2,0},{4,6},{6,4},{1,3},{3,1},{5,7},{7,5},{8,10},{10,8},{12,... | collective-permute-start | bytes 294920 | tf_op jit(solution)/shard_map/ppermute | solution.py:104
  874.7 13.7 %collective-permute-start.34 = (f32[12,2048]{1,0:T(8,128)S(1)}, f32[12,2048]{1,0:T(8,128)S(1)}, u32[]{:S(2)}, u32[]{:S(2)}) collective-permute-start(f32[12,2048]{1,0:T(8,128)S(1)} %add.195), channel_id=1, source_target_pairs={{0,4},{2,6},{4,0},{6,2},{1,5},{3,7},{5,1},{7,3},{8,12},{10,14},{12... | collective-permute-start | bytes 294920 | tf_op jit(solution)/shard_map/ppermute | solution.py:104
  880.2 20.1 %copy-start.1 = (f32[2048,4]{0,1:T(4,128)S(1)}, f32[2048,4]{0,1:T(4,128)}, u32[]{:S(2)}) copy-start(f32[2048,4]{0,1:T(4,128)} %param.23) | copy-start | bytes 98308
  (39 other events, 295.9 us)
Sparse Core Ops, SparseCore 0:
  11.4 84.9 all-gather.6
  114.9 92.3 all-gather.4
  309.4 76.8 all-gather.8
  467.7 106.4 reduce-scatter.2
  578.2 92.6 all-gather.10
  710.9 128.0 reduce-scatter.4

commit v15 on v13

--- a/solution.py
+++ b/solution.py
@@ -210,11 +210,11 @@
     rows, kv_rows = query.shape[1], kv.shape[1]
     sent = jnp.concatenate([query, kv[:, :, :half], kv[:, :, half:]], axis=1)
     sent = after(sent, *others)
-    here = exchange(sent).astype(F32)
+    here = exchange(sent)
     whole = [
         join_blocks(here[:, rows + k * kv_rows : rows + (k + 1) * kv_rows]) for k in range(2)
     ]
-    return join_blocks(here[:, :rows]), jnp.concatenate(whole, axis=1), sent
+    return join_blocks(here[:, :rows]).astype(F32), jnp.concatenate(whole, axis=1).astype(F32), sent
 
 
 def own_places():
@@ -755,14 +755,14 @@
     d_query = d_query[None]
     d_out = mm("tf,td->fd", gated, all_mid).reshape(inner, -1, width)
     d_out = from_order([d_out[k] for k in range(inner)], "i")
-    d_out = d_out[:1] + list(after(d_out[1:], kv_arrived))
-    d_output = ring_scatter(d_out, "i", d_query)[None]
+    d_out = d_out[:1] + list(after(d_out[1:], d_kv_last))
+    d_output = ring_scatter(d_out, "i", heads_sent)[None]
     rows_out = part_second(*after((rows_first, rows_second), kv_arrived))
     layer_out = middle + rows_out.astype(F32) + mlp_bias
     d_upper = (after(upper_last, kv_sent).astype(F32) + upper_own).reshape(up_weight.shape)
     d_lower = (lower_last.astype(F32) + lower_own)[None]
     d_attn_input = after(d_attn_input, summed)
-    summed = sum_over(after(summed, heads_sent), ("c", "o", "y"))
+    summed = sum_over(after(summed, heads_sent), ("c", "y", "o"))
     d_norm_one, _ = norm_back(
         residual, inverse_one, norm_gain1, d_attn_input.astype(F32) + d_att_from_router
     )

time: 869 us -> 868 us (level)
  waiting for transfers between devices: 336 us -> 327 us
    ppermute x5, waiting for transfers between devices: 32.5 us -> 22.5 us  [sum_over(): lax.ppermute(value, axis, [(k, k ^ step) for k in range(size)])]
  transfers between devices with their start and end apart: 48 -> 48, of which waited for: 24 -> 25; matrix products, arithmetic and copies ran while one was open for 23% -> 23% of each run, Pallas kernels for 16% -> 16%
where the time goes in v15:
time: 868 us; the launch traced here: 858 us
  waiting for transfers between devices  327 us (38%)
  Pallas kernels  170 us (20%)
  matrix products  115 us (13%)
  starting transfers between devices  101 us (12%)
  other arithmetic  80 us (9%)
  local copies, waits for them, and re-layouts  36.8 us (4%)
  between operations  15.4 us (2%)
  blocking collectives  13.1 us (2%)
    ppermute x31, waiting for transfers between devices, shift(): return lax.ppermute(value, axis, [((k + 1) % size, k) for k in range(size)])  223 us
    pallas_call x6, Pallas kernels, call(): pl.pallas_call(kernel, grid_spec=pltpu.PrefetchScalarGridSpec(num_scalar_...  170 us
    dot_general x9, matrix products, mm(): return jnp.einsum(form, first, second, preferred_element_type=F32)  108 us
    all_gather x4, waiting for transfers between devices, meet(): return lax.all_gather(rows, GROUP, axis=0, tiled=True)  78.5 us
    ppermute x31, starting transfers between devices, shift(): return lax.ppermute(value, axis, [((k + 1) % size, k) for k in range(size)])  61.2 us
    ppermute x5, waiting for transfers between devices, sum_over(): lax.ppermute(value, axis, [(k, k ^ step) for k in range(size)])  22.5 us
    convert_element_type x18, other arithmetic, add_low(): return (first.astype(F32) + second.astype(F32)).astype(BF16)  18.1 us
  transfers between devices with their start and end apart: 48, of which 25 were waited for; matrix products, arithmetic and copies ran while one was open for 23% of the time, Pallas kernels for 16%

profile of v15, /device:TPU:0, one launch (start us, length us, event | category | flops | bytes accessed | tf_op | source)
XLA Modules:
  0.0 858.3 jit_solution(155186654562598294)
XLA Ops:
  11.1 3.0 collective-permute-start
  16.7 4.9 all-to-all-start
  21.5 55.4 %collective-permute-done.refs_3_ = bf16[704,2048]{1,0:T(8,128)(2,1)} collective-permute-done((bf16[704,2048]{1,0:T(8,128)(2,1)}, bf16[704,2048]{1,0:T(8,128)(2,1)}, u32[]{:S(2)}, u32[]{:S(2)}) %collective-permute-start) | collective-permute-done | bytes 2883616 | tf_op jit(solution)/shard_map/ppermute | solution.py:55
  78.9 11.3 %collective-permute-done.1 = bf16[4,2,64,512]{3,2,1,0:T(8,128)(2,1)S(1)} collective-permute-done((bf16[4,2,64,512]{3,2,1,0:T(8,128)(2,1)S(1)}, bf16[4,2,64,512]{3,2,1,0:T(8,128)(2,1)S(1)}, u32[]{:S(2)}, u32[]{:S(2)}) %collective-permute-start.1) | collective-permute-done | bytes 524320 | tf_op jit(solution)/shard_map/ppermute | solution.py:55
  94.8 18.9 %collective-permute-done.2 = bf16[4,256,512]{2,1,0:T(8,128)(2,1)S(1)} collective-permute-done((bf16[4,256,512]{2,1,0:T(8,128)(2,1)S(1)}, bf16[4,256,512]{2,1,0:T(8,128)(2,1)S(1)}, u32[]{:S(2)}, u32[]{:S(2)}) %collective-permute-start.2) | collective-permute-done | bytes 1048608 | tf_op jit(solution)/shard_map/ppermute | solution.py:55
  113.7 6.3 collective-permute-done.3
  121.0 3.1 pad_maximum_fusion.1.own_ref
  125.9 4.8 all-to-all-start.1
  137.9 26.2 %attend.1 = (bf16[2048,1536]{1,0:T(8,128)(2,1)}, bf16[2048,512]{1,0:T(8,128)(2,1)}, bf16[2048,1024]{1,0:T(8,128)(2,1)}) custom-call(s32[4]{0:T(128)} %pad_add_fusion.places_ref, bf16[2048,2048]{1,0:T(8,128)(2,1)} %all-gather.7.cloned.1.call-done.x_ref, f32[16,2,128]{2,1,0:T(2,128)} %copy-done.37, f32[128,128]{1,0:T(8,128)} %get-tuple-element.191.cos_ref, ...), custom_call_target="tpu_custom_call" | custom-call | flops 13421772800 | bytes 25165824 | tf_op jit(solution)/shard_map/attend/pallas_call | solution.py:462
  167.0 10.5 %rows.2 = (bf16[2,4,128,2048]{3,2,1,0:T(8,128)(2,1)}, bf16[2,4,128,2048]{3,2,1,0:T(8,128)(2,1)}) custom-call(s32[4]{0:T(128)} %pad_add_fusion.places_ref, bf16[2048,512]{1,0:T(8,128)(2,1)} %get-tuple-element.89.refs_0_, bf16[512,2048]{1,0:T(8,128)(2,1)} %bitcast.308), custom_call_target="tpu_custom_call" | custom-call | flops 4294967296 | bytes 20971520 | tf_op jit(solution)/shard_map/rows/pallas_call | solution.py:462
  177.5 2.7 copy.72
  180.4 7.3 collective-permute-done.6
  190.0 3.6 collective-permute-start.11
  196.1 9.2 %collective-permute-done.11 = bf16[2,64,2048]{2,1,0:T(8,128)(2,1)S(1)} collective-permute-done((bf16[2,64,2048]{2,1,0:T(8,128)(2,1)S(1)}, bf16[2,64,2048]{2,1,0:T(8,128)(2,1)S(1)}, u32[]{:S(2)}, u32[]{:S(2)}) %collective-permute-start.11) | collective-permute-done | bytes 524320 | tf_op jit(solution)/shard_map/ppermute | solution.py:55
  205.4 4.3 collective-permute-start.12
  209.8 11.3 %convolution_convert_fusion.1.d_units_ref = bf16[2048,704]{1,0:T(8,128)(2,1)} fusion(bf16[2048,2048]{1,0:T(8,128)(2,1)} %all-gather.5.cloned.1.call-done, bf16[704,2048]{1,0:T(8,128)(2,1)} %collective-permute-done.refs_3_), kind=kOutput, calls=%fused_computation.9 | convolution fusion | flops 5907021824 | bytes 14155776 | tf_op jit(solution)/shard_map/td,fd->tf/dot_general | solution.py:149
  221.2 3.9 collective-permute-start.13
  225.6 8.1 convolution_convert_fusion.2.d_units_ref
  233.7 7.0 collective-permute-done.8
  240.8 4.3 collective-permute-start.9
  246.1 2.9 collective-permute-done.9
  249.1 4.3 collective-permute-start.10
  253.5 3.8 collective-permute-done.10
  261.1 13.1 %all_to_all.32.info_ref = f32[16,1,128]{2,1,0:T(1,128)} all-to-all(f32[16,1,128]{2,1,0:T(1,128)S(1)} %bitcast.321), channel_id=1, replica_groups=mesh['y'=2,'c'=2,'o'=4,'i'=2] {'y','c','o'}, dimensions={0} | all-to-all | bytes 16384 | tf_op jit(solution)/shard_map/all_to_all | solution.py:131
  274.2 60.6 %all-gather.9.cloned.1.call-done.x_ref = bf16[2048,2048]{1,0:T(8,128)(2,1)} async-done(((bf16[128,2048]{1,0:T(8,128)(2,1)}), bf16[2048,2048]{1,0:T(8,128)(2,1)}) %all-gather.9.cloned.1.call-update) | async-done | bytes 8388624 | tf_op jit(solution)/shard_map/all_gather | solution.py:141
  334.9 35.5 %units.2 = (bf16[2048,1408]{1,0:T(8,128)(2,1)}, bf16[2048,704]{1,0:T(8,128)(2,1)}, f32[2048,2048]{1,0:T(8,128)}, f32[16,1,128]{2,1,0:T(1,128)}) custom-call(s32[4]{0:T(128)} %pad_add_fusion.places_ref, bf16[2048,2048]{1,0:T(8,128)(2,1)} %all-gather.9.cloned.1.call-done.x_ref, f32[16,1,128]{2,1,0:T(1,128)} %all_to_all.32.info_ref, ...), custom_call_target="tpu_custom_call" | custom-call | tf_op jit(solution)/shard_map/units/pallas_call | solution.py:462
  370.4 10.8 %collective-permute-done.15.first_ref.second_ref = bf16[1408,2048]{1,0:T(8,128)(2,1)} collective-permute-done((bf16[1408,2048]{1,0:T(8,128)(2,1)}, bf16[1408,2048]{1,0:T(8,128)(2,1)}, u32[]{:S(2)}, u32[]{:S(2)}) %collective-permute-start.15) | collective-permute-done | bytes 5767200 | tf_op jit(solution)/shard_map/ppermute | solution.py:55
  381.2 35.9 %units.3 = (bf16[2048,1408]{1,0:T(8,128)(2,1)}, bf16[2048,704]{1,0:T(8,128)(2,1)}, bf16[2048,2048]{1,0:T(8,128)(2,1)}, f32[16,1,128]{2,1,0:T(1,128)}) custom-call(s32[4]{0:T(128)} %pad_add_fusion.places_ref, bf16[2048,2048]{1,0:T(8,128)(2,1)} %all-gather.9.cloned.1.call-done.x_ref, f32[16,1,128]{2,1,0:T(1,128)} %all_to_all.32.info_ref, ...), custom_call_target="tpu_custom_call" | custom-call | tf_op jit(solution)/shard_map/units/pallas_call | solution.py:462
  417.1 10.7 %convolution_convert_fusion.3 = bf16[704,2048]{1,0:T(8,128)(2,1)} fusion(bf16[2048,704]{1,0:T(8,128)(2,1)} %get-tuple-element.104.refs_1_, bf16[2048,2048]{1,0:T(8,128)(2,1)} %all-gather.5.cloned.1.call-done), kind=kOutput, calls=%fused_computation.11 | convolution fusion | flops 5907021824 | bytes 14155776 | tf_op jit(solution)/shard_map/tf,td->fd/dot_general | solution.py:149
  427.8 21.8 %rows.3 = (bf16[2,4,128,2048]{3,2,1,0:T(8,128)(2,1)}, bf16[2,4,128,2048]{3,2,1,0:T(8,128)(2,1)}) custom-call(s32[4]{0:T(128)} %pad_add_fusion.places_ref, bf16[2048,704]{1,0:T(8,128)(2,1)} %get-tuple-element.103.refs_0_, bf16[2048,704]{1,0:T(8,128)(2,1)} %get-tuple-element.104.refs_1_, bf16[704,2048]{1,0:T(8,128)(2,1)} %bitcast.335, ...), custom_call_target="tpu_custom_call" | custom-call | flops 11811160064 | bytes 28311552 | tf_op jit(solution)/shard_map/rows/pallas_call | solution.py:462
  449.7 4.9 copy.75
  456.2 6.2 all-to-all-start.3
  462.5 18.0 %convolution_convert_fusion = bf16[1408,2048]{1,0:T(8,128)(2,1)} fusion(bf16[2048,1408]{1,0:T(8,128)(2,1)} %get-tuple-element.108, bf16[2048,2048]{1,0:T(8,128)(2,1)} %all-gather.9.cloned.1.call-done.x_ref), kind=kOutput, calls=%fused_computation.3 | convolution fusion | flops 11814043648 | bytes 19922944 | tf_op jit(solution)/shard_map/tf,td->fd/dot_general | solution.py:149
  480.6 7.9 add_convert_fusion
  488.5 31.3 %collective-permute-done.20 = bf16[704,2048]{1,0:T(8,128)(2,1)} collective-permute-done((bf16[704,2048]{1,0:T(8,128)(2,1)}, bf16[704,2048]{1,0:T(8,128)(2,1)}, u32[]{:S(2)}, u32[]{:S(2)}) %collective-permute-start.20) | collective-permute-done | bytes 2883616 | tf_op jit(solution)/shard_map/ppermute | solution.py:55
  519.8 2.9 reduce-scatter.3.cloned.1.call-done
  529.9 21.2 %collective-permute-done.17 = bf16[2,64,2048]{2,1,0:T(8,128)(2,1)S(1)} collective-permute-done((bf16[2,64,2048]{2,1,0:T(8,128)(2,1)S(1)}, bf16[2,64,2048]{2,1,0:T(8,128)(2,1)S(1)}, u32[]{:S(2)}, u32[]{:S(2)}) %collective-permute-start.17) | collective-permute-done | bytes 524320 | tf_op jit(solution)/shard_map/ppermute | solution.py:55
  554.8 14.7 %collective-permute-done.18 = bf16[2,64,2048]{2,1,0:T(8,128)(2,1)S(1)} collective-permute-done((bf16[2,64,2048]{2,1,0:T(8,128)(2,1)S(1)}, bf16[2,64,2048]{2,1,0:T(8,128)(2,1)S(1)}, u32[]{:S(2)}, u32[]{:S(2)}) %collective-permute-start.18) | collective-permute-done | bytes 524320 | tf_op jit(solution)/shard_map/ppermute | solution.py:55
  570.7 4.1 collective-permute-start.19
  574.8 19.6 %fusion.61 = f32[1408,2048]{1,0:T(8,128)} fusion(bf16[2048,1408]{1,0:T(8,128)(2,1)} %get-tuple-element.144, bf16[2048,2048]{1,0:T(8,128)(2,1)} %all-gather.9.cloned.1.call-done.x_ref), kind=kOutput, calls=%fused_computation.198 | convolution fusion | flops 11811160064 | bytes 25690112 | tf_op jit(solution)/shard_map/tf,td->fd/dot_general | solution.py:149
  596.2 4.3 collective-permute-done.19
  601.5 17.9 %all-gather.11.cloned.1.call-done.mid_ref = bf16[2048,2048]{1,0:T(8,128)(2,1)} async-done(((bf16[128,2048]{1,0:T(8,128)(2,1)}), bf16[2048,2048]{1,0:T(8,128)(2,1)}) %all-gather.11.cloned.1.call-update) | async-done | bytes 8388624 | tf_op jit(solution)/shard_map/all_gather | solution.py:141
  619.4 39.6 %attend_back.1 = (bf16[2048,512]{1,0:T(8,128)(2,1)}, bf16[2048,1024]{1,0:T(8,128)(2,1)}, bf16[2048,2048]{1,0:T(8,128)(2,1)}, f32[16,1,128]{2,1,0:T(1,128)}, f32[1,2048]{1,0:T(1,128)}) custom-call(s32[4]{0:T(128)} %pad_add_fusion.places_ref, bf16[2048,2048]{1,0:T(8,128)(2,1)} %all-gather.11.cloned.1.call-done.mid_ref, f32[16,2,128]{2,1,0:T(2,128)} %copy-done.37, ...), custom_call_target="tpu_custom_call" | custom-call | flops 18522046464 | bytes 46137344 | tf_op jit(solution)/shard_map/attend_back/pallas_call | solution.py:462
  659.0 8.6 all-to-all-start.4
  671.9 13.8 %fusion.56 = f32[2048,1024]{1,0:T(8,128)S(1)} fusion(bf16[2048,2048]{1,0:T(8,128)(2,1)} %all-gather.7.cloned.1.call-done.x_ref, bf16[2048,1024]{1,0:T(8,128)(2,1)} %get-tuple-element.117), kind=kOutput, calls=%fused_computation.193 | convolution fusion | flops 8589934592 | bytes 20971520 | tf_op jit(solution)/shard_map/td,tf->df/dot_general | solution.py:149
  685.7 3.2 copy-done.5
  694.0 11.8 %add_bitcast_fusion = f32[1,704,2048]{2,1,0:T(8,128)} fusion(bf16[704,2048]{1,0:T(8,128)(2,1)} %collective-permute-done.20, bf16[2048,704]{1,0:T(8,128)(2,1)} %get-tuple-element.103.refs_0_, bf16[2048,2048]{1,0:T(8,128)(2,1)} %all-gather.5.cloned.1.call-done), kind=kOutput, calls=%fused_computation.4 | convolution fusion | flops 5908463616 | bytes 19922944 | tf_op jit(solution)/shard_map/tf,td->fd/dot_general | solution.py:149
  706.6 2.6 fusion.1
  709.2 5.7 bitcast_add_fusion
  718.1 7.2 fusion.59
  729.5 13.5 %convert_add_fusion = f32[1408,2048]{1,0:T(8,128)} fusion(f32[1408,2048]{1,0:T(8,128)} %fusion.61, bf16[1408,2048]{1,0:T(8,128)(2,1)} %collective-permute-done.36), kind=kLoop, calls=%fused_computation | loop fusion | flops 5767168 | bytes 28835840 | tf_op jit(solution)/shard_map/add | solution.py:762
  743.1 7.7 fusion.60
  754.3 3.2 collective-permute-start.24
  763.7 5.3 collective-permute-done.24
  769.0 4.4 collective-permute-start.25
  773.5 11.7 %collective-permute-done.25 = bf16[64,2048]{1,0:T(8,128)(2,1)S(1)} collective-permute-done((bf16[64,2048]{1,0:T(8,128)(2,1)S(1)}, bf16[64,2048]{1,0:T(8,128)(2,1)S(1)}, u32[]{:S(2)}, u32[]{:S(2)}) %collective-permute-start.25) | collective-permute-done | bytes 262176 | tf_op jit(solution)/shard_map/ppermute | solution.py:55
  785.2 4.3 collective-permute-start.26
  794.2 5.7 all-to-all-start.5
  802.4 5.7 collective-permute-done.32
  810.2 3.0 fusion.12
  813.3 11.5 %collective-permute-done.33 = f32[12,2048]{1,0:T(8,128)S(1)} collective-permute-done((f32[12,2048]{1,0:T(8,128)S(1)}, f32[12,2048]{1,0:T(8,128)S(1)}, u32[]{:S(2)}, u32[]{:S(2)}) %collective-permute-start.33) | collective-permute-done | bytes 98336 | tf_op jit(solution)/shard_map/ppermute | solution.py:104
  824.8 6.2 collective-permute-start.34
  831.0 3.0 add_bitcast_fusion.1
  834.0 5.1 collective-permute-done.34
  (291 shorter events, 101.2 us)
Async XLA Ops:
  7.2 252.2 %copy-start = (f32[2048,4]{0,1:T(4,128)S(1)}, f32[2048,4]{0,1:T(4,128)}, u32[]{:S(2)}) copy-start(f32[2048,4]{0,1:T(4,128)} %param.23) | copy-start | bytes 98308
  7.2 130.1 %all-gather.7.cloned.1.call-start = ((), (), s32[]{:S(2)}) async-start(), calls=%async_computation.9 | async-start | bytes 8912896 | tf_op jit(solution)/shard_map/all_gather | solution.py:141
  11.1 65.8 %collective-permute-start = (bf16[704,2048]{1,0:T(8,128)(2,1)}, bf16[704,2048]{1,0:T(8,128)(2,1)}, u32[]{:S(2)}, u32[]{:S(2)}) collective-permute-start(bf16[704,2048]{1,0:T(8,128)(2,1)} %bitcast.334), channel_id=1, source_target_pairs={{1,0},{0,1},{3,2},{2,3},{5,4},{4,5},{7,6},{6,7},{9,8},{8,9},{11,10... | collective-permute-start | bytes 8650760 | tf_op jit(solution)/shard_map/ppermute | solution.py:55
  16.7 60.3 %all-to-all-start = ((bf16[4,384,512]{2,1,0:T(8,128)(2,1)}), bf16[4,384,512]{2,1,0:T(8,128)(2,1)S(1)}, u32[]{:S(2)}, u32[]{:S(2)}) async-start(bf16[4,384,512]{2,1,0:T(8,128)(2,1)} %maximum_maximum_fusion), calls=%async_computation | async-start | bytes 3145728 | tf_op jit(solution)/shard_map/all_to_all | solution.py:162
  21.5 71.8 %copy-start.19 = (f32[128,2048]{1,0:T(8,128)S(1)}, f32[128,2048]{1,0:T(8,128)}, u32[]{:S(2)}) copy-start(f32[128,2048]{1,0:T(8,128)} %param.31) | copy-start | bytes 3145732
  21.5 188.2 %all-gather.5.cloned.1.call-start = ((), (), s32[]{:S(2)}) async-start(), calls=%async_computation.8 | async-start | bytes 8912896 | tf_op jit(solution)/shard_map/all_gather | solution.py:141
  77.0 13.2 %collective-permute-start.1 = (bf16[4,2,64,512]{3,2,1,0:T(8,128)(2,1)S(1)}, bf16[4,2,64,512]{3,2,1,0:T(8,128)(2,1)S(1)}, u32[]{:S(2)}, u32[]{:S(2)}) collective-permute-start(bf16[4,2,64,512]{3,2,1,0:T(8,128)(2,1)S(1)} %bitcast.310), channel_id=1, source_target_pairs={{1,0},{0,1},{3,2},{2,3},{5,4},{4,5},{7,6},{6,7},{9,8},{8,9},{11,10... | collective-permute-start | bytes 1572872 | tf_op jit(solution)/shard_map/ppermute | solution.py:55
  90.1 23.5 %collective-permute-start.2 = (bf16[4,256,512]{2,1,0:T(8,128)(2,1)S(1)}, bf16[4,256,512]{2,1,0:T(8,128)(2,1)S(1)}, u32[]{:S(2)}, u32[]{:S(2)}) collective-permute-start(bf16[4,256,512]{2,1,0:T(8,128)(2,1)S(1)} %slice.265), channel_id=1, source_target_pairs={{1,0},{0,1},{3,2},{2,3},{5,4},{4,5},{7,6},{6,7},{9,8},{8,9},{11,10... | collective-permute-start | bytes 3145736 | tf_op jit(solution)/shard_map/ppermute | solution.py:55
  91.7 22.0 %copy-start.22 = (bf16[2,4,2,64,512]{4,3,2,1,0:T(8,128)(2,1)}, bf16[2,4,2,64,512]{4,3,2,1,0:T(8,128)(2,1)S(1)}, u32[]{:S(2)}) copy-start(bf16[2,4,2,64,512]{4,3,2,1,0:T(8,128)(2,1)S(1)} %pad_maximum_fusion.4) | copy-start | bytes 3145732
  91.7 32.4 %copy-start.14 = (bf16[128,2048]{1,0:T(8,128)(2,1)S(1)}, bf16[128,2048]{1,0:T(8,128)(2,1)}, u32[]{:S(2)}) copy-start(bf16[128,2048]{1,0:T(8,128)(2,1)} %fusion.6) | copy-start | bytes 1572868
  91.7 32.4 %copy-start.31 = (f32[2048,4]{0,1:T(4,128)S(1)}, f32[2048,4]{0,1:T(4,128)}, u32[]{:S(2)}) copy-start(f32[2048,4]{0,1:T(4,128)} %param.22) | copy-start | bytes 98308
  91.7 32.9 %copy-start.39 = (s32[128,2]{0,1:T(2,128)S(1)}, s32[128,2]{0,1:T(2,128)}, u32[]{:S(2)}) copy-start(s32[128,2]{0,1:T(2,128)} %param.18) | copy-start | bytes 3076
  91.7 33.5 %copy-start.54 = (s32[1,128]{1,0:T(1,128)S(1)}, s32[1,128]{1,0:T(1,128)}, u32[]{:S(2)}) copy-start(s32[1,128]{1,0:T(1,128)} %param.17) | copy-start | bytes 1540
  91.7 28.3 %collective-permute-start.3 = (bf16[2,4,2,64,512]{4,3,2,1,0:T(8,128)(2,1)S(1)}, bf16[2,4,2,64,512]{4,3,2,1,0:T(8,128)(2,1)S(1)}, u32[]{:S(2)}, u32[]{:S(2)}) collective-permute-start(bf16[2,4,2,64,512]{4,3,2,1,0:T(8,128)(2,1)S(1)} %pad_maximum_fusion.4), channel_id=1, source_target_pairs={{16,0},{0,16},{17,1},{1,17},{18,2},{2,18},{19,3},{3,19},{20,4},{4,... | collective-permute-start | bytes 3145736 | tf_op jit(solution)/shard_map/ppermute | solution.py:55
  94.8 39.2 %copy-start.21 = (bf16[4,256,512]{2,1,0:T(8,128)(2,1)S(1)}, bf16[4,256,512]{2,1,0:T(8,128)(2,1)}, u32[]{:S(2)}) copy-start(bf16[4,256,512]{2,1,0:T(8,128)(2,1)} %copy-done.20) | copy-start | bytes 3145732
  124.0 13.2 %collective-permute-start.4 = (bf16[2,2,4,2,64,512]{5,4,3,2,1,0:T(8,128)(2,1)}, bf16[2,2,4,2,64,512]{5,4,3,2,1,0:T(8,128)(2,1)}, u32[]{:S(2)}, u32[]{:S(2)}) collective-permute-start(bf16[2,2,4,2,64,512]{5,4,3,2,1,0:T(8,128)(2,1)} %pad_maximum_fusion.1.own_ref), channel_id=1, source_target_pairs={{8,0},{0,8},{9,1},{1,9},{10,2},{2,10},{11,3},{3,11},{12,4},{4,12},... | collective-permute-start | bytes 6291464 | tf_op jit(solution)/shard_map/ppermute | solution.py:55
  125.9 11.4 %all-to-all-start.1 = ((f32[16,2,128]{2,1,0:T(2,128)}), f32[16,2,128]{2,1,0:T(2,128)S(1)}, u32[]{:S(2)}, u32[]{:S(2)}) async-start(f32[16,2,128]{2,1,0:T(2,128)} %pad_maximum_fusion.8), calls=%async_computation.1 | async-start | bytes 32768 | tf_op jit(solution)/shard_map/all_to_all | solution.py:131
  130.7 204.1 %all-gather.9.cloned.1.call-start = ((), (), s32[]{:S(2)}) async-start(), calls=%async_computation.10 | async-start | bytes 8912896 | tf_op jit(solution)/shard_map/all_gather | solution.py:141
  132.5 31.6 %collective-permute-start.5 = (bf16[256,2048]{1,0:T(8,128)(2,1)}, bf16[256,2048]{1,0:T(8,128)(2,1)}, u32[]{:S(2)}, u32[]{:S(2)}) collective-permute-start(bf16[256,2048]{1,0:T(8,128)(2,1)} %bitcast.312), channel_id=1, source_target_pairs={{1,0},{0,1},{3,2},{2,3},{5,4},{4,5},{7,6},{6,7},{9,8},{8,9},{11,10... | collective-permute-start | bytes 3145736 | tf_op jit(solution)/shard_map/ppermute | solution.py:55
  137.9 26.2 %copy-start.25 = (bf16[1,256,2048]{2,1,0:T(8,128)(2,1)S(1)}, bf16[1,256,2048]{2,1,0:T(8,128)(2,1)}, u32[]{:S(2)}) copy-start(bf16[1,256,2048]{2,1,0:T(8,128)(2,1)} %param.26) | copy-start | bytes 3145732
  180.2 7.5 collective-permute-start.6
  190.0 15.3 %collective-permute-start.11 = (bf16[2,64,2048]{2,1,0:T(8,128)(2,1)S(1)}, bf16[2,64,2048]{2,1,0:T(8,128)(2,1)S(1)}, u32[]{:S(2)}, u32[]{:S(2)}) collective-permute-start(bf16[2,64,2048]{2,1,0:T(8,128)(2,1)S(1)} %slice_bitcast_fusion.14), channel_id=1, source_target_pairs={{2,0},{4,2},{6,4},{0,6},{3,1},{5,3},{7,5},{1,7},{10,8},{12,10},{14... | collective-permute-start | bytes 1572872 | tf_op jit(solution)/shard_map/ppermute | solution.py:55
  194.6 30.5 %collective-permute-start.7 = (bf16[4,64,2048]{2,1,0:T(8,128)(2,1)}, bf16[4,64,2048]{2,1,0:T(8,128)(2,1)S(1)}, u32[]{:S(2)}, u32[]{:S(2)}) collective-permute-start(bf16[4,64,2048]{2,1,0:T(8,128)(2,1)} %slice_bitcast_fusion.6), channel_id=1, source_target_pairs={{16,0},{0,16},{17,1},{1,17},{18,2},{2,18},{19,3},{3,19},{20,4},{4,... | collective-permute-start | bytes 3145736 | tf_op jit(solution)/shard_map/ppermute | solution.py:55
  205.4 15.6 %collective-permute-start.12 = (bf16[2,64,2048]{2,1,0:T(8,128)(2,1)S(1)}, bf16[2,64,2048]{2,1,0:T(8,128)(2,1)S(1)}, u32[]{:S(2)}, u32[]{:S(2)}) collective-permute-start(bf16[2,64,2048]{2,1,0:T(8,128)(2,1)S(1)} %fusion.20), channel_id=1, source_target_pairs={{2,0},{4,2},{6,4},{0,6},{3,1},{5,3},{7,5},{1,7},{10,8},{12,10},{14... | collective-permute-start | bytes 1572872 | tf_op jit(solution)/shard_map/ppermute | solution.py:55
  221.2 23.9 %collective-permute-start.13 = (bf16[2,64,2048]{2,1,0:T(8,128)(2,1)S(1)}, bf16[2,64,2048]{2,1,0:T(8,128)(2,1)S(1)}, u32[]{:S(2)}, u32[]{:S(2)}) collective-permute-start(bf16[2,64,2048]{2,1,0:T(8,128)(2,1)S(1)} %fusion.19), channel_id=1, source_target_pairs={{2,0},{4,2},{6,4},{0,6},{3,1},{5,3},{7,5},{1,7},{10,8},{12,10},{14... | collective-permute-start | bytes 1572872 | tf_op jit(solution)/shard_map/ppermute | solution.py:55
  225.6 15.2 %collective-permute-start.8 = (bf16[64,2048]{1,0:T(8,128)(2,1)S(1)}, bf16[64,2048]{1,0:T(8,128)(2,1)S(1)}, u32[]{:S(2)}, u32[]{:S(2)}) collective-permute-start(bf16[64,2048]{1,0:T(8,128)(2,1)S(1)} %slice_bitcast_fusion.20), channel_id=1, source_target_pairs={{2,0},{4,2},{6,4},{0,6},{3,1},{5,3},{7,5},{1,7},{10,8},{12,10},{14... | collective-permute-start | bytes 786440 | tf_op jit(solution)/shard_map/ppermute | solution.py:55
  233.7 23.8 %copy-start.2 = (bf16[128,2048]{1,0:T(8,128)(2,1)S(1)}, bf16[128,2048]{1,0:T(8,128)(2,1)}, u32[]{:S(2)}) copy-start(bf16[128,2048]{1,0:T(8,128)(2,1)} %param.16) | copy-start | bytes 1572868
  233.7 23.8 %copy-start.29 = (f32[2048]{0:T(1024)S(1)}, f32[2048]{0:T(1024)}, u32[]{:S(2)}) copy-start(f32[2048]{0:T(1024)} %param.27) | copy-start | bytes 24580
  240.8 17.0 %copy-start.35 = (f32[2048]{0:T(1024)S(1)}, f32[2048]{0:T(1024)}, u32[]{:S(2)}) copy-start(f32[2048]{0:T(1024)} %param.21) | copy-start | bytes 24580
  240.8 8.2 collective-permute-start.9
  245.3 8.1 collective-permute-start.14
  249.1 8.2 collective-permute-start.10
  258.9 263.8 %reduce-scatter.3.cloned.1.call-start = ((), (), s32[]{:S(2)}) async-start(), calls=%async_computation.11 | async-start | bytes 8912896 | tf_op jit(solution)/shard_map/reduce_scatter | solution.py:145
  258.9 122.3 %collective-permute-start.15 = (bf16[1408,2048]{1,0:T(8,128)(2,1)}, bf16[1408,2048]{1,0:T(8,128)(2,1)}, u32[]{:S(2)}, u32[]{:S(2)}) collective-permute-start(bf16[1408,2048]{1,0:T(8,128)(2,1)} %bitcast.296), channel_id=1, source_target_pairs={{1,0},{0,1},{3,2},{2,3},{5,4},{4,5},{7,6},{6,7},{9,8},{8,9},{11,10... | collective-permute-start | bytes 17301512 | tf_op jit(solution)/shard_map/ppermute | solution.py:55
  454.6 26.0 %collective-permute-start.16 = (bf16[2,4,128,2048]{3,2,0,1:T(8,128)(2,1)}, bf16[2,4,128,2048]{3,2,0,1:T(8,128)(2,1)}, u32[]{:S(2)}, u32[]{:S(2)}) collective-permute-start(bf16[2,4,128,2048]{3,2,0,1:T(8,128)(2,1)} %copy.75), channel_id=1, source_target_pairs={{8,0},{0,8},{9,1},{1,9},{10,2},{2,10},{11,3},{3,11},{12,4},{4,12},... | collective-permute-start | bytes 12582920 | tf_op jit(solution)/shard_map/ppermute | solution.py:55
  454.6 65.2 %collective-permute-start.20 = (bf16[704,2048]{1,0:T(8,128)(2,1)}, bf16[704,2048]{1,0:T(8,128)(2,1)}, u32[]{:S(2)}, u32[]{:S(2)}) collective-permute-start(bf16[704,2048]{1,0:T(8,128)(2,1)} %convolution_convert_fusion.3), channel_id=1, source_target_pairs={{1,0},{0,1},{3,2},{2,3},{5,4},{4,5},{7,6},{6,7},{9,8},{8,9},{11,10... | collective-permute-start | bytes 8650760 | tf_op jit(solution)/shard_map/ppermute | solution.py:55
  456.2 24.3 %all-to-all-start.3 = ((f32[16,1,128]{2,1,0:T(1,128)}), f32[16,1,128]{2,1,0:T(1,128)S(1)}, u32[]{:S(2)}, u32[]{:S(2)}) async-start(f32[16,1,128]{2,1,0:T(1,128)} %add.174), calls=%async_computation.4 | async-start | bytes 16384 | tf_op jit(solution)/shard_map/all_to_all | solution.py:135
  462.4 157.0 %all-gather.11.cloned.1.call-start = ((), (), s32[]{:S(2)}) async-start(), calls=%async_computation.12 | async-start | bytes 8912896 | tf_op jit(solution)/shard_map/all_gather | solution.py:141
  526.5 267.6 %reduce-scatter.5.cloned.1.call-start = ((), (), s32[]{:S(2)}) async-start(), calls=%async_computation.13 | async-start | bytes 8912896 | tf_op jit(solution)/shard_map/reduce_scatter | solution.py:145
  527.7 23.4 %collective-permute-start.17 = (bf16[2,64,2048]{2,1,0:T(8,128)(2,1)S(1)}, bf16[2,64,2048]{2,1,0:T(8,128)(2,1)S(1)}, u32[]{:S(2)}, u32[]{:S(2)}) collective-permute-start(bf16[2,64,2048]{2,1,0:T(8,128)(2,1)S(1)} %slice_bitcast_fusion.10), channel_id=1, source_target_pairs={{2,0},{4,2},{6,4},{0,6},{3,1},{5,3},{7,5},{1,7},{10,8},{12,10},{14... | collective-permute-start | bytes 1572872 | tf_op jit(solution)/shard_map/ppermute | solution.py:55
  552.3 17.2 %collective-permute-start.18 = (bf16[2,64,2048]{2,1,0:T(8,128)(2,1)S(1)}, bf16[2,64,2048]{2,1,0:T(8,128)(2,1)S(1)}, u32[]{:S(2)}, u32[]{:S(2)}) collective-permute-start(bf16[2,64,2048]{2,1,0:T(8,128)(2,1)S(1)} %fusion.17), channel_id=1, source_target_pairs={{2,0},{4,2},{6,4},{0,6},{3,1},{5,3},{7,5},{1,7},{10,8},{12,10},{14... | collective-permute-start | bytes 1572872 | tf_op jit(solution)/shard_map/ppermute | solution.py:55
  553.4 176.1 %collective-permute-start.36 = (bf16[1408,2048]{1,0:T(8,128)(2,1)}, bf16[1408,2048]{1,0:T(8,128)(2,1)}, u32[]{:S(2)}, u32[]{:S(2)}) collective-permute-start(bf16[1408,2048]{1,0:T(8,128)(2,1)} %convolution_convert_fusion), channel_id=1, source_target_pairs={{1,0},{0,1},{3,2},{2,3},{5,4},{4,5},{7,6},{6,7},{9,8},{8,9},{11,10... | collective-permute-start | bytes 17301512 | tf_op jit(solution)/shard_map/ppermute | solution.py:55
  570.7 29.8 %collective-permute-start.19 = (bf16[2,64,2048]{2,1,0:T(8,128)(2,1)S(1)}, bf16[2,64,2048]{2,1,0:T(8,128)(2,1)S(1)}, u32[]{:S(2)}, u32[]{:S(2)}) collective-permute-start(bf16[2,64,2048]{2,1,0:T(8,128)(2,1)S(1)} %fusion.16), channel_id=1, source_target_pairs={{2,0},{4,2},{6,4},{0,6},{3,1},{5,3},{7,5},{1,7},{10,8},{12,10},{14... | collective-permute-start | bytes 1572872 | tf_op jit(solution)/shard_map/ppermute | solution.py:55
  574.8 19.6 %copy-start.16 = (bf16[128,2048]{1,0:T(8,128)(2,1)S(1)}, bf16[128,2048]{1,0:T(8,128)(2,1)}, u32[]{:S(2)}) copy-start(bf16[128,2048]{1,0:T(8,128)(2,1)} %multiply_convert_fusion) | copy-start | bytes 1572868
  574.8 20.0 %copy-start.8 = (bf16[2,4,128,2048]{3,2,0,1:T(8,128)(2,1)S(1)}, bf16[2,4,128,2048]{3,2,0,1:T(8,128)(2,1)}, u32[]{:S(2)}) copy-start(bf16[2,4,128,2048]{3,2,0,1:T(8,128)(2,1)} %add_convert_fusion) | copy-start | bytes 12582916
  659.0 31.8 %all-to-all-start.4 = ((f32[16,1,128]{2,1,0:T(1,128)}), f32[16,1,128]{2,1,0:T(1,128)S(1)}, u32[]{:S(2)}, u32[]{:S(2)}) async-start(f32[16,1,128]{2,1,0:T(1,128)} %get-tuple-element.124), calls=%async_computation.5 | async-start | bytes 16384 | tf_op jit(solution)/shard_map/all_to_all | solution.py:135
  669.9 36.6 %collective-permute-start.23 = (bf16[4,64,2048]{2,1,0:T(8,128)(2,1)}, bf16[4,64,2048]{2,1,0:T(8,128)(2,1)}, u32[]{:S(2)}, u32[]{:S(2)}) collective-permute-start(bf16[4,64,2048]{2,1,0:T(8,128)(2,1)} %slice_bitcast_fusion.4), channel_id=1, source_target_pairs={{16,0},{0,16},{17,1},{1,17},{18,2},{2,18},{19,3},{3,19},{20,4},{4,... | collective-permute-start | bytes 3145736 | tf_op jit(solution)/shard_map/ppermute | solution.py:55
  690.8 18.4 %collective-permute-start.21 = (bf16[2,512,1024]{2,1,0:T(8,128)(2,1)}, bf16[2,512,1024]{2,1,0:T(8,128)(2,1)}, u32[]{:S(2)}, u32[]{:S(2)}) collective-permute-start(bf16[2,512,1024]{2,1,0:T(8,128)(2,1)} %fusion), channel_id=1, source_target_pairs={{0,8},{8,0},{1,9},{9,1},{2,10},{10,2},{3,11},{11,3},{4,12},{12,4},... | collective-permute-start | bytes 6291464 | tf_op jit(solution)/shard_map/ppermute | solution.py:197
  692.5 13.4 %collective-permute-start.28 = (f32[12,2048]{1,0:T(8,128)S(1)}, f32[12,2048]{1,0:T(8,128)S(1)}, u32[]{:S(2)}, u32[]{:S(2)}) collective-permute-start(f32[12,2048]{1,0:T(8,128)S(1)} %concatenate.43), channel_id=1, source_target_pairs={{0,1},{1,0},{2,3},{3,2},{4,5},{5,4},{6,7},{7,6},{8,9},{9,8},{10,11... | collective-permute-start | bytes 294920 | tf_op jit(solution)/shard_map/ppermute | solution.py:104
  716.1 37.9 %collective-permute-start.22 = (bf16[4,2,64,1024]{3,2,1,0:T(8,128)(2,1)}, bf16[4,2,64,1024]{3,2,1,0:T(8,128)(2,1)}, u32[]{:S(2)}, u32[]{:S(2)}) collective-permute-start(bf16[4,2,64,1024]{3,2,1,0:T(8,128)(2,1)} %bitcast.60), channel_id=1, source_target_pairs={{16,0},{0,16},{17,1},{1,17},{18,2},{2,18},{19,3},{3,19},{20,4},{4,... | collective-permute-start | bytes 3145736 | tf_op jit(solution)/shard_map/ppermute | solution.py:55
  728.4 33.3 %collective-permute-start.29 = (bf16[4,256,512]{2,1,0:T(8,128)(2,1)}, bf16[4,256,512]{2,1,0:T(8,128)(2,1)}, u32[]{:S(2)}, u32[]{:S(2)}) collective-permute-start(bf16[4,256,512]{2,1,0:T(8,128)(2,1)} %select_bitcast_fusion), channel_id=1, source_target_pairs={{1,0},{0,1},{3,2},{2,3},{5,4},{4,5},{7,6},{6,7},{9,8},{8,9},{11,10... | collective-permute-start | bytes 3145736 | tf_op jit(solution)/shard_map/ppermute | solution.py:55
  754.3 14.6 %collective-permute-start.24 = (bf16[64,2048]{1,0:T(8,128)(2,1)S(1)}, bf16[64,2048]{1,0:T(8,128)(2,1)S(1)}, u32[]{:S(2)}, u32[]{:S(2)}) collective-permute-start(bf16[64,2048]{1,0:T(8,128)(2,1)S(1)} %slice_bitcast_fusion.26), channel_id=1, source_target_pairs={{2,0},{4,2},{6,4},{0,6},{3,1},{5,3},{7,5},{1,7},{10,8},{12,10},{14... | collective-permute-start | bytes 786440 | tf_op jit(solution)/shard_map/ppermute | solution.py:55
  757.6 15.9 %collective-permute-start.27 = (bf16[64,2048]{1,0:T(8,128)(2,1)S(1)}, bf16[64,2048]{1,0:T(8,128)(2,1)S(1)}, u32[]{:S(2)}, u32[]{:S(2)}) collective-permute-start(bf16[64,2048]{1,0:T(8,128)(2,1)S(1)} %slice_bitcast_fusion.25), channel_id=1, source_target_pairs={{16,0},{0,16},{17,1},{1,17},{18,2},{2,18},{19,3},{3,19},{20,4},{4,... | collective-permute-start | bytes 786440 | tf_op jit(solution)/shard_map/ppermute | solution.py:55
  760.1 29.4 %collective-permute-start.30 = (bf16[4,64,1024]{2,1,0:T(8,128)(2,1)S(1)}, bf16[4,64,1024]{2,1,0:T(8,128)(2,1)S(1)}, u32[]{:S(2)}, u32[]{:S(2)}) collective-permute-start(bf16[4,64,1024]{2,1,0:T(8,128)(2,1)S(1)} %fusion.22), channel_id=1, source_target_pairs={{1,0},{0,1},{3,2},{2,3},{5,4},{4,5},{7,6},{6,7},{9,8},{8,9},{11,10... | collective-permute-start | bytes 1572872 | tf_op jit(solution)/shard_map/ppermute | solution.py:55
  769.0 16.1 %collective-permute-start.25 = (bf16[64,2048]{1,0:T(8,128)(2,1)S(1)}, bf16[64,2048]{1,0:T(8,128)(2,1)S(1)}, u32[]{:S(2)}, u32[]{:S(2)}) collective-permute-start(bf16[64,2048]{1,0:T(8,128)(2,1)S(1)} %fusion.26), channel_id=1, source_target_pairs={{2,0},{4,2},{6,4},{0,6},{3,1},{5,3},{7,5},{1,7},{10,8},{12,10},{14... | collective-permute-start | bytes 786440 | tf_op jit(solution)/shard_map/ppermute | solution.py:55
  785.2 8.2 collective-permute-start.26
  789.8 23.4 %collective-permute-start.35 = (bf16[256,2048]{1,0:T(8,128)(2,1)}, bf16[256,2048]{1,0:T(8,128)(2,1)}, u32[]{:S(2)}, u32[]{:S(2)}) collective-permute-start(bf16[256,2048]{1,0:T(8,128)(2,1)} %slice_select_fusion), channel_id=1, source_target_pairs={{1,0},{0,1},{3,2},{2,3},{5,4},{4,5},{7,6},{6,7},{9,8},{8,9},{11,10... | collective-permute-start | bytes 3145736 | tf_op jit(solution)/shard_map/ppermute | solution.py:55
  794.2 16.0 %copy-start.51 = (f32[128]{0:T(128)S(1)}, f32[128]{0:T(128)}, u32[]{:S(2)}) copy-start(f32[128]{0:T(128)} %get-tuple-element.181) | copy-start | bytes 1540
  794.2 46.2 %all-to-all-start.5 = ((bf16[4,384,512]{2,1,0:T(8,128)(2,1)}), bf16[4,384,512]{2,1,0:T(8,128)(2,1)}, u32[]{:S(2)}, u32[]{:S(2)}) async-start(bf16[4,384,512]{2,1,0:T(8,128)(2,1)} %pad_maximum_fusion.3), calls=%async_computation.7 | async-start | bytes 3145728 | tf_op jit(solution)/shard_map/all_to_all | solution.py:162
  799.9 1.6 collective-permute-start.31
  802.3 5.8 collective-permute-start.32
  808.1 16.7 %collective-permute-start.33 = (f32[12,2048]{1,0:T(8,128)S(1)}, f32[12,2048]{1,0:T(8,128)S(1)}, u32[]{:S(2)}, u32[]{:S(2)}) collective-permute-start(f32[12,2048]{1,0:T(8,128)S(1)} %add.194), channel_id=1, source_target_pairs={{0,2},{2,0},{4,6},{6,4},{1,3},{3,1},{5,7},{7,5},{8,10},{10,8},{12,... | collective-permute-start | bytes 294920 | tf_op jit(solution)/shard_map/ppermute | solution.py:104
  810.2 20.7 %copy-start.12 = (f32[512,2048]{1,0:T(8,128)S(1)}, f32[512,2048]{1,0:T(8,128)}, u32[]{:S(2)}) copy-start(f32[512,2048]{1,0:T(8,128)} %copy-done.11) | copy-start | bytes 12582916
  824.8 14.3 %collective-permute-start.34 = (f32[12,2048]{1,0:T(8,128)S(1)}, f32[12,2048]{1,0:T(8,128)S(1)}, u32[]{:S(2)}, u32[]{:S(2)}) collective-permute-start(f32[12,2048]{1,0:T(8,128)S(1)} %add.195), channel_id=1, source_target_pairs={{0,4},{2,6},{4,0},{6,2},{1,5},{3,7},{5,1},{7,3},{8,12},{10,14},{12... | collective-permute-start | bytes 294920 | tf_op jit(solution)/shard_map/ppermute | solution.py:104
  (40 other events, 239.4 us)
Sparse Core Ops, SparseCore 0:
  11.2 106.3 all-gather.6
  121.1 75.4 all-gather.4
  259.0 75.8 all-gather.8
  417.2 105.4 reduce-scatter.2
  526.7 92.6 all-gather.10
  659.1 127.8 reduce-scatter.4

commit v16 on v15

--- a/solution.py
+++ b/solution.py
@@ -207,14 +207,11 @@
 
 def scatter_heads(query, kv, *others):
     half = kv.shape[2] // 2
-    rows, kv_rows = query.shape[1], kv.shape[1]
-    sent = jnp.concatenate([query, kv[:, :, :half], kv[:, :, half:]], axis=1)
-    sent = after(sent, *others)
+    query = exchange(query)
+    sent = after(kv, query, *others)
     here = exchange(sent)
-    whole = [
-        join_blocks(here[:, rows + k * kv_rows : rows + (k + 1) * kv_rows]) for k in range(2)
-    ]
-    return join_blocks(here[:, :rows]).astype(F32), jnp.concatenate(whole, axis=1).astype(F32), sent
+    whole = [join_blocks(here[:, :, :half]), join_blocks(here[:, :, half:])]
+    return join_blocks(query).astype(F32), jnp.concatenate(whole, axis=1).astype(F32), sent
 
 
 def own_places():

time: 868 us -> 879 us (1.013)
  waiting for transfers between devices: 327 us -> 338 us
    ppermute x31, waiting for transfers between devices: 223 us -> 246 us  [shift(): return lax.ppermute(value, axis, [((k + 1) % size, k) for k in range(size)])]
    ppermute x5, waiting for transfers between devices: 22.5 us -> 10.5 us  [sum_over(): lax.ppermute(value, axis, [(k, k ^ step) for k in range(size)])]
  transfers between devices with their start and end apart: 48 -> 49, of which waited for: 25 -> 25; matrix products, arithmetic and copies ran while one was open for 23% -> 24% of each run, Pallas kernels for 16% -> 15%
where the time goes in v16:
time: 879 us; the launch traced here: 869 us
  waiting for transfers between devices  338 us (38%)
  Pallas kernels  170 us (19%)
  matrix products  115 us (13%)
  starting transfers between devices  97.2 us (11%)
  other arithmetic  82.3 us (9%)
  local copies, waits for them, and re-layouts  38.5 us (4%)
  between operations  15.4 us (2%)
  blocking collectives  13.3 us (2%)
    ppermute x31, waiting for transfers between devices, shift(): return lax.ppermute(value, axis, [((k + 1) % size, k) for k in range(size)])  246 us
    pallas_call x6, Pallas kernels, call(): pl.pallas_call(kernel, grid_spec=pltpu.PrefetchScalarGridSpec(num_scalar_...  170 us
    dot_general x9, matrix products, mm(): return jnp.einsum(form, first, second, preferred_element_type=F32)  108 us
    all_gather x4, waiting for transfers between devices, meet(): return lax.all_gather(rows, GROUP, axis=0, tiled=True)  78.3 us
    ppermute x31, starting transfers between devices, shift(): return lax.ppermute(value, axis, [((k + 1) % size, k) for k in range(size)])  58 us
    convert_element_type x18, other arithmetic, add_low(): return (first.astype(F32) + second.astype(F32)).astype(BF16)  18.1 us
  transfers between devices with their start and end apart: 49, of which 25 were waited for; matrix products, arithmetic and copies ran while one was open for 24% of the time, Pallas kernels for 15%

profile of v16, /device:TPU:0, one launch (start us, length us, event | category | flops | bytes accessed | tf_op | source)
XLA Modules:
  0.0 868.9 jit_solution(9918668848423425542)
XLA Ops:
  11.2 3.0 collective-permute-start
  16.8 4.9 all-to-all-start
  21.6 55.4 %collective-permute-done.refs_3_ = bf16[704,2048]{1,0:T(8,128)(2,1)} collective-permute-done((bf16[704,2048]{1,0:T(8,128)(2,1)}, bf16[704,2048]{1,0:T(8,128)(2,1)}, u32[]{:S(2)}, u32[]{:S(2)}) %collective-permute-start) | collective-permute-done | bytes 2883616 | tf_op jit(solution)/shard_map/ppermute | solution.py:55
  78.9 11.3 %collective-permute-done.1 = bf16[4,2,64,512]{3,2,1,0:T(8,128)(2,1)S(1)} collective-permute-done((bf16[4,2,64,512]{3,2,1,0:T(8,128)(2,1)S(1)}, bf16[4,2,64,512]{3,2,1,0:T(8,128)(2,1)S(1)}, u32[]{:S(2)}, u32[]{:S(2)}) %collective-permute-start.1) | collective-permute-done | bytes 524320 | tf_op jit(solution)/shard_map/ppermute | solution.py:55
  94.9 18.9 %collective-permute-done.2 = bf16[4,256,512]{2,1,0:T(8,128)(2,1)S(1)} collective-permute-done((bf16[4,256,512]{2,1,0:T(8,128)(2,1)S(1)}, bf16[4,256,512]{2,1,0:T(8,128)(2,1)S(1)}, u32[]{:S(2)}, u32[]{:S(2)}) %collective-permute-start.2) | collective-permute-done | bytes 1048608 | tf_op jit(solution)/shard_map/ppermute | solution.py:55
  113.8 6.3 collective-permute-done.3
  121.1 3.1 pad_maximum_fusion.1.own_ref
  125.9 4.8 all-to-all-start.1
  137.9 26.2 %attend.1 = (bf16[2048,1536]{1,0:T(8,128)(2,1)}, bf16[2048,512]{1,0:T(8,128)(2,1)}, bf16[2048,1024]{1,0:T(8,128)(2,1)}) custom-call(s32[4]{0:T(128)} %pad_add_fusion.places_ref, bf16[2048,2048]{1,0:T(8,128)(2,1)} %all-gather.7.cloned.1.call-done.x_ref, f32[16,2,128]{2,1,0:T(2,128)} %copy-done.37, f32[128,128]{1,0:T(8,128)} %get-tuple-element.189.cos_ref, ...), custom_call_target="tpu_custom_call" | custom-call | flops 13421772800 | bytes 25165824 | tf_op jit(solution)/shard_map/attend/pallas_call | solution.py:459
  167.0 10.5 %rows.2 = (bf16[2,4,128,2048]{3,2,1,0:T(8,128)(2,1)}, bf16[2,4,128,2048]{3,2,1,0:T(8,128)(2,1)}) custom-call(s32[4]{0:T(128)} %pad_add_fusion.places_ref, bf16[2048,512]{1,0:T(8,128)(2,1)} %get-tuple-element.89.refs_0_, bf16[512,2048]{1,0:T(8,128)(2,1)} %bitcast.308), custom_call_target="tpu_custom_call" | custom-call | flops 4294967296 | bytes 20971520 | tf_op jit(solution)/shard_map/rows/pallas_call | solution.py:459
  177.5 2.7 copy.72
  180.4 7.4 collective-permute-done.6
  190.1 3.6 collective-permute-start.11
  196.0 9.3 %collective-permute-done.11 = bf16[2,64,2048]{2,1,0:T(8,128)(2,1)S(1)} collective-permute-done((bf16[2,64,2048]{2,1,0:T(8,128)(2,1)S(1)}, bf16[2,64,2048]{2,1,0:T(8,128)(2,1)S(1)}, u32[]{:S(2)}, u32[]{:S(2)}) %collective-permute-start.11) | collective-permute-done | bytes 524320 | tf_op jit(solution)/shard_map/ppermute | solution.py:55
  205.5 4.3 collective-permute-start.12
  209.9 11.3 %convolution_convert_fusion.1.d_units_ref = bf16[2048,704]{1,0:T(8,128)(2,1)} fusion(bf16[2048,2048]{1,0:T(8,128)(2,1)} %all-gather.5.cloned.1.call-done, bf16[704,2048]{1,0:T(8,128)(2,1)} %collective-permute-done.refs_3_), kind=kOutput, calls=%fused_computation.9 | convolution fusion | flops 5907021824 | bytes 14155776 | tf_op jit(solution)/shard_map/td,fd->tf/dot_general | solution.py:149
  221.3 3.9 collective-permute-start.13
  225.7 8.1 convolution_convert_fusion.2.d_units_ref
  233.8 7.0 collective-permute-done.8
  240.9 4.3 collective-permute-start.9
  246.1 3.1 collective-permute-done.9
  249.2 4.3 collective-permute-start.10
  253.6 3.8 collective-permute-done.10
  261.2 13.3 %all_to_all.37.info_ref = f32[16,1,128]{2,1,0:T(1,128)} all-to-all(f32[16,1,128]{2,1,0:T(1,128)S(1)} %bitcast.321), channel_id=1, replica_groups=mesh['y'=2,'c'=2,'o'=4,'i'=2] {'y','c','o'}, dimensions={0} | all-to-all | bytes 16384 | tf_op jit(solution)/shard_map/all_to_all | solution.py:131
  274.5 60.5 %all-gather.9.cloned.1.call-done.x_ref = bf16[2048,2048]{1,0:T(8,128)(2,1)} async-done(((bf16[128,2048]{1,0:T(8,128)(2,1)}), bf16[2048,2048]{1,0:T(8,128)(2,1)}) %all-gather.9.cloned.1.call-update) | async-done | bytes 8388624 | tf_op jit(solution)/shard_map/all_gather | solution.py:141
  334.9 35.5 %units.2 = (bf16[2048,1408]{1,0:T(8,128)(2,1)}, bf16[2048,704]{1,0:T(8,128)(2,1)}, f32[2048,2048]{1,0:T(8,128)}, f32[16,1,128]{2,1,0:T(1,128)}) custom-call(s32[4]{0:T(128)} %pad_add_fusion.places_ref, bf16[2048,2048]{1,0:T(8,128)(2,1)} %all-gather.9.cloned.1.call-done.x_ref, f32[16,1,128]{2,1,0:T(1,128)} %all_to_all.37.info_ref, ...), custom_call_target="tpu_custom_call" | custom-call | tf_op jit(solution)/shard_map/units/pallas_call | solution.py:459
  370.5 10.8 %collective-permute-done.15.first_ref.second_ref = bf16[1408,2048]{1,0:T(8,128)(2,1)} collective-permute-done((bf16[1408,2048]{1,0:T(8,128)(2,1)}, bf16[1408,2048]{1,0:T(8,128)(2,1)}, u32[]{:S(2)}, u32[]{:S(2)}) %collective-permute-start.15) | collective-permute-done | bytes 5767200 | tf_op jit(solution)/shard_map/ppermute | solution.py:55
  381.3 35.9 %units.3 = (bf16[2048,1408]{1,0:T(8,128)(2,1)}, bf16[2048,704]{1,0:T(8,128)(2,1)}, bf16[2048,2048]{1,0:T(8,128)(2,1)}, f32[16,1,128]{2,1,0:T(1,128)}) custom-call(s32[4]{0:T(128)} %pad_add_fusion.places_ref, bf16[2048,2048]{1,0:T(8,128)(2,1)} %all-gather.9.cloned.1.call-done.x_ref, f32[16,1,128]{2,1,0:T(1,128)} %all_to_all.37.info_ref, ...), custom_call_target="tpu_custom_call" | custom-call | tf_op jit(solution)/shard_map/units/pallas_call | solution.py:459
  417.2 10.7 %convolution_convert_fusion.3 = bf16[704,2048]{1,0:T(8,128)(2,1)} fusion(bf16[2048,704]{1,0:T(8,128)(2,1)} %get-tuple-element.104.refs_1_, bf16[2048,2048]{1,0:T(8,128)(2,1)} %all-gather.5.cloned.1.call-done), kind=kOutput, calls=%fused_computation.11 | convolution fusion | flops 5907021824 | bytes 14155776 | tf_op jit(solution)/shard_map/tf,td->fd/dot_general | solution.py:149
  427.9 21.8 %rows.3 = (bf16[2,4,128,2048]{3,2,1,0:T(8,128)(2,1)}, bf16[2,4,128,2048]{3,2,1,0:T(8,128)(2,1)}) custom-call(s32[4]{0:T(128)} %pad_add_fusion.places_ref, bf16[2048,704]{1,0:T(8,128)(2,1)} %get-tuple-element.103.refs_0_, bf16[2048,704]{1,0:T(8,128)(2,1)} %get-tuple-element.104.refs_1_, bf16[704,2048]{1,0:T(8,128)(2,1)} %bitcast.335, ...), custom_call_target="tpu_custom_call" | custom-call | flops 11811160064 | bytes 28311552 | tf_op jit(solution)/shard_map/rows/pallas_call | solution.py:459
  449.7 4.9 copy.75
  456.2 6.2 all-to-all-start.3
  462.5 18.0 %convolution_convert_fusion = bf16[1408,2048]{1,0:T(8,128)(2,1)} fusion(bf16[2048,1408]{1,0:T(8,128)(2,1)} %get-tuple-element.108, bf16[2048,2048]{1,0:T(8,128)(2,1)} %all-gather.9.cloned.1.call-done.x_ref), kind=kOutput, calls=%fused_computation.3 | convolution fusion | flops 11814043648 | bytes 19922944 | tf_op jit(solution)/shard_map/tf,td->fd/dot_general | solution.py:149
  480.6 7.9 add_convert_fusion
  488.5 31.3 %collective-permute-done.20 = bf16[704,2048]{1,0:T(8,128)(2,1)} collective-permute-done((bf16[704,2048]{1,0:T(8,128)(2,1)}, bf16[704,2048]{1,0:T(8,128)(2,1)}, u32[]{:S(2)}, u32[]{:S(2)}) %collective-permute-start.20) | collective-permute-done | bytes 2883616 | tf_op jit(solution)/shard_map/ppermute | solution.py:55
  519.8 2.9 reduce-scatter.3.cloned.1.call-done
  529.9 21.3 %collective-permute-done.17 = bf16[2,64,2048]{2,1,0:T(8,128)(2,1)S(1)} collective-permute-done((bf16[2,64,2048]{2,1,0:T(8,128)(2,1)S(1)}, bf16[2,64,2048]{2,1,0:T(8,128)(2,1)S(1)}, u32[]{:S(2)}, u32[]{:S(2)}) %collective-permute-start.17) | collective-permute-done | bytes 524320 | tf_op jit(solution)/shard_map/ppermute | solution.py:55
  554.9 14.7 %collective-permute-done.18 = bf16[2,64,2048]{2,1,0:T(8,128)(2,1)S(1)} collective-permute-done((bf16[2,64,2048]{2,1,0:T(8,128)(2,1)S(1)}, bf16[2,64,2048]{2,1,0:T(8,128)(2,1)S(1)}, u32[]{:S(2)}, u32[]{:S(2)}) %collective-permute-start.18) | collective-permute-done | bytes 524320 | tf_op jit(solution)/shard_map/ppermute | solution.py:55
  570.7 4.1 collective-permute-start.19
  574.9 19.6 %fusion.60 = f32[1408,2048]{1,0:T(8,128)} fusion(bf16[2048,1408]{1,0:T(8,128)(2,1)} %get-tuple-element.144, bf16[2048,2048]{1,0:T(8,128)(2,1)} %all-gather.9.cloned.1.call-done.x_ref), kind=kOutput, calls=%fused_computation.196 | convolution fusion | flops 11811160064 | bytes 25690112 | tf_op jit(solution)/shard_map/tf,td->fd/dot_general | solution.py:149
  596.3 4.4 collective-permute-done.19
  601.6 17.8 %all-gather.11.cloned.1.call-done.mid_ref = bf16[2048,2048]{1,0:T(8,128)(2,1)} async-done(((bf16[128,2048]{1,0:T(8,128)(2,1)}), bf16[2048,2048]{1,0:T(8,128)(2,1)}) %all-gather.11.cloned.1.call-update) | async-done | bytes 8388624 | tf_op jit(solution)/shard_map/all_gather | solution.py:141
  619.4 39.7 %attend_back.1 = (bf16[2048,512]{1,0:T(8,128)(2,1)}, bf16[2048,1024]{1,0:T(8,128)(2,1)}, bf16[2048,2048]{1,0:T(8,128)(2,1)}, f32[16,1,128]{2,1,0:T(1,128)}, f32[1,2048]{1,0:T(1,128)}) custom-call(s32[4]{0:T(128)} %pad_add_fusion.places_ref, bf16[2048,2048]{1,0:T(8,128)(2,1)} %all-gather.11.cloned.1.call-done.mid_ref, f32[16,2,128]{2,1,0:T(2,128)} %copy-done.37, ...), custom_call_target="tpu_custom_call" | custom-call | flops 18522046464 | bytes 46137344 | tf_op jit(solution)/shard_map/attend_back/pallas_call | solution.py:459
  659.1 8.6 all-to-all-start.4
  672.1 13.8 %fusion.55 = f32[2048,1024]{1,0:T(8,128)S(1)} fusion(bf16[2048,2048]{1,0:T(8,128)(2,1)} %all-gather.7.cloned.1.call-done.x_ref, bf16[2048,1024]{1,0:T(8,128)(2,1)} %get-tuple-element.117), kind=kOutput, calls=%fused_computation.191 | convolution fusion | flops 8589934592 | bytes 20971520 | tf_op jit(solution)/shard_map/td,tf->df/dot_general | solution.py:149
  685.9 3.3 copy-done.5
  694.2 11.8 %add_bitcast_fusion = f32[1,704,2048]{2,1,0:T(8,128)} fusion(bf16[704,2048]{1,0:T(8,128)(2,1)} %collective-permute-done.20, bf16[2048,704]{1,0:T(8,128)(2,1)} %get-tuple-element.103.refs_0_, bf16[2048,2048]{1,0:T(8,128)(2,1)} %all-gather.5.cloned.1.call-done), kind=kOutput, calls=%fused_computation.4 | convolution fusion | flops 5908463616 | bytes 19922944 | tf_op jit(solution)/shard_map/tf,td->fd/dot_general | solution.py:149
  706.7 2.6 fusion.1
  709.3 5.7 bitcast_add_fusion
  718.2 7.2 fusion.58
  729.7 13.5 %convert_add_fusion = f32[1408,2048]{1,0:T(8,128)} fusion(f32[1408,2048]{1,0:T(8,128)} %fusion.60, bf16[1408,2048]{1,0:T(8,128)(2,1)} %collective-permute-done.36), kind=kLoop, calls=%fused_computation | loop fusion | flops 5767168 | bytes 28835840 | tf_op jit(solution)/shard_map/add | solution.py:759
  743.2 7.7 fusion.59
  755.8 2.8 fusion.3
  758.6 4.4 all-to-all-start.5
  764.0 3.9 collective-permute-start.24
  773.4 24.3 %collective-permute-done.24 = bf16[64,2048]{1,0:T(8,128)(2,1)S(1)} collective-permute-done((bf16[64,2048]{1,0:T(8,128)(2,1)S(1)}, bf16[64,2048]{1,0:T(8,128)(2,1)S(1)}, u32[]{:S(2)}, u32[]{:S(2)}) %collective-permute-start.24) | collective-permute-done | bytes 262176 | tf_op jit(solution)/shard_map/ppermute | solution.py:55
  797.8 4.3 collective-permute-start.25
  802.2 11.4 %collective-permute-done.25 = bf16[64,2048]{1,0:T(8,128)(2,1)S(1)} collective-permute-done((bf16[64,2048]{1,0:T(8,128)(2,1)S(1)}, bf16[64,2048]{1,0:T(8,128)(2,1)S(1)}, u32[]{:S(2)}, u32[]{:S(2)}) %collective-permute-start.25) | collective-permute-done | bytes 262176 | tf_op jit(solution)/shard_map/ppermute | solution.py:55
  816.2 5.1 collective-permute-done.26
  825.0 4.1 all-to-all-start.6
  833.1 4.4 collective-permute-done.32
  839.4 3.0 fusion.12
  845.4 3.0 add_bitcast_fusion.1
  848.5 4.1 collective-permute-done.34
  (291 shorter events, 105.4 us)
Async XLA Ops:
  7.2 252.3 %copy-start = (f32[2048,4]{0,1:T(4,128)S(1)}, f32[2048,4]{0,1:T(4,128)}, u32[]{:S(2)}) copy-start(f32[2048,4]{0,1:T(4,128)} %param.23) | copy-start | bytes 98308
  7.2 130.1 %all-gather.7.cloned.1.call-start = ((), (), s32[]{:S(2)}) async-start(), calls=%async_computation.10 | async-start | bytes 8912896 | tf_op jit(solution)/shard_map/all_gather | solution.py:141
  11.2 65.8 %collective-permute-start = (bf16[704,2048]{1,0:T(8,128)(2,1)}, bf16[704,2048]{1,0:T(8,128)(2,1)}, u32[]{:S(2)}, u32[]{:S(2)}) collective-permute-start(bf16[704,2048]{1,0:T(8,128)(2,1)} %bitcast.334), channel_id=1, source_target_pairs={{1,0},{0,1},{3,2},{2,3},{5,4},{4,5},{7,6},{6,7},{9,8},{8,9},{11,10... | collective-permute-start | bytes 8650760 | tf_op jit(solution)/shard_map/ppermute | solution.py:55
  16.8 60.3 %all-to-all-start = ((bf16[4,384,512]{2,1,0:T(8,128)(2,1)}), bf16[4,384,512]{2,1,0:T(8,128)(2,1)S(1)}, u32[]{:S(2)}, u32[]{:S(2)}) async-start(bf16[4,384,512]{2,1,0:T(8,128)(2,1)} %maximum_maximum_fusion), calls=%async_computation | async-start | bytes 3145728 | tf_op jit(solution)/shard_map/all_to_all | solution.py:162
  21.6 71.8 %copy-start.19 = (f32[128,2048]{1,0:T(8,128)S(1)}, f32[128,2048]{1,0:T(8,128)}, u32[]{:S(2)}) copy-start(f32[128,2048]{1,0:T(8,128)} %param.31) | copy-start | bytes 3145732
  21.6 188.2 %all-gather.5.cloned.1.call-start = ((), (), s32[]{:S(2)}) async-start(), calls=%async_computation.9 | async-start | bytes 8912896 | tf_op jit(solution)/shard_map/all_gather | solution.py:141
  77.0 13.2 %collective-permute-start.1 = (bf16[4,2,64,512]{3,2,1,0:T(8,128)(2,1)S(1)}, bf16[4,2,64,512]{3,2,1,0:T(8,128)(2,1)S(1)}, u32[]{:S(2)}, u32[]{:S(2)}) collective-permute-start(bf16[4,2,64,512]{3,2,1,0:T(8,128)(2,1)S(1)} %bitcast.310), channel_id=1, source_target_pairs={{1,0},{0,1},{3,2},{2,3},{5,4},{4,5},{7,6},{6,7},{9,8},{8,9},{11,10... | collective-permute-start | bytes 1572872 | tf_op jit(solution)/shard_map/ppermute | solution.py:55
  90.2 23.5 %collective-permute-start.2 = (bf16[4,256,512]{2,1,0:T(8,128)(2,1)S(1)}, bf16[4,256,512]{2,1,0:T(8,128)(2,1)S(1)}, u32[]{:S(2)}, u32[]{:S(2)}) collective-permute-start(bf16[4,256,512]{2,1,0:T(8,128)(2,1)S(1)} %slice.254), channel_id=1, source_target_pairs={{1,0},{0,1},{3,2},{2,3},{5,4},{4,5},{7,6},{6,7},{9,8},{8,9},{11,10... | collective-permute-start | bytes 3145736 | tf_op jit(solution)/shard_map/ppermute | solution.py:55
  91.7 22.0 %copy-start.22 = (bf16[2,4,2,64,512]{4,3,2,1,0:T(8,128)(2,1)}, bf16[2,4,2,64,512]{4,3,2,1,0:T(8,128)(2,1)S(1)}, u32[]{:S(2)}) copy-start(bf16[2,4,2,64,512]{4,3,2,1,0:T(8,128)(2,1)S(1)} %pad_maximum_fusion.3) | copy-start | bytes 3145732
  91.8 32.4 %copy-start.14 = (bf16[128,2048]{1,0:T(8,128)(2,1)S(1)}, bf16[128,2048]{1,0:T(8,128)(2,1)}, u32[]{:S(2)}) copy-start(bf16[128,2048]{1,0:T(8,128)(2,1)} %fusion.6) | copy-start | bytes 1572868
  91.8 32.4 %copy-start.31 = (f32[2048,4]{0,1:T(4,128)S(1)}, f32[2048,4]{0,1:T(4,128)}, u32[]{:S(2)}) copy-start(f32[2048,4]{0,1:T(4,128)} %param.22) | copy-start | bytes 98308
  91.8 32.9 %copy-start.39 = (s32[128,2]{0,1:T(2,128)S(1)}, s32[128,2]{0,1:T(2,128)}, u32[]{:S(2)}) copy-start(s32[128,2]{0,1:T(2,128)} %param.18) | copy-start | bytes 3076
  91.8 33.5 %copy-start.54 = (s32[1,128]{1,0:T(1,128)S(1)}, s32[1,128]{1,0:T(1,128)}, u32[]{:S(2)}) copy-start(s32[1,128]{1,0:T(1,128)} %param.17) | copy-start | bytes 1540
  91.8 28.3 %collective-permute-start.3 = (bf16[2,4,2,64,512]{4,3,2,1,0:T(8,128)(2,1)S(1)}, bf16[2,4,2,64,512]{4,3,2,1,0:T(8,128)(2,1)S(1)}, u32[]{:S(2)}, u32[]{:S(2)}) collective-permute-start(bf16[2,4,2,64,512]{4,3,2,1,0:T(8,128)(2,1)S(1)} %pad_maximum_fusion.3), channel_id=1, source_target_pairs={{16,0},{0,16},{17,1},{1,17},{18,2},{2,18},{19,3},{3,19},{20,4},{4,... | collective-permute-start | bytes 3145736 | tf_op jit(solution)/shard_map/ppermute | solution.py:55
  94.9 39.0 %copy-start.21 = (bf16[4,256,512]{2,1,0:T(8,128)(2,1)S(1)}, bf16[4,256,512]{2,1,0:T(8,128)(2,1)}, u32[]{:S(2)}) copy-start(bf16[4,256,512]{2,1,0:T(8,128)(2,1)} %copy-done.20) | copy-start | bytes 3145732
  124.1 13.2 %collective-permute-start.4 = (bf16[2,2,4,2,64,512]{5,4,3,2,1,0:T(8,128)(2,1)}, bf16[2,2,4,2,64,512]{5,4,3,2,1,0:T(8,128)(2,1)}, u32[]{:S(2)}, u32[]{:S(2)}) collective-permute-start(bf16[2,2,4,2,64,512]{5,4,3,2,1,0:T(8,128)(2,1)} %pad_maximum_fusion.1.own_ref), channel_id=1, source_target_pairs={{8,0},{0,8},{9,1},{1,9},{10,2},{2,10},{11,3},{3,11},{12,4},{4,12},... | collective-permute-start | bytes 6291464 | tf_op jit(solution)/shard_map/ppermute | solution.py:55
  125.9 11.4 %all-to-all-start.1 = ((f32[16,2,128]{2,1,0:T(2,128)}), f32[16,2,128]{2,1,0:T(2,128)S(1)}, u32[]{:S(2)}, u32[]{:S(2)}) async-start(f32[16,2,128]{2,1,0:T(2,128)} %pad_maximum_fusion.7), calls=%async_computation.1 | async-start | bytes 32768 | tf_op jit(solution)/shard_map/all_to_all | solution.py:131
  130.8 204.2 %all-gather.9.cloned.1.call-start = ((), (), s32[]{:S(2)}) async-start(), calls=%async_computation.11 | async-start | bytes 8912896 | tf_op jit(solution)/shard_map/all_gather | solution.py:141
  132.4 31.7 %collective-permute-start.5 = (bf16[256,2048]{1,0:T(8,128)(2,1)}, bf16[256,2048]{1,0:T(8,128)(2,1)}, u32[]{:S(2)}, u32[]{:S(2)}) collective-permute-start(bf16[256,2048]{1,0:T(8,128)(2,1)} %bitcast.312), channel_id=1, source_target_pairs={{1,0},{0,1},{3,2},{2,3},{5,4},{4,5},{7,6},{6,7},{9,8},{8,9},{11,10... | collective-permute-start | bytes 3145736 | tf_op jit(solution)/shard_map/ppermute | solution.py:55
  137.9 26.2 %copy-start.25 = (bf16[1,256,2048]{2,1,0:T(8,128)(2,1)S(1)}, bf16[1,256,2048]{2,1,0:T(8,128)(2,1)}, u32[]{:S(2)}) copy-start(bf16[1,256,2048]{2,1,0:T(8,128)(2,1)} %param.26) | copy-start | bytes 3145732
  180.2 7.6 collective-permute-start.6
  190.1 15.3 %collective-permute-start.11 = (bf16[2,64,2048]{2,1,0:T(8,128)(2,1)S(1)}, bf16[2,64,2048]{2,1,0:T(8,128)(2,1)S(1)}, u32[]{:S(2)}, u32[]{:S(2)}) collective-permute-start(bf16[2,64,2048]{2,1,0:T(8,128)(2,1)S(1)} %slice_bitcast_fusion.14), channel_id=1, source_target_pairs={{2,0},{4,2},{6,4},{0,6},{3,1},{5,3},{7,5},{1,7},{10,8},{12,10},{14... | collective-permute-start | bytes 1572872 | tf_op jit(solution)/shard_map/ppermute | solution.py:55
  194.7 30.5 %collective-permute-start.7 = (bf16[4,64,2048]{2,1,0:T(8,128)(2,1)}, bf16[4,64,2048]{2,1,0:T(8,128)(2,1)S(1)}, u32[]{:S(2)}, u32[]{:S(2)}) collective-permute-start(bf16[4,64,2048]{2,1,0:T(8,128)(2,1)} %slice_bitcast_fusion.6), channel_id=1, source_target_pairs={{16,0},{0,16},{17,1},{1,17},{18,2},{2,18},{19,3},{3,19},{20,4},{4,... | collective-permute-start | bytes 3145736 | tf_op jit(solution)/shard_map/ppermute | solution.py:55
  205.5 15.6 %collective-permute-start.12 = (bf16[2,64,2048]{2,1,0:T(8,128)(2,1)S(1)}, bf16[2,64,2048]{2,1,0:T(8,128)(2,1)S(1)}, u32[]{:S(2)}, u32[]{:S(2)}) collective-permute-start(bf16[2,64,2048]{2,1,0:T(8,128)(2,1)S(1)} %fusion.20), channel_id=1, source_target_pairs={{2,0},{4,2},{6,4},{0,6},{3,1},{5,3},{7,5},{1,7},{10,8},{12,10},{14... | collective-permute-start | bytes 1572872 | tf_op jit(solution)/shard_map/ppermute | solution.py:55
  221.3 24.0 %collective-permute-start.13 = (bf16[2,64,2048]{2,1,0:T(8,128)(2,1)S(1)}, bf16[2,64,2048]{2,1,0:T(8,128)(2,1)S(1)}, u32[]{:S(2)}, u32[]{:S(2)}) collective-permute-start(bf16[2,64,2048]{2,1,0:T(8,128)(2,1)S(1)} %fusion.19), channel_id=1, source_target_pairs={{2,0},{4,2},{6,4},{0,6},{3,1},{5,3},{7,5},{1,7},{10,8},{12,10},{14... | collective-permute-start | bytes 1572872 | tf_op jit(solution)/shard_map/ppermute | solution.py:55
  225.6 15.2 %collective-permute-start.8 = (bf16[64,2048]{1,0:T(8,128)(2,1)S(1)}, bf16[64,2048]{1,0:T(8,128)(2,1)S(1)}, u32[]{:S(2)}, u32[]{:S(2)}) collective-permute-start(bf16[64,2048]{1,0:T(8,128)(2,1)S(1)} %slice_bitcast_fusion.20), channel_id=1, source_target_pairs={{2,0},{4,2},{6,4},{0,6},{3,1},{5,3},{7,5},{1,7},{10,8},{12,10},{14... | collective-permute-start | bytes 786440 | tf_op jit(solution)/shard_map/ppermute | solution.py:55
  233.8 23.8 %copy-start.2 = (bf16[128,2048]{1,0:T(8,128)(2,1)S(1)}, bf16[128,2048]{1,0:T(8,128)(2,1)}, u32[]{:S(2)}) copy-start(bf16[128,2048]{1,0:T(8,128)(2,1)} %param.16) | copy-start | bytes 1572868
  233.8 23.8 %copy-start.29 = (f32[2048]{0:T(1024)S(1)}, f32[2048]{0:T(1024)}, u32[]{:S(2)}) copy-start(f32[2048]{0:T(1024)} %param.27) | copy-start | bytes 24580
  240.9 8.2 collective-permute-start.9
  245.4 8.1 collective-permute-start.14
  249.2 8.2 collective-permute-start.10
  259.0 263.8 %reduce-scatter.3.cloned.1.call-start = ((), (), s32[]{:S(2)}) async-start(), calls=%async_computation.12 | async-start | bytes 8912896 | tf_op jit(solution)/shard_map/reduce_scatter | solution.py:145
  259.0 122.3 %collective-permute-start.15 = (bf16[1408,2048]{1,0:T(8,128)(2,1)}, bf16[1408,2048]{1,0:T(8,128)(2,1)}, u32[]{:S(2)}, u32[]{:S(2)}) collective-permute-start(bf16[1408,2048]{1,0:T(8,128)(2,1)} %bitcast.296), channel_id=1, source_target_pairs={{1,0},{0,1},{3,2},{2,3},{5,4},{4,5},{7,6},{6,7},{9,8},{8,9},{11,10... | collective-permute-start | bytes 17301512 | tf_op jit(solution)/shard_map/ppermute | solution.py:55
  454.6 26.0 %collective-permute-start.16 = (bf16[2,4,128,2048]{3,2,0,1:T(8,128)(2,1)}, bf16[2,4,128,2048]{3,2,0,1:T(8,128)(2,1)}, u32[]{:S(2)}, u32[]{:S(2)}) collective-permute-start(bf16[2,4,128,2048]{3,2,0,1:T(8,128)(2,1)} %copy.75), channel_id=1, source_target_pairs={{8,0},{0,8},{9,1},{1,9},{10,2},{2,10},{11,3},{3,11},{12,4},{4,12},... | collective-permute-start | bytes 12582920 | tf_op jit(solution)/shard_map/ppermute | solution.py:55
  454.6 65.2 %collective-permute-start.20 = (bf16[704,2048]{1,0:T(8,128)(2,1)}, bf16[704,2048]{1,0:T(8,128)(2,1)}, u32[]{:S(2)}, u32[]{:S(2)}) collective-permute-start(bf16[704,2048]{1,0:T(8,128)(2,1)} %convolution_convert_fusion.3), channel_id=1, source_target_pairs={{1,0},{0,1},{3,2},{2,3},{5,4},{4,5},{7,6},{6,7},{9,8},{8,9},{11,10... | collective-permute-start | bytes 8650760 | tf_op jit(solution)/shard_map/ppermute | solution.py:55
  456.2 24.3 %all-to-all-start.3 = ((f32[16,1,128]{2,1,0:T(1,128)}), f32[16,1,128]{2,1,0:T(1,128)S(1)}, u32[]{:S(2)}, u32[]{:S(2)}) async-start(f32[16,1,128]{2,1,0:T(1,128)} %add.174), calls=%async_computation.4 | async-start | bytes 16384 | tf_op jit(solution)/shard_map/all_to_all | solution.py:135
  462.4 157.0 %all-gather.11.cloned.1.call-start = ((), (), s32[]{:S(2)}) async-start(), calls=%async_computation.13 | async-start | bytes 8912896 | tf_op jit(solution)/shard_map/all_gather | solution.py:141
  526.6 298.4 %reduce-scatter.5.cloned.1.call-start = ((), (), s32[]{:S(2)}) async-start(), calls=%async_computation.14 | async-start | bytes 8912896 | tf_op jit(solution)/shard_map/reduce_scatter | solution.py:145
  527.7 23.5 %collective-permute-start.17 = (bf16[2,64,2048]{2,1,0:T(8,128)(2,1)S(1)}, bf16[2,64,2048]{2,1,0:T(8,128)(2,1)S(1)}, u32[]{:S(2)}, u32[]{:S(2)}) collective-permute-start(bf16[2,64,2048]{2,1,0:T(8,128)(2,1)S(1)} %slice_bitcast_fusion.10), channel_id=1, source_target_pairs={{2,0},{4,2},{6,4},{0,6},{3,1},{5,3},{7,5},{1,7},{10,8},{12,10},{14... | collective-permute-start | bytes 1572872 | tf_op jit(solution)/shard_map/ppermute | solution.py:55
  552.3 17.2 %collective-permute-start.18 = (bf16[2,64,2048]{2,1,0:T(8,128)(2,1)S(1)}, bf16[2,64,2048]{2,1,0:T(8,128)(2,1)S(1)}, u32[]{:S(2)}, u32[]{:S(2)}) collective-permute-start(bf16[2,64,2048]{2,1,0:T(8,128)(2,1)S(1)} %fusion.17), channel_id=1, source_target_pairs={{2,0},{4,2},{6,4},{0,6},{3,1},{5,3},{7,5},{1,7},{10,8},{12,10},{14... | collective-permute-start | bytes 1572872 | tf_op jit(solution)/shard_map/ppermute | solution.py:55
  553.5 176.2 %collective-permute-start.36 = (bf16[1408,2048]{1,0:T(8,128)(2,1)}, bf16[1408,2048]{1,0:T(8,128)(2,1)}, u32[]{:S(2)}, u32[]{:S(2)}) collective-permute-start(bf16[1408,2048]{1,0:T(8,128)(2,1)} %convolution_convert_fusion), channel_id=1, source_target_pairs={{1,0},{0,1},{3,2},{2,3},{5,4},{4,5},{7,6},{6,7},{9,8},{8,9},{11,10... | collective-permute-start | bytes 17301512 | tf_op jit(solution)/shard_map/ppermute | solution.py:55
  570.7 29.9 %collective-permute-start.19 = (bf16[2,64,2048]{2,1,0:T(8,128)(2,1)S(1)}, bf16[2,64,2048]{2,1,0:T(8,128)(2,1)S(1)}, u32[]{:S(2)}, u32[]{:S(2)}) collective-permute-start(bf16[2,64,2048]{2,1,0:T(8,128)(2,1)S(1)} %fusion.16), channel_id=1, source_target_pairs={{2,0},{4,2},{6,4},{0,6},{3,1},{5,3},{7,5},{1,7},{10,8},{12,10},{14... | collective-permute-start | bytes 1572872 | tf_op jit(solution)/shard_map/ppermute | solution.py:55
  574.9 19.6 %copy-start.16 = (bf16[128,2048]{1,0:T(8,128)(2,1)S(1)}, bf16[128,2048]{1,0:T(8,128)(2,1)}, u32[]{:S(2)}) copy-start(bf16[128,2048]{1,0:T(8,128)(2,1)} %multiply_convert_fusion) | copy-start | bytes 1572868
  574.9 20.0 %copy-start.8 = (bf16[2,4,128,2048]{3,2,0,1:T(8,128)(2,1)S(1)}, bf16[2,4,128,2048]{3,2,0,1:T(8,128)(2,1)}, u32[]{:S(2)}) copy-start(bf16[2,4,128,2048]{3,2,0,1:T(8,128)(2,1)} %add_convert_fusion) | copy-start | bytes 12582916
  659.1 31.8 %all-to-all-start.4 = ((f32[16,1,128]{2,1,0:T(1,128)}), f32[16,1,128]{2,1,0:T(1,128)S(1)}, u32[]{:S(2)}, u32[]{:S(2)}) async-start(f32[16,1,128]{2,1,0:T(1,128)} %get-tuple-element.124), calls=%async_computation.5 | async-start | bytes 16384 | tf_op jit(solution)/shard_map/all_to_all | solution.py:135
  670.1 36.6 %collective-permute-start.23 = (bf16[4,64,2048]{2,1,0:T(8,128)(2,1)}, bf16[4,64,2048]{2,1,0:T(8,128)(2,1)}, u32[]{:S(2)}, u32[]{:S(2)}) collective-permute-start(bf16[4,64,2048]{2,1,0:T(8,128)(2,1)} %slice_bitcast_fusion.4), channel_id=1, source_target_pairs={{16,0},{0,16},{17,1},{1,17},{18,2},{2,18},{19,3},{3,19},{20,4},{4,... | collective-permute-start | bytes 3145736 | tf_op jit(solution)/shard_map/ppermute | solution.py:55
  690.9 18.4 %collective-permute-start.21 = (bf16[2,512,1024]{2,1,0:T(8,128)(2,1)}, bf16[2,512,1024]{2,1,0:T(8,128)(2,1)}, u32[]{:S(2)}, u32[]{:S(2)}) collective-permute-start(bf16[2,512,1024]{2,1,0:T(8,128)(2,1)} %fusion), channel_id=1, source_target_pairs={{0,8},{8,0},{1,9},{9,1},{2,10},{10,2},{3,11},{11,3},{4,12},{12,4},... | collective-permute-start | bytes 6291464 | tf_op jit(solution)/shard_map/ppermute | solution.py:197
  692.7 13.3 %collective-permute-start.28 = (f32[12,2048]{1,0:T(8,128)S(1)}, f32[12,2048]{1,0:T(8,128)S(1)}, u32[]{:S(2)}, u32[]{:S(2)}) collective-permute-start(f32[12,2048]{1,0:T(8,128)S(1)} %concatenate.40), channel_id=1, source_target_pairs={{0,1},{1,0},{2,3},{3,2},{4,5},{5,4},{6,7},{7,6},{8,9},{9,8},{10,11... | collective-permute-start | bytes 294920 | tf_op jit(solution)/shard_map/ppermute | solution.py:104
  716.2 46.8 %collective-permute-start.22 = (bf16[4,2,64,1024]{3,2,1,0:T(8,128)(2,1)}, bf16[4,2,64,1024]{3,2,1,0:T(8,128)(2,1)}, u32[]{:S(2)}, u32[]{:S(2)}) collective-permute-start(bf16[4,2,64,1024]{3,2,1,0:T(8,128)(2,1)} %bitcast.60), channel_id=1, source_target_pairs={{16,0},{0,16},{17,1},{1,17},{18,2},{2,18},{19,3},{3,19},{20,4},{4,... | collective-permute-start | bytes 3145736 | tf_op jit(solution)/shard_map/ppermute | solution.py:55
  728.5 26.7 %collective-permute-start.29 = (bf16[4,256,512]{2,1,0:T(8,128)(2,1)}, bf16[4,256,512]{2,1,0:T(8,128)(2,1)}, u32[]{:S(2)}, u32[]{:S(2)}) collective-permute-start(bf16[4,256,512]{2,1,0:T(8,128)(2,1)} %select_bitcast_fusion), channel_id=1, source_target_pairs={{1,0},{0,1},{3,2},{2,3},{5,4},{4,5},{7,6},{6,7},{9,8},{8,9},{11,10... | collective-permute-start | bytes 3145736 | tf_op jit(solution)/shard_map/ppermute | solution.py:55
  758.6 63.6 %all-to-all-start.5 = ((bf16[4,256,512]{2,1,0:T(8,128)(2,1)}), bf16[4,256,512]{2,1,0:T(8,128)(2,1)}, u32[]{:S(2)}, u32[]{:S(2)}) async-start(bf16[4,256,512]{2,1,0:T(8,128)(2,1)} %fusion.3), calls=%async_computation.7 | async-start | bytes 2097152 | tf_op jit(solution)/shard_map/all_to_all | solution.py:162
  764.0 33.8 %collective-permute-start.24 = (bf16[64,2048]{1,0:T(8,128)(2,1)S(1)}, bf16[64,2048]{1,0:T(8,128)(2,1)S(1)}, u32[]{:S(2)}, u32[]{:S(2)}) collective-permute-start(bf16[64,2048]{1,0:T(8,128)(2,1)S(1)} %slice_bitcast_fusion.26), channel_id=1, source_target_pairs={{2,0},{4,2},{6,4},{0,6},{3,1},{5,3},{7,5},{1,7},{10,8},{12,10},{14... | collective-permute-start | bytes 786440 | tf_op jit(solution)/shard_map/ppermute | solution.py:55
  768.8 33.3 %collective-permute-start.27 = (bf16[64,2048]{1,0:T(8,128)(2,1)S(1)}, bf16[64,2048]{1,0:T(8,128)(2,1)S(1)}, u32[]{:S(2)}, u32[]{:S(2)}) collective-permute-start(bf16[64,2048]{1,0:T(8,128)(2,1)S(1)} %slice_bitcast_fusion.25), channel_id=1, source_target_pairs={{16,0},{0,16},{17,1},{1,17},{18,2},{2,18},{19,3},{3,19},{20,4},{4,... | collective-permute-start | bytes 786440 | tf_op jit(solution)/shard_map/ppermute | solution.py:55
  769.5 28.2 %copy-start.18 = (bf16[4,64,2048]{2,1,0:T(8,128)(2,1)S(1)}, bf16[4,64,2048]{2,1,0:T(8,128)(2,1)}, u32[]{:S(2)}) copy-start(bf16[4,64,2048]{2,1,0:T(8,128)(2,1)} %fusion.1) | copy-start | bytes 3145732
  769.5 32.6 %copy-start.23 = (bf16[2,64,2048]{2,1,0:T(8,128)(2,1)S(1)}, bf16[2,64,2048]{2,1,0:T(8,128)(2,1)}, u32[]{:S(2)}) copy-start(bf16[2,64,2048]{2,1,0:T(8,128)(2,1)} %fusion.15) | copy-start | bytes 1572868
  771.9 41.8 %collective-permute-start.30 = (bf16[4,64,1024]{2,1,0:T(8,128)(2,1)S(1)}, bf16[4,64,1024]{2,1,0:T(8,128)(2,1)S(1)}, u32[]{:S(2)}, u32[]{:S(2)}) collective-permute-start(bf16[4,64,1024]{2,1,0:T(8,128)(2,1)S(1)} %fusion.22), channel_id=1, source_target_pairs={{1,0},{0,1},{3,2},{2,3},{5,4},{4,5},{7,6},{6,7},{9,8},{8,9},{11,10... | collective-permute-start | bytes 1572872 | tf_op jit(solution)/shard_map/ppermute | solution.py:55
  797.8 15.8 %collective-permute-start.25 = (bf16[64,2048]{1,0:T(8,128)(2,1)S(1)}, bf16[64,2048]{1,0:T(8,128)(2,1)S(1)}, u32[]{:S(2)}, u32[]{:S(2)}) collective-permute-start(bf16[64,2048]{1,0:T(8,128)(2,1)S(1)} %fusion.26), channel_id=1, source_target_pairs={{2,0},{4,2},{6,4},{0,6},{3,1},{5,3},{7,5},{1,7},{10,8},{12,10},{14... | collective-permute-start | bytes 786440 | tf_op jit(solution)/shard_map/ppermute | solution.py:55
  813.7 7.7 collective-permute-start.26
  814.8 27.7 %collective-permute-start.35 = (bf16[256,2048]{1,0:T(8,128)(2,1)}, bf16[256,2048]{1,0:T(8,128)(2,1)}, u32[]{:S(2)}, u32[]{:S(2)}) collective-permute-start(bf16[256,2048]{1,0:T(8,128)(2,1)} %slice_select_fusion), channel_id=1, source_target_pairs={{1,0},{0,1},{3,2},{2,3},{5,4},{4,5},{7,6},{6,7},{9,8},{8,9},{11,10... | collective-permute-start | bytes 3145736 | tf_op jit(solution)/shard_map/ppermute | solution.py:55
  825.0 28.8 %all-to-all-start.6 = ((bf16[4,64,1024]{2,1,0:T(8,128)(2,1)}), bf16[4,64,1024]{2,1,0:T(8,128)(2,1)}, u32[]{:S(2)}, u32[]{:S(2)}) async-start(bf16[4,64,1024]{2,1,0:T(8,128)(2,1)} %fusion.21), calls=%async_computation.8 | async-start | bytes 1048576 | tf_op jit(solution)/shard_map/all_to_all | solution.py:162
  829.1 1.6 collective-permute-start.31
  831.7 5.8 collective-permute-start.32
  837.5 6.9 collective-permute-start.33
  844.4 8.1 collective-permute-start.34
  (41 other events, 285.8 us)
Sparse Core Ops, SparseCore 0:
  11.3 106.3 all-gather.6
  121.2 75.4 all-gather.4
  259.1 75.8 all-gather.8
  417.3 105.3 reduce-scatter.2
  526.7 92.6 all-gather.10
  659.2 131.5 reduce-scatter.4

commit v17 on v15

--- a/solution.py
+++ b/solution.py
@@ -104,6 +104,13 @@
             value = value + lax.ppermute(value, axis, [(k, k ^ step) for k in range(size)])
             step *= 2
     return value
+
+
+def sum_outer(value):
+    one, two, three = [
+        lax.ppermute(value, "o", [((k + j) % OUTER, k) for k in range(OUTER)]) for j in (1, 2, 3)
+    ]
+    return (value + two) + (one + three)
 
 
 def pair_gates(normed, router, route, experts):
@@ -762,7 +769,7 @@
     d_upper = (after(upper_last, kv_sent).astype(F32) + upper_own).reshape(up_weight.shape)
     d_lower = (lower_last.astype(F32) + lower_own)[None]
     d_attn_input = after(d_attn_input, summed)
-    summed = sum_over(after(summed, heads_sent), ("c", "y", "o"))
+    summed = sum_outer(sum_over(after(summed, heads_sent), ("c", "y")))
     d_norm_one, _ = norm_back(
         residual, inverse_one, norm_gain1, d_attn_input.astype(F32) + d_att_from_router
     )

time: 868 us -> 874 us (level)
  waiting for transfers between devices: 327 us -> 337 us
    ppermute x0 -> x3, waiting for transfers between devices: none -> 25 us  [sum_outer(): lax.ppermute(value, 'o', [((k + j) % OUTER, k) for k in range(OUTER)])]
    ppermute x5 -> x3, waiting for transfers between devices: 22.5 us -> 0.23 us  [sum_over(): lax.ppermute(value, axis, [(k, k ^ step) for k in range(size)])]
  transfers between devices with their start and end apart: 48 -> 49, of which waited for: 25 -> 25; matrix products, arithmetic and copies ran while one was open for 23% -> 23% of each run, Pallas kernels for 16% -> 15%
where the time goes in v17:
time: 874 us; the launch traced here: 864 us
  waiting for transfers between devices  337 us (39%)
  Pallas kernels  170 us (19%)
  matrix products  115 us (13%)
  starting transfers between devices  96.9 us (11%)
  other arithmetic  80.1 us (9%)
  local copies, waits for them, and re-layouts  36.8 us (4%)
  between operations  15.4 us (2%)
  blocking collectives  13.1 us (1%)
    ppermute x31, waiting for transfers between devices, shift(): return lax.ppermute(value, axis, [((k + 1) % size, k) for k in range(size)])  230 us
    pallas_call x6, Pallas kernels, call(): pl.pallas_call(kernel, grid_spec=pltpu.PrefetchScalarGridSpec(num_scalar_...  170 us
    dot_general x9, matrix products, mm(): return jnp.einsum(form, first, second, preferred_element_type=F32)  108 us
    all_gather x4, waiting for transfers between devices, meet(): return lax.all_gather(rows, GROUP, axis=0, tiled=True)  78.5 us
    ppermute x31, starting transfers between devices, shift(): return lax.ppermute(value, axis, [((k + 1) % size, k) for k in range(size)])  61.2 us
    ppermute x3, waiting for transfers between devices, sum_outer(): lax.ppermute(value, 'o', [((k + j) % OUTER, k) for k in range(OUTER)])  25 us
    convert_element_type x18, other arithmetic, add_low(): return (first.astype(F32) + second.astype(F32)).astype(BF16)  18.1 us
  transfers between devices with their start and end apart: 49, of which 25 were waited for; matrix products, arithmetic and copies ran while one was open for 23% of the time, Pallas kernels for 15%

profile of v17, /device:TPU:0, one launch (start us, length us, event | category | flops | bytes accessed | tf_op | source)
XLA Modules:
  0.0 863.8 jit_solution(6863684617976490939)
XLA Ops:
  11.1 3.0 collective-permute-start
  16.7 4.9 all-to-all-start
  21.5 55.4 %collective-permute-done.refs_3_ = bf16[704,2048]{1,0:T(8,128)(2,1)} collective-permute-done((bf16[704,2048]{1,0:T(8,128)(2,1)}, bf16[704,2048]{1,0:T(8,128)(2,1)}, u32[]{:S(2)}, u32[]{:S(2)}) %collective-permute-start) | collective-permute-done | bytes 2883616 | tf_op jit(solution)/shard_map/ppermute | solution.py:55
  78.9 11.3 %collective-permute-done.1 = bf16[4,2,64,512]{3,2,1,0:T(8,128)(2,1)S(1)} collective-permute-done((bf16[4,2,64,512]{3,2,1,0:T(8,128)(2,1)S(1)}, bf16[4,2,64,512]{3,2,1,0:T(8,128)(2,1)S(1)}, u32[]{:S(2)}, u32[]{:S(2)}) %collective-permute-start.1) | collective-permute-done | bytes 524320 | tf_op jit(solution)/shard_map/ppermute | solution.py:55
  94.8 18.9 %collective-permute-done.2 = bf16[4,256,512]{2,1,0:T(8,128)(2,1)S(1)} collective-permute-done((bf16[4,256,512]{2,1,0:T(8,128)(2,1)S(1)}, bf16[4,256,512]{2,1,0:T(8,128)(2,1)S(1)}, u32[]{:S(2)}, u32[]{:S(2)}) %collective-permute-start.2) | collective-permute-done | bytes 1048608 | tf_op jit(solution)/shard_map/ppermute | solution.py:55
  113.7 6.3 collective-permute-done.3
  121.0 3.1 pad_maximum_fusion.1.own_ref
  125.9 4.8 all-to-all-start.1
  137.9 26.2 %attend.1 = (bf16[2048,1536]{1,0:T(8,128)(2,1)}, bf16[2048,512]{1,0:T(8,128)(2,1)}, bf16[2048,1024]{1,0:T(8,128)(2,1)}) custom-call(s32[4]{0:T(128)} %pad_add_fusion.places_ref, bf16[2048,2048]{1,0:T(8,128)(2,1)} %all-gather.7.cloned.1.call-done.x_ref, f32[16,2,128]{2,1,0:T(2,128)} %copy-done.36, f32[128,128]{1,0:T(8,128)} %get-tuple-element.191.cos_ref, ...), custom_call_target="tpu_custom_call" | custom-call | flops 13421772800 | bytes 25165824 | tf_op jit(solution)/shard_map/attend/pallas_call | solution.py:469
  167.0 10.5 %rows.2 = (bf16[2,4,128,2048]{3,2,1,0:T(8,128)(2,1)}, bf16[2,4,128,2048]{3,2,1,0:T(8,128)(2,1)}) custom-call(s32[4]{0:T(128)} %pad_add_fusion.places_ref, bf16[2048,512]{1,0:T(8,128)(2,1)} %get-tuple-element.89.refs_0_, bf16[512,2048]{1,0:T(8,128)(2,1)} %bitcast.308), custom_call_target="tpu_custom_call" | custom-call | flops 4294967296 | bytes 20971520 | tf_op jit(solution)/shard_map/rows/pallas_call | solution.py:469
  177.5 2.7 copy.72
  180.4 7.3 collective-permute-done.6
  190.0 3.6 collective-permute-start.11
  196.1 9.2 %collective-permute-done.11 = bf16[2,64,2048]{2,1,0:T(8,128)(2,1)S(1)} collective-permute-done((bf16[2,64,2048]{2,1,0:T(8,128)(2,1)S(1)}, bf16[2,64,2048]{2,1,0:T(8,128)(2,1)S(1)}, u32[]{:S(2)}, u32[]{:S(2)}) %collective-permute-start.11) | collective-permute-done | bytes 524320 | tf_op jit(solution)/shard_map/ppermute | solution.py:55
  205.4 4.3 collective-permute-start.12
  209.8 11.3 %convolution_convert_fusion.1.d_units_ref = bf16[2048,704]{1,0:T(8,128)(2,1)} fusion(bf16[2048,2048]{1,0:T(8,128)(2,1)} %all-gather.5.cloned.1.call-done, bf16[704,2048]{1,0:T(8,128)(2,1)} %collective-permute-done.refs_3_), kind=kOutput, calls=%fused_computation.9 | convolution fusion | flops 5907021824 | bytes 14155776 | tf_op jit(solution)/shard_map/td,fd->tf/dot_general | solution.py:156
  221.2 3.9 collective-permute-start.13
  225.6 8.1 convolution_convert_fusion.2.d_units_ref
  233.7 7.0 collective-permute-done.8
  240.8 4.3 collective-permute-start.9
  246.1 2.9 collective-permute-done.9
  249.1 4.3 collective-permute-start.10
  253.5 3.8 collective-permute-done.10
  261.1 13.1 %all_to_all.32.info_ref = f32[16,1,128]{2,1,0:T(1,128)} all-to-all(f32[16,1,128]{2,1,0:T(1,128)S(1)} %bitcast.321), channel_id=1, replica_groups=mesh['y'=2,'c'=2,'o'=4,'i'=2] {'y','c','o'}, dimensions={0} | all-to-all | bytes 16384 | tf_op jit(solution)/shard_map/all_to_all | solution.py:138
  274.2 60.6 %all-gather.9.cloned.1.call-done.x_ref = bf16[2048,2048]{1,0:T(8,128)(2,1)} async-done(((bf16[128,2048]{1,0:T(8,128)(2,1)}), bf16[2048,2048]{1,0:T(8,128)(2,1)}) %all-gather.9.cloned.1.call-update) | async-done | bytes 8388624 | tf_op jit(solution)/shard_map/all_gather | solution.py:148
  334.9 35.5 %units.2 = (bf16[2048,1408]{1,0:T(8,128)(2,1)}, bf16[2048,704]{1,0:T(8,128)(2,1)}, f32[2048,2048]{1,0:T(8,128)}, f32[16,1,128]{2,1,0:T(1,128)}) custom-call(s32[4]{0:T(128)} %pad_add_fusion.places_ref, bf16[2048,2048]{1,0:T(8,128)(2,1)} %all-gather.9.cloned.1.call-done.x_ref, f32[16,1,128]{2,1,0:T(1,128)} %all_to_all.32.info_ref, ...), custom_call_target="tpu_custom_call" | custom-call | tf_op jit(solution)/shard_map/units/pallas_call | solution.py:469
  370.4 10.8 %collective-permute-done.15.first_ref.second_ref = bf16[1408,2048]{1,0:T(8,128)(2,1)} collective-permute-done((bf16[1408,2048]{1,0:T(8,128)(2,1)}, bf16[1408,2048]{1,0:T(8,128)(2,1)}, u32[]{:S(2)}, u32[]{:S(2)}) %collective-permute-start.15) | collective-permute-done | bytes 5767200 | tf_op jit(solution)/shard_map/ppermute | solution.py:55
  381.2 35.9 %units.3 = (bf16[2048,1408]{1,0:T(8,128)(2,1)}, bf16[2048,704]{1,0:T(8,128)(2,1)}, bf16[2048,2048]{1,0:T(8,128)(2,1)}, f32[16,1,128]{2,1,0:T(1,128)}) custom-call(s32[4]{0:T(128)} %pad_add_fusion.places_ref, bf16[2048,2048]{1,0:T(8,128)(2,1)} %all-gather.9.cloned.1.call-done.x_ref, f32[16,1,128]{2,1,0:T(1,128)} %all_to_all.32.info_ref, ...), custom_call_target="tpu_custom_call" | custom-call | tf_op jit(solution)/shard_map/units/pallas_call | solution.py:469
  417.1 10.7 %convolution_convert_fusion.3 = bf16[704,2048]{1,0:T(8,128)(2,1)} fusion(bf16[2048,704]{1,0:T(8,128)(2,1)} %get-tuple-element.104.refs_1_, bf16[2048,2048]{1,0:T(8,128)(2,1)} %all-gather.5.cloned.1.call-done), kind=kOutput, calls=%fused_computation.11 | convolution fusion | flops 5907021824 | bytes 14155776 | tf_op jit(solution)/shard_map/tf,td->fd/dot_general | solution.py:156
  427.8 21.8 %rows.3 = (bf16[2,4,128,2048]{3,2,1,0:T(8,128)(2,1)}, bf16[2,4,128,2048]{3,2,1,0:T(8,128)(2,1)}) custom-call(s32[4]{0:T(128)} %pad_add_fusion.places_ref, bf16[2048,704]{1,0:T(8,128)(2,1)} %get-tuple-element.103.refs_0_, bf16[2048,704]{1,0:T(8,128)(2,1)} %get-tuple-element.104.refs_1_, bf16[704,2048]{1,0:T(8,128)(2,1)} %bitcast.335, ...), custom_call_target="tpu_custom_call" | custom-call | flops 11811160064 | bytes 28311552 | tf_op jit(solution)/shard_map/rows/pallas_call | solution.py:469
  449.7 4.9 copy.75
  456.2 6.2 all-to-all-start.3
  462.5 18.0 %convolution_convert_fusion = bf16[1408,2048]{1,0:T(8,128)(2,1)} fusion(bf16[2048,1408]{1,0:T(8,128)(2,1)} %get-tuple-element.108, bf16[2048,2048]{1,0:T(8,128)(2,1)} %all-gather.9.cloned.1.call-done.x_ref), kind=kOutput, calls=%fused_computation.3 | convolution fusion | flops 11814043648 | bytes 19922944 | tf_op jit(solution)/shard_map/tf,td->fd/dot_general | solution.py:156
  480.6 7.9 add_convert_fusion
  488.5 31.3 %collective-permute-done.20 = bf16[704,2048]{1,0:T(8,128)(2,1)} collective-permute-done((bf16[704,2048]{1,0:T(8,128)(2,1)}, bf16[704,2048]{1,0:T(8,128)(2,1)}, u32[]{:S(2)}, u32[]{:S(2)}) %collective-permute-start.20) | collective-permute-done | bytes 2883616 | tf_op jit(solution)/shard_map/ppermute | solution.py:55
  519.8 2.9 reduce-scatter.3.cloned.1.call-done
  529.9 21.2 %collective-permute-done.17 = bf16[2,64,2048]{2,1,0:T(8,128)(2,1)S(1)} collective-permute-done((bf16[2,64,2048]{2,1,0:T(8,128)(2,1)S(1)}, bf16[2,64,2048]{2,1,0:T(8,128)(2,1)S(1)}, u32[]{:S(2)}, u32[]{:S(2)}) %collective-permute-start.17) | collective-permute-done | bytes 524320 | tf_op jit(solution)/shard_map/ppermute | solution.py:55
  554.8 14.7 %collective-permute-done.18 = bf16[2,64,2048]{2,1,0:T(8,128)(2,1)S(1)} collective-permute-done((bf16[2,64,2048]{2,1,0:T(8,128)(2,1)S(1)}, bf16[2,64,2048]{2,1,0:T(8,128)(2,1)S(1)}, u32[]{:S(2)}, u32[]{:S(2)}) %collective-permute-start.18) | collective-permute-done | bytes 524320 | tf_op jit(solution)/shard_map/ppermute | solution.py:55
  570.7 4.1 collective-permute-start.19
  574.8 19.6 %fusion.61 = f32[1408,2048]{1,0:T(8,128)} fusion(bf16[2048,1408]{1,0:T(8,128)(2,1)} %get-tuple-element.144, bf16[2048,2048]{1,0:T(8,128)(2,1)} %all-gather.9.cloned.1.call-done.x_ref), kind=kOutput, calls=%fused_computation.199 | convolution fusion | flops 11811160064 | bytes 25690112 | tf_op jit(solution)/shard_map/tf,td->fd/dot_general | solution.py:156
  596.2 4.3 collective-permute-done.19
  601.5 17.9 %all-gather.11.cloned.1.call-done.mid_ref = bf16[2048,2048]{1,0:T(8,128)(2,1)} async-done(((bf16[128,2048]{1,0:T(8,128)(2,1)}), bf16[2048,2048]{1,0:T(8,128)(2,1)}) %all-gather.11.cloned.1.call-update) | async-done | bytes 8388624 | tf_op jit(solution)/shard_map/all_gather | solution.py:148
  619.4 39.6 %attend_back.1 = (bf16[2048,512]{1,0:T(8,128)(2,1)}, bf16[2048,1024]{1,0:T(8,128)(2,1)}, bf16[2048,2048]{1,0:T(8,128)(2,1)}, f32[16,1,128]{2,1,0:T(1,128)}, f32[1,2048]{1,0:T(1,128)}) custom-call(s32[4]{0:T(128)} %pad_add_fusion.places_ref, bf16[2048,2048]{1,0:T(8,128)(2,1)} %all-gather.11.cloned.1.call-done.mid_ref, f32[16,2,128]{2,1,0:T(2,128)} %copy-done.36, ...), custom_call_target="tpu_custom_call" | custom-call | flops 18522046464 | bytes 46137344 | tf_op jit(solution)/shard_map/attend_back/pallas_call | solution.py:469
  659.0 8.6 all-to-all-start.4
  671.9 13.8 %fusion.56 = f32[2048,1024]{1,0:T(8,128)S(1)} fusion(bf16[2048,2048]{1,0:T(8,128)(2,1)} %all-gather.7.cloned.1.call-done.x_ref, bf16[2048,1024]{1,0:T(8,128)(2,1)} %get-tuple-element.117), kind=kOutput, calls=%fused_computation.194 | convolution fusion | flops 8589934592 | bytes 20971520 | tf_op jit(solution)/shard_map/td,tf->df/dot_general | solution.py:156
  685.7 3.2 copy-done.5
  694.0 11.8 %add_bitcast_fusion = f32[1,704,2048]{2,1,0:T(8,128)} fusion(bf16[704,2048]{1,0:T(8,128)(2,1)} %collective-permute-done.20, bf16[2048,704]{1,0:T(8,128)(2,1)} %get-tuple-element.103.refs_0_, bf16[2048,2048]{1,0:T(8,128)(2,1)} %all-gather.5.cloned.1.call-done), kind=kOutput, calls=%fused_computation.4 | convolution fusion | flops 5908463616 | bytes 19922944 | tf_op jit(solution)/shard_map/tf,td->fd/dot_general | solution.py:156
  706.6 2.6 fusion.1
  709.2 5.7 bitcast_add_fusion
  718.1 7.2 fusion.59
  729.5 13.5 %convert_add_fusion = f32[1408,2048]{1,0:T(8,128)} fusion(f32[1408,2048]{1,0:T(8,128)} %fusion.61, bf16[1408,2048]{1,0:T(8,128)(2,1)} %collective-permute-done.37), kind=kLoop, calls=%fused_computation | loop fusion | flops 5767168 | bytes 28835840 | tf_op jit(solution)/shard_map/add | solution.py:769
  743.1 7.7 fusion.60
  754.3 3.2 collective-permute-start.24
  763.7 5.3 collective-permute-done.24
  769.0 4.4 collective-permute-start.25
  773.5 11.7 %collective-permute-done.25 = bf16[64,2048]{1,0:T(8,128)(2,1)S(1)} collective-permute-done((bf16[64,2048]{1,0:T(8,128)(2,1)S(1)}, bf16[64,2048]{1,0:T(8,128)(2,1)S(1)}, u32[]{:S(2)}, u32[]{:S(2)}) %collective-permute-start.25) | collective-permute-done | bytes 262176 | tf_op jit(solution)/shard_map/ppermute | solution.py:55
  785.2 4.3 collective-permute-start.26
  794.2 5.5 all-to-all-start.5
  802.3 3.2 fusion.12
  805.5 7.2 collective-permute-done.36
  812.7 3.8 collective-permute-start.34
  816.6 3.0 add_bitcast_fusion.1
  819.6 11.9 %collective-permute-done.35 = f32[12,2048]{1,0:T(8,128)S(1)} collective-permute-done((f32[12,2048]{1,0:T(8,128)S(1)}, f32[12,2048]{1,0:T(8,128)S(1)}, u32[]{:S(2)}, u32[]{:S(2)}) %collective-permute-start.35) | collective-permute-done | bytes 98336 | tf_op jit(solution)/shard_map/ppermute | solution.py:111
  831.5 13.1 %collective-permute-done.33 = f32[12,2048]{1,0:T(8,128)S(1)} collective-permute-done((f32[12,2048]{1,0:T(8,128)S(1)}, f32[12,2048]{1,0:T(8,128)S(1)}, u32[]{:S(2)}, u32[]{:S(2)}) %collective-permute-start.33) | collective-permute-done | bytes 98336 | tf_op jit(solution)/shard_map/ppermute | solution.py:111
  (290 shorter events, 99.2 us)
Async XLA Ops:
  7.2 252.2 %copy-start = (f32[2048,4]{0,1:T(4,128)S(1)}, f32[2048,4]{0,1:T(4,128)}, u32[]{:S(2)}) copy-start(f32[2048,4]{0,1:T(4,128)} %param.23) | copy-start | bytes 98308
  7.2 130.1 %all-gather.7.cloned.1.call-start = ((), (), s32[]{:S(2)}) async-start(), calls=%async_computation.9 | async-start | bytes 8912896 | tf_op jit(solution)/shard_map/all_gather | solution.py:148
  11.1 65.8 %collective-permute-start = (bf16[704,2048]{1,0:T(8,128)(2,1)}, bf16[704,2048]{1,0:T(8,128)(2,1)}, u32[]{:S(2)}, u32[]{:S(2)}) collective-permute-start(bf16[704,2048]{1,0:T(8,128)(2,1)} %bitcast.334), channel_id=1, source_target_pairs={{1,0},{0,1},{3,2},{2,3},{5,4},{4,5},{7,6},{6,7},{9,8},{8,9},{11,10... | collective-permute-start | bytes 8650760 | tf_op jit(solution)/shard_map/ppermute | solution.py:55
  16.7 60.3 %all-to-all-start = ((bf16[4,384,512]{2,1,0:T(8,128)(2,1)}), bf16[4,384,512]{2,1,0:T(8,128)(2,1)S(1)}, u32[]{:S(2)}, u32[]{:S(2)}) async-start(bf16[4,384,512]{2,1,0:T(8,128)(2,1)} %maximum_maximum_fusion), calls=%async_computation | async-start | bytes 3145728 | tf_op jit(solution)/shard_map/all_to_all | solution.py:169
  21.5 71.8 %copy-start.19 = (f32[128,2048]{1,0:T(8,128)S(1)}, f32[128,2048]{1,0:T(8,128)}, u32[]{:S(2)}) copy-start(f32[128,2048]{1,0:T(8,128)} %param.31) | copy-start | bytes 3145732
  21.5 188.2 %all-gather.5.cloned.1.call-start = ((), (), s32[]{:S(2)}) async-start(), calls=%async_computation.8 | async-start | bytes 8912896 | tf_op jit(solution)/shard_map/all_gather | solution.py:148
  77.0 13.2 %collective-permute-start.1 = (bf16[4,2,64,512]{3,2,1,0:T(8,128)(2,1)S(1)}, bf16[4,2,64,512]{3,2,1,0:T(8,128)(2,1)S(1)}, u32[]{:S(2)}, u32[]{:S(2)}) collective-permute-start(bf16[4,2,64,512]{3,2,1,0:T(8,128)(2,1)S(1)} %bitcast.310), channel_id=1, source_target_pairs={{1,0},{0,1},{3,2},{2,3},{5,4},{4,5},{7,6},{6,7},{9,8},{8,9},{11,10... | collective-permute-start | bytes 1572872 | tf_op jit(solution)/shard_map/ppermute | solution.py:55
  90.1 23.5 %collective-permute-start.2 = (bf16[4,256,512]{2,1,0:T(8,128)(2,1)S(1)}, bf16[4,256,512]{2,1,0:T(8,128)(2,1)S(1)}, u32[]{:S(2)}, u32[]{:S(2)}) collective-permute-start(bf16[4,256,512]{2,1,0:T(8,128)(2,1)S(1)} %slice.265), channel_id=1, source_target_pairs={{1,0},{0,1},{3,2},{2,3},{5,4},{4,5},{7,6},{6,7},{9,8},{8,9},{11,10... | collective-permute-start | bytes 3145736 | tf_op jit(solution)/shard_map/ppermute | solution.py:55
  91.7 22.0 %copy-start.22 = (bf16[2,4,2,64,512]{4,3,2,1,0:T(8,128)(2,1)}, bf16[2,4,2,64,512]{4,3,2,1,0:T(8,128)(2,1)S(1)}, u32[]{:S(2)}) copy-start(bf16[2,4,2,64,512]{4,3,2,1,0:T(8,128)(2,1)S(1)} %pad_maximum_fusion.4) | copy-start | bytes 3145732
  91.7 32.4 %copy-start.14 = (bf16[128,2048]{1,0:T(8,128)(2,1)S(1)}, bf16[128,2048]{1,0:T(8,128)(2,1)}, u32[]{:S(2)}) copy-start(bf16[128,2048]{1,0:T(8,128)(2,1)} %fusion.6) | copy-start | bytes 1572868
  91.7 32.4 %copy-start.30 = (f32[2048,4]{0,1:T(4,128)S(1)}, f32[2048,4]{0,1:T(4,128)}, u32[]{:S(2)}) copy-start(f32[2048,4]{0,1:T(4,128)} %param.22) | copy-start | bytes 98308
  91.7 32.9 %copy-start.38 = (s32[128,2]{0,1:T(2,128)S(1)}, s32[128,2]{0,1:T(2,128)}, u32[]{:S(2)}) copy-start(s32[128,2]{0,1:T(2,128)} %param.18) | copy-start | bytes 3076
  91.7 33.5 %copy-start.53 = (s32[1,128]{1,0:T(1,128)S(1)}, s32[1,128]{1,0:T(1,128)}, u32[]{:S(2)}) copy-start(s32[1,128]{1,0:T(1,128)} %param.17) | copy-start | bytes 1540
  91.7 28.3 %collective-permute-start.3 = (bf16[2,4,2,64,512]{4,3,2,1,0:T(8,128)(2,1)S(1)}, bf16[2,4,2,64,512]{4,3,2,1,0:T(8,128)(2,1)S(1)}, u32[]{:S(2)}, u32[]{:S(2)}) collective-permute-start(bf16[2,4,2,64,512]{4,3,2,1,0:T(8,128)(2,1)S(1)} %pad_maximum_fusion.4), channel_id=1, source_target_pairs={{16,0},{0,16},{17,1},{1,17},{18,2},{2,18},{19,3},{3,19},{20,4},{4,... | collective-permute-start | bytes 3145736 | tf_op jit(solution)/shard_map/ppermute | solution.py:55
  94.8 39.2 %copy-start.21 = (bf16[4,256,512]{2,1,0:T(8,128)(2,1)S(1)}, bf16[4,256,512]{2,1,0:T(8,128)(2,1)}, u32[]{:S(2)}) copy-start(bf16[4,256,512]{2,1,0:T(8,128)(2,1)} %copy-done.20) | copy-start | bytes 3145732
  124.0 13.2 %collective-permute-start.4 = (bf16[2,2,4,2,64,512]{5,4,3,2,1,0:T(8,128)(2,1)}, bf16[2,2,4,2,64,512]{5,4,3,2,1,0:T(8,128)(2,1)}, u32[]{:S(2)}, u32[]{:S(2)}) collective-permute-start(bf16[2,2,4,2,64,512]{5,4,3,2,1,0:T(8,128)(2,1)} %pad_maximum_fusion.1.own_ref), channel_id=1, source_target_pairs={{8,0},{0,8},{9,1},{1,9},{10,2},{2,10},{11,3},{3,11},{12,4},{4,12},... | collective-permute-start | bytes 6291464 | tf_op jit(solution)/shard_map/ppermute | solution.py:55
  125.9 11.4 %all-to-all-start.1 = ((f32[16,2,128]{2,1,0:T(2,128)}), f32[16,2,128]{2,1,0:T(2,128)S(1)}, u32[]{:S(2)}, u32[]{:S(2)}) async-start(f32[16,2,128]{2,1,0:T(2,128)} %pad_maximum_fusion.8), calls=%async_computation.1 | async-start | bytes 32768 | tf_op jit(solution)/shard_map/all_to_all | solution.py:138
  130.7 204.1 %all-gather.9.cloned.1.call-start = ((), (), s32[]{:S(2)}) async-start(), calls=%async_computation.10 | async-start | bytes 8912896 | tf_op jit(solution)/shard_map/all_gather | solution.py:148
  132.5 31.6 %collective-permute-start.5 = (bf16[256,2048]{1,0:T(8,128)(2,1)}, bf16[256,2048]{1,0:T(8,128)(2,1)}, u32[]{:S(2)}, u32[]{:S(2)}) collective-permute-start(bf16[256,2048]{1,0:T(8,128)(2,1)} %bitcast.312), channel_id=1, source_target_pairs={{1,0},{0,1},{3,2},{2,3},{5,4},{4,5},{7,6},{6,7},{9,8},{8,9},{11,10... | collective-permute-start | bytes 3145736 | tf_op jit(solution)/shard_map/ppermute | solution.py:55
  137.9 26.2 %copy-start.24 = (bf16[1,256,2048]{2,1,0:T(8,128)(2,1)S(1)}, bf16[1,256,2048]{2,1,0:T(8,128)(2,1)}, u32[]{:S(2)}) copy-start(bf16[1,256,2048]{2,1,0:T(8,128)(2,1)} %param.26) | copy-start | bytes 3145732
  180.2 7.5 collective-permute-start.6
  190.0 15.3 %collective-permute-start.11 = (bf16[2,64,2048]{2,1,0:T(8,128)(2,1)S(1)}, bf16[2,64,2048]{2,1,0:T(8,128)(2,1)S(1)}, u32[]{:S(2)}, u32[]{:S(2)}) collective-permute-start(bf16[2,64,2048]{2,1,0:T(8,128)(2,1)S(1)} %slice_bitcast_fusion.14), channel_id=1, source_target_pairs={{2,0},{4,2},{6,4},{0,6},{3,1},{5,3},{7,5},{1,7},{10,8},{12,10},{14... | collective-permute-start | bytes 1572872 | tf_op jit(solution)/shard_map/ppermute | solution.py:55
  194.6 30.5 %collective-permute-start.7 = (bf16[4,64,2048]{2,1,0:T(8,128)(2,1)}, bf16[4,64,2048]{2,1,0:T(8,128)(2,1)S(1)}, u32[]{:S(2)}, u32[]{:S(2)}) collective-permute-start(bf16[4,64,2048]{2,1,0:T(8,128)(2,1)} %slice_bitcast_fusion.6), channel_id=1, source_target_pairs={{16,0},{0,16},{17,1},{1,17},{18,2},{2,18},{19,3},{3,19},{20,4},{4,... | collective-permute-start | bytes 3145736 | tf_op jit(solution)/shard_map/ppermute | solution.py:55
  205.4 15.6 %collective-permute-start.12 = (bf16[2,64,2048]{2,1,0:T(8,128)(2,1)S(1)}, bf16[2,64,2048]{2,1,0:T(8,128)(2,1)S(1)}, u32[]{:S(2)}, u32[]{:S(2)}) collective-permute-start(bf16[2,64,2048]{2,1,0:T(8,128)(2,1)S(1)} %fusion.20), channel_id=1, source_target_pairs={{2,0},{4,2},{6,4},{0,6},{3,1},{5,3},{7,5},{1,7},{10,8},{12,10},{14... | collective-permute-start | bytes 1572872 | tf_op jit(solution)/shard_map/ppermute | solution.py:55
  209.8 15.9 %copy-start.51 = (bf16[2048,2048]{1,0:T(8,128)(2,1)S(1)}, bf16[2048,2048]{1,0:T(8,128)(2,1)}, u32[]{:S(2)}) copy-start(bf16[2048,2048]{1,0:T(8,128)(2,1)} %all-gather.5.cloned.1.call-done) | copy-start | bytes 25165828
  221.2 23.9 %collective-permute-start.13 = (bf16[2,64,2048]{2,1,0:T(8,128)(2,1)S(1)}, bf16[2,64,2048]{2,1,0:T(8,128)(2,1)S(1)}, u32[]{:S(2)}, u32[]{:S(2)}) collective-permute-start(bf16[2,64,2048]{2,1,0:T(8,128)(2,1)S(1)} %fusion.19), channel_id=1, source_target_pairs={{2,0},{4,2},{6,4},{0,6},{3,1},{5,3},{7,5},{1,7},{10,8},{12,10},{14... | collective-permute-start | bytes 1572872 | tf_op jit(solution)/shard_map/ppermute | solution.py:55
  225.6 15.2 %collective-permute-start.8 = (bf16[64,2048]{1,0:T(8,128)(2,1)S(1)}, bf16[64,2048]{1,0:T(8,128)(2,1)S(1)}, u32[]{:S(2)}, u32[]{:S(2)}) collective-permute-start(bf16[64,2048]{1,0:T(8,128)(2,1)S(1)} %slice_bitcast_fusion.20), channel_id=1, source_target_pairs={{2,0},{4,2},{6,4},{0,6},{3,1},{5,3},{7,5},{1,7},{10,8},{12,10},{14... | collective-permute-start | bytes 786440 | tf_op jit(solution)/shard_map/ppermute | solution.py:55
  233.7 23.8 %copy-start.2 = (bf16[128,2048]{1,0:T(8,128)(2,1)S(1)}, bf16[128,2048]{1,0:T(8,128)(2,1)}, u32[]{:S(2)}) copy-start(bf16[128,2048]{1,0:T(8,128)(2,1)} %param.16) | copy-start | bytes 1572868
  233.7 23.8 %copy-start.28 = (f32[2048]{0:T(1024)S(1)}, f32[2048]{0:T(1024)}, u32[]{:S(2)}) copy-start(f32[2048]{0:T(1024)} %param.27) | copy-start | bytes 24580
  240.8 17.0 %copy-start.34 = (f32[2048]{0:T(1024)S(1)}, f32[2048]{0:T(1024)}, u32[]{:S(2)}) copy-start(f32[2048]{0:T(1024)} %param.21) | copy-start | bytes 24580
  240.8 8.2 collective-permute-start.9
  245.3 8.1 collective-permute-start.14
  249.1 8.2 collective-permute-start.10
  258.9 263.8 %reduce-scatter.3.cloned.1.call-start = ((), (), s32[]{:S(2)}) async-start(), calls=%async_computation.11 | async-start | bytes 8912896 | tf_op jit(solution)/shard_map/reduce_scatter | solution.py:152
  258.9 122.3 %collective-permute-start.15 = (bf16[1408,2048]{1,0:T(8,128)(2,1)}, bf16[1408,2048]{1,0:T(8,128)(2,1)}, u32[]{:S(2)}, u32[]{:S(2)}) collective-permute-start(bf16[1408,2048]{1,0:T(8,128)(2,1)} %bitcast.296), channel_id=1, source_target_pairs={{1,0},{0,1},{3,2},{2,3},{5,4},{4,5},{7,6},{6,7},{9,8},{8,9},{11,10... | collective-permute-start | bytes 17301512 | tf_op jit(solution)/shard_map/ppermute | solution.py:55
  454.6 26.0 %collective-permute-start.16 = (bf16[2,4,128,2048]{3,2,0,1:T(8,128)(2,1)}, bf16[2,4,128,2048]{3,2,0,1:T(8,128)(2,1)}, u32[]{:S(2)}, u32[]{:S(2)}) collective-permute-start(bf16[2,4,128,2048]{3,2,0,1:T(8,128)(2,1)} %copy.75), channel_id=1, source_target_pairs={{8,0},{0,8},{9,1},{1,9},{10,2},{2,10},{11,3},{3,11},{12,4},{4,12},... | collective-permute-start | bytes 12582920 | tf_op jit(solution)/shard_map/ppermute | solution.py:55
  454.6 65.2 %collective-permute-start.20 = (bf16[704,2048]{1,0:T(8,128)(2,1)}, bf16[704,2048]{1,0:T(8,128)(2,1)}, u32[]{:S(2)}, u32[]{:S(2)}) collective-permute-start(bf16[704,2048]{1,0:T(8,128)(2,1)} %convolution_convert_fusion.3), channel_id=1, source_target_pairs={{1,0},{0,1},{3,2},{2,3},{5,4},{4,5},{7,6},{6,7},{9,8},{8,9},{11,10... | collective-permute-start | bytes 8650760 | tf_op jit(solution)/shard_map/ppermute | solution.py:55
  456.2 24.3 %all-to-all-start.3 = ((f32[16,1,128]{2,1,0:T(1,128)}), f32[16,1,128]{2,1,0:T(1,128)S(1)}, u32[]{:S(2)}, u32[]{:S(2)}) async-start(f32[16,1,128]{2,1,0:T(1,128)} %add.177), calls=%async_computation.4 | async-start | bytes 16384 | tf_op jit(solution)/shard_map/all_to_all | solution.py:142
  462.4 157.0 %all-gather.11.cloned.1.call-start = ((), (), s32[]{:S(2)}) async-start(), calls=%async_computation.12 | async-start | bytes 8912896 | tf_op jit(solution)/shard_map/all_gather | solution.py:148
  526.5 267.6 %reduce-scatter.5.cloned.1.call-start = ((), (), s32[]{:S(2)}) async-start(), calls=%async_computation.13 | async-start | bytes 8912896 | tf_op jit(solution)/shard_map/reduce_scatter | solution.py:152
  527.7 23.4 %collective-permute-start.17 = (bf16[2,64,2048]{2,1,0:T(8,128)(2,1)S(1)}, bf16[2,64,2048]{2,1,0:T(8,128)(2,1)S(1)}, u32[]{:S(2)}, u32[]{:S(2)}) collective-permute-start(bf16[2,64,2048]{2,1,0:T(8,128)(2,1)S(1)} %slice_bitcast_fusion.10), channel_id=1, source_target_pairs={{2,0},{4,2},{6,4},{0,6},{3,1},{5,3},{7,5},{1,7},{10,8},{12,10},{14... | collective-permute-start | bytes 1572872 | tf_op jit(solution)/shard_map/ppermute | solution.py:55
  552.3 17.2 %collective-permute-start.18 = (bf16[2,64,2048]{2,1,0:T(8,128)(2,1)S(1)}, bf16[2,64,2048]{2,1,0:T(8,128)(2,1)S(1)}, u32[]{:S(2)}, u32[]{:S(2)}) collective-permute-start(bf16[2,64,2048]{2,1,0:T(8,128)(2,1)S(1)} %fusion.17), channel_id=1, source_target_pairs={{2,0},{4,2},{6,4},{0,6},{3,1},{5,3},{7,5},{1,7},{10,8},{12,10},{14... | collective-permute-start | bytes 1572872 | tf_op jit(solution)/shard_map/ppermute | solution.py:55
  553.4 176.1 %collective-permute-start.37 = (bf16[1408,2048]{1,0:T(8,128)(2,1)}, bf16[1408,2048]{1,0:T(8,128)(2,1)}, u32[]{:S(2)}, u32[]{:S(2)}) collective-permute-start(bf16[1408,2048]{1,0:T(8,128)(2,1)} %convolution_convert_fusion), channel_id=1, source_target_pairs={{1,0},{0,1},{3,2},{2,3},{5,4},{4,5},{7,6},{6,7},{9,8},{8,9},{11,10... | collective-permute-start | bytes 17301512 | tf_op jit(solution)/shard_map/ppermute | solution.py:55
  570.7 29.8 %collective-permute-start.19 = (bf16[2,64,2048]{2,1,0:T(8,128)(2,1)S(1)}, bf16[2,64,2048]{2,1,0:T(8,128)(2,1)S(1)}, u32[]{:S(2)}, u32[]{:S(2)}) collective-permute-start(bf16[2,64,2048]{2,1,0:T(8,128)(2,1)S(1)} %fusion.16), channel_id=1, source_target_pairs={{2,0},{4,2},{6,4},{0,6},{3,1},{5,3},{7,5},{1,7},{10,8},{12,10},{14... | collective-permute-start | bytes 1572872 | tf_op jit(solution)/shard_map/ppermute | solution.py:55
  574.8 19.6 %copy-start.16 = (bf16[128,2048]{1,0:T(8,128)(2,1)S(1)}, bf16[128,2048]{1,0:T(8,128)(2,1)}, u32[]{:S(2)}) copy-start(bf16[128,2048]{1,0:T(8,128)(2,1)} %multiply_convert_fusion) | copy-start | bytes 1572868
  574.8 20.0 %copy-start.8 = (bf16[2,4,128,2048]{3,2,0,1:T(8,128)(2,1)S(1)}, bf16[2,4,128,2048]{3,2,0,1:T(8,128)(2,1)}, u32[]{:S(2)}) copy-start(bf16[2,4,128,2048]{3,2,0,1:T(8,128)(2,1)} %add_convert_fusion) | copy-start | bytes 12582916
  659.0 31.8 %all-to-all-start.4 = ((f32[16,1,128]{2,1,0:T(1,128)}), f32[16,1,128]{2,1,0:T(1,128)S(1)}, u32[]{:S(2)}, u32[]{:S(2)}) async-start(f32[16,1,128]{2,1,0:T(1,128)} %get-tuple-element.124), calls=%async_computation.5 | async-start | bytes 16384 | tf_op jit(solution)/shard_map/all_to_all | solution.py:142
  669.9 36.6 %collective-permute-start.23 = (bf16[4,64,2048]{2,1,0:T(8,128)(2,1)}, bf16[4,64,2048]{2,1,0:T(8,128)(2,1)}, u32[]{:S(2)}, u32[]{:S(2)}) collective-permute-start(bf16[4,64,2048]{2,1,0:T(8,128)(2,1)} %slice_bitcast_fusion.4), channel_id=1, source_target_pairs={{16,0},{0,16},{17,1},{1,17},{18,2},{2,18},{19,3},{3,19},{20,4},{4,... | collective-permute-start | bytes 3145736 | tf_op jit(solution)/shard_map/ppermute | solution.py:55
  690.8 18.4 %collective-permute-start.21 = (bf16[2,512,1024]{2,1,0:T(8,128)(2,1)}, bf16[2,512,1024]{2,1,0:T(8,128)(2,1)}, u32[]{:S(2)}, u32[]{:S(2)}) collective-permute-start(bf16[2,512,1024]{2,1,0:T(8,128)(2,1)} %fusion), channel_id=1, source_target_pairs={{0,8},{8,0},{1,9},{9,1},{2,10},{10,2},{3,11},{11,3},{4,12},{12,4},... | collective-permute-start | bytes 6291464 | tf_op jit(solution)/shard_map/ppermute | solution.py:204
  692.5 13.4 %collective-permute-start.28 = (f32[12,2048]{1,0:T(8,128)S(1)}, f32[12,2048]{1,0:T(8,128)S(1)}, u32[]{:S(2)}, u32[]{:S(2)}) collective-permute-start(f32[12,2048]{1,0:T(8,128)S(1)} %concatenate.43), channel_id=1, source_target_pairs={{0,1},{1,0},{2,3},{3,2},{4,5},{5,4},{6,7},{7,6},{8,9},{9,8},{10,11... | collective-permute-start | bytes 294920 | tf_op jit(solution)/shard_map/ppermute | solution.py:104
  716.1 37.9 %collective-permute-start.22 = (bf16[4,2,64,1024]{3,2,1,0:T(8,128)(2,1)}, bf16[4,2,64,1024]{3,2,1,0:T(8,128)(2,1)}, u32[]{:S(2)}, u32[]{:S(2)}) collective-permute-start(bf16[4,2,64,1024]{3,2,1,0:T(8,128)(2,1)} %bitcast.60), channel_id=1, source_target_pairs={{16,0},{0,16},{17,1},{1,17},{18,2},{2,18},{19,3},{3,19},{20,4},{4,... | collective-permute-start | bytes 3145736 | tf_op jit(solution)/shard_map/ppermute | solution.py:55
  728.4 33.3 %collective-permute-start.29 = (bf16[4,256,512]{2,1,0:T(8,128)(2,1)}, bf16[4,256,512]{2,1,0:T(8,128)(2,1)}, u32[]{:S(2)}, u32[]{:S(2)}) collective-permute-start(bf16[4,256,512]{2,1,0:T(8,128)(2,1)} %select_bitcast_fusion), channel_id=1, source_target_pairs={{1,0},{0,1},{3,2},{2,3},{5,4},{4,5},{7,6},{6,7},{9,8},{8,9},{11,10... | collective-permute-start | bytes 3145736 | tf_op jit(solution)/shard_map/ppermute | solution.py:55
  754.3 14.6 %collective-permute-start.24 = (bf16[64,2048]{1,0:T(8,128)(2,1)S(1)}, bf16[64,2048]{1,0:T(8,128)(2,1)S(1)}, u32[]{:S(2)}, u32[]{:S(2)}) collective-permute-start(bf16[64,2048]{1,0:T(8,128)(2,1)S(1)} %slice_bitcast_fusion.26), channel_id=1, source_target_pairs={{2,0},{4,2},{6,4},{0,6},{3,1},{5,3},{7,5},{1,7},{10,8},{12,10},{14... | collective-permute-start | bytes 786440 | tf_op jit(solution)/shard_map/ppermute | solution.py:55
  757.6 15.9 %collective-permute-start.27 = (bf16[64,2048]{1,0:T(8,128)(2,1)S(1)}, bf16[64,2048]{1,0:T(8,128)(2,1)S(1)}, u32[]{:S(2)}, u32[]{:S(2)}) collective-permute-start(bf16[64,2048]{1,0:T(8,128)(2,1)S(1)} %slice_bitcast_fusion.25), channel_id=1, source_target_pairs={{16,0},{0,16},{17,1},{1,17},{18,2},{2,18},{19,3},{3,19},{20,4},{4,... | collective-permute-start | bytes 786440 | tf_op jit(solution)/shard_map/ppermute | solution.py:55
  760.1 29.4 %collective-permute-start.30 = (bf16[4,64,1024]{2,1,0:T(8,128)(2,1)S(1)}, bf16[4,64,1024]{2,1,0:T(8,128)(2,1)S(1)}, u32[]{:S(2)}, u32[]{:S(2)}) collective-permute-start(bf16[4,64,1024]{2,1,0:T(8,128)(2,1)S(1)} %fusion.22), channel_id=1, source_target_pairs={{1,0},{0,1},{3,2},{2,3},{5,4},{4,5},{7,6},{6,7},{9,8},{8,9},{11,10... | collective-permute-start | bytes 1572872 | tf_op jit(solution)/shard_map/ppermute | solution.py:55
  769.0 16.1 %collective-permute-start.25 = (bf16[64,2048]{1,0:T(8,128)(2,1)S(1)}, bf16[64,2048]{1,0:T(8,128)(2,1)S(1)}, u32[]{:S(2)}, u32[]{:S(2)}) collective-permute-start(bf16[64,2048]{1,0:T(8,128)(2,1)S(1)} %fusion.26), channel_id=1, source_target_pairs={{2,0},{4,2},{6,4},{0,6},{3,1},{5,3},{7,5},{1,7},{10,8},{12,10},{14... | collective-permute-start | bytes 786440 | tf_op jit(solution)/shard_map/ppermute | solution.py:55
  785.2 8.2 collective-permute-start.26
  789.8 22.8 %collective-permute-start.36 = (bf16[256,2048]{1,0:T(8,128)(2,1)}, bf16[256,2048]{1,0:T(8,128)(2,1)}, u32[]{:S(2)}, u32[]{:S(2)}) collective-permute-start(bf16[256,2048]{1,0:T(8,128)(2,1)} %slice_select_fusion), channel_id=1, source_target_pairs={{1,0},{0,1},{3,2},{2,3},{5,4},{4,5},{7,6},{6,7},{9,8},{8,9},{11,10... | collective-permute-start | bytes 3145736 | tf_op jit(solution)/shard_map/ppermute | solution.py:55
  794.2 51.7 %all-to-all-start.5 = ((bf16[4,384,512]{2,1,0:T(8,128)(2,1)}), bf16[4,384,512]{2,1,0:T(8,128)(2,1)}, u32[]{:S(2)}, u32[]{:S(2)}) async-start(bf16[4,384,512]{2,1,0:T(8,128)(2,1)} %pad_maximum_fusion.3), calls=%async_computation.7 | async-start | bytes 3145728 | tf_op jit(solution)/shard_map/all_to_all | solution.py:169
  799.7 1.6 collective-permute-start.31
  802.2 10.5 %collective-permute-start.32 = (f32[12,2048]{1,0:T(8,128)S(1)}, f32[12,2048]{1,0:T(8,128)S(1)}, u32[]{:S(2)}, u32[]{:S(2)}) collective-permute-start(f32[12,2048]{1,0:T(8,128)S(1)} %add.196), channel_id=1, source_target_pairs={{0,16},{16,0},{1,17},{17,1},{2,18},{18,2},{3,19},{19,3},{4,20},{20... | collective-permute-start | bytes 294920 | tf_op jit(solution)/shard_map/ppermute | solution.py:104
  812.7 18.9 %collective-permute-start.35 = (f32[12,2048]{1,0:T(8,128)S(1)}, f32[12,2048]{1,0:T(8,128)S(1)}, u32[]{:S(2)}, u32[]{:S(2)}) collective-permute-start(f32[12,2048]{1,0:T(8,128)S(1)} %add.197), channel_id=1, source_target_pairs={{6,0},{0,2},{2,4},{4,6},{7,1},{1,3},{3,5},{5,7},{14,8},{8,10},{10,... | collective-permute-start | bytes 294920 | tf_op jit(solution)/shard_map/ppermute | solution.py:111
  812.7 18.8 %collective-permute-start.34 = (f32[12,2048]{1,0:T(8,128)S(1)}, f32[12,2048]{1,0:T(8,128)S(1)}, u32[]{:S(2)}, u32[]{:S(2)}) collective-permute-start(f32[12,2048]{1,0:T(8,128)S(1)} %add.197), channel_id=1, source_target_pairs={{2,0},{4,2},{6,4},{0,6},{3,1},{5,3},{7,5},{1,7},{10,8},{12,10},{14... | collective-permute-start | bytes 294920 | tf_op jit(solution)/shard_map/ppermute | solution.py:111
  816.6 28.0 %collective-permute-start.33 = (f32[12,2048]{1,0:T(8,128)S(1)}, f32[12,2048]{1,0:T(8,128)S(1)}, u32[]{:S(2)}, u32[]{:S(2)}) collective-permute-start(f32[12,2048]{1,0:T(8,128)S(1)} %add.197), channel_id=1, source_target_pairs={{4,0},{6,2},{0,4},{2,6},{5,1},{7,3},{1,5},{3,7},{12,8},{14,10},{8,... | collective-permute-start | bytes 294920 | tf_op jit(solution)/shard_map/ppermute | solution.py:111
  (40 other events, 232.5 us)
Sparse Core Ops, SparseCore 0:
  11.2 106.3 all-gather.6
  121.1 75.4 all-gather.4
  259.0 75.8 all-gather.8
  417.2 105.4 reduce-scatter.2
  526.7 92.6 all-gather.10
  659.1 127.8 reduce-scatter.4
